TPU v7x, 32 devices: a whole 2x2x4 slice. The times are simulated.
32 devices in a mesh: tile: 8 (over z, y), grp: 4 (over x, core).
Axes of the slice: x: 2, y: 2, z: 4, core: 2. Of those that a mesh axis runs over, the one named last changes fastest.
Arguments:
- object_field: float32 [2, 2, 2048, 512], P(None, None, 'tile', 'grp'), may hold values from -5 to 5
- probe: float32 [2, 256, 256], replicated, may hold values from -5 to 5
- offsets: int32 [8, 8, 2], P('tile', 'grp'), may hold values from 0 to 256, as said below
- slot_range: int32 [8, 2], P('tile'), may hold values from 0 to 8, as said below
- measured: float32 [8, 8, 256, 256], P('tile', 'grp'), may hold values from 0 to 2
Outputs:
- object_grad: float32 [2, 2, 2048, 512], P(None, None, 'tile', 'grp')
- probe_grad: float32 [2, 256, 256], replicated
Inputs may be any that keep to these rules, and one draw needn't show every extreme that they name: `offsets`: the first number is a row offset within the strip, 0 to 255, and 0 for every slot of the last strip; the second is a column offset of 0 to 256. `slot_range`: for each pair of strips 2i and 2i+1 there is one b with strip 2i using slots 0 to b - 1 and strip 2i+1 using slots b to 7; other slots are empty.
All inputs are finite; a program needn't handle non-finite values.
Results may differ from a plain program's by a relative error of at most 0.00017.
Values sent between devices are 32-bit elements; how exact they have to be, the bound alone decides.
No kernel may reach another device: no remote copies, remote signals or barrier semaphores. Data moves between devices by JAX's collectives and lax.ppermute only.
A program may use at most 64 MiB of HBM per device.

v0:
```python
import math

import jax
import jax.numpy as jnp
from jax import lax
from jax.sharding import PartitionSpec as P

GRAD_WEIGHT = 0.0625


def from_behind(value, axis, steps):
    count = lax.axis_size(axis)
    leading, last = (max(0, -steps), min(count, count - steps))
    return lax.ppermute(value, axis, [(source, source + steps) for source in range(leading, last)])


def matmul(left, right):
    return jnp.dot(left, right, precision=lax.Precision.HIGHEST, preferred_element_type=jnp.float32)


def dft_tables(width, sign):
    index = jnp.arange(width, dtype=jnp.int32)
    product = index[:, None] * index[None, :] % width
    angle = 2.0 * math.pi / width * product.astype(jnp.float32)
    scale = 1.0 / math.sqrt(width)
    real_part = jnp.cos(angle) * scale
    imag_part = -sign * jnp.sin(angle) * scale
    return (real_part, real_part + imag_part, imag_part - real_part)


def fresnel_kernel(width):
    freq = jnp.arange(width, dtype=jnp.int32)
    freq = jnp.where(freq < width // 2, freq, freq - width)
    total = (freq[:, None] * freq[:, None] + freq[None, :] * freq[None, :]) % (2 * width)
    phase = -math.pi / width * total.astype(jnp.float32)
    return (jnp.cos(phase), jnp.sin(phase))


def transform(data_re, data_im, tables):
    plain, summed, differ = tables
    first = matmul(plain, data_re + data_im)
    second = matmul(summed, data_im)
    third = matmul(differ, data_re)
    mid_re = first - second
    mid_im = first + third
    first = matmul(mid_re + mid_im, plain)
    second = matmul(mid_im, summed)
    third = matmul(mid_re, differ)
    return (first - second, first + third)


def position_grad(patch, probe, target, kernel, forward, backward):
    kern_re, kern_im = kernel
    layers = patch.shape[1]
    wave_re, wave_im = (probe[0], probe[1])
    entering = []
    for layer in range(layers):
        trans_re, trans_im = (patch[0, layer], patch[1, layer])
        entering.append((wave_re, wave_im))
        exit_re = wave_re * trans_re - wave_im * trans_im
        exit_im = wave_re * trans_im + wave_im * trans_re
        if layer < layers - 1:
            spec_re, spec_im = transform(exit_re, exit_im, forward)
            spec_re, spec_im = (
                spec_re * kern_re - spec_im * kern_im,
                spec_re * kern_im + spec_im * kern_re,
            )
            wave_re, wave_im = transform(spec_re, spec_im, backward)
        else:
            far_re, far_im = transform(exit_re, exit_im, forward)
    excess = 2.0 * GRAD_WEIGHT * (far_re * far_re + far_im * far_im - target)
    back_re, back_im = transform(excess * far_re, excess * far_im, backward)
    grads = []
    for layer in reversed(range(layers)):
        trans_re, trans_im = (patch[0, layer], patch[1, layer])
        enter_re, enter_im = entering[layer]
        grads.append(
            (enter_re * back_re + enter_im * back_im, enter_re * back_im - enter_im * back_re)
        )
        up_re = trans_re * back_re + trans_im * back_im
        up_im = trans_re * back_im - trans_im * back_re
        if layer > 0:
            spec_re, spec_im = transform(up_re, up_im, forward)
            spec_re, spec_im = (
                spec_re * kern_re + spec_im * kern_im,
                spec_im * kern_re - spec_re * kern_im,
            )
            back_re, back_im = transform(spec_re, spec_im, backward)
    grads = grads[::-1]
    object_term = jnp.stack(
        [jnp.stack([pair[0] for pair in grads]), jnp.stack([pair[1] for pair in grads])]
    )
    return (object_term, jnp.stack([up_re, up_im]))


def cut_patch(extended, place_at, width):
    zero = jnp.zeros((), jnp.int32)
    start = (zero, zero, place_at[0], place_at[1])
    return lax.dynamic_slice(extended, start, (2, extended.shape[1], width, width))


def place_patch(total, piece, place_at):
    zero = jnp.zeros((), jnp.int32)
    start = (zero, zero, place_at[0], place_at[1])
    current = lax.dynamic_slice(total, start, piece.shape)
    return lax.dynamic_update_slice(total, current + piece, start)


def local(object_field, probe, offsets, slot_range, measured):
    width = probe.shape[-1]
    forward = dft_tables(width, 1.0)
    backward = dft_tables(width, -1.0)
    kernel = fresnel_kernel(width)
    strip = lax.all_gather(object_field, "grp", axis=3, tiled=True)
    below = from_behind(strip, "tile", -1)
    extended = jnp.concatenate([strip, below], axis=2)
    rows = strip.shape[2]
    per_dev = offsets.shape[1]
    slot_ids = lax.axis_index("grp") * per_dev + jnp.arange(per_dev, dtype=jnp.int32)
    used = (slot_ids >= slot_range[0, 0]) & (slot_ids < slot_range[0, 1])
    live = jnp.where(used, 1.0, 0.0).astype(jnp.float32)
    places = offsets[0]
    intensity = measured[0]
    totals = (jnp.zeros_like(extended), jnp.zeros_like(probe))

    def gradients(patch, target):
        return position_grad(patch, probe, target, kernel, forward, backward)

    def cut_one(place_at):
        return cut_patch(extended, place_at, width)

    def visit(carry, item):
        place_at, target, weight = item
        object_term, probe_term = gradients(cut_one(place_at), target)
        return (
            (place_patch(carry[0], object_term * weight, place_at), carry[1] + probe_term * weight),
            None,
        )

    (object_total, probe_local), unused = lax.scan(visit, totals, (places, intensity, live))
    own_rows = object_total[:, :, :rows]
    lower_rows = object_total[:, :, rows:]
    from_above = from_behind(lower_rows, "tile", 1)
    object_grad = lax.psum_scatter(own_rows + from_above, "grp", scatter_dimension=3, tiled=True)
    probe_grad = lax.psum(probe_local, ("tile", "grp"))
    return (object_grad, probe_grad)


def solution(mesh):
    in_specs = (
        P(None, None, "tile", "grp"),
        P(),
        P("tile", "grp", None),
        P("tile", None),
        P("tile", "grp", None, None),
    )
    out_specs = (P(None, None, "tile", "grp"), P())
    return jax.shard_map(local, mesh=mesh, in_specs=in_specs, out_specs=out_specs, check_vma=False)
```

profile of v0, /device:TPU:0, one launch (start us, length us, event | category | flops | bytes accessed | tf_op | source)
XLA Modules:
  0.0 454.3 jit_solution(3730595943811109161)
XLA Ops:
  7.9 27.2 %all-gather.2.cloned.1.call-done = f32[2,2,256,512]{3,2,1,0:T(8,128)} async-done(((f32[2,2,256,128]{3,2,1,0:T(8,128)}), f32[2,2,256,512]{3,2,1,0:T(8,128)}) %all-gather.2.cloned.1.call-update) | async-done | bytes 2097168 | tf_op jit(solution)/shard_map/all_gather | solution.py:114
  39.2 45.8 %collective-permute-done = f32[2,2,256,512]{3,2,1,0:T(8,128)S(1)} collective-permute-done((f32[2,2,256,512]{3,2,1,0:T(8,128)}, f32[2,2,256,512]{3,2,1,0:T(8,128)S(1)}, u32[]{:S(2)}, u32[]{:S(2)}) %collective-permute-start) | collective-permute-done | bytes 2097184 | tf_op jit(solution)/shard_map/ppermute | solution.py:14
  85.0 4.0 pad_maximum_fusion
  89.0 2.5 broadcast_in_dim.10
  91.5 182.3 %while.17 = (s32[]{:T(128)}, f32[2,2,512,512]{3,2,1,0:T(8,128)}, f32[2,256,256]{2,1,0:T(8,128)S(1)}, s32[2,2]{1,0:T(2,128)S(1)}, f32[2,256,256]{2,1,0:T(8,128)S(...) while((s32[]{:T(128)}, f32[2,2,512,512]{3,2,1,0:T(8,128)}, ...), condition=%wide.region_1.2_spmd.clone.clone.clone.clone, body=%wide.region_0.1_spmd.clone.clone.clone.clone.sunk | while | flops 7299727360 | bytes 46143828 | solution.py:140
  104.3 1.6 convolution_subtract_fusion.23
  105.8 1.6 convolution_add_fusion.23
  107.4 3.2 fusion.380
  110.6 2.7 convolution_add_fusion.24
  113.3 2.7 convolution_subtract_fusion.24
  119.1 3.3 multiply_add_fusion.32
  123.8 1.6 convolution_add_fusion.25
  125.4 1.6 convolution_subtract_fusion.26
  128.5 1.6 convolution_subtract_fusion.27
  130.0 1.6 fusion.384
  133.1 2.6 convolution_add_fusion.26
  140.4 3.1 add_bitcast_fusion.4
  149.6 1.6 convolution_subtract_fusion.30
  152.7 2.8 fusion.389
  155.5 2.7 convolution_add_fusion.30
  158.2 2.7 convolution_subtract_fusion.31
  163.9 3.1 add_bitcast_fusion.5
  167.1 2.4 fusion.391
  170.2 11.9 %dynamic_update_slice.9 = f32[2,2,512,512]{3,2,1,0:T(8,128)} dynamic-update-slice(f32[2,2,512,512]{3,2,1,0:T(8,128)} %get-tuple-element.562, f32[2,2,256,256]{3,2,1,0:T(8,128)S(1)} %fusion.391, s32[]{:T(128)} %constant.60.clone.1..sunk, s32[]{:T(128)} %constant.60.clone.1..sunk, s32[]{:T(128)S(6)} %select_n.419, s32[]{:T(128)S(6)} %select_n.420) | dynamic-update-slice | bytes 2097156 | tf_op jit(solution)/shard_map/while/body/eval_jaxpr/dynamic_update_slice | solution.py:106
  194.8 1.6 convolution_subtract_fusion.23
  197.9 3.0 fusion.380
  200.9 2.7 convolution_add_fusion.24
  203.6 2.7 convolution_subtract_fusion.24
  209.4 3.3 multiply_add_fusion.32
  215.7 1.6 convolution_subtract_fusion.26
  218.8 1.6 convolution_subtract_fusion.27
  220.4 1.6 fusion.384
  223.4 2.6 convolution_add_fusion.26
  230.7 3.1 add_bitcast_fusion.4
  239.9 1.6 convolution_subtract_fusion.30
  243.0 2.8 fusion.389
  245.8 2.7 convolution_add_fusion.30
  248.5 2.7 convolution_subtract_fusion.31
  254.3 3.1 add_bitcast_fusion.5
  257.4 2.4 fusion.391
  260.5 11.7 %dynamic_update_slice.9 = f32[2,2,512,512]{3,2,1,0:T(8,128)} dynamic-update-slice(f32[2,2,512,512]{3,2,1,0:T(8,128)} %get-tuple-element.562, f32[2,2,256,256]{3,2,1,0:T(8,128)S(1)} %fusion.391, s32[]{:T(128)} %constant.60.clone.1..sunk, s32[]{:T(128)} %constant.60.clone.1..sunk, s32[]{:T(128)S(6)} %select_n.419, s32[]{:T(128)S(6)} %select_n.420) | dynamic-update-slice | bytes 2097156 | tf_op jit(solution)/shard_map/while/body/eval_jaxpr/dynamic_update_slice | solution.py:106
  273.9 3.3 slice.55
  277.1 6.3 %collective-permute-start.1 = (f32[2,2,256,512]{3,2,1,0:T(8,128)}, f32[2,2,256,512]{3,2,1,0:T(8,128)}, u32[]{:S(2)}, u32[]{:S(2)}) collective-permute-start(f32[2,2,256,512]{3,2,1,0:T(8,128)} %slice.55), channel_id=1, source_target_pairs={{0,4},{4,8},{8,12},{12,16},{16,20},{20,24},{24,28},{1,5},{5,9},{9,... | collective-permute-start | bytes 6291464 | tf_op jit(solution)/shard_map/ppermute | solution.py:14
  283.6 44.4 %collective-permute-done.1 = f32[2,2,256,512]{3,2,1,0:T(8,128)} collective-permute-done((f32[2,2,256,512]{3,2,1,0:T(8,128)}, f32[2,2,256,512]{3,2,1,0:T(8,128)}, u32[]{:S(2)}, u32[]{:S(2)}) %collective-permute-start.1) | collective-permute-done | bytes 2097184 | tf_op jit(solution)/shard_map/ppermute | solution.py:14
  328.0 4.0 slice_add_fusion
  332.0 79.9 %all-reduce.2.cloned.1.call-done = f32[2,256,256]{2,1,0:T(8,128)} async-done(((f32[2,256,256]{2,1,0:T(8,128)}), f32[2,256,256]{2,1,0:T(8,128)}) %all-reduce.2.cloned.1.call-update) | async-done | bytes 524304 | tf_op jit(solution)/shard_map/psum | solution.py:145
  411.9 33.7 %reduce-scatter.2.cloned.1.call-done = f32[2,2,256,128]{3,2,1,0:T(8,128)} async-done(((f32[2,2,256,512]{3,2,1,0:T(8,128)}), f32[2,2,256,128]{3,2,1,0:T(8,128)}) %reduce-scatter.2.cloned.1.call-update) | async-done | bytes 524304 | tf_op jit(solution)/shard_map/reduce_scatter | solution.py:144
  445.6 1.9 copy.18
  (71 shorter events, 72.2 us)
Async XLA Ops:
  7.2 28.0 %all-gather.2.cloned.1.call-start = ((), (), s32[]{:S(2)}) async-start(), calls=%async_computation.1 | async-start | bytes 2621440 | tf_op jit(solution)/shard_map/all_gather | solution.py:114
  7.9 404.0 %all-reduce.2.cloned.1.call-start = ((), (), s32[]{:S(2)}) async-start(), calls=%async_computation.3 | async-start | bytes 1048576 | tf_op jit(solution)/shard_map/psum | solution.py:145
  35.1 49.9 %collective-permute-start = (f32[2,2,256,512]{3,2,1,0:T(8,128)}, f32[2,2,256,512]{3,2,1,0:T(8,128)S(1)}, u32[]{:S(2)}, u32[]{:S(2)}) collective-permute-start(f32[2,2,256,512]{3,2,1,0:T(8,128)} %all-gather.2.cloned.1.call-done), channel_id=1, source_target_pairs={{4,0},{8,4},{12,8},{16,12},{20,16},{24,20},{28,24},{5,1},{9,5},{13... | collective-permute-start | bytes 6291464 | tf_op jit(solution)/shard_map/ppermute | solution.py:14
  89.0 2.5 copy-start
  89.0 2.5 copy-start.2
  89.0 2.5 copy-start.3
  273.9 9.6 %copy-start.1 = (f32[2,256,256]{2,1,0:T(8,128)}, f32[2,256,256]{2,1,0:T(8,128)S(1)}, u32[]{:S(2)}) copy-start(f32[2,256,256]{2,1,0:T(8,128)S(1)} %get-tuple-element.228) | copy-start | bytes 1572868
  277.1 50.8 %collective-permute-start.1 = (f32[2,2,256,512]{3,2,1,0:T(8,128)}, f32[2,2,256,512]{3,2,1,0:T(8,128)}, u32[]{:S(2)}, u32[]{:S(2)}) collective-permute-start(f32[2,2,256,512]{3,2,1,0:T(8,128)} %slice.55), channel_id=1, source_target_pairs={{0,4},{4,8},{8,12},{12,16},{16,20},{20,24},{24,28},{1,5},{5,9},{9,... | collective-permute-start | bytes 6291464 | tf_op jit(solution)/shard_map/ppermute | solution.py:14
  283.5 162.1 %reduce-scatter.2.cloned.1.call-start = ((), (), s32[]{:S(2)}) async-start(), calls=%async_computation.2 | async-start | bytes 2621440 | tf_op jit(solution)/shard_map/reduce_scatter | solution.py:144
Sparse Core Ops, SparseCore 0:
  9.5 25.5 all-gather.1
  283.6 128.2 all-reduce.1
  415.2 30.4 reduce-scatter.1
where the time goes:
time: 457 us; the launch traced here: 454 us
  waiting for transfers between devices  232 us (51%)
  matrix products  137 us (30%)
  local copies, waits for them, and re-layouts  35 us (8%)
  other arithmetic  18.3 us (4%)
  between operations  14.1 us (3%)
  loops' own time  10.4 us (2%)
  starting transfers between devices  7.73 us (2%)
    dot_general x72, matrix products, matmul(): jnp.dot(left, right, precision=lax.Precision.HIGHEST, preferred_element_t...  137 us
    ppermute x2, waiting for transfers between devices, from_behind(): lax.ppermute(value, axis, [(source, source + steps) for source in range(l...  90.3 us
    psum x1, waiting for transfers between devices, local(): probe_grad = lax.psum(probe_local, ('tile', 'grp'))  79.9 us
    reduce_scatter x1, waiting for transfers between devices, local(): lax.psum_scatter(own_rows + from_above, 'grp', scatter_dimension=3, tiled...  33.7 us
    all_gather x1, waiting for transfers between devices, local(): strip = lax.all_gather(object_field, 'grp', axis=3, tiled=True)  27.2 us
    dynamic_update_slice x2, local copies, waits for them, and re-layouts, place_patch(): return lax.dynamic_update_slice(total, current + piece, start)  23.6 us
    another operation x1, loops' own time, local(): lax.scan(visit, totals, (places, intensity, live))  10.4 us
  transfers between devices with their start and end apart: 5, of which 5 were waited for; matrix products, arithmetic and copies ran while one was open for 1% of the time, Pallas kernels for 0%

commit v1 on v0

v1 whole, which is shorter than its diff:
```python
import functools
import math

import jax
import jax.numpy as jnp
import ml_dtypes
import numpy as np
from jax import lax
from jax.experimental import pallas as pl
from jax.experimental.pallas import tpu as pltpu
from jax.sharding import Mesh, PartitionSpec as P

GRAD_WEIGHT = 0.0625
PLANE = ("half", "col", "core")
VMEM_LIMIT = 48 * 1024 * 1024


def split_bf16(table):
    high = table.astype(ml_dtypes.bfloat16)
    low = (table - high.astype(np.float64)).astype(ml_dtypes.bfloat16)
    return high, low


def tables(width):
    index = np.arange(width, dtype=np.int64)
    scale = 1.0 / math.sqrt(width)
    phase = -2.0 * math.pi / width * (index[:, None] * index[None, :] % width)
    shift = index[:, None] - index[None, :]
    chirp = math.pi / width * (shift * shift % (2 * width)) - math.pi / 4.0
    out = []
    for angle in (phase, chirp):
        real, imag = np.cos(angle) * scale, np.sin(angle) * scale
        for axis in (0, 1):
            out.extend(split_bf16(np.concatenate([real, imag], axis=axis)))
    return out


def split(value):
    high = value.astype(jnp.bfloat16)
    low = (value - high.astype(jnp.float32)).astype(jnp.bfloat16)
    return high, low


def dot(left, right):
    return jnp.dot(left, right, preferred_element_type=jnp.float32)


def times_right(re, im, high, low, conj):
    width = re.shape[0]
    sign = 1.0 if conj else -1.0
    left = jnp.concatenate(
        [jnp.concatenate([re, sign * im], 1), jnp.concatenate([im, -sign * re], 1)], 0
    )
    left_high, left_low = split(left)
    out = dot(left_high, high) + dot(left_low, high) + dot(left_high, low)
    return out[:width], out[width:]


def times_left(re, im, high, low, conj):
    width = re.shape[0]
    sign = 1.0 if conj else -1.0
    right = jnp.concatenate(
        [jnp.concatenate([re, im], 1), jnp.concatenate([sign * im, -sign * re], 1)], 0
    )
    right_high, right_low = split(right)
    out = dot(high, right_high) + dot(high, right_low) + dot(low, right_high)
    return out[:, :width], out[:, width:]


def transform(re, im, tabs, conj):
    right_high, right_low, left_high, left_low = (tab[...] for tab in tabs)
    re, im = times_right(re, im, right_high, right_low, conj)
    return times_left(re, im, left_high, left_low, conj)


def position_kernel(
    place, patch, probe, meas, fr_h, fr_l, fl_h, fl_l, cr_h, cr_l, cl_h, cl_l, grad, probe_grad
):
    far_tabs = (fr_h, fr_l, fl_h, fl_l)
    near_tabs = (cr_h, cr_l, cl_h, cl_l)
    row, col, mine = place[0], place[1], place[2]
    width = probe.shape[-1]

    def load(plane):
        return jnp.concatenate([patch[plane, 0], patch[plane, 1]], axis=1)

    def store(plane, value):
        half = width // 2
        grad[plane, 0] = value[:, :half]
        grad[plane, 1] = value[:, half:]

    def roll(value, rows, cols):
        return pltpu.roll(pltpu.roll(value, rows, 0), cols, 1)

    wave_re, wave_im = roll(probe[0], row, col), roll(probe[1], row, col)
    o0_re, o0_im, o1_re, o1_im = load(0), load(2), load(1), load(3)
    exit_re = wave_re * o0_re - wave_im * o0_im
    exit_im = wave_re * o0_im + wave_im * o0_re
    mid_re, mid_im = transform(exit_re, exit_im, near_tabs, False)
    exit_re = mid_re * o1_re - mid_im * o1_im
    exit_im = mid_re * o1_im + mid_im * o1_re
    far_re, far_im = transform(exit_re, exit_im, far_tabs, False)
    target = jnp.where(mine == 1, meas[0], meas[1])
    excess = 2.0 * GRAD_WEIGHT * (far_re * far_re + far_im * far_im - target)
    back_re, back_im = transform(excess * far_re, excess * far_im, far_tabs, True)
    store(1, mid_re * back_re + mid_im * back_im)
    store(3, mid_re * back_im - mid_im * back_re)
    up_re = o1_re * back_re + o1_im * back_im
    up_im = o1_re * back_im - o1_im * back_re
    back_re, back_im = transform(up_re, up_im, near_tabs, True)
    wave_re, wave_im = roll(probe[0], row, col), roll(probe[1], row, col)
    o0_re, o0_im = load(0), load(2)
    store(0, wave_re * back_re + wave_im * back_im)
    store(2, wave_re * back_im - wave_im * back_re)
    up_re = o0_re * back_re + o0_im * back_im
    up_im = o0_re * back_im - o0_im * back_re
    back_row, back_col = lax.rem(width - row, width), lax.rem(2 * width - col, width)
    probe_grad[0] = roll(up_re, back_row, back_col)
    probe_grad[1] = roll(up_im, back_row, back_col)


def receivers():
    return [2 * (2 * col + core) + half for half in range(2) for col in range(2) for core in range(2)]


def pick_kernel(info, where, own, below, out):
    rows, cols = out.shape[1], out.shape[2]
    row_ids = lax.broadcasted_iota(jnp.int32, (rows, cols), 0)
    col_ids = lax.broadcasted_iota(jnp.int32, (rows, cols), 1) + where[0] * cols
    for place, slot in enumerate(receivers()):
        lower, row, col = info[slot, 0], info[slot, 1], info[slot, 2]
        upper_rows = row_ids >= row
        left_cols = col_ids >= col

        def merged(half, lower=lower, upper_rows=upper_rows):
            second = own[1, half]
            top = jnp.where(lower == 1, second, own[0, half])
            bottom = jnp.where(lower == 1, below[half], second)
            return jnp.where(upper_rows, top, bottom)

        out[place] = jnp.where(left_cols, merged(0), merged(1))


def add_kernel(info, where, parts, own, below):
    rows, cols = parts.shape[1], parts.shape[2]
    row_ids = lax.broadcasted_iota(jnp.int32, (rows, cols), 0)
    col_ids = lax.broadcasted_iota(jnp.int32, (rows, cols), 1) + where[0] * cols
    slots = receivers()
    for strip in range(3):
        sums = [jnp.zeros((rows, cols), jnp.float32)] * 2
        for place, slot in enumerate(slots):
            lower, row, col = info[slot, 0], info[slot, 1], info[slot, 2]
            first = jnp.where(strip == lower, row, jnp.where(strip == lower + 1, 0, rows))
            last = jnp.where(strip == lower, rows, jnp.where(strip == lower + 1, row, 0))
            part = jnp.where((row_ids >= first) & (row_ids < last), parts[place], 0.0)
            left = jnp.where(col_ids >= col, part, 0.0)
            sums = [sums[0] + left, sums[1] + (part - left)]
        for half in range(2):
            if strip < 2:
                own[strip, half] = sums[half]
            else:
                below[half] = sums[half]


SMEM = pl.BlockSpec(memory_space=pltpu.SMEM)
VMEM = pl.BlockSpec(memory_space=pltpu.VMEM)


def call(kernel, out_shape, scalars, arrays, flops, **kwargs):
    outs = out_shape if isinstance(out_shape, (list, tuple)) else [out_shape]
    moved = sum(math.prod(x.shape) * x.dtype.itemsize for x in [*arrays, *outs])
    return pl.pallas_call(
        kernel,
        out_shape=out_shape,
        in_specs=[SMEM] * len(scalars) + [VMEM] * len(arrays),
        out_specs=jax.tree.map(lambda unused: VMEM, out_shape),
        compiler_params=pltpu.CompilerParams(vmem_limit_bytes=VMEM_LIMIT),
        cost_estimate=pl.CostEstimate(flops=flops, bytes_accessed=moved, transcendentals=0),
        **kwargs,
    )(*scalars, *arrays)


def shape(*dims):
    return jax.ShapeDtypeStruct(dims, jnp.float32)


def local(object_field, probe, offsets, slot_range, measured):
    width = probe.shape[-1]
    planes, rows, cols = 4, object_field.shape[2], object_field.shape[3]
    pairs = lax.axis_size("pair")
    half, core = lax.axis_index("half"), lax.axis_index("core")

    places = lax.all_gather(offsets[0], PLANE, axis=0, tiled=False)
    places = places.reshape(2, -1, offsets.shape[2])
    split_at = jnp.where(half == 0, slot_range[0, 1], slot_range[0, 0])
    slots = jnp.arange(places.shape[1], dtype=jnp.int32)
    lower = (slots >= split_at).astype(jnp.int32)
    place = jnp.where(lower[:, None] == 1, places[1], places[0])
    info = jnp.concatenate([lower[:, None], place], axis=1)
    where = core[None]
    my_slot = 2 * (2 * lax.axis_index("col") + core) + half
    my_info = lax.dynamic_slice_in_dim(info, my_slot, 1, 0)[0]
    mine = (my_info[0] == half).astype(jnp.int32)
    my_place = jnp.stack([my_info[1], my_info[2], mine])

    kept = lax.dynamic_index_in_dim(measured[0], half, 0, keepdims=False)
    given = lax.dynamic_index_in_dim(measured[0], 1 - half, 0, keepdims=False)
    taken = lax.ppermute(given, "half", [(0, 1), (1, 0)])
    meas = jnp.stack([kept, taken])

    block = object_field.reshape(planes, rows, cols)
    own = lax.all_to_all(block, ("half", "col"), 0, 0, tiled=True).reshape(2, 2, rows, cols)
    below = lax.ppermute(own[0], "pair", [(k, k - 1) for k in range(1, pairs)])
    parts = call(pick_kernel, shape(8, rows, cols), (info, where), (own, below), 8 * rows * cols)
    patch = lax.all_to_all(parts, PLANE, 0, 0, tiled=True).reshape(planes, 2, rows, cols)

    tabs = [jnp.asarray(tab) for tab in tables(width)]
    far_right, near_right = tabs[0:2], tabs[4:6]
    far_left, near_left = tabs[2:4], tabs[6:8]
    order = [*far_right, *far_left, *near_right, *near_left]
    grad, probe_part = call(
        position_kernel,
        [shape(planes, 2, rows, cols), shape(2, width, width)],
        (my_place,),
        (patch, probe, meas, *order),
        8 * 24 * width**3,
    )

    got = lax.all_to_all(grad.reshape(8, rows, cols), PLANE, 0, 0, tiled=True)
    sums, lower_sums = call(
        add_kernel,
        [shape(2, 2, rows, cols), shape(2, rows, cols)],
        (info, where),
        (got,),
        48 * rows * cols,
    )
    above = lax.ppermute(lower_sums, "pair", [(k, k + 1) for k in range(pairs - 1)])
    total = jnp.stack([sums[0] + above, sums[1]])
    mine_out = lax.all_to_all(total.reshape(4, rows, cols), ("half", "col"), 0, 0, tiled=True)
    object_grad = mine_out.reshape(object_field.shape)

    band = lax.psum_scatter(probe_part, PLANE, scatter_dimension=1, tiled=True)
    band = lax.psum(band, "pair")
    probe_grad = lax.all_gather(band, PLANE, axis=1, tiled=True)
    return (object_grad, probe_grad)


def solution(mesh):
    tile, grp = mesh.shape["tile"], mesh.shape["grp"]
    devices = mesh.devices.reshape(tile // 2, 2, 2, grp // 2)
    inner = Mesh(devices, ("pair", "half", "col", "core"))
    strip, cols = ("pair", "half"), ("col", "core")
    in_specs = (
        P(None, None, strip, cols),
        P(),
        P(strip, cols, None),
        P(strip, None),
        P(strip, cols, None, None),
    )
    out_specs = (P(None, None, strip, cols), P())
    return jax.shard_map(local, mesh=inner, in_specs=in_specs, out_specs=out_specs, check_vma=False)
```

time: 457 us -> 186 us (0.41)
  waiting for transfers between devices: 232 us -> 87.4 us
  matrix products: 137 us -> 0 us
  blocking collectives: 0 us -> 38 us
  local copies, waits for them, and re-layouts: 35 us -> 8.59 us
  other arithmetic: 18.3 us -> 3.45 us
  Pallas kernels: 0 us -> 12.7 us
  starting transfers between devices: 7.73 us -> 19.6 us
  loops' own time: 10.4 us -> 0 us
    dot_general x72 -> x0, matrix products: 137 us -> none  [matmul(): jnp.dot(left, right, precision=lax.Precision.HIGHEST, preferred_element_t...]
    ppermute x2 -> x3, waiting for transfers between devices: 90.3 us -> 28.6 us  [the longest x1 14.8 us: local(): taken = lax.ppermute(given, 'half', [(0, 1), (1, 0)])]
    psum x1, waiting for transfers between devices: 79.9 us -> 36.4 us  [local(): band = lax.psum(band, 'pair')]
    all_gather x1 -> x0, waiting for transfers between devices: 27.2 us -> none  [local(): strip = lax.all_gather(object_field, 'grp', axis=3, tiled=True)]
    dynamic_update_slice x2 -> x0, local copies, waits for them, and re-layouts: 23.6 us -> none  [place_patch(): return lax.dynamic_update_slice(total, current + piece, start)]
    all_gather x0 -> x2, blocking collectives: none -> 20.1 us  [the longest x1 10.1 us: local(): probe_grad = lax.all_gather(band, PLANE, axis=1, tiled=True)]
    all_to_all x0 -> x1, blocking collectives: none -> 17.9 us  [local(): got = lax.all_to_all(grad.reshape(8, rows, cols), PLANE, 0, 0, tiled=True)]
    add x7 -> x0, other arithmetic: 12.8 us -> none  [the longest x2 4.72 us: place_patch(): return lax.dynamic_update_slice(total, current + piece, start)]
  transfers between devices with their start and end apart: 5 -> 8, of which waited for: 5 -> 5; matrix products, arithmetic and copies ran while one was open for 1% -> 3% of each run, Pallas kernels for 0% -> 0%
where the time goes in v1:
time: 186 us
  waiting for transfers between devices  87.4 us (47%)
  blocking collectives  38 us (20%)
  starting transfers between devices  19.6 us (11%)
  between operations  16.1 us (9%)
  Pallas kernels  12.7 us (7%)
  local copies, waits for them, and re-layouts  8.59 us (5%)
  other arithmetic  3.45 us (2%)
    psum x1, waiting for transfers between devices, local(): band = lax.psum(band, 'pair')  36.4 us
    reduce_scatter x1, waiting for transfers between devices, local(): band = lax.psum_scatter(probe_part, PLANE, scatter_dimension=1, tiled=True)  22.3 us
    all_to_all x1, blocking collectives, local(): got = lax.all_to_all(grad.reshape(8, rows, cols), PLANE, 0, 0, tiled=True)  17.9 us
    ppermute x1, waiting for transfers between devices, local(): taken = lax.ppermute(given, 'half', [(0, 1), (1, 0)])  14.8 us
    pallas_call x3, Pallas kernels, call(): pl.pallas_call(kernel, out_shape=out_shape, in_specs=[SMEM] * len(scalars...  12.7 us
    all_gather x1, blocking collectives, local(): probe_grad = lax.all_gather(band, PLANE, axis=1, tiled=True)  10.1 us
    all_gather x1, blocking collectives, local(): places = lax.all_gather(offsets[0], PLANE, axis=0, tiled=False)  10.1 us
    ppermute x1, waiting for transfers between devices, local(): below = lax.ppermute(own[0], 'pair', [(k, k - 1) for k in range(1, pairs)])  8.97 us
  transfers between devices with their start and end apart: 8, of which 5 were waited for; matrix products, arithmetic and copies ran while one was open for 3% of the time, Pallas kernels for 0%

profile of v1, /device:TPU:0, one launch (start us, length us, event | category | flops | bytes accessed | tf_op | source)
XLA Modules:
  0.0 185.8 jit_solution(3543802133364992617)
XLA Ops:
  7.2 5.2 %all-to-all-start = ((f32[4,256,128]{2,1,0:T(8,128)}), f32[4,256,128]{2,1,0:T(8,128)S(1)}, u32[]{:S(2)}, u32[]{:S(2)}) async-start(f32[4,256,128]{2,1,0:T(8,128)} %bitcast.30), calls=%async_computation | async-start | bytes 1048576 | tf_op jit(solution)/shard_map/all_to_all | solution.py:212
  12.3 0.7 copy-done.12
  13.0 10.1 %all_gather.6 = s32[8,2,2]{2,1,0:T(2,128)S(1)} all-gather(s32[1,2,2]{2,1,0:T(2,128)S(1)} %copy-done.12), channel_id=1, replica_groups=mesh['pair'=4,'half'=2,'col'=2,'core'=2] {'half','col','core'}, dimensions={0}, use_global_device_ids=true | all-gather | bytes 144 | tf_op jit(solution)/shard_map/all_gather | solution.py:193
  23.1 0.7 copy-done.11
  23.7 0.6 fusion.5
  25.6 0.0 all-to-all-done
  25.7 1.3 collective-permute-start
  27.0 0.1 broadcast_select_fusion
  27.1 0.1 pad_add_fusion.info
  27.1 9.0 %collective-permute-done.below = f32[2,256,128]{2,1,0:T(8,128)S(1)} collective-permute-done((f32[2,256,128]{2,1,0:T(8,128)S(1)}, f32[2,256,128]{2,1,0:T(8,128)S(1)}, u32[]{:S(2)}, u32[]{:S(2)}) %collective-permute-start) | collective-permute-done | bytes 262176 | tf_op jit(solution)/shard_map/ppermute | solution.py:213
  36.1 2.0 %shard_map.140 = f32[8,256,128]{2,1,0:T(8,128)} custom-call(s32[8,3]{1,0:T(8,128)S(1)} %pad_add_fusion.info, s32[1]{0:T(128)} %bitcast.4.where, f32[2,2,256,128]{3,2,1,0:T(8,128)S(1)} %bitcast.26, f32[2,256,128]{2,1,0:T(8,128)S(1)} %collective-permute-done.below), custom_call_target="tpu_custom_call" | custom-call | flops 262144 | bytes 1835008 | tf_op jit(solution)/shard_map/pallas_call | solution.py:172
  38.1 4.1 %all-to-all-start.1 = ((f32[8,256,128]{2,1,0:T(8,128)}), f32[8,256,128]{2,1,0:T(8,128)S(1)}, u32[]{:S(2)}, u32[]{:S(2)}) async-start(f32[8,256,128]{2,1,0:T(8,128)} %shard_map.140), calls=%async_computation.1 | async-start | bytes 2097152 | tf_op jit(solution)/shard_map/all_to_all | solution.py:215
  42.1 0.0 reduce-scatter.2.cloned.1.call-start
  42.2 0.0 copy-done.9
  42.2 0.0 copy-start.3
  42.2 0.0 copy-start.4
  42.2 0.0 copy-start.5
  42.2 0.7 dynamic-slice_bitcast_fusion.1
  43.0 2.0 %collective-permute-start.1 = (f32[256,256]{1,0:T(8,128)S(1)}, f32[256,256]{1,0:T(8,128)S(1)}, u32[]{:S(2)}, u32[]{:S(2)}) collective-permute-start(f32[256,256]{1,0:T(8,128)S(1)} %get-tuple-element.11), channel_id=1, source_target_pairs={{0,4},{4,0},{1,5},{5,1},{2,6},{6,2},{3,7},{7,3},{8,12},{12,8},{9,1... | collective-permute-start | bytes 786440 | tf_op jit(solution)/shard_map/ppermute | solution.py:208
  45.0 0.6 fusion.4
  46.1 1.3 pad_add_fusion.1.place
  47.4 14.8 %collective-permute-done.1 = f32[256,256]{1,0:T(8,128)S(1)} collective-permute-done((f32[256,256]{1,0:T(8,128)S(1)}, f32[256,256]{1,0:T(8,128)S(1)}, u32[]{:S(2)}, u32[]{:S(2)}) %collective-permute-start.1) | collective-permute-done | bytes 262176 | tf_op jit(solution)/shard_map/ppermute | solution.py:208
  62.2 0.7 copy-done.10
  62.9 1.2 pad_maximum_fusion.meas
  64.1 0.0 all-to-all-done.1
  64.1 0.0 copy-done.3
  64.1 0.0 copy-done.4
  64.1 0.1 copy-done.1
  64.2 0.1 copy-done.2
  64.3 0.9 copy-done.6
  65.2 0.9 copy-done.7
  66.2 0.9 copy-done.8
  67.1 9.1 %shard_map.141 = (f32[4,2,256,128]{3,2,1,0:T(8,128)S(1)}, f32[2,256,256]{2,1,0:T(8,128)}) custom-call(s32[3]{0:T(128)S(1)} %pad_add_fusion.1.place, f32[4,2,256,128]{3,2,1,0:T(8,128)S(1)} %bitcast.27, f32[2,256,256]{2,1,0:T(8,128)S(1)} %copy-done, f32[2,256,256]{2,1,0:T(8,128)S(1)} %pad_maximum_fusion.meas, bf16[512,256]{1,0:T(8,128)(2,1)S(1)} %copy-done.8, ...), custom_call_target="tpu_custom_call" | custom-call | flops 3221225472 | bytes 5767168 | tf_op jit(solution)/shard_map/pallas_call | solution.py:172
  76.2 17.9 %all_to_all.20.parts = f32[8,256,128]{2,1,0:T(8,128)S(1)} all-to-all(f32[8,256,128]{2,1,0:T(8,128)S(1)} %bitcast.28), channel_id=1, replica_groups=mesh['pair'=4,'half'=2,'col'=2,'core'=2] {'half','col','core'}, dimensions={0} | all-to-all | bytes 2097152 | tf_op jit(solution)/shard_map/all_to_all | solution.py:229
  94.1 1.7 shard_map.142
  95.8 3.5 %collective-permute-start.2 = (f32[2,256,128]{2,1,0:T(8,128)S(1)}, f32[2,256,128]{2,1,0:T(8,128)S(1)}, u32[]{:S(2)}, u32[]{:S(2)}) collective-permute-start(f32[2,256,128]{2,1,0:T(8,128)S(1)} %get-tuple-element.8), channel_id=1, source_target_pairs={{0,8},{8,16},{16,24},{1,9},{9,17},{17,25},{2,10},{10,18},{18,26},{... | collective-permute-start | bytes 786440 | tf_op jit(solution)/shard_map/ppermute | solution.py:237
  99.3 0.0 reduce-scatter.2.cloned.1.call-update
  99.3 4.8 %collective-permute-done.2 = f32[2,256,128]{2,1,0:T(8,128)S(1)} collective-permute-done((f32[2,256,128]{2,1,0:T(8,128)S(1)}, f32[2,256,128]{2,1,0:T(8,128)S(1)}, u32[]{:S(2)}, u32[]{:S(2)}) %collective-permute-start.2) | collective-permute-done | bytes 262176 | tf_op jit(solution)/shard_map/ppermute | solution.py:237
  104.2 0.8 pad_maximum_fusion.1
  105.0 3.5 %all-to-all-start.3 = ((f32[4,256,128]{2,1,0:T(8,128)}), f32[4,256,128]{2,1,0:T(8,128)S(1)}, u32[]{:S(2)}, u32[]{:S(2)}) async-start(f32[4,256,128]{2,1,0:T(8,128)} %bitcast.18), calls=%async_computation.3 | async-start | bytes 1048576 | tf_op jit(solution)/shard_map/all_to_all | solution.py:239
  108.5 0.0 all-reduce.2.cloned.1.call-start
  108.6 22.3 %reduce-scatter.2.cloned.1.call-done = f32[2,32,256]{2,1,0:T(8,128)} async-done(((f32[2,256,256]{2,1,0:T(8,128)}), f32[2,32,256]{2,1,0:T(8,128)}) %reduce-scatter.2.cloned.1.call-update) | async-done | bytes 65552 | tf_op jit(solution)/shard_map/reduce_scatter | solution.py:242
  130.9 0.0 all-reduce.2.cloned.1.call-update
  130.9 36.4 %all-reduce.2.cloned.1.call-done = f32[2,32,256]{2,1,0:T(8,128)} async-done(((f32[2,32,256]{2,1,0:T(8,128)}), f32[2,32,256]{2,1,0:T(8,128)}) %all-reduce.2.cloned.1.call-update) | async-done | bytes 65552 | tf_op jit(solution)/shard_map/psum | solution.py:243
  167.3 10.1 %all_gather.7 = f32[2,256,256]{2,1,0:T(8,128)S(1)} all-gather(f32[2,32,256]{2,1,0:T(8,128)} %all-reduce.2.cloned.1.call-done), channel_id=1, replica_groups=mesh['pair'=4,'half'=2,'col'=2,'core'=2] {'half','col','core'}, dimensions={1}, use_global_device_ids=true | all-gather | bytes 589824 | tf_op jit(solution)/shard_map/all_gather | solution.py:244
  177.4 0.0 all-to-all-done.3
  177.4 0.8 copy.32
  178.2 0.8 copy.33
  (19 shorter events, 0.1 us)
Async XLA Ops:
  7.2 18.5 %all-to-all-start = ((f32[4,256,128]{2,1,0:T(8,128)}), f32[4,256,128]{2,1,0:T(8,128)S(1)}, u32[]{:S(2)}, u32[]{:S(2)}) async-start(f32[4,256,128]{2,1,0:T(8,128)} %bitcast.30), calls=%async_computation | async-start | bytes 1048576 | tf_op jit(solution)/shard_map/all_to_all | solution.py:212
  12.3 0.7 copy-start.12
  23.1 0.7 copy-start.11
  25.7 10.4 %collective-permute-start = (f32[2,256,128]{2,1,0:T(8,128)S(1)}, f32[2,256,128]{2,1,0:T(8,128)S(1)}, u32[]{:S(2)}, u32[]{:S(2)}) collective-permute-start(f32[2,256,128]{2,1,0:T(8,128)S(1)} %slice.54), channel_id=1, source_target_pairs={{8,0},{16,8},{24,16},{9,1},{17,9},{25,17},{10,2},{18,10},{26,18},{... | collective-permute-start | bytes 786440 | tf_op jit(solution)/shard_map/ppermute | solution.py:213
  38.1 4.1 %copy-start.9 = (f32[1,2,256,256]{3,2,1,0:T(8,128)S(1)}, f32[1,2,256,256]{3,2,1,0:T(8,128)}, u32[]{:S(2)}) copy-start(f32[1,2,256,256]{3,2,1,0:T(8,128)} %param.17) | copy-start | bytes 1572868
  38.1 26.0 %all-to-all-start.1 = ((f32[8,256,128]{2,1,0:T(8,128)}), f32[8,256,128]{2,1,0:T(8,128)S(1)}, u32[]{:S(2)}, u32[]{:S(2)}) async-start(f32[8,256,128]{2,1,0:T(8,128)} %shard_map.140), calls=%async_computation.1 | async-start | bytes 2097152 | tf_op jit(solution)/shard_map/all_to_all | solution.py:215
  42.1 88.8 %reduce-scatter.2.cloned.1.call-start = ((), (), s32[]{:S(2)}) async-start(), calls=%async_computation.5 | async-start | bytes 589824 | tf_op jit(solution)/shard_map/reduce_scatter | solution.py:242
  42.2 21.9 %copy-start.3 = (bf16[512,256]{1,0:T(8,128)(2,1)S(1)}, bf16[512,256]{1,0:T(8,128)(2,1)}, u32[]{:S(2)}) copy-start(bf16[512,256]{1,0:T(8,128)(2,1)} %constant.50.clone.cr_l) | copy-start | bytes 786436
  42.2 21.9 %copy-start.4 = (bf16[512,256]{1,0:T(8,128)(2,1)S(1)}, bf16[512,256]{1,0:T(8,128)(2,1)}, u32[]{:S(2)}) copy-start(bf16[512,256]{1,0:T(8,128)(2,1)} %constant.49.clone.cr_h) | copy-start | bytes 786436
  42.2 21.9 %copy-start.5 = (bf16[256,512]{1,0:T(8,128)(2,1)S(1)}, bf16[256,512]{1,0:T(8,128)(2,1)}, u32[]{:S(2)}) copy-start(bf16[256,512]{1,0:T(8,128)(2,1)} %constant.48.clone.fl_l) | copy-start | bytes 786436
  43.0 19.2 %collective-permute-start.1 = (f32[256,256]{1,0:T(8,128)S(1)}, f32[256,256]{1,0:T(8,128)S(1)}, u32[]{:S(2)}, u32[]{:S(2)}) collective-permute-start(f32[256,256]{1,0:T(8,128)S(1)} %get-tuple-element.11), channel_id=1, source_target_pairs={{0,4},{4,0},{1,5},{5,1},{2,6},{6,2},{3,7},{7,3},{8,12},{12,8},{9,1... | collective-permute-start | bytes 786440 | tf_op jit(solution)/shard_map/ppermute | solution.py:208
  62.2 0.7 copy-start.10
  62.9 1.2 copy-start
  62.9 1.3 copy-start.1
  62.9 1.3 copy-start.2
  64.3 0.9 copy-start.6
  65.2 0.9 copy-start.7
  66.2 0.9 copy-start.8
  95.8 8.4 %collective-permute-start.2 = (f32[2,256,128]{2,1,0:T(8,128)S(1)}, f32[2,256,128]{2,1,0:T(8,128)S(1)}, u32[]{:S(2)}, u32[]{:S(2)}) collective-permute-start(f32[2,256,128]{2,1,0:T(8,128)S(1)} %get-tuple-element.8), channel_id=1, source_target_pairs={{0,8},{8,16},{16,24},{1,9},{9,17},{17,25},{2,10},{10,18},{18,26},{... | collective-permute-start | bytes 786440 | tf_op jit(solution)/shard_map/ppermute | solution.py:237
  105.0 72.4 %all-to-all-start.3 = ((f32[4,256,128]{2,1,0:T(8,128)}), f32[4,256,128]{2,1,0:T(8,128)S(1)}, u32[]{:S(2)}, u32[]{:S(2)}) async-start(f32[4,256,128]{2,1,0:T(8,128)} %bitcast.18), calls=%async_computation.3 | async-start | bytes 1048576 | tf_op jit(solution)/shard_map/all_to_all | solution.py:239
  108.5 58.8 %all-reduce.2.cloned.1.call-start = ((), (), s32[]{:S(2)}) async-start(), calls=%async_computation.6 | async-start | bytes 131072 | tf_op jit(solution)/shard_map/psum | solution.py:243
Sparse Core Ops, SparseCore 0:
  99.4 31.4 reduce-scatter.1
  133.3 33.9 all-reduce.1

commit v2 on v1

v2 whole, which is shorter than its diff:
```python
import functools
import math

import jax
import jax.numpy as jnp
import ml_dtypes
import numpy as np
from jax import lax
from jax.experimental import pallas as pl
from jax.experimental.pallas import tpu as pltpu
from jax.sharding import Mesh, PartitionSpec as P

GRAD_WEIGHT = 0.0625
PLANE = ("half", "col", "core")
VMEM_LIMIT = 48 * 1024 * 1024


def tables(width):
    index = np.arange(width, dtype=np.int64)
    scale = 1.0 / math.sqrt(width)
    phase = -2.0 * math.pi / width * (index[:, None] * index[None, :] % width)
    shift = index[:, None] - index[None, :]
    chirp = math.pi / width * (shift * shift % (2 * width)) - math.pi / 4.0
    out = []
    for angle in (phase, chirp):
        table = np.concatenate([np.cos(angle) * scale, np.sin(angle) * scale], axis=0)
        high = table.astype(ml_dtypes.bfloat16)
        low = (table - high.astype(np.float64)).astype(ml_dtypes.bfloat16)
        out.extend([high, low])
    return out


def split(value):
    high = value.astype(jnp.bfloat16)
    low = (value - high.astype(jnp.float32)).astype(jnp.bfloat16)
    return high, low


def dot(left, right):
    return jnp.dot(left, right, preferred_element_type=jnp.float32)


def parts_of(re, im, conj):
    sign = 1.0 if conj else -1.0
    re_high, re_low = split(re)
    im_high, im_low = split(im)
    return (re_high, im_high, sign * im_high, -sign * re_high), (re_low, im_low, sign * im_low, -sign * re_low)


def times_right(re, im, high, low, conj):
    width = re.shape[0]

    def stack(part):
        return jnp.concatenate(
            [jnp.concatenate([part[0], part[2]], 1), jnp.concatenate([part[1], part[3]], 1)], 0
        )

    left_high, left_low = (stack(part) for part in parts_of(re, im, conj))
    out = dot(left_high, high[...]) + dot(left_low, high[...]) + dot(left_high, low[...])
    return out[:width], out[width:]


def times_left(re, im, high, low, conj):
    width = re.shape[0]
    part_high, part_low = parts_of(re, im, conj)

    def product(table, part):
        plain = dot(table[:width], jnp.concatenate(part[:2], 1))
        return plain + dot(table[width:], jnp.concatenate(part[2:], 1))

    out = product(high, part_high) + product(high, part_low) + product(low, part_high)
    return out[:, :width], out[:, width:]


def transform(re, im, tabs, conj):
    re, im = times_right(re, im, *tabs, conj)
    return times_left(re, im, *tabs, conj)


def slot_place(offs, split_at, flat, slot):
    lower = jnp.where(slot >= split_at, 1, 0)
    holder = jnp.bitwise_xor(4 * lower + slot // 2, flat)
    at = 2 * (slot % 2)
    return lower, offs[holder, at], offs[holder, at + 1]


def slot_of(half, col, core):
    return 2 * (2 * col + core) + half


def receivers():
    return [slot_of(half, col, core) for half in range(2) for col in range(2) for core in range(2)]


def position_kernel(
    where, slot_range, offs, patch, probe, measured, taken, far_high, far_low, near_high, near_low, grad
):
    far_tabs, near_tabs = (far_high, far_low), (near_high, near_low)
    half, col, core = where[0], where[1], where[2]
    split_at = slot_range[0, 1 - half]
    lower, row_at, col_at = slot_place(offs, split_at, 4 * half + 2 * col + core, slot_of(half, col, core))
    width = probe.shape[-1]
    lanes = width // 2

    def load(plane):
        return jnp.concatenate([patch[2 * plane], patch[2 * plane + 1]], axis=1)

    def store(plane, value):
        grad[2 * plane, :width] = value[:, :lanes]
        grad[2 * plane + 1, :width] = value[:, lanes:]

    def roll(value, rows, cols):
        return pltpu.roll(pltpu.roll(value, rows, 0), cols, 1)

    wave_re, wave_im = roll(probe[0], row_at, col_at), roll(probe[1], row_at, col_at)
    o0_re, o0_im, o1_re, o1_im = load(0), load(2), load(1), load(3)
    exit_re = wave_re * o0_re - wave_im * o0_im
    exit_im = wave_re * o0_im + wave_im * o0_re
    mid_re, mid_im = transform(exit_re, exit_im, near_tabs, False)
    exit_re = mid_re * o1_re - mid_im * o1_im
    exit_im = mid_re * o1_im + mid_im * o1_re
    far_re, far_im = transform(exit_re, exit_im, far_tabs, False)
    target = jnp.where(lower == half, measured[0, half], taken[...])
    excess = 2.0 * GRAD_WEIGHT * (far_re * far_re + far_im * far_im - target)
    back_re, back_im = transform(excess * far_re, excess * far_im, far_tabs, True)
    store(1, mid_re * back_re + mid_im * back_im)
    store(3, mid_re * back_im - mid_im * back_re)
    up_re = o1_re * back_re + o1_im * back_im
    up_im = o1_re * back_im - o1_im * back_re
    back_re, back_im = transform(up_re, up_im, near_tabs, True)
    wave_re, wave_im = roll(probe[0], row_at, col_at), roll(probe[1], row_at, col_at)
    o0_re, o0_im = load(0), load(2)
    store(0, wave_re * back_re + wave_im * back_im)
    store(2, wave_re * back_im - wave_im * back_re)
    up_re = o0_re * back_re + o0_im * back_im
    up_im = o0_re * back_im - o0_im * back_re
    back_row, back_col = lax.rem(width - row_at, width), lax.rem(2 * width - col_at, width)
    band = 2 * width // 8
    for part, value in enumerate((up_re, up_im)):
        value = roll(value, back_row, back_col)
        for step in range(4):
            rows = value[step * band : (step + 1) * band]
            grad[4 * part + step, width : width + band] = rows[:, :lanes]
            grad[4 * part + step, width + band :] = rows[:, lanes:]


def pick_kernel(where, slot_range, offs, own, below00, below01, below10, below11, out):
    rows, cols = out.shape[1], out.shape[2]
    half, col, core = where[0], where[1], where[2]
    flat = 4 * half + 2 * col + core
    split_at = slot_range[0, 1 - half]
    row_ids = lax.broadcasted_iota(jnp.int32, (rows, cols), 0)
    col_ids = lax.broadcasted_iota(jnp.int32, (rows, cols), 1) + core * cols
    same = jnp.where(half == 0, below00[...], below10[...])
    other = jnp.where(half == 0, below01[...], below11[...])
    below = (jnp.where(col == 0, same, other), jnp.where(col == 0, other, same))
    for place, slot in enumerate(receivers()):
        lower, row_at, col_at = slot_place(offs, split_at, flat, slot)
        upper_rows = row_ids >= row_at
        left_cols = col_ids >= col_at

        def merged(side, lower=lower, upper_rows=upper_rows):
            second = own[2 + side]
            top = jnp.where(lower == 1, second, own[side])
            bottom = jnp.where(lower == 1, below[side], second)
            return jnp.where(upper_rows, top, bottom)

        out[place] = jnp.where(left_cols, merged(0), merged(1))


def add_kernel(where, slot_range, offs, parts, own, below0, below1, probe_band):
    rows, cols = own.shape[1], own.shape[2]
    half, col, core = where[0], where[1], where[2]
    flat = 4 * half + 2 * col + core
    split_at = slot_range[0, 1 - half]
    row_ids = lax.broadcasted_iota(jnp.int32, (rows, cols), 0)
    col_ids = lax.broadcasted_iota(jnp.int32, (rows, cols), 1) + core * cols
    slots = receivers()
    for strip in range(3):
        sums = [jnp.zeros((rows, cols), jnp.float32)] * 2
        for place, slot in enumerate(slots):
            lower, row_at, col_at = slot_place(offs, split_at, flat, slot)
            first = jnp.where(strip == lower, row_at, jnp.where(strip == lower + 1, 0, rows))
            last = jnp.where(strip == lower, rows, jnp.where(strip == lower + 1, row_at, 0))
            part = jnp.where((row_ids >= first) & (row_ids < last), parts[place, :rows], 0.0)
            left = jnp.where(col_ids >= col_at, part, 0.0)
            sums = [sums[0] + left, sums[1] + (part - left)]
        if strip < 2:
            own[2 * strip], own[2 * strip + 1] = sums
        else:
            below0[...] = jnp.where(col == 0, sums[0], sums[1])
            below1[...] = jnp.where(col == 0, sums[1], sums[0])
    band = probe_band.shape[0]
    total = parts[0, rows:]
    for place in range(1, len(slots)):
        total = total + parts[place, rows:]
    probe_band[:, :cols] = total[:band]
    probe_band[:, cols:] = total[band:]


SMEM = pl.BlockSpec(memory_space=pltpu.SMEM)
VMEM = pl.BlockSpec(memory_space=pltpu.VMEM)


def call(kernel, out_shape, scalars, arrays, flops, **kwargs):
    outs = out_shape if isinstance(out_shape, (list, tuple)) else [out_shape]
    moved = sum(math.prod(x.shape) * x.dtype.itemsize for x in [*arrays, *outs])
    return pl.pallas_call(
        kernel,
        out_shape=out_shape,
        in_specs=[SMEM] * len(scalars) + [VMEM] * len(arrays),
        out_specs=jax.tree.map(lambda unused: VMEM, out_shape),
        compiler_params=pltpu.CompilerParams(vmem_limit_bytes=VMEM_LIMIT),
        cost_estimate=pl.CostEstimate(flops=flops, bytes_accessed=moved, transcendentals=0),
        **kwargs,
    )(*scalars, *arrays)


def shape(*dims):
    return jax.ShapeDtypeStruct(dims, jnp.float32)


def shift_pairs(pairs, step, half, turn):
    out = []
    for pair in range(pairs - 1):
        for col in range(2):
            lower, upper = 4 * (pair + 1) + (col ^ turn), 4 * pair + 2 * half + col
            out.append((lower, upper) if step == 1 else (upper, lower))
    return out


def local(object_field, probe, offsets, slot_range, measured):
    width = probe.shape[-1]
    planes, rows, cols = 4, object_field.shape[2], object_field.shape[3]
    pairs = lax.axis_size("pair")
    half, col, core = (lax.axis_index(name) for name in PLANE)
    where = jnp.stack([half, col, core])

    block = object_field.reshape(planes, rows, cols)
    own = lax.all_to_all(block, ("half", "col"), 0, 0, tiled=True)
    mine = offsets.reshape(1, -1)
    offs = [mine] + [lax.ppermute(mine, PLANE, [(k, k ^ turn) for k in range(8)]) for turn in range(1, 8)]
    offs = jnp.concatenate(offs, axis=0)
    below = []
    for to_half in range(2):
        for turn in range(2):
            plane = lax.dynamic_index_in_dim(block, 2 * to_half + (col ^ turn), 0, keepdims=False)
            below.append(lax.ppermute(plane, ("pair", "half", "col"), shift_pairs(pairs, 1, to_half, turn)))
    given = lax.dynamic_index_in_dim(measured[0], 1 - half, 0, keepdims=False)
    taken = lax.ppermute(given, "half", [(0, 1), (1, 0)])

    scalars = (where, slot_range, offs)
    parts = call(pick_kernel, shape(8, rows, cols), scalars, (own, *below), 8 * rows * cols)
    patch = lax.all_to_all(parts, PLANE, 0, 0, tiled=True)
    tabs = [jnp.asarray(tab) for tab in tables(width)]
    band = 2 * width // 8
    grad = call(
        position_kernel,
        shape(8, rows + 2 * band, cols),
        scalars,
        (patch, probe, measured, taken, *tabs),
        8 * 24 * width**3,
    )
    got = lax.all_to_all(grad, PLANE, 0, 0, tiled=True)
    sums, *lower_sums, probe_band = call(
        add_kernel,
        [shape(4, rows, cols), shape(rows, cols), shape(rows, cols), shape(band, width)],
        scalars,
        (got,),
        48 * rows * cols,
    )
    added = []
    for from_half in range(2):
        for turn in range(2):
            perm = shift_pairs(pairs, -1, from_half, turn)
            added.append(lax.ppermute(lower_sums[turn], ("pair", "half", "col"), perm))
    mine_out = lax.all_to_all(sums, ("half", "col"), 0, 0, tiled=True)
    probe_band = jnp.sum(lax.all_gather(probe_band, "pair", axis=0), axis=0)
    probe_grad = lax.all_gather(probe_band, PLANE, axis=0, tiled=True).reshape(probe.shape)
    straight = [jnp.where(col == 0, added[2 * k], added[2 * k + 1]) for k in range(2)]
    crossed = [jnp.where(col == 0, added[2 * k + 1], added[2 * k]) for k in range(2)]
    above = jnp.stack([straight[0], crossed[0], straight[1], crossed[1]])
    object_grad = (mine_out + above).reshape(object_field.shape)
    return (object_grad, probe_grad)


def solution(mesh):
    tile, grp = mesh.shape["tile"], mesh.shape["grp"]
    devices = mesh.devices.reshape(tile // 2, 2, 2, grp // 2)
    inner = Mesh(devices, ("pair", "half", "col", "core"))
    strip, cols = ("pair", "half"), ("col", "core")
    in_specs = (
        P(None, None, strip, cols),
        P(),
        P(strip, cols, None),
        P(strip, None),
        P(strip, cols, None, None),
    )
    out_specs = (P(None, None, strip, cols), P())
    return jax.shard_map(local, mesh=inner, in_specs=in_specs, out_specs=out_specs, check_vma=False)
```

time: 186 us -> 142 us (0.76)
  waiting for transfers between devices: 87.4 us -> 51.8 us
  starting transfers between devices: 19.6 us -> 47.3 us
  between operations: 16.1 us -> 0.9 us
  blocking collectives: 38 us -> 24.8 us
  local copies, waits for them, and re-layouts: 8.59 us -> 2.09 us
  other arithmetic: 3.45 us -> 0.98 us
    psum x1 -> x0, waiting for transfers between devices: 36.4 us -> none  [local(): band = lax.psum(band, 'pair')]
    ppermute x2 -> x15, starting transfers between devices: 4.8 us -> 28.6 us  [the longest x4 14.7 us: local(): added.append(lax.ppermute(lower_sums[turn], ('pair', 'half', 'col'), perm))]
    reduce_scatter x1 -> x0, waiting for transfers between devices: 22.3 us -> none  [local(): band = lax.psum_scatter(probe_part, PLANE, scatter_dimension=1, tiled=True)]
    all_to_all x3 -> x4, waiting for transfers between devices: 0.01 us -> 21 us  [the longest x1 21 us: local(): got = lax.all_to_all(grad, PLANE, 0, 0, tiled=True)]
    all_to_all x1 -> x0, blocking collectives: 17.9 us -> none  [local(): got = lax.all_to_all(grad.reshape(8, rows, cols), PLANE, 0, 0, tiled=True)]
    unnamed x28 -> x17, local copies, waits for them, and re-layouts: 6.63 us -> 0.83 us
    all_gather x2, blocking collectives: 20.1 us -> 24.8 us  [the longest x1 14.1 us: local(): probe_band = jnp.sum(lax.all_gather(probe_band, 'pair', axis=0), axis=0)]
    all_to_all x3 -> x4, starting transfers between devices: 12.7 us -> 16.7 us  [the longest x1 5.31 us: local(): own = lax.all_to_all(block, ('half', 'col'), 0, 0, tiled=True)]
  transfers between devices with their start and end apart: 8 -> 20, of which waited for: 5 -> 9; matrix products, arithmetic and copies ran while one was open for 3% -> 1% of each run, Pallas kernels for 0% -> 0%
where the time goes in v2:
time: 142 us
  waiting for transfers between devices  51.8 us (36%)
  starting transfers between devices  47.3 us (33%)
  blocking collectives  24.8 us (17%)
  Pallas kernels  14 us (10%)
  local copies, waits for them, and re-layouts  2.09 us (1%)
    all_to_all x1, waiting for transfers between devices, local(): got = lax.all_to_all(grad, PLANE, 0, 0, tiled=True)  21 us
    ppermute x1, waiting for transfers between devices, local(): taken = lax.ppermute(given, 'half', [(0, 1), (1, 0)])  18 us
    ppermute x4, starting transfers between devices, local(): added.append(lax.ppermute(lower_sums[turn], ('pair', 'half', 'col'), perm))  14.7 us
    all_gather x1, blocking collectives, local(): probe_band = jnp.sum(lax.all_gather(probe_band, 'pair', axis=0), axis=0)  14.1 us
    pallas_call x3, Pallas kernels, call(): pl.pallas_call(kernel, out_shape=out_shape, in_specs=[SMEM] * len(scalars...  14 us
    ppermute x7, waiting for transfers between devices, local(): lax.ppermute(mine, PLANE, [(k, k ^ turn) for k in range(8)])  12.9 us
    all_gather x1, blocking collectives, local(): lax.all_gather(probe_band, PLANE, axis=0, tiled=True).reshape(probe.shape)  10.7 us
    ppermute x7, starting transfers between devices, local(): lax.ppermute(mine, PLANE, [(k, k ^ turn) for k in range(8)])  9.91 us
  transfers between devices with their start and end apart: 20, of which 9 were waited for; matrix products, arithmetic and copies ran while one was open for 1% of the time, Pallas kernels for 0%

profile of v2, /device:TPU:0, one launch (start us, length us, event | category | flops | bytes accessed | tf_op | source)
XLA Modules:
  0.0 141.9 jit_solution(11613548522213192494)
XLA Ops:
  0.6 5.3 %all-to-all-start = ((f32[4,256,128]{2,1,0:T(8,128)}), f32[4,256,128]{2,1,0:T(8,128)S(1)}, u32[]{:S(2)}, u32[]{:S(2)}) async-start(f32[4,256,128]{2,1,0:T(8,128)} %bitcast.25), calls=%async_computation | async-start | bytes 1048576 | tf_op jit(solution)/shard_map/all_to_all | solution.py:240
  6.0 1.1 dynamic-slice_bitcast_fusion.1
  7.1 0.7 collective-permute-start.10
  7.8 0.7 collective-permute-start.9
  8.4 1.3 collective-permute-start.8
  9.7 1.3 collective-permute-start.7
  11.1 0.1 reshape.18
  11.1 1.8 %collective-permute-start.6 = (s32[1,4]{1,0:T(1,128)S(1)}, s32[1,4]{1,0:T(1,128)S(1)}, u32[]{:S(2)}, u32[]{:S(2)}) collective-permute-start(s32[1,4]{1,0:T(1,128)S(1)} %reshape.18), channel_id=1, source_target_pairs={{0,7},{1,6},{2,5},{3,4},{4,3},{5,2},{6,1},{7,0},{8,15},{9,14},{10,... | collective-permute-start | bytes 56 | tf_op jit(solution)/shard_map/ppermute | solution.py:242
  12.9 0.1 pad_add_fusion.where
  13.0 2.0 %collective-permute-done.6 = s32[1,4]{1,0:T(1,128)S(1)} collective-permute-done((s32[1,4]{1,0:T(1,128)S(1)}, s32[1,4]{1,0:T(1,128)S(1)}, u32[]{:S(2)}, u32[]{:S(2)}) %collective-permute-start.6) | collective-permute-done | bytes 48 | tf_op jit(solution)/shard_map/ppermute | solution.py:242
  15.0 3.3 %collective-permute-start.5 = (s32[1,4]{1,0:T(1,128)S(1)}, s32[1,4]{1,0:T(1,128)S(1)}, u32[]{:S(2)}, u32[]{:S(2)}) collective-permute-start(s32[1,4]{1,0:T(1,128)S(1)} %reshape.18), channel_id=1, source_target_pairs={{0,6},{1,7},{2,4},{3,5},{4,2},{5,3},{6,0},{7,1},{8,14},{9,15},{10,... | collective-permute-start | bytes 56 | tf_op jit(solution)/shard_map/ppermute | solution.py:242
  18.3 1.5 %collective-permute-done.5 = s32[1,4]{1,0:T(1,128)S(1)} collective-permute-done((s32[1,4]{1,0:T(1,128)S(1)}, s32[1,4]{1,0:T(1,128)S(1)}, u32[]{:S(2)}, u32[]{:S(2)}) %collective-permute-start.5) | collective-permute-done | bytes 48 | tf_op jit(solution)/shard_map/ppermute | solution.py:242
  19.9 0.7 collective-permute-start.4
  20.5 2.3 %collective-permute-done.4 = s32[1,4]{1,0:T(1,128)S(1)} collective-permute-done((s32[1,4]{1,0:T(1,128)S(1)}, s32[1,4]{1,0:T(1,128)S(1)}, u32[]{:S(2)}, u32[]{:S(2)}) %collective-permute-start.4) | collective-permute-done | bytes 48 | tf_op jit(solution)/shard_map/ppermute | solution.py:242
  22.8 1.9 %collective-permute-start.3 = (s32[1,4]{1,0:T(1,128)S(1)}, s32[1,4]{1,0:T(1,128)S(1)}, u32[]{:S(2)}, u32[]{:S(2)}) collective-permute-start(s32[1,4]{1,0:T(1,128)S(1)} %reshape.18), channel_id=1, source_target_pairs={{0,4},{1,5},{2,6},{3,7},{4,0},{5,1},{6,2},{7,3},{8,12},{9,13},{10,... | collective-permute-start | bytes 56 | tf_op jit(solution)/shard_map/ppermute | solution.py:242
  24.7 1.7 %collective-permute-done.3 = s32[1,4]{1,0:T(1,128)S(1)} collective-permute-done((s32[1,4]{1,0:T(1,128)S(1)}, s32[1,4]{1,0:T(1,128)S(1)}, u32[]{:S(2)}, u32[]{:S(2)}) %collective-permute-start.3) | collective-permute-done | bytes 48 | tf_op jit(solution)/shard_map/ppermute | solution.py:242
  26.4 0.6 collective-permute-start.2
  27.0 2.4 %collective-permute-done.2 = s32[1,4]{1,0:T(1,128)S(1)} collective-permute-done((s32[1,4]{1,0:T(1,128)S(1)}, s32[1,4]{1,0:T(1,128)S(1)}, u32[]{:S(2)}, u32[]{:S(2)}) %collective-permute-start.2) | collective-permute-done | bytes 48 | tf_op jit(solution)/shard_map/ppermute | solution.py:242
  29.3 1.6 %collective-permute-start.1 = (s32[1,4]{1,0:T(1,128)S(1)}, s32[1,4]{1,0:T(1,128)S(1)}, u32[]{:S(2)}, u32[]{:S(2)}) collective-permute-start(s32[1,4]{1,0:T(1,128)S(1)} %reshape.18), channel_id=1, source_target_pairs={{0,2},{1,3},{2,0},{3,1},{4,6},{5,7},{6,4},{7,5},{8,10},{9,11},{10,... | collective-permute-start | bytes 56 | tf_op jit(solution)/shard_map/ppermute | solution.py:242
  30.9 1.9 %collective-permute-done.1 = s32[1,4]{1,0:T(1,128)S(1)} collective-permute-done((s32[1,4]{1,0:T(1,128)S(1)}, s32[1,4]{1,0:T(1,128)S(1)}, u32[]{:S(2)}, u32[]{:S(2)}) %collective-permute-start.1) | collective-permute-done | bytes 48 | tf_op jit(solution)/shard_map/ppermute | solution.py:242
  32.9 0.0 collective-permute-start
  32.9 1.1 collective-permute-done
  34.0 0.0 collective-permute-done.10.below11
  34.0 0.0 collective-permute-done.9.below10
  34.0 0.0 collective-permute-done.8.below01
  34.0 0.0 collective-permute-done.7.below00
  34.1 0.0 all-to-all-done.own
  34.1 2.0 %shard_map.104 = f32[8,256,128]{2,1,0:T(8,128)} custom-call(s32[3]{0:T(128)S(1)} %pad_add_fusion.where, s32[1,2]{1,0:T(1,128)S(1)} %copy-done.1, s32[8,4]{1,0:T(8,128)S(1)} %concatenate.3.offs, f32[4,256,128]{2,1,0:T(8,128)S(1)} %all-to-all-done.own, f32[256,128]{1,0:T(8,128)S(1)} %collective-permute-done.7.below00, ...), custom_call_target="tpu_custom_call" | custom-call | flops 262144 | bytes 2097152 | tf_op jit(solution)/shard_map/pallas_call | solution.py:208
  36.0 0.0 copy-start.5
  36.1 0.0 copy-start.6
  36.1 4.3 %all-to-all-start.1 = ((f32[8,256,128]{2,1,0:T(8,128)}), f32[8,256,128]{2,1,0:T(8,128)S(1)}, u32[]{:S(2)}, u32[]{:S(2)}) async-start(f32[8,256,128]{2,1,0:T(8,128)} %shard_map.104), calls=%async_computation.1 | async-start | bytes 2097152 | tf_op jit(solution)/shard_map/all_to_all | solution.py:254
  40.5 2.1 %collective-permute-start.11 = (f32[256,256]{1,0:T(8,128)S(1)}, f32[256,256]{1,0:T(8,128)S(1)}, u32[]{:S(2)}, u32[]{:S(2)}) collective-permute-start(f32[256,256]{1,0:T(8,128)S(1)} %dynamic-slice_bitcast_fusion), channel_id=1, source_target_pairs={{0,4},{4,0},{1,5},{5,1},{2,6},{6,2},{3,7},{7,3},{8,12},{12,8},{9,1... | collective-permute-start | bytes 786440 | tf_op jit(solution)/shard_map/ppermute | solution.py:250
  42.5 18.0 %collective-permute-done.11.taken = f32[256,256]{1,0:T(8,128)S(1)} collective-permute-done((f32[256,256]{1,0:T(8,128)S(1)}, f32[256,256]{1,0:T(8,128)S(1)}, u32[]{:S(2)}, u32[]{:S(2)}) %collective-permute-start.11) | collective-permute-done | bytes 262176 | tf_op jit(solution)/shard_map/ppermute | solution.py:250
  60.5 0.0 all-to-all-done.1.patch
  60.5 9.9 %shard_map.105 = f32[8,384,128]{2,1,0:T(8,128)} custom-call(s32[3]{0:T(128)S(1)} %pad_add_fusion.where, s32[1,2]{1,0:T(1,128)S(1)} %copy-done.1, s32[8,4]{1,0:T(8,128)S(1)} %concatenate.3.offs, f32[8,256,128]{2,1,0:T(8,128)S(1)} %all-to-all-done.1.patch, f32[2,256,256]{2,1,0:T(8,128)S(1)} %copy-done.2, f32[1,2,256,256]{3,2,1,0:T(8,128)S(1)} %copy-done, ...), custom_call_target="tpu_custom_call" | custom-call | flops 3221225472 | bytes 4980736 | tf_op jit(solution)/shard_map/pallas_call | solution.py:208
  70.4 3.6 %all-to-all-start.2 = ((f32[8,384,128]{2,1,0:T(8,128)}), f32[8,384,128]{2,1,0:T(8,128)S(1)}, u32[]{:S(2)}, u32[]{:S(2)}) async-start(f32[8,384,128]{2,1,0:T(8,128)} %shard_map.105), calls=%async_computation.2 | async-start | bytes 3145728 | tf_op jit(solution)/shard_map/all_to_all | solution.py:264
  74.0 21.0 %all-to-all-done.2.parts = f32[8,384,128]{2,1,0:T(8,128)S(1)} async-done(((f32[8,384,128]{2,1,0:T(8,128)}), f32[8,384,128]{2,1,0:T(8,128)S(1)}, u32[]{:S(2)}, u32[]{:S(2)}) %all-to-all-start.2) | async-done | bytes 1572896 | tf_op jit(solution)/shard_map/all_to_all | solution.py:264
  95.0 2.1 %shard_map.106 = (f32[4,256,128]{2,1,0:T(8,128)}, f32[256,128]{1,0:T(8,128)S(1)}, f32[256,128]{1,0:T(8,128)S(1)}, f32[64,256]{1,0:T(8,128)S(1)}) custom-call(s32[3]{0:T(128)S(1)} %pad_add_fusion.where, s32[1,2]{1,0:T(1,128)S(1)} %copy-done.1, s32[8,4]{1,0:T(8,128)S(1)} %concatenate.3.offs, f32[8,384,128]{2,1,0:T(8,128)S(1)} %all-to-all-done.2.parts), custom_call_target="tpu_custom_call" | custom-call | flops 1572864 | bytes 2424832 | tf_op jit(solution)/shard_map/pallas_call | solution.py:208
  97.1 0.7 collective-permute-start.14
  97.8 8.9 %collective-permute-start.12 = (f32[256,128]{1,0:T(8,128)S(1)}, f32[256,128]{1,0:T(8,128)S(1)}, u32[]{:S(2)}, u32[]{:S(2)}) collective-permute-start(f32[256,128]{1,0:T(8,128)S(1)} %get-tuple-element.7), channel_id=1, source_target_pairs={{0,8},{2,10},{8,16},{10,18},{16,24},{18,26},{1,9},{3,11},{9,17},{1... | collective-permute-start | bytes 393224 | tf_op jit(solution)/shard_map/ppermute | solution.py:276
  106.7 0.7 collective-permute-start.15
  107.4 4.5 %collective-permute-start.13 = (f32[256,128]{1,0:T(8,128)S(1)}, f32[256,128]{1,0:T(8,128)S(1)}, u32[]{:S(2)}, u32[]{:S(2)}) collective-permute-start(f32[256,128]{1,0:T(8,128)S(1)} %get-tuple-element.8), channel_id=1, source_target_pairs={{0,10},{2,8},{8,18},{10,16},{16,26},{18,24},{1,11},{3,9},{9,19},{1... | collective-permute-start | bytes 393224 | tf_op jit(solution)/shard_map/ppermute | solution.py:276
  111.9 3.5 %all-to-all-start.3 = ((f32[4,256,128]{2,1,0:T(8,128)}), f32[4,256,128]{2,1,0:T(8,128)S(1)}, u32[]{:S(2)}, u32[]{:S(2)}) async-start(f32[4,256,128]{2,1,0:T(8,128)} %get-tuple-element.6), calls=%async_computation.3 | async-start | bytes 1048576 | tf_op jit(solution)/shard_map/all_to_all | solution.py:277
  115.4 14.1 %all-gather = f32[256,256]{1,0:T(8,128)S(1)} all-gather(f32[64,256]{1,0:T(8,128)S(1)} %get-tuple-element.9), channel_id=2, replica_groups=mesh['pair'=4,'half'=2,'col'=2,'core'=2] {'pair'}, dimensions={0}, use_global_device_ids=true | all-gather | bytes 327680 | tf_op jit(solution)/shard_map/all_gather | solution.py:278
  129.5 10.7 %all_gather.11 = f32[512,256]{1,0:T(8,128)S(1)} all-gather(f32[64,256]{1,0:T(8,128)S(1)} %reduce_sum.9), channel_id=1, replica_groups=mesh['pair'=4,'half'=2,'col'=2,'core'=2] {'half','col','core'}, dimensions={0}, use_global_device_ids=true | all-gather | bytes 589824 | tf_op jit(solution)/shard_map/all_gather | solution.py:279
  140.3 0.0 all-to-all-done.3
  140.3 0.8 maximum_add_fusion
  141.1 0.8 copy.12
  (23 shorter events, 0.1 us)
Async XLA Ops:
  0.6 10.4 %copy-start.7 = (s32[1,2,2]{2,1,0:T(2,128)S(1)}, s32[1,2,2]{2,1,0:T(2,128)}, u32[]{:S(2)}) copy-start(s32[1,2,2]{2,1,0:T(2,128)} %param.11) | copy-start | bytes 52
  0.6 33.4 %copy-start.1 = (s32[1,2]{1,0:T(1,128)S(1)}, s32[1,2]{1,0:T(1,128)}, u32[]{:S(2)}) copy-start(s32[1,2]{1,0:T(1,128)} %slot_range.5) | copy-start | bytes 28
  0.6 33.4 %all-to-all-start = ((f32[4,256,128]{2,1,0:T(8,128)}), f32[4,256,128]{2,1,0:T(8,128)S(1)}, u32[]{:S(2)}, u32[]{:S(2)}) async-start(f32[4,256,128]{2,1,0:T(8,128)} %bitcast.25), calls=%async_computation | async-start | bytes 1048576 | tf_op jit(solution)/shard_map/all_to_all | solution.py:240
  7.1 26.9 %collective-permute-start.10 = (f32[256,128]{1,0:T(8,128)S(1)}, f32[256,128]{1,0:T(8,128)S(1)}, u32[]{:S(2)}, u32[]{:S(2)}) collective-permute-start(f32[256,128]{1,0:T(8,128)S(1)} %get-tuple-element.10), channel_id=1, source_target_pairs={{10,4},{8,6},{18,12},{16,14},{26,20},{24,22},{11,5},{9,7},{19,13},... | collective-permute-start | bytes 393224 | tf_op jit(solution)/shard_map/ppermute | solution.py:248
  7.8 26.3 %collective-permute-start.9 = (f32[256,128]{1,0:T(8,128)S(1)}, f32[256,128]{1,0:T(8,128)S(1)}, u32[]{:S(2)}, u32[]{:S(2)}) collective-permute-start(f32[256,128]{1,0:T(8,128)S(1)} %get-tuple-element.11), channel_id=1, source_target_pairs={{8,4},{10,6},{16,12},{18,14},{24,20},{26,22},{9,5},{11,7},{17,13},... | collective-permute-start | bytes 393224 | tf_op jit(solution)/shard_map/ppermute | solution.py:248
  8.4 25.6 %collective-permute-start.8 = (f32[256,128]{1,0:T(8,128)S(1)}, f32[256,128]{1,0:T(8,128)S(1)}, u32[]{:S(2)}, u32[]{:S(2)}) collective-permute-start(f32[256,128]{1,0:T(8,128)S(1)} %get-tuple-element.12), channel_id=1, source_target_pairs={{10,0},{8,2},{18,8},{16,10},{26,16},{24,18},{11,1},{9,3},{19,9},{1... | collective-permute-start | bytes 393224 | tf_op jit(solution)/shard_map/ppermute | solution.py:248
  9.7 24.3 %collective-permute-start.7 = (f32[256,128]{1,0:T(8,128)S(1)}, f32[256,128]{1,0:T(8,128)S(1)}, u32[]{:S(2)}, u32[]{:S(2)}) collective-permute-start(f32[256,128]{1,0:T(8,128)S(1)} %get-tuple-element.13), channel_id=1, source_target_pairs={{8,0},{10,2},{16,8},{18,10},{24,16},{26,18},{9,1},{11,3},{17,9},{1... | collective-permute-start | bytes 393224 | tf_op jit(solution)/shard_map/ppermute | solution.py:248
  11.1 3.9 %collective-permute-start.6 = (s32[1,4]{1,0:T(1,128)S(1)}, s32[1,4]{1,0:T(1,128)S(1)}, u32[]{:S(2)}, u32[]{:S(2)}) collective-permute-start(s32[1,4]{1,0:T(1,128)S(1)} %reshape.18), channel_id=1, source_target_pairs={{0,7},{1,6},{2,5},{3,4},{4,3},{5,2},{6,1},{7,0},{8,15},{9,14},{10,... | collective-permute-start | bytes 56 | tf_op jit(solution)/shard_map/ppermute | solution.py:242
  15.0 4.9 %collective-permute-start.5 = (s32[1,4]{1,0:T(1,128)S(1)}, s32[1,4]{1,0:T(1,128)S(1)}, u32[]{:S(2)}, u32[]{:S(2)}) collective-permute-start(s32[1,4]{1,0:T(1,128)S(1)} %reshape.18), channel_id=1, source_target_pairs={{0,6},{1,7},{2,4},{3,5},{4,2},{5,3},{6,0},{7,1},{8,14},{9,15},{10,... | collective-permute-start | bytes 56 | tf_op jit(solution)/shard_map/ppermute | solution.py:242
  19.9 3.0 %collective-permute-start.4 = (s32[1,4]{1,0:T(1,128)S(1)}, s32[1,4]{1,0:T(1,128)S(1)}, u32[]{:S(2)}, u32[]{:S(2)}) collective-permute-start(s32[1,4]{1,0:T(1,128)S(1)} %reshape.18), channel_id=1, source_target_pairs={{0,5},{1,4},{2,7},{3,6},{4,1},{5,0},{6,3},{7,2},{8,13},{9,12},{10,... | collective-permute-start | bytes 56 | tf_op jit(solution)/shard_map/ppermute | solution.py:242
  22.8 3.5 %collective-permute-start.3 = (s32[1,4]{1,0:T(1,128)S(1)}, s32[1,4]{1,0:T(1,128)S(1)}, u32[]{:S(2)}, u32[]{:S(2)}) collective-permute-start(s32[1,4]{1,0:T(1,128)S(1)} %reshape.18), channel_id=1, source_target_pairs={{0,4},{1,5},{2,6},{3,7},{4,0},{5,1},{6,2},{7,3},{8,12},{9,13},{10,... | collective-permute-start | bytes 56 | tf_op jit(solution)/shard_map/ppermute | solution.py:242
  26.4 3.0 %collective-permute-start.2 = (s32[1,4]{1,0:T(1,128)S(1)}, s32[1,4]{1,0:T(1,128)S(1)}, u32[]{:S(2)}, u32[]{:S(2)}) collective-permute-start(s32[1,4]{1,0:T(1,128)S(1)} %reshape.18), channel_id=1, source_target_pairs={{0,3},{1,2},{2,1},{3,0},{4,7},{5,6},{6,5},{7,4},{8,11},{9,10},{10,... | collective-permute-start | bytes 56 | tf_op jit(solution)/shard_map/ppermute | solution.py:242
  29.3 3.5 %collective-permute-start.1 = (s32[1,4]{1,0:T(1,128)S(1)}, s32[1,4]{1,0:T(1,128)S(1)}, u32[]{:S(2)}, u32[]{:S(2)}) collective-permute-start(s32[1,4]{1,0:T(1,128)S(1)} %reshape.18), channel_id=1, source_target_pairs={{0,2},{1,3},{2,0},{3,1},{4,6},{5,7},{6,4},{7,5},{8,10},{9,11},{10,... | collective-permute-start | bytes 56 | tf_op jit(solution)/shard_map/ppermute | solution.py:242
  32.9 1.1 collective-permute-start
  36.0 4.4 %copy-start = (f32[1,2,256,256]{3,2,1,0:T(8,128)S(1)}, f32[1,2,256,256]{3,2,1,0:T(8,128)}, u32[]{:S(2)}) copy-start(f32[1,2,256,256]{3,2,1,0:T(8,128)} %measured.1) | copy-start | bytes 1572868
  36.0 24.5 %copy-start.2 = (f32[2,256,256]{2,1,0:T(8,128)S(1)}, f32[2,256,256]{2,1,0:T(8,128)}, u32[]{:S(2)}) copy-start(f32[2,256,256]{2,1,0:T(8,128)} %probe.1) | copy-start | bytes 1572868
  36.0 24.5 %copy-start.3 = (bf16[512,256]{1,0:T(8,128)(2,1)S(1)}, bf16[512,256]{1,0:T(8,128)(2,1)}, u32[]{:S(2)}) copy-start(bf16[512,256]{1,0:T(8,128)(2,1)} %constant.50.clone.near_low) | copy-start | bytes 786436
  36.0 24.5 %copy-start.4 = (bf16[512,256]{1,0:T(8,128)(2,1)S(1)}, bf16[512,256]{1,0:T(8,128)(2,1)}, u32[]{:S(2)}) copy-start(bf16[512,256]{1,0:T(8,128)(2,1)} %constant.49.clone.near_high) | copy-start | bytes 786436
  36.0 24.5 %copy-start.5 = (bf16[512,256]{1,0:T(8,128)(2,1)S(1)}, bf16[512,256]{1,0:T(8,128)(2,1)}, u32[]{:S(2)}) copy-start(bf16[512,256]{1,0:T(8,128)(2,1)} %constant.48.clone.far_low) | copy-start | bytes 786436
  36.1 24.5 %copy-start.6 = (bf16[512,256]{1,0:T(8,128)(2,1)S(1)}, bf16[512,256]{1,0:T(8,128)(2,1)}, u32[]{:S(2)}) copy-start(bf16[512,256]{1,0:T(8,128)(2,1)} %constant.47.clone.far_high) | copy-start | bytes 786436
  36.1 24.4 %all-to-all-start.1 = ((f32[8,256,128]{2,1,0:T(8,128)}), f32[8,256,128]{2,1,0:T(8,128)S(1)}, u32[]{:S(2)}, u32[]{:S(2)}) async-start(f32[8,256,128]{2,1,0:T(8,128)} %shard_map.104), calls=%async_computation.1 | async-start | bytes 2097152 | tf_op jit(solution)/shard_map/all_to_all | solution.py:254
  40.5 20.0 %collective-permute-start.11 = (f32[256,256]{1,0:T(8,128)S(1)}, f32[256,256]{1,0:T(8,128)S(1)}, u32[]{:S(2)}, u32[]{:S(2)}) collective-permute-start(f32[256,256]{1,0:T(8,128)S(1)} %dynamic-slice_bitcast_fusion), channel_id=1, source_target_pairs={{0,4},{4,0},{1,5},{5,1},{2,6},{6,2},{3,7},{7,3},{8,12},{12,8},{9,1... | collective-permute-start | bytes 786440 | tf_op jit(solution)/shard_map/ppermute | solution.py:250
  70.4 24.5 %all-to-all-start.2 = ((f32[8,384,128]{2,1,0:T(8,128)}), f32[8,384,128]{2,1,0:T(8,128)S(1)}, u32[]{:S(2)}, u32[]{:S(2)}) async-start(f32[8,384,128]{2,1,0:T(8,128)} %shard_map.105), calls=%async_computation.2 | async-start | bytes 3145728 | tf_op jit(solution)/shard_map/all_to_all | solution.py:264
  97.1 43.1 %collective-permute-start.14 = (f32[256,128]{1,0:T(8,128)S(1)}, f32[256,128]{1,0:T(8,128)S(1)}, u32[]{:S(2)}, u32[]{:S(2)}) collective-permute-start(f32[256,128]{1,0:T(8,128)S(1)} %get-tuple-element.7), channel_id=1, source_target_pairs={{4,8},{6,10},{12,16},{14,18},{20,24},{22,26},{5,9},{7,11},{13,17},... | collective-permute-start | bytes 393224 | tf_op jit(solution)/shard_map/ppermute | solution.py:276
  97.8 42.5 %collective-permute-start.12 = (f32[256,128]{1,0:T(8,128)S(1)}, f32[256,128]{1,0:T(8,128)S(1)}, u32[]{:S(2)}, u32[]{:S(2)}) collective-permute-start(f32[256,128]{1,0:T(8,128)S(1)} %get-tuple-element.7), channel_id=1, source_target_pairs={{0,8},{2,10},{8,16},{10,18},{16,24},{18,26},{1,9},{3,11},{9,17},{1... | collective-permute-start | bytes 393224 | tf_op jit(solution)/shard_map/ppermute | solution.py:276
  106.7 33.5 %collective-permute-start.15 = (f32[256,128]{1,0:T(8,128)S(1)}, f32[256,128]{1,0:T(8,128)S(1)}, u32[]{:S(2)}, u32[]{:S(2)}) collective-permute-start(f32[256,128]{1,0:T(8,128)S(1)} %get-tuple-element.8), channel_id=1, source_target_pairs={{4,10},{6,8},{12,18},{14,16},{20,26},{22,24},{5,11},{7,9},{13,19},... | collective-permute-start | bytes 393224 | tf_op jit(solution)/shard_map/ppermute | solution.py:276
  107.4 32.9 %collective-permute-start.13 = (f32[256,128]{1,0:T(8,128)S(1)}, f32[256,128]{1,0:T(8,128)S(1)}, u32[]{:S(2)}, u32[]{:S(2)}) collective-permute-start(f32[256,128]{1,0:T(8,128)S(1)} %get-tuple-element.8), channel_id=1, source_target_pairs={{0,10},{2,8},{8,18},{10,16},{16,26},{18,24},{1,11},{3,9},{9,19},{1... | collective-permute-start | bytes 393224 | tf_op jit(solution)/shard_map/ppermute | solution.py:276
  111.9 28.4 %all-to-all-start.3 = ((f32[4,256,128]{2,1,0:T(8,128)}), f32[4,256,128]{2,1,0:T(8,128)S(1)}, u32[]{:S(2)}, u32[]{:S(2)}) async-start(f32[4,256,128]{2,1,0:T(8,128)} %get-tuple-element.6), calls=%async_computation.3 | async-start | bytes 1048576 | tf_op jit(solution)/shard_map/all_to_all | solution.py:277

commit v3 on v2

--- a/solution.py
+++ b/solution.py
@@ -77,19 +77,18 @@
     return times_left(re, im, *tabs, conj)
 
 
-def slot_place(offs, split_at, flat, slot):
-    lower = jnp.where(slot >= split_at, 1, 0)
-    holder = jnp.bitwise_xor(4 * lower + slot // 2, flat)
-    at = 2 * (slot % 2)
-    return lower, offs[holder, at], offs[holder, at + 1]
-
-
 def slot_of(half, col, core):
     return 2 * (2 * col + core) + half
 
 
 def receivers():
     return [slot_of(half, col, core) for half in range(2) for col in range(2) for core in range(2)]
+
+
+def slot_place(offs, split_at, slot):
+    lower = jnp.where(slot >= split_at, 1, 0)
+    at = 2 * (slot % 4)
+    return lower, offs[2 * lower + slot // 4, at], offs[2 * lower + slot // 4, at + 1]
 
 
 def position_kernel(
@@ -98,7 +97,7 @@
     far_tabs, near_tabs = (far_high, far_low), (near_high, near_low)
     half, col, core = where[0], where[1], where[2]
     split_at = slot_range[0, 1 - half]
-    lower, row_at, col_at = slot_place(offs, split_at, 4 * half + 2 * col + core, slot_of(half, col, core))
+    lower, row_at, col_at = slot_place(offs, split_at, slot_of(half, col, core))
     width = probe.shape[-1]
     lanes = width // 2
 
@@ -144,24 +143,25 @@
             grad[4 * part + step, width + band :] = rows[:, lanes:]
 
 
-def pick_kernel(where, slot_range, offs, own, below00, below01, below10, below11, out):
+def pick_kernel(where, slot_range, own, below00, below01, below10, below11, out):
     rows, cols = out.shape[1], out.shape[2]
     half, col, core = where[0], where[1], where[2]
-    flat = 4 * half + 2 * col + core
     split_at = slot_range[0, 1 - half]
-    row_ids = lax.broadcasted_iota(jnp.int32, (rows, cols), 0)
-    col_ids = lax.broadcasted_iota(jnp.int32, (rows, cols), 1) + core * cols
+    row_ids = lax.broadcasted_iota(jnp.int32, (rows, cols), 0).astype(jnp.float32)
+    col_ids = (lax.broadcasted_iota(jnp.int32, (rows, cols), 1) + core * cols).astype(jnp.float32)
     same = jnp.where(half == 0, below00[...], below10[...])
     other = jnp.where(half == 0, below01[...], below11[...])
     below = (jnp.where(col == 0, same, other), jnp.where(col == 0, other, same))
     for place, slot in enumerate(receivers()):
-        lower, row_at, col_at = slot_place(offs, split_at, flat, slot)
-        upper_rows = row_ids >= row_at
-        left_cols = col_ids >= col_at
+        lower = jnp.where(slot >= split_at, 1, 0)
+        at = rows + 2 * (slot % 4)
+        offs = jnp.where(lower == 1, own[2 + slot // 4, at : at + 2], own[slot // 4, at : at + 2])
+        upper_rows = row_ids >= offs[0:1]
+        left_cols = col_ids >= offs[1:2]
 
         def merged(side, lower=lower, upper_rows=upper_rows):
-            second = own[2 + side]
-            top = jnp.where(lower == 1, second, own[side])
+            second = own[2 + side, :rows]
+            top = jnp.where(lower == 1, second, own[side, :rows])
             bottom = jnp.where(lower == 1, below[side], second)
             return jnp.where(upper_rows, top, bottom)
 
@@ -171,7 +171,6 @@
 def add_kernel(where, slot_range, offs, parts, own, below0, below1, probe_band):
     rows, cols = own.shape[1], own.shape[2]
     half, col, core = where[0], where[1], where[2]
-    flat = 4 * half + 2 * col + core
     split_at = slot_range[0, 1 - half]
     row_ids = lax.broadcasted_iota(jnp.int32, (rows, cols), 0)
     col_ids = lax.broadcasted_iota(jnp.int32, (rows, cols), 1) + core * cols
@@ -179,7 +178,7 @@
     for strip in range(3):
         sums = [jnp.zeros((rows, cols), jnp.float32)] * 2
         for place, slot in enumerate(slots):
-            lower, row_at, col_at = slot_place(offs, split_at, flat, slot)
+            lower, row_at, col_at = slot_place(offs, split_at, slot)
             first = jnp.where(strip == lower, row_at, jnp.where(strip == lower + 1, 0, rows))
             last = jnp.where(strip == lower, rows, jnp.where(strip == lower + 1, row_at, 0))
             part = jnp.where((row_ids >= first) & (row_ids < last), parts[place, :rows], 0.0)
@@ -229,6 +228,16 @@
     return out
 
 
+def sum_over(value, axis, size):
+    if size & (size - 1):
+        return lax.psum(value, axis)
+    step = 1
+    while step < size:
+        value = value + lax.ppermute(value, axis, [(k, k ^ step) for k in range(size)])
+        step *= 2
+    return value
+
+
 def local(object_field, probe, offsets, slot_range, measured):
     width = probe.shape[-1]
     planes, rows, cols = 4, object_field.shape[2], object_field.shape[3]
@@ -237,10 +246,11 @@
     where = jnp.stack([half, col, core])
 
     block = object_field.reshape(planes, rows, cols)
-    own = lax.all_to_all(block, ("half", "col"), 0, 0, tiled=True)
-    mine = offsets.reshape(1, -1)
-    offs = [mine] + [lax.ppermute(mine, PLANE, [(k, k ^ turn) for k in range(8)]) for turn in range(1, 8)]
-    offs = jnp.concatenate(offs, axis=0)
+    mine = offsets.reshape(1, -1).astype(jnp.float32)
+    sibling = lax.ppermute(mine, "core", [(0, 1), (1, 0)])
+    places = jnp.where(core == 0, jnp.concatenate([mine, sibling], 1), jnp.concatenate([sibling, mine], 1))
+    places = jnp.broadcast_to(places.reshape(1, -1, 1), (planes, places.size, cols))
+    own = lax.all_to_all(jnp.concatenate([block, places], axis=1), ("half", "col"), 0, 0, tiled=True)
     below = []
     for to_half in range(2):
         for turn in range(2):
@@ -249,8 +259,9 @@
     given = lax.dynamic_index_in_dim(measured[0], 1 - half, 0, keepdims=False)
     taken = lax.ppermute(given, "half", [(0, 1), (1, 0)])
 
-    scalars = (where, slot_range, offs)
-    parts = call(pick_kernel, shape(8, rows, cols), scalars, (own, *below), 8 * rows * cols)
+    own, taken = lax.optimization_barrier((own, taken))
+    parts = call(pick_kernel, shape(8, rows, cols), (where, slot_range), (own, *below), 8 * rows * cols)
+    scalars = (where, slot_range, own[:, rows:, 0].astype(jnp.int32))
     patch = lax.all_to_all(parts, PLANE, 0, 0, tiled=True)
     tabs = [jnp.asarray(tab) for tab in tables(width)]
     band = 2 * width // 8
@@ -275,7 +286,7 @@
             perm = shift_pairs(pairs, -1, from_half, turn)
             added.append(lax.ppermute(lower_sums[turn], ("pair", "half", "col"), perm))
     mine_out = lax.all_to_all(sums, ("half", "col"), 0, 0, tiled=True)
-    probe_band = jnp.sum(lax.all_gather(probe_band, "pair", axis=0), axis=0)
+    probe_band = sum_over(probe_band, "pair", pairs)
     probe_grad = lax.all_gather(probe_band, PLANE, axis=0, tiled=True).reshape(probe.shape)
     straight = [jnp.where(col == 0, added[2 * k], added[2 * k + 1]) for k in range(2)]
     crossed = [jnp.where(col == 0, added[2 * k + 1], added[2 * k]) for k in range(2)]

time: 142 us -> 118 us (0.83)
  waiting for transfers between devices: 51.8 us -> 30.7 us
  starting transfers between devices: 47.3 us -> 31.1 us
  blocking collectives: 24.8 us -> 35.2 us
  other arithmetic: 0.98 us -> 3.93 us
    all_to_all x0 -> x1, blocking collectives: none -> 23.4 us  [local(): got = lax.all_to_all(grad, PLANE, 0, 0, tiled=True)]
    all_to_all x2 -> x1, waiting for transfers between devices: 21 us -> 0.01 us  [local(): lax.all_to_all(jnp.concatenate([block, places], axis=1), ('half', 'col'),...]
    all_to_all x1, waiting for transfers between devices: 0.01 us -> 15.3 us  [local(): patch = lax.all_to_all(parts, PLANE, 0, 0, tiled=True)]
    all_gather x1 -> x0, blocking collectives: 14.1 us -> none  [local(): probe_band = jnp.sum(lax.all_gather(probe_band, 'pair', axis=0), axis=0)]
    ppermute x7 -> x3, waiting for transfers between devices: 12.9 us -> 3.42 us  [the longest x2 2.69 us: sum_over(): lax.ppermute(value, axis, [(k, k ^ step) for k in range(size)])]
    ppermute x4, starting transfers between devices: 14.7 us -> 7.28 us  [local(): added.append(lax.ppermute(lower_sums[turn], ('pair', 'half', 'col'), perm))]
    ppermute x1, waiting for transfers between devices: 18 us -> 11.4 us  [local(): taken = lax.ppermute(given, 'half', [(0, 1), (1, 0)])]
    ppermute x7 -> x3, starting transfers between devices: 9.91 us -> 4.7 us  [the longest x2 4.24 us: sum_over(): lax.ppermute(value, axis, [(k, k ^ step) for k in range(size)])]
  transfers between devices with their start and end apart: 20 -> 15, of which waited for: 9 -> 5; matrix products, arithmetic and copies ran while one was open for 1% -> 0% of each run, Pallas kernels for 0% -> 0%
where the time goes in v3:
time: 118 us; the launch traced here: 117 us
  blocking collectives  35.2 us (30%)
  starting transfers between devices  31.1 us (26%)
  waiting for transfers between devices  30.7 us (26%)
  Pallas kernels  12.6 us (11%)
  other arithmetic  3.93 us (3%)
  local copies, waits for them, and re-layouts  2.94 us (2%)
    all_to_all x1, blocking collectives, local(): got = lax.all_to_all(grad, PLANE, 0, 0, tiled=True)  23.4 us
    all_to_all x1, waiting for transfers between devices, local(): patch = lax.all_to_all(parts, PLANE, 0, 0, tiled=True)  15.3 us
    pallas_call x3, Pallas kernels, call(): pl.pallas_call(kernel, out_shape=out_shape, in_specs=[SMEM] * len(scalars...  12.6 us
    all_gather x1, blocking collectives, local(): lax.all_gather(probe_band, PLANE, axis=0, tiled=True).reshape(probe.shape)  11.8 us
    ppermute x1, waiting for transfers between devices, local(): taken = lax.ppermute(given, 'half', [(0, 1), (1, 0)])  11.4 us
    ppermute x4, starting transfers between devices, local(): added.append(lax.ppermute(lower_sums[turn], ('pair', 'half', 'col'), perm))  7.28 us
    all_to_all x1, starting transfers between devices, local(): lax.all_to_all(jnp.concatenate([block, places], axis=1), ('half', 'col'),...  5.14 us
    all_to_all x1, starting transfers between devices, local(): patch = lax.all_to_all(parts, PLANE, 0, 0, tiled=True)  4.48 us
  transfers between devices with their start and end apart: 15, of which 5 were waited for; matrix products, arithmetic and copies ran while one was open for 0% of the time, Pallas kernels for 0%

profile of v3, /device:TPU:0, one launch (start us, length us, event | category | flops | bytes accessed | tf_op | source)
XLA Modules:
  0.0 117.3 jit_solution(4893556274656714345)
XLA Ops:
  0.6 0.0 copy-start.7
  0.7 0.8 convert_element_type.27
  1.4 0.1 convert_element_type.29
  1.5 0.5 collective-permute-start
  2.0 0.1 convert_element_type.28
  2.0 0.7 collective-permute-done
  2.8 0.1 broadcast_select_fusion
  2.9 2.0 %pad_maximum_fusion = f32[4,264,128]{2,1,0:T(8,128)} fusion(f32[4,256,128]{2,1,0:T(8,128)} %bitcast.25, f32[264]{0:T(512)S(1)} %pad.5.clone), kind=kLoop, calls=%fused_computation | loop fusion | flops 135168 | bytes 1066016 | tf_op jit(solution)/shard_map/concatenate | solution.py:253
  4.8 5.1 %all-to-all-start = ((f32[4,264,128]{2,1,0:T(8,128)}), f32[4,264,128]{2,1,0:T(8,128)S(1)}, u32[]{:S(2)}, u32[]{:S(2)}) async-start(f32[4,264,128]{2,1,0:T(8,128)} %pad_maximum_fusion), calls=%async_computation | async-start | bytes 1081344 | tf_op jit(solution)/shard_map/all_to_all | solution.py:253
  10.0 2.1 %collective-permute-start.1 = (f32[256,256]{1,0:T(8,128)S(1)}, f32[256,256]{1,0:T(8,128)S(1)}, u32[]{:S(2)}, u32[]{:S(2)}) collective-permute-start(f32[256,256]{1,0:T(8,128)S(1)} %dynamic-slice_bitcast_fusion), channel_id=1, source_target_pairs={{0,4},{4,0},{1,5},{5,1},{2,6},{6,2},{3,7},{7,3},{8,12},{12,8},{9,1... | collective-permute-start | bytes 786440 | tf_op jit(solution)/shard_map/ppermute | solution.py:260
  12.1 0.7 collective-permute-start.5
  12.8 0.7 collective-permute-start.4
  13.5 1.3 %collective-permute-start.3 = (f32[256,128]{1,0:T(8,128)S(1)}, f32[256,128]{1,0:T(8,128)S(1)}, u32[]{:S(2)}, u32[]{:S(2)}) collective-permute-start(f32[256,128]{1,0:T(8,128)S(1)} %get-tuple-element.16), channel_id=1, source_target_pairs={{10,0},{8,2},{18,8},{16,10},{26,16},{24,18},{11,1},{9,3},{19,9},{1... | collective-permute-start | bytes 393224 | tf_op jit(solution)/shard_map/ppermute | solution.py:258
  14.8 1.3 %collective-permute-start.2 = (f32[256,128]{1,0:T(8,128)S(1)}, f32[256,128]{1,0:T(8,128)S(1)}, u32[]{:S(2)}, u32[]{:S(2)}) collective-permute-start(f32[256,128]{1,0:T(8,128)S(1)} %get-tuple-element.17), channel_id=1, source_target_pairs={{8,0},{10,2},{16,8},{18,10},{24,16},{26,18},{9,1},{11,3},{17,9},{1... | collective-permute-start | bytes 393224 | tf_op jit(solution)/shard_map/ppermute | solution.py:258
  16.1 0.1 pad_add_fusion.where
  16.2 11.4 %collective-permute-done.1.taken = f32[256,256]{1,0:T(8,128)S(1)} collective-permute-done((f32[256,256]{1,0:T(8,128)S(1)}, f32[256,256]{1,0:T(8,128)S(1)}, u32[]{:S(2)}, u32[]{:S(2)}) %collective-permute-start.1) | collective-permute-done | bytes 262176 | tf_op jit(solution)/shard_map/ppermute | solution.py:260
  27.5 0.0 all-to-all-done.own
  27.5 0.0 collective-permute-done.5.below11
  27.5 0.0 collective-permute-done.4.below10
  27.5 0.0 collective-permute-done.3.below01
  27.5 0.6 collective-permute-done.2.below00
  28.2 1.9 %shard_map.104 = f32[8,256,128]{2,1,0:T(8,128)} custom-call(s32[3]{0:T(128)S(1)} %pad_add_fusion.where, s32[1,2]{1,0:T(1,128)S(1)} %copy-done.1, f32[4,264,128]{2,1,0:T(8,128)S(1)} %all-to-all-done.own, f32[256,128]{1,0:T(8,128)S(1)} %collective-permute-done.2.below00, f32[256,128]{1,0:T(8,128)S(1)} %collective-permute-done.3.below01, ...), custom_call_target="tpu_custom_call" | custom-call | flops 262144 | bytes 2113536 | tf_op jit(solution)/shard_map/pallas_call | solution.py:207
  30.1 4.5 %all-to-all-start.1 = ((f32[8,256,128]{2,1,0:T(8,128)}), f32[8,256,128]{2,1,0:T(8,128)S(1)}, u32[]{:S(2)}, u32[]{:S(2)}) async-start(f32[8,256,128]{2,1,0:T(8,128)} %shard_map.104), calls=%async_computation.1 | async-start | bytes 2097152 | tf_op jit(solution)/shard_map/all_to_all | solution.py:265
  34.6 0.1 convert_reduce_fusion.offs
  34.7 15.3 %all-to-all-done.1.patch = f32[8,256,128]{2,1,0:T(8,128)S(1)} async-done(((f32[8,256,128]{2,1,0:T(8,128)}), f32[8,256,128]{2,1,0:T(8,128)S(1)}, u32[]{:S(2)}, u32[]{:S(2)}) %all-to-all-start.1) | async-done | bytes 1048608 | tf_op jit(solution)/shard_map/all_to_all | solution.py:265
  50.0 0.0 copy-start.5
  50.0 0.9 copy-done.5
  50.9 0.9 copy-done.6
  51.9 8.6 %shard_map.105 = f32[8,384,128]{2,1,0:T(8,128)S(1)} custom-call(s32[3]{0:T(128)S(1)} %pad_add_fusion.where, s32[1,2]{1,0:T(1,128)S(1)} %copy-done.1, s32[4,8]{1,0:T(4,128)S(1)} %convert_reduce_fusion.offs, f32[8,256,128]{2,1,0:T(8,128)S(1)} %all-to-all-done.1.patch, f32[2,256,256]{2,1,0:T(8,128)S(1)} %copy-done.2, f32[1,2,256,256]{3,2,1,0:T(8,128)S(1)} %copy-done, ...), custom_call_target="tpu_custom_call" | custom-call | flops 3221225472 | bytes 4980736 | tf_op jit(solution)/shard_map/pallas_call | solution.py:207
  60.5 23.4 %all_to_all.20.parts = f32[8,384,128]{2,1,0:T(8,128)S(1)} all-to-all(f32[8,384,128]{2,1,0:T(8,128)S(1)} %shard_map.105), channel_id=1, replica_groups=mesh['pair'=4,'half'=2,'col'=2,'core'=2] {'half','col','core'}, dimensions={0} | all-to-all | bytes 3145728 | tf_op jit(solution)/shard_map/all_to_all | solution.py:275
  83.9 2.1 %shard_map.106 = (f32[4,256,128]{2,1,0:T(8,128)}, f32[256,128]{1,0:T(8,128)S(1)}, f32[256,128]{1,0:T(8,128)S(1)}, f32[64,256]{1,0:T(8,128)S(1)}) custom-call(s32[3]{0:T(128)S(1)} %pad_add_fusion.where, s32[1,2]{1,0:T(1,128)S(1)} %copy-done.1, s32[4,8]{1,0:T(4,128)S(1)} %convert_reduce_fusion.offs, f32[8,384,128]{2,1,0:T(8,128)S(1)} %all_to_all.20.parts), custom_call_target="tpu_custom_call" | custom-call | flops 1572864 | bytes 2424832 | tf_op jit(solution)/shard_map/pallas_call | solution.py:207
  86.0 1.6 %collective-permute-start.10 = (f32[64,256]{1,0:T(8,128)S(1)}, f32[64,256]{1,0:T(8,128)S(1)}, u32[]{:S(2)}, u32[]{:S(2)}) collective-permute-start(f32[64,256]{1,0:T(8,128)S(1)} %get-tuple-element.13), channel_id=1, source_target_pairs={{0,8},{8,0},{16,24},{24,16},{1,9},{9,1},{17,25},{25,17},{2,10},{10... | collective-permute-start | bytes 196616 | tf_op jit(solution)/shard_map/ppermute | solution.py:236
  87.6 2.7 %collective-permute-done.10 = f32[64,256]{1,0:T(8,128)S(1)} collective-permute-done((f32[64,256]{1,0:T(8,128)S(1)}, f32[64,256]{1,0:T(8,128)S(1)}, u32[]{:S(2)}, u32[]{:S(2)}) %collective-permute-start.10) | collective-permute-done | bytes 65568 | tf_op jit(solution)/shard_map/ppermute | solution.py:236
  90.3 2.7 %collective-permute-start.11 = (f32[64,256]{1,0:T(8,128)S(1)}, f32[64,256]{1,0:T(8,128)S(1)}, u32[]{:S(2)}, u32[]{:S(2)}) collective-permute-start(f32[64,256]{1,0:T(8,128)S(1)} %add.45), channel_id=1, source_target_pairs={{0,16},{8,24},{16,0},{24,8},{1,17},{9,25},{17,1},{25,9},{2,18},{10... | collective-permute-start | bytes 196616 | tf_op jit(solution)/shard_map/ppermute | solution.py:236
  93.0 0.7 collective-permute-start.8
  93.6 0.7 collective-permute-start.9
  94.3 3.2 %collective-permute-start.6 = (f32[256,128]{1,0:T(8,128)S(1)}, f32[256,128]{1,0:T(8,128)S(1)}, u32[]{:S(2)}, u32[]{:S(2)}) collective-permute-start(f32[256,128]{1,0:T(8,128)S(1)} %get-tuple-element.11), channel_id=1, source_target_pairs={{0,8},{2,10},{8,16},{10,18},{16,24},{18,26},{1,9},{3,11},{9,17},{1... | collective-permute-start | bytes 393224 | tf_op jit(solution)/shard_map/ppermute | solution.py:287
  97.5 2.8 %collective-permute-start.7 = (f32[256,128]{1,0:T(8,128)S(1)}, f32[256,128]{1,0:T(8,128)S(1)}, u32[]{:S(2)}, u32[]{:S(2)}) collective-permute-start(f32[256,128]{1,0:T(8,128)S(1)} %get-tuple-element.12), channel_id=1, source_target_pairs={{0,10},{2,8},{8,18},{10,16},{16,26},{18,24},{1,11},{3,9},{9,19},{1... | collective-permute-start | bytes 393224 | tf_op jit(solution)/shard_map/ppermute | solution.py:287
  100.3 3.5 %all-to-all-start.3 = ((f32[4,256,128]{2,1,0:T(8,128)}), f32[4,256,128]{2,1,0:T(8,128)S(1)}, u32[]{:S(2)}, u32[]{:S(2)}) async-start(f32[4,256,128]{2,1,0:T(8,128)} %get-tuple-element.10), calls=%async_computation.3 | async-start | bytes 1048576 | tf_op jit(solution)/shard_map/all_to_all | solution.py:288
  103.8 0.0 collective-permute-done.11
  103.8 11.8 %all_gather.3 = f32[512,256]{1,0:T(8,128)S(1)} all-gather(f32[64,256]{1,0:T(8,128)S(1)} %add.46), channel_id=1, replica_groups=mesh['pair'=4,'half'=2,'col'=2,'core'=2] {'half','col','core'}, dimensions={0}, use_global_device_ids=true | all-gather | bytes 589824 | tf_op jit(solution)/shard_map/all_gather | solution.py:290
  115.6 0.0 collective-permute-done.8
  115.6 0.0 collective-permute-done.9
  115.6 0.0 collective-permute-done.6
  115.6 0.0 collective-permute-done.7
  115.7 0.0 all-to-all-done.3
  115.7 0.8 maximum_add_fusion
  116.5 0.8 copy.12
  (19 shorter events, 0.1 us)
Async XLA Ops:
  0.6 11.5 %copy-start.7 = (f32[2,2,256,128]{3,2,1,0:T(8,128)S(1)}, f32[2,2,256,128]{3,2,1,0:T(8,128)}, u32[]{:S(2)}) copy-start(f32[2,2,256,128]{3,2,1,0:T(8,128)} %param.9) | copy-start | bytes 1572868
  0.6 9.3 %copy-start = (f32[1,2,256,256]{3,2,1,0:T(8,128)S(1)}, f32[1,2,256,256]{3,2,1,0:T(8,128)}, u32[]{:S(2)}) copy-start(f32[1,2,256,256]{3,2,1,0:T(8,128)} %measured.1) | copy-start | bytes 1572868
  1.5 1.3 %collective-permute-start = (f32[1,4]{1,0:T(1,128)S(1)}, f32[1,4]{1,0:T(1,128)S(1)}, u32[]{:S(2)}, u32[]{:S(2)}) collective-permute-start(f32[1,4]{1,0:T(1,128)S(1)} %convert_element_type.29), channel_id=1, source_target_pairs={{0,1},{1,0},{2,3},{3,2},{4,5},{5,4},{6,7},{7,6},{8,9},{9,8},{10,11... | collective-permute-start | bytes 56 | tf_op jit(solution)/shard_map/ppermute | solution.py:250
  4.8 23.3 %copy-start.1 = (s32[1,2]{1,0:T(1,128)S(1)}, s32[1,2]{1,0:T(1,128)}, u32[]{:S(2)}) copy-start(s32[1,2]{1,0:T(1,128)} %slot_range.5) | copy-start | bytes 28
  4.8 22.7 %all-to-all-start = ((f32[4,264,128]{2,1,0:T(8,128)}), f32[4,264,128]{2,1,0:T(8,128)S(1)}, u32[]{:S(2)}, u32[]{:S(2)}) async-start(f32[4,264,128]{2,1,0:T(8,128)} %pad_maximum_fusion), calls=%async_computation | async-start | bytes 1081344 | tf_op jit(solution)/shard_map/all_to_all | solution.py:253
  10.0 17.5 %collective-permute-start.1 = (f32[256,256]{1,0:T(8,128)S(1)}, f32[256,256]{1,0:T(8,128)S(1)}, u32[]{:S(2)}, u32[]{:S(2)}) collective-permute-start(f32[256,256]{1,0:T(8,128)S(1)} %dynamic-slice_bitcast_fusion), channel_id=1, source_target_pairs={{0,4},{4,0},{1,5},{5,1},{2,6},{6,2},{3,7},{7,3},{8,12},{12,8},{9,1... | collective-permute-start | bytes 786440 | tf_op jit(solution)/shard_map/ppermute | solution.py:260
  12.1 15.4 %collective-permute-start.5 = (f32[256,128]{1,0:T(8,128)S(1)}, f32[256,128]{1,0:T(8,128)S(1)}, u32[]{:S(2)}, u32[]{:S(2)}) collective-permute-start(f32[256,128]{1,0:T(8,128)S(1)} %get-tuple-element.14), channel_id=1, source_target_pairs={{10,4},{8,6},{18,12},{16,14},{26,20},{24,22},{11,5},{9,7},{19,13},... | collective-permute-start | bytes 393224 | tf_op jit(solution)/shard_map/ppermute | solution.py:258
  12.8 14.7 %collective-permute-start.4 = (f32[256,128]{1,0:T(8,128)S(1)}, f32[256,128]{1,0:T(8,128)S(1)}, u32[]{:S(2)}, u32[]{:S(2)}) collective-permute-start(f32[256,128]{1,0:T(8,128)S(1)} %get-tuple-element.15), channel_id=1, source_target_pairs={{8,4},{10,6},{16,12},{18,14},{24,20},{26,22},{9,5},{11,7},{17,13},... | collective-permute-start | bytes 393224 | tf_op jit(solution)/shard_map/ppermute | solution.py:258
  13.5 14.1 %collective-permute-start.3 = (f32[256,128]{1,0:T(8,128)S(1)}, f32[256,128]{1,0:T(8,128)S(1)}, u32[]{:S(2)}, u32[]{:S(2)}) collective-permute-start(f32[256,128]{1,0:T(8,128)S(1)} %get-tuple-element.16), channel_id=1, source_target_pairs={{10,0},{8,2},{18,8},{16,10},{26,16},{24,18},{11,1},{9,3},{19,9},{1... | collective-permute-start | bytes 393224 | tf_op jit(solution)/shard_map/ppermute | solution.py:258
  14.8 13.4 %collective-permute-start.2 = (f32[256,128]{1,0:T(8,128)S(1)}, f32[256,128]{1,0:T(8,128)S(1)}, u32[]{:S(2)}, u32[]{:S(2)}) collective-permute-start(f32[256,128]{1,0:T(8,128)S(1)} %get-tuple-element.17), channel_id=1, source_target_pairs={{8,0},{10,2},{16,8},{18,10},{24,16},{26,18},{9,1},{11,3},{17,9},{1... | collective-permute-start | bytes 393224 | tf_op jit(solution)/shard_map/ppermute | solution.py:258
  30.1 19.9 %copy-start.2 = (f32[2,256,256]{2,1,0:T(8,128)S(1)}, f32[2,256,256]{2,1,0:T(8,128)}, u32[]{:S(2)}) copy-start(f32[2,256,256]{2,1,0:T(8,128)} %probe.1) | copy-start | bytes 1572868
  30.1 19.9 %copy-start.3 = (bf16[512,256]{1,0:T(8,128)(2,1)S(1)}, bf16[512,256]{1,0:T(8,128)(2,1)}, u32[]{:S(2)}) copy-start(bf16[512,256]{1,0:T(8,128)(2,1)} %constant.48.clone.near_low) | copy-start | bytes 786436
  30.1 19.9 %copy-start.4 = (bf16[512,256]{1,0:T(8,128)(2,1)S(1)}, bf16[512,256]{1,0:T(8,128)(2,1)}, u32[]{:S(2)}) copy-start(bf16[512,256]{1,0:T(8,128)(2,1)} %constant.47.clone.near_high) | copy-start | bytes 786436
  30.1 19.9 %all-to-all-start.1 = ((f32[8,256,128]{2,1,0:T(8,128)}), f32[8,256,128]{2,1,0:T(8,128)S(1)}, u32[]{:S(2)}, u32[]{:S(2)}) async-start(f32[8,256,128]{2,1,0:T(8,128)} %shard_map.104), calls=%async_computation.1 | async-start | bytes 2097152 | tf_op jit(solution)/shard_map/all_to_all | solution.py:265
  50.0 1.0 copy-start.5
  50.9 0.9 copy-start.6
  86.0 4.3 %collective-permute-start.10 = (f32[64,256]{1,0:T(8,128)S(1)}, f32[64,256]{1,0:T(8,128)S(1)}, u32[]{:S(2)}, u32[]{:S(2)}) collective-permute-start(f32[64,256]{1,0:T(8,128)S(1)} %get-tuple-element.13), channel_id=1, source_target_pairs={{0,8},{8,0},{16,24},{24,16},{1,9},{9,1},{17,25},{25,17},{2,10},{10... | collective-permute-start | bytes 196616 | tf_op jit(solution)/shard_map/ppermute | solution.py:236
  90.3 13.5 %collective-permute-start.11 = (f32[64,256]{1,0:T(8,128)S(1)}, f32[64,256]{1,0:T(8,128)S(1)}, u32[]{:S(2)}, u32[]{:S(2)}) collective-permute-start(f32[64,256]{1,0:T(8,128)S(1)} %add.45), channel_id=1, source_target_pairs={{0,16},{8,24},{16,0},{24,8},{1,17},{9,25},{17,1},{25,9},{2,18},{10... | collective-permute-start | bytes 196616 | tf_op jit(solution)/shard_map/ppermute | solution.py:236
  93.0 22.6 %collective-permute-start.8 = (f32[256,128]{1,0:T(8,128)S(1)}, f32[256,128]{1,0:T(8,128)S(1)}, u32[]{:S(2)}, u32[]{:S(2)}) collective-permute-start(f32[256,128]{1,0:T(8,128)S(1)} %get-tuple-element.11), channel_id=1, source_target_pairs={{4,8},{6,10},{12,16},{14,18},{20,24},{22,26},{5,9},{7,11},{13,17},... | collective-permute-start | bytes 393224 | tf_op jit(solution)/shard_map/ppermute | solution.py:287
  93.6 22.0 %collective-permute-start.9 = (f32[256,128]{1,0:T(8,128)S(1)}, f32[256,128]{1,0:T(8,128)S(1)}, u32[]{:S(2)}, u32[]{:S(2)}) collective-permute-start(f32[256,128]{1,0:T(8,128)S(1)} %get-tuple-element.12), channel_id=1, source_target_pairs={{4,10},{6,8},{12,18},{14,16},{20,26},{22,24},{5,11},{7,9},{13,19},... | collective-permute-start | bytes 393224 | tf_op jit(solution)/shard_map/ppermute | solution.py:287
  94.3 21.3 %collective-permute-start.6 = (f32[256,128]{1,0:T(8,128)S(1)}, f32[256,128]{1,0:T(8,128)S(1)}, u32[]{:S(2)}, u32[]{:S(2)}) collective-permute-start(f32[256,128]{1,0:T(8,128)S(1)} %get-tuple-element.11), channel_id=1, source_target_pairs={{0,8},{2,10},{8,16},{10,18},{16,24},{18,26},{1,9},{3,11},{9,17},{1... | collective-permute-start | bytes 393224 | tf_op jit(solution)/shard_map/ppermute | solution.py:287
  97.5 18.2 %collective-permute-start.7 = (f32[256,128]{1,0:T(8,128)S(1)}, f32[256,128]{1,0:T(8,128)S(1)}, u32[]{:S(2)}, u32[]{:S(2)}) collective-permute-start(f32[256,128]{1,0:T(8,128)S(1)} %get-tuple-element.12), channel_id=1, source_target_pairs={{0,10},{2,8},{8,18},{10,16},{16,26},{18,24},{1,11},{3,9},{9,19},{1... | collective-permute-start | bytes 393224 | tf_op jit(solution)/shard_map/ppermute | solution.py:287
  100.3 15.4 %all-to-all-start.3 = ((f32[4,256,128]{2,1,0:T(8,128)}), f32[4,256,128]{2,1,0:T(8,128)S(1)}, u32[]{:S(2)}, u32[]{:S(2)}) async-start(f32[4,256,128]{2,1,0:T(8,128)} %get-tuple-element.10), calls=%async_computation.3 | async-start | bytes 1048576 | tf_op jit(solution)/shard_map/all_to_all | solution.py:288

commit v4 on v3

v4 whole, which is shorter than its diff:
```python
import functools
import math

import jax
import jax.numpy as jnp
import ml_dtypes
import numpy as np
from jax import lax
from jax.experimental import pallas as pl
from jax.experimental.pallas import tpu as pltpu
from jax.sharding import Mesh, PartitionSpec as P

GRAD_WEIGHT = 0.0625
PLANE = ("half", "col", "core")
VMEM_LIMIT = 24 * 1024 * 1024


def tables(width):
    index = np.arange(width, dtype=np.int64)
    scale = 1.0 / math.sqrt(width)
    phase = -2.0 * math.pi / width * (index[:, None] * index[None, :] % width)
    shift = index[:, None] - index[None, :]
    chirp = math.pi / width * (shift * shift % (2 * width)) - math.pi / 4.0
    out = []
    for angle in (phase, chirp):
        real, imag = np.cos(angle) * scale, np.sin(angle) * scale
        table = np.concatenate([-imag, real, imag, real, -imag], axis=0)
        high = table.astype(ml_dtypes.bfloat16)
        low = (table - high.astype(np.float64)).astype(ml_dtypes.bfloat16)
        out.extend([high, low])
    return np.stack(out)


def split(value):
    high = value.astype(jnp.bfloat16)
    low = (value - high.astype(jnp.float32)).astype(jnp.bfloat16)
    return high, low


def dot(left, right):
    return jnp.dot(left, right, preferred_element_type=jnp.float32)


def transform(re, im, tabs, first, conj):
    width = re.shape[0]

    def rows(which, start):
        return tabs[first + which, start * width : (start + 2) * width]

    re_high, re_low = split(re)
    im_high, im_low = split(im)
    high = jnp.concatenate([re_high, im_high], 1)
    both = jnp.concatenate([high, jnp.concatenate([re_low, im_low], 1)], 0)

    def product(start):
        twice = dot(both, rows(0, start))
        return twice[:width] + (twice[width:] + dot(high, rows(1, start)))

    re, im = (product(1), product(0)) if conj else (product(3), product(2))
    by_re, by_im = (3, 2) if conj else (1, 0)
    re_high, re_low = split(re)
    im_high, im_low = split(im)
    out = dot(rows(0, by_re), re_low) + dot(rows(0, by_im), im_low)
    out += dot(rows(1, by_re), re_high) + dot(rows(1, by_im), im_high)
    out += dot(rows(0, by_re), re_high) + dot(rows(0, by_im), im_high)
    return out[:width], out[width:]


def slot_of(half, col, core):
    return 2 * (2 * col + core) + half


def receivers():
    return [slot_of(half, col, core) for half in range(2) for col in range(2) for core in range(2)]


def slot_place(offs, split_at, slot):
    lower = jnp.where(slot >= split_at, 1, 0)
    holder, at = 4 * lower + slot // 2, 2 * (slot % 2)
    return lower, offs[holder, at], offs[holder, at + 1]


def position_kernel(where, slot_range, offs, patch, probe, measured, taken, tabs, grad):
    half, col, core = where[0], where[1], where[2]
    split_at = slot_range[0, 1 - half]
    lower, row_at, col_at = slot_place(offs, split_at, slot_of(half, col, core))
    width = probe.shape[-1]
    rows, band = width // 2, width // 4

    def load(plane):
        return jnp.concatenate([patch[2 * plane], patch[2 * plane + 1]], axis=0)

    def store(plane, value):
        grad[2 * plane, :rows] = value[:rows]
        grad[2 * plane + 1, :rows] = value[rows:]

    def roll(value, rows, cols):
        return pltpu.roll(pltpu.roll(value, rows, 0), cols, 1)

    wave_re, wave_im = roll(probe[0], row_at, col_at), roll(probe[1], row_at, col_at)
    o0_re, o0_im, o1_re, o1_im = load(0), load(2), load(1), load(3)
    exit_re = wave_re * o0_re - wave_im * o0_im
    exit_im = wave_re * o0_im + wave_im * o0_re
    mid_re, mid_im = transform(exit_re, exit_im, tabs, 2, False)
    exit_re = mid_re * o1_re - mid_im * o1_im
    exit_im = mid_re * o1_im + mid_im * o1_re
    far_re, far_im = transform(exit_re, exit_im, tabs, 0, False)
    target = jnp.where(lower == half, measured[0, half], taken[...])
    excess = 2.0 * GRAD_WEIGHT * (far_re * far_re + far_im * far_im - target)
    back_re, back_im = transform(excess * far_re, excess * far_im, tabs, 0, True)
    store(1, mid_re * back_re + mid_im * back_im)
    store(3, mid_re * back_im - mid_im * back_re)
    up_re = o1_re * back_re + o1_im * back_im
    up_im = o1_re * back_im - o1_im * back_re
    back_re, back_im = transform(up_re, up_im, tabs, 2, True)
    wave_re, wave_im = roll(probe[0], row_at, col_at), roll(probe[1], row_at, col_at)
    o0_re, o0_im = load(0), load(2)
    store(0, wave_re * back_re + wave_im * back_im)
    store(2, wave_re * back_im - wave_im * back_re)
    up_re = o0_re * back_re + o0_im * back_im
    up_im = o0_re * back_im - o0_im * back_re
    back_row, back_col = lax.rem(width - row_at, width), lax.rem(2 * width - col_at, width)
    for part, value in enumerate((up_re, up_im)):
        value = roll(value, back_row, back_col)
        for step in range(4):
            grad[4 * part + step, rows:] = value[step * band : (step + 1) * band]


def pick_kernel(where, slot_range, offs, own, below, out):
    rows, lanes = out.shape[1], out.shape[2] // 2
    half, core = where[0], where[2]
    split_at = slot_range[0, 1 - half]
    row_ids = lax.broadcasted_iota(jnp.int32, (rows, lanes), 0) + core * rows
    col_ids = lax.broadcasted_iota(jnp.int32, (rows, lanes), 1)
    for place, slot in enumerate(receivers()):
        lower, row_at, col_at = slot_place(offs, split_at, slot)
        upper_rows = row_ids >= row_at
        for part in range(2):

            def merged(side, lower=lower, upper_rows=upper_rows, part=part):
                at = 2 * side + part
                second = own[4 + at, :rows]
                top = jnp.where(lower == 1, second, own[at, :rows])
                bottom = jnp.where(lower == 1, below[at, :rows], second)
                return jnp.where(upper_rows, top, bottom)

            left_cols = col_ids + part * lanes >= col_at
            out[place, :, part * lanes : (part + 1) * lanes] = jnp.where(left_cols, merged(0), merged(1))


def add_kernel(where, slot_range, offs, parts, own, below, probe_band):
    rows, lanes = own.shape[1], own.shape[2]
    half, core = where[0], where[2]
    split_at = slot_range[0, 1 - half]
    row_ids = lax.broadcasted_iota(jnp.int32, (rows, lanes), 0) + core * rows
    col_ids = lax.broadcasted_iota(jnp.int32, (rows, lanes), 1)
    slots = receivers()
    for strip in range(3):
        for part in range(2):
            sums = [jnp.zeros((rows, lanes), jnp.float32)] * 2
            for place, slot in enumerate(slots):
                lower, row_at, col_at = slot_place(offs, split_at, slot)
                first = jnp.where(strip == lower, row_at, jnp.where(strip == lower + 1, 0, 2 * rows))
                last = jnp.where(strip == lower, 2 * rows, jnp.where(strip == lower + 1, row_at, 0))
                value = parts[place, :rows, part * lanes : (part + 1) * lanes]
                value = jnp.where((row_ids >= first) & (row_ids < last), value, 0.0)
                left = jnp.where(col_ids + part * lanes >= col_at, value, 0.0)
                sums = [sums[0] + left, sums[1] + (value - left)]
            for side in range(2):
                if strip < 2:
                    own[4 * strip + 2 * side + part] = sums[side]
                else:
                    below[2 * side + part] = sums[side]
    total = parts[0, rows:]
    for place in range(1, len(slots)):
        total = total + parts[place, rows:]
    probe_band[...] = total


SMEM = pl.BlockSpec(memory_space=pltpu.SMEM)
VMEM = pl.BlockSpec(memory_space=pltpu.VMEM)


def call(kernel, out_shape, scalars, arrays, flops, **kwargs):
    outs = out_shape if isinstance(out_shape, (list, tuple)) else [out_shape]
    moved = sum(math.prod(x.shape) * x.dtype.itemsize for x in [*arrays, *outs])
    return pl.pallas_call(
        kernel,
        out_shape=out_shape,
        in_specs=[SMEM] * len(scalars) + [VMEM] * len(arrays),
        out_specs=jax.tree.map(lambda unused: VMEM, out_shape),
        compiler_params=pltpu.CompilerParams(vmem_limit_bytes=VMEM_LIMIT),
        cost_estimate=pl.CostEstimate(flops=flops, bytes_accessed=moved, transcendentals=0),
        **kwargs,
    )(*scalars, *arrays)


def shape(*dims):
    return jax.ShapeDtypeStruct(dims, jnp.float32)


def sum_over(value, axis, size):
    if size & (size - 1):
        return lax.psum(value, axis)
    step = 1
    while step < size:
        value = value + lax.ppermute(value, axis, [(k, k ^ step) for k in range(size)])
        step *= 2
    return value


def local(object_field, probe, offsets, slot_range, measured):
    width, cols = probe.shape[-1], object_field.shape[3]
    rows, band = width // 2, width // 4
    pairs = lax.axis_size("pair")
    half, col, core = (lax.axis_index(name) for name in PLANE)
    where = jnp.stack([half, col, core])

    block = object_field.reshape(8, rows, cols)
    places = jnp.pad(offsets.reshape(1, -1, 1).astype(jnp.float32), ((0, 0), (0, 4), (0, 0)))
    places = jnp.broadcast_to(places, (8, places.shape[1], cols))
    own = lax.all_to_all(jnp.concatenate([block, places], axis=1), PLANE, 0, 0, tiled=True)
    given = lax.dynamic_index_in_dim(measured[0], 1 - half, 0, keepdims=False)
    own, given = lax.optimization_barrier((own, given))
    below = lax.ppermute(own[:4], "pair", [(k, k - 1) for k in range(1, pairs)])
    taken = lax.ppermute(given, "half", [(0, 1), (1, 0)])
    below, taken = lax.optimization_barrier((below, taken))

    scalars = (where, slot_range, own[:, rows : rows + 4, 0].astype(jnp.int32))
    parts = call(pick_kernel, shape(8, rows, width), scalars, (own, below), 32 * rows * width)
    patch = lax.all_to_all(parts, PLANE, 0, 0, tiled=True)
    grad = call(
        position_kernel,
        shape(8, rows + band, width),
        scalars,
        (patch, probe, measured, taken, jnp.asarray(tables(width))),
        8 * 24 * width**3,
    )
    got = lax.all_to_all(grad, PLANE, 0, 0, tiled=True)
    sums, lower_sums, probe_band = call(
        add_kernel,
        [shape(8, rows, cols), shape(4, rows, cols), shape(band, width)],
        scalars,
        (got,),
        96 * rows * width,
    )
    above = lax.ppermute(lower_sums, "pair", [(k, k + 1) for k in range(pairs - 1)])
    probe_band = sum_over(probe_band, "pair", pairs)
    total = jnp.concatenate([sums[:4] + above, sums[4:]])
    object_grad = lax.all_to_all(total, PLANE, 0, 0, tiled=True).reshape(object_field.shape)
    probe_grad = lax.all_gather(probe_band, PLANE, axis=0, tiled=True).reshape(probe.shape)
    return (object_grad, probe_grad)


def solution(mesh):
    tile, grp = mesh.shape["tile"], mesh.shape["grp"]
    devices = mesh.devices.reshape(tile // 2, 2, 2, grp // 2)
    inner = Mesh(devices, ("pair", "half", "col", "core"))
    strip, cols = ("pair", "half"), ("col", "core")
    in_specs = (
        P(None, None, strip, cols),
        P(),
        P(strip, cols, None),
        P(strip, None),
        P(strip, cols, None, None),
    )
    out_specs = (P(None, None, strip, cols), P())
    return jax.shard_map(local, mesh=inner, in_specs=in_specs, out_specs=out_specs, check_vma=False)
```

time: 118 us -> 117 us (level)
  blocking collectives: 35.2 us -> 53 us
  starting transfers between devices: 31.1 us -> 19.4 us
  waiting for transfers between devices: 30.7 us -> 27.3 us
  Pallas kernels: 12.6 us -> 10.8 us
    all_to_all x0 -> x1, blocking collectives: none -> 19.7 us  [local(): patch = lax.all_to_all(parts, PLANE, 0, 0, tiled=True)]
    ppermute x1, waiting for transfers between devices: 11.4 us -> 4.21 us  [local(): taken = lax.ppermute(given, 'half', [(0, 1), (1, 0)])]
    ppermute x9 -> x2, starting transfers between devices: 11.7 us -> 4.79 us  [the longest x1 3.5 us: local(): lax.ppermute(lower_sums, 'pair', [(k, k + 1) for k in range(pairs - 1)])]
    ppermute x9 -> x2, waiting for transfers between devices: 1.37 us -> 7.53 us  [the longest x1 4.88 us: local(): lax.ppermute(lower_sums, 'pair', [(k, k + 1) for k in range(pairs - 1)])]
    all_to_all x3 -> x2, waiting for transfers between devices: 15.3 us -> 10.1 us  [the longest x1 10.1 us: local(): lax.all_to_all(jnp.concatenate([block, places], axis=1), PLANE, 0, 0, til...]
    all_to_all x3 -> x2, starting transfers between devices: 13.1 us -> 8.66 us  [the longest x1 5.17 us: local(): lax.all_to_all(jnp.concatenate([block, places], axis=1), PLANE, 0, 0, til...]
    ppermute x2, waiting for transfers between devices: 2.69 us -> 5.45 us  [sum_over(): lax.ppermute(value, axis, [(k, k ^ step) for k in range(size)])]
    all_gather x1, blocking collectives: 11.8 us -> 9.91 us  [local(): lax.all_gather(probe_band, PLANE, axis=0, tiled=True).reshape(probe.shape)]
  transfers between devices with their start and end apart: 15 -> 7, of which waited for: 5 -> 6; matrix products, arithmetic and copies ran while one was open for 0% -> 0% of each run, Pallas kernels for 0% -> 0%
where the time goes in v4:
time: 117 us
  blocking collectives  53 us (45%)
  waiting for transfers between devices  27.3 us (23%)
  starting transfers between devices  19.4 us (17%)
  Pallas kernels  10.8 us (9%)
  other arithmetic  3.68 us (3%)
  local copies, waits for them, and re-layouts  1.93 us (2%)
    all_to_all x1, blocking collectives, local(): got = lax.all_to_all(grad, PLANE, 0, 0, tiled=True)  23.4 us
    all_to_all x1, blocking collectives, local(): patch = lax.all_to_all(parts, PLANE, 0, 0, tiled=True)  19.7 us
    pallas_call x3, Pallas kernels, call(): pl.pallas_call(kernel, out_shape=out_shape, in_specs=[SMEM] * len(scalars...  10.8 us
    all_to_all x1, waiting for transfers between devices, local(): lax.all_to_all(jnp.concatenate([block, places], axis=1), PLANE, 0, 0, til...  10.1 us
    all_gather x1, blocking collectives, local(): lax.all_gather(probe_band, PLANE, axis=0, tiled=True).reshape(probe.shape)  9.91 us
    ppermute x2, waiting for transfers between devices, sum_over(): lax.ppermute(value, axis, [(k, k ^ step) for k in range(size)])  5.45 us
    ppermute x2, starting transfers between devices, sum_over(): lax.ppermute(value, axis, [(k, k ^ step) for k in range(size)])  5.37 us
    all_to_all x1, starting transfers between devices, local(): lax.all_to_all(jnp.concatenate([block, places], axis=1), PLANE, 0, 0, til...  5.17 us
  transfers between devices with their start and end apart: 7, of which 6 were waited for; matrix products, arithmetic and copies ran while one was open for 0% of the time, Pallas kernels for 0%

profile of v4, /device:TPU:0, one launch (start us, length us, event | category | flops | bytes accessed | tf_op | source)
XLA Modules:
  0.0 116.8 jit_solution(9115172690000517119)
XLA Ops:
  0.6 0.0 copy-start
  0.6 0.7 convert_element_type.21
  1.4 0.1 convert_element_type.22
  1.5 0.0 copy-start.1
  1.5 2.0 %pad_maximum_fusion = f32[8,136,128]{2,1,0:T(8,128)} fusion(f32[8,128,128]{2,1,0:T(8,128)} %bitcast.13, f32[136]{0:T(256)S(1)} %pad.8.clone), kind=kLoop, calls=%fused_computation | loop fusion | flops 139264 | bytes 1081888 | tf_op jit(solution)/shard_map/concatenate | solution.py:222
  3.4 5.2 %all-to-all-start = ((f32[8,136,128]{2,1,0:T(8,128)}), f32[8,136,128]{2,1,0:T(8,128)S(1)}, u32[]{:S(2)}, u32[]{:S(2)}) async-start(f32[8,136,128]{2,1,0:T(8,128)} %pad_maximum_fusion), calls=%async_computation | async-start | bytes 1114112 | tf_op jit(solution)/shard_map/all_to_all | solution.py:222
  8.6 0.0 copy-done
  8.7 10.1 %all-to-all-done.own = f32[8,136,128]{2,1,0:T(8,128)S(1)} async-done(((f32[8,136,128]{2,1,0:T(8,128)}), f32[8,136,128]{2,1,0:T(8,128)S(1)}, u32[]{:S(2)}, u32[]{:S(2)}) %all-to-all-start) | async-done | bytes 557088 | tf_op jit(solution)/shard_map/all_to_all | solution.py:222
  18.7 0.6 collective-permute-start.1
  19.3 1.3 %collective-permute-start = (f32[4,136,128]{2,1,0:T(8,128)S(1)}, f32[4,136,128]{2,1,0:T(8,128)S(1)}, u32[]{:S(2)}, u32[]{:S(2)}) collective-permute-start(f32[4,136,128]{2,1,0:T(8,128)S(1)} %slice.13), channel_id=1, source_target_pairs={{8,0},{16,8},{24,16},{9,1},{17,9},{25,17},{10,2},{18,10},{26,18},{... | collective-permute-start | bytes 835592 | tf_op jit(solution)/shard_map/ppermute | solution.py:225
  20.6 0.1 pad_add_fusion.where
  20.7 0.1 copy.12
  20.8 0.1 copy.15.offs
  20.9 0.0 copy-start.2
  20.9 0.0 copy-start.3
  20.9 4.2 %collective-permute-done.1.taken = f32[256,256]{1,0:T(8,128)S(1)} collective-permute-done((f32[256,256]{1,0:T(8,128)S(1)}, f32[256,256]{1,0:T(8,128)S(1)}, u32[]{:S(2)}, u32[]{:S(2)}) %collective-permute-start.1) | collective-permute-done | bytes 262176 | tf_op jit(solution)/shard_map/ppermute | solution.py:226
  25.1 2.6 %collective-permute-done.below = f32[4,136,128]{2,1,0:T(8,128)S(1)} collective-permute-done((f32[4,136,128]{2,1,0:T(8,128)S(1)}, f32[4,136,128]{2,1,0:T(8,128)S(1)}, u32[]{:S(2)}, u32[]{:S(2)}) %collective-permute-start) | collective-permute-done | bytes 278560 | tf_op jit(solution)/shard_map/ppermute | solution.py:225
  27.7 0.0 copy-done.1
  27.7 1.0 shard_map.77
  28.7 19.7 %all_to_all.20.patch = f32[8,128,256]{2,1,0:T(8,128)S(1)} all-to-all(f32[8,128,256]{2,1,0:T(8,128)S(1)} %shard_map.77), channel_id=1, replica_groups=mesh['pair'=4,'half'=2,'col'=2,'core'=2] {'half','col','core'}, dimensions={0} | all-to-all | bytes 2097152 | tf_op jit(solution)/shard_map/all_to_all | solution.py:231
  48.4 0.0 copy-done.2
  48.4 0.0 copy-done.3
  48.4 8.3 %shard_map.78 = f32[8,192,256]{2,1,0:T(8,128)S(1)} custom-call(s32[3]{0:T(128)S(1)} %pad_add_fusion.where, s32[1,2]{1,0:T(1,128)S(1)} %copy-done.1, s32[8,4]{1,0:T(8,128)S(1)} %copy.15.offs, f32[8,128,256]{2,1,0:T(8,128)S(1)} %all_to_all.20.patch, f32[2,256,256]{2,1,0:T(8,128)S(1)} %copy-done.2, f32[1,2,256,256]{3,2,1,0:T(8,128)S(1)} %copy-done, ...), custom_call_target="tpu_custom_call" | custom-call | flops 3221225472 | bytes 6553600 | tf_op jit(solution)/shard_map/pallas_call | solution.py:187
  56.7 23.4 %all_to_all.21.parts = f32[8,192,256]{2,1,0:T(8,128)S(1)} all-to-all(f32[8,192,256]{2,1,0:T(8,128)S(1)} %shard_map.78), channel_id=1, replica_groups=mesh['pair'=4,'half'=2,'col'=2,'core'=2] {'half','col','core'}, dimensions={0} | all-to-all | bytes 3145728 | tf_op jit(solution)/shard_map/all_to_all | solution.py:239
  80.1 1.5 %shard_map.79 = (f32[8,128,128]{2,1,0:T(8,128)S(1)}, f32[4,128,128]{2,1,0:T(8,128)S(1)}, f32[64,256]{1,0:T(8,128)S(1)}) custom-call(s32[3]{0:T(128)S(1)} %pad_add_fusion.where, s32[1,2]{1,0:T(1,128)S(1)} %copy-done.1, s32[8,4]{1,0:T(8,128)S(1)} %copy.15.offs, f32[8,192,256]{2,1,0:T(8,128)S(1)} %all_to_all.21.parts), custom_call_target="tpu_custom_call" | custom-call | flops 3145728 | bytes 2424832 | tf_op jit(solution)/shard_map/pallas_call | solution.py:187
  81.7 3.5 %collective-permute-start.2 = (f32[4,128,128]{2,1,0:T(8,128)S(1)}, f32[4,128,128]{2,1,0:T(8,128)S(1)}, u32[]{:S(2)}, u32[]{:S(2)}) collective-permute-start(f32[4,128,128]{2,1,0:T(8,128)S(1)} %get-tuple-element.14), channel_id=1, source_target_pairs={{0,8},{8,16},{16,24},{1,9},{9,17},{17,25},{2,10},{10,18},{18,26},{... | collective-permute-start | bytes 786440 | tf_op jit(solution)/shard_map/ppermute | solution.py:247
  85.2 4.9 %collective-permute-done.2 = f32[4,128,128]{2,1,0:T(8,128)S(1)} collective-permute-done((f32[4,128,128]{2,1,0:T(8,128)S(1)}, f32[4,128,128]{2,1,0:T(8,128)S(1)}, u32[]{:S(2)}, u32[]{:S(2)}) %collective-permute-start.2) | collective-permute-done | bytes 262176 | tf_op jit(solution)/shard_map/ppermute | solution.py:247
  90.1 0.1 slice_add_fusion
  90.1 0.8 pad_maximum_fusion.1
  90.9 3.5 %all-to-all-start.3 = ((f32[8,128,128]{2,1,0:T(8,128)}), f32[8,128,128]{2,1,0:T(8,128)S(1)}, u32[]{:S(2)}, u32[]{:S(2)}) async-start(f32[8,128,128]{2,1,0:T(8,128)} %pad_maximum_fusion.1), calls=%async_computation.3 | async-start | bytes 1048576 | tf_op jit(solution)/shard_map/all_to_all | solution.py:250
  94.5 2.5 %collective-permute-start.3 = (f32[64,256]{1,0:T(8,128)S(1)}, f32[64,256]{1,0:T(8,128)S(1)}, u32[]{:S(2)}, u32[]{:S(2)}) collective-permute-start(f32[64,256]{1,0:T(8,128)S(1)} %get-tuple-element.15), channel_id=1, source_target_pairs={{0,8},{8,0},{16,24},{24,16},{1,9},{9,1},{17,25},{25,17},{2,10},{10... | collective-permute-start | bytes 196616 | tf_op jit(solution)/shard_map/ppermute | solution.py:207
  97.0 2.6 %collective-permute-done.3 = f32[64,256]{1,0:T(8,128)S(1)} collective-permute-done((f32[64,256]{1,0:T(8,128)S(1)}, f32[64,256]{1,0:T(8,128)S(1)}, u32[]{:S(2)}, u32[]{:S(2)}) %collective-permute-start.3) | collective-permute-done | bytes 65568 | tf_op jit(solution)/shard_map/ppermute | solution.py:207
  99.6 2.8 %collective-permute-start.4 = (f32[64,256]{1,0:T(8,128)S(1)}, f32[64,256]{1,0:T(8,128)S(1)}, u32[]{:S(2)}, u32[]{:S(2)}) collective-permute-start(f32[64,256]{1,0:T(8,128)S(1)} %add.18), channel_id=1, source_target_pairs={{0,16},{8,24},{16,0},{24,8},{1,17},{9,25},{17,1},{25,9},{2,18},{10... | collective-permute-start | bytes 196616 | tf_op jit(solution)/shard_map/ppermute | solution.py:207
  102.4 2.9 %collective-permute-done.4 = f32[64,256]{1,0:T(8,128)S(1)} collective-permute-done((f32[64,256]{1,0:T(8,128)S(1)}, f32[64,256]{1,0:T(8,128)S(1)}, u32[]{:S(2)}, u32[]{:S(2)}) %collective-permute-start.4) | collective-permute-done | bytes 65568 | tf_op jit(solution)/shard_map/ppermute | solution.py:207
  105.3 9.9 %all_gather.3 = f32[512,256]{1,0:T(8,128)S(1)} all-gather(f32[64,256]{1,0:T(8,128)S(1)} %add.19), channel_id=1, replica_groups=mesh['pair'=4,'half'=2,'col'=2,'core'=2] {'half','col','core'}, dimensions={0}, use_global_device_ids=true | all-gather | bytes 589824 | tf_op jit(solution)/shard_map/all_gather | solution.py:251
  115.2 0.0 all-to-all-done.3
  115.2 0.8 copy.18
  116.0 0.8 copy.19
  (7 shorter events, 0.1 us)
Async XLA Ops:
  0.6 8.0 %copy-start = (f32[1,2,256,256]{3,2,1,0:T(8,128)S(1)}, f32[1,2,256,256]{3,2,1,0:T(8,128)}, u32[]{:S(2)}) copy-start(f32[1,2,256,256]{3,2,1,0:T(8,128)} %measured.1) | copy-start | bytes 1572868
  1.5 26.3 %copy-start.1 = (s32[1,2]{1,0:T(1,128)S(1)}, s32[1,2]{1,0:T(1,128)}, u32[]{:S(2)}) copy-start(s32[1,2]{1,0:T(1,128)} %slot_range.5) | copy-start | bytes 28
  3.4 15.3 %all-to-all-start = ((f32[8,136,128]{2,1,0:T(8,128)}), f32[8,136,128]{2,1,0:T(8,128)S(1)}, u32[]{:S(2)}, u32[]{:S(2)}) async-start(f32[8,136,128]{2,1,0:T(8,128)} %pad_maximum_fusion), calls=%async_computation | async-start | bytes 1114112 | tf_op jit(solution)/shard_map/all_to_all | solution.py:222
  18.7 6.4 %collective-permute-start.1 = (f32[256,256]{1,0:T(8,128)S(1)}, f32[256,256]{1,0:T(8,128)S(1)}, u32[]{:S(2)}, u32[]{:S(2)}) collective-permute-start(f32[256,256]{1,0:T(8,128)S(1)} %dynamic-slice_bitcast_fusion), channel_id=1, source_target_pairs={{0,4},{4,0},{1,5},{5,1},{2,6},{6,2},{3,7},{7,3},{8,12},{12,8},{9,1... | collective-permute-start | bytes 786440 | tf_op jit(solution)/shard_map/ppermute | solution.py:226
  19.3 8.4 %collective-permute-start = (f32[4,136,128]{2,1,0:T(8,128)S(1)}, f32[4,136,128]{2,1,0:T(8,128)S(1)}, u32[]{:S(2)}, u32[]{:S(2)}) collective-permute-start(f32[4,136,128]{2,1,0:T(8,128)S(1)} %slice.13), channel_id=1, source_target_pairs={{8,0},{16,8},{24,16},{9,1},{17,9},{25,17},{10,2},{18,10},{26,18},{... | collective-permute-start | bytes 835592 | tf_op jit(solution)/shard_map/ppermute | solution.py:225
  20.9 27.5 %copy-start.2 = (f32[2,256,256]{2,1,0:T(8,128)S(1)}, f32[2,256,256]{2,1,0:T(8,128)}, u32[]{:S(2)}) copy-start(f32[2,256,256]{2,1,0:T(8,128)} %probe.1) | copy-start | bytes 1572868
  20.9 27.5 %copy-start.3 = (bf16[4,1280,256]{2,1,0:T(8,128)(2,1)S(1)}, bf16[4,1280,256]{2,1,0:T(8,128)(2,1)}, u32[]{:S(2)}) copy-start(bf16[4,1280,256]{2,1,0:T(8,128)(2,1)} %constant.25.clone.tabs) | copy-start | bytes 7864324
  81.7 8.4 %collective-permute-start.2 = (f32[4,128,128]{2,1,0:T(8,128)S(1)}, f32[4,128,128]{2,1,0:T(8,128)S(1)}, u32[]{:S(2)}, u32[]{:S(2)}) collective-permute-start(f32[4,128,128]{2,1,0:T(8,128)S(1)} %get-tuple-element.14), channel_id=1, source_target_pairs={{0,8},{8,16},{16,24},{1,9},{9,17},{17,25},{2,10},{10,18},{18,26},{... | collective-permute-start | bytes 786440 | tf_op jit(solution)/shard_map/ppermute | solution.py:247
  90.9 24.3 %all-to-all-start.3 = ((f32[8,128,128]{2,1,0:T(8,128)}), f32[8,128,128]{2,1,0:T(8,128)S(1)}, u32[]{:S(2)}, u32[]{:S(2)}) async-start(f32[8,128,128]{2,1,0:T(8,128)} %pad_maximum_fusion.1), calls=%async_computation.3 | async-start | bytes 1048576 | tf_op jit(solution)/shard_map/all_to_all | solution.py:250
  94.5 5.1 %collective-permute-start.3 = (f32[64,256]{1,0:T(8,128)S(1)}, f32[64,256]{1,0:T(8,128)S(1)}, u32[]{:S(2)}, u32[]{:S(2)}) collective-permute-start(f32[64,256]{1,0:T(8,128)S(1)} %get-tuple-element.15), channel_id=1, source_target_pairs={{0,8},{8,0},{16,24},{24,16},{1,9},{9,1},{17,25},{25,17},{2,10},{10... | collective-permute-start | bytes 196616 | tf_op jit(solution)/shard_map/ppermute | solution.py:207
  99.6 5.7 %collective-permute-start.4 = (f32[64,256]{1,0:T(8,128)S(1)}, f32[64,256]{1,0:T(8,128)S(1)}, u32[]{:S(2)}, u32[]{:S(2)}) collective-permute-start(f32[64,256]{1,0:T(8,128)S(1)} %add.18), channel_id=1, source_target_pairs={{0,16},{8,24},{16,0},{24,8},{1,17},{9,25},{17,1},{25,9},{2,18},{10... | collective-permute-start | bytes 196616 | tf_op jit(solution)/shard_map/ppermute | solution.py:207

commit v5 on v4

v5 whole, which is shorter than its diff:
```python
import functools
import math

import jax
import jax.numpy as jnp
import ml_dtypes
import numpy as np
from jax import lax
from jax.experimental import pallas as pl
from jax.experimental.pallas import tpu as pltpu
from jax.sharding import Mesh, PartitionSpec as P

GRAD_WEIGHT = 0.0625
PLANE = ("half", "col", "core")
AROUND = ("pair", "half", "col")
VMEM_LIMIT = 24 * 1024 * 1024


def tables(width):
    index = np.arange(width, dtype=np.int64)
    scale = 1.0 / math.sqrt(width)
    phase = -2.0 * math.pi / width * (index[:, None] * index[None, :] % width)
    shift = index[:, None] - index[None, :]
    chirp = math.pi / width * (shift * shift % (2 * width)) - math.pi / 4.0
    out = []
    for angle in (phase, chirp):
        real, imag = np.cos(angle) * scale, np.sin(angle) * scale
        table = np.concatenate([-imag, real, imag, real, -imag], axis=0)
        high = table.astype(ml_dtypes.bfloat16)
        low = (table - high.astype(np.float64)).astype(ml_dtypes.bfloat16)
        out.extend([high, low])
    return np.stack(out)


def split(value):
    high = value.astype(jnp.bfloat16)
    low = (value - high.astype(jnp.float32)).astype(jnp.bfloat16)
    return high, low


def dot(left, right):
    return jnp.dot(left, right, preferred_element_type=jnp.float32)


def transform(re, im, tabs, first, conj):
    width = re.shape[0]

    def rows(which, start):
        return tabs[first + which, start * width : (start + 2) * width]

    re_high, re_low = split(re)
    im_high, im_low = split(im)
    high = jnp.concatenate([re_high, im_high], 1)
    both = jnp.concatenate([high, jnp.concatenate([re_low, im_low], 1)], 0)

    def product(start):
        twice = dot(both, rows(0, start))
        return twice[:width] + (twice[width:] + dot(high, rows(1, start)))

    re, im = (product(1), product(0)) if conj else (product(3), product(2))
    by_re, by_im = (3, 2) if conj else (1, 0)
    re_high, re_low = split(re)
    im_high, im_low = split(im)
    out = dot(rows(0, by_re), re_low) + dot(rows(0, by_im), im_low)
    out += dot(rows(1, by_re), re_high) + dot(rows(1, by_im), im_high)
    out += dot(rows(0, by_re), re_high) + dot(rows(0, by_im), im_high)
    return out[:width], out[width:]


def slot_of(half, col, core):
    return 2 * (2 * col + core) + half


def receivers():
    return [slot_of(half, col, core) for half in range(2) for col in range(2) for core in range(2)]


def slot_place(offs, mine, split_at, slot):
    lower = jnp.where(slot >= split_at, 1, 0)
    holder, at = jnp.bitwise_xor(2 * lower + slot // 4, mine), 2 * (slot % 4)
    return lower, offs[holder, at], offs[holder, at + 1]


def deal_kernel(where, offsets, sibling, block, *outs):
    mine, core = 2 * where[0] + where[1], where[2]
    rows, cols = block.shape[1:]
    lines = []
    for holder in range(2):
        for slot in range(2):
            for axis in range(2):
                value = jnp.where(core == holder, offsets[0, slot, axis], sibling[0, slot, axis])
                lines.append(jnp.full((1, cols), value, jnp.int32))
    lines = jnp.concatenate(lines, axis=0).astype(jnp.float32)
    for turn, out in enumerate(outs):
        out[:rows] = block[jnp.bitwise_xor(mine, turn)]
        out[rows:] = lines


def pick_kernel(where, slot_range, *refs):
    gotten, lower_planes, outs, (own, below, parts) = refs[:4], refs[4:8], refs[8:16], refs[16:]
    rows, cols = outs[0].shape
    half, col, core = where[0], where[1], where[2]
    mine = 2 * half + col
    for turn in range(4):
        own[jnp.bitwise_xor(mine, turn)] = gotten[turn][...]
    for turn in range(2):
        plane = jnp.where(half == 0, lower_planes[turn][:rows], lower_planes[2 + turn][:rows])
        below[jnp.bitwise_xor(col, turn)] = plane
    split_at = slot_range[0, 1 - half]
    row_ids = lax.broadcasted_iota(jnp.int32, (rows, cols), 0).astype(jnp.float32)
    col_ids = (lax.broadcasted_iota(jnp.int32, (rows, cols), 1) + core * cols).astype(jnp.float32)
    for place, slot in enumerate(receivers()):
        lower = jnp.where(slot >= split_at, 1, 0)
        at = rows + 2 * (slot % 4)
        offs = own[2 * lower + slot // 4, at : at + 2]
        upper_rows = row_ids >= offs[0:1]
        left_cols = col_ids >= offs[1:2]

        def merged(side, lower=lower, upper_rows=upper_rows):
            second = own[2 + side, :rows]
            top = jnp.where(lower == 1, second, own[side, :rows])
            bottom = jnp.where(lower == 1, below[side], second)
            return jnp.where(upper_rows, top, bottom)

        parts[place] = jnp.where(left_cols, merged(0), merged(1))
    for turn, out in enumerate(outs):
        out[...] = parts[jnp.bitwise_xor(2 * mine + core, turn)]


def position_kernel(where, slot_range, offs, *refs):
    gotten, (probe, measured, taken, tabs), outs, (patch, grad) = refs[:8], refs[8:12], refs[12:20], refs[20:]
    half, col, core = where[0], where[1], where[2]
    mine = 2 * half + col
    flat = 2 * mine + core
    lower, row_at, col_at = slot_place(offs, mine, slot_range[0, 1 - half], slot_of(half, col, core))
    width = probe.shape[-1]
    lanes, band = width // 2, width // 4
    for turn in range(8):
        patch[jnp.bitwise_xor(flat, turn)] = gotten[turn][...]

    def load(plane):
        return jnp.concatenate([patch[2 * plane], patch[2 * plane + 1]], axis=1)

    def store(plane, value):
        grad[2 * plane, :width] = value[:, :lanes]
        grad[2 * plane + 1, :width] = value[:, lanes:]

    def roll(value, rows, cols):
        return pltpu.roll(pltpu.roll(value, rows, 0), cols, 1)

    wave_re, wave_im = roll(probe[0], row_at, col_at), roll(probe[1], row_at, col_at)
    o0_re, o0_im, o1_re, o1_im = load(0), load(2), load(1), load(3)
    exit_re = wave_re * o0_re - wave_im * o0_im
    exit_im = wave_re * o0_im + wave_im * o0_re
    mid_re, mid_im = transform(exit_re, exit_im, tabs, 2, False)
    exit_re = mid_re * o1_re - mid_im * o1_im
    exit_im = mid_re * o1_im + mid_im * o1_re
    far_re, far_im = transform(exit_re, exit_im, tabs, 0, False)
    target = jnp.where(lower == half, measured[0, half], taken[...])
    excess = 2.0 * GRAD_WEIGHT * (far_re * far_re + far_im * far_im - target)
    back_re, back_im = transform(excess * far_re, excess * far_im, tabs, 0, True)
    store(1, mid_re * back_re + mid_im * back_im)
    store(3, mid_re * back_im - mid_im * back_re)
    up_re = o1_re * back_re + o1_im * back_im
    up_im = o1_re * back_im - o1_im * back_re
    back_re, back_im = transform(up_re, up_im, tabs, 2, True)
    wave_re, wave_im = roll(probe[0], row_at, col_at), roll(probe[1], row_at, col_at)
    o0_re, o0_im = load(0), load(2)
    store(0, wave_re * back_re + wave_im * back_im)
    store(2, wave_re * back_im - wave_im * back_re)
    up_re = o0_re * back_re + o0_im * back_im
    up_im = o0_re * back_im - o0_im * back_re
    back_row, back_col = lax.rem(width - row_at, width), lax.rem(2 * width - col_at, width)
    for part, value in enumerate((up_re, up_im)):
        value = roll(value, back_row, back_col)
        for step in range(4):
            rows = value[step * band : (step + 1) * band]
            grad[4 * part + step, width : width + band] = rows[:, :lanes]
            grad[4 * part + step, width + band :] = rows[:, lanes:]
    for turn, out in enumerate(outs):
        out[...] = grad[jnp.bitwise_xor(flat, turn)]


def add_kernel(where, slot_range, offs, *refs):
    parts, outs, below, probe_band, own = refs[:8], refs[8:12], refs[12:14], refs[14], refs[15]
    rows, cols = outs[0].shape
    half, col, core = where[0], where[1], where[2]
    mine = 2 * half + col
    split_at = slot_range[0, 1 - half]
    row_ids = lax.broadcasted_iota(jnp.int32, (rows, cols), 0)
    col_ids = lax.broadcasted_iota(jnp.int32, (rows, cols), 1) + core * cols
    places = []
    for turn in range(8):
        flat = jnp.bitwise_xor(2 * mine + core, turn)
        slot = slot_of(flat // 4, (flat // 2) % 2, flat % 2)
        places.append(slot_place(offs, mine, split_at, slot))
    for strip in range(3):
        sums = [jnp.zeros((rows, cols), jnp.float32)] * 2
        for part, (lower, row_at, col_at) in zip(parts, places):
            first = jnp.where(strip == lower, row_at, jnp.where(strip == lower + 1, 0, rows))
            last = jnp.where(strip == lower, rows, jnp.where(strip == lower + 1, row_at, 0))
            value = jnp.where((row_ids >= first) & (row_ids < last), part[:rows], 0.0)
            left = jnp.where(col_ids >= col_at, value, 0.0)
            sums = [sums[0] + left, sums[1] + (value - left)]
        if strip < 2:
            own[2 * strip], own[2 * strip + 1] = sums
        else:
            below[0][...] = jnp.where(col == 0, sums[0], sums[1])
            below[1][...] = jnp.where(col == 0, sums[1], sums[0])
    for turn, out in enumerate(outs):
        out[...] = own[jnp.bitwise_xor(mine, turn)]
    total = parts[0][rows:]
    for part in parts[1:]:
        total = total + part[rows:]
    band = probe_band.shape[0]
    probe_band[:, :cols] = total[:band]
    probe_band[:, cols:] = total[band:]


def join_kernel(where, *refs):
    mine = 2 * where[0] + where[1]
    for turn in range(4):
        refs[8][jnp.bitwise_xor(mine, turn)] = refs[turn][...] + refs[4 + turn][...]


SMEM = pl.BlockSpec(memory_space=pltpu.SMEM)
VMEM = pl.BlockSpec(memory_space=pltpu.VMEM)


def call(kernel, out_shape, scalars, arrays, flops, scratch=()):
    outs = out_shape if isinstance(out_shape, (list, tuple)) else [out_shape]
    moved = sum(math.prod(x.shape) * x.dtype.itemsize for x in [*arrays, *outs])
    return pl.pallas_call(
        kernel,
        out_shape=out_shape,
        in_specs=[SMEM] * len(scalars) + [VMEM] * len(arrays),
        out_specs=jax.tree.map(lambda unused: VMEM, out_shape),
        compiler_params=pltpu.CompilerParams(vmem_limit_bytes=VMEM_LIMIT),
        cost_estimate=pl.CostEstimate(flops=flops, bytes_accessed=moved, transcendentals=0),
        scratch_shapes=[pltpu.VMEM(dims, jnp.float32) for dims in scratch],
    )(*scalars, *arrays)


def shape(*dims):
    return jax.ShapeDtypeStruct(dims, jnp.float32)


def sum_over(value, axis, size):
    if size & (size - 1):
        return lax.psum(value, axis)
    step = 1
    while step < size:
        value = value + lax.ppermute(value, axis, [(k, k ^ step) for k in range(size)])
        step *= 2
    return value


def deal(values, axes):
    count = len(values)
    return [
        value if turn == 0 else lax.ppermute(value, axes, [(k, k ^ turn) for k in range(count)])
        for turn, value in enumerate(values)
    ]


def shift_pairs(pairs, step, half, turn):
    out = []
    for pair in range(pairs - 1):
        for col in range(2):
            lower, upper = 4 * (pair + 1) + (col ^ turn), 4 * pair + 2 * half + col
            out.append((lower, upper) if step == 1 else (upper, lower))
    return out


def local(object_field, probe, offsets, slot_range, measured):
    width = probe.shape[-1]
    planes, rows, cols = 4, object_field.shape[2], object_field.shape[3]
    band = width // 4
    pairs = lax.axis_size("pair")
    half, col, core = (lax.axis_index(name) for name in PLANE)
    where = jnp.stack([half, col, core])

    sibling = lax.ppermute(offsets, "core", [(0, 1), (1, 0)])
    block = object_field.reshape(planes, rows, cols)
    dealt = call(deal_kernel, [shape(rows + 8, cols)] * 4, (where, offsets, sibling), (block,), 0)
    given = lax.dynamic_index_in_dim(measured[0], 1 - half, 0, keepdims=False)
    below = []
    for turn in range(4):
        below.append(lax.ppermute(dealt[turn], AROUND, shift_pairs(pairs, 1, turn // 2, turn % 2)))
    own = deal(dealt, PLANE[:2])
    taken = lax.ppermute(given, "half", [(0, 1), (1, 0)])
    own[0], taken = lax.optimization_barrier((own[0], taken))

    parts = call(
        pick_kernel,
        [shape(rows, cols)] * 8,
        (where, slot_range),
        (*own, *below),
        32 * rows * width,
        [(planes, rows + 8, cols), (2, rows, cols), (8, rows, cols)],
    )
    scalars = (where, slot_range, jnp.stack([value[rows:, 0] for value in own]).astype(jnp.int32))
    grad = call(
        position_kernel,
        [shape(rows + 2 * band, cols)] * 8,
        scalars,
        (*deal(parts, PLANE), probe, measured, taken, jnp.asarray(tables(width))),
        8 * 24 * width**3,
        [(8, rows, cols), (8, rows + 2 * band, cols)],
    )
    *sums, lower0, lower1, probe_band = call(
        add_kernel,
        [shape(rows, cols)] * 6 + [shape(band, width)],
        scalars,
        deal(grad, PLANE),
        96 * rows * width,
        [(planes, rows, cols)],
    )
    above = []
    for turn in range(4):
        lower = (lower0, lower1)[turn % 2]
        above.append(lax.ppermute(lower, AROUND, shift_pairs(pairs, -1, turn // 2, turn % 2)))
    sums = deal(sums, PLANE[:2])
    probe_band = sum_over(probe_band, "pair", pairs)
    probe_grad = lax.all_gather(probe_band, PLANE, axis=0, tiled=True).reshape(probe.shape)
    object_grad = call(join_kernel, shape(planes, rows, cols), (where,), (*sums, *above), planes * rows * cols)
    return (object_grad.reshape(object_field.shape), probe_grad)


def solution(mesh):
    tile, grp = mesh.shape["tile"], mesh.shape["grp"]
    devices = mesh.devices.reshape(tile // 2, 2, 2, grp // 2)
    inner = Mesh(devices, ("pair", "half", "col", "core"))
    strip, cols = ("pair", "half"), ("col", "core")
    in_specs = (
        P(None, None, strip, cols),
        P(),
        P(strip, cols, None),
        P(strip, None),
        P(strip, cols, None, None),
    )
    out_specs = (P(None, None, strip, cols), P())
    return jax.shard_map(local, mesh=inner, in_specs=in_specs, out_specs=out_specs, check_vma=False)
```

time: 117 us -> 112 us (0.957)
  blocking collectives: 53 us -> 9.93 us
  starting transfers between devices: 19.4 us -> 45.2 us
  local copies, waits for them, and re-layouts: 1.93 us -> 9.07 us
  waiting for transfers between devices: 27.3 us -> 32.7 us
  other arithmetic: 3.68 us -> 0.11 us
  Pallas kernels: 10.8 us -> 13.8 us
    all_to_all x2 -> x0, blocking collectives: 43.1 us -> none  [the longest x1 23.4 us: local(): got = lax.all_to_all(grad, PLANE, 0, 0, tiled=True)]
    ppermute x2 -> x29, starting transfers between devices: 4.79 us -> 38.6 us  [the longest x20 25.7 us: deal(): lax.ppermute(value, axes, [(k, k ^ turn) for k in range(count)])]
    ppermute x2 -> x29, waiting for transfers between devices: 7.53 us -> 32.7 us  [the longest x20 28.7 us: deal(): lax.ppermute(value, axes, [(k, k ^ turn) for k in range(count)])]
    all_to_all x2 -> x0, waiting for transfers between devices: 10.1 us -> none  [the longest x1 10.1 us: local(): lax.all_to_all(jnp.concatenate([block, places], axis=1), PLANE, 0, 0, til...]
    all_to_all x2 -> x0, starting transfers between devices: 8.66 us -> none  [the longest x1 5.17 us: local(): lax.all_to_all(jnp.concatenate([block, places], axis=1), PLANE, 0, 0, til...]
    unnamed x10 -> x15, local copies, waits for them, and re-layouts: 1.6 us -> 7.65 us
    ppermute x2, waiting for transfers between devices: 5.45 us -> 0.01 us  [sum_over(): lax.ppermute(value, axis, [(k, k ^ step) for k in range(size)])]
    ppermute x1, waiting for transfers between devices: 4.21 us -> 0.01 us  [local(): taken = lax.ppermute(given, 'half', [(0, 1), (1, 0)])]
  transfers between devices with their start and end apart: 7 -> 32, of which waited for: 6 -> 8; matrix products, arithmetic and copies ran while one was open for 0% -> 1% of each run, Pallas kernels for 0% -> 1%
where the time goes in v5:
time: 112 us
  starting transfers between devices  45.2 us (40%)
  waiting for transfers between devices  32.7 us (29%)
  Pallas kernels  13.8 us (12%)
  blocking collectives  9.93 us (9%)
  local copies, waits for them, and re-layouts  9.07 us (8%)
    ppermute x20, waiting for transfers between devices, deal(): lax.ppermute(value, axes, [(k, k ^ turn) for k in range(count)])  28.7 us
    ppermute x20, starting transfers between devices, deal(): lax.ppermute(value, axes, [(k, k ^ turn) for k in range(count)])  25.7 us
    pallas_call x5, Pallas kernels, call(): pl.pallas_call(kernel, out_shape=out_shape, in_specs=[SMEM] * len(scalars...  13.8 us
    all_gather x1, blocking collectives, local(): lax.all_gather(probe_band, PLANE, axis=0, tiled=True).reshape(probe.shape)  9.93 us
    ppermute x4, starting transfers between devices, local(): lax.ppermute(lower, AROUND, shift_pairs(pairs, -1, turn // 2, turn % 2))  8.97 us
    unnamed x15, local copies, waits for them, and re-layouts  7.65 us
    ppermute x4, starting transfers between devices, local(): lax.ppermute(dealt[turn], AROUND, shift_pairs(pairs, 1, turn // 2, turn %...  3.9 us
    ppermute x2, starting transfers between devices, sum_over(): lax.ppermute(value, axis, [(k, k ^ step) for k in range(size)])  3.6 us
  transfers between devices with their start and end apart: 32, of which 8 were waited for; matrix products, arithmetic and copies ran while one was open for 1% of the time, Pallas kernels for 1%

profile of v5, /device:TPU:0, one launch (start us, length us, event | category | flops | bytes accessed | tf_op | source)
XLA Modules:
  0.0 111.7 jit_solution(15240992982539386412)
XLA Ops:
  0.6 1.0 dynamic-slice_bitcast_fusion
  1.6 3.0 %collective-permute-start.1 = (f32[256,256]{1,0:T(8,128)S(1)}, f32[256,256]{1,0:T(8,128)S(1)}, u32[]{:S(2)}, u32[]{:S(2)}) collective-permute-start(f32[256,256]{1,0:T(8,128)S(1)} %dynamic-slice_bitcast_fusion), channel_id=1, source_target_pairs={{0,4},{4,0},{1,5},{5,1},{2,6},{6,2},{3,7},{7,3},{8,12},{12,8},{9,1... | collective-permute-start | bytes 786440 | tf_op jit(solution)/shard_map/ppermute | solution.py:291
  4.7 1.3 %collective-permute-done.sibling = s32[1,2,2]{2,1,0:T(2,128)S(1)} collective-permute-done((s32[1,2,2]{2,1,0:T(2,128)}, s32[1,2,2]{2,1,0:T(2,128)S(1)}, u32[]{:S(2)}, u32[]{:S(2)}) %collective-permute-start) | collective-permute-done | bytes 48 | tf_op jit(solution)/shard_map/ppermute | solution.py:283
  6.0 1.0 copy-done
  7.0 0.7 copy-done.4
  7.7 0.6 shard_map.77
  8.3 1.3 %collective-permute-start.5 = (f32[264,128]{1,0:T(8,128)S(1)}, f32[264,128]{1,0:T(8,128)S(1)}, u32[]{:S(2)}, u32[]{:S(2)}) collective-permute-start(f32[264,128]{1,0:T(8,128)S(1)} %get-tuple-element.32.refs_0_), channel_id=1, source_target_pairs={{8,0},{10,2},{16,8},{18,10},{24,16},{26,18},{9,1},{11,3},{17,9},{1... | collective-permute-start | bytes 405512 | tf_op jit(solution)/shard_map/ppermute | solution.py:289
  9.6 1.6 %collective-permute-start.2 = (f32[264,128]{1,0:T(8,128)S(1)}, f32[264,128]{1,0:T(8,128)S(1)}, u32[]{:S(2)}, u32[]{:S(2)}) collective-permute-start(f32[264,128]{1,0:T(8,128)S(1)} %get-tuple-element.33), channel_id=1, source_target_pairs={{0,2},{2,0},{4,6},{6,4},{1,3},{3,1},{5,7},{7,5},{8,10},{10,8},{12,... | collective-permute-start | bytes 405512 | tf_op jit(solution)/shard_map/ppermute | solution.py:261
  11.2 1.3 %collective-permute-start.6 = (f32[264,128]{1,0:T(8,128)S(1)}, f32[264,128]{1,0:T(8,128)S(1)}, u32[]{:S(2)}, u32[]{:S(2)}) collective-permute-start(f32[264,128]{1,0:T(8,128)S(1)} %get-tuple-element.33), channel_id=1, source_target_pairs={{10,0},{8,2},{18,8},{16,10},{26,16},{24,18},{11,1},{9,3},{19,9},{1... | collective-permute-start | bytes 405512 | tf_op jit(solution)/shard_map/ppermute | solution.py:289
  12.5 0.7 collective-permute-start.7
  13.2 2.8 %collective-permute-done.5.refs_4_ = f32[264,128]{1,0:T(8,128)S(1)} collective-permute-done((f32[264,128]{1,0:T(8,128)S(1)}, f32[264,128]{1,0:T(8,128)S(1)}, u32[]{:S(2)}, u32[]{:S(2)}) %collective-permute-start.5) | collective-permute-done | bytes 135200 | tf_op jit(solution)/shard_map/ppermute | solution.py:289
  15.9 0.7 collective-permute-start.8
  16.6 3.9 %collective-permute-start.4 = (f32[264,128]{1,0:T(8,128)S(1)}, f32[264,128]{1,0:T(8,128)S(1)}, u32[]{:S(2)}, u32[]{:S(2)}) collective-permute-start(f32[264,128]{1,0:T(8,128)S(1)} %get-tuple-element.35), channel_id=1, source_target_pairs={{0,6},{2,4},{4,2},{6,0},{1,7},{3,5},{5,3},{7,1},{8,14},{10,12},{12... | collective-permute-start | bytes 405512 | tf_op jit(solution)/shard_map/ppermute | solution.py:261
  20.6 6.6 %collective-permute-done.3.refs_2_ = f32[264,128]{1,0:T(8,128)S(1)} collective-permute-done((f32[264,128]{1,0:T(8,128)S(1)}, f32[264,128]{1,0:T(8,128)S(1)}, u32[]{:S(2)}, u32[]{:S(2)}) %collective-permute-start.3) | collective-permute-done | bytes 135200 | tf_op jit(solution)/shard_map/ppermute | solution.py:261
  27.3 0.7 copy-done.2
  27.9 1.3 %shard_map.78 = (f32[256,128]{1,0:T(8,128)S(1)}, f32[256,128]{1,0:T(8,128)S(1)}, f32[256,128]{1,0:T(8,128)S(1)}, f32[256,128]{1,0:T(8,128)S(1)}, f32[256,128]{1,...) custom-call(s32[3]{0:T(128)S(1)} %pad_add_fusion.where, ...), custom_call_target="tpu_custom_call" | custom-call | flops 2097152 | bytes 2129920 | tf_op jit(solution)/shard_map/pallas_call | solution.py:233
  29.3 1.6 %collective-permute-start.10 = (f32[256,128]{1,0:T(8,128)S(1)}, f32[256,128]{1,0:T(8,128)S(1)}, u32[]{:S(2)}, u32[]{:S(2)}) collective-permute-start(f32[256,128]{1,0:T(8,128)S(1)} %get-tuple-element.38), channel_id=1, source_target_pairs={{0,2},{1,3},{2,0},{3,1},{4,6},{5,7},{6,4},{7,5},{8,10},{9,11},{10,... | collective-permute-start | bytes 393224 | tf_op jit(solution)/shard_map/ppermute | solution.py:261
  31.1 0.3 collective-permute-start.11
  31.4 2.5 %collective-permute-start.12 = (f32[256,128]{1,0:T(8,128)S(1)}, f32[256,128]{1,0:T(8,128)S(1)}, u32[]{:S(2)}, u32[]{:S(2)}) collective-permute-start(f32[256,128]{1,0:T(8,128)S(1)} %get-tuple-element.40), channel_id=1, source_target_pairs={{0,4},{1,5},{2,6},{3,7},{4,0},{5,1},{6,2},{7,3},{8,12},{9,13},{10,... | collective-permute-start | bytes 393224 | tf_op jit(solution)/shard_map/ppermute | solution.py:261
  33.9 2.7 %collective-permute-start.14 = (f32[256,128]{1,0:T(8,128)S(1)}, f32[256,128]{1,0:T(8,128)S(1)}, u32[]{:S(2)}, u32[]{:S(2)}) collective-permute-start(f32[256,128]{1,0:T(8,128)S(1)} %get-tuple-element.42), channel_id=1, source_target_pairs={{0,6},{1,7},{2,4},{3,5},{4,2},{5,3},{6,0},{7,1},{8,14},{9,15},{10,... | collective-permute-start | bytes 393224 | tf_op jit(solution)/shard_map/ppermute | solution.py:261
  36.6 1.3 %collective-permute-start.15 = (f32[256,128]{1,0:T(8,128)S(1)}, f32[256,128]{1,0:T(8,128)S(1)}, u32[]{:S(2)}, u32[]{:S(2)}) collective-permute-start(f32[256,128]{1,0:T(8,128)S(1)} %get-tuple-element.43), channel_id=1, source_target_pairs={{0,7},{1,6},{2,5},{3,4},{4,3},{5,2},{6,1},{7,0},{8,15},{9,14},{10,... | collective-permute-start | bytes 393224 | tf_op jit(solution)/shard_map/ppermute | solution.py:261
  38.0 5.2 %collective-permute-done.12.refs_4_ = f32[256,128]{1,0:T(8,128)S(1)} collective-permute-done((f32[256,128]{1,0:T(8,128)S(1)}, f32[256,128]{1,0:T(8,128)S(1)}, u32[]{:S(2)}, u32[]{:S(2)}) %collective-permute-start.12) | collective-permute-done | bytes 131104 | tf_op jit(solution)/shard_map/ppermute | solution.py:261
  43.2 2.8 %collective-permute-done.13.refs_5_ = f32[256,128]{1,0:T(8,128)S(1)} collective-permute-done((f32[256,128]{1,0:T(8,128)S(1)}, f32[256,128]{1,0:T(8,128)S(1)}, u32[]{:S(2)}, u32[]{:S(2)}) %collective-permute-start.13) | collective-permute-done | bytes 131104 | tf_op jit(solution)/shard_map/ppermute | solution.py:261
  46.0 1.0 copy-done.1
  47.0 0.7 copy-done.3
  47.7 1.0 copy-done.5
  48.7 1.7 %copy-done.6 = bf16[4,1280,256]{2,1,0:T(8,128)(2,1)S(1)} copy-done((bf16[4,1280,256]{2,1,0:T(8,128)(2,1)S(1)}, bf16[4,1280,256]{2,1,0:T(8,128)(2,1)}, u32[]{:S(2)}) %copy-start.6) | copy-done | bytes 2621464
  50.5 8.3 %shard_map.79 = (f32[384,128]{1,0:T(8,128)S(1)}, f32[384,128]{1,0:T(8,128)S(1)}, f32[384,128]{1,0:T(8,128)S(1)}, f32[384,128]{1,0:T(8,128)S(1)}, f32[384,128]{1,...) custom-call(s32[3]{0:T(128)S(1)} %pad_add_fusion.where, ...), custom_call_target="tpu_custom_call" | custom-call | flops 3221225472 | bytes 6553600 | tf_op jit(solution)/shard_map/pallas_call | solution.py:233
  59.0 1.6 %collective-permute-start.17 = (f32[384,128]{1,0:T(8,128)S(1)}, f32[384,128]{1,0:T(8,128)S(1)}, u32[]{:S(2)}, u32[]{:S(2)}) collective-permute-start(f32[384,128]{1,0:T(8,128)S(1)} %get-tuple-element.47), channel_id=1, source_target_pairs={{0,2},{1,3},{2,0},{3,1},{4,6},{5,7},{6,4},{7,5},{8,10},{9,11},{10,... | collective-permute-start | bytes 589832 | tf_op jit(solution)/shard_map/ppermute | solution.py:261
  60.7 1.6 %collective-permute-start.19 = (f32[384,128]{1,0:T(8,128)S(1)}, f32[384,128]{1,0:T(8,128)S(1)}, u32[]{:S(2)}, u32[]{:S(2)}) collective-permute-start(f32[384,128]{1,0:T(8,128)S(1)} %get-tuple-element.49), channel_id=1, source_target_pairs={{0,4},{1,5},{2,6},{3,7},{4,0},{5,1},{6,2},{7,3},{8,12},{9,13},{10,... | collective-permute-start | bytes 589832 | tf_op jit(solution)/shard_map/ppermute | solution.py:261
  62.6 2.7 %collective-permute-start.21 = (f32[384,128]{1,0:T(8,128)S(1)}, f32[384,128]{1,0:T(8,128)S(1)}, u32[]{:S(2)}, u32[]{:S(2)}) collective-permute-start(f32[384,128]{1,0:T(8,128)S(1)} %get-tuple-element.51), channel_id=1, source_target_pairs={{0,6},{1,7},{2,4},{3,5},{4,2},{5,3},{6,0},{7,1},{8,14},{9,15},{10,... | collective-permute-start | bytes 589832 | tf_op jit(solution)/shard_map/ppermute | solution.py:261
  65.3 1.5 %collective-permute-done.17.refs_2_ = f32[384,128]{1,0:T(8,128)S(1)} collective-permute-done((f32[384,128]{1,0:T(8,128)S(1)}, f32[384,128]{1,0:T(8,128)S(1)}, u32[]{:S(2)}, u32[]{:S(2)}) %collective-permute-start.17) | collective-permute-done | bytes 196640 | tf_op jit(solution)/shard_map/ppermute | solution.py:261
  66.8 0.8 collective-permute-start.22
  67.6 2.5 %collective-permute-done.18.refs_3_ = f32[384,128]{1,0:T(8,128)S(1)} collective-permute-done((f32[384,128]{1,0:T(8,128)S(1)}, f32[384,128]{1,0:T(8,128)S(1)}, u32[]{:S(2)}, u32[]{:S(2)}) %collective-permute-start.18) | collective-permute-done | bytes 196640 | tf_op jit(solution)/shard_map/ppermute | solution.py:261
  70.1 10.1 %collective-permute-done.20.refs_5_ = f32[384,128]{1,0:T(8,128)S(1)} collective-permute-done((f32[384,128]{1,0:T(8,128)S(1)}, f32[384,128]{1,0:T(8,128)S(1)}, u32[]{:S(2)}, u32[]{:S(2)}) %collective-permute-start.20) | collective-permute-done | bytes 196640 | tf_op jit(solution)/shard_map/ppermute | solution.py:261
  80.2 2.2 %shard_map.80 = (f32[256,128]{1,0:T(8,128)S(1)}, f32[256,128]{1,0:T(8,128)S(1)}, f32[256,128]{1,0:T(8,128)S(1)}, f32[256,128]{1,0:T(8,128)S(1)}, f32[256,128]{1,...) custom-call(s32[3]{0:T(128)S(1)} %pad_add_fusion.where, s32[1,2]{1,0:T(1,128)S(1)} %copy-done.3, ...), custom_call_target="tpu_custom_call" | custom-call | flops 6291456 | bytes 2424832 | tf_op jit(solution)/shard_map/pallas_call | solution.py:233
  82.4 1.6 %collective-permute-start.30 = (f32[64,256]{1,0:T(8,128)S(1)}, f32[64,256]{1,0:T(8,128)S(1)}, u32[]{:S(2)}, u32[]{:S(2)}) collective-permute-start(f32[64,256]{1,0:T(8,128)S(1)} %get-tuple-element.59), channel_id=1, source_target_pairs={{0,8},{8,0},{16,24},{24,16},{1,9},{9,1},{17,25},{25,17},{2,10},{10... | collective-permute-start | bytes 196616 | tf_op jit(solution)/shard_map/ppermute | solution.py:253
  84.0 1.5 %collective-permute-start.23 = (f32[256,128]{1,0:T(8,128)S(1)}, f32[256,128]{1,0:T(8,128)S(1)}, u32[]{:S(2)}, u32[]{:S(2)}) collective-permute-start(f32[256,128]{1,0:T(8,128)S(1)} %get-tuple-element.54), channel_id=1, source_target_pairs={{0,2},{2,0},{4,6},{6,4},{1,3},{3,1},{5,7},{7,5},{8,10},{10,8},{12,... | collective-permute-start | bytes 393224 | tf_op jit(solution)/shard_map/ppermute | solution.py:261
  85.5 1.9 %collective-permute-start.24 = (f32[256,128]{1,0:T(8,128)S(1)}, f32[256,128]{1,0:T(8,128)S(1)}, u32[]{:S(2)}, u32[]{:S(2)}) collective-permute-start(f32[256,128]{1,0:T(8,128)S(1)} %get-tuple-element.55), channel_id=1, source_target_pairs={{0,4},{2,6},{4,0},{6,2},{1,5},{3,7},{5,1},{7,3},{8,12},{10,14},{12... | collective-permute-start | bytes 393224 | tf_op jit(solution)/shard_map/ppermute | solution.py:261
  87.5 2.0 %collective-permute-start.31 = (f32[64,256]{1,0:T(8,128)S(1)}, f32[64,256]{1,0:T(8,128)S(1)}, u32[]{:S(2)}, u32[]{:S(2)}) collective-permute-start(f32[64,256]{1,0:T(8,128)S(1)} %add.12), channel_id=1, source_target_pairs={{0,16},{8,24},{16,0},{24,8},{1,17},{9,25},{17,1},{25,9},{2,18},{10... | collective-permute-start | bytes 196616 | tf_op jit(solution)/shard_map/ppermute | solution.py:253
  89.4 0.7 collective-permute-start.28
  90.1 3.7 %collective-permute-start.26 = (f32[256,128]{1,0:T(8,128)S(1)}, f32[256,128]{1,0:T(8,128)S(1)}, u32[]{:S(2)}, u32[]{:S(2)}) collective-permute-start(f32[256,128]{1,0:T(8,128)S(1)} %get-tuple-element.57), channel_id=1, source_target_pairs={{0,8},{2,10},{8,16},{10,18},{16,24},{18,26},{1,9},{3,11},{9,17},{1... | collective-permute-start | bytes 393224 | tf_op jit(solution)/shard_map/ppermute | solution.py:322
  93.8 1.1 collective-permute-start.25
  94.9 0.7 collective-permute-start.29
  95.6 4.0 %collective-permute-start.27 = (f32[256,128]{1,0:T(8,128)S(1)}, f32[256,128]{1,0:T(8,128)S(1)}, u32[]{:S(2)}, u32[]{:S(2)}) collective-permute-start(f32[256,128]{1,0:T(8,128)S(1)} %get-tuple-element.58), channel_id=1, source_target_pairs={{0,10},{2,8},{8,18},{10,16},{16,26},{18,24},{1,11},{3,9},{9,19},{1... | collective-permute-start | bytes 393224 | tf_op jit(solution)/shard_map/ppermute | solution.py:322
  99.5 9.9 %all_gather.3 = f32[512,256]{1,0:T(8,128)S(1)} all-gather(f32[64,256]{1,0:T(8,128)S(1)} %add.13), channel_id=1, replica_groups=mesh['pair'=4,'half'=2,'col'=2,'core'=2] {'half','col','core'}, dimensions={0}, use_global_device_ids=true | all-gather | bytes 589824 | tf_op jit(solution)/shard_map/all_gather | solution.py:325
  109.5 1.4 %shard_map.81 = f32[4,256,128]{2,1,0:T(8,128)} custom-call(s32[3]{0:T(128)S(1)} %pad_add_fusion.where, f32[256,128]{1,0:T(8,128)S(1)} %get-tuple-element.53.refs_0_, f32[256,128]{1,0:T(8,128)S(1)} %collective-permute-done.23.refs_1_, f32[256,128]{1,0:T(8,128)S(1)} %collective-permute-done.24.refs_2_, f32[256,128]{1,0:T(8,128)S(1)} %collective-permute-done.25.refs_3_, ...), custom_call_target="tpu_custom_call" | custom-call | flops 131072 | bytes 1572864 | tf_op jit(solution)/shard_map/pallas_call | solution.py:233
  110.9 0.8 copy.9
  (46 shorter events, 1.3 us)
Async XLA Ops:
  1.6 15.0 %collective-permute-start.1 = (f32[256,256]{1,0:T(8,128)S(1)}, f32[256,256]{1,0:T(8,128)S(1)}, u32[]{:S(2)}, u32[]{:S(2)}) collective-permute-start(f32[256,256]{1,0:T(8,128)S(1)} %dynamic-slice_bitcast_fusion), channel_id=1, source_target_pairs={{0,4},{4,0},{1,5},{5,1},{2,6},{6,2},{3,7},{7,3},{8,12},{12,8},{9,1... | collective-permute-start | bytes 786440 | tf_op jit(solution)/shard_map/ppermute | solution.py:291
  4.6 1.4 %collective-permute-start = (s32[1,2,2]{2,1,0:T(2,128)}, s32[1,2,2]{2,1,0:T(2,128)S(1)}, u32[]{:S(2)}, u32[]{:S(2)}) collective-permute-start(s32[1,2,2]{2,1,0:T(2,128)} %offsets.1), channel_id=1, source_target_pairs={{0,1},{1,0},{2,3},{3,2},{4,5},{5,4},{6,7},{7,6},{8,9},{9,8},{10,11... | collective-permute-start | bytes 56 | tf_op jit(solution)/shard_map/ppermute | solution.py:283
  6.0 1.0 copy-start
  7.0 0.7 copy-start.4
  8.3 7.6 %collective-permute-start.5 = (f32[264,128]{1,0:T(8,128)S(1)}, f32[264,128]{1,0:T(8,128)S(1)}, u32[]{:S(2)}, u32[]{:S(2)}) collective-permute-start(f32[264,128]{1,0:T(8,128)S(1)} %get-tuple-element.32.refs_0_), channel_id=1, source_target_pairs={{8,0},{10,2},{16,8},{18,10},{24,16},{26,18},{9,1},{11,3},{17,9},{1... | collective-permute-start | bytes 405512 | tf_op jit(solution)/shard_map/ppermute | solution.py:289
  9.6 6.3 %collective-permute-start.2 = (f32[264,128]{1,0:T(8,128)S(1)}, f32[264,128]{1,0:T(8,128)S(1)}, u32[]{:S(2)}, u32[]{:S(2)}) collective-permute-start(f32[264,128]{1,0:T(8,128)S(1)} %get-tuple-element.33), channel_id=1, source_target_pairs={{0,2},{2,0},{4,6},{6,4},{1,3},{3,1},{5,7},{7,5},{8,10},{10,8},{12,... | collective-permute-start | bytes 405512 | tf_op jit(solution)/shard_map/ppermute | solution.py:261
  11.2 9.4 %collective-permute-start.6 = (f32[264,128]{1,0:T(8,128)S(1)}, f32[264,128]{1,0:T(8,128)S(1)}, u32[]{:S(2)}, u32[]{:S(2)}) collective-permute-start(f32[264,128]{1,0:T(8,128)S(1)} %get-tuple-element.33), channel_id=1, source_target_pairs={{10,0},{8,2},{18,8},{16,10},{26,16},{24,18},{11,1},{9,3},{19,9},{1... | collective-permute-start | bytes 405512 | tf_op jit(solution)/shard_map/ppermute | solution.py:289
  12.5 8.2 %collective-permute-start.7 = (f32[264,128]{1,0:T(8,128)S(1)}, f32[264,128]{1,0:T(8,128)S(1)}, u32[]{:S(2)}, u32[]{:S(2)}) collective-permute-start(f32[264,128]{1,0:T(8,128)S(1)} %get-tuple-element.34), channel_id=1, source_target_pairs={{8,4},{10,6},{16,12},{18,14},{24,20},{26,22},{9,5},{11,7},{17,13},... | collective-permute-start | bytes 405512 | tf_op jit(solution)/shard_map/ppermute | solution.py:289
  15.9 11.4 %collective-permute-start.3 = (f32[264,128]{1,0:T(8,128)S(1)}, f32[264,128]{1,0:T(8,128)S(1)}, u32[]{:S(2)}, u32[]{:S(2)}) collective-permute-start(f32[264,128]{1,0:T(8,128)S(1)} %get-tuple-element.34), channel_id=1, source_target_pairs={{0,4},{2,6},{4,0},{6,2},{1,5},{3,7},{5,1},{7,3},{8,12},{10,14},{12... | collective-permute-start | bytes 405512 | tf_op jit(solution)/shard_map/ppermute | solution.py:261
  15.9 11.4 %collective-permute-start.8 = (f32[264,128]{1,0:T(8,128)S(1)}, f32[264,128]{1,0:T(8,128)S(1)}, u32[]{:S(2)}, u32[]{:S(2)}) collective-permute-start(f32[264,128]{1,0:T(8,128)S(1)} %get-tuple-element.35), channel_id=1, source_target_pairs={{10,4},{8,6},{18,12},{16,14},{26,20},{24,22},{11,5},{9,7},{19,13},... | collective-permute-start | bytes 405512 | tf_op jit(solution)/shard_map/ppermute | solution.py:289
  16.6 10.7 %collective-permute-start.4 = (f32[264,128]{1,0:T(8,128)S(1)}, f32[264,128]{1,0:T(8,128)S(1)}, u32[]{:S(2)}, u32[]{:S(2)}) collective-permute-start(f32[264,128]{1,0:T(8,128)S(1)} %get-tuple-element.35), channel_id=1, source_target_pairs={{0,6},{2,4},{4,2},{6,0},{1,7},{3,5},{5,3},{7,1},{8,14},{10,12},{12... | collective-permute-start | bytes 405512 | tf_op jit(solution)/shard_map/ppermute | solution.py:261
  27.3 0.7 copy-start.2
  29.2 4.7 %collective-permute-start.9 = (f32[256,128]{1,0:T(8,128)S(1)}, f32[256,128]{1,0:T(8,128)S(1)}, u32[]{:S(2)}, u32[]{:S(2)}) collective-permute-start(f32[256,128]{1,0:T(8,128)S(1)} %get-tuple-element.37), channel_id=1, source_target_pairs={{0,1},{1,0},{2,3},{3,2},{4,5},{5,4},{6,7},{7,6},{8,9},{9,8},{10,11... | collective-permute-start | bytes 393224 | tf_op jit(solution)/shard_map/ppermute | solution.py:261
  29.3 7.3 %collective-permute-start.10 = (f32[256,128]{1,0:T(8,128)S(1)}, f32[256,128]{1,0:T(8,128)S(1)}, u32[]{:S(2)}, u32[]{:S(2)}) collective-permute-start(f32[256,128]{1,0:T(8,128)S(1)} %get-tuple-element.38), channel_id=1, source_target_pairs={{0,2},{1,3},{2,0},{3,1},{4,6},{5,7},{6,4},{7,5},{8,10},{9,11},{10,... | collective-permute-start | bytes 393224 | tf_op jit(solution)/shard_map/ppermute | solution.py:261
  31.1 6.9 %collective-permute-start.11 = (f32[256,128]{1,0:T(8,128)S(1)}, f32[256,128]{1,0:T(8,128)S(1)}, u32[]{:S(2)}, u32[]{:S(2)}) collective-permute-start(f32[256,128]{1,0:T(8,128)S(1)} %get-tuple-element.39), channel_id=1, source_target_pairs={{0,3},{1,2},{2,1},{3,0},{4,7},{5,6},{6,5},{7,4},{8,11},{9,10},{10,... | collective-permute-start | bytes 393224 | tf_op jit(solution)/shard_map/ppermute | solution.py:261
  31.4 11.8 %collective-permute-start.12 = (f32[256,128]{1,0:T(8,128)S(1)}, f32[256,128]{1,0:T(8,128)S(1)}, u32[]{:S(2)}, u32[]{:S(2)}) collective-permute-start(f32[256,128]{1,0:T(8,128)S(1)} %get-tuple-element.40), channel_id=1, source_target_pairs={{0,4},{1,5},{2,6},{3,7},{4,0},{5,1},{6,2},{7,3},{8,12},{9,13},{10,... | collective-permute-start | bytes 393224 | tf_op jit(solution)/shard_map/ppermute | solution.py:261
  33.9 12.1 %collective-permute-start.13 = (f32[256,128]{1,0:T(8,128)S(1)}, f32[256,128]{1,0:T(8,128)S(1)}, u32[]{:S(2)}, u32[]{:S(2)}) collective-permute-start(f32[256,128]{1,0:T(8,128)S(1)} %get-tuple-element.41), channel_id=1, source_target_pairs={{0,5},{1,4},{2,7},{3,6},{4,1},{5,0},{6,3},{7,2},{8,13},{9,12},{10,... | collective-permute-start | bytes 393224 | tf_op jit(solution)/shard_map/ppermute | solution.py:261
  33.9 12.1 %collective-permute-start.14 = (f32[256,128]{1,0:T(8,128)S(1)}, f32[256,128]{1,0:T(8,128)S(1)}, u32[]{:S(2)}, u32[]{:S(2)}) collective-permute-start(f32[256,128]{1,0:T(8,128)S(1)} %get-tuple-element.42), channel_id=1, source_target_pairs={{0,6},{1,7},{2,4},{3,5},{4,2},{5,3},{6,0},{7,1},{8,14},{9,15},{10,... | collective-permute-start | bytes 393224 | tf_op jit(solution)/shard_map/ppermute | solution.py:261
  36.6 9.4 %collective-permute-start.15 = (f32[256,128]{1,0:T(8,128)S(1)}, f32[256,128]{1,0:T(8,128)S(1)}, u32[]{:S(2)}, u32[]{:S(2)}) collective-permute-start(f32[256,128]{1,0:T(8,128)S(1)} %get-tuple-element.43), channel_id=1, source_target_pairs={{0,7},{1,6},{2,5},{3,4},{4,3},{5,2},{6,1},{7,0},{8,15},{9,14},{10,... | collective-permute-start | bytes 393224 | tf_op jit(solution)/shard_map/ppermute | solution.py:261
  46.0 1.0 copy-start.1
  47.0 0.7 copy-start.3
  47.7 1.0 copy-start.5
  48.7 1.7 %copy-start.6 = (bf16[4,1280,256]{2,1,0:T(8,128)(2,1)S(1)}, bf16[4,1280,256]{2,1,0:T(8,128)(2,1)}, u32[]{:S(2)}) copy-start(bf16[4,1280,256]{2,1,0:T(8,128)(2,1)} %constant.22.clone.refs_11_) | copy-start | bytes 7864324
  58.8 3.8 %collective-permute-start.16 = (f32[384,128]{1,0:T(8,128)S(1)}, f32[384,128]{1,0:T(8,128)S(1)}, u32[]{:S(2)}, u32[]{:S(2)}) collective-permute-start(f32[384,128]{1,0:T(8,128)S(1)} %get-tuple-element.46), channel_id=1, source_target_pairs={{0,1},{1,0},{2,3},{3,2},{4,5},{5,4},{6,7},{7,6},{8,9},{9,8},{10,11... | collective-permute-start | bytes 589832 | tf_op jit(solution)/shard_map/ppermute | solution.py:261
  59.0 7.7 %collective-permute-start.17 = (f32[384,128]{1,0:T(8,128)S(1)}, f32[384,128]{1,0:T(8,128)S(1)}, u32[]{:S(2)}, u32[]{:S(2)}) collective-permute-start(f32[384,128]{1,0:T(8,128)S(1)} %get-tuple-element.47), channel_id=1, source_target_pairs={{0,2},{1,3},{2,0},{3,1},{4,6},{5,7},{6,4},{7,5},{8,10},{9,11},{10,... | collective-permute-start | bytes 589832 | tf_op jit(solution)/shard_map/ppermute | solution.py:261
  60.6 9.5 %collective-permute-start.18 = (f32[384,128]{1,0:T(8,128)S(1)}, f32[384,128]{1,0:T(8,128)S(1)}, u32[]{:S(2)}, u32[]{:S(2)}) collective-permute-start(f32[384,128]{1,0:T(8,128)S(1)} %get-tuple-element.48), channel_id=1, source_target_pairs={{0,3},{1,2},{2,1},{3,0},{4,7},{5,6},{6,5},{7,4},{8,11},{9,10},{10,... | collective-permute-start | bytes 589832 | tf_op jit(solution)/shard_map/ppermute | solution.py:261
  60.7 9.3 %collective-permute-start.19 = (f32[384,128]{1,0:T(8,128)S(1)}, f32[384,128]{1,0:T(8,128)S(1)}, u32[]{:S(2)}, u32[]{:S(2)}) collective-permute-start(f32[384,128]{1,0:T(8,128)S(1)} %get-tuple-element.49), channel_id=1, source_target_pairs={{0,4},{1,5},{2,6},{3,7},{4,0},{5,1},{6,2},{7,3},{8,12},{9,13},{10,... | collective-permute-start | bytes 589832 | tf_op jit(solution)/shard_map/ppermute | solution.py:261
  62.3 17.8 %collective-permute-start.20 = (f32[384,128]{1,0:T(8,128)S(1)}, f32[384,128]{1,0:T(8,128)S(1)}, u32[]{:S(2)}, u32[]{:S(2)}) collective-permute-start(f32[384,128]{1,0:T(8,128)S(1)} %get-tuple-element.50), channel_id=1, source_target_pairs={{0,5},{1,4},{2,7},{3,6},{4,1},{5,0},{6,3},{7,2},{8,13},{9,12},{10,... | collective-permute-start | bytes 589832 | tf_op jit(solution)/shard_map/ppermute | solution.py:261
  62.6 17.6 %collective-permute-start.21 = (f32[384,128]{1,0:T(8,128)S(1)}, f32[384,128]{1,0:T(8,128)S(1)}, u32[]{:S(2)}, u32[]{:S(2)}) collective-permute-start(f32[384,128]{1,0:T(8,128)S(1)} %get-tuple-element.51), channel_id=1, source_target_pairs={{0,6},{1,7},{2,4},{3,5},{4,2},{5,3},{6,0},{7,1},{8,14},{9,15},{10,... | collective-permute-start | bytes 589832 | tf_op jit(solution)/shard_map/ppermute | solution.py:261
  66.8 13.4 %collective-permute-start.22 = (f32[384,128]{1,0:T(8,128)S(1)}, f32[384,128]{1,0:T(8,128)S(1)}, u32[]{:S(2)}, u32[]{:S(2)}) collective-permute-start(f32[384,128]{1,0:T(8,128)S(1)} %get-tuple-element.52), channel_id=1, source_target_pairs={{0,7},{1,6},{2,5},{3,4},{4,3},{5,2},{6,1},{7,0},{8,15},{9,14},{10,... | collective-permute-start | bytes 589832 | tf_op jit(solution)/shard_map/ppermute | solution.py:261
  82.4 5.1 %collective-permute-start.30 = (f32[64,256]{1,0:T(8,128)S(1)}, f32[64,256]{1,0:T(8,128)S(1)}, u32[]{:S(2)}, u32[]{:S(2)}) collective-permute-start(f32[64,256]{1,0:T(8,128)S(1)} %get-tuple-element.59), channel_id=1, source_target_pairs={{0,8},{8,0},{16,24},{24,16},{1,9},{9,1},{17,25},{25,17},{2,10},{10... | collective-permute-start | bytes 196616 | tf_op jit(solution)/shard_map/ppermute | solution.py:253
  84.0 10.8 %collective-permute-start.23 = (f32[256,128]{1,0:T(8,128)S(1)}, f32[256,128]{1,0:T(8,128)S(1)}, u32[]{:S(2)}, u32[]{:S(2)}) collective-permute-start(f32[256,128]{1,0:T(8,128)S(1)} %get-tuple-element.54), channel_id=1, source_target_pairs={{0,2},{2,0},{4,6},{6,4},{1,3},{3,1},{5,7},{7,5},{8,10},{10,8},{12,... | collective-permute-start | bytes 393224 | tf_op jit(solution)/shard_map/ppermute | solution.py:261
  85.5 10.0 %collective-permute-start.24 = (f32[256,128]{1,0:T(8,128)S(1)}, f32[256,128]{1,0:T(8,128)S(1)}, u32[]{:S(2)}, u32[]{:S(2)}) collective-permute-start(f32[256,128]{1,0:T(8,128)S(1)} %get-tuple-element.55), channel_id=1, source_target_pairs={{0,4},{2,6},{4,0},{6,2},{1,5},{3,7},{5,1},{7,3},{8,12},{10,14},{12... | collective-permute-start | bytes 393224 | tf_op jit(solution)/shard_map/ppermute | solution.py:261
  87.5 6.3 %collective-permute-start.31 = (f32[64,256]{1,0:T(8,128)S(1)}, f32[64,256]{1,0:T(8,128)S(1)}, u32[]{:S(2)}, u32[]{:S(2)}) collective-permute-start(f32[64,256]{1,0:T(8,128)S(1)} %add.12), channel_id=1, source_target_pairs={{0,16},{8,24},{16,0},{24,8},{1,17},{9,25},{17,1},{25,9},{2,18},{10... | collective-permute-start | bytes 196616 | tf_op jit(solution)/shard_map/ppermute | solution.py:253
  89.4 20.0 %collective-permute-start.28 = (f32[256,128]{1,0:T(8,128)S(1)}, f32[256,128]{1,0:T(8,128)S(1)}, u32[]{:S(2)}, u32[]{:S(2)}) collective-permute-start(f32[256,128]{1,0:T(8,128)S(1)} %get-tuple-element.57), channel_id=1, source_target_pairs={{4,8},{6,10},{12,16},{14,18},{20,24},{22,26},{5,9},{7,11},{13,17},... | collective-permute-start | bytes 393224 | tf_op jit(solution)/shard_map/ppermute | solution.py:322
  90.1 19.4 %collective-permute-start.26 = (f32[256,128]{1,0:T(8,128)S(1)}, f32[256,128]{1,0:T(8,128)S(1)}, u32[]{:S(2)}, u32[]{:S(2)}) collective-permute-start(f32[256,128]{1,0:T(8,128)S(1)} %get-tuple-element.57), channel_id=1, source_target_pairs={{0,8},{2,10},{8,16},{10,18},{16,24},{18,26},{1,9},{3,11},{9,17},{1... | collective-permute-start | bytes 393224 | tf_op jit(solution)/shard_map/ppermute | solution.py:322
  93.8 15.6 %collective-permute-start.25 = (f32[256,128]{1,0:T(8,128)S(1)}, f32[256,128]{1,0:T(8,128)S(1)}, u32[]{:S(2)}, u32[]{:S(2)}) collective-permute-start(f32[256,128]{1,0:T(8,128)S(1)} %get-tuple-element.56), channel_id=1, source_target_pairs={{0,6},{2,4},{4,2},{6,0},{1,7},{3,5},{5,3},{7,1},{8,14},{10,12},{12... | collective-permute-start | bytes 393224 | tf_op jit(solution)/shard_map/ppermute | solution.py:261
  94.9 14.6 %collective-permute-start.29 = (f32[256,128]{1,0:T(8,128)S(1)}, f32[256,128]{1,0:T(8,128)S(1)}, u32[]{:S(2)}, u32[]{:S(2)}) collective-permute-start(f32[256,128]{1,0:T(8,128)S(1)} %get-tuple-element.58), channel_id=1, source_target_pairs={{4,10},{6,8},{12,18},{14,16},{20,26},{22,24},{5,11},{7,9},{13,19},... | collective-permute-start | bytes 393224 | tf_op jit(solution)/shard_map/ppermute | solution.py:322
  95.6 13.9 %collective-permute-start.27 = (f32[256,128]{1,0:T(8,128)S(1)}, f32[256,128]{1,0:T(8,128)S(1)}, u32[]{:S(2)}, u32[]{:S(2)}) collective-permute-start(f32[256,128]{1,0:T(8,128)S(1)} %get-tuple-element.58), channel_id=1, source_target_pairs={{0,10},{2,8},{8,18},{10,16},{16,26},{18,24},{1,11},{3,9},{9,19},{1... | collective-permute-start | bytes 393224 | tf_op jit(solution)/shard_map/ppermute | solution.py:322

commit v6 on v5

--- a/solution.py
+++ b/solution.py
@@ -81,9 +81,19 @@
     return lower, offs[holder, at], offs[holder, at + 1]
 
 
-def deal_kernel(where, offsets, sibling, block, *outs):
+def fetch(pairs, sems):
+    copies = [pltpu.make_async_copy(source, into, sems.at[k]) for k, (source, into) in enumerate(pairs)]
+    for copy in copies:
+        copy.start()
+    return copies
+
+
+def deal_kernel(where, offsets, sibling, block, measured, *refs):
+    outs, given, sems = refs[:4], refs[4], refs[5]
     mine, core = 2 * where[0] + where[1], where[2]
     rows, cols = block.shape[1:]
+    pairs = [(block.at[jnp.bitwise_xor(mine, turn)], out.at[pl.ds(0, rows)]) for turn, out in enumerate(outs)]
+    copies = fetch([*pairs, (measured.at[0, 1 - where[0]], given)], sems)
     lines = []
     for holder in range(2):
         for slot in range(2):
@@ -91,9 +101,10 @@
                 value = jnp.where(core == holder, offsets[0, slot, axis], sibling[0, slot, axis])
                 lines.append(jnp.full((1, cols), value, jnp.int32))
     lines = jnp.concatenate(lines, axis=0).astype(jnp.float32)
-    for turn, out in enumerate(outs):
-        out[:rows] = block[jnp.bitwise_xor(mine, turn)]
+    for out in outs:
         out[rows:] = lines
+    for copy in copies:
+        copy.wait()
 
 
 def pick_kernel(where, slot_range, *refs):
@@ -128,13 +139,23 @@
 
 
 def position_kernel(where, slot_range, offs, *refs):
-    gotten, (probe, measured, taken, tabs), outs, (patch, grad) = refs[:8], refs[8:12], refs[12:20], refs[20:]
+    gotten, taken, (probe_from, measured, tabs_from), outs = refs[:8], refs[8], refs[9:12], refs[12:20]
+    patch, grad, probe, kept, tabs, sems = refs[20:]
     half, col, core = where[0], where[1], where[2]
     mine = 2 * half + col
     flat = 2 * mine + core
     lower, row_at, col_at = slot_place(offs, mine, slot_range[0, 1 - half], slot_of(half, col, core))
     width = probe.shape[-1]
     lanes, band = width // 2, width // 4
+    probe_copy, near_copy, far_copy, kept_copy = fetch(
+        [
+            (probe_from, probe),
+            (tabs_from.at[pl.ds(2, 2)], tabs.at[pl.ds(2, 2)]),
+            (tabs_from.at[pl.ds(0, 2)], tabs.at[pl.ds(0, 2)]),
+            (measured.at[0, half], kept),
+        ],
+        sems,
+    )
     for turn in range(8):
         patch[jnp.bitwise_xor(flat, turn)] = gotten[turn][...]
 
@@ -148,15 +169,19 @@
     def roll(value, rows, cols):
         return pltpu.roll(pltpu.roll(value, rows, 0), cols, 1)
 
+    probe_copy.wait()
     wave_re, wave_im = roll(probe[0], row_at, col_at), roll(probe[1], row_at, col_at)
     o0_re, o0_im, o1_re, o1_im = load(0), load(2), load(1), load(3)
     exit_re = wave_re * o0_re - wave_im * o0_im
     exit_im = wave_re * o0_im + wave_im * o0_re
+    near_copy.wait()
     mid_re, mid_im = transform(exit_re, exit_im, tabs, 2, False)
     exit_re = mid_re * o1_re - mid_im * o1_im
     exit_im = mid_re * o1_im + mid_im * o1_re
+    far_copy.wait()
     far_re, far_im = transform(exit_re, exit_im, tabs, 0, False)
-    target = jnp.where(lower == half, measured[0, half], taken[...])
+    kept_copy.wait()
+    target = jnp.where(lower == half, kept[...], taken[...])
     excess = 2.0 * GRAD_WEIGHT * (far_re * far_re + far_im * far_im - target)
     back_re, back_im = transform(excess * far_re, excess * far_im, tabs, 0, True)
     store(1, mid_re * back_re + mid_im * back_im)
@@ -218,27 +243,35 @@
 
 
 def join_kernel(where, *refs):
+    (probe, out, probe_out, sums, sems) = refs[8:]
+    copies = fetch([(probe, probe_out)], sems)
     mine = 2 * where[0] + where[1]
     for turn in range(4):
-        refs[8][jnp.bitwise_xor(mine, turn)] = refs[turn][...] + refs[4 + turn][...]
+        sums[turn] = refs[turn][...] + refs[4 + turn][...]
+        copies += fetch([(sums.at[turn], out.at[jnp.bitwise_xor(mine, turn)])], sems.at[pl.ds(1 + turn, 1)])
+    for copy in copies:
+        copy.wait()
 
 
 SMEM = pl.BlockSpec(memory_space=pltpu.SMEM)
 VMEM = pl.BlockSpec(memory_space=pltpu.VMEM)
-
-
-def call(kernel, out_shape, scalars, arrays, flops, scratch=()):
-    outs = out_shape if isinstance(out_shape, (list, tuple)) else [out_shape]
-    moved = sum(math.prod(x.shape) * x.dtype.itemsize for x in [*arrays, *outs])
+HBM = pl.BlockSpec(memory_space=pltpu.HBM)
+ANY = pl.BlockSpec(memory_space=pl.ANY)
+
+
+def call(kernel, outs, scalars, arrays, flops, scratch=(), copies=0):
+    outs, arrays = ([x if isinstance(x, tuple) else (x, VMEM) for x in xs] for xs in (outs, arrays))
+    moved = sum(math.prod(x.shape) * x.dtype.itemsize for x, unused in [*arrays, *outs])
+    scratch = [pltpu.VMEM(dims, jnp.float32) if isinstance(dims, tuple) else dims for dims in scratch]
     return pl.pallas_call(
         kernel,
-        out_shape=out_shape,
-        in_specs=[SMEM] * len(scalars) + [VMEM] * len(arrays),
-        out_specs=jax.tree.map(lambda unused: VMEM, out_shape),
+        out_shape=[x for x, unused in outs],
+        in_specs=[SMEM] * len(scalars) + [spec for unused, spec in arrays],
+        out_specs=[spec for unused, spec in outs],
+        scratch_shapes=scratch + [pltpu.SemaphoreType.DMA((copies,))] * (copies > 0),
         compiler_params=pltpu.CompilerParams(vmem_limit_bytes=VMEM_LIMIT),
         cost_estimate=pl.CostEstimate(flops=flops, bytes_accessed=moved, transcendentals=0),
-        scratch_shapes=[pltpu.VMEM(dims, jnp.float32) for dims in scratch],
-    )(*scalars, *arrays)
+    )(*scalars, *(pltpu.with_memory_space_constraint(x, pltpu.HBM) if spec is HBM else x for x, spec in arrays))
 
 
 def shape(*dims):
@@ -257,10 +290,10 @@
 
 def deal(values, axes):
     count = len(values)
-    return [
-        value if turn == 0 else lax.ppermute(value, axes, [(k, k ^ turn) for k in range(count)])
-        for turn, value in enumerate(values)
-    ]
+    out = list(values)
+    for turn in (6, 7, 2, 4, 3, 5, 1) if count == 8 else (3, 1, 2):
+        out[turn] = lax.ppermute(values[turn], axes, [(k, k ^ turn) for k in range(count)])
+    return out
 
 
 def shift_pairs(pairs, step, half, turn):
@@ -281,9 +314,16 @@
     where = jnp.stack([half, col, core])
 
     sibling = lax.ppermute(offsets, "core", [(0, 1), (1, 0)])
+    offsets, slot_range = (pltpu.with_memory_space_constraint(x, pltpu.HBM) for x in (offsets, slot_range))
     block = object_field.reshape(planes, rows, cols)
-    dealt = call(deal_kernel, [shape(rows + 8, cols)] * 4, (where, offsets, sibling), (block,), 0)
-    given = lax.dynamic_index_in_dim(measured[0], 1 - half, 0, keepdims=False)
+    *dealt, given = call(
+        deal_kernel,
+        [shape(rows + 8, cols)] * 4 + [shape(width, width)],
+        (where, offsets, sibling),
+        ((block, HBM), (measured, HBM)),
+        0,
+        copies=5,
+    )
     below = []
     for turn in range(4):
         below.append(lax.ppermute(dealt[turn], AROUND, shift_pairs(pairs, 1, turn // 2, turn % 2)))
@@ -300,13 +340,15 @@
         [(planes, rows + 8, cols), (2, rows, cols), (8, rows, cols)],
     )
     scalars = (where, slot_range, jnp.stack([value[rows:, 0] for value in own]).astype(jnp.int32))
+    tabs = jnp.asarray(tables(width))
     grad = call(
         position_kernel,
         [shape(rows + 2 * band, cols)] * 8,
         scalars,
-        (*deal(parts, PLANE), probe, measured, taken, jnp.asarray(tables(width))),
+        (*deal(parts, PLANE), taken, (probe, HBM), (measured, HBM), (tabs, HBM)),
         8 * 24 * width**3,
-        [(8, rows, cols), (8, rows + 2 * band, cols)],
+        [(8, rows, cols), (8, rows + 2 * band, cols), probe.shape, (width, width), pltpu.VMEM(tabs.shape, tabs.dtype)],
+        copies=4,
     )
     *sums, lower0, lower1, probe_band = call(
         add_kernel,
@@ -322,9 +364,17 @@
         above.append(lax.ppermute(lower, AROUND, shift_pairs(pairs, -1, turn // 2, turn % 2)))
     sums = deal(sums, PLANE[:2])
     probe_band = sum_over(probe_band, "pair", pairs)
-    probe_grad = lax.all_gather(probe_band, PLANE, axis=0, tiled=True).reshape(probe.shape)
-    object_grad = call(join_kernel, shape(planes, rows, cols), (where,), (*sums, *above), planes * rows * cols)
-    return (object_grad.reshape(object_field.shape), probe_grad)
+    probe_grad = lax.all_gather(probe_band, PLANE, axis=0, tiled=True)
+    object_grad, probe_grad = call(
+        join_kernel,
+        [(shape(planes, rows, cols), HBM), (shape(*probe_grad.shape), HBM)],
+        (where,),
+        (*sums, *above, (probe_grad, ANY)),
+        planes * rows * cols,
+        [(planes, rows, cols)],
+        copies=5,
+    )
+    return (object_grad.reshape(object_field.shape), probe_grad.reshape(probe.shape))
 
 
 def solution(mesh):

time: 112 us -> 106 us (0.946)
  local copies, waits for them, and re-layouts: 9.07 us -> 0.46 us
  Pallas kernels: 13.8 us -> 17 us
  waiting for transfers between devices: 32.7 us -> 31.5 us
    unnamed x15 -> x0, local copies, waits for them, and re-layouts: 7.65 us -> none
    pallas_call x5, Pallas kernels: 13.8 us -> 17 us  [call(): pl.pallas_call(kernel, out_shape=[x for x, unused in outs], in_specs=[SME...]
  transfers between devices with their start and end apart: 32 -> 32, of which waited for: 8 -> 9; matrix products, arithmetic and copies ran while one was open for 1% -> 1% of each run, Pallas kernels for 1% -> 0%
where the time goes in v6:
time: 106 us
  starting transfers between devices  46.1 us (43%)
  waiting for transfers between devices  31.5 us (30%)
  Pallas kernels  17 us (16%)
  blocking collectives  9.61 us (9%)
    ppermute x20, waiting for transfers between devices, deal(): lax.ppermute(values[turn], axes, [(k, k ^ turn) for k in range(count)])  28 us
    ppermute x20, starting transfers between devices, deal(): lax.ppermute(values[turn], axes, [(k, k ^ turn) for k in range(count)])  25.7 us
    pallas_call x5, Pallas kernels, call(): pl.pallas_call(kernel, out_shape=[x for x, unused in outs], in_specs=[SME...  17 us
    all_gather x1, blocking collectives, local(): probe_grad = lax.all_gather(probe_band, PLANE, axis=0, tiled=True)  9.61 us
    ppermute x4, starting transfers between devices, local(): lax.ppermute(lower, AROUND, shift_pairs(pairs, -1, turn // 2, turn % 2))  9.04 us
    ppermute x2, starting transfers between devices, sum_over(): lax.ppermute(value, axis, [(k, k ^ step) for k in range(size)])  4.12 us
    ppermute x4, starting transfers between devices, local(): lax.ppermute(dealt[turn], AROUND, shift_pairs(pairs, 1, turn // 2, turn %...  3.89 us
    ppermute x1, starting transfers between devices, local(): taken = lax.ppermute(given, 'half', [(0, 1), (1, 0)])  2.9 us
  transfers between devices with their start and end apart: 32, of which 9 were waited for; matrix products, arithmetic and copies ran while one was open for 1% of the time, Pallas kernels for 0%

profile of v6, /device:TPU:0, one launch (start us, length us, event | category | flops | bytes accessed | tf_op | source)
XLA Modules:
  0.0 105.7 jit_solution(2073245023710662902)
XLA Ops:
  0.6 0.5 collective-permute-start
  1.1 0.1 pad_add_fusion.where
  1.2 1.0 collective-permute-done.sibling
  2.2 2.0 %shard_map.77 = (f32[264,128]{1,0:T(8,128)S(1)}, f32[264,128]{1,0:T(8,128)S(1)}, f32[264,128]{1,0:T(8,128)S(1)}, f32[264,128]{1,0:T(8,128)S(1)}, f32[256,256]{1,0:T(8,128)S(1)}) custom-call(s32[3]{0:T(128)S(1)} %pad_add_fusion.where, s32[1,2,2]{2,1,0:T(2,128)} %offsets.1, s32[1,2,2]{2,1,0:T(2,128)S(1)} %collective-permute-done.sibling, ...), custom_call_target="tpu_custom_call" | custom-call | bytes 1851392 | tf_op jit(solution)/shard_map/pallas_call | solution.py:266
  4.2 2.9 %collective-permute-start.1 = (f32[256,256]{1,0:T(8,128)S(1)}, f32[256,256]{1,0:T(8,128)S(1)}, u32[]{:S(2)}, u32[]{:S(2)}) collective-permute-start(f32[256,256]{1,0:T(8,128)S(1)} %get-tuple-element.35), channel_id=1, source_target_pairs={{0,4},{4,0},{1,5},{5,1},{2,6},{6,2},{3,7},{7,3},{8,12},{12,8},{9,1... | collective-permute-start | bytes 786440 | tf_op jit(solution)/shard_map/ppermute | solution.py:331
  7.1 1.3 %collective-permute-start.5 = (f32[264,128]{1,0:T(8,128)S(1)}, f32[264,128]{1,0:T(8,128)S(1)}, u32[]{:S(2)}, u32[]{:S(2)}) collective-permute-start(f32[264,128]{1,0:T(8,128)S(1)} %get-tuple-element.36.refs_0_), channel_id=1, source_target_pairs={{8,0},{10,2},{16,8},{18,10},{24,16},{26,18},{9,1},{11,3},{17,9},{1... | collective-permute-start | bytes 405512 | tf_op jit(solution)/shard_map/ppermute | solution.py:329
  8.3 1.6 %collective-permute-start.2 = (f32[264,128]{1,0:T(8,128)S(1)}, f32[264,128]{1,0:T(8,128)S(1)}, u32[]{:S(2)}, u32[]{:S(2)}) collective-permute-start(f32[264,128]{1,0:T(8,128)S(1)} %get-tuple-element.37), channel_id=1, source_target_pairs={{0,2},{2,0},{4,6},{6,4},{1,3},{3,1},{5,7},{7,5},{8,10},{10,8},{12,... | collective-permute-start | bytes 405512 | tf_op jit(solution)/shard_map/ppermute | solution.py:295
  9.9 1.3 %collective-permute-start.6 = (f32[264,128]{1,0:T(8,128)S(1)}, f32[264,128]{1,0:T(8,128)S(1)}, u32[]{:S(2)}, u32[]{:S(2)}) collective-permute-start(f32[264,128]{1,0:T(8,128)S(1)} %get-tuple-element.37), channel_id=1, source_target_pairs={{10,0},{8,2},{18,8},{16,10},{26,16},{24,18},{11,1},{9,3},{19,9},{1... | collective-permute-start | bytes 405512 | tf_op jit(solution)/shard_map/ppermute | solution.py:329
  11.2 0.7 collective-permute-start.7
  11.9 2.5 %collective-permute-done.5.refs_4_ = f32[264,128]{1,0:T(8,128)S(1)} collective-permute-done((f32[264,128]{1,0:T(8,128)S(1)}, f32[264,128]{1,0:T(8,128)S(1)}, u32[]{:S(2)}, u32[]{:S(2)}) %collective-permute-start.5) | collective-permute-done | bytes 135200 | tf_op jit(solution)/shard_map/ppermute | solution.py:329
  14.3 0.7 collective-permute-start.8
  15.0 3.9 %collective-permute-start.4 = (f32[264,128]{1,0:T(8,128)S(1)}, f32[264,128]{1,0:T(8,128)S(1)}, u32[]{:S(2)}, u32[]{:S(2)}) collective-permute-start(f32[264,128]{1,0:T(8,128)S(1)} %get-tuple-element.39), channel_id=1, source_target_pairs={{0,6},{2,4},{4,2},{6,0},{1,7},{3,5},{5,3},{7,1},{8,14},{10,12},{12... | collective-permute-start | bytes 405512 | tf_op jit(solution)/shard_map/ppermute | solution.py:295
  18.9 0.1 slice_reduce_fusion.2
  19.1 0.1 collective-permute-done.6.refs_5_
  19.2 6.3 %collective-permute-done.3.refs_2_ = f32[264,128]{1,0:T(8,128)S(1)} collective-permute-done((f32[264,128]{1,0:T(8,128)S(1)}, f32[264,128]{1,0:T(8,128)S(1)}, u32[]{:S(2)}, u32[]{:S(2)}) %collective-permute-start.3) | collective-permute-done | bytes 135200 | tf_op jit(solution)/shard_map/ppermute | solution.py:295
  25.4 1.4 %shard_map.78 = (f32[256,128]{1,0:T(8,128)S(1)}, f32[256,128]{1,0:T(8,128)S(1)}, f32[256,128]{1,0:T(8,128)S(1)}, f32[256,128]{1,0:T(8,128)S(1)}, f32[256,128]{1,...) custom-call(s32[3]{0:T(128)S(1)} %pad_add_fusion.where, ...), custom_call_target="tpu_custom_call" | custom-call | flops 2097152 | bytes 2129920 | tf_op jit(solution)/shard_map/pallas_call | solution.py:266
  26.9 1.7 %collective-permute-start.10 = (f32[256,128]{1,0:T(8,128)S(1)}, f32[256,128]{1,0:T(8,128)S(1)}, u32[]{:S(2)}, u32[]{:S(2)}) collective-permute-start(f32[256,128]{1,0:T(8,128)S(1)} %get-tuple-element.42), channel_id=1, source_target_pairs={{0,2},{1,3},{2,0},{3,1},{4,6},{5,7},{6,4},{7,5},{8,10},{9,11},{10,... | collective-permute-start | bytes 393224 | tf_op jit(solution)/shard_map/ppermute | solution.py:295
  28.6 0.1 slice_reduce_fusion.1
  28.8 0.1 slice_reduce_fusion
  28.9 0.2 collective-permute-start.11
  29.1 2.5 %collective-permute-start.12 = (f32[256,128]{1,0:T(8,128)S(1)}, f32[256,128]{1,0:T(8,128)S(1)}, u32[]{:S(2)}, u32[]{:S(2)}) collective-permute-start(f32[256,128]{1,0:T(8,128)S(1)} %get-tuple-element.44), channel_id=1, source_target_pairs={{0,4},{1,5},{2,6},{3,7},{4,0},{5,1},{6,2},{7,3},{8,12},{9,13},{10,... | collective-permute-start | bytes 393224 | tf_op jit(solution)/shard_map/ppermute | solution.py:295
  31.5 2.8 %collective-permute-start.14 = (f32[256,128]{1,0:T(8,128)S(1)}, f32[256,128]{1,0:T(8,128)S(1)}, u32[]{:S(2)}, u32[]{:S(2)}) collective-permute-start(f32[256,128]{1,0:T(8,128)S(1)} %get-tuple-element.46), channel_id=1, source_target_pairs={{0,6},{1,7},{2,4},{3,5},{4,2},{5,3},{6,0},{7,1},{8,14},{9,15},{10,... | collective-permute-start | bytes 393224 | tf_op jit(solution)/shard_map/ppermute | solution.py:295
  34.3 1.3 %collective-permute-start.15 = (f32[256,128]{1,0:T(8,128)S(1)}, f32[256,128]{1,0:T(8,128)S(1)}, u32[]{:S(2)}, u32[]{:S(2)}) collective-permute-start(f32[256,128]{1,0:T(8,128)S(1)} %get-tuple-element.47), channel_id=1, source_target_pairs={{0,7},{1,6},{2,5},{3,4},{4,3},{5,2},{6,1},{7,0},{8,15},{9,14},{10,... | collective-permute-start | bytes 393224 | tf_op jit(solution)/shard_map/ppermute | solution.py:295
  35.6 0.1 slice_reduce_fusion.3
  35.8 5.1 %collective-permute-done.12.refs_4_ = f32[256,128]{1,0:T(8,128)S(1)} collective-permute-done((f32[256,128]{1,0:T(8,128)S(1)}, f32[256,128]{1,0:T(8,128)S(1)}, u32[]{:S(2)}, u32[]{:S(2)}) %collective-permute-start.12) | collective-permute-done | bytes 131104 | tf_op jit(solution)/shard_map/ppermute | solution.py:295
  40.8 2.8 %collective-permute-done.13.refs_5_ = f32[256,128]{1,0:T(8,128)S(1)} collective-permute-done((f32[256,128]{1,0:T(8,128)S(1)}, f32[256,128]{1,0:T(8,128)S(1)}, u32[]{:S(2)}, u32[]{:S(2)}) %collective-permute-start.13) | collective-permute-done | bytes 131104 | tf_op jit(solution)/shard_map/ppermute | solution.py:295
  43.6 9.8 %shard_map.79 = (f32[384,128]{1,0:T(8,128)S(1)}, f32[384,128]{1,0:T(8,128)S(1)}, f32[384,128]{1,0:T(8,128)S(1)}, f32[384,128]{1,0:T(8,128)S(1)}, f32[384,128]{1,...) custom-call(s32[3]{0:T(128)S(1)} %pad_add_fusion.where, ...), custom_call_target="tpu_custom_call" | custom-call | flops 3221225472 | bytes 6553600 | tf_op jit(solution)/shard_map/pallas_call | solution.py:266
  53.4 0.2 collective-permute-start.16
  53.6 1.7 %collective-permute-start.17 = (f32[384,128]{1,0:T(8,128)S(1)}, f32[384,128]{1,0:T(8,128)S(1)}, u32[]{:S(2)}, u32[]{:S(2)}) collective-permute-start(f32[384,128]{1,0:T(8,128)S(1)} %get-tuple-element.51), channel_id=1, source_target_pairs={{0,2},{1,3},{2,0},{3,1},{4,6},{5,7},{6,4},{7,5},{8,10},{9,11},{10,... | collective-permute-start | bytes 589832 | tf_op jit(solution)/shard_map/ppermute | solution.py:295
  55.3 1.7 %collective-permute-start.19 = (f32[384,128]{1,0:T(8,128)S(1)}, f32[384,128]{1,0:T(8,128)S(1)}, u32[]{:S(2)}, u32[]{:S(2)}) collective-permute-start(f32[384,128]{1,0:T(8,128)S(1)} %get-tuple-element.53), channel_id=1, source_target_pairs={{0,4},{1,5},{2,6},{3,7},{4,0},{5,1},{6,2},{7,3},{8,12},{9,13},{10,... | collective-permute-start | bytes 589832 | tf_op jit(solution)/shard_map/ppermute | solution.py:295
  57.0 0.1 collective-permute-start.20
  57.1 2.8 %collective-permute-start.21 = (f32[384,128]{1,0:T(8,128)S(1)}, f32[384,128]{1,0:T(8,128)S(1)}, u32[]{:S(2)}, u32[]{:S(2)}) collective-permute-start(f32[384,128]{1,0:T(8,128)S(1)} %get-tuple-element.55), channel_id=1, source_target_pairs={{0,6},{1,7},{2,4},{3,5},{4,2},{5,3},{6,0},{7,1},{8,14},{9,15},{10,... | collective-permute-start | bytes 589832 | tf_op jit(solution)/shard_map/ppermute | solution.py:295
  60.0 1.4 %collective-permute-done.17.refs_2_ = f32[384,128]{1,0:T(8,128)S(1)} collective-permute-done((f32[384,128]{1,0:T(8,128)S(1)}, f32[384,128]{1,0:T(8,128)S(1)}, u32[]{:S(2)}, u32[]{:S(2)}) %collective-permute-start.17) | collective-permute-done | bytes 196640 | tf_op jit(solution)/shard_map/ppermute | solution.py:295
  61.3 0.9 collective-permute-start.22
  62.2 2.5 %collective-permute-done.18.refs_3_ = f32[384,128]{1,0:T(8,128)S(1)} collective-permute-done((f32[384,128]{1,0:T(8,128)S(1)}, f32[384,128]{1,0:T(8,128)S(1)}, u32[]{:S(2)}, u32[]{:S(2)}) %collective-permute-start.18) | collective-permute-done | bytes 196640 | tf_op jit(solution)/shard_map/ppermute | solution.py:295
  64.7 10.0 %collective-permute-done.20.refs_5_ = f32[384,128]{1,0:T(8,128)S(1)} collective-permute-done((f32[384,128]{1,0:T(8,128)S(1)}, f32[384,128]{1,0:T(8,128)S(1)}, u32[]{:S(2)}, u32[]{:S(2)}) %collective-permute-start.20) | collective-permute-done | bytes 196640 | tf_op jit(solution)/shard_map/ppermute | solution.py:295
  74.8 2.3 %shard_map.80 = (f32[256,128]{1,0:T(8,128)S(1)}, f32[256,128]{1,0:T(8,128)S(1)}, f32[256,128]{1,0:T(8,128)S(1)}, f32[256,128]{1,0:T(8,128)S(1)}, f32[256,128]{1,...) custom-call(s32[3]{0:T(128)S(1)} %pad_add_fusion.where, s32[1,2]{1,0:T(1,128)} %slot_range.5, ...), custom_call_target="tpu_custom_call" | custom-call | flops 6291456 | bytes 2424832 | tf_op jit(solution)/shard_map/pallas_call | solution.py:266
  77.1 1.8 %collective-permute-start.30 = (f32[64,256]{1,0:T(8,128)S(1)}, f32[64,256]{1,0:T(8,128)S(1)}, u32[]{:S(2)}, u32[]{:S(2)}) collective-permute-start(f32[64,256]{1,0:T(8,128)S(1)} %get-tuple-element.63), channel_id=1, source_target_pairs={{0,8},{8,0},{16,24},{24,16},{1,9},{9,1},{17,25},{25,17},{2,10},{10... | collective-permute-start | bytes 196616 | tf_op jit(solution)/shard_map/ppermute | solution.py:286
  78.9 1.3 %collective-permute-start.23 = (f32[256,128]{1,0:T(8,128)S(1)}, f32[256,128]{1,0:T(8,128)S(1)}, u32[]{:S(2)}, u32[]{:S(2)}) collective-permute-start(f32[256,128]{1,0:T(8,128)S(1)} %get-tuple-element.58), channel_id=1, source_target_pairs={{0,2},{2,0},{4,6},{6,4},{1,3},{3,1},{5,7},{7,5},{8,10},{10,8},{12,... | collective-permute-start | bytes 393224 | tf_op jit(solution)/shard_map/ppermute | solution.py:295
  80.2 1.9 %collective-permute-start.24 = (f32[256,128]{1,0:T(8,128)S(1)}, f32[256,128]{1,0:T(8,128)S(1)}, u32[]{:S(2)}, u32[]{:S(2)}) collective-permute-start(f32[256,128]{1,0:T(8,128)S(1)} %get-tuple-element.59), channel_id=1, source_target_pairs={{0,4},{2,6},{4,0},{6,2},{1,5},{3,7},{5,1},{7,3},{8,12},{10,14},{12... | collective-permute-start | bytes 393224 | tf_op jit(solution)/shard_map/ppermute | solution.py:295
  82.1 2.3 %collective-permute-start.31 = (f32[64,256]{1,0:T(8,128)S(1)}, f32[64,256]{1,0:T(8,128)S(1)}, u32[]{:S(2)}, u32[]{:S(2)}) collective-permute-start(f32[64,256]{1,0:T(8,128)S(1)} %add.6), channel_id=1, source_target_pairs={{0,16},{8,24},{16,0},{24,8},{1,17},{9,25},{17,1},{25,9},{2,18},{10... | collective-permute-start | bytes 196616 | tf_op jit(solution)/shard_map/ppermute | solution.py:286
  84.4 0.7 collective-permute-start.28
  85.1 3.7 %collective-permute-start.26 = (f32[256,128]{1,0:T(8,128)S(1)}, f32[256,128]{1,0:T(8,128)S(1)}, u32[]{:S(2)}, u32[]{:S(2)}) collective-permute-start(f32[256,128]{1,0:T(8,128)S(1)} %get-tuple-element.61), channel_id=1, source_target_pairs={{0,8},{2,10},{8,16},{10,18},{16,24},{18,26},{1,9},{3,11},{9,17},{1... | collective-permute-start | bytes 393224 | tf_op jit(solution)/shard_map/ppermute | solution.py:364
  88.8 1.0 collective-permute-start.25
  89.7 0.7 collective-permute-start.29
  90.4 4.0 %collective-permute-start.27 = (f32[256,128]{1,0:T(8,128)S(1)}, f32[256,128]{1,0:T(8,128)S(1)}, u32[]{:S(2)}, u32[]{:S(2)}) collective-permute-start(f32[256,128]{1,0:T(8,128)S(1)} %get-tuple-element.62), channel_id=1, source_target_pairs={{0,10},{2,8},{8,18},{10,16},{16,26},{18,24},{1,11},{3,9},{9,19},{1... | collective-permute-start | bytes 393224 | tf_op jit(solution)/shard_map/ppermute | solution.py:364
  94.5 9.6 %all_gather.3.refs_8_ = f32[512,256]{1,0:T(8,128)S(1)} all-gather(f32[64,256]{1,0:T(8,128)S(1)} %add.7), channel_id=1, replica_groups=mesh['pair'=4,'half'=2,'col'=2,'core'=2] {'half','col','core'}, dimensions={0}, use_global_device_ids=true | all-gather | bytes 589824 | tf_op jit(solution)/shard_map/all_gather | solution.py:367
  104.1 1.5 %shard_map.81 = (f32[4,256,128]{2,1,0:T(8,128)}, f32[512,256]{1,0:T(8,128)}) custom-call(s32[3]{0:T(128)S(1)} %pad_add_fusion.where, f32[256,128]{1,0:T(8,128)S(1)} %get-tuple-element.57.refs_0_, f32[256,128]{1,0:T(8,128)S(1)} %collective-permute-done.23.refs_1_, f32[256,128]{1,0:T(8,128)S(1)} %collective-permute-done.24.refs_2_, ...), custom_call_target="tpu_custom_call" | custom-call | flops 131072 | bytes 2621440 | tf_op jit(solution)/shard_map/pallas_call | solution.py:266
  (30 shorter events, 0.2 us)
Async XLA Ops:
  0.6 1.5 %collective-permute-start = (s32[1,2,2]{2,1,0:T(2,128)}, s32[1,2,2]{2,1,0:T(2,128)S(1)}, u32[]{:S(2)}, u32[]{:S(2)}) collective-permute-start(s32[1,2,2]{2,1,0:T(2,128)} %offsets.1), channel_id=1, source_target_pairs={{0,1},{1,0},{2,3},{3,2},{4,5},{5,4},{6,7},{7,6},{8,9},{9,8},{10,11... | collective-permute-start | bytes 56 | tf_op jit(solution)/shard_map/ppermute | solution.py:316
  4.2 10.9 %collective-permute-start.1 = (f32[256,256]{1,0:T(8,128)S(1)}, f32[256,256]{1,0:T(8,128)S(1)}, u32[]{:S(2)}, u32[]{:S(2)}) collective-permute-start(f32[256,256]{1,0:T(8,128)S(1)} %get-tuple-element.35), channel_id=1, source_target_pairs={{0,4},{4,0},{1,5},{5,1},{2,6},{6,2},{3,7},{7,3},{8,12},{12,8},{9,1... | collective-permute-start | bytes 786440 | tf_op jit(solution)/shard_map/ppermute | solution.py:331
  7.1 7.3 %collective-permute-start.5 = (f32[264,128]{1,0:T(8,128)S(1)}, f32[264,128]{1,0:T(8,128)S(1)}, u32[]{:S(2)}, u32[]{:S(2)}) collective-permute-start(f32[264,128]{1,0:T(8,128)S(1)} %get-tuple-element.36.refs_0_), channel_id=1, source_target_pairs={{8,0},{10,2},{16,8},{18,10},{24,16},{26,18},{9,1},{11,3},{17,9},{1... | collective-permute-start | bytes 405512 | tf_op jit(solution)/shard_map/ppermute | solution.py:329
  8.3 6.0 %collective-permute-start.2 = (f32[264,128]{1,0:T(8,128)S(1)}, f32[264,128]{1,0:T(8,128)S(1)}, u32[]{:S(2)}, u32[]{:S(2)}) collective-permute-start(f32[264,128]{1,0:T(8,128)S(1)} %get-tuple-element.37), channel_id=1, source_target_pairs={{0,2},{2,0},{4,6},{6,4},{1,3},{3,1},{5,7},{7,5},{8,10},{10,8},{12,... | collective-permute-start | bytes 405512 | tf_op jit(solution)/shard_map/ppermute | solution.py:295
  9.9 9.3 %collective-permute-start.6 = (f32[264,128]{1,0:T(8,128)S(1)}, f32[264,128]{1,0:T(8,128)S(1)}, u32[]{:S(2)}, u32[]{:S(2)}) collective-permute-start(f32[264,128]{1,0:T(8,128)S(1)} %get-tuple-element.37), channel_id=1, source_target_pairs={{10,0},{8,2},{18,8},{16,10},{26,16},{24,18},{11,1},{9,3},{19,9},{1... | collective-permute-start | bytes 405512 | tf_op jit(solution)/shard_map/ppermute | solution.py:329
  11.2 8.0 %collective-permute-start.7 = (f32[264,128]{1,0:T(8,128)S(1)}, f32[264,128]{1,0:T(8,128)S(1)}, u32[]{:S(2)}, u32[]{:S(2)}) collective-permute-start(f32[264,128]{1,0:T(8,128)S(1)} %get-tuple-element.38), channel_id=1, source_target_pairs={{8,4},{10,6},{16,12},{18,14},{24,20},{26,22},{9,5},{11,7},{17,13},... | collective-permute-start | bytes 405512 | tf_op jit(solution)/shard_map/ppermute | solution.py:329
  14.3 11.1 %collective-permute-start.3 = (f32[264,128]{1,0:T(8,128)S(1)}, f32[264,128]{1,0:T(8,128)S(1)}, u32[]{:S(2)}, u32[]{:S(2)}) collective-permute-start(f32[264,128]{1,0:T(8,128)S(1)} %get-tuple-element.38), channel_id=1, source_target_pairs={{0,4},{2,6},{4,0},{6,2},{1,5},{3,7},{5,1},{7,3},{8,12},{10,14},{12... | collective-permute-start | bytes 405512 | tf_op jit(solution)/shard_map/ppermute | solution.py:295
  14.3 11.1 %collective-permute-start.8 = (f32[264,128]{1,0:T(8,128)S(1)}, f32[264,128]{1,0:T(8,128)S(1)}, u32[]{:S(2)}, u32[]{:S(2)}) collective-permute-start(f32[264,128]{1,0:T(8,128)S(1)} %get-tuple-element.39), channel_id=1, source_target_pairs={{10,4},{8,6},{18,12},{16,14},{26,20},{24,22},{11,5},{9,7},{19,13},... | collective-permute-start | bytes 405512 | tf_op jit(solution)/shard_map/ppermute | solution.py:329
  15.0 10.4 %collective-permute-start.4 = (f32[264,128]{1,0:T(8,128)S(1)}, f32[264,128]{1,0:T(8,128)S(1)}, u32[]{:S(2)}, u32[]{:S(2)}) collective-permute-start(f32[264,128]{1,0:T(8,128)S(1)} %get-tuple-element.39), channel_id=1, source_target_pairs={{0,6},{2,4},{4,2},{6,0},{1,7},{3,5},{5,3},{7,1},{8,14},{10,12},{12... | collective-permute-start | bytes 405512 | tf_op jit(solution)/shard_map/ppermute | solution.py:295
  26.8 4.7 %collective-permute-start.9 = (f32[256,128]{1,0:T(8,128)S(1)}, f32[256,128]{1,0:T(8,128)S(1)}, u32[]{:S(2)}, u32[]{:S(2)}) collective-permute-start(f32[256,128]{1,0:T(8,128)S(1)} %get-tuple-element.41), channel_id=1, source_target_pairs={{0,1},{1,0},{2,3},{3,2},{4,5},{5,4},{6,7},{7,6},{8,9},{9,8},{10,11... | collective-permute-start | bytes 393224 | tf_op jit(solution)/shard_map/ppermute | solution.py:295
  26.9 7.4 %collective-permute-start.10 = (f32[256,128]{1,0:T(8,128)S(1)}, f32[256,128]{1,0:T(8,128)S(1)}, u32[]{:S(2)}, u32[]{:S(2)}) collective-permute-start(f32[256,128]{1,0:T(8,128)S(1)} %get-tuple-element.42), channel_id=1, source_target_pairs={{0,2},{1,3},{2,0},{3,1},{4,6},{5,7},{6,4},{7,5},{8,10},{9,11},{10,... | collective-permute-start | bytes 393224 | tf_op jit(solution)/shard_map/ppermute | solution.py:295
  28.9 6.9 %collective-permute-start.11 = (f32[256,128]{1,0:T(8,128)S(1)}, f32[256,128]{1,0:T(8,128)S(1)}, u32[]{:S(2)}, u32[]{:S(2)}) collective-permute-start(f32[256,128]{1,0:T(8,128)S(1)} %get-tuple-element.43), channel_id=1, source_target_pairs={{0,3},{1,2},{2,1},{3,0},{4,7},{5,6},{6,5},{7,4},{8,11},{9,10},{10,... | collective-permute-start | bytes 393224 | tf_op jit(solution)/shard_map/ppermute | solution.py:295
  29.1 11.8 %collective-permute-start.12 = (f32[256,128]{1,0:T(8,128)S(1)}, f32[256,128]{1,0:T(8,128)S(1)}, u32[]{:S(2)}, u32[]{:S(2)}) collective-permute-start(f32[256,128]{1,0:T(8,128)S(1)} %get-tuple-element.44), channel_id=1, source_target_pairs={{0,4},{1,5},{2,6},{3,7},{4,0},{5,1},{6,2},{7,3},{8,12},{9,13},{10,... | collective-permute-start | bytes 393224 | tf_op jit(solution)/shard_map/ppermute | solution.py:295
  31.5 12.1 %collective-permute-start.13 = (f32[256,128]{1,0:T(8,128)S(1)}, f32[256,128]{1,0:T(8,128)S(1)}, u32[]{:S(2)}, u32[]{:S(2)}) collective-permute-start(f32[256,128]{1,0:T(8,128)S(1)} %get-tuple-element.45), channel_id=1, source_target_pairs={{0,5},{1,4},{2,7},{3,6},{4,1},{5,0},{6,3},{7,2},{8,13},{9,12},{10,... | collective-permute-start | bytes 393224 | tf_op jit(solution)/shard_map/ppermute | solution.py:295
  31.5 12.1 %collective-permute-start.14 = (f32[256,128]{1,0:T(8,128)S(1)}, f32[256,128]{1,0:T(8,128)S(1)}, u32[]{:S(2)}, u32[]{:S(2)}) collective-permute-start(f32[256,128]{1,0:T(8,128)S(1)} %get-tuple-element.46), channel_id=1, source_target_pairs={{0,6},{1,7},{2,4},{3,5},{4,2},{5,3},{6,0},{7,1},{8,14},{9,15},{10,... | collective-permute-start | bytes 393224 | tf_op jit(solution)/shard_map/ppermute | solution.py:295
  34.3 9.3 %collective-permute-start.15 = (f32[256,128]{1,0:T(8,128)S(1)}, f32[256,128]{1,0:T(8,128)S(1)}, u32[]{:S(2)}, u32[]{:S(2)}) collective-permute-start(f32[256,128]{1,0:T(8,128)S(1)} %get-tuple-element.47), channel_id=1, source_target_pairs={{0,7},{1,6},{2,5},{3,4},{4,3},{5,2},{6,1},{7,0},{8,15},{9,14},{10,... | collective-permute-start | bytes 393224 | tf_op jit(solution)/shard_map/ppermute | solution.py:295
  53.4 3.8 %collective-permute-start.16 = (f32[384,128]{1,0:T(8,128)S(1)}, f32[384,128]{1,0:T(8,128)S(1)}, u32[]{:S(2)}, u32[]{:S(2)}) collective-permute-start(f32[384,128]{1,0:T(8,128)S(1)} %get-tuple-element.50), channel_id=1, source_target_pairs={{0,1},{1,0},{2,3},{3,2},{4,5},{5,4},{6,7},{7,6},{8,9},{9,8},{10,11... | collective-permute-start | bytes 589832 | tf_op jit(solution)/shard_map/ppermute | solution.py:295
  53.6 7.7 %collective-permute-start.17 = (f32[384,128]{1,0:T(8,128)S(1)}, f32[384,128]{1,0:T(8,128)S(1)}, u32[]{:S(2)}, u32[]{:S(2)}) collective-permute-start(f32[384,128]{1,0:T(8,128)S(1)} %get-tuple-element.51), channel_id=1, source_target_pairs={{0,2},{1,3},{2,0},{3,1},{4,6},{5,7},{6,4},{7,5},{8,10},{9,11},{10,... | collective-permute-start | bytes 589832 | tf_op jit(solution)/shard_map/ppermute | solution.py:295
  55.3 9.5 %collective-permute-start.18 = (f32[384,128]{1,0:T(8,128)S(1)}, f32[384,128]{1,0:T(8,128)S(1)}, u32[]{:S(2)}, u32[]{:S(2)}) collective-permute-start(f32[384,128]{1,0:T(8,128)S(1)} %get-tuple-element.52), channel_id=1, source_target_pairs={{0,3},{1,2},{2,1},{3,0},{4,7},{5,6},{6,5},{7,4},{8,11},{9,10},{10,... | collective-permute-start | bytes 589832 | tf_op jit(solution)/shard_map/ppermute | solution.py:295
  55.3 9.4 %collective-permute-start.19 = (f32[384,128]{1,0:T(8,128)S(1)}, f32[384,128]{1,0:T(8,128)S(1)}, u32[]{:S(2)}, u32[]{:S(2)}) collective-permute-start(f32[384,128]{1,0:T(8,128)S(1)} %get-tuple-element.53), channel_id=1, source_target_pairs={{0,4},{1,5},{2,6},{3,7},{4,0},{5,1},{6,2},{7,3},{8,12},{9,13},{10,... | collective-permute-start | bytes 589832 | tf_op jit(solution)/shard_map/ppermute | solution.py:295
  57.0 17.7 %collective-permute-start.20 = (f32[384,128]{1,0:T(8,128)S(1)}, f32[384,128]{1,0:T(8,128)S(1)}, u32[]{:S(2)}, u32[]{:S(2)}) collective-permute-start(f32[384,128]{1,0:T(8,128)S(1)} %get-tuple-element.54), channel_id=1, source_target_pairs={{0,5},{1,4},{2,7},{3,6},{4,1},{5,0},{6,3},{7,2},{8,13},{9,12},{10,... | collective-permute-start | bytes 589832 | tf_op jit(solution)/shard_map/ppermute | solution.py:295
  57.1 17.6 %collective-permute-start.21 = (f32[384,128]{1,0:T(8,128)S(1)}, f32[384,128]{1,0:T(8,128)S(1)}, u32[]{:S(2)}, u32[]{:S(2)}) collective-permute-start(f32[384,128]{1,0:T(8,128)S(1)} %get-tuple-element.55), channel_id=1, source_target_pairs={{0,6},{1,7},{2,4},{3,5},{4,2},{5,3},{6,0},{7,1},{8,14},{9,15},{10,... | collective-permute-start | bytes 589832 | tf_op jit(solution)/shard_map/ppermute | solution.py:295
  61.3 13.4 %collective-permute-start.22 = (f32[384,128]{1,0:T(8,128)S(1)}, f32[384,128]{1,0:T(8,128)S(1)}, u32[]{:S(2)}, u32[]{:S(2)}) collective-permute-start(f32[384,128]{1,0:T(8,128)S(1)} %get-tuple-element.56), channel_id=1, source_target_pairs={{0,7},{1,6},{2,5},{3,4},{4,3},{5,2},{6,1},{7,0},{8,15},{9,14},{10,... | collective-permute-start | bytes 589832 | tf_op jit(solution)/shard_map/ppermute | solution.py:295
  77.1 5.0 %collective-permute-start.30 = (f32[64,256]{1,0:T(8,128)S(1)}, f32[64,256]{1,0:T(8,128)S(1)}, u32[]{:S(2)}, u32[]{:S(2)}) collective-permute-start(f32[64,256]{1,0:T(8,128)S(1)} %get-tuple-element.63), channel_id=1, source_target_pairs={{0,8},{8,0},{16,24},{24,16},{1,9},{9,1},{17,25},{25,17},{2,10},{10... | collective-permute-start | bytes 196616 | tf_op jit(solution)/shard_map/ppermute | solution.py:286
  78.9 10.8 %collective-permute-start.23 = (f32[256,128]{1,0:T(8,128)S(1)}, f32[256,128]{1,0:T(8,128)S(1)}, u32[]{:S(2)}, u32[]{:S(2)}) collective-permute-start(f32[256,128]{1,0:T(8,128)S(1)} %get-tuple-element.58), channel_id=1, source_target_pairs={{0,2},{2,0},{4,6},{6,4},{1,3},{3,1},{5,7},{7,5},{8,10},{10,8},{12,... | collective-permute-start | bytes 393224 | tf_op jit(solution)/shard_map/ppermute | solution.py:295
  80.2 10.2 %collective-permute-start.24 = (f32[256,128]{1,0:T(8,128)S(1)}, f32[256,128]{1,0:T(8,128)S(1)}, u32[]{:S(2)}, u32[]{:S(2)}) collective-permute-start(f32[256,128]{1,0:T(8,128)S(1)} %get-tuple-element.59), channel_id=1, source_target_pairs={{0,4},{2,6},{4,0},{6,2},{1,5},{3,7},{5,1},{7,3},{8,12},{10,14},{12... | collective-permute-start | bytes 393224 | tf_op jit(solution)/shard_map/ppermute | solution.py:295
  82.1 6.7 %collective-permute-start.31 = (f32[64,256]{1,0:T(8,128)S(1)}, f32[64,256]{1,0:T(8,128)S(1)}, u32[]{:S(2)}, u32[]{:S(2)}) collective-permute-start(f32[64,256]{1,0:T(8,128)S(1)} %add.6), channel_id=1, source_target_pairs={{0,16},{8,24},{16,0},{24,8},{1,17},{9,25},{17,1},{25,9},{2,18},{10... | collective-permute-start | bytes 196616 | tf_op jit(solution)/shard_map/ppermute | solution.py:286
  84.4 19.7 %collective-permute-start.28 = (f32[256,128]{1,0:T(8,128)S(1)}, f32[256,128]{1,0:T(8,128)S(1)}, u32[]{:S(2)}, u32[]{:S(2)}) collective-permute-start(f32[256,128]{1,0:T(8,128)S(1)} %get-tuple-element.61), channel_id=1, source_target_pairs={{4,8},{6,10},{12,16},{14,18},{20,24},{22,26},{5,9},{7,11},{13,17},... | collective-permute-start | bytes 393224 | tf_op jit(solution)/shard_map/ppermute | solution.py:364
  85.1 19.0 %collective-permute-start.26 = (f32[256,128]{1,0:T(8,128)S(1)}, f32[256,128]{1,0:T(8,128)S(1)}, u32[]{:S(2)}, u32[]{:S(2)}) collective-permute-start(f32[256,128]{1,0:T(8,128)S(1)} %get-tuple-element.61), channel_id=1, source_target_pairs={{0,8},{2,10},{8,16},{10,18},{16,24},{18,26},{1,9},{3,11},{9,17},{1... | collective-permute-start | bytes 393224 | tf_op jit(solution)/shard_map/ppermute | solution.py:364
  88.8 15.3 %collective-permute-start.25 = (f32[256,128]{1,0:T(8,128)S(1)}, f32[256,128]{1,0:T(8,128)S(1)}, u32[]{:S(2)}, u32[]{:S(2)}) collective-permute-start(f32[256,128]{1,0:T(8,128)S(1)} %get-tuple-element.60), channel_id=1, source_target_pairs={{0,6},{2,4},{4,2},{6,0},{1,7},{3,5},{5,3},{7,1},{8,14},{10,12},{12... | collective-permute-start | bytes 393224 | tf_op jit(solution)/shard_map/ppermute | solution.py:295
  89.7 14.4 %collective-permute-start.29 = (f32[256,128]{1,0:T(8,128)S(1)}, f32[256,128]{1,0:T(8,128)S(1)}, u32[]{:S(2)}, u32[]{:S(2)}) collective-permute-start(f32[256,128]{1,0:T(8,128)S(1)} %get-tuple-element.62), channel_id=1, source_target_pairs={{4,10},{6,8},{12,18},{14,16},{20,26},{22,24},{5,11},{7,9},{13,19},... | collective-permute-start | bytes 393224 | tf_op jit(solution)/shard_map/ppermute | solution.py:364
  90.4 13.7 %collective-permute-start.27 = (f32[256,128]{1,0:T(8,128)S(1)}, f32[256,128]{1,0:T(8,128)S(1)}, u32[]{:S(2)}, u32[]{:S(2)}) collective-permute-start(f32[256,128]{1,0:T(8,128)S(1)} %get-tuple-element.62), channel_id=1, source_target_pairs={{0,10},{2,8},{8,18},{10,16},{16,26},{18,24},{1,11},{3,9},{9,19},{1... | collective-permute-start | bytes 393224 | tf_op jit(solution)/shard_map/ppermute | solution.py:364

commit v7 on v6

--- a/solution.py
+++ b/solution.py
@@ -12,7 +12,7 @@
 
 GRAD_WEIGHT = 0.0625
 PLANE = ("half", "col", "core")
-AROUND = ("pair", "half", "col")
+EIGHT, FOUR = (1, 2, 6, 7, 4, 3, 5, 0), (3, 1, 2, 0)
 VMEM_LIMIT = 24 * 1024 * 1024
 
 
@@ -92,7 +92,7 @@
     outs, given, sems = refs[:4], refs[4], refs[5]
     mine, core = 2 * where[0] + where[1], where[2]
     rows, cols = block.shape[1:]
-    pairs = [(block.at[jnp.bitwise_xor(mine, turn)], out.at[pl.ds(0, rows)]) for turn, out in enumerate(outs)]
+    pairs = [(block.at[jnp.bitwise_xor(mine, turn)], out.at[pl.ds(0, rows)]) for turn, out in zip(FOUR, outs)]
     copies = fetch([*pairs, (measured.at[0, 1 - where[0]], given)], sems)
     lines = []
     for holder in range(2):
@@ -107,16 +107,20 @@
         copy.wait()
 
 
+def lowest_kernel(where, *refs):
+    gotten, out = dict(zip(FOUR, refs)), refs[4]
+    rows = out.shape[1]
+    for turn in range(2):
+        out[turn] = jnp.where(where[0] == 0, gotten[turn][:rows], gotten[2 + turn][:rows])
+
+
 def pick_kernel(where, slot_range, *refs):
-    gotten, lower_planes, outs, (own, below, parts) = refs[:4], refs[4:8], refs[8:16], refs[16:]
+    gotten, below, outs, (own, parts) = dict(zip(FOUR, refs)), refs[4], refs[5:13], refs[13:]
     rows, cols = outs[0].shape
     half, col, core = where[0], where[1], where[2]
     mine = 2 * half + col
     for turn in range(4):
         own[jnp.bitwise_xor(mine, turn)] = gotten[turn][...]
-    for turn in range(2):
-        plane = jnp.where(half == 0, lower_planes[turn][:rows], lower_planes[2 + turn][:rows])
-        below[jnp.bitwise_xor(col, turn)] = plane
     split_at = slot_range[0, 1 - half]
     row_ids = lax.broadcasted_iota(jnp.int32, (rows, cols), 0).astype(jnp.float32)
     col_ids = (lax.broadcasted_iota(jnp.int32, (rows, cols), 1) + core * cols).astype(jnp.float32)
@@ -130,16 +134,16 @@
         def merged(side, lower=lower, upper_rows=upper_rows):
             second = own[2 + side, :rows]
             top = jnp.where(lower == 1, second, own[side, :rows])
-            bottom = jnp.where(lower == 1, below[side], second)
+            bottom = jnp.where(lower == 1, below[jnp.bitwise_xor(col, side)], second)
             return jnp.where(upper_rows, top, bottom)
 
         parts[place] = jnp.where(left_cols, merged(0), merged(1))
-    for turn, out in enumerate(outs):
+    for turn, out in zip(EIGHT, outs):
         out[...] = parts[jnp.bitwise_xor(2 * mine + core, turn)]
 
 
 def position_kernel(where, slot_range, offs, *refs):
-    gotten, taken, (probe_from, measured, tabs_from), outs = refs[:8], refs[8], refs[9:12], refs[12:20]
+    gotten, taken, (probe_from, measured, tabs_from), outs = dict(zip(EIGHT, refs)), refs[8], refs[9:12], refs[12:20]
     patch, grad, probe, kept, tabs, sems = refs[20:]
     half, col, core = where[0], where[1], where[2]
     mine = 2 * half + col
@@ -202,20 +206,20 @@
             rows = value[step * band : (step + 1) * band]
             grad[4 * part + step, width : width + band] = rows[:, :lanes]
             grad[4 * part + step, width + band :] = rows[:, lanes:]
-    for turn, out in enumerate(outs):
+    for turn, out in zip(EIGHT, outs):
         out[...] = grad[jnp.bitwise_xor(flat, turn)]
 
 
 def add_kernel(where, slot_range, offs, *refs):
-    parts, outs, below, probe_band, own = refs[:8], refs[8:12], refs[12:14], refs[14], refs[15]
-    rows, cols = outs[0].shape
+    parts, (own, below, probe_band) = refs[:8], refs[8:]
+    rows, cols = own.shape[1:]
     half, col, core = where[0], where[1], where[2]
     mine = 2 * half + col
     split_at = slot_range[0, 1 - half]
     row_ids = lax.broadcasted_iota(jnp.int32, (rows, cols), 0)
     col_ids = lax.broadcasted_iota(jnp.int32, (rows, cols), 1) + core * cols
     places = []
-    for turn in range(8):
+    for turn in EIGHT:
         flat = jnp.bitwise_xor(2 * mine + core, turn)
         slot = slot_of(flat // 4, (flat // 2) % 2, flat % 2)
         places.append(slot_place(offs, mine, split_at, slot))
@@ -227,13 +231,11 @@
             value = jnp.where((row_ids >= first) & (row_ids < last), part[:rows], 0.0)
             left = jnp.where(col_ids >= col_at, value, 0.0)
             sums = [sums[0] + left, sums[1] + (value - left)]
-        if strip < 2:
-            own[2 * strip], own[2 * strip + 1] = sums
-        else:
-            below[0][...] = jnp.where(col == 0, sums[0], sums[1])
-            below[1][...] = jnp.where(col == 0, sums[1], sums[0])
-    for turn, out in enumerate(outs):
-        out[...] = own[jnp.bitwise_xor(mine, turn)]
+        for side in range(2):
+            if strip < 2:
+                own[2 * strip + side] = sums[side]
+            else:
+                below[jnp.bitwise_xor(col, side)] = sums[side]
     total = parts[0][rows:]
     for part in parts[1:]:
         total = total + part[rows:]
@@ -242,14 +244,18 @@
     probe_band[:, cols:] = total[band:]
 
 
+def top_kernel(where, own, above, *outs):
+    mine = 2 * where[0] + where[1]
+    for turn, out in zip(FOUR, outs):
+        extra = jnp.where(where[0] == turn // 2, above[turn % 2], 0.0)
+        out[...] = own[jnp.bitwise_xor(mine, turn)] + extra
+
+
 def join_kernel(where, *refs):
-    (probe, out, probe_out, sums, sems) = refs[8:]
-    copies = fetch([(probe, probe_out)], sems)
+    probe, out, probe_out, sems = refs[4:]
     mine = 2 * where[0] + where[1]
-    for turn in range(4):
-        sums[turn] = refs[turn][...] + refs[4 + turn][...]
-        copies += fetch([(sums.at[turn], out.at[jnp.bitwise_xor(mine, turn)])], sems.at[pl.ds(1 + turn, 1)])
-    for copy in copies:
+    pairs = [(ref, out.at[jnp.bitwise_xor(mine, turn)]) for turn, ref in zip(FOUR, refs)]
+    for copy in fetch([(probe, probe_out), *pairs], sems):
         copy.wait()
 
 
@@ -290,19 +296,21 @@
 
 def deal(values, axes):
     count = len(values)
-    out = list(values)
-    for turn in (6, 7, 2, 4, 3, 5, 1) if count == 8 else (3, 1, 2):
-        out[turn] = lax.ppermute(values[turn], axes, [(k, k ^ turn) for k in range(count)])
-    return out
-
-
-def shift_pairs(pairs, step, half, turn):
-    out = []
-    for pair in range(pairs - 1):
-        for col in range(2):
-            lower, upper = 4 * (pair + 1) + (col ^ turn), 4 * pair + 2 * half + col
-            out.append((lower, upper) if step == 1 else (upper, lower))
-    return out
+    order = EIGHT if count == 8 else FOUR
+    return [
+        lax.ppermute(value, axes, [(k, k ^ turn) for k in range(count)]) if turn else value
+        for turn, value in zip(order, values)
+    ]
+
+
+def sum_over(value, axis, size):
+    if size & (size - 1):
+        return lax.psum(value, axis)
+    step = 1
+    while step < size:
+        value = value + lax.ppermute(value, axis, [(k, k ^ step) for k in range(size)])
+        step *= 2
+    return value
 
 
 def local(object_field, probe, offsets, slot_range, measured):
@@ -324,22 +332,23 @@
         0,
         copies=5,
     )
-    below = []
-    for turn in range(4):
-        below.append(lax.ppermute(dealt[turn], AROUND, shift_pairs(pairs, 1, turn // 2, turn % 2)))
     own = deal(dealt, PLANE[:2])
+    (lowest,) = call(lowest_kernel, [shape(2, rows, cols)], (where,), own, 0)
+    lowest, given = lax.optimization_barrier((lowest, given))
+    below = lax.ppermute(lowest, "pair", [(k, k - 1) for k in range(1, pairs)])
     taken = lax.ppermute(given, "half", [(0, 1), (1, 0)])
-    own[0], taken = lax.optimization_barrier((own[0], taken))
+    below, taken = lax.optimization_barrier((below, taken))
 
     parts = call(
         pick_kernel,
         [shape(rows, cols)] * 8,
         (where, slot_range),
-        (*own, *below),
+        (*own, below),
         32 * rows * width,
-        [(planes, rows + 8, cols), (2, rows, cols), (8, rows, cols)],
-    )
-    scalars = (where, slot_range, jnp.stack([value[rows:, 0] for value in own]).astype(jnp.int32))
+        [(planes, rows + 8, cols), (8, rows, cols)],
+    )
+    offs = [own[FOUR.index(turn)][rows:, 0] for turn in range(4)]
+    scalars = (where, slot_range, jnp.stack(offs).astype(jnp.int32))
     tabs = jnp.asarray(tables(width))
     grad = call(
         position_kernel,
@@ -350,18 +359,15 @@
         [(8, rows, cols), (8, rows + 2 * band, cols), probe.shape, (width, width), pltpu.VMEM(tabs.shape, tabs.dtype)],
         copies=4,
     )
-    *sums, lower0, lower1, probe_band = call(
+    sums, lower_sums, probe_band = call(
         add_kernel,
-        [shape(rows, cols)] * 6 + [shape(band, width)],
+        [shape(planes, rows, cols), shape(2, rows, cols), shape(band, width)],
         scalars,
         deal(grad, PLANE),
         96 * rows * width,
-        [(planes, rows, cols)],
-    )
-    above = []
-    for turn in range(4):
-        lower = (lower0, lower1)[turn % 2]
-        above.append(lax.ppermute(lower, AROUND, shift_pairs(pairs, -1, turn // 2, turn % 2)))
+    )
+    above = lax.ppermute(lower_sums, "pair", [(k, k + 1) for k in range(pairs - 1)])
+    sums = call(top_kernel, [shape(rows, cols)] * 4, (where,), (sums, above), planes * rows * cols)
     sums = deal(sums, PLANE[:2])
     probe_band = sum_over(probe_band, "pair", pairs)
     probe_grad = lax.all_gather(probe_band, PLANE, axis=0, tiled=True)
@@ -369,9 +375,8 @@
         join_kernel,
         [(shape(planes, rows, cols), HBM), (shape(*probe_grad.shape), HBM)],
         (where,),
-        (*sums, *above, (probe_grad, ANY)),
-        planes * rows * cols,
-        [(planes, rows, cols)],
+        [(x, ANY) for x in (*sums, probe_grad)],
+        0,
         copies=5,
     )
     return (object_grad.reshape(object_field.shape), probe_grad.reshape(probe.shape))

time: 106 us -> 109 us (1.028)
  waiting for transfers between devices: 31.5 us -> 48.8 us
  starting transfers between devices: 46.1 us -> 30.8 us
    ppermute x28 -> x22, starting transfers between devices: 38.6 us -> 24.5 us  [the longest x20 19.5 us: deal(): lax.ppermute(value, axes, [(k, k ^ turn) for k in range(count)])]
    ppermute x28 -> x22, waiting for transfers between devices: 30.6 us -> 42.2 us  [the longest x20 36 us: deal(): lax.ppermute(value, axes, [(k, k ^ turn) for k in range(count)])]
    ppermute x2, waiting for transfers between devices: 0.01 us -> 5.69 us  [sum_over(): lax.ppermute(value, axis, [(k, k ^ step) for k in range(size)])]
    ppermute x1, starting transfers between devices: 2.9 us -> 1.58 us  [local(): taken = lax.ppermute(given, 'half', [(0, 1), (1, 0)])]
    pallas_call x5 -> x7, Pallas kernels: 17 us -> 17.8 us  [call(): pl.pallas_call(kernel, out_shape=[x for x, unused in outs], in_specs=[SME...]
  transfers between devices with their start and end apart: 32 -> 26, of which waited for: 9 -> 16; matrix products, arithmetic and copies ran while one was open for 1% -> 1% of each run, Pallas kernels for 0% -> 1%
where the time goes in v7:
time: 109 us
  waiting for transfers between devices  48.8 us (45%)
  starting transfers between devices  30.8 us (28%)
  Pallas kernels  17.8 us (16%)
  blocking collectives  9.93 us (9%)
    ppermute x20, waiting for transfers between devices, deal(): lax.ppermute(value, axes, [(k, k ^ turn) for k in range(count)])  36 us
    ppermute x20, starting transfers between devices, deal(): lax.ppermute(value, axes, [(k, k ^ turn) for k in range(count)])  19.5 us
    pallas_call x7, Pallas kernels, call(): pl.pallas_call(kernel, out_shape=[x for x, unused in outs], in_specs=[SME...  17.8 us
    all_gather x1, blocking collectives, local(): probe_grad = lax.all_gather(probe_band, PLANE, axis=0, tiled=True)  9.93 us
    ppermute x1, waiting for transfers between devices, local(): below = lax.ppermute(lowest, 'pair', [(k, k - 1) for k in range(1, pairs)])  6.12 us
    ppermute x2, waiting for transfers between devices, sum_over(): lax.ppermute(value, axis, [(k, k ^ step) for k in range(size)])  5.69 us
    ppermute x2, starting transfers between devices, sum_over(): lax.ppermute(value, axis, [(k, k ^ step) for k in range(size)])  4.13 us
    ppermute x1, starting transfers between devices, local(): lax.ppermute(lower_sums, 'pair', [(k, k + 1) for k in range(pairs - 1)])  3.75 us
  transfers between devices with their start and end apart: 26, of which 16 were waited for; matrix products, arithmetic and copies ran while one was open for 1% of the time, Pallas kernels for 1%

profile of v7, /device:TPU:0, one launch (start us, length us, event | category | flops | bytes accessed | tf_op | source)
XLA Modules:
  0.0 108.6 jit_solution(8760102890993355602)
XLA Ops:
  0.6 0.5 collective-permute-start
  1.2 1.0 collective-permute-done.sibling
  2.2 2.0 %shard_map.77 = (f32[264,128]{1,0:T(8,128)S(1)}, f32[264,128]{1,0:T(8,128)S(1)}, f32[264,128]{1,0:T(8,128)S(1)}, f32[264,128]{1,0:T(8,128)S(1)}, f32[256,256]{1,0:T(8,128)S(1)}) custom-call(s32[3]{0:T(128)S(1)} %pad_add_fusion.where, s32[1,2,2]{2,1,0:T(2,128)} %offsets.1, s32[1,2,2]{2,1,0:T(2,128)S(1)} %collective-permute-done.sibling, ...), custom_call_target="tpu_custom_call" | custom-call | bytes 1851392 | tf_op jit(solution)/shard_map/pallas_call | solution.py:272
  4.2 2.9 %collective-permute-start.1 = (f32[264,128]{1,0:T(8,128)S(1)}, f32[264,128]{1,0:T(8,128)S(1)}, u32[]{:S(2)}, u32[]{:S(2)}) collective-permute-start(f32[264,128]{1,0:T(8,128)S(1)} %get-tuple-element.37), channel_id=1, source_target_pairs={{0,2},{2,0},{4,6},{6,4},{1,3},{3,1},{5,7},{7,5},{8,10},{10,8},{12,... | collective-permute-start | bytes 405512 | tf_op jit(solution)/shard_map/ppermute | solution.py:301
  7.0 1.5 %collective-permute-start.2 = (f32[264,128]{1,0:T(8,128)S(1)}, f32[264,128]{1,0:T(8,128)S(1)}, u32[]{:S(2)}, u32[]{:S(2)}) collective-permute-start(f32[264,128]{1,0:T(8,128)S(1)} %get-tuple-element.38), channel_id=1, source_target_pairs={{0,4},{2,6},{4,0},{6,2},{1,5},{3,7},{5,1},{7,3},{8,12},{10,14},{12... | collective-permute-start | bytes 405512 | tf_op jit(solution)/shard_map/ppermute | solution.py:301
  8.6 2.6 %collective-permute-done.1.refs_1_ = f32[264,128]{1,0:T(8,128)S(1)} collective-permute-done((f32[264,128]{1,0:T(8,128)S(1)}, f32[264,128]{1,0:T(8,128)S(1)}, u32[]{:S(2)}, u32[]{:S(2)}) %collective-permute-start.1) | collective-permute-done | bytes 135200 | tf_op jit(solution)/shard_map/ppermute | solution.py:301
  11.1 4.2 %collective-permute-done.2.refs_2_ = f32[264,128]{1,0:T(8,128)S(1)} collective-permute-done((f32[264,128]{1,0:T(8,128)S(1)}, f32[264,128]{1,0:T(8,128)S(1)}, u32[]{:S(2)}, u32[]{:S(2)}) %collective-permute-start.2) | collective-permute-done | bytes 135200 | tf_op jit(solution)/shard_map/ppermute | solution.py:301
  15.3 0.6 shard_map.78
  15.9 1.3 %collective-permute-start.4 = (f32[2,256,128]{2,1,0:T(8,128)S(1)}, f32[2,256,128]{2,1,0:T(8,128)S(1)}, u32[]{:S(2)}, u32[]{:S(2)}) collective-permute-start(f32[2,256,128]{2,1,0:T(8,128)S(1)} %shard_map.78), channel_id=1, source_target_pairs={{8,0},{16,8},{24,16},{9,1},{17,9},{25,17},{10,2},{18,10},{26,18},{... | collective-permute-start | bytes 786440 | tf_op jit(solution)/shard_map/ppermute | solution.py:338
  17.2 1.6 %collective-permute-start.5 = (f32[256,256]{1,0:T(8,128)S(1)}, f32[256,256]{1,0:T(8,128)S(1)}, u32[]{:S(2)}, u32[]{:S(2)}) collective-permute-start(f32[256,256]{1,0:T(8,128)S(1)} %get-tuple-element.42), channel_id=1, source_target_pairs={{0,4},{4,0},{1,5},{5,1},{2,6},{6,2},{3,7},{7,3},{8,12},{12,8},{9,1... | collective-permute-start | bytes 786440 | tf_op jit(solution)/shard_map/ppermute | solution.py:339
  18.9 6.1 %collective-permute-done.4.refs_4_ = f32[2,256,128]{2,1,0:T(8,128)S(1)} collective-permute-done((f32[2,256,128]{2,1,0:T(8,128)S(1)}, f32[2,256,128]{2,1,0:T(8,128)S(1)}, u32[]{:S(2)}, u32[]{:S(2)}) %collective-permute-start.4) | collective-permute-done | bytes 262176 | tf_op jit(solution)/shard_map/ppermute | solution.py:338
  25.0 1.4 %shard_map.79 = (f32[256,128]{1,0:T(8,128)S(1)}, f32[256,128]{1,0:T(8,128)S(1)}, f32[256,128]{1,0:T(8,128)S(1)}, f32[256,128]{1,0:T(8,128)S(1)}, f32[256,128]{1,...) custom-call(s32[3]{0:T(128)S(1)} %pad_add_fusion.where, ...), custom_call_target="tpu_custom_call" | custom-call | flops 2097152 | bytes 1851392 | tf_op jit(solution)/shard_map/pallas_call | solution.py:272
  26.5 1.6 %collective-permute-start.7 = (f32[256,128]{1,0:T(8,128)S(1)}, f32[256,128]{1,0:T(8,128)S(1)}, u32[]{:S(2)}, u32[]{:S(2)}) collective-permute-start(f32[256,128]{1,0:T(8,128)S(1)} %get-tuple-element.45), channel_id=1, source_target_pairs={{0,2},{1,3},{2,0},{3,1},{4,6},{5,7},{6,4},{7,5},{8,10},{9,11},{10,... | collective-permute-start | bytes 393224 | tf_op jit(solution)/shard_map/ppermute | solution.py:301
  28.2 0.1 slice_reduce_fusion.2
  28.3 0.1 slice_reduce_fusion.1
  28.4 1.5 %collective-permute-start.8 = (f32[256,128]{1,0:T(8,128)S(1)}, f32[256,128]{1,0:T(8,128)S(1)}, u32[]{:S(2)}, u32[]{:S(2)}) collective-permute-start(f32[256,128]{1,0:T(8,128)S(1)} %get-tuple-element.46), channel_id=1, source_target_pairs={{0,6},{1,7},{2,4},{3,5},{4,2},{5,3},{6,0},{7,1},{8,14},{9,15},{10,... | collective-permute-start | bytes 393224 | tf_op jit(solution)/shard_map/ppermute | solution.py:301
  29.9 1.0 collective-permute-start.9
  30.9 0.6 collective-permute-start.10
  31.4 1.4 %collective-permute-start.11 = (f32[256,128]{1,0:T(8,128)S(1)}, f32[256,128]{1,0:T(8,128)S(1)}, u32[]{:S(2)}, u32[]{:S(2)}) collective-permute-start(f32[256,128]{1,0:T(8,128)S(1)} %get-tuple-element.49), channel_id=1, source_target_pairs={{0,3},{1,2},{2,1},{3,0},{4,7},{5,6},{6,5},{7,4},{8,11},{9,10},{10,... | collective-permute-start | bytes 393224 | tf_op jit(solution)/shard_map/ppermute | solution.py:301
  32.9 0.4 collective-permute-start.12
  33.4 3.4 %collective-permute-done.8.refs_2_ = f32[256,128]{1,0:T(8,128)S(1)} collective-permute-done((f32[256,128]{1,0:T(8,128)S(1)}, f32[256,128]{1,0:T(8,128)S(1)}, u32[]{:S(2)}, u32[]{:S(2)}) %collective-permute-start.8) | collective-permute-done | bytes 131104 | tf_op jit(solution)/shard_map/ppermute | solution.py:301
  36.8 1.9 %collective-permute-done.9.refs_3_ = f32[256,128]{1,0:T(8,128)S(1)} collective-permute-done((f32[256,128]{1,0:T(8,128)S(1)}, f32[256,128]{1,0:T(8,128)S(1)}, u32[]{:S(2)}, u32[]{:S(2)}) %collective-permute-start.9) | collective-permute-done | bytes 131104 | tf_op jit(solution)/shard_map/ppermute | solution.py:301
  38.7 3.2 %collective-permute-done.10.refs_4_ = f32[256,128]{1,0:T(8,128)S(1)} collective-permute-done((f32[256,128]{1,0:T(8,128)S(1)}, f32[256,128]{1,0:T(8,128)S(1)}, u32[]{:S(2)}, u32[]{:S(2)}) %collective-permute-start.10) | collective-permute-done | bytes 131104 | tf_op jit(solution)/shard_map/ppermute | solution.py:301
  41.9 2.7 %collective-permute-done.12.refs_6_ = f32[256,128]{1,0:T(8,128)S(1)} collective-permute-done((f32[256,128]{1,0:T(8,128)S(1)}, f32[256,128]{1,0:T(8,128)S(1)}, u32[]{:S(2)}, u32[]{:S(2)}) %collective-permute-start.12) | collective-permute-done | bytes 131104 | tf_op jit(solution)/shard_map/ppermute | solution.py:301
  44.6 9.8 %shard_map.80 = (f32[384,128]{1,0:T(8,128)S(1)}, f32[384,128]{1,0:T(8,128)S(1)}, f32[384,128]{1,0:T(8,128)S(1)}, f32[384,128]{1,0:T(8,128)S(1)}, f32[384,128]{1,...) custom-call(s32[3]{0:T(128)S(1)} %pad_add_fusion.where, ...), custom_call_target="tpu_custom_call" | custom-call | flops 3221225472 | bytes 6553600 | tf_op jit(solution)/shard_map/pallas_call | solution.py:272
  54.4 0.2 collective-permute-start.13
  54.6 0.6 collective-permute-start.14
  55.2 1.3 %collective-permute-start.15 = (f32[384,128]{1,0:T(8,128)S(1)}, f32[384,128]{1,0:T(8,128)S(1)}, u32[]{:S(2)}, u32[]{:S(2)}) collective-permute-start(f32[384,128]{1,0:T(8,128)S(1)} %get-tuple-element.55), channel_id=1, source_target_pairs={{0,6},{1,7},{2,4},{3,5},{4,2},{5,3},{6,0},{7,1},{8,14},{9,15},{10,... | collective-permute-start | bytes 589832 | tf_op jit(solution)/shard_map/ppermute | solution.py:301
  56.5 1.0 collective-permute-start.16
  57.5 1.5 %collective-permute-start.17 = (f32[384,128]{1,0:T(8,128)S(1)}, f32[384,128]{1,0:T(8,128)S(1)}, u32[]{:S(2)}, u32[]{:S(2)}) collective-permute-start(f32[384,128]{1,0:T(8,128)S(1)} %get-tuple-element.57), channel_id=1, source_target_pairs={{0,4},{1,5},{2,6},{3,7},{4,0},{5,1},{6,2},{7,3},{8,12},{9,13},{10,... | collective-permute-start | bytes 589832 | tf_op jit(solution)/shard_map/ppermute | solution.py:301
  59.0 0.4 collective-permute-start.18
  59.4 2.8 %collective-permute-done.14.refs_1_ = f32[384,128]{1,0:T(8,128)S(1)} collective-permute-done((f32[384,128]{1,0:T(8,128)S(1)}, f32[384,128]{1,0:T(8,128)S(1)}, u32[]{:S(2)}, u32[]{:S(2)}) %collective-permute-start.14) | collective-permute-done | bytes 196640 | tf_op jit(solution)/shard_map/ppermute | solution.py:301
  62.3 4.2 %collective-permute-done.15.refs_2_ = f32[384,128]{1,0:T(8,128)S(1)} collective-permute-done((f32[384,128]{1,0:T(8,128)S(1)}, f32[384,128]{1,0:T(8,128)S(1)}, u32[]{:S(2)}, u32[]{:S(2)}) %collective-permute-start.15) | collective-permute-done | bytes 196640 | tf_op jit(solution)/shard_map/ppermute | solution.py:301
  66.5 3.3 %collective-permute-done.16.refs_3_ = f32[384,128]{1,0:T(8,128)S(1)} collective-permute-done((f32[384,128]{1,0:T(8,128)S(1)}, f32[384,128]{1,0:T(8,128)S(1)}, u32[]{:S(2)}, u32[]{:S(2)}) %collective-permute-start.16) | collective-permute-done | bytes 196640 | tf_op jit(solution)/shard_map/ppermute | solution.py:301
  69.8 3.9 %collective-permute-done.17.refs_4_ = f32[384,128]{1,0:T(8,128)S(1)} collective-permute-done((f32[384,128]{1,0:T(8,128)S(1)}, f32[384,128]{1,0:T(8,128)S(1)}, u32[]{:S(2)}, u32[]{:S(2)}) %collective-permute-start.17) | collective-permute-done | bytes 196640 | tf_op jit(solution)/shard_map/ppermute | solution.py:301
  73.7 0.3 collective-permute-done.18.refs_5_
  74.0 3.4 %collective-permute-done.19.refs_6_ = f32[384,128]{1,0:T(8,128)S(1)} collective-permute-done((f32[384,128]{1,0:T(8,128)S(1)}, f32[384,128]{1,0:T(8,128)S(1)}, u32[]{:S(2)}, u32[]{:S(2)}) %collective-permute-start.19) | collective-permute-done | bytes 196640 | tf_op jit(solution)/shard_map/ppermute | solution.py:301
  77.4 1.9 %shard_map.81 = (f32[4,256,128]{2,1,0:T(8,128)S(1)}, f32[2,256,128]{2,1,0:T(8,128)S(1)}, f32[64,256]{1,0:T(8,128)S(1)}) custom-call(s32[3]{0:T(128)S(1)} %pad_add_fusion.where, s32[1,2]{1,0:T(1,128)} %slot_range.5, s32[4,8]{1,0:T(4,128)S(1)} %maximum_convert_fusion.offs, f32[384,128]{1,0:T(8,128)S(1)} %collective-permute-done.13.refs_0_, ...), custom_call_target="tpu_custom_call" | custom-call | flops 6291456 | bytes 2424832 | tf_op jit(solution)/shard_map/pallas_call | solution.py:272
  79.3 3.7 %collective-permute-start.20 = (f32[2,256,128]{2,1,0:T(8,128)S(1)}, f32[2,256,128]{2,1,0:T(8,128)S(1)}, u32[]{:S(2)}, u32[]{:S(2)}) collective-permute-start(f32[2,256,128]{2,1,0:T(8,128)S(1)} %get-tuple-element.62), channel_id=1, source_target_pairs={{0,8},{8,16},{16,24},{1,9},{9,17},{17,25},{2,10},{10,18},{18,26},{... | collective-permute-start | bytes 786440 | tf_op jit(solution)/shard_map/ppermute | solution.py:369
  83.1 1.5 %collective-permute-start.24 = (f32[64,256]{1,0:T(8,128)S(1)}, f32[64,256]{1,0:T(8,128)S(1)}, u32[]{:S(2)}, u32[]{:S(2)}) collective-permute-start(f32[64,256]{1,0:T(8,128)S(1)} %get-tuple-element.67), channel_id=1, source_target_pairs={{0,8},{8,0},{16,24},{24,16},{1,9},{9,1},{17,25},{25,17},{2,10},{10... | collective-permute-start | bytes 196616 | tf_op jit(solution)/shard_map/ppermute | solution.py:311
  84.6 5.7 %collective-permute-done.24 = f32[64,256]{1,0:T(8,128)S(1)} collective-permute-done((f32[64,256]{1,0:T(8,128)S(1)}, f32[64,256]{1,0:T(8,128)S(1)}, u32[]{:S(2)}, u32[]{:S(2)}) %collective-permute-start.24) | collective-permute-done | bytes 65568 | tf_op jit(solution)/shard_map/ppermute | solution.py:311
  90.3 2.6 %collective-permute-start.25 = (f32[64,256]{1,0:T(8,128)S(1)}, f32[64,256]{1,0:T(8,128)S(1)}, u32[]{:S(2)}, u32[]{:S(2)}) collective-permute-start(f32[64,256]{1,0:T(8,128)S(1)} %add.6), channel_id=1, source_target_pairs={{0,16},{8,24},{16,0},{24,8},{1,17},{9,25},{17,1},{25,9},{2,18},{10... | collective-permute-start | bytes 196616 | tf_op jit(solution)/shard_map/ppermute | solution.py:311
  92.9 0.6 shard_map.82
  93.5 1.4 %collective-permute-start.21 = (f32[256,128]{1,0:T(8,128)S(1)}, f32[256,128]{1,0:T(8,128)S(1)}, u32[]{:S(2)}, u32[]{:S(2)}) collective-permute-start(f32[256,128]{1,0:T(8,128)S(1)} %get-tuple-element.63), channel_id=1, source_target_pairs={{0,6},{2,4},{4,2},{6,0},{1,7},{3,5},{5,3},{7,1},{8,14},{10,12},{12... | collective-permute-start | bytes 393224 | tf_op jit(solution)/shard_map/ppermute | solution.py:301
  94.9 1.6 %collective-permute-start.22 = (f32[256,128]{1,0:T(8,128)S(1)}, f32[256,128]{1,0:T(8,128)S(1)}, u32[]{:S(2)}, u32[]{:S(2)}) collective-permute-start(f32[256,128]{1,0:T(8,128)S(1)} %get-tuple-element.64), channel_id=1, source_target_pairs={{0,2},{2,0},{4,6},{6,4},{1,3},{3,1},{5,7},{7,5},{8,10},{10,8},{12,... | collective-permute-start | bytes 393224 | tf_op jit(solution)/shard_map/ppermute | solution.py:301
  96.5 0.6 collective-permute-start.23
  97.1 9.9 %all_gather.3.refs_4_ = f32[512,256]{1,0:T(8,128)S(1)} all-gather(f32[64,256]{1,0:T(8,128)S(1)} %add.7), channel_id=1, replica_groups=mesh['pair'=4,'half'=2,'col'=2,'core'=2] {'half','col','core'}, dimensions={0}, use_global_device_ids=true | all-gather | bytes 589824 | tf_op jit(solution)/shard_map/all_gather | solution.py:373
  107.0 1.5 %shard_map.83 = (f32[4,256,128]{2,1,0:T(8,128)}, f32[512,256]{1,0:T(8,128)}) custom-call(s32[3]{0:T(128)S(1)} %pad_add_fusion.where, f32[256,128]{1,0:T(8,128)S(1)} %collective-permute-done.21.refs_0_, f32[256,128]{1,0:T(8,128)S(1)} %collective-permute-done.22.refs_1_, f32[256,128]{1,0:T(8,128)S(1)} %collective-permute-done.23.refs_2_, ...), custom_call_target="tpu_custom_call" | custom-call | bytes 2097152 | tf_op jit(solution)/shard_map/pallas_call | solution.py:272
  (20 shorter events, 0.5 us)
Async XLA Ops:
  0.6 1.5 %collective-permute-start = (s32[1,2,2]{2,1,0:T(2,128)}, s32[1,2,2]{2,1,0:T(2,128)S(1)}, u32[]{:S(2)}, u32[]{:S(2)}) collective-permute-start(s32[1,2,2]{2,1,0:T(2,128)} %offsets.1), channel_id=1, source_target_pairs={{0,1},{1,0},{2,3},{3,2},{4,5},{5,4},{6,7},{7,6},{8,9},{9,8},{10,11... | collective-permute-start | bytes 56 | tf_op jit(solution)/shard_map/ppermute | solution.py:324
  4.2 7.0 %collective-permute-start.1 = (f32[264,128]{1,0:T(8,128)S(1)}, f32[264,128]{1,0:T(8,128)S(1)}, u32[]{:S(2)}, u32[]{:S(2)}) collective-permute-start(f32[264,128]{1,0:T(8,128)S(1)} %get-tuple-element.37), channel_id=1, source_target_pairs={{0,2},{2,0},{4,6},{6,4},{1,3},{3,1},{5,7},{7,5},{8,10},{10,8},{12,... | collective-permute-start | bytes 405512 | tf_op jit(solution)/shard_map/ppermute | solution.py:301
  7.0 8.3 %collective-permute-start.2 = (f32[264,128]{1,0:T(8,128)S(1)}, f32[264,128]{1,0:T(8,128)S(1)}, u32[]{:S(2)}, u32[]{:S(2)}) collective-permute-start(f32[264,128]{1,0:T(8,128)S(1)} %get-tuple-element.38), channel_id=1, source_target_pairs={{0,4},{2,6},{4,0},{6,2},{1,5},{3,7},{5,1},{7,3},{8,12},{10,14},{12... | collective-permute-start | bytes 405512 | tf_op jit(solution)/shard_map/ppermute | solution.py:301
  8.5 6.8 %collective-permute-start.3 = (f32[264,128]{1,0:T(8,128)S(1)}, f32[264,128]{1,0:T(8,128)S(1)}, u32[]{:S(2)}, u32[]{:S(2)}) collective-permute-start(f32[264,128]{1,0:T(8,128)S(1)} %get-tuple-element.39), channel_id=1, source_target_pairs={{0,6},{2,4},{4,2},{6,0},{1,7},{3,5},{5,3},{7,1},{8,14},{10,12},{12... | collective-permute-start | bytes 405512 | tf_op jit(solution)/shard_map/ppermute | solution.py:301
  15.9 9.1 %collective-permute-start.4 = (f32[2,256,128]{2,1,0:T(8,128)S(1)}, f32[2,256,128]{2,1,0:T(8,128)S(1)}, u32[]{:S(2)}, u32[]{:S(2)}) collective-permute-start(f32[2,256,128]{2,1,0:T(8,128)S(1)} %shard_map.78), channel_id=1, source_target_pairs={{8,0},{16,8},{24,16},{9,1},{17,9},{25,17},{10,2},{18,10},{26,18},{... | collective-permute-start | bytes 786440 | tf_op jit(solution)/shard_map/ppermute | solution.py:338
  17.2 7.8 %collective-permute-start.5 = (f32[256,256]{1,0:T(8,128)S(1)}, f32[256,256]{1,0:T(8,128)S(1)}, u32[]{:S(2)}, u32[]{:S(2)}) collective-permute-start(f32[256,256]{1,0:T(8,128)S(1)} %get-tuple-element.42), channel_id=1, source_target_pairs={{0,4},{4,0},{1,5},{5,1},{2,6},{6,2},{3,7},{7,3},{8,12},{12,8},{9,1... | collective-permute-start | bytes 786440 | tf_op jit(solution)/shard_map/ppermute | solution.py:339
  26.5 5.0 %collective-permute-start.6 = (f32[256,128]{1,0:T(8,128)S(1)}, f32[256,128]{1,0:T(8,128)S(1)}, u32[]{:S(2)}, u32[]{:S(2)}) collective-permute-start(f32[256,128]{1,0:T(8,128)S(1)} %get-tuple-element.44), channel_id=1, source_target_pairs={{0,1},{1,0},{2,3},{3,2},{4,5},{5,4},{6,7},{7,6},{8,9},{9,8},{10,11... | collective-permute-start | bytes 393224 | tf_op jit(solution)/shard_map/ppermute | solution.py:301
  26.5 6.4 %collective-permute-start.7 = (f32[256,128]{1,0:T(8,128)S(1)}, f32[256,128]{1,0:T(8,128)S(1)}, u32[]{:S(2)}, u32[]{:S(2)}) collective-permute-start(f32[256,128]{1,0:T(8,128)S(1)} %get-tuple-element.45), channel_id=1, source_target_pairs={{0,2},{1,3},{2,0},{3,1},{4,6},{5,7},{6,4},{7,5},{8,10},{9,11},{10,... | collective-permute-start | bytes 393224 | tf_op jit(solution)/shard_map/ppermute | solution.py:301
  28.4 8.4 %collective-permute-start.8 = (f32[256,128]{1,0:T(8,128)S(1)}, f32[256,128]{1,0:T(8,128)S(1)}, u32[]{:S(2)}, u32[]{:S(2)}) collective-permute-start(f32[256,128]{1,0:T(8,128)S(1)} %get-tuple-element.46), channel_id=1, source_target_pairs={{0,6},{1,7},{2,4},{3,5},{4,2},{5,3},{6,0},{7,1},{8,14},{9,15},{10,... | collective-permute-start | bytes 393224 | tf_op jit(solution)/shard_map/ppermute | solution.py:301
  29.9 8.8 %collective-permute-start.9 = (f32[256,128]{1,0:T(8,128)S(1)}, f32[256,128]{1,0:T(8,128)S(1)}, u32[]{:S(2)}, u32[]{:S(2)}) collective-permute-start(f32[256,128]{1,0:T(8,128)S(1)} %get-tuple-element.47), channel_id=1, source_target_pairs={{0,7},{1,6},{2,5},{3,4},{4,3},{5,2},{6,1},{7,0},{8,15},{9,14},{10,... | collective-permute-start | bytes 393224 | tf_op jit(solution)/shard_map/ppermute | solution.py:301
  30.9 11.0 %collective-permute-start.10 = (f32[256,128]{1,0:T(8,128)S(1)}, f32[256,128]{1,0:T(8,128)S(1)}, u32[]{:S(2)}, u32[]{:S(2)}) collective-permute-start(f32[256,128]{1,0:T(8,128)S(1)} %get-tuple-element.48), channel_id=1, source_target_pairs={{0,4},{1,5},{2,6},{3,7},{4,0},{5,1},{6,2},{7,3},{8,12},{9,13},{10,... | collective-permute-start | bytes 393224 | tf_op jit(solution)/shard_map/ppermute | solution.py:301
  31.4 10.4 %collective-permute-start.11 = (f32[256,128]{1,0:T(8,128)S(1)}, f32[256,128]{1,0:T(8,128)S(1)}, u32[]{:S(2)}, u32[]{:S(2)}) collective-permute-start(f32[256,128]{1,0:T(8,128)S(1)} %get-tuple-element.49), channel_id=1, source_target_pairs={{0,3},{1,2},{2,1},{3,0},{4,7},{5,6},{6,5},{7,4},{8,11},{9,10},{10,... | collective-permute-start | bytes 393224 | tf_op jit(solution)/shard_map/ppermute | solution.py:301
  32.9 11.7 %collective-permute-start.12 = (f32[256,128]{1,0:T(8,128)S(1)}, f32[256,128]{1,0:T(8,128)S(1)}, u32[]{:S(2)}, u32[]{:S(2)}) collective-permute-start(f32[256,128]{1,0:T(8,128)S(1)} %get-tuple-element.50), channel_id=1, source_target_pairs={{0,5},{1,4},{2,7},{3,6},{4,1},{5,0},{6,3},{7,2},{8,13},{9,12},{10,... | collective-permute-start | bytes 393224 | tf_op jit(solution)/shard_map/ppermute | solution.py:301
  54.4 4.6 %collective-permute-start.13 = (f32[384,128]{1,0:T(8,128)S(1)}, f32[384,128]{1,0:T(8,128)S(1)}, u32[]{:S(2)}, u32[]{:S(2)}) collective-permute-start(f32[384,128]{1,0:T(8,128)S(1)} %get-tuple-element.53), channel_id=1, source_target_pairs={{0,1},{1,0},{2,3},{3,2},{4,5},{5,4},{6,7},{7,6},{8,9},{9,8},{10,11... | collective-permute-start | bytes 589832 | tf_op jit(solution)/shard_map/ppermute | solution.py:301
  54.6 7.7 %collective-permute-start.14 = (f32[384,128]{1,0:T(8,128)S(1)}, f32[384,128]{1,0:T(8,128)S(1)}, u32[]{:S(2)}, u32[]{:S(2)}) collective-permute-start(f32[384,128]{1,0:T(8,128)S(1)} %get-tuple-element.54), channel_id=1, source_target_pairs={{0,2},{1,3},{2,0},{3,1},{4,6},{5,7},{6,4},{7,5},{8,10},{9,11},{10,... | collective-permute-start | bytes 589832 | tf_op jit(solution)/shard_map/ppermute | solution.py:301
  55.2 11.3 %collective-permute-start.15 = (f32[384,128]{1,0:T(8,128)S(1)}, f32[384,128]{1,0:T(8,128)S(1)}, u32[]{:S(2)}, u32[]{:S(2)}) collective-permute-start(f32[384,128]{1,0:T(8,128)S(1)} %get-tuple-element.55), channel_id=1, source_target_pairs={{0,6},{1,7},{2,4},{3,5},{4,2},{5,3},{6,0},{7,1},{8,14},{9,15},{10,... | collective-permute-start | bytes 589832 | tf_op jit(solution)/shard_map/ppermute | solution.py:301
  56.5 13.3 %collective-permute-start.16 = (f32[384,128]{1,0:T(8,128)S(1)}, f32[384,128]{1,0:T(8,128)S(1)}, u32[]{:S(2)}, u32[]{:S(2)}) collective-permute-start(f32[384,128]{1,0:T(8,128)S(1)} %get-tuple-element.56), channel_id=1, source_target_pairs={{0,7},{1,6},{2,5},{3,4},{4,3},{5,2},{6,1},{7,0},{8,15},{9,14},{10,... | collective-permute-start | bytes 589832 | tf_op jit(solution)/shard_map/ppermute | solution.py:301
  57.5 16.2 %collective-permute-start.17 = (f32[384,128]{1,0:T(8,128)S(1)}, f32[384,128]{1,0:T(8,128)S(1)}, u32[]{:S(2)}, u32[]{:S(2)}) collective-permute-start(f32[384,128]{1,0:T(8,128)S(1)} %get-tuple-element.57), channel_id=1, source_target_pairs={{0,4},{1,5},{2,6},{3,7},{4,0},{5,1},{6,2},{7,3},{8,12},{9,13},{10,... | collective-permute-start | bytes 589832 | tf_op jit(solution)/shard_map/ppermute | solution.py:301
  59.0 15.0 %collective-permute-start.18 = (f32[384,128]{1,0:T(8,128)S(1)}, f32[384,128]{1,0:T(8,128)S(1)}, u32[]{:S(2)}, u32[]{:S(2)}) collective-permute-start(f32[384,128]{1,0:T(8,128)S(1)} %get-tuple-element.58), channel_id=1, source_target_pairs={{0,3},{1,2},{2,1},{3,0},{4,7},{5,6},{6,5},{7,4},{8,11},{9,10},{10,... | collective-permute-start | bytes 589832 | tf_op jit(solution)/shard_map/ppermute | solution.py:301
  62.3 15.1 %collective-permute-start.19 = (f32[384,128]{1,0:T(8,128)S(1)}, f32[384,128]{1,0:T(8,128)S(1)}, u32[]{:S(2)}, u32[]{:S(2)}) collective-permute-start(f32[384,128]{1,0:T(8,128)S(1)} %get-tuple-element.59), channel_id=1, source_target_pairs={{0,5},{1,4},{2,7},{3,6},{4,1},{5,0},{6,3},{7,2},{8,13},{9,12},{10,... | collective-permute-start | bytes 589832 | tf_op jit(solution)/shard_map/ppermute | solution.py:301
  79.3 13.6 %collective-permute-start.20 = (f32[2,256,128]{2,1,0:T(8,128)S(1)}, f32[2,256,128]{2,1,0:T(8,128)S(1)}, u32[]{:S(2)}, u32[]{:S(2)}) collective-permute-start(f32[2,256,128]{2,1,0:T(8,128)S(1)} %get-tuple-element.62), channel_id=1, source_target_pairs={{0,8},{8,16},{16,24},{1,9},{9,17},{17,25},{2,10},{10,18},{18,26},{... | collective-permute-start | bytes 786440 | tf_op jit(solution)/shard_map/ppermute | solution.py:369
  83.1 7.2 %collective-permute-start.24 = (f32[64,256]{1,0:T(8,128)S(1)}, f32[64,256]{1,0:T(8,128)S(1)}, u32[]{:S(2)}, u32[]{:S(2)}) collective-permute-start(f32[64,256]{1,0:T(8,128)S(1)} %get-tuple-element.67), channel_id=1, source_target_pairs={{0,8},{8,0},{16,24},{24,16},{1,9},{9,1},{17,25},{25,17},{2,10},{10... | collective-permute-start | bytes 196616 | tf_op jit(solution)/shard_map/ppermute | solution.py:311
  90.3 6.8 %collective-permute-start.25 = (f32[64,256]{1,0:T(8,128)S(1)}, f32[64,256]{1,0:T(8,128)S(1)}, u32[]{:S(2)}, u32[]{:S(2)}) collective-permute-start(f32[64,256]{1,0:T(8,128)S(1)} %add.6), channel_id=1, source_target_pairs={{0,16},{8,24},{16,0},{24,8},{1,17},{9,25},{17,1},{25,9},{2,18},{10... | collective-permute-start | bytes 196616 | tf_op jit(solution)/shard_map/ppermute | solution.py:311
  93.5 13.5 %collective-permute-start.21 = (f32[256,128]{1,0:T(8,128)S(1)}, f32[256,128]{1,0:T(8,128)S(1)}, u32[]{:S(2)}, u32[]{:S(2)}) collective-permute-start(f32[256,128]{1,0:T(8,128)S(1)} %get-tuple-element.63), channel_id=1, source_target_pairs={{0,6},{2,4},{4,2},{6,0},{1,7},{3,5},{5,3},{7,1},{8,14},{10,12},{12... | collective-permute-start | bytes 393224 | tf_op jit(solution)/shard_map/ppermute | solution.py:301
  94.9 12.1 %collective-permute-start.22 = (f32[256,128]{1,0:T(8,128)S(1)}, f32[256,128]{1,0:T(8,128)S(1)}, u32[]{:S(2)}, u32[]{:S(2)}) collective-permute-start(f32[256,128]{1,0:T(8,128)S(1)} %get-tuple-element.64), channel_id=1, source_target_pairs={{0,2},{2,0},{4,6},{6,4},{1,3},{3,1},{5,7},{7,5},{8,10},{10,8},{12,... | collective-permute-start | bytes 393224 | tf_op jit(solution)/shard_map/ppermute | solution.py:301
  96.5 10.5 %collective-permute-start.23 = (f32[256,128]{1,0:T(8,128)S(1)}, f32[256,128]{1,0:T(8,128)S(1)}, u32[]{:S(2)}, u32[]{:S(2)}) collective-permute-start(f32[256,128]{1,0:T(8,128)S(1)} %get-tuple-element.65), channel_id=1, source_target_pairs={{0,4},{2,6},{4,0},{6,2},{1,5},{3,7},{5,1},{7,3},{8,12},{10,14},{12... | collective-permute-start | bytes 393224 | tf_op jit(solution)/shard_map/ppermute | solution.py:301

commit v8 on v7

--- a/solution.py
+++ b/solution.py
@@ -12,7 +12,7 @@
 
 GRAD_WEIGHT = 0.0625
 PLANE = ("half", "col", "core")
-EIGHT, FOUR = (1, 2, 6, 7, 4, 3, 5, 0), (3, 1, 2, 0)
+EIGHT, FOUR = (4, 2, 5, 3, 6, 7, 1, 0), (2, 1, 3, 0)
 VMEM_LIMIT = 24 * 1024 * 1024
 
 
@@ -142,24 +142,31 @@
         out[...] = parts[jnp.bitwise_xor(2 * mine + core, turn)]
 
 
+def roll(value, rows, cols):
+    return pltpu.roll(pltpu.roll(value, rows, 0), cols, 1)
+
+
+def ready_kernel(where, slot_range, offs, probe_from, measured, tabs_from, probe, kept, tabs, sems):
+    half, col, core = where[0], where[1], where[2]
+    copies = fetch([(probe_from, probe), (tabs_from, tabs), (measured.at[0, half], kept)], sems)
+    slot = slot_of(half, col, core)
+    unused, row_at, col_at = slot_place(offs, 2 * half + col, slot_range[0, 1 - half], slot)
+    copies[0].wait()
+    for part in range(2):
+        probe[part] = roll(probe[part], row_at, col_at)
+    copies[1].wait()
+    copies[2].wait()
+
+
 def position_kernel(where, slot_range, offs, *refs):
-    gotten, taken, (probe_from, measured, tabs_from), outs = dict(zip(EIGHT, refs)), refs[8], refs[9:12], refs[12:20]
-    patch, grad, probe, kept, tabs, sems = refs[20:]
+    gotten, (probe, kept, taken, tabs) = dict(zip(EIGHT, refs)), refs[8:12]
+    outs, patch, grad = refs[12:20], refs[20], refs[21]
     half, col, core = where[0], where[1], where[2]
     mine = 2 * half + col
     flat = 2 * mine + core
     lower, row_at, col_at = slot_place(offs, mine, slot_range[0, 1 - half], slot_of(half, col, core))
     width = probe.shape[-1]
     lanes, band = width // 2, width // 4
-    probe_copy, near_copy, far_copy, kept_copy = fetch(
-        [
-            (probe_from, probe),
-            (tabs_from.at[pl.ds(2, 2)], tabs.at[pl.ds(2, 2)]),
-            (tabs_from.at[pl.ds(0, 2)], tabs.at[pl.ds(0, 2)]),
-            (measured.at[0, half], kept),
-        ],
-        sems,
-    )
     for turn in range(8):
         patch[jnp.bitwise_xor(flat, turn)] = gotten[turn][...]
 
@@ -170,21 +177,14 @@
         grad[2 * plane, :width] = value[:, :lanes]
         grad[2 * plane + 1, :width] = value[:, lanes:]
 
-    def roll(value, rows, cols):
-        return pltpu.roll(pltpu.roll(value, rows, 0), cols, 1)
-
-    probe_copy.wait()
-    wave_re, wave_im = roll(probe[0], row_at, col_at), roll(probe[1], row_at, col_at)
+    wave_re, wave_im = probe[0], probe[1]
     o0_re, o0_im, o1_re, o1_im = load(0), load(2), load(1), load(3)
     exit_re = wave_re * o0_re - wave_im * o0_im
     exit_im = wave_re * o0_im + wave_im * o0_re
-    near_copy.wait()
     mid_re, mid_im = transform(exit_re, exit_im, tabs, 2, False)
     exit_re = mid_re * o1_re - mid_im * o1_im
     exit_im = mid_re * o1_im + mid_im * o1_re
-    far_copy.wait()
     far_re, far_im = transform(exit_re, exit_im, tabs, 0, False)
-    kept_copy.wait()
     target = jnp.where(lower == half, kept[...], taken[...])
     excess = 2.0 * GRAD_WEIGHT * (far_re * far_re + far_im * far_im - target)
     back_re, back_im = transform(excess * far_re, excess * far_im, tabs, 0, True)
@@ -193,7 +193,7 @@
     up_re = o1_re * back_re + o1_im * back_im
     up_im = o1_re * back_im - o1_im * back_re
     back_re, back_im = transform(up_re, up_im, tabs, 2, True)
-    wave_re, wave_im = roll(probe[0], row_at, col_at), roll(probe[1], row_at, col_at)
+    wave_re, wave_im = probe[0], probe[1]
     o0_re, o0_im = load(0), load(2)
     store(0, wave_re * back_re + wave_im * back_im)
     store(2, wave_re * back_im - wave_im * back_re)
@@ -210,38 +210,43 @@
         out[...] = grad[jnp.bitwise_xor(flat, turn)]
 
 
-def add_kernel(where, slot_range, offs, *refs):
-    parts, (own, below, probe_band) = refs[:8], refs[8:]
-    rows, cols = own.shape[1:]
+def add_parts(where, slot_range, offs, parts, strip, rows, cols):
     half, col, core = where[0], where[1], where[2]
     mine = 2 * half + col
-    split_at = slot_range[0, 1 - half]
     row_ids = lax.broadcasted_iota(jnp.int32, (rows, cols), 0)
     col_ids = lax.broadcasted_iota(jnp.int32, (rows, cols), 1) + core * cols
-    places = []
-    for turn in EIGHT:
+    sums = [jnp.zeros((rows, cols), jnp.float32)] * 2
+    for turn, part in zip(EIGHT, parts):
         flat = jnp.bitwise_xor(2 * mine + core, turn)
         slot = slot_of(flat // 4, (flat // 2) % 2, flat % 2)
-        places.append(slot_place(offs, mine, split_at, slot))
-    for strip in range(3):
-        sums = [jnp.zeros((rows, cols), jnp.float32)] * 2
-        for part, (lower, row_at, col_at) in zip(parts, places):
-            first = jnp.where(strip == lower, row_at, jnp.where(strip == lower + 1, 0, rows))
-            last = jnp.where(strip == lower, rows, jnp.where(strip == lower + 1, row_at, 0))
-            value = jnp.where((row_ids >= first) & (row_ids < last), part[:rows], 0.0)
-            left = jnp.where(col_ids >= col_at, value, 0.0)
-            sums = [sums[0] + left, sums[1] + (value - left)]
-        for side in range(2):
-            if strip < 2:
-                own[2 * strip + side] = sums[side]
-            else:
-                below[jnp.bitwise_xor(col, side)] = sums[side]
+        lower, row_at, col_at = slot_place(offs, mine, slot_range[0, 1 - half], slot)
+        first = jnp.where(strip == lower, row_at, jnp.where(strip == lower + 1, 0, rows))
+        last = jnp.where(strip == lower, rows, jnp.where(strip == lower + 1, row_at, 0))
+        value = jnp.where((row_ids >= first) & (row_ids < last), part[:rows], 0.0)
+        left = jnp.where(col_ids >= col_at, value, 0.0)
+        sums = [sums[0] + left, sums[1] + (value - left)]
+    return sums
+
+
+def add_below_kernel(where, slot_range, offs, *refs):
+    parts, (below, probe_band) = refs[:8], refs[8:]
+    rows, cols = below.shape[1:]
+    sums = add_parts(where, slot_range, offs, parts, 2, rows, cols)
+    for side in range(2):
+        below[jnp.bitwise_xor(where[1], side)] = sums[side]
     total = parts[0][rows:]
     for part in parts[1:]:
         total = total + part[rows:]
     band = probe_band.shape[0]
     probe_band[:, :cols] = total[:band]
     probe_band[:, cols:] = total[band:]
+
+
+def add_own_kernel(where, slot_range, offs, *refs):
+    parts, own = refs[:8], refs[8]
+    rows, cols = own.shape[1:]
+    for strip in range(2):
+        own[2 * strip], own[2 * strip + 1] = add_parts(where, slot_range, offs, parts, strip, rows, cols)
 
 
 def top_kernel(where, own, above, *outs):
@@ -350,26 +355,35 @@
     offs = [own[FOUR.index(turn)][rows:, 0] for turn in range(4)]
     scalars = (where, slot_range, jnp.stack(offs).astype(jnp.int32))
     tabs = jnp.asarray(tables(width))
+    probe, kept, tabs = call(
+        ready_kernel,
+        [shape(*probe.shape), shape(width, width), jax.ShapeDtypeStruct(tabs.shape, tabs.dtype)],
+        scalars,
+        ((probe, HBM), (measured, HBM), (tabs, HBM)),
+        probe.size,
+        copies=3,
+    )
     grad = call(
         position_kernel,
         [shape(rows + 2 * band, cols)] * 8,
         scalars,
-        (*deal(parts, PLANE), taken, (probe, HBM), (measured, HBM), (tabs, HBM)),
+        (*deal(parts, PLANE), probe, kept, taken, tabs),
         8 * 24 * width**3,
-        [(8, rows, cols), (8, rows + 2 * band, cols), probe.shape, (width, width), pltpu.VMEM(tabs.shape, tabs.dtype)],
-        copies=4,
-    )
-    sums, lower_sums, probe_band = call(
-        add_kernel,
-        [shape(planes, rows, cols), shape(2, rows, cols), shape(band, width)],
+        [(8, rows, cols), (8, rows + 2 * band, cols)],
+    )
+    got = deal(grad, PLANE)
+    lower_sums, probe_band = call(
+        add_below_kernel,
+        [shape(2, rows, cols), shape(band, width)],
         scalars,
-        deal(grad, PLANE),
-        96 * rows * width,
-    )
+        got,
+        32 * rows * width,
+    )
+    probe_band = sum_over(probe_band, "pair", pairs)
+    (sums,) = call(add_own_kernel, [shape(planes, rows, cols)], scalars, got, 64 * rows * width)
     above = lax.ppermute(lower_sums, "pair", [(k, k + 1) for k in range(pairs - 1)])
     sums = call(top_kernel, [shape(rows, cols)] * 4, (where,), (sums, above), planes * rows * cols)
     sums = deal(sums, PLANE[:2])
-    probe_band = sum_over(probe_band, "pair", pairs)
     probe_grad = lax.all_gather(probe_band, PLANE, axis=0, tiled=True)
     object_grad, probe_grad = call(
         join_kernel,

time: 109 us -> 102 us (0.936)
  waiting for transfers between devices: 48.8 us -> 38.8 us
  Pallas kernels: 17.8 us -> 19.6 us
  starting transfers between devices: 30.8 us -> 32.2 us
    ppermute x20, waiting for transfers between devices: 36 us -> 25.7 us  [deal(): lax.ppermute(value, axes, [(k, k ^ turn) for k in range(count)])]
    pallas_call x7 -> x9, Pallas kernels: 17.8 us -> 19.6 us  [call(): pl.pallas_call(kernel, out_shape=[x for x, unused in outs], in_specs=[SME...]
    ppermute x20, starting transfers between devices: 19.5 us -> 20.8 us  [deal(): lax.ppermute(value, axes, [(k, k ^ turn) for k in range(count)])]
  transfers between devices with their start and end apart: 26 -> 26, of which waited for: 16 -> 14; matrix products, arithmetic and copies ran while one was open for 1% -> 1% of each run, Pallas kernels for 1% -> 5%
where the time goes in v8:
time: 102 us
  waiting for transfers between devices  38.8 us (38%)
  starting transfers between devices  32.2 us (32%)
  Pallas kernels  19.6 us (19%)
  blocking collectives  10.3 us (10%)
    ppermute x20, waiting for transfers between devices, deal(): lax.ppermute(value, axes, [(k, k ^ turn) for k in range(count)])  25.7 us
    ppermute x20, starting transfers between devices, deal(): lax.ppermute(value, axes, [(k, k ^ turn) for k in range(count)])  20.8 us
    pallas_call x9, Pallas kernels, call(): pl.pallas_call(kernel, out_shape=[x for x, unused in outs], in_specs=[SME...  19.6 us
    all_gather x1, blocking collectives, local(): probe_grad = lax.all_gather(probe_band, PLANE, axis=0, tiled=True)  10.3 us
    ppermute x1, waiting for transfers between devices, local(): below = lax.ppermute(lowest, 'pair', [(k, k - 1) for k in range(1, pairs)])  6.12 us
    ppermute x2, waiting for transfers between devices, sum_over(): lax.ppermute(value, axis, [(k, k ^ step) for k in range(size)])  5.98 us
    ppermute x2, starting transfers between devices, sum_over(): lax.ppermute(value, axis, [(k, k ^ step) for k in range(size)])  4.32 us
    ppermute x1, starting transfers between devices, local(): lax.ppermute(lower_sums, 'pair', [(k, k + 1) for k in range(pairs - 1)])  3.75 us
  transfers between devices with their start and end apart: 26, of which 14 were waited for; matrix products, arithmetic and copies ran while one was open for 1% of the time, Pallas kernels for 5%

profile of v8, /device:TPU:0, one launch (start us, length us, event | category | flops | bytes accessed | tf_op | source)
XLA Modules:
  0.0 102.2 jit_solution(14977600644603078605)
XLA Ops:
  0.6 0.5 collective-permute-start
  1.2 1.0 collective-permute-done.sibling
  2.2 2.0 %shard_map.77 = (f32[264,128]{1,0:T(8,128)S(1)}, f32[264,128]{1,0:T(8,128)S(1)}, f32[264,128]{1,0:T(8,128)S(1)}, f32[264,128]{1,0:T(8,128)S(1)}, f32[256,256]{1,0:T(8,128)S(1)}) custom-call(s32[3]{0:T(128)S(1)} %pad_add_fusion.where, s32[1,2,2]{2,1,0:T(2,128)} %offsets.1, s32[1,2,2]{2,1,0:T(2,128)S(1)} %collective-permute-done.sibling, ...), custom_call_target="tpu_custom_call" | custom-call | bytes 1851392 | tf_op jit(solution)/shard_map/pallas_call | solution.py:277
  4.2 2.9 %collective-permute-start.1 = (f32[264,128]{1,0:T(8,128)S(1)}, f32[264,128]{1,0:T(8,128)S(1)}, u32[]{:S(2)}, u32[]{:S(2)}) collective-permute-start(f32[264,128]{1,0:T(8,128)S(1)} %get-tuple-element.39), channel_id=1, source_target_pairs={{0,2},{2,0},{4,6},{6,4},{1,3},{3,1},{5,7},{7,5},{8,10},{10,8},{12,... | collective-permute-start | bytes 405512 | tf_op jit(solution)/shard_map/ppermute | solution.py:306
  7.0 1.5 %collective-permute-start.2 = (f32[264,128]{1,0:T(8,128)S(1)}, f32[264,128]{1,0:T(8,128)S(1)}, u32[]{:S(2)}, u32[]{:S(2)}) collective-permute-start(f32[264,128]{1,0:T(8,128)S(1)} %get-tuple-element.40), channel_id=1, source_target_pairs={{0,4},{2,6},{4,0},{6,2},{1,5},{3,7},{5,1},{7,3},{8,12},{10,14},{12... | collective-permute-start | bytes 405512 | tf_op jit(solution)/shard_map/ppermute | solution.py:306
  8.6 2.6 %collective-permute-done.1.refs_1_ = f32[264,128]{1,0:T(8,128)S(1)} collective-permute-done((f32[264,128]{1,0:T(8,128)S(1)}, f32[264,128]{1,0:T(8,128)S(1)}, u32[]{:S(2)}, u32[]{:S(2)}) %collective-permute-start.1) | collective-permute-done | bytes 135200 | tf_op jit(solution)/shard_map/ppermute | solution.py:306
  11.1 4.2 %collective-permute-done.2.refs_0_ = f32[264,128]{1,0:T(8,128)S(1)} collective-permute-done((f32[264,128]{1,0:T(8,128)S(1)}, f32[264,128]{1,0:T(8,128)S(1)}, u32[]{:S(2)}, u32[]{:S(2)}) %collective-permute-start.2) | collective-permute-done | bytes 135200 | tf_op jit(solution)/shard_map/ppermute | solution.py:306
  15.3 0.6 shard_map.78
  15.9 1.3 %collective-permute-start.4 = (f32[2,256,128]{2,1,0:T(8,128)S(1)}, f32[2,256,128]{2,1,0:T(8,128)S(1)}, u32[]{:S(2)}, u32[]{:S(2)}) collective-permute-start(f32[2,256,128]{2,1,0:T(8,128)S(1)} %shard_map.78), channel_id=1, source_target_pairs={{8,0},{16,8},{24,16},{9,1},{17,9},{25,17},{10,2},{18,10},{26,18},{... | collective-permute-start | bytes 786440 | tf_op jit(solution)/shard_map/ppermute | solution.py:343
  17.2 1.6 %collective-permute-start.5 = (f32[256,256]{1,0:T(8,128)S(1)}, f32[256,256]{1,0:T(8,128)S(1)}, u32[]{:S(2)}, u32[]{:S(2)}) collective-permute-start(f32[256,256]{1,0:T(8,128)S(1)} %get-tuple-element.44), channel_id=1, source_target_pairs={{0,4},{4,0},{1,5},{5,1},{2,6},{6,2},{3,7},{7,3},{8,12},{12,8},{9,1... | collective-permute-start | bytes 786440 | tf_op jit(solution)/shard_map/ppermute | solution.py:344
  18.8 0.1 slice_reduce_fusion.3
  18.9 6.1 %collective-permute-done.4.refs_4_ = f32[2,256,128]{2,1,0:T(8,128)S(1)} collective-permute-done((f32[2,256,128]{2,1,0:T(8,128)S(1)}, f32[2,256,128]{2,1,0:T(8,128)S(1)}, u32[]{:S(2)}, u32[]{:S(2)}) %collective-permute-start.4) | collective-permute-done | bytes 262176 | tf_op jit(solution)/shard_map/ppermute | solution.py:343
  25.0 1.4 %shard_map.79 = (f32[256,128]{1,0:T(8,128)S(1)}, f32[256,128]{1,0:T(8,128)S(1)}, f32[256,128]{1,0:T(8,128)S(1)}, f32[256,128]{1,0:T(8,128)S(1)}, f32[256,128]{1,...) custom-call(s32[3]{0:T(128)S(1)} %pad_add_fusion.where, ...), custom_call_target="tpu_custom_call" | custom-call | flops 2097152 | bytes 1851392 | tf_op jit(solution)/shard_map/pallas_call | solution.py:277
  26.4 1.6 %collective-permute-start.6 = (f32[256,128]{1,0:T(8,128)S(1)}, f32[256,128]{1,0:T(8,128)S(1)}, u32[]{:S(2)}, u32[]{:S(2)}) collective-permute-start(f32[256,128]{1,0:T(8,128)S(1)} %get-tuple-element.46), channel_id=1, source_target_pairs={{0,4},{1,5},{2,6},{3,7},{4,0},{5,1},{6,2},{7,3},{8,12},{9,13},{10,... | collective-permute-start | bytes 393224 | tf_op jit(solution)/shard_map/ppermute | solution.py:306
  28.1 0.6 collective-permute-start.7
  29.0 1.6 %collective-permute-start.9 = (f32[256,128]{1,0:T(8,128)S(1)}, f32[256,128]{1,0:T(8,128)S(1)}, u32[]{:S(2)}, u32[]{:S(2)}) collective-permute-start(f32[256,128]{1,0:T(8,128)S(1)} %get-tuple-element.49), channel_id=1, source_target_pairs={{0,3},{1,2},{2,1},{3,0},{4,7},{5,6},{6,5},{7,4},{8,11},{9,10},{10,... | collective-permute-start | bytes 393224 | tf_op jit(solution)/shard_map/ppermute | solution.py:306
  30.6 1.6 %collective-permute-start.10 = (f32[256,128]{1,0:T(8,128)S(1)}, f32[256,128]{1,0:T(8,128)S(1)}, u32[]{:S(2)}, u32[]{:S(2)}) collective-permute-start(f32[256,128]{1,0:T(8,128)S(1)} %get-tuple-element.50), channel_id=1, source_target_pairs={{0,6},{1,7},{2,4},{3,5},{4,2},{5,3},{6,0},{7,1},{8,14},{9,15},{10,... | collective-permute-start | bytes 393224 | tf_op jit(solution)/shard_map/ppermute | solution.py:306
  32.1 0.7 collective-permute-start.11
  32.8 1.3 %collective-permute-done.7.refs_1_ = f32[256,128]{1,0:T(8,128)S(1)} collective-permute-done((f32[256,128]{1,0:T(8,128)S(1)}, f32[256,128]{1,0:T(8,128)S(1)}, u32[]{:S(2)}, u32[]{:S(2)}) %collective-permute-start.7) | collective-permute-done | bytes 131104 | tf_op jit(solution)/shard_map/ppermute | solution.py:306
  34.3 2.6 %shard_map.80 = (f32[2,256,256]{2,1,0:T(8,128)S(1)}, f32[256,256]{1,0:T(8,128)S(1)}, bf16[4,1280,256]{2,1,0:T(8,128)(2,1)S(1)}) custom-call(s32[3]{0:T(128)S(1)} %pad_add_fusion.where, s32[1,2]{1,0:T(1,128)} %slot_range.9, s32[4,8]{1,0:T(4,128)S(1)} %maximum_convert_fusion.offs, f32[2,256,256]{2,1,0:T(8,128)} %probe_from.1, f32[1,2,256,256]{3,2,1,0:T(8,128)} %measured.3, ...), custom_call_target="tpu_custom_call" | custom-call | flops 131072 | bytes 7077888 | tf_op jit(solution)/shard_map/pallas_call | solution.py:277
  36.9 2.3 %collective-permute-done.10.refs_4_ = f32[256,128]{1,0:T(8,128)S(1)} collective-permute-done((f32[256,128]{1,0:T(8,128)S(1)}, f32[256,128]{1,0:T(8,128)S(1)}, u32[]{:S(2)}, u32[]{:S(2)}) %collective-permute-start.10) | collective-permute-done | bytes 131104 | tf_op jit(solution)/shard_map/ppermute | solution.py:306
  39.3 1.4 %collective-permute-done.11.refs_5_ = f32[256,128]{1,0:T(8,128)S(1)} collective-permute-done((f32[256,128]{1,0:T(8,128)S(1)}, f32[256,128]{1,0:T(8,128)S(1)}, u32[]{:S(2)}, u32[]{:S(2)}) %collective-permute-start.11) | collective-permute-done | bytes 131104 | tf_op jit(solution)/shard_map/ppermute | solution.py:306
  40.7 8.2 %shard_map.81 = (f32[384,128]{1,0:T(8,128)S(1)}, f32[384,128]{1,0:T(8,128)S(1)}, f32[384,128]{1,0:T(8,128)S(1)}, f32[384,128]{1,0:T(8,128)S(1)}, f32[384,128]{1,...) custom-call(s32[3]{0:T(128)S(1)} %pad_add_fusion.where, ...), custom_call_target="tpu_custom_call" | custom-call | flops 3221225472 | bytes 6291456 | tf_op jit(solution)/shard_map/pallas_call | solution.py:277
  48.9 1.2 %collective-permute-start.13 = (f32[384,128]{1,0:T(8,128)S(1)}, f32[384,128]{1,0:T(8,128)S(1)}, u32[]{:S(2)}, u32[]{:S(2)}) collective-permute-start(f32[384,128]{1,0:T(8,128)S(1)} %get-tuple-element.58), channel_id=1, source_target_pairs={{0,4},{1,5},{2,6},{3,7},{4,0},{5,1},{6,2},{7,3},{8,12},{9,13},{10,... | collective-permute-start | bytes 589832 | tf_op jit(solution)/shard_map/ppermute | solution.py:306
  50.1 1.2 %collective-permute-start.14 = (f32[384,128]{1,0:T(8,128)S(1)}, f32[384,128]{1,0:T(8,128)S(1)}, u32[]{:S(2)}, u32[]{:S(2)}) collective-permute-start(f32[384,128]{1,0:T(8,128)S(1)} %get-tuple-element.59), channel_id=1, source_target_pairs={{0,2},{1,3},{2,0},{3,1},{4,6},{5,7},{6,4},{7,5},{8,10},{9,11},{10,... | collective-permute-start | bytes 589832 | tf_op jit(solution)/shard_map/ppermute | solution.py:306
  51.3 0.9 collective-permute-start.15
  52.2 0.6 collective-permute-start.16
  52.7 1.8 %collective-permute-start.17 = (f32[384,128]{1,0:T(8,128)S(1)}, f32[384,128]{1,0:T(8,128)S(1)}, u32[]{:S(2)}, u32[]{:S(2)}) collective-permute-start(f32[384,128]{1,0:T(8,128)S(1)} %get-tuple-element.62), channel_id=1, source_target_pairs={{0,6},{1,7},{2,4},{3,5},{4,2},{5,3},{6,0},{7,1},{8,14},{9,15},{10,... | collective-permute-start | bytes 589832 | tf_op jit(solution)/shard_map/ppermute | solution.py:306
  54.5 2.1 %collective-permute-done.13.refs_0_ = f32[384,128]{1,0:T(8,128)S(1)} collective-permute-done((f32[384,128]{1,0:T(8,128)S(1)}, f32[384,128]{1,0:T(8,128)S(1)}, u32[]{:S(2)}, u32[]{:S(2)}) %collective-permute-start.13) | collective-permute-done | bytes 196640 | tf_op jit(solution)/shard_map/ppermute | solution.py:306
  56.6 0.3 collective-permute-start.18
  57.0 0.9 collective-permute-done.14.refs_1_
  57.9 0.7 collective-permute-start.19
  58.6 1.5 %collective-permute-done.15.refs_2_ = f32[384,128]{1,0:T(8,128)S(1)} collective-permute-done((f32[384,128]{1,0:T(8,128)S(1)}, f32[384,128]{1,0:T(8,128)S(1)}, u32[]{:S(2)}, u32[]{:S(2)}) %collective-permute-start.15) | collective-permute-done | bytes 196640 | tf_op jit(solution)/shard_map/ppermute | solution.py:306
  60.1 1.3 %collective-permute-done.16.refs_3_ = f32[384,128]{1,0:T(8,128)S(1)} collective-permute-done((f32[384,128]{1,0:T(8,128)S(1)}, f32[384,128]{1,0:T(8,128)S(1)}, u32[]{:S(2)}, u32[]{:S(2)}) %collective-permute-start.16) | collective-permute-done | bytes 196640 | tf_op jit(solution)/shard_map/ppermute | solution.py:306
  61.4 5.1 %collective-permute-done.17.refs_4_ = f32[384,128]{1,0:T(8,128)S(1)} collective-permute-done((f32[384,128]{1,0:T(8,128)S(1)}, f32[384,128]{1,0:T(8,128)S(1)}, u32[]{:S(2)}, u32[]{:S(2)}) %collective-permute-start.17) | collective-permute-done | bytes 196640 | tf_op jit(solution)/shard_map/ppermute | solution.py:306
  66.6 2.8 %collective-permute-done.18.refs_5_ = f32[384,128]{1,0:T(8,128)S(1)} collective-permute-done((f32[384,128]{1,0:T(8,128)S(1)}, f32[384,128]{1,0:T(8,128)S(1)}, u32[]{:S(2)}, u32[]{:S(2)}) %collective-permute-start.18) | collective-permute-done | bytes 196640 | tf_op jit(solution)/shard_map/ppermute | solution.py:306
  69.4 1.1 %shard_map.83 = (f32[2,256,128]{2,1,0:T(8,128)S(1)}, f32[64,256]{1,0:T(8,128)S(1)}) custom-call(s32[3]{0:T(128)S(1)} %pad_add_fusion.where, s32[1,2]{1,0:T(1,128)} %slot_range.9, s32[4,8]{1,0:T(4,128)S(1)} %maximum_convert_fusion.offs, f32[384,128]{1,0:T(8,128)S(1)} %collective-permute-done.13.refs_0_, f32[384,128]{1,0:T(8,128)S(1)} %collective-permute-done.14.refs_1_, ...), custom_call_target="tpu_custom_call" | custom-call | flops 2097152 | bytes 1900544 | tf_op jit(solution)/shard_map/pallas_call | solution.py:277
  70.5 3.8 %collective-permute-start.20 = (f32[2,256,128]{2,1,0:T(8,128)S(1)}, f32[2,256,128]{2,1,0:T(8,128)S(1)}, u32[]{:S(2)}, u32[]{:S(2)}) collective-permute-start(f32[2,256,128]{2,1,0:T(8,128)S(1)} %get-tuple-element.66), channel_id=1, source_target_pairs={{0,8},{8,16},{16,24},{1,9},{9,17},{17,25},{2,10},{10,18},{18,26},{... | collective-permute-start | bytes 786440 | tf_op jit(solution)/shard_map/ppermute | solution.py:384
  74.3 1.6 %collective-permute-start.24 = (f32[64,256]{1,0:T(8,128)S(1)}, f32[64,256]{1,0:T(8,128)S(1)}, u32[]{:S(2)}, u32[]{:S(2)}) collective-permute-start(f32[64,256]{1,0:T(8,128)S(1)} %get-tuple-element.71), channel_id=1, source_target_pairs={{0,8},{8,0},{16,24},{24,16},{1,9},{9,1},{17,25},{25,17},{2,10},{10... | collective-permute-start | bytes 196616 | tf_op jit(solution)/shard_map/ppermute | solution.py:316
  75.9 6.0 %collective-permute-done.24 = f32[64,256]{1,0:T(8,128)S(1)} collective-permute-done((f32[64,256]{1,0:T(8,128)S(1)}, f32[64,256]{1,0:T(8,128)S(1)}, u32[]{:S(2)}, u32[]{:S(2)}) %collective-permute-start.24) | collective-permute-done | bytes 65568 | tf_op jit(solution)/shard_map/ppermute | solution.py:316
  81.9 2.7 %collective-permute-start.25 = (f32[64,256]{1,0:T(8,128)S(1)}, f32[64,256]{1,0:T(8,128)S(1)}, u32[]{:S(2)}, u32[]{:S(2)}) collective-permute-start(f32[64,256]{1,0:T(8,128)S(1)} %add.6), channel_id=1, source_target_pairs={{0,16},{8,24},{16,0},{24,8},{1,17},{9,25},{17,1},{25,9},{2,18},{10... | collective-permute-start | bytes 196616 | tf_op jit(solution)/shard_map/ppermute | solution.py:316
  84.6 1.6 %shard_map.82.own = f32[4,256,128]{2,1,0:T(8,128)S(1)} custom-call(s32[3]{0:T(128)S(1)} %pad_add_fusion.where, s32[1,2]{1,0:T(1,128)} %slot_range.9, s32[4,8]{1,0:T(4,128)S(1)} %maximum_convert_fusion.offs, f32[384,128]{1,0:T(8,128)S(1)} %collective-permute-done.13.refs_0_, f32[384,128]{1,0:T(8,128)S(1)} %collective-permute-done.14.refs_1_, ...), custom_call_target="tpu_custom_call" | custom-call | flops 4194304 | bytes 2097152 | tf_op jit(solution)/shard_map/pallas_call | solution.py:277
  86.2 0.6 shard_map.84
  86.8 1.6 %collective-permute-start.21 = (f32[256,128]{1,0:T(8,128)S(1)}, f32[256,128]{1,0:T(8,128)S(1)}, u32[]{:S(2)}, u32[]{:S(2)}) collective-permute-start(f32[256,128]{1,0:T(8,128)S(1)} %get-tuple-element.67), channel_id=1, source_target_pairs={{0,4},{2,6},{4,0},{6,2},{1,5},{3,7},{5,1},{7,3},{8,12},{10,14},{12... | collective-permute-start | bytes 393224 | tf_op jit(solution)/shard_map/ppermute | solution.py:306
  88.4 0.6 collective-permute-start.22
  89.0 1.4 %collective-permute-start.23 = (f32[256,128]{1,0:T(8,128)S(1)}, f32[256,128]{1,0:T(8,128)S(1)}, u32[]{:S(2)}, u32[]{:S(2)}) collective-permute-start(f32[256,128]{1,0:T(8,128)S(1)} %get-tuple-element.69), channel_id=1, source_target_pairs={{0,6},{2,4},{4,2},{6,0},{1,7},{3,5},{5,3},{7,1},{8,14},{10,12},{12... | collective-permute-start | bytes 393224 | tf_op jit(solution)/shard_map/ppermute | solution.py:306
  90.4 10.3 %all_gather.3.refs_4_ = f32[512,256]{1,0:T(8,128)S(1)} all-gather(f32[64,256]{1,0:T(8,128)S(1)} %add.7), channel_id=1, replica_groups=mesh['pair'=4,'half'=2,'col'=2,'core'=2] {'half','col','core'}, dimensions={0}, use_global_device_ids=true | all-gather | bytes 589824 | tf_op jit(solution)/shard_map/all_gather | solution.py:387
  100.6 1.5 %shard_map.85 = (f32[4,256,128]{2,1,0:T(8,128)}, f32[512,256]{1,0:T(8,128)}) custom-call(s32[3]{0:T(128)S(1)} %pad_add_fusion.where, f32[256,128]{1,0:T(8,128)S(1)} %collective-permute-done.21.refs_0_, f32[256,128]{1,0:T(8,128)S(1)} %collective-permute-done.22.refs_1_, f32[256,128]{1,0:T(8,128)S(1)} %collective-permute-done.23.refs_2_, ...), custom_call_target="tpu_custom_call" | custom-call | bytes 2097152 | tf_op jit(solution)/shard_map/pallas_call | solution.py:277
  (22 shorter events, 0.6 us)
Async XLA Ops:
  0.6 1.5 %collective-permute-start = (s32[1,2,2]{2,1,0:T(2,128)}, s32[1,2,2]{2,1,0:T(2,128)S(1)}, u32[]{:S(2)}, u32[]{:S(2)}) collective-permute-start(s32[1,2,2]{2,1,0:T(2,128)} %offsets.1), channel_id=1, source_target_pairs={{0,1},{1,0},{2,3},{3,2},{4,5},{5,4},{6,7},{7,6},{8,9},{9,8},{10,11... | collective-permute-start | bytes 56 | tf_op jit(solution)/shard_map/ppermute | solution.py:329
  4.2 7.0 %collective-permute-start.1 = (f32[264,128]{1,0:T(8,128)S(1)}, f32[264,128]{1,0:T(8,128)S(1)}, u32[]{:S(2)}, u32[]{:S(2)}) collective-permute-start(f32[264,128]{1,0:T(8,128)S(1)} %get-tuple-element.39), channel_id=1, source_target_pairs={{0,2},{2,0},{4,6},{6,4},{1,3},{3,1},{5,7},{7,5},{8,10},{10,8},{12,... | collective-permute-start | bytes 405512 | tf_op jit(solution)/shard_map/ppermute | solution.py:306
  7.0 8.3 %collective-permute-start.2 = (f32[264,128]{1,0:T(8,128)S(1)}, f32[264,128]{1,0:T(8,128)S(1)}, u32[]{:S(2)}, u32[]{:S(2)}) collective-permute-start(f32[264,128]{1,0:T(8,128)S(1)} %get-tuple-element.40), channel_id=1, source_target_pairs={{0,4},{2,6},{4,0},{6,2},{1,5},{3,7},{5,1},{7,3},{8,12},{10,14},{12... | collective-permute-start | bytes 405512 | tf_op jit(solution)/shard_map/ppermute | solution.py:306
  8.5 6.8 %collective-permute-start.3 = (f32[264,128]{1,0:T(8,128)S(1)}, f32[264,128]{1,0:T(8,128)S(1)}, u32[]{:S(2)}, u32[]{:S(2)}) collective-permute-start(f32[264,128]{1,0:T(8,128)S(1)} %get-tuple-element.41), channel_id=1, source_target_pairs={{0,6},{2,4},{4,2},{6,0},{1,7},{3,5},{5,3},{7,1},{8,14},{10,12},{12... | collective-permute-start | bytes 405512 | tf_op jit(solution)/shard_map/ppermute | solution.py:306
  15.9 9.1 %collective-permute-start.4 = (f32[2,256,128]{2,1,0:T(8,128)S(1)}, f32[2,256,128]{2,1,0:T(8,128)S(1)}, u32[]{:S(2)}, u32[]{:S(2)}) collective-permute-start(f32[2,256,128]{2,1,0:T(8,128)S(1)} %shard_map.78), channel_id=1, source_target_pairs={{8,0},{16,8},{24,16},{9,1},{17,9},{25,17},{10,2},{18,10},{26,18},{... | collective-permute-start | bytes 786440 | tf_op jit(solution)/shard_map/ppermute | solution.py:343
  17.2 7.8 %collective-permute-start.5 = (f32[256,256]{1,0:T(8,128)S(1)}, f32[256,256]{1,0:T(8,128)S(1)}, u32[]{:S(2)}, u32[]{:S(2)}) collective-permute-start(f32[256,256]{1,0:T(8,128)S(1)} %get-tuple-element.44), channel_id=1, source_target_pairs={{0,4},{4,0},{1,5},{5,1},{2,6},{6,2},{3,7},{7,3},{8,12},{12,8},{9,1... | collective-permute-start | bytes 786440 | tf_op jit(solution)/shard_map/ppermute | solution.py:344
  26.4 5.7 %collective-permute-start.6 = (f32[256,128]{1,0:T(8,128)S(1)}, f32[256,128]{1,0:T(8,128)S(1)}, u32[]{:S(2)}, u32[]{:S(2)}) collective-permute-start(f32[256,128]{1,0:T(8,128)S(1)} %get-tuple-element.46), channel_id=1, source_target_pairs={{0,4},{1,5},{2,6},{3,7},{4,0},{5,1},{6,2},{7,3},{8,12},{9,13},{10,... | collective-permute-start | bytes 393224 | tf_op jit(solution)/shard_map/ppermute | solution.py:306
  28.1 6.1 %collective-permute-start.7 = (f32[256,128]{1,0:T(8,128)S(1)}, f32[256,128]{1,0:T(8,128)S(1)}, u32[]{:S(2)}, u32[]{:S(2)}) collective-permute-start(f32[256,128]{1,0:T(8,128)S(1)} %get-tuple-element.47), channel_id=1, source_target_pairs={{0,2},{1,3},{2,0},{3,1},{4,6},{5,7},{6,4},{7,5},{8,10},{9,11},{10,... | collective-permute-start | bytes 393224 | tf_op jit(solution)/shard_map/ppermute | solution.py:306
  28.9 8.0 %collective-permute-start.8 = (f32[256,128]{1,0:T(8,128)S(1)}, f32[256,128]{1,0:T(8,128)S(1)}, u32[]{:S(2)}, u32[]{:S(2)}) collective-permute-start(f32[256,128]{1,0:T(8,128)S(1)} %get-tuple-element.48), channel_id=1, source_target_pairs={{0,5},{1,4},{2,7},{3,6},{4,1},{5,0},{6,3},{7,2},{8,13},{9,12},{10,... | collective-permute-start | bytes 393224 | tf_op jit(solution)/shard_map/ppermute | solution.py:306
  29.0 8.0 %collective-permute-start.9 = (f32[256,128]{1,0:T(8,128)S(1)}, f32[256,128]{1,0:T(8,128)S(1)}, u32[]{:S(2)}, u32[]{:S(2)}) collective-permute-start(f32[256,128]{1,0:T(8,128)S(1)} %get-tuple-element.49), channel_id=1, source_target_pairs={{0,3},{1,2},{2,1},{3,0},{4,7},{5,6},{6,5},{7,4},{8,11},{9,10},{10,... | collective-permute-start | bytes 393224 | tf_op jit(solution)/shard_map/ppermute | solution.py:306
  30.6 8.7 %collective-permute-start.10 = (f32[256,128]{1,0:T(8,128)S(1)}, f32[256,128]{1,0:T(8,128)S(1)}, u32[]{:S(2)}, u32[]{:S(2)}) collective-permute-start(f32[256,128]{1,0:T(8,128)S(1)} %get-tuple-element.50), channel_id=1, source_target_pairs={{0,6},{1,7},{2,4},{3,5},{4,2},{5,3},{6,0},{7,1},{8,14},{9,15},{10,... | collective-permute-start | bytes 393224 | tf_op jit(solution)/shard_map/ppermute | solution.py:306
  32.1 8.5 %collective-permute-start.11 = (f32[256,128]{1,0:T(8,128)S(1)}, f32[256,128]{1,0:T(8,128)S(1)}, u32[]{:S(2)}, u32[]{:S(2)}) collective-permute-start(f32[256,128]{1,0:T(8,128)S(1)} %get-tuple-element.51), channel_id=1, source_target_pairs={{0,7},{1,6},{2,5},{3,4},{4,3},{5,2},{6,1},{7,0},{8,15},{9,14},{10,... | collective-permute-start | bytes 393224 | tf_op jit(solution)/shard_map/ppermute | solution.py:306
  34.1 6.5 %collective-permute-start.12 = (f32[256,128]{1,0:T(8,128)S(1)}, f32[256,128]{1,0:T(8,128)S(1)}, u32[]{:S(2)}, u32[]{:S(2)}) collective-permute-start(f32[256,128]{1,0:T(8,128)S(1)} %get-tuple-element.52), channel_id=1, source_target_pairs={{0,1},{1,0},{2,3},{3,2},{4,5},{5,4},{6,7},{7,6},{8,9},{9,8},{10,11... | collective-permute-start | bytes 393224 | tf_op jit(solution)/shard_map/ppermute | solution.py:306
  48.9 7.8 %collective-permute-start.13 = (f32[384,128]{1,0:T(8,128)S(1)}, f32[384,128]{1,0:T(8,128)S(1)}, u32[]{:S(2)}, u32[]{:S(2)}) collective-permute-start(f32[384,128]{1,0:T(8,128)S(1)} %get-tuple-element.58), channel_id=1, source_target_pairs={{0,4},{1,5},{2,6},{3,7},{4,0},{5,1},{6,2},{7,3},{8,12},{9,13},{10,... | collective-permute-start | bytes 589832 | tf_op jit(solution)/shard_map/ppermute | solution.py:306
  50.1 7.8 %collective-permute-start.14 = (f32[384,128]{1,0:T(8,128)S(1)}, f32[384,128]{1,0:T(8,128)S(1)}, u32[]{:S(2)}, u32[]{:S(2)}) collective-permute-start(f32[384,128]{1,0:T(8,128)S(1)} %get-tuple-element.59), channel_id=1, source_target_pairs={{0,2},{1,3},{2,0},{3,1},{4,6},{5,7},{6,4},{7,5},{8,10},{9,11},{10,... | collective-permute-start | bytes 589832 | tf_op jit(solution)/shard_map/ppermute | solution.py:306
  51.3 8.8 %collective-permute-start.15 = (f32[384,128]{1,0:T(8,128)S(1)}, f32[384,128]{1,0:T(8,128)S(1)}, u32[]{:S(2)}, u32[]{:S(2)}) collective-permute-start(f32[384,128]{1,0:T(8,128)S(1)} %get-tuple-element.60), channel_id=1, source_target_pairs={{0,5},{1,4},{2,7},{3,6},{4,1},{5,0},{6,3},{7,2},{8,13},{9,12},{10,... | collective-permute-start | bytes 589832 | tf_op jit(solution)/shard_map/ppermute | solution.py:306
  52.2 9.3 %collective-permute-start.16 = (f32[384,128]{1,0:T(8,128)S(1)}, f32[384,128]{1,0:T(8,128)S(1)}, u32[]{:S(2)}, u32[]{:S(2)}) collective-permute-start(f32[384,128]{1,0:T(8,128)S(1)} %get-tuple-element.61), channel_id=1, source_target_pairs={{0,3},{1,2},{2,1},{3,0},{4,7},{5,6},{6,5},{7,4},{8,11},{9,10},{10,... | collective-permute-start | bytes 589832 | tf_op jit(solution)/shard_map/ppermute | solution.py:306
  52.7 13.8 %collective-permute-start.17 = (f32[384,128]{1,0:T(8,128)S(1)}, f32[384,128]{1,0:T(8,128)S(1)}, u32[]{:S(2)}, u32[]{:S(2)}) collective-permute-start(f32[384,128]{1,0:T(8,128)S(1)} %get-tuple-element.62), channel_id=1, source_target_pairs={{0,6},{1,7},{2,4},{3,5},{4,2},{5,3},{6,0},{7,1},{8,14},{9,15},{10,... | collective-permute-start | bytes 589832 | tf_op jit(solution)/shard_map/ppermute | solution.py:306
  56.6 12.8 %collective-permute-start.18 = (f32[384,128]{1,0:T(8,128)S(1)}, f32[384,128]{1,0:T(8,128)S(1)}, u32[]{:S(2)}, u32[]{:S(2)}) collective-permute-start(f32[384,128]{1,0:T(8,128)S(1)} %get-tuple-element.63), channel_id=1, source_target_pairs={{0,7},{1,6},{2,5},{3,4},{4,3},{5,2},{6,1},{7,0},{8,15},{9,14},{10,... | collective-permute-start | bytes 589832 | tf_op jit(solution)/shard_map/ppermute | solution.py:306
  57.9 11.6 %collective-permute-start.19 = (f32[384,128]{1,0:T(8,128)S(1)}, f32[384,128]{1,0:T(8,128)S(1)}, u32[]{:S(2)}, u32[]{:S(2)}) collective-permute-start(f32[384,128]{1,0:T(8,128)S(1)} %get-tuple-element.64), channel_id=1, source_target_pairs={{0,1},{1,0},{2,3},{3,2},{4,5},{5,4},{6,7},{7,6},{8,9},{9,8},{10,11... | collective-permute-start | bytes 589832 | tf_op jit(solution)/shard_map/ppermute | solution.py:306
  70.5 15.6 %collective-permute-start.20 = (f32[2,256,128]{2,1,0:T(8,128)S(1)}, f32[2,256,128]{2,1,0:T(8,128)S(1)}, u32[]{:S(2)}, u32[]{:S(2)}) collective-permute-start(f32[2,256,128]{2,1,0:T(8,128)S(1)} %get-tuple-element.66), channel_id=1, source_target_pairs={{0,8},{8,16},{16,24},{1,9},{9,17},{17,25},{2,10},{10,18},{18,26},{... | collective-permute-start | bytes 786440 | tf_op jit(solution)/shard_map/ppermute | solution.py:384
  74.3 7.6 %collective-permute-start.24 = (f32[64,256]{1,0:T(8,128)S(1)}, f32[64,256]{1,0:T(8,128)S(1)}, u32[]{:S(2)}, u32[]{:S(2)}) collective-permute-start(f32[64,256]{1,0:T(8,128)S(1)} %get-tuple-element.71), channel_id=1, source_target_pairs={{0,8},{8,0},{16,24},{24,16},{1,9},{9,1},{17,25},{25,17},{2,10},{10... | collective-permute-start | bytes 196616 | tf_op jit(solution)/shard_map/ppermute | solution.py:316
  81.9 8.4 %collective-permute-start.25 = (f32[64,256]{1,0:T(8,128)S(1)}, f32[64,256]{1,0:T(8,128)S(1)}, u32[]{:S(2)}, u32[]{:S(2)}) collective-permute-start(f32[64,256]{1,0:T(8,128)S(1)} %add.6), channel_id=1, source_target_pairs={{0,16},{8,24},{16,0},{24,8},{1,17},{9,25},{17,1},{25,9},{2,18},{10... | collective-permute-start | bytes 196616 | tf_op jit(solution)/shard_map/ppermute | solution.py:316
  86.8 13.8 %collective-permute-start.21 = (f32[256,128]{1,0:T(8,128)S(1)}, f32[256,128]{1,0:T(8,128)S(1)}, u32[]{:S(2)}, u32[]{:S(2)}) collective-permute-start(f32[256,128]{1,0:T(8,128)S(1)} %get-tuple-element.67), channel_id=1, source_target_pairs={{0,4},{2,6},{4,0},{6,2},{1,5},{3,7},{5,1},{7,3},{8,12},{10,14},{12... | collective-permute-start | bytes 393224 | tf_op jit(solution)/shard_map/ppermute | solution.py:306
  88.4 12.2 %collective-permute-start.22 = (f32[256,128]{1,0:T(8,128)S(1)}, f32[256,128]{1,0:T(8,128)S(1)}, u32[]{:S(2)}, u32[]{:S(2)}) collective-permute-start(f32[256,128]{1,0:T(8,128)S(1)} %get-tuple-element.68), channel_id=1, source_target_pairs={{0,2},{2,0},{4,6},{6,4},{1,3},{3,1},{5,7},{7,5},{8,10},{10,8},{12,... | collective-permute-start | bytes 393224 | tf_op jit(solution)/shard_map/ppermute | solution.py:306
  89.0 11.7 %collective-permute-start.23 = (f32[256,128]{1,0:T(8,128)S(1)}, f32[256,128]{1,0:T(8,128)S(1)}, u32[]{:S(2)}, u32[]{:S(2)}) collective-permute-start(f32[256,128]{1,0:T(8,128)S(1)} %get-tuple-element.69), channel_id=1, source_target_pairs={{0,6},{2,4},{4,2},{6,0},{1,7},{3,5},{5,3},{7,1},{8,14},{10,12},{12... | collective-permute-start | bytes 393224 | tf_op jit(solution)/shard_map/ppermute | solution.py:306

commit v9 on v8

--- a/solution.py
+++ b/solution.py
@@ -381,6 +381,7 @@
     )
     probe_band = sum_over(probe_band, "pair", pairs)
     (sums,) = call(add_own_kernel, [shape(planes, rows, cols)], scalars, got, 64 * rows * width)
+    lower_sums, sums = lax.optimization_barrier((lower_sums, sums))
     above = lax.ppermute(lower_sums, "pair", [(k, k + 1) for k in range(pairs - 1)])
     sums = call(top_kernel, [shape(rows, cols)] * 4, (where,), (sums, above), planes * rows * cols)
     sums = deal(sums, PLANE[:2])

time: 102 us -> 102 us (level)
  transfers between devices with their start and end apart: 26 -> 26, of which waited for: 14 -> 14; matrix products, arithmetic and copies ran while one was open for 1% -> 1% of each run, Pallas kernels for 5% -> 3%
where the time goes in v9:
time: 102 us
  waiting for transfers between devices  38.8 us (38%)
  starting transfers between devices  32.2 us (32%)
  Pallas kernels  19.6 us (19%)
  blocking collectives  10.3 us (10%)
    ppermute x20, waiting for transfers between devices, deal(): lax.ppermute(value, axes, [(k, k ^ turn) for k in range(count)])  25.7 us
    ppermute x20, starting transfers between devices, deal(): lax.ppermute(value, axes, [(k, k ^ turn) for k in range(count)])  20.8 us
    pallas_call x9, Pallas kernels, call(): pl.pallas_call(kernel, out_shape=[x for x, unused in outs], in_specs=[SME...  19.6 us
    all_gather x1, blocking collectives, local(): probe_grad = lax.all_gather(probe_band, PLANE, axis=0, tiled=True)  10.3 us
    ppermute x1, waiting for transfers between devices, local(): below = lax.ppermute(lowest, 'pair', [(k, k - 1) for k in range(1, pairs)])  6.12 us
    ppermute x2, waiting for transfers between devices, sum_over(): lax.ppermute(value, axis, [(k, k ^ step) for k in range(size)])  5.98 us
    ppermute x2, starting transfers between devices, sum_over(): lax.ppermute(value, axis, [(k, k ^ step) for k in range(size)])  4.32 us
    ppermute x1, starting transfers between devices, local(): lax.ppermute(lower_sums, 'pair', [(k, k + 1) for k in range(pairs - 1)])  3.74 us
  transfers between devices with their start and end apart: 26, of which 14 were waited for; matrix products, arithmetic and copies ran while one was open for 1% of the time, Pallas kernels for 3%

profile of v9, /device:TPU:0, one launch (start us, length us, event | category | flops | bytes accessed | tf_op | source)
XLA Modules:
  0.0 102.2 jit_solution(10464378728261658393)
XLA Ops:
  0.6 0.5 collective-permute-start
  1.2 1.0 collective-permute-done.sibling
  2.2 2.0 %shard_map.77 = (f32[264,128]{1,0:T(8,128)S(1)}, f32[264,128]{1,0:T(8,128)S(1)}, f32[264,128]{1,0:T(8,128)S(1)}, f32[264,128]{1,0:T(8,128)S(1)}, f32[256,256]{1,0:T(8,128)S(1)}) custom-call(s32[3]{0:T(128)S(1)} %pad_add_fusion.where, s32[1,2,2]{2,1,0:T(2,128)} %offsets.1, s32[1,2,2]{2,1,0:T(2,128)S(1)} %collective-permute-done.sibling, ...), custom_call_target="tpu_custom_call" | custom-call | bytes 1851392 | tf_op jit(solution)/shard_map/pallas_call | solution.py:277
  4.2 2.9 %collective-permute-start.1 = (f32[264,128]{1,0:T(8,128)S(1)}, f32[264,128]{1,0:T(8,128)S(1)}, u32[]{:S(2)}, u32[]{:S(2)}) collective-permute-start(f32[264,128]{1,0:T(8,128)S(1)} %get-tuple-element.41), channel_id=1, source_target_pairs={{0,2},{2,0},{4,6},{6,4},{1,3},{3,1},{5,7},{7,5},{8,10},{10,8},{12,... | collective-permute-start | bytes 405512 | tf_op jit(solution)/shard_map/ppermute | solution.py:306
  7.0 1.5 %collective-permute-start.2 = (f32[264,128]{1,0:T(8,128)S(1)}, f32[264,128]{1,0:T(8,128)S(1)}, u32[]{:S(2)}, u32[]{:S(2)}) collective-permute-start(f32[264,128]{1,0:T(8,128)S(1)} %get-tuple-element.42), channel_id=1, source_target_pairs={{0,4},{2,6},{4,0},{6,2},{1,5},{3,7},{5,1},{7,3},{8,12},{10,14},{12... | collective-permute-start | bytes 405512 | tf_op jit(solution)/shard_map/ppermute | solution.py:306
  8.6 2.6 %collective-permute-done.1.refs_1_ = f32[264,128]{1,0:T(8,128)S(1)} collective-permute-done((f32[264,128]{1,0:T(8,128)S(1)}, f32[264,128]{1,0:T(8,128)S(1)}, u32[]{:S(2)}, u32[]{:S(2)}) %collective-permute-start.1) | collective-permute-done | bytes 135200 | tf_op jit(solution)/shard_map/ppermute | solution.py:306
  11.1 4.2 %collective-permute-done.2.refs_0_ = f32[264,128]{1,0:T(8,128)S(1)} collective-permute-done((f32[264,128]{1,0:T(8,128)S(1)}, f32[264,128]{1,0:T(8,128)S(1)}, u32[]{:S(2)}, u32[]{:S(2)}) %collective-permute-start.2) | collective-permute-done | bytes 135200 | tf_op jit(solution)/shard_map/ppermute | solution.py:306
  15.3 0.6 shard_map.78
  15.9 1.3 %collective-permute-start.4 = (f32[2,256,128]{2,1,0:T(8,128)S(1)}, f32[2,256,128]{2,1,0:T(8,128)S(1)}, u32[]{:S(2)}, u32[]{:S(2)}) collective-permute-start(f32[2,256,128]{2,1,0:T(8,128)S(1)} %shard_map.78), channel_id=1, source_target_pairs={{8,0},{16,8},{24,16},{9,1},{17,9},{25,17},{10,2},{18,10},{26,18},{... | collective-permute-start | bytes 786440 | tf_op jit(solution)/shard_map/ppermute | solution.py:343
  17.2 1.6 %collective-permute-start.5 = (f32[256,256]{1,0:T(8,128)S(1)}, f32[256,256]{1,0:T(8,128)S(1)}, u32[]{:S(2)}, u32[]{:S(2)}) collective-permute-start(f32[256,256]{1,0:T(8,128)S(1)} %get-tuple-element.46), channel_id=1, source_target_pairs={{0,4},{4,0},{1,5},{5,1},{2,6},{6,2},{3,7},{7,3},{8,12},{12,8},{9,1... | collective-permute-start | bytes 786440 | tf_op jit(solution)/shard_map/ppermute | solution.py:344
  18.8 0.1 slice_reduce_fusion.3
  18.9 6.1 %collective-permute-done.4.refs_4_ = f32[2,256,128]{2,1,0:T(8,128)S(1)} collective-permute-done((f32[2,256,128]{2,1,0:T(8,128)S(1)}, f32[2,256,128]{2,1,0:T(8,128)S(1)}, u32[]{:S(2)}, u32[]{:S(2)}) %collective-permute-start.4) | collective-permute-done | bytes 262176 | tf_op jit(solution)/shard_map/ppermute | solution.py:343
  25.0 1.4 %shard_map.79 = (f32[256,128]{1,0:T(8,128)S(1)}, f32[256,128]{1,0:T(8,128)S(1)}, f32[256,128]{1,0:T(8,128)S(1)}, f32[256,128]{1,0:T(8,128)S(1)}, f32[256,128]{1,...) custom-call(s32[3]{0:T(128)S(1)} %pad_add_fusion.where, ...), custom_call_target="tpu_custom_call" | custom-call | flops 2097152 | bytes 1851392 | tf_op jit(solution)/shard_map/pallas_call | solution.py:277
  26.4 1.6 %collective-permute-start.6 = (f32[256,128]{1,0:T(8,128)S(1)}, f32[256,128]{1,0:T(8,128)S(1)}, u32[]{:S(2)}, u32[]{:S(2)}) collective-permute-start(f32[256,128]{1,0:T(8,128)S(1)} %get-tuple-element.48), channel_id=1, source_target_pairs={{0,4},{1,5},{2,6},{3,7},{4,0},{5,1},{6,2},{7,3},{8,12},{9,13},{10,... | collective-permute-start | bytes 393224 | tf_op jit(solution)/shard_map/ppermute | solution.py:306
  28.1 0.6 collective-permute-start.7
  28.9 1.6 %collective-permute-start.9 = (f32[256,128]{1,0:T(8,128)S(1)}, f32[256,128]{1,0:T(8,128)S(1)}, u32[]{:S(2)}, u32[]{:S(2)}) collective-permute-start(f32[256,128]{1,0:T(8,128)S(1)} %get-tuple-element.51), channel_id=1, source_target_pairs={{0,3},{1,2},{2,1},{3,0},{4,7},{5,6},{6,5},{7,4},{8,11},{9,10},{10,... | collective-permute-start | bytes 393224 | tf_op jit(solution)/shard_map/ppermute | solution.py:306
  30.6 1.6 %collective-permute-start.10 = (f32[256,128]{1,0:T(8,128)S(1)}, f32[256,128]{1,0:T(8,128)S(1)}, u32[]{:S(2)}, u32[]{:S(2)}) collective-permute-start(f32[256,128]{1,0:T(8,128)S(1)} %get-tuple-element.52), channel_id=1, source_target_pairs={{0,6},{1,7},{2,4},{3,5},{4,2},{5,3},{6,0},{7,1},{8,14},{9,15},{10,... | collective-permute-start | bytes 393224 | tf_op jit(solution)/shard_map/ppermute | solution.py:306
  32.1 0.7 collective-permute-start.11
  32.8 1.3 %collective-permute-done.7.refs_1_ = f32[256,128]{1,0:T(8,128)S(1)} collective-permute-done((f32[256,128]{1,0:T(8,128)S(1)}, f32[256,128]{1,0:T(8,128)S(1)}, u32[]{:S(2)}, u32[]{:S(2)}) %collective-permute-start.7) | collective-permute-done | bytes 131104 | tf_op jit(solution)/shard_map/ppermute | solution.py:306
  34.3 2.6 %shard_map.80 = (f32[2,256,256]{2,1,0:T(8,128)S(1)}, f32[256,256]{1,0:T(8,128)S(1)}, bf16[4,1280,256]{2,1,0:T(8,128)(2,1)S(1)}) custom-call(s32[3]{0:T(128)S(1)} %pad_add_fusion.where, s32[1,2]{1,0:T(1,128)} %slot_range.9, s32[4,8]{1,0:T(4,128)S(1)} %maximum_convert_fusion.offs, f32[2,256,256]{2,1,0:T(8,128)} %probe_from.1, f32[1,2,256,256]{3,2,1,0:T(8,128)} %measured.3, ...), custom_call_target="tpu_custom_call" | custom-call | flops 131072 | bytes 7077888 | tf_op jit(solution)/shard_map/pallas_call | solution.py:277
  36.9 2.3 %collective-permute-done.10.refs_4_ = f32[256,128]{1,0:T(8,128)S(1)} collective-permute-done((f32[256,128]{1,0:T(8,128)S(1)}, f32[256,128]{1,0:T(8,128)S(1)}, u32[]{:S(2)}, u32[]{:S(2)}) %collective-permute-start.10) | collective-permute-done | bytes 131104 | tf_op jit(solution)/shard_map/ppermute | solution.py:306
  39.3 1.4 %collective-permute-done.11.refs_5_ = f32[256,128]{1,0:T(8,128)S(1)} collective-permute-done((f32[256,128]{1,0:T(8,128)S(1)}, f32[256,128]{1,0:T(8,128)S(1)}, u32[]{:S(2)}, u32[]{:S(2)}) %collective-permute-start.11) | collective-permute-done | bytes 131104 | tf_op jit(solution)/shard_map/ppermute | solution.py:306
  40.7 8.2 %shard_map.81 = (f32[384,128]{1,0:T(8,128)S(1)}, f32[384,128]{1,0:T(8,128)S(1)}, f32[384,128]{1,0:T(8,128)S(1)}, f32[384,128]{1,0:T(8,128)S(1)}, f32[384,128]{1,...) custom-call(s32[3]{0:T(128)S(1)} %pad_add_fusion.where, ...), custom_call_target="tpu_custom_call" | custom-call | flops 3221225472 | bytes 6291456 | tf_op jit(solution)/shard_map/pallas_call | solution.py:277
  48.9 1.2 %collective-permute-start.13 = (f32[384,128]{1,0:T(8,128)S(1)}, f32[384,128]{1,0:T(8,128)S(1)}, u32[]{:S(2)}, u32[]{:S(2)}) collective-permute-start(f32[384,128]{1,0:T(8,128)S(1)} %get-tuple-element.60), channel_id=1, source_target_pairs={{0,4},{1,5},{2,6},{3,7},{4,0},{5,1},{6,2},{7,3},{8,12},{9,13},{10,... | collective-permute-start | bytes 589832 | tf_op jit(solution)/shard_map/ppermute | solution.py:306
  50.1 1.2 %collective-permute-start.14 = (f32[384,128]{1,0:T(8,128)S(1)}, f32[384,128]{1,0:T(8,128)S(1)}, u32[]{:S(2)}, u32[]{:S(2)}) collective-permute-start(f32[384,128]{1,0:T(8,128)S(1)} %get-tuple-element.61), channel_id=1, source_target_pairs={{0,2},{1,3},{2,0},{3,1},{4,6},{5,7},{6,4},{7,5},{8,10},{9,11},{10,... | collective-permute-start | bytes 589832 | tf_op jit(solution)/shard_map/ppermute | solution.py:306
  51.3 0.8 collective-permute-start.15
  52.1 0.6 collective-permute-start.16
  52.7 1.8 %collective-permute-start.17 = (f32[384,128]{1,0:T(8,128)S(1)}, f32[384,128]{1,0:T(8,128)S(1)}, u32[]{:S(2)}, u32[]{:S(2)}) collective-permute-start(f32[384,128]{1,0:T(8,128)S(1)} %get-tuple-element.64), channel_id=1, source_target_pairs={{0,6},{1,7},{2,4},{3,5},{4,2},{5,3},{6,0},{7,1},{8,14},{9,15},{10,... | collective-permute-start | bytes 589832 | tf_op jit(solution)/shard_map/ppermute | solution.py:306
  54.5 2.1 %collective-permute-done.13.refs_0_ = f32[384,128]{1,0:T(8,128)S(1)} collective-permute-done((f32[384,128]{1,0:T(8,128)S(1)}, f32[384,128]{1,0:T(8,128)S(1)}, u32[]{:S(2)}, u32[]{:S(2)}) %collective-permute-start.13) | collective-permute-done | bytes 196640 | tf_op jit(solution)/shard_map/ppermute | solution.py:306
  56.6 0.3 collective-permute-start.18
  57.0 0.9 collective-permute-done.14.refs_1_
  57.9 0.7 collective-permute-start.19
  58.6 1.5 %collective-permute-done.15.refs_2_ = f32[384,128]{1,0:T(8,128)S(1)} collective-permute-done((f32[384,128]{1,0:T(8,128)S(1)}, f32[384,128]{1,0:T(8,128)S(1)}, u32[]{:S(2)}, u32[]{:S(2)}) %collective-permute-start.15) | collective-permute-done | bytes 196640 | tf_op jit(solution)/shard_map/ppermute | solution.py:306
  60.1 1.3 %collective-permute-done.16.refs_3_ = f32[384,128]{1,0:T(8,128)S(1)} collective-permute-done((f32[384,128]{1,0:T(8,128)S(1)}, f32[384,128]{1,0:T(8,128)S(1)}, u32[]{:S(2)}, u32[]{:S(2)}) %collective-permute-start.16) | collective-permute-done | bytes 196640 | tf_op jit(solution)/shard_map/ppermute | solution.py:306
  61.4 5.1 %collective-permute-done.17.refs_4_ = f32[384,128]{1,0:T(8,128)S(1)} collective-permute-done((f32[384,128]{1,0:T(8,128)S(1)}, f32[384,128]{1,0:T(8,128)S(1)}, u32[]{:S(2)}, u32[]{:S(2)}) %collective-permute-start.17) | collective-permute-done | bytes 196640 | tf_op jit(solution)/shard_map/ppermute | solution.py:306
  66.6 2.9 %collective-permute-done.18.refs_5_ = f32[384,128]{1,0:T(8,128)S(1)} collective-permute-done((f32[384,128]{1,0:T(8,128)S(1)}, f32[384,128]{1,0:T(8,128)S(1)}, u32[]{:S(2)}, u32[]{:S(2)}) %collective-permute-start.18) | collective-permute-done | bytes 196640 | tf_op jit(solution)/shard_map/ppermute | solution.py:306
  69.4 1.1 %shard_map.82 = (f32[2,256,128]{2,1,0:T(8,128)S(1)}, f32[64,256]{1,0:T(8,128)S(1)}) custom-call(s32[3]{0:T(128)S(1)} %pad_add_fusion.where, s32[1,2]{1,0:T(1,128)} %slot_range.9, s32[4,8]{1,0:T(4,128)S(1)} %maximum_convert_fusion.offs, f32[384,128]{1,0:T(8,128)S(1)} %collective-permute-done.13.refs_0_, f32[384,128]{1,0:T(8,128)S(1)} %collective-permute-done.14.refs_1_, ...), custom_call_target="tpu_custom_call" | custom-call | flops 2097152 | bytes 1900544 | tf_op jit(solution)/shard_map/pallas_call | solution.py:277
  70.6 1.6 %shard_map.83.own = f32[4,256,128]{2,1,0:T(8,128)S(1)} custom-call(s32[3]{0:T(128)S(1)} %pad_add_fusion.where, s32[1,2]{1,0:T(1,128)} %slot_range.9, s32[4,8]{1,0:T(4,128)S(1)} %maximum_convert_fusion.offs, f32[384,128]{1,0:T(8,128)S(1)} %collective-permute-done.13.refs_0_, f32[384,128]{1,0:T(8,128)S(1)} %collective-permute-done.14.refs_1_, ...), custom_call_target="tpu_custom_call" | custom-call | flops 4194304 | bytes 2097152 | tf_op jit(solution)/shard_map/pallas_call | solution.py:277
  72.1 3.7 %collective-permute-start.20 = (f32[2,256,128]{2,1,0:T(8,128)S(1)}, f32[2,256,128]{2,1,0:T(8,128)S(1)}, u32[]{:S(2)}, u32[]{:S(2)}) collective-permute-start(f32[2,256,128]{2,1,0:T(8,128)S(1)} %get-tuple-element.70), channel_id=1, source_target_pairs={{0,8},{8,16},{16,24},{1,9},{9,17},{17,25},{2,10},{10,18},{18,26},{... | collective-permute-start | bytes 786440 | tf_op jit(solution)/shard_map/ppermute | solution.py:385
  75.9 1.6 %collective-permute-start.24 = (f32[64,256]{1,0:T(8,128)S(1)}, f32[64,256]{1,0:T(8,128)S(1)}, u32[]{:S(2)}, u32[]{:S(2)}) collective-permute-start(f32[64,256]{1,0:T(8,128)S(1)} %get-tuple-element.75), channel_id=1, source_target_pairs={{0,8},{8,0},{16,24},{24,16},{1,9},{9,1},{17,25},{25,17},{2,10},{10... | collective-permute-start | bytes 196616 | tf_op jit(solution)/shard_map/ppermute | solution.py:316
  77.5 6.0 %collective-permute-done.24 = f32[64,256]{1,0:T(8,128)S(1)} collective-permute-done((f32[64,256]{1,0:T(8,128)S(1)}, f32[64,256]{1,0:T(8,128)S(1)}, u32[]{:S(2)}, u32[]{:S(2)}) %collective-permute-start.24) | collective-permute-done | bytes 65568 | tf_op jit(solution)/shard_map/ppermute | solution.py:316
  83.5 2.7 %collective-permute-start.25 = (f32[64,256]{1,0:T(8,128)S(1)}, f32[64,256]{1,0:T(8,128)S(1)}, u32[]{:S(2)}, u32[]{:S(2)}) collective-permute-start(f32[64,256]{1,0:T(8,128)S(1)} %add.6), channel_id=1, source_target_pairs={{0,16},{8,24},{16,0},{24,8},{1,17},{9,25},{17,1},{25,9},{2,18},{10... | collective-permute-start | bytes 196616 | tf_op jit(solution)/shard_map/ppermute | solution.py:316
  86.2 0.6 shard_map.84
  86.8 1.6 %collective-permute-start.21 = (f32[256,128]{1,0:T(8,128)S(1)}, f32[256,128]{1,0:T(8,128)S(1)}, u32[]{:S(2)}, u32[]{:S(2)}) collective-permute-start(f32[256,128]{1,0:T(8,128)S(1)} %get-tuple-element.71), channel_id=1, source_target_pairs={{0,4},{2,6},{4,0},{6,2},{1,5},{3,7},{5,1},{7,3},{8,12},{10,14},{12... | collective-permute-start | bytes 393224 | tf_op jit(solution)/shard_map/ppermute | solution.py:306
  88.4 0.6 collective-permute-start.22
  89.0 1.4 %collective-permute-start.23 = (f32[256,128]{1,0:T(8,128)S(1)}, f32[256,128]{1,0:T(8,128)S(1)}, u32[]{:S(2)}, u32[]{:S(2)}) collective-permute-start(f32[256,128]{1,0:T(8,128)S(1)} %get-tuple-element.73), channel_id=1, source_target_pairs={{0,6},{2,4},{4,2},{6,0},{1,7},{3,5},{5,3},{7,1},{8,14},{10,12},{12... | collective-permute-start | bytes 393224 | tf_op jit(solution)/shard_map/ppermute | solution.py:306
  90.4 10.3 %all_gather.3.refs_4_ = f32[512,256]{1,0:T(8,128)S(1)} all-gather(f32[64,256]{1,0:T(8,128)S(1)} %add.7), channel_id=1, replica_groups=mesh['pair'=4,'half'=2,'col'=2,'core'=2] {'half','col','core'}, dimensions={0}, use_global_device_ids=true | all-gather | bytes 589824 | tf_op jit(solution)/shard_map/all_gather | solution.py:388
  100.6 1.5 %shard_map.85 = (f32[4,256,128]{2,1,0:T(8,128)}, f32[512,256]{1,0:T(8,128)}) custom-call(s32[3]{0:T(128)S(1)} %pad_add_fusion.where, f32[256,128]{1,0:T(8,128)S(1)} %collective-permute-done.21.refs_0_, f32[256,128]{1,0:T(8,128)S(1)} %collective-permute-done.22.refs_1_, f32[256,128]{1,0:T(8,128)S(1)} %collective-permute-done.23.refs_2_, ...), custom_call_target="tpu_custom_call" | custom-call | bytes 2097152 | tf_op jit(solution)/shard_map/pallas_call | solution.py:277
  (22 shorter events, 0.6 us)
Async XLA Ops:
  0.6 1.5 %collective-permute-start = (s32[1,2,2]{2,1,0:T(2,128)}, s32[1,2,2]{2,1,0:T(2,128)S(1)}, u32[]{:S(2)}, u32[]{:S(2)}) collective-permute-start(s32[1,2,2]{2,1,0:T(2,128)} %offsets.1), channel_id=1, source_target_pairs={{0,1},{1,0},{2,3},{3,2},{4,5},{5,4},{6,7},{7,6},{8,9},{9,8},{10,11... | collective-permute-start | bytes 56 | tf_op jit(solution)/shard_map/ppermute | solution.py:329
  4.2 7.0 %collective-permute-start.1 = (f32[264,128]{1,0:T(8,128)S(1)}, f32[264,128]{1,0:T(8,128)S(1)}, u32[]{:S(2)}, u32[]{:S(2)}) collective-permute-start(f32[264,128]{1,0:T(8,128)S(1)} %get-tuple-element.41), channel_id=1, source_target_pairs={{0,2},{2,0},{4,6},{6,4},{1,3},{3,1},{5,7},{7,5},{8,10},{10,8},{12,... | collective-permute-start | bytes 405512 | tf_op jit(solution)/shard_map/ppermute | solution.py:306
  7.0 8.3 %collective-permute-start.2 = (f32[264,128]{1,0:T(8,128)S(1)}, f32[264,128]{1,0:T(8,128)S(1)}, u32[]{:S(2)}, u32[]{:S(2)}) collective-permute-start(f32[264,128]{1,0:T(8,128)S(1)} %get-tuple-element.42), channel_id=1, source_target_pairs={{0,4},{2,6},{4,0},{6,2},{1,5},{3,7},{5,1},{7,3},{8,12},{10,14},{12... | collective-permute-start | bytes 405512 | tf_op jit(solution)/shard_map/ppermute | solution.py:306
  8.5 6.8 %collective-permute-start.3 = (f32[264,128]{1,0:T(8,128)S(1)}, f32[264,128]{1,0:T(8,128)S(1)}, u32[]{:S(2)}, u32[]{:S(2)}) collective-permute-start(f32[264,128]{1,0:T(8,128)S(1)} %get-tuple-element.43), channel_id=1, source_target_pairs={{0,6},{2,4},{4,2},{6,0},{1,7},{3,5},{5,3},{7,1},{8,14},{10,12},{12... | collective-permute-start | bytes 405512 | tf_op jit(solution)/shard_map/ppermute | solution.py:306
  15.9 9.1 %collective-permute-start.4 = (f32[2,256,128]{2,1,0:T(8,128)S(1)}, f32[2,256,128]{2,1,0:T(8,128)S(1)}, u32[]{:S(2)}, u32[]{:S(2)}) collective-permute-start(f32[2,256,128]{2,1,0:T(8,128)S(1)} %shard_map.78), channel_id=1, source_target_pairs={{8,0},{16,8},{24,16},{9,1},{17,9},{25,17},{10,2},{18,10},{26,18},{... | collective-permute-start | bytes 786440 | tf_op jit(solution)/shard_map/ppermute | solution.py:343
  17.2 7.8 %collective-permute-start.5 = (f32[256,256]{1,0:T(8,128)S(1)}, f32[256,256]{1,0:T(8,128)S(1)}, u32[]{:S(2)}, u32[]{:S(2)}) collective-permute-start(f32[256,256]{1,0:T(8,128)S(1)} %get-tuple-element.46), channel_id=1, source_target_pairs={{0,4},{4,0},{1,5},{5,1},{2,6},{6,2},{3,7},{7,3},{8,12},{12,8},{9,1... | collective-permute-start | bytes 786440 | tf_op jit(solution)/shard_map/ppermute | solution.py:344
  26.4 5.7 %collective-permute-start.6 = (f32[256,128]{1,0:T(8,128)S(1)}, f32[256,128]{1,0:T(8,128)S(1)}, u32[]{:S(2)}, u32[]{:S(2)}) collective-permute-start(f32[256,128]{1,0:T(8,128)S(1)} %get-tuple-element.48), channel_id=1, source_target_pairs={{0,4},{1,5},{2,6},{3,7},{4,0},{5,1},{6,2},{7,3},{8,12},{9,13},{10,... | collective-permute-start | bytes 393224 | tf_op jit(solution)/shard_map/ppermute | solution.py:306
  28.1 6.1 %collective-permute-start.7 = (f32[256,128]{1,0:T(8,128)S(1)}, f32[256,128]{1,0:T(8,128)S(1)}, u32[]{:S(2)}, u32[]{:S(2)}) collective-permute-start(f32[256,128]{1,0:T(8,128)S(1)} %get-tuple-element.49), channel_id=1, source_target_pairs={{0,2},{1,3},{2,0},{3,1},{4,6},{5,7},{6,4},{7,5},{8,10},{9,11},{10,... | collective-permute-start | bytes 393224 | tf_op jit(solution)/shard_map/ppermute | solution.py:306
  28.9 8.0 %collective-permute-start.8 = (f32[256,128]{1,0:T(8,128)S(1)}, f32[256,128]{1,0:T(8,128)S(1)}, u32[]{:S(2)}, u32[]{:S(2)}) collective-permute-start(f32[256,128]{1,0:T(8,128)S(1)} %get-tuple-element.50), channel_id=1, source_target_pairs={{0,5},{1,4},{2,7},{3,6},{4,1},{5,0},{6,3},{7,2},{8,13},{9,12},{10,... | collective-permute-start | bytes 393224 | tf_op jit(solution)/shard_map/ppermute | solution.py:306
  28.9 8.0 %collective-permute-start.9 = (f32[256,128]{1,0:T(8,128)S(1)}, f32[256,128]{1,0:T(8,128)S(1)}, u32[]{:S(2)}, u32[]{:S(2)}) collective-permute-start(f32[256,128]{1,0:T(8,128)S(1)} %get-tuple-element.51), channel_id=1, source_target_pairs={{0,3},{1,2},{2,1},{3,0},{4,7},{5,6},{6,5},{7,4},{8,11},{9,10},{10,... | collective-permute-start | bytes 393224 | tf_op jit(solution)/shard_map/ppermute | solution.py:306
  30.6 8.7 %collective-permute-start.10 = (f32[256,128]{1,0:T(8,128)S(1)}, f32[256,128]{1,0:T(8,128)S(1)}, u32[]{:S(2)}, u32[]{:S(2)}) collective-permute-start(f32[256,128]{1,0:T(8,128)S(1)} %get-tuple-element.52), channel_id=1, source_target_pairs={{0,6},{1,7},{2,4},{3,5},{4,2},{5,3},{6,0},{7,1},{8,14},{9,15},{10,... | collective-permute-start | bytes 393224 | tf_op jit(solution)/shard_map/ppermute | solution.py:306
  32.1 8.5 %collective-permute-start.11 = (f32[256,128]{1,0:T(8,128)S(1)}, f32[256,128]{1,0:T(8,128)S(1)}, u32[]{:S(2)}, u32[]{:S(2)}) collective-permute-start(f32[256,128]{1,0:T(8,128)S(1)} %get-tuple-element.53), channel_id=1, source_target_pairs={{0,7},{1,6},{2,5},{3,4},{4,3},{5,2},{6,1},{7,0},{8,15},{9,14},{10,... | collective-permute-start | bytes 393224 | tf_op jit(solution)/shard_map/ppermute | solution.py:306
  34.1 6.5 %collective-permute-start.12 = (f32[256,128]{1,0:T(8,128)S(1)}, f32[256,128]{1,0:T(8,128)S(1)}, u32[]{:S(2)}, u32[]{:S(2)}) collective-permute-start(f32[256,128]{1,0:T(8,128)S(1)} %get-tuple-element.54), channel_id=1, source_target_pairs={{0,1},{1,0},{2,3},{3,2},{4,5},{5,4},{6,7},{7,6},{8,9},{9,8},{10,11... | collective-permute-start | bytes 393224 | tf_op jit(solution)/shard_map/ppermute | solution.py:306
  48.9 7.8 %collective-permute-start.13 = (f32[384,128]{1,0:T(8,128)S(1)}, f32[384,128]{1,0:T(8,128)S(1)}, u32[]{:S(2)}, u32[]{:S(2)}) collective-permute-start(f32[384,128]{1,0:T(8,128)S(1)} %get-tuple-element.60), channel_id=1, source_target_pairs={{0,4},{1,5},{2,6},{3,7},{4,0},{5,1},{6,2},{7,3},{8,12},{9,13},{10,... | collective-permute-start | bytes 589832 | tf_op jit(solution)/shard_map/ppermute | solution.py:306
  50.1 7.8 %collective-permute-start.14 = (f32[384,128]{1,0:T(8,128)S(1)}, f32[384,128]{1,0:T(8,128)S(1)}, u32[]{:S(2)}, u32[]{:S(2)}) collective-permute-start(f32[384,128]{1,0:T(8,128)S(1)} %get-tuple-element.61), channel_id=1, source_target_pairs={{0,2},{1,3},{2,0},{3,1},{4,6},{5,7},{6,4},{7,5},{8,10},{9,11},{10,... | collective-permute-start | bytes 589832 | tf_op jit(solution)/shard_map/ppermute | solution.py:306
  51.3 8.8 %collective-permute-start.15 = (f32[384,128]{1,0:T(8,128)S(1)}, f32[384,128]{1,0:T(8,128)S(1)}, u32[]{:S(2)}, u32[]{:S(2)}) collective-permute-start(f32[384,128]{1,0:T(8,128)S(1)} %get-tuple-element.62), channel_id=1, source_target_pairs={{0,5},{1,4},{2,7},{3,6},{4,1},{5,0},{6,3},{7,2},{8,13},{9,12},{10,... | collective-permute-start | bytes 589832 | tf_op jit(solution)/shard_map/ppermute | solution.py:306
  52.1 9.3 %collective-permute-start.16 = (f32[384,128]{1,0:T(8,128)S(1)}, f32[384,128]{1,0:T(8,128)S(1)}, u32[]{:S(2)}, u32[]{:S(2)}) collective-permute-start(f32[384,128]{1,0:T(8,128)S(1)} %get-tuple-element.63), channel_id=1, source_target_pairs={{0,3},{1,2},{2,1},{3,0},{4,7},{5,6},{6,5},{7,4},{8,11},{9,10},{10,... | collective-permute-start | bytes 589832 | tf_op jit(solution)/shard_map/ppermute | solution.py:306
  52.7 13.8 %collective-permute-start.17 = (f32[384,128]{1,0:T(8,128)S(1)}, f32[384,128]{1,0:T(8,128)S(1)}, u32[]{:S(2)}, u32[]{:S(2)}) collective-permute-start(f32[384,128]{1,0:T(8,128)S(1)} %get-tuple-element.64), channel_id=1, source_target_pairs={{0,6},{1,7},{2,4},{3,5},{4,2},{5,3},{6,0},{7,1},{8,14},{9,15},{10,... | collective-permute-start | bytes 589832 | tf_op jit(solution)/shard_map/ppermute | solution.py:306
  56.6 12.8 %collective-permute-start.18 = (f32[384,128]{1,0:T(8,128)S(1)}, f32[384,128]{1,0:T(8,128)S(1)}, u32[]{:S(2)}, u32[]{:S(2)}) collective-permute-start(f32[384,128]{1,0:T(8,128)S(1)} %get-tuple-element.65), channel_id=1, source_target_pairs={{0,7},{1,6},{2,5},{3,4},{4,3},{5,2},{6,1},{7,0},{8,15},{9,14},{10,... | collective-permute-start | bytes 589832 | tf_op jit(solution)/shard_map/ppermute | solution.py:306
  57.9 11.6 %collective-permute-start.19 = (f32[384,128]{1,0:T(8,128)S(1)}, f32[384,128]{1,0:T(8,128)S(1)}, u32[]{:S(2)}, u32[]{:S(2)}) collective-permute-start(f32[384,128]{1,0:T(8,128)S(1)} %get-tuple-element.66), channel_id=1, source_target_pairs={{0,1},{1,0},{2,3},{3,2},{4,5},{5,4},{6,7},{7,6},{8,9},{9,8},{10,11... | collective-permute-start | bytes 589832 | tf_op jit(solution)/shard_map/ppermute | solution.py:306
  72.1 14.1 %collective-permute-start.20 = (f32[2,256,128]{2,1,0:T(8,128)S(1)}, f32[2,256,128]{2,1,0:T(8,128)S(1)}, u32[]{:S(2)}, u32[]{:S(2)}) collective-permute-start(f32[2,256,128]{2,1,0:T(8,128)S(1)} %get-tuple-element.70), channel_id=1, source_target_pairs={{0,8},{8,16},{16,24},{1,9},{9,17},{17,25},{2,10},{10,18},{18,26},{... | collective-permute-start | bytes 786440 | tf_op jit(solution)/shard_map/ppermute | solution.py:385
  75.9 7.6 %collective-permute-start.24 = (f32[64,256]{1,0:T(8,128)S(1)}, f32[64,256]{1,0:T(8,128)S(1)}, u32[]{:S(2)}, u32[]{:S(2)}) collective-permute-start(f32[64,256]{1,0:T(8,128)S(1)} %get-tuple-element.75), channel_id=1, source_target_pairs={{0,8},{8,0},{16,24},{24,16},{1,9},{9,1},{17,25},{25,17},{2,10},{10... | collective-permute-start | bytes 196616 | tf_op jit(solution)/shard_map/ppermute | solution.py:316
  83.5 6.8 %collective-permute-start.25 = (f32[64,256]{1,0:T(8,128)S(1)}, f32[64,256]{1,0:T(8,128)S(1)}, u32[]{:S(2)}, u32[]{:S(2)}) collective-permute-start(f32[64,256]{1,0:T(8,128)S(1)} %add.6), channel_id=1, source_target_pairs={{0,16},{8,24},{16,0},{24,8},{1,17},{9,25},{17,1},{25,9},{2,18},{10... | collective-permute-start | bytes 196616 | tf_op jit(solution)/shard_map/ppermute | solution.py:316
  86.8 13.8 %collective-permute-start.21 = (f32[256,128]{1,0:T(8,128)S(1)}, f32[256,128]{1,0:T(8,128)S(1)}, u32[]{:S(2)}, u32[]{:S(2)}) collective-permute-start(f32[256,128]{1,0:T(8,128)S(1)} %get-tuple-element.71), channel_id=1, source_target_pairs={{0,4},{2,6},{4,0},{6,2},{1,5},{3,7},{5,1},{7,3},{8,12},{10,14},{12... | collective-permute-start | bytes 393224 | tf_op jit(solution)/shard_map/ppermute | solution.py:306
  88.4 12.2 %collective-permute-start.22 = (f32[256,128]{1,0:T(8,128)S(1)}, f32[256,128]{1,0:T(8,128)S(1)}, u32[]{:S(2)}, u32[]{:S(2)}) collective-permute-start(f32[256,128]{1,0:T(8,128)S(1)} %get-tuple-element.72), channel_id=1, source_target_pairs={{0,2},{2,0},{4,6},{6,4},{1,3},{3,1},{5,7},{7,5},{8,10},{10,8},{12,... | collective-permute-start | bytes 393224 | tf_op jit(solution)/shard_map/ppermute | solution.py:306
  89.0 11.7 %collective-permute-start.23 = (f32[256,128]{1,0:T(8,128)S(1)}, f32[256,128]{1,0:T(8,128)S(1)}, u32[]{:S(2)}, u32[]{:S(2)}) collective-permute-start(f32[256,128]{1,0:T(8,128)S(1)} %get-tuple-element.73), channel_id=1, source_target_pairs={{0,6},{2,4},{4,2},{6,0},{1,7},{3,5},{5,3},{7,1},{8,14},{10,12},{12... | collective-permute-start | bytes 393224 | tf_op jit(solution)/shard_map/ppermute | solution.py:306

commit v10 on v8

--- a/solution.py
+++ b/solution.py
@@ -17,19 +17,30 @@
 
 
 def tables(width):
-    index = np.arange(width, dtype=np.int64)
+    half = width // 2
+    index = np.arange(half, dtype=np.int64)
     scale = 1.0 / math.sqrt(width)
-    phase = -2.0 * math.pi / width * (index[:, None] * index[None, :] % width)
-    shift = index[:, None] - index[None, :]
-    chirp = math.pi / width * (shift * shift % (2 * width)) - math.pi / 4.0
-    out = []
-    for angle in (phase, chirp):
-        real, imag = np.cos(angle) * scale, np.sin(angle) * scale
-        table = np.concatenate([-imag, real, imag, real, -imag], axis=0)
-        high = table.astype(ml_dtypes.bfloat16)
-        low = (table - high.astype(np.float64)).astype(ml_dtypes.bfloat16)
-        out.extend([high, low])
-    return np.stack(out)
+    far = np.exp(-2j * math.pi / half * (index[:, None] * index[None, :] % half)) * scale
+    near = []
+    for offset in (0, half):
+        shift = index[:, None] - index[None, :] + offset
+        near.append(np.exp(1j * (math.pi / width * (shift * shift % (2 * width)) - math.pi / 4.0)) * scale)
+    products = []
+    for matrix in ((near[0] + near[1]) / 2.0, (near[0] - near[1]) / 2.0, far):
+        for imag in (matrix.imag, -matrix.imag):
+            table = np.block([[matrix.real, imag], [-imag, matrix.real]])
+            high = table.astype(ml_dtypes.bfloat16)
+            low = (table - high.astype(np.float64)).astype(ml_dtypes.bfloat16)
+            products.append(np.concatenate([high, low], axis=0))
+    angle = -2.0 * math.pi / width * index
+    twiddles = []
+    for part in (np.cos(angle), np.sin(angle)):
+        rows = np.broadcast_to(part[:, None], (half, half))
+        twiddles.append(np.concatenate([rows, np.broadcast_to(part[None, :], (8, half))], axis=0))
+    order = np.zeros((width, width))
+    order[np.arange(width), np.concatenate([2 * index, 2 * index + 1])] = 1.0
+    order = np.stack([order, order.T]).astype(ml_dtypes.bfloat16)
+    return np.stack(products), np.stack(twiddles).astype(np.float32), order
 
 
 def split(value):
@@ -42,29 +53,78 @@
     return jnp.dot(left, right, preferred_element_type=jnp.float32)
 
 
-def transform(re, im, tabs, first, conj):
-    width = re.shape[0]
-
-    def rows(which, start):
-        return tabs[first + which, start * width : (start + 2) * width]
-
-    re_high, re_low = split(re)
-    im_high, im_low = split(im)
-    high = jnp.concatenate([re_high, im_high], 1)
-    both = jnp.concatenate([high, jnp.concatenate([re_low, im_low], 1)], 0)
-
-    def product(start):
-        twice = dot(both, rows(0, start))
-        return twice[:width] + (twice[width:] + dot(high, rows(1, start)))
-
-    re, im = (product(1), product(0)) if conj else (product(3), product(2))
-    by_re, by_im = (3, 2) if conj else (1, 0)
-    re_high, re_low = split(re)
-    im_high, im_low = split(im)
-    out = dot(rows(0, by_re), re_low) + dot(rows(0, by_im), im_low)
-    out += dot(rows(1, by_re), re_high) + dot(rows(1, by_im), im_high)
-    out += dot(rows(0, by_re), re_high) + dot(rows(0, by_im), im_high)
-    return out[:width], out[width:]
+PLUS, MINUS, FAR = 0, 2, 4
+
+
+def times_right(re, im, table):
+    width = table.shape[1]
+    high, low = split(jnp.concatenate([re, im], axis=1))
+    twice = dot(jnp.concatenate([high, low], axis=0), table[:width])
+    count = re.shape[0]
+    out = twice[:count] + (twice[count:] + dot(high, table[width:]))
+    return out[:, : width // 2], out[:, width // 2 :]
+
+
+def times_left(re, im, table):
+    width = table.shape[1]
+    high, low = split(jnp.concatenate([re, im], axis=0))
+    twice = dot(table[...], high)
+    out = twice[:width] + (twice[width:] + dot(table[:width], low))
+    return out[: width // 2], out[width // 2 :]
+
+
+def butterfly(first, second):
+    return first + second, first - second
+
+
+def halves(value, axis):
+    half = value.shape[axis] // 2
+    return (value[:half], value[half:]) if axis == 0 else (value[:, :half], value[:, half:])
+
+
+def turn_by(re, im, cos, sin):
+    return re * cos - im * sin, re * sin + im * cos
+
+
+def propagate(re, im, tabs, conj):
+    for axis in (1, 0):
+        (plus_re, minus_re), (plus_im, minus_im) = (butterfly(*halves(x, axis)) for x in (re, im))
+        times = times_right if axis else times_left
+        pick = int(conj) if axis else 1 - int(conj)
+        plus_re, plus_im = times(plus_re, plus_im, tabs.at[PLUS + pick])
+        minus_re, minus_im = times(minus_re, minus_im, tabs.at[MINUS + pick])
+        re = jnp.concatenate(butterfly(plus_re, minus_re), axis=axis)
+        im = jnp.concatenate(butterfly(plus_im, minus_im), axis=axis)
+    return re, im
+
+
+def twiddle(factors, axis, width):
+    half = factors.shape[2]
+    if axis:
+        return factors[0, half : half + 1], factors[1, half : half + 1]
+    return tuple(jnp.concatenate([factors[k, :half]] * (width // half), axis=1) for k in range(2))
+
+
+def to_far(re, im, tabs, factors):
+    for axis in (1, 0):
+        (even_re, odd_re), (even_im, odd_im) = (butterfly(*halves(x, axis)) for x in (re, im))
+        odd_re, odd_im = turn_by(odd_re, odd_im, *twiddle(factors, axis, re.shape[1]))
+        times, table = (times_right, tabs.at[FAR]) if axis else (times_left, tabs.at[FAR + 1])
+        (even_re, even_im), (odd_re, odd_im) = times(even_re, even_im, table), times(odd_re, odd_im, table)
+        re, im = jnp.concatenate([even_re, odd_re], axis=axis), jnp.concatenate([even_im, odd_im], axis=axis)
+    return re, im
+
+
+def from_far(re, im, tabs, factors):
+    for axis in (0, 1):
+        (even_re, odd_re), (even_im, odd_im) = halves(re, axis), halves(im, axis)
+        times, table = (times_right, tabs.at[FAR + 1]) if axis else (times_left, tabs.at[FAR])
+        (even_re, even_im), (odd_re, odd_im) = times(even_re, even_im, table), times(odd_re, odd_im, table)
+        cos, sin = twiddle(factors, axis, re.shape[1])
+        odd_re, odd_im = turn_by(odd_re, odd_im, cos, -sin)
+        re = jnp.concatenate(butterfly(even_re, odd_re), axis=axis)
+        im = jnp.concatenate(butterfly(even_im, odd_im), axis=axis)
+    return re, im
 
 
 def slot_of(half, col, core):
@@ -146,25 +206,35 @@
     return pltpu.roll(pltpu.roll(value, rows, 0), cols, 1)
 
 
-def ready_kernel(where, slot_range, offs, probe_from, measured, tabs_from, probe, kept, tabs, sems):
+def ready_kernel(where, slot_range, offs, taken, probe_from, measured, tabs_from, order_from, probe, target, tabs, kept, order, sems):
     half, col, core = where[0], where[1], where[2]
-    copies = fetch([(probe_from, probe), (tabs_from, tabs), (measured.at[0, half], kept)], sems)
+    probe_copy, kept_copy, order_copy, tabs_copy = fetch(
+        [(probe_from, probe), (measured.at[0, half], kept), (order_from, order), (tabs_from, tabs)], sems
+    )
     slot = slot_of(half, col, core)
-    unused, row_at, col_at = slot_place(offs, 2 * half + col, slot_range[0, 1 - half], slot)
-    copies[0].wait()
+    lower, row_at, col_at = slot_place(offs, 2 * half + col, slot_range[0, 1 - half], slot)
+    probe_copy.wait()
     for part in range(2):
         probe[part] = roll(probe[part], row_at, col_at)
-    copies[1].wait()
-    copies[2].wait()
+    kept_copy.wait()
+    order_copy.wait()
+    rest = jnp.where(lower == half, kept[...], taken[...])
+    total = jnp.zeros_like(rest)
+    for unused in range(3):
+        part = rest.astype(jnp.bfloat16)
+        rest = rest - part.astype(jnp.float32)
+        total += dot(order[0], dot(part, order[1]).astype(jnp.bfloat16))
+    target[...] = total
+    tabs_copy.wait()
 
 
 def position_kernel(where, slot_range, offs, *refs):
-    gotten, (probe, kept, taken, tabs) = dict(zip(EIGHT, refs)), refs[8:12]
+    gotten, (probe, target, tabs, factors) = dict(zip(EIGHT, refs)), refs[8:12]
     outs, patch, grad = refs[12:20], refs[20], refs[21]
     half, col, core = where[0], where[1], where[2]
     mine = 2 * half + col
     flat = 2 * mine + core
-    lower, row_at, col_at = slot_place(offs, mine, slot_range[0, 1 - half], slot_of(half, col, core))
+    unused, row_at, col_at = slot_place(offs, mine, slot_range[0, 1 - half], slot_of(half, col, core))
     width = probe.shape[-1]
     lanes, band = width // 2, width // 4
     for turn in range(8):
@@ -181,18 +251,17 @@
     o0_re, o0_im, o1_re, o1_im = load(0), load(2), load(1), load(3)
     exit_re = wave_re * o0_re - wave_im * o0_im
     exit_im = wave_re * o0_im + wave_im * o0_re
-    mid_re, mid_im = transform(exit_re, exit_im, tabs, 2, False)
+    mid_re, mid_im = propagate(exit_re, exit_im, tabs, False)
     exit_re = mid_re * o1_re - mid_im * o1_im
     exit_im = mid_re * o1_im + mid_im * o1_re
-    far_re, far_im = transform(exit_re, exit_im, tabs, 0, False)
-    target = jnp.where(lower == half, kept[...], taken[...])
-    excess = 2.0 * GRAD_WEIGHT * (far_re * far_re + far_im * far_im - target)
-    back_re, back_im = transform(excess * far_re, excess * far_im, tabs, 0, True)
+    far_re, far_im = to_far(exit_re, exit_im, tabs, factors)
+    excess = 2.0 * GRAD_WEIGHT * (far_re * far_re + far_im * far_im - target[...])
+    back_re, back_im = from_far(excess * far_re, excess * far_im, tabs, factors)
     store(1, mid_re * back_re + mid_im * back_im)
     store(3, mid_re * back_im - mid_im * back_re)
     up_re = o1_re * back_re + o1_im * back_im
     up_im = o1_re * back_im - o1_im * back_re
-    back_re, back_im = transform(up_re, up_im, tabs, 2, True)
+    back_re, back_im = propagate(up_re, up_im, tabs, True)
     wave_re, wave_im = probe[0], probe[1]
     o0_re, o0_im = load(0), load(2)
     store(0, wave_re * back_re + wave_im * back_im)
@@ -289,16 +358,6 @@
     return jax.ShapeDtypeStruct(dims, jnp.float32)
 
 
-def sum_over(value, axis, size):
-    if size & (size - 1):
-        return lax.psum(value, axis)
-    step = 1
-    while step < size:
-        value = value + lax.ppermute(value, axis, [(k, k ^ step) for k in range(size)])
-        step *= 2
-    return value
-
-
 def deal(values, axes):
     count = len(values)
     order = EIGHT if count == 8 else FOUR
@@ -308,13 +367,15 @@
     ]
 
 
-def sum_over(value, axis, size):
+def sum_over(value, axis, size, first):
     if size & (size - 1):
-        return lax.psum(value, axis)
-    step = 1
+        return value if first else lax.psum(value, axis)
+    step = 1 << first
     while step < size:
         value = value + lax.ppermute(value, axis, [(k, k ^ step) for k in range(size)])
         step *= 2
+        if first == 0:
+            break
     return value
 
 
@@ -354,21 +415,22 @@
     )
     offs = [own[FOUR.index(turn)][rows:, 0] for turn in range(4)]
     scalars = (where, slot_range, jnp.stack(offs).astype(jnp.int32))
-    tabs = jnp.asarray(tables(width))
-    probe, kept, tabs = call(
+    tabs, factors, order = (jnp.asarray(table) for table in tables(width))
+    probe, target, tabs = call(
         ready_kernel,
         [shape(*probe.shape), shape(width, width), jax.ShapeDtypeStruct(tabs.shape, tabs.dtype)],
         scalars,
-        ((probe, HBM), (measured, HBM), (tabs, HBM)),
-        probe.size,
-        copies=3,
+        (taken, (probe, HBM), (measured, HBM), (tabs, HBM), (order, HBM)),
+        12 * width**3,
+        [(width, width), pltpu.VMEM(order.shape, order.dtype)],
+        copies=4,
     )
     grad = call(
         position_kernel,
         [shape(rows + 2 * band, cols)] * 8,
         scalars,
-        (*deal(parts, PLANE), probe, kept, taken, tabs),
-        8 * 24 * width**3,
+        (*deal(parts, PLANE), probe, target, tabs, factors),
+        8 * 12 * width**3,
         [(8, rows, cols), (8, rows + 2 * band, cols)],
     )
     got = deal(grad, PLANE)
@@ -379,11 +441,13 @@
         got,
         32 * rows * width,
     )
-    probe_band = sum_over(probe_band, "pair", pairs)
+    probe_band = sum_over(probe_band, "pair", pairs, 0)
     (sums,) = call(add_own_kernel, [shape(planes, rows, cols)], scalars, got, 64 * rows * width)
+    lower_sums, sums, probe_band = lax.optimization_barrier((lower_sums, sums, probe_band))
     above = lax.ppermute(lower_sums, "pair", [(k, k + 1) for k in range(pairs - 1)])
     sums = call(top_kernel, [shape(rows, cols)] * 4, (where,), (sums, above), planes * rows * cols)
     sums = deal(sums, PLANE[:2])
+    probe_band = sum_over(probe_band, "pair", pairs, 1)
     probe_grad = lax.all_gather(probe_band, PLANE, axis=0, tiled=True)
     object_grad, probe_grad = call(
         join_kernel,

time: 102 us -> 97.8 us (0.959); the launches traced: 102 us -> 96.1 us
  Pallas kernels: 19.6 us -> 15.8 us
  waiting for transfers between devices: 38.8 us -> 37.3 us
    ppermute x2, waiting for transfers between devices: 5.98 us -> 1.2 us  [sum_over(): lax.ppermute(value, axis, [(k, k ^ step) for k in range(size)])]
    pallas_call x9, Pallas kernels: 19.6 us -> 15.8 us  [call(): pl.pallas_call(kernel, out_shape=[x for x, unused in outs], in_specs=[SME...]
    ppermute x1, waiting for transfers between devices: 0.01 us -> 3.46 us  [local(): lax.ppermute(lower_sums, 'pair', [(k, k + 1) for k in range(pairs - 1)])]
  transfers between devices with their start and end apart: 26 -> 26, of which waited for: 14 -> 15; matrix products, arithmetic and copies ran while one was open for 1% -> 1% of each run, Pallas kernels for 5% -> 5%
where the time goes in v10:
time: 97.8 us; the launch traced here: 96.1 us
  waiting for transfers between devices  37.3 us (38%)
  starting transfers between devices  32.4 us (33%)
  Pallas kernels  15.8 us (16%)
  blocking collectives  9.32 us (10%)
    ppermute x20, waiting for transfers between devices, deal(): lax.ppermute(value, axes, [(k, k ^ turn) for k in range(count)])  25.7 us
    ppermute x20, starting transfers between devices, deal(): lax.ppermute(value, axes, [(k, k ^ turn) for k in range(count)])  20.8 us
    pallas_call x9, Pallas kernels, call(): pl.pallas_call(kernel, out_shape=[x for x, unused in outs], in_specs=[SME...  15.8 us
    all_gather x1, blocking collectives, local(): probe_grad = lax.all_gather(probe_band, PLANE, axis=0, tiled=True)  9.32 us
    ppermute x1, waiting for transfers between devices, local(): below = lax.ppermute(lowest, 'pair', [(k, k - 1) for k in range(1, pairs)])  6.01 us
    ppermute x2, starting transfers between devices, sum_over(): lax.ppermute(value, axis, [(k, k ^ step) for k in range(size)])  4.55 us
    ppermute x1, starting transfers between devices, local(): lax.ppermute(lower_sums, 'pair', [(k, k + 1) for k in range(pairs - 1)])  3.66 us
    ppermute x1, waiting for transfers between devices, local(): lax.ppermute(lower_sums, 'pair', [(k, k + 1) for k in range(pairs - 1)])  3.46 us
  transfers between devices with their start and end apart: 26, of which 15 were waited for; matrix products, arithmetic and copies ran while one was open for 1% of the time, Pallas kernels for 5%

profile of v10, /device:TPU:0, one launch (start us, length us, event | category | flops | bytes accessed | tf_op | source)
XLA Modules:
  0.0 96.1 jit_solution(11749039457983960966)
XLA Ops:
  0.6 0.5 collective-permute-start
  1.2 1.0 collective-permute-done.sibling
  2.2 2.0 %shard_map.95 = (f32[264,128]{1,0:T(8,128)S(1)}, f32[264,128]{1,0:T(8,128)S(1)}, f32[264,128]{1,0:T(8,128)S(1)}, f32[264,128]{1,0:T(8,128)S(1)}, f32[256,256]{1,0:T(8,128)S(1)}) custom-call(s32[3]{0:T(128)S(1)} %pad_add_fusion.where, s32[1,2,2]{2,1,0:T(2,128)} %offsets.1, s32[1,2,2]{2,1,0:T(2,128)S(1)} %collective-permute-done.sibling, ...), custom_call_target="tpu_custom_call" | custom-call | bytes 1851392 | tf_op jit(solution)/shard_map/pallas_call | solution.py:346
  4.2 2.9 %collective-permute-start.1 = (f32[264,128]{1,0:T(8,128)S(1)}, f32[264,128]{1,0:T(8,128)S(1)}, u32[]{:S(2)}, u32[]{:S(2)}) collective-permute-start(f32[264,128]{1,0:T(8,128)S(1)} %get-tuple-element.42), channel_id=1, source_target_pairs={{0,2},{2,0},{4,6},{6,4},{1,3},{3,1},{5,7},{7,5},{8,10},{10,8},{12,... | collective-permute-start | bytes 405512 | tf_op jit(solution)/shard_map/ppermute | solution.py:365
  7.0 1.5 %collective-permute-start.2 = (f32[264,128]{1,0:T(8,128)S(1)}, f32[264,128]{1,0:T(8,128)S(1)}, u32[]{:S(2)}, u32[]{:S(2)}) collective-permute-start(f32[264,128]{1,0:T(8,128)S(1)} %get-tuple-element.43), channel_id=1, source_target_pairs={{0,4},{2,6},{4,0},{6,2},{1,5},{3,7},{5,1},{7,3},{8,12},{10,14},{12... | collective-permute-start | bytes 405512 | tf_op jit(solution)/shard_map/ppermute | solution.py:365
  8.6 2.6 %collective-permute-done.1.refs_1_ = f32[264,128]{1,0:T(8,128)S(1)} collective-permute-done((f32[264,128]{1,0:T(8,128)S(1)}, f32[264,128]{1,0:T(8,128)S(1)}, u32[]{:S(2)}, u32[]{:S(2)}) %collective-permute-start.1) | collective-permute-done | bytes 135200 | tf_op jit(solution)/shard_map/ppermute | solution.py:365
  11.1 4.2 %collective-permute-done.2.refs_0_ = f32[264,128]{1,0:T(8,128)S(1)} collective-permute-done((f32[264,128]{1,0:T(8,128)S(1)}, f32[264,128]{1,0:T(8,128)S(1)}, u32[]{:S(2)}, u32[]{:S(2)}) %collective-permute-start.2) | collective-permute-done | bytes 135200 | tf_op jit(solution)/shard_map/ppermute | solution.py:365
  15.3 0.6 shard_map.96
  15.9 1.3 %collective-permute-start.4 = (f32[2,256,128]{2,1,0:T(8,128)S(1)}, f32[2,256,128]{2,1,0:T(8,128)S(1)}, u32[]{:S(2)}, u32[]{:S(2)}) collective-permute-start(f32[2,256,128]{2,1,0:T(8,128)S(1)} %shard_map.96), channel_id=1, source_target_pairs={{8,0},{16,8},{24,16},{9,1},{17,9},{25,17},{10,2},{18,10},{26,18},{... | collective-permute-start | bytes 786440 | tf_op jit(solution)/shard_map/ppermute | solution.py:404
  17.2 1.6 %collective-permute-start.5 = (f32[256,256]{1,0:T(8,128)S(1)}, f32[256,256]{1,0:T(8,128)S(1)}, u32[]{:S(2)}, u32[]{:S(2)}) collective-permute-start(f32[256,256]{1,0:T(8,128)S(1)} %get-tuple-element.47), channel_id=1, source_target_pairs={{0,4},{4,0},{1,5},{5,1},{2,6},{6,2},{3,7},{7,3},{8,12},{12,8},{9,1... | collective-permute-start | bytes 786440 | tf_op jit(solution)/shard_map/ppermute | solution.py:405
  19.0 6.0 %collective-permute-done.4.refs_4_ = f32[2,256,128]{2,1,0:T(8,128)S(1)} collective-permute-done((f32[2,256,128]{2,1,0:T(8,128)S(1)}, f32[2,256,128]{2,1,0:T(8,128)S(1)}, u32[]{:S(2)}, u32[]{:S(2)}) %collective-permute-start.4) | collective-permute-done | bytes 262176 | tf_op jit(solution)/shard_map/ppermute | solution.py:404
  25.0 1.4 %shard_map.97 = (f32[256,128]{1,0:T(8,128)S(1)}, f32[256,128]{1,0:T(8,128)S(1)}, f32[256,128]{1,0:T(8,128)S(1)}, f32[256,128]{1,0:T(8,128)S(1)}, f32[256,128]{1,...) custom-call(s32[3]{0:T(128)S(1)} %pad_add_fusion.where, ...), custom_call_target="tpu_custom_call" | custom-call | flops 2097152 | bytes 1851392 | tf_op jit(solution)/shard_map/pallas_call | solution.py:346
  26.4 1.6 %collective-permute-start.6 = (f32[256,128]{1,0:T(8,128)S(1)}, f32[256,128]{1,0:T(8,128)S(1)}, u32[]{:S(2)}, u32[]{:S(2)}) collective-permute-start(f32[256,128]{1,0:T(8,128)S(1)} %get-tuple-element.49), channel_id=1, source_target_pairs={{0,4},{1,5},{2,6},{3,7},{4,0},{5,1},{6,2},{7,3},{8,12},{9,13},{10,... | collective-permute-start | bytes 393224 | tf_op jit(solution)/shard_map/ppermute | solution.py:365
  28.1 0.6 collective-permute-start.7
  28.9 1.6 %collective-permute-start.9 = (f32[256,128]{1,0:T(8,128)S(1)}, f32[256,128]{1,0:T(8,128)S(1)}, u32[]{:S(2)}, u32[]{:S(2)}) collective-permute-start(f32[256,128]{1,0:T(8,128)S(1)} %get-tuple-element.52), channel_id=1, source_target_pairs={{0,3},{1,2},{2,1},{3,0},{4,7},{5,6},{6,5},{7,4},{8,11},{9,10},{10,... | collective-permute-start | bytes 393224 | tf_op jit(solution)/shard_map/ppermute | solution.py:365
  30.6 1.6 %collective-permute-start.10 = (f32[256,128]{1,0:T(8,128)S(1)}, f32[256,128]{1,0:T(8,128)S(1)}, u32[]{:S(2)}, u32[]{:S(2)}) collective-permute-start(f32[256,128]{1,0:T(8,128)S(1)} %get-tuple-element.53), channel_id=1, source_target_pairs={{0,6},{1,7},{2,4},{3,5},{4,2},{5,3},{6,0},{7,1},{8,14},{9,15},{10,... | collective-permute-start | bytes 393224 | tf_op jit(solution)/shard_map/ppermute | solution.py:365
  32.1 0.7 collective-permute-start.11
  32.8 1.3 %collective-permute-done.7.refs_1_ = f32[256,128]{1,0:T(8,128)S(1)} collective-permute-done((f32[256,128]{1,0:T(8,128)S(1)}, f32[256,128]{1,0:T(8,128)S(1)}, u32[]{:S(2)}, u32[]{:S(2)}) %collective-permute-start.7) | collective-permute-done | bytes 131104 | tf_op jit(solution)/shard_map/ppermute | solution.py:365
  34.2 2.7 %shard_map.98 = (f32[2,256,256]{2,1,0:T(8,128)S(1)}, f32[256,256]{1,0:T(8,128)S(1)}, bf16[6,512,256]{2,1,0:T(8,128)(2,1)S(1)}) custom-call(s32[3]{0:T(128)S(1)} %pad_add_fusion.where, s32[1,2]{1,0:T(1,128)} %slot_range.9, s32[4,8]{1,0:T(4,128)S(1)} %maximum_convert_fusion.offs, f32[256,256]{1,0:T(8,128)S(1)} %collective-permute-done.5.taken, ...), custom_call_target="tpu_custom_call" | custom-call | flops 201326592 | bytes 5505024 | tf_op jit(solution)/shard_map/pallas_call | solution.py:346
  36.9 2.3 %collective-permute-done.10.refs_4_ = f32[256,128]{1,0:T(8,128)S(1)} collective-permute-done((f32[256,128]{1,0:T(8,128)S(1)}, f32[256,128]{1,0:T(8,128)S(1)}, u32[]{:S(2)}, u32[]{:S(2)}) %collective-permute-start.10) | collective-permute-done | bytes 131104 | tf_op jit(solution)/shard_map/ppermute | solution.py:365
  39.3 1.4 %collective-permute-done.11.refs_5_ = f32[256,128]{1,0:T(8,128)S(1)} collective-permute-done((f32[256,128]{1,0:T(8,128)S(1)}, f32[256,128]{1,0:T(8,128)S(1)}, u32[]{:S(2)}, u32[]{:S(2)}) %collective-permute-start.11) | collective-permute-done | bytes 131104 | tf_op jit(solution)/shard_map/ppermute | solution.py:365
  40.7 4.3 %shard_map.99 = (f32[384,128]{1,0:T(8,128)S(1)}, f32[384,128]{1,0:T(8,128)S(1)}, f32[384,128]{1,0:T(8,128)S(1)}, f32[384,128]{1,0:T(8,128)S(1)}, f32[384,128]{1,...) custom-call(s32[3]{0:T(128)S(1)} %pad_add_fusion.where, ...), custom_call_target="tpu_custom_call" | custom-call | flops 1610612736 | bytes 5120000 | tf_op jit(solution)/shard_map/pallas_call | solution.py:346
  45.0 1.2 %collective-permute-start.13 = (f32[384,128]{1,0:T(8,128)S(1)}, f32[384,128]{1,0:T(8,128)S(1)}, u32[]{:S(2)}, u32[]{:S(2)}) collective-permute-start(f32[384,128]{1,0:T(8,128)S(1)} %get-tuple-element.61), channel_id=1, source_target_pairs={{0,4},{1,5},{2,6},{3,7},{4,0},{5,1},{6,2},{7,3},{8,12},{9,13},{10,... | collective-permute-start | bytes 589832 | tf_op jit(solution)/shard_map/ppermute | solution.py:365
  46.2 1.2 %collective-permute-start.14 = (f32[384,128]{1,0:T(8,128)S(1)}, f32[384,128]{1,0:T(8,128)S(1)}, u32[]{:S(2)}, u32[]{:S(2)}) collective-permute-start(f32[384,128]{1,0:T(8,128)S(1)} %get-tuple-element.62), channel_id=1, source_target_pairs={{0,2},{1,3},{2,0},{3,1},{4,6},{5,7},{6,4},{7,5},{8,10},{9,11},{10,... | collective-permute-start | bytes 589832 | tf_op jit(solution)/shard_map/ppermute | solution.py:365
  47.4 0.9 collective-permute-start.15
  48.2 0.6 collective-permute-start.16
  48.8 1.8 %collective-permute-start.17 = (f32[384,128]{1,0:T(8,128)S(1)}, f32[384,128]{1,0:T(8,128)S(1)}, u32[]{:S(2)}, u32[]{:S(2)}) collective-permute-start(f32[384,128]{1,0:T(8,128)S(1)} %get-tuple-element.65), channel_id=1, source_target_pairs={{0,6},{1,7},{2,4},{3,5},{4,2},{5,3},{6,0},{7,1},{8,14},{9,15},{10,... | collective-permute-start | bytes 589832 | tf_op jit(solution)/shard_map/ppermute | solution.py:365
  50.6 2.1 %collective-permute-done.13.refs_0_ = f32[384,128]{1,0:T(8,128)S(1)} collective-permute-done((f32[384,128]{1,0:T(8,128)S(1)}, f32[384,128]{1,0:T(8,128)S(1)}, u32[]{:S(2)}, u32[]{:S(2)}) %collective-permute-start.13) | collective-permute-done | bytes 196640 | tf_op jit(solution)/shard_map/ppermute | solution.py:365
  52.7 0.3 collective-permute-start.18
  53.0 0.9 collective-permute-done.14.refs_1_
  54.0 0.7 collective-permute-start.19
  54.7 1.6 %collective-permute-done.15.refs_2_ = f32[384,128]{1,0:T(8,128)S(1)} collective-permute-done((f32[384,128]{1,0:T(8,128)S(1)}, f32[384,128]{1,0:T(8,128)S(1)}, u32[]{:S(2)}, u32[]{:S(2)}) %collective-permute-start.15) | collective-permute-done | bytes 196640 | tf_op jit(solution)/shard_map/ppermute | solution.py:365
  56.2 1.3 %collective-permute-done.16.refs_3_ = f32[384,128]{1,0:T(8,128)S(1)} collective-permute-done((f32[384,128]{1,0:T(8,128)S(1)}, f32[384,128]{1,0:T(8,128)S(1)}, u32[]{:S(2)}, u32[]{:S(2)}) %collective-permute-start.16) | collective-permute-done | bytes 196640 | tf_op jit(solution)/shard_map/ppermute | solution.py:365
  57.5 5.1 %collective-permute-done.17.refs_4_ = f32[384,128]{1,0:T(8,128)S(1)} collective-permute-done((f32[384,128]{1,0:T(8,128)S(1)}, f32[384,128]{1,0:T(8,128)S(1)}, u32[]{:S(2)}, u32[]{:S(2)}) %collective-permute-start.17) | collective-permute-done | bytes 196640 | tf_op jit(solution)/shard_map/ppermute | solution.py:365
  62.7 2.9 %collective-permute-done.18.refs_5_ = f32[384,128]{1,0:T(8,128)S(1)} collective-permute-done((f32[384,128]{1,0:T(8,128)S(1)}, f32[384,128]{1,0:T(8,128)S(1)}, u32[]{:S(2)}, u32[]{:S(2)}) %collective-permute-start.18) | collective-permute-done | bytes 196640 | tf_op jit(solution)/shard_map/ppermute | solution.py:365
  65.5 1.1 %shard_map.100 = (f32[2,256,128]{2,1,0:T(8,128)S(1)}, f32[64,256]{1,0:T(8,128)S(1)}) custom-call(s32[3]{0:T(128)S(1)} %pad_add_fusion.where, s32[1,2]{1,0:T(1,128)} %slot_range.9, s32[4,8]{1,0:T(4,128)S(1)} %maximum_convert_fusion.offs, f32[384,128]{1,0:T(8,128)S(1)} %collective-permute-done.13.refs_0_, f32[384,128]{1,0:T(8,128)S(1)} %collective-permute-done.14.refs_1_, ...), custom_call_target="tpu_custom_call" | custom-call | flops 2097152 | bytes 1900544 | tf_op jit(solution)/shard_map/pallas_call | solution.py:346
  66.6 1.9 %collective-permute-start.20 = (f32[64,256]{1,0:T(8,128)S(1)}, f32[64,256]{1,0:T(8,128)S(1)}, u32[]{:S(2)}, u32[]{:S(2)}) collective-permute-start(f32[64,256]{1,0:T(8,128)S(1)} %get-tuple-element.70), channel_id=1, source_target_pairs={{0,8},{8,0},{16,24},{24,16},{1,9},{9,1},{17,25},{25,17},{2,10},{10... | collective-permute-start | bytes 196616 | tf_op jit(solution)/shard_map/ppermute | solution.py:375
  68.5 1.6 %shard_map.101.own = f32[4,256,128]{2,1,0:T(8,128)S(1)} custom-call(s32[3]{0:T(128)S(1)} %pad_add_fusion.where, s32[1,2]{1,0:T(1,128)} %slot_range.9, s32[4,8]{1,0:T(4,128)S(1)} %maximum_convert_fusion.offs, f32[384,128]{1,0:T(8,128)S(1)} %collective-permute-done.13.refs_0_, f32[384,128]{1,0:T(8,128)S(1)} %collective-permute-done.14.refs_1_, ...), custom_call_target="tpu_custom_call" | custom-call | flops 4194304 | bytes 2097152 | tf_op jit(solution)/shard_map/pallas_call | solution.py:346
  70.1 1.2 %collective-permute-done.20 = f32[64,256]{1,0:T(8,128)S(1)} collective-permute-done((f32[64,256]{1,0:T(8,128)S(1)}, f32[64,256]{1,0:T(8,128)S(1)}, u32[]{:S(2)}, u32[]{:S(2)}) %collective-permute-start.20) | collective-permute-done | bytes 65568 | tf_op jit(solution)/shard_map/ppermute | solution.py:375
  71.3 3.7 %collective-permute-start.21 = (f32[2,256,128]{2,1,0:T(8,128)S(1)}, f32[2,256,128]{2,1,0:T(8,128)S(1)}, u32[]{:S(2)}, u32[]{:S(2)}) collective-permute-start(f32[2,256,128]{2,1,0:T(8,128)S(1)} %get-tuple-element.72), channel_id=1, source_target_pairs={{0,8},{8,16},{16,24},{1,9},{9,17},{17,25},{2,10},{10,18},{18,26},{... | collective-permute-start | bytes 786440 | tf_op jit(solution)/shard_map/ppermute | solution.py:447
  75.0 2.7 %collective-permute-start.25 = (f32[64,256]{1,0:T(8,128)S(1)}, f32[64,256]{1,0:T(8,128)S(1)}, u32[]{:S(2)}, u32[]{:S(2)}) collective-permute-start(f32[64,256]{1,0:T(8,128)S(1)} %add.6), channel_id=1, source_target_pairs={{0,16},{8,24},{16,0},{24,8},{1,17},{9,25},{17,1},{25,9},{2,18},{10... | collective-permute-start | bytes 196616 | tf_op jit(solution)/shard_map/ppermute | solution.py:375
  77.6 3.5 %collective-permute-done.21.above = f32[2,256,128]{2,1,0:T(8,128)S(1)} collective-permute-done((f32[2,256,128]{2,1,0:T(8,128)S(1)}, f32[2,256,128]{2,1,0:T(8,128)S(1)}, u32[]{:S(2)}, u32[]{:S(2)}) %collective-permute-start.21) | collective-permute-done | bytes 262176 | tf_op jit(solution)/shard_map/ppermute | solution.py:447
  81.1 0.6 shard_map.102
  81.7 1.0 %collective-permute-start.22 = (f32[256,128]{1,0:T(8,128)S(1)}, f32[256,128]{1,0:T(8,128)S(1)}, u32[]{:S(2)}, u32[]{:S(2)}) collective-permute-start(f32[256,128]{1,0:T(8,128)S(1)} %get-tuple-element.73), channel_id=1, source_target_pairs={{0,4},{2,6},{4,0},{6,2},{1,5},{3,7},{5,1},{7,3},{8,12},{10,14},{12... | collective-permute-start | bytes 393224 | tf_op jit(solution)/shard_map/ppermute | solution.py:365
  82.7 1.4 %collective-permute-start.23 = (f32[256,128]{1,0:T(8,128)S(1)}, f32[256,128]{1,0:T(8,128)S(1)}, u32[]{:S(2)}, u32[]{:S(2)}) collective-permute-start(f32[256,128]{1,0:T(8,128)S(1)} %get-tuple-element.74), channel_id=1, source_target_pairs={{0,2},{2,0},{4,6},{6,4},{1,3},{3,1},{5,7},{7,5},{8,10},{10,8},{12,... | collective-permute-start | bytes 393224 | tf_op jit(solution)/shard_map/ppermute | solution.py:365
  84.1 1.2 %collective-permute-start.24 = (f32[256,128]{1,0:T(8,128)S(1)}, f32[256,128]{1,0:T(8,128)S(1)}, u32[]{:S(2)}, u32[]{:S(2)}) collective-permute-start(f32[256,128]{1,0:T(8,128)S(1)} %get-tuple-element.75), channel_id=1, source_target_pairs={{0,6},{2,4},{4,2},{6,0},{1,7},{3,5},{5,3},{7,1},{8,14},{10,12},{12... | collective-permute-start | bytes 393224 | tf_op jit(solution)/shard_map/ppermute | solution.py:365
  85.3 9.3 %all_gather.3.refs_4_ = f32[512,256]{1,0:T(8,128)S(1)} all-gather(f32[64,256]{1,0:T(8,128)S(1)} %add.7), channel_id=1, replica_groups=mesh['pair'=4,'half'=2,'col'=2,'core'=2] {'half','col','core'}, dimensions={0}, use_global_device_ids=true | all-gather | bytes 589824 | tf_op jit(solution)/shard_map/all_gather | solution.py:451
  94.6 1.5 %shard_map.103 = (f32[4,256,128]{2,1,0:T(8,128)}, f32[512,256]{1,0:T(8,128)}) custom-call(s32[3]{0:T(128)S(1)} %pad_add_fusion.where, f32[256,128]{1,0:T(8,128)S(1)} %collective-permute-done.22.refs_0_, f32[256,128]{1,0:T(8,128)S(1)} %collective-permute-done.23.refs_1_, f32[256,128]{1,0:T(8,128)S(1)} %collective-permute-done.24.refs_2_, ...), custom_call_target="tpu_custom_call" | custom-call | bytes 2097152 | tf_op jit(solution)/shard_map/pallas_call | solution.py:346
  (24 shorter events, 0.7 us)
Async XLA Ops:
  0.6 1.5 %collective-permute-start = (s32[1,2,2]{2,1,0:T(2,128)}, s32[1,2,2]{2,1,0:T(2,128)S(1)}, u32[]{:S(2)}, u32[]{:S(2)}) collective-permute-start(s32[1,2,2]{2,1,0:T(2,128)} %offsets.1), channel_id=1, source_target_pairs={{0,1},{1,0},{2,3},{3,2},{4,5},{5,4},{6,7},{7,6},{8,9},{9,8},{10,11... | collective-permute-start | bytes 56 | tf_op jit(solution)/shard_map/ppermute | solution.py:390
  4.2 7.0 %collective-permute-start.1 = (f32[264,128]{1,0:T(8,128)S(1)}, f32[264,128]{1,0:T(8,128)S(1)}, u32[]{:S(2)}, u32[]{:S(2)}) collective-permute-start(f32[264,128]{1,0:T(8,128)S(1)} %get-tuple-element.42), channel_id=1, source_target_pairs={{0,2},{2,0},{4,6},{6,4},{1,3},{3,1},{5,7},{7,5},{8,10},{10,8},{12,... | collective-permute-start | bytes 405512 | tf_op jit(solution)/shard_map/ppermute | solution.py:365
  7.0 8.3 %collective-permute-start.2 = (f32[264,128]{1,0:T(8,128)S(1)}, f32[264,128]{1,0:T(8,128)S(1)}, u32[]{:S(2)}, u32[]{:S(2)}) collective-permute-start(f32[264,128]{1,0:T(8,128)S(1)} %get-tuple-element.43), channel_id=1, source_target_pairs={{0,4},{2,6},{4,0},{6,2},{1,5},{3,7},{5,1},{7,3},{8,12},{10,14},{12... | collective-permute-start | bytes 405512 | tf_op jit(solution)/shard_map/ppermute | solution.py:365
  8.5 6.8 %collective-permute-start.3 = (f32[264,128]{1,0:T(8,128)S(1)}, f32[264,128]{1,0:T(8,128)S(1)}, u32[]{:S(2)}, u32[]{:S(2)}) collective-permute-start(f32[264,128]{1,0:T(8,128)S(1)} %get-tuple-element.44), channel_id=1, source_target_pairs={{0,6},{2,4},{4,2},{6,0},{1,7},{3,5},{5,3},{7,1},{8,14},{10,12},{12... | collective-permute-start | bytes 405512 | tf_op jit(solution)/shard_map/ppermute | solution.py:365
  15.9 9.1 %collective-permute-start.4 = (f32[2,256,128]{2,1,0:T(8,128)S(1)}, f32[2,256,128]{2,1,0:T(8,128)S(1)}, u32[]{:S(2)}, u32[]{:S(2)}) collective-permute-start(f32[2,256,128]{2,1,0:T(8,128)S(1)} %shard_map.96), channel_id=1, source_target_pairs={{8,0},{16,8},{24,16},{9,1},{17,9},{25,17},{10,2},{18,10},{26,18},{... | collective-permute-start | bytes 786440 | tf_op jit(solution)/shard_map/ppermute | solution.py:404
  17.2 7.8 %collective-permute-start.5 = (f32[256,256]{1,0:T(8,128)S(1)}, f32[256,256]{1,0:T(8,128)S(1)}, u32[]{:S(2)}, u32[]{:S(2)}) collective-permute-start(f32[256,256]{1,0:T(8,128)S(1)} %get-tuple-element.47), channel_id=1, source_target_pairs={{0,4},{4,0},{1,5},{5,1},{2,6},{6,2},{3,7},{7,3},{8,12},{12,8},{9,1... | collective-permute-start | bytes 786440 | tf_op jit(solution)/shard_map/ppermute | solution.py:405
  26.4 5.7 %collective-permute-start.6 = (f32[256,128]{1,0:T(8,128)S(1)}, f32[256,128]{1,0:T(8,128)S(1)}, u32[]{:S(2)}, u32[]{:S(2)}) collective-permute-start(f32[256,128]{1,0:T(8,128)S(1)} %get-tuple-element.49), channel_id=1, source_target_pairs={{0,4},{1,5},{2,6},{3,7},{4,0},{5,1},{6,2},{7,3},{8,12},{9,13},{10,... | collective-permute-start | bytes 393224 | tf_op jit(solution)/shard_map/ppermute | solution.py:365
  28.1 6.1 %collective-permute-start.7 = (f32[256,128]{1,0:T(8,128)S(1)}, f32[256,128]{1,0:T(8,128)S(1)}, u32[]{:S(2)}, u32[]{:S(2)}) collective-permute-start(f32[256,128]{1,0:T(8,128)S(1)} %get-tuple-element.50), channel_id=1, source_target_pairs={{0,2},{1,3},{2,0},{3,1},{4,6},{5,7},{6,4},{7,5},{8,10},{9,11},{10,... | collective-permute-start | bytes 393224 | tf_op jit(solution)/shard_map/ppermute | solution.py:365
  28.9 8.0 %collective-permute-start.8 = (f32[256,128]{1,0:T(8,128)S(1)}, f32[256,128]{1,0:T(8,128)S(1)}, u32[]{:S(2)}, u32[]{:S(2)}) collective-permute-start(f32[256,128]{1,0:T(8,128)S(1)} %get-tuple-element.51), channel_id=1, source_target_pairs={{0,5},{1,4},{2,7},{3,6},{4,1},{5,0},{6,3},{7,2},{8,13},{9,12},{10,... | collective-permute-start | bytes 393224 | tf_op jit(solution)/shard_map/ppermute | solution.py:365
  28.9 8.0 %collective-permute-start.9 = (f32[256,128]{1,0:T(8,128)S(1)}, f32[256,128]{1,0:T(8,128)S(1)}, u32[]{:S(2)}, u32[]{:S(2)}) collective-permute-start(f32[256,128]{1,0:T(8,128)S(1)} %get-tuple-element.52), channel_id=1, source_target_pairs={{0,3},{1,2},{2,1},{3,0},{4,7},{5,6},{6,5},{7,4},{8,11},{9,10},{10,... | collective-permute-start | bytes 393224 | tf_op jit(solution)/shard_map/ppermute | solution.py:365
  30.6 8.7 %collective-permute-start.10 = (f32[256,128]{1,0:T(8,128)S(1)}, f32[256,128]{1,0:T(8,128)S(1)}, u32[]{:S(2)}, u32[]{:S(2)}) collective-permute-start(f32[256,128]{1,0:T(8,128)S(1)} %get-tuple-element.53), channel_id=1, source_target_pairs={{0,6},{1,7},{2,4},{3,5},{4,2},{5,3},{6,0},{7,1},{8,14},{9,15},{10,... | collective-permute-start | bytes 393224 | tf_op jit(solution)/shard_map/ppermute | solution.py:365
  32.1 8.5 %collective-permute-start.11 = (f32[256,128]{1,0:T(8,128)S(1)}, f32[256,128]{1,0:T(8,128)S(1)}, u32[]{:S(2)}, u32[]{:S(2)}) collective-permute-start(f32[256,128]{1,0:T(8,128)S(1)} %get-tuple-element.54), channel_id=1, source_target_pairs={{0,7},{1,6},{2,5},{3,4},{4,3},{5,2},{6,1},{7,0},{8,15},{9,14},{10,... | collective-permute-start | bytes 393224 | tf_op jit(solution)/shard_map/ppermute | solution.py:365
  34.1 6.5 %collective-permute-start.12 = (f32[256,128]{1,0:T(8,128)S(1)}, f32[256,128]{1,0:T(8,128)S(1)}, u32[]{:S(2)}, u32[]{:S(2)}) collective-permute-start(f32[256,128]{1,0:T(8,128)S(1)} %get-tuple-element.55), channel_id=1, source_target_pairs={{0,1},{1,0},{2,3},{3,2},{4,5},{5,4},{6,7},{7,6},{8,9},{9,8},{10,11... | collective-permute-start | bytes 393224 | tf_op jit(solution)/shard_map/ppermute | solution.py:365
  34.2 6.5 %copy-start = (f32[2,136,128]{2,1,0:T(8,128)S(1)}, f32[2,136,128]{2,1,0:T(8,128)}, u32[]{:S(2)}) copy-start(f32[2,136,128]{2,1,0:T(8,128)} %constant.17.clone.refs_11_) | copy-start | bytes 417796
  45.0 7.8 %collective-permute-start.13 = (f32[384,128]{1,0:T(8,128)S(1)}, f32[384,128]{1,0:T(8,128)S(1)}, u32[]{:S(2)}, u32[]{:S(2)}) collective-permute-start(f32[384,128]{1,0:T(8,128)S(1)} %get-tuple-element.61), channel_id=1, source_target_pairs={{0,4},{1,5},{2,6},{3,7},{4,0},{5,1},{6,2},{7,3},{8,12},{9,13},{10,... | collective-permute-start | bytes 589832 | tf_op jit(solution)/shard_map/ppermute | solution.py:365
  46.2 7.8 %collective-permute-start.14 = (f32[384,128]{1,0:T(8,128)S(1)}, f32[384,128]{1,0:T(8,128)S(1)}, u32[]{:S(2)}, u32[]{:S(2)}) collective-permute-start(f32[384,128]{1,0:T(8,128)S(1)} %get-tuple-element.62), channel_id=1, source_target_pairs={{0,2},{1,3},{2,0},{3,1},{4,6},{5,7},{6,4},{7,5},{8,10},{9,11},{10,... | collective-permute-start | bytes 589832 | tf_op jit(solution)/shard_map/ppermute | solution.py:365
  47.4 8.8 %collective-permute-start.15 = (f32[384,128]{1,0:T(8,128)S(1)}, f32[384,128]{1,0:T(8,128)S(1)}, u32[]{:S(2)}, u32[]{:S(2)}) collective-permute-start(f32[384,128]{1,0:T(8,128)S(1)} %get-tuple-element.63), channel_id=1, source_target_pairs={{0,5},{1,4},{2,7},{3,6},{4,1},{5,0},{6,3},{7,2},{8,13},{9,12},{10,... | collective-permute-start | bytes 589832 | tf_op jit(solution)/shard_map/ppermute | solution.py:365
  48.2 9.3 %collective-permute-start.16 = (f32[384,128]{1,0:T(8,128)S(1)}, f32[384,128]{1,0:T(8,128)S(1)}, u32[]{:S(2)}, u32[]{:S(2)}) collective-permute-start(f32[384,128]{1,0:T(8,128)S(1)} %get-tuple-element.64), channel_id=1, source_target_pairs={{0,3},{1,2},{2,1},{3,0},{4,7},{5,6},{6,5},{7,4},{8,11},{9,10},{10,... | collective-permute-start | bytes 589832 | tf_op jit(solution)/shard_map/ppermute | solution.py:365
  48.8 13.8 %collective-permute-start.17 = (f32[384,128]{1,0:T(8,128)S(1)}, f32[384,128]{1,0:T(8,128)S(1)}, u32[]{:S(2)}, u32[]{:S(2)}) collective-permute-start(f32[384,128]{1,0:T(8,128)S(1)} %get-tuple-element.65), channel_id=1, source_target_pairs={{0,6},{1,7},{2,4},{3,5},{4,2},{5,3},{6,0},{7,1},{8,14},{9,15},{10,... | collective-permute-start | bytes 589832 | tf_op jit(solution)/shard_map/ppermute | solution.py:365
  52.7 12.8 %collective-permute-start.18 = (f32[384,128]{1,0:T(8,128)S(1)}, f32[384,128]{1,0:T(8,128)S(1)}, u32[]{:S(2)}, u32[]{:S(2)}) collective-permute-start(f32[384,128]{1,0:T(8,128)S(1)} %get-tuple-element.66), channel_id=1, source_target_pairs={{0,7},{1,6},{2,5},{3,4},{4,3},{5,2},{6,1},{7,0},{8,15},{9,14},{10,... | collective-permute-start | bytes 589832 | tf_op jit(solution)/shard_map/ppermute | solution.py:365
  54.0 11.6 %collective-permute-start.19 = (f32[384,128]{1,0:T(8,128)S(1)}, f32[384,128]{1,0:T(8,128)S(1)}, u32[]{:S(2)}, u32[]{:S(2)}) collective-permute-start(f32[384,128]{1,0:T(8,128)S(1)} %get-tuple-element.67), channel_id=1, source_target_pairs={{0,1},{1,0},{2,3},{3,2},{4,5},{5,4},{6,7},{7,6},{8,9},{9,8},{10,11... | collective-permute-start | bytes 589832 | tf_op jit(solution)/shard_map/ppermute | solution.py:365
  66.6 4.7 %collective-permute-start.20 = (f32[64,256]{1,0:T(8,128)S(1)}, f32[64,256]{1,0:T(8,128)S(1)}, u32[]{:S(2)}, u32[]{:S(2)}) collective-permute-start(f32[64,256]{1,0:T(8,128)S(1)} %get-tuple-element.70), channel_id=1, source_target_pairs={{0,8},{8,0},{16,24},{24,16},{1,9},{9,1},{17,25},{25,17},{2,10},{10... | collective-permute-start | bytes 196616 | tf_op jit(solution)/shard_map/ppermute | solution.py:375
  71.3 9.8 %collective-permute-start.21 = (f32[2,256,128]{2,1,0:T(8,128)S(1)}, f32[2,256,128]{2,1,0:T(8,128)S(1)}, u32[]{:S(2)}, u32[]{:S(2)}) collective-permute-start(f32[2,256,128]{2,1,0:T(8,128)S(1)} %get-tuple-element.72), channel_id=1, source_target_pairs={{0,8},{8,16},{16,24},{1,9},{9,17},{17,25},{2,10},{10,18},{18,26},{... | collective-permute-start | bytes 786440 | tf_op jit(solution)/shard_map/ppermute | solution.py:447
  75.0 10.3 %collective-permute-start.25 = (f32[64,256]{1,0:T(8,128)S(1)}, f32[64,256]{1,0:T(8,128)S(1)}, u32[]{:S(2)}, u32[]{:S(2)}) collective-permute-start(f32[64,256]{1,0:T(8,128)S(1)} %add.6), channel_id=1, source_target_pairs={{0,16},{8,24},{16,0},{24,8},{1,17},{9,25},{17,1},{25,9},{2,18},{10... | collective-permute-start | bytes 196616 | tf_op jit(solution)/shard_map/ppermute | solution.py:375
  81.7 12.9 %collective-permute-start.22 = (f32[256,128]{1,0:T(8,128)S(1)}, f32[256,128]{1,0:T(8,128)S(1)}, u32[]{:S(2)}, u32[]{:S(2)}) collective-permute-start(f32[256,128]{1,0:T(8,128)S(1)} %get-tuple-element.73), channel_id=1, source_target_pairs={{0,4},{2,6},{4,0},{6,2},{1,5},{3,7},{5,1},{7,3},{8,12},{10,14},{12... | collective-permute-start | bytes 393224 | tf_op jit(solution)/shard_map/ppermute | solution.py:365
  82.7 11.9 %collective-permute-start.23 = (f32[256,128]{1,0:T(8,128)S(1)}, f32[256,128]{1,0:T(8,128)S(1)}, u32[]{:S(2)}, u32[]{:S(2)}) collective-permute-start(f32[256,128]{1,0:T(8,128)S(1)} %get-tuple-element.74), channel_id=1, source_target_pairs={{0,2},{2,0},{4,6},{6,4},{1,3},{3,1},{5,7},{7,5},{8,10},{10,8},{12,... | collective-permute-start | bytes 393224 | tf_op jit(solution)/shard_map/ppermute | solution.py:365
  84.1 10.5 %collective-permute-start.24 = (f32[256,128]{1,0:T(8,128)S(1)}, f32[256,128]{1,0:T(8,128)S(1)}, u32[]{:S(2)}, u32[]{:S(2)}) collective-permute-start(f32[256,128]{1,0:T(8,128)S(1)} %get-tuple-element.75), channel_id=1, source_target_pairs={{0,6},{2,4},{4,2},{6,0},{1,7},{3,5},{5,3},{7,1},{8,14},{10,12},{12... | collective-permute-start | bytes 393224 | tf_op jit(solution)/shard_map/ppermute | solution.py:365

commit v11 on v10

--- a/solution.py
+++ b/solution.py
@@ -148,53 +148,45 @@
     return copies
 
 
-def deal_kernel(where, offsets, sibling, block, measured, *refs):
+def deal_kernel(where, offsets, block, measured, *refs):
     outs, given, sems = refs[:4], refs[4], refs[5]
-    mine, core = 2 * where[0] + where[1], where[2]
+    mine = 2 * where[0] + where[1]
     rows, cols = block.shape[1:]
     pairs = [(block.at[jnp.bitwise_xor(mine, turn)], out.at[pl.ds(0, rows)]) for turn, out in zip(FOUR, outs)]
     copies = fetch([*pairs, (measured.at[0, 1 - where[0]], given)], sems)
-    lines = []
-    for holder in range(2):
-        for slot in range(2):
-            for axis in range(2):
-                value = jnp.where(core == holder, offsets[0, slot, axis], sibling[0, slot, axis])
-                lines.append(jnp.full((1, cols), value, jnp.int32))
-    lines = jnp.concatenate(lines, axis=0).astype(jnp.float32)
+    lines = [jnp.full((1, cols), offsets[0, slot, axis], jnp.int32) for slot in range(2) for axis in range(2)]
+    lines = jnp.concatenate(lines * 2, axis=0).astype(jnp.float32)
     for out in outs:
         out[rows:] = lines
     for copy in copies:
         copy.wait()
 
 
-def lowest_kernel(where, *refs):
-    gotten, out = dict(zip(FOUR, refs)), refs[4]
-    rows = out.shape[1]
-    for turn in range(2):
-        out[turn] = jnp.where(where[0] == 0, gotten[turn][:rows], gotten[2 + turn][:rows])
-
-
-def pick_kernel(where, slot_range, *refs):
-    gotten, below, outs, (own, parts) = dict(zip(FOUR, refs)), refs[4], refs[5:13], refs[13:]
+def lowest_kernel(where, first, second, out):
+    rows = out.shape[0]
+    out[...] = jnp.where(where[0] == 0, first[:rows], second[:rows])
+
+
+def pick_kernel(where, slot_range, offs, *refs):
+    gotten, below, outs, (own, parts) = dict(zip(FOUR, refs)), refs[4:6], refs[6:14], refs[14:]
     rows, cols = outs[0].shape
     half, col, core = where[0], where[1], where[2]
     mine = 2 * half + col
     for turn in range(4):
-        own[jnp.bitwise_xor(mine, turn)] = gotten[turn][...]
+        own[jnp.bitwise_xor(mine, turn)] = gotten[turn][:rows]
     split_at = slot_range[0, 1 - half]
-    row_ids = lax.broadcasted_iota(jnp.int32, (rows, cols), 0).astype(jnp.float32)
-    col_ids = (lax.broadcasted_iota(jnp.int32, (rows, cols), 1) + core * cols).astype(jnp.float32)
+    row_ids = lax.broadcasted_iota(jnp.int32, (rows, cols), 0)
+    col_ids = lax.broadcasted_iota(jnp.int32, (rows, cols), 1) + core * cols
+    below = [jnp.where(col == side, below[0][...], below[1][...]) for side in range(2)]
     for place, slot in enumerate(receivers()):
-        lower = jnp.where(slot >= split_at, 1, 0)
-        at = rows + 2 * (slot % 4)
-        offs = own[2 * lower + slot // 4, at : at + 2]
-        upper_rows = row_ids >= offs[0:1]
-        left_cols = col_ids >= offs[1:2]
+        lower, row_at, col_at = slot_place(offs, mine, split_at, slot)
+        upper_rows = row_ids >= row_at
+        left_cols = col_ids >= col_at
 
         def merged(side, lower=lower, upper_rows=upper_rows):
-            second = own[2 + side, :rows]
-            top = jnp.where(lower == 1, second, own[side, :rows])
-            bottom = jnp.where(lower == 1, below[jnp.bitwise_xor(col, side)], second)
+            second = own[2 + side]
+            top = jnp.where(lower == 1, second, own[side])
+            bottom = jnp.where(lower == 1, below[side], second)
             return jnp.where(upper_rows, top, bottom)
 
         parts[place] = jnp.where(left_cols, merged(0), merged(1))
@@ -298,11 +290,11 @@
 
 
 def add_below_kernel(where, slot_range, offs, *refs):
-    parts, (below, probe_band) = refs[:8], refs[8:]
-    rows, cols = below.shape[1:]
+    parts, (below0, below1, probe_band) = refs[:8], refs[8:]
+    rows, cols = below0.shape
     sums = add_parts(where, slot_range, offs, parts, 2, rows, cols)
-    for side in range(2):
-        below[jnp.bitwise_xor(where[1], side)] = sums[side]
+    below0[...] = jnp.where(where[1] == 0, sums[0], sums[1])
+    below1[...] = jnp.where(where[1] == 0, sums[1], sums[0])
     total = parts[0][rows:]
     for part in parts[1:]:
         total = total + part[rows:]
@@ -318,10 +310,10 @@
         own[2 * strip], own[2 * strip + 1] = add_parts(where, slot_range, offs, parts, strip, rows, cols)
 
 
-def top_kernel(where, own, above, *outs):
+def top_kernel(turns, where, own, above, *outs):
     mine = 2 * where[0] + where[1]
-    for turn, out in zip(FOUR, outs):
-        extra = jnp.where(where[0] == turn // 2, above[turn % 2], 0.0)
+    for turn, out in zip(turns, outs):
+        extra = jnp.where(where[0] == turn // 2, above[...], 0.0)
         out[...] = own[jnp.bitwise_xor(mine, turn)] + extra
 
 
@@ -387,34 +379,39 @@
     half, col, core = (lax.axis_index(name) for name in PLANE)
     where = jnp.stack([half, col, core])
 
-    sibling = lax.ppermute(offsets, "core", [(0, 1), (1, 0)])
     offsets, slot_range = (pltpu.with_memory_space_constraint(x, pltpu.HBM) for x in (offsets, slot_range))
     block = object_field.reshape(planes, rows, cols)
     *dealt, given = call(
         deal_kernel,
         [shape(rows + 8, cols)] * 4 + [shape(width, width)],
-        (where, offsets, sibling),
+        (where, offsets),
         ((block, HBM), (measured, HBM)),
         0,
         copies=5,
     )
     own = deal(dealt, PLANE[:2])
-    (lowest,) = call(lowest_kernel, [shape(2, rows, cols)], (where,), own, 0)
-    lowest, given = lax.optimization_barrier((lowest, given))
-    below = lax.ppermute(lowest, "pair", [(k, k - 1) for k in range(1, pairs)])
+    turned = dict(zip(FOUR, own))
+    offs = jnp.stack([turned[turn][rows : rows + 4, 0] for turn in range(4)]).astype(jnp.int32)
+    others = lax.ppermute(offs, "core", [(0, 1), (1, 0)])
+    offs = jnp.concatenate([jnp.where(core == 0, offs, others), jnp.where(core == 0, others, offs)], axis=1)
+    below, lowest = [], given
+    for turn in range(2):
+        first, lowest = lax.optimization_barrier((turned[turn], lowest))
+        (lowest,) = call(lowest_kernel, [shape(rows, cols)], (where,), (first, turned[2 + turn]), 0)
+        below.append(lax.ppermute(lowest, "pair", [(k, k - 1) for k in range(1, pairs)]))
+    given, offs = lax.optimization_barrier((given, offs))
     taken = lax.ppermute(given, "half", [(0, 1), (1, 0)])
-    below, taken = lax.optimization_barrier((below, taken))
+    below[1], taken = lax.optimization_barrier((below[1], taken))
+    scalars = (where, slot_range, offs)
 
     parts = call(
         pick_kernel,
         [shape(rows, cols)] * 8,
-        (where, slot_range),
-        (*own, below),
+        scalars,
+        (*own, *below),
         32 * rows * width,
-        [(planes, rows + 8, cols), (8, rows, cols)],
-    )
-    offs = [own[FOUR.index(turn)][rows:, 0] for turn in range(4)]
-    scalars = (where, slot_range, jnp.stack(offs).astype(jnp.int32))
+        [(planes, rows, cols), (8, rows, cols)],
+    )
     tabs, factors, order = (jnp.asarray(table) for table in tables(width))
     probe, target, tabs = call(
         ready_kernel,
@@ -434,19 +431,23 @@
         [(8, rows, cols), (8, rows + 2 * band, cols)],
     )
     got = deal(grad, PLANE)
-    lower_sums, probe_band = call(
+    *lower_sums, probe_band = call(
         add_below_kernel,
-        [shape(2, rows, cols), shape(band, width)],
+        [shape(rows, cols)] * 2 + [shape(band, width)],
         scalars,
         got,
         32 * rows * width,
     )
     probe_band = sum_over(probe_band, "pair", pairs, 0)
     (sums,) = call(add_own_kernel, [shape(planes, rows, cols)], scalars, got, 64 * rows * width)
-    lower_sums, sums, probe_band = lax.optimization_barrier((lower_sums, sums, probe_band))
-    above = lax.ppermute(lower_sums, "pair", [(k, k + 1) for k in range(pairs - 1)])
-    sums = call(top_kernel, [shape(rows, cols)] * 4, (where,), (sums, above), planes * rows * cols)
-    sums = deal(sums, PLANE[:2])
+    *lower_sums, sums, probe_band = lax.optimization_barrier((*lower_sums, sums, probe_band))
+    turned = {}
+    for turn in range(2):
+        above = lax.ppermute(lower_sums[turn], "pair", [(k, k + 1) for k in range(pairs - 1)])
+        turns = (turn, 2 + turn)
+        kernel = functools.partial(top_kernel, turns)
+        turned.update(zip(turns, call(kernel, [shape(rows, cols)] * 2, (where,), (sums, above), 4 * rows * cols)))
+    sums = deal([turned[turn] for turn in FOUR], PLANE[:2])
     probe_band = sum_over(probe_band, "pair", pairs, 1)
     probe_grad = lax.all_gather(probe_band, PLANE, axis=0, tiled=True)
     object_grad, probe_grad = call(

time: 97.8 us -> 99.6 us (1.018)
  Pallas kernels: 15.8 us -> 16.8 us
    ppermute x3 -> x5, starting transfers between devices: 5.47 us -> 9.62 us  [the longest x2 6.96 us: local(): lax.ppermute(lower_sums[turn], 'pair', [(k, k + 1) for k in range(pairs -...]
    ppermute x2, starting transfers between devices: 4.55 us -> 1.72 us  [sum_over(): lax.ppermute(value, axis, [(k, k ^ step) for k in range(size)])]
    ppermute x20, starting transfers between devices: 20.8 us -> 19.5 us  [deal(): lax.ppermute(value, axes, [(k, k ^ turn) for k in range(count)])]
    pallas_call x9 -> x11, Pallas kernels: 15.8 us -> 16.8 us  [call(): pl.pallas_call(kernel, out_shape=[x for x, unused in outs], in_specs=[SME...]
    ppermute x3 -> x5, waiting for transfers between devices: 10.4 us -> 10.1 us  [the longest x2 7.39 us: local(): lax.ppermute(lowest, 'pair', [(k, k - 1) for k in range(1, pairs)])]
  transfers between devices with their start and end apart: 26 -> 28, of which waited for: 15 -> 15; matrix products, arithmetic and copies ran while one was open for 1% -> 0% of each run, Pallas kernels for 5% -> 7%
where the time goes in v11:
time: 99.6 us; the launch traced here: 98 us
  waiting for transfers between devices  37.9 us (38%)
  starting transfers between devices  32.3 us (32%)
  Pallas kernels  16.8 us (17%)
  blocking collectives  9.48 us (10%)
    ppermute x20, waiting for transfers between devices, deal(): lax.ppermute(value, axes, [(k, k ^ turn) for k in range(count)])  26.6 us
    ppermute x20, starting transfers between devices, deal(): lax.ppermute(value, axes, [(k, k ^ turn) for k in range(count)])  19.5 us
    pallas_call x11, Pallas kernels, call(): pl.pallas_call(kernel, out_shape=[x for x, unused in outs], in_specs=[SME...  16.8 us
    all_gather x1, blocking collectives, local(): probe_grad = lax.all_gather(probe_band, PLANE, axis=0, tiled=True)  9.48 us
    ppermute x2, waiting for transfers between devices, local(): lax.ppermute(lowest, 'pair', [(k, k - 1) for k in range(1, pairs)])  7.39 us
    ppermute x2, starting transfers between devices, local(): lax.ppermute(lower_sums[turn], 'pair', [(k, k + 1) for k in range(pairs -...  6.96 us
    ppermute x2, starting transfers between devices, local(): lax.ppermute(lowest, 'pair', [(k, k - 1) for k in range(1, pairs)])  2.58 us
  transfers between devices with their start and end apart: 28, of which 15 were waited for; matrix products, arithmetic and copies ran while one was open for 0% of the time, Pallas kernels for 7%

profile of v11, /device:TPU:0, one launch (start us, length us, event | category | flops | bytes accessed | tf_op | source)
XLA Modules:
  0.0 98.0 jit_solution(553095808040831738)
XLA Ops:
  0.7 2.0 %shard_map.95 = (f32[264,128]{1,0:T(8,128)S(1)}, f32[264,128]{1,0:T(8,128)S(1)}, f32[264,128]{1,0:T(8,128)S(1)}, f32[264,128]{1,0:T(8,128)S(1)}, f32[256,256]{1,0:T(8,128)S(1)}) custom-call(s32[3]{0:T(128)S(1)} %pad_add_fusion.1.where, s32[1,2,2]{2,1,0:T(2,128)} %offsets.1, f32[4,256,128]{2,1,0:T(8,128)} %bitcast.10, f32[1,2,256,256]{3,2,1,0:T(8,128)} %measured.3), custom_call_target="tpu_custom_call" | custom-call | bytes 1851392 | tf_op jit(solution)/shard_map/pallas_call | solution.py:338
  2.7 3.0 %collective-permute-start = (f32[264,128]{1,0:T(8,128)S(1)}, f32[264,128]{1,0:T(8,128)S(1)}, u32[]{:S(2)}, u32[]{:S(2)}) collective-permute-start(f32[264,128]{1,0:T(8,128)S(1)} %get-tuple-element.47), channel_id=1, source_target_pairs={{0,2},{2,0},{4,6},{6,4},{1,3},{3,1},{5,7},{7,5},{8,10},{10,8},{12,... | collective-permute-start | bytes 405512 | tf_op jit(solution)/shard_map/ppermute | solution.py:357
  5.7 1.5 %collective-permute-start.1 = (f32[264,128]{1,0:T(8,128)S(1)}, f32[264,128]{1,0:T(8,128)S(1)}, u32[]{:S(2)}, u32[]{:S(2)}) collective-permute-start(f32[264,128]{1,0:T(8,128)S(1)} %get-tuple-element.48), channel_id=1, source_target_pairs={{0,4},{2,6},{4,0},{6,2},{1,5},{3,7},{5,1},{7,3},{8,12},{10,14},{12... | collective-permute-start | bytes 405512 | tf_op jit(solution)/shard_map/ppermute | solution.py:357
  7.3 2.3 %collective-permute-done.first.refs_1_ = f32[264,128]{1,0:T(8,128)S(1)} collective-permute-done((f32[264,128]{1,0:T(8,128)S(1)}, f32[264,128]{1,0:T(8,128)S(1)}, u32[]{:S(2)}, u32[]{:S(2)}) %collective-permute-start) | collective-permute-done | bytes 135200 | tf_op jit(solution)/shard_map/ppermute | solution.py:357
  9.8 3.8 %collective-permute-done.1.second.refs_0_ = f32[264,128]{1,0:T(8,128)S(1)} collective-permute-done((f32[264,128]{1,0:T(8,128)S(1)}, f32[264,128]{1,0:T(8,128)S(1)}, u32[]{:S(2)}, u32[]{:S(2)}) %collective-permute-start.1) | collective-permute-done | bytes 135200 | tf_op jit(solution)/shard_map/ppermute | solution.py:357
  14.0 1.1 %collective-permute-done.3 = s32[4,4]{1,0:T(4,128)S(1)} collective-permute-done((s32[4,4]{1,0:T(4,128)S(1)}, s32[4,4]{1,0:T(4,128)S(1)}, u32[]{:S(2)}, u32[]{:S(2)}) %collective-permute-start.3) | collective-permute-done | bytes 96 | tf_op jit(solution)/shard_map/ppermute | solution.py:395
  15.2 1.5 %collective-permute-start.6 = (f32[256,256]{1,0:T(8,128)S(1)}, f32[256,256]{1,0:T(8,128)S(1)}, u32[]{:S(2)}, u32[]{:S(2)}) collective-permute-start(f32[256,256]{1,0:T(8,128)S(1)} %get-tuple-element.53), channel_id=1, source_target_pairs={{0,4},{4,0},{1,5},{5,1},{2,6},{6,2},{3,7},{7,3},{8,12},{12,8},{9,1... | collective-permute-start | bytes 786440 | tf_op jit(solution)/shard_map/ppermute | solution.py:403
  16.7 0.6 shard_map.96
  17.3 0.6 shard_map.97
  17.8 1.3 %collective-permute-start.5 = (f32[256,128]{1,0:T(8,128)S(1)}, f32[256,128]{1,0:T(8,128)S(1)}, u32[]{:S(2)}, u32[]{:S(2)}) collective-permute-start(f32[256,128]{1,0:T(8,128)S(1)} %shard_map.97), channel_id=1, source_target_pairs={{8,0},{16,8},{24,16},{9,1},{17,9},{25,17},{10,2},{18,10},{26,18},{... | collective-permute-start | bytes 393224 | tf_op jit(solution)/shard_map/ppermute | solution.py:401
  19.1 1.3 %collective-permute-start.4 = (f32[256,128]{1,0:T(8,128)S(1)}, f32[256,128]{1,0:T(8,128)S(1)}, u32[]{:S(2)}, u32[]{:S(2)}) collective-permute-start(f32[256,128]{1,0:T(8,128)S(1)} %shard_map.96), channel_id=1, source_target_pairs={{8,0},{16,8},{24,16},{9,1},{17,9},{25,17},{10,2},{18,10},{26,18},{... | collective-permute-start | bytes 393224 | tf_op jit(solution)/shard_map/ppermute | solution.py:401
  20.4 5.5 %collective-permute-done.5.refs_5_ = f32[256,128]{1,0:T(8,128)S(1)} collective-permute-done((f32[256,128]{1,0:T(8,128)S(1)}, f32[256,128]{1,0:T(8,128)S(1)}, u32[]{:S(2)}, u32[]{:S(2)}) %collective-permute-start.5) | collective-permute-done | bytes 131104 | tf_op jit(solution)/shard_map/ppermute | solution.py:401
  25.9 1.9 %collective-permute-done.4.refs_4_ = f32[256,128]{1,0:T(8,128)S(1)} collective-permute-done((f32[256,128]{1,0:T(8,128)S(1)}, f32[256,128]{1,0:T(8,128)S(1)}, u32[]{:S(2)}, u32[]{:S(2)}) %collective-permute-start.4) | collective-permute-done | bytes 131104 | tf_op jit(solution)/shard_map/ppermute | solution.py:401
  27.8 1.4 %shard_map.98 = (f32[256,128]{1,0:T(8,128)S(1)}, f32[256,128]{1,0:T(8,128)S(1)}, f32[256,128]{1,0:T(8,128)S(1)}, f32[256,128]{1,0:T(8,128)S(1)}, f32[256,128]{1,...) custom-call(s32[3]{0:T(128)S(1)} %pad_add_fusion.1.where, ...), custom_call_target="tpu_custom_call" | custom-call | flops 2097152 | bytes 1851392 | tf_op jit(solution)/shard_map/pallas_call | solution.py:338
  29.3 0.6 collective-permute-start.7
  29.9 1.1 %collective-permute-start.8 = (f32[256,128]{1,0:T(8,128)S(1)}, f32[256,128]{1,0:T(8,128)S(1)}, u32[]{:S(2)}, u32[]{:S(2)}) collective-permute-start(f32[256,128]{1,0:T(8,128)S(1)} %get-tuple-element.56), channel_id=1, source_target_pairs={{0,2},{1,3},{2,0},{3,1},{4,6},{5,7},{6,4},{7,5},{8,10},{9,11},{10,... | collective-permute-start | bytes 393224 | tf_op jit(solution)/shard_map/ppermute | solution.py:357
  31.0 2.1 %collective-permute-start.10 = (f32[256,128]{1,0:T(8,128)S(1)}, f32[256,128]{1,0:T(8,128)S(1)}, u32[]{:S(2)}, u32[]{:S(2)}) collective-permute-start(f32[256,128]{1,0:T(8,128)S(1)} %get-tuple-element.58), channel_id=1, source_target_pairs={{0,3},{1,2},{2,1},{3,0},{4,7},{5,6},{6,5},{7,4},{8,11},{9,10},{10,... | collective-permute-start | bytes 393224 | tf_op jit(solution)/shard_map/ppermute | solution.py:357
  33.1 1.1 %collective-permute-start.11 = (f32[256,128]{1,0:T(8,128)S(1)}, f32[256,128]{1,0:T(8,128)S(1)}, u32[]{:S(2)}, u32[]{:S(2)}) collective-permute-start(f32[256,128]{1,0:T(8,128)S(1)} %get-tuple-element.59), channel_id=1, source_target_pairs={{0,6},{1,7},{2,4},{3,5},{4,2},{5,3},{6,0},{7,1},{8,14},{9,15},{10,... | collective-permute-start | bytes 393224 | tf_op jit(solution)/shard_map/ppermute | solution.py:357
  34.2 0.5 collective-permute-done.7.refs_0_
  34.7 0.6 collective-permute-done.8.refs_1_
  35.3 0.9 collective-permute-start.13
  36.2 2.6 %shard_map.99 = (f32[2,256,256]{2,1,0:T(8,128)S(1)}, f32[256,256]{1,0:T(8,128)S(1)}, bf16[6,512,256]{2,1,0:T(8,128)(2,1)S(1)}) custom-call(s32[3]{0:T(128)S(1)} %pad_add_fusion.1.where, s32[1,2]{1,0:T(1,128)} %slot_range.9, s32[4,8]{1,0:T(4,128)S(1)} %pad_add_fusion.offs, f32[256,256]{1,0:T(8,128)S(1)} %collective-permute-done.6.taken, ...), custom_call_target="tpu_custom_call" | custom-call | flops 201326592 | bytes 5505024 | tf_op jit(solution)/shard_map/pallas_call | solution.py:338
  38.8 4.0 %collective-permute-done.11.refs_4_ = f32[256,128]{1,0:T(8,128)S(1)} collective-permute-done((f32[256,128]{1,0:T(8,128)S(1)}, f32[256,128]{1,0:T(8,128)S(1)}, u32[]{:S(2)}, u32[]{:S(2)}) %collective-permute-start.11) | collective-permute-done | bytes 131104 | tf_op jit(solution)/shard_map/ppermute | solution.py:357
  42.8 4.3 %shard_map.100 = (f32[384,128]{1,0:T(8,128)S(1)}, f32[384,128]{1,0:T(8,128)S(1)}, f32[384,128]{1,0:T(8,128)S(1)}, f32[384,128]{1,0:T(8,128)S(1)}, f32[384,128]{1...) custom-call(s32[3]{0:T(128)S(1)} %pad_add_fusion.1.where, ...), custom_call_target="tpu_custom_call" | custom-call | flops 1610612736 | bytes 5120000 | tf_op jit(solution)/shard_map/pallas_call | solution.py:338
  47.1 1.5 %collective-permute-start.14 = (f32[384,128]{1,0:T(8,128)S(1)}, f32[384,128]{1,0:T(8,128)S(1)}, u32[]{:S(2)}, u32[]{:S(2)}) collective-permute-start(f32[384,128]{1,0:T(8,128)S(1)} %get-tuple-element.67), channel_id=1, source_target_pairs={{0,4},{1,5},{2,6},{3,7},{4,0},{5,1},{6,2},{7,3},{8,12},{9,13},{10,... | collective-permute-start | bytes 589832 | tf_op jit(solution)/shard_map/ppermute | solution.py:357
  48.6 0.5 collective-permute-start.15
  49.1 0.9 collective-permute-start.16
  50.0 0.9 collective-permute-start.17
  50.9 1.4 %collective-permute-start.18 = (f32[384,128]{1,0:T(8,128)S(1)}, f32[384,128]{1,0:T(8,128)S(1)}, u32[]{:S(2)}, u32[]{:S(2)}) collective-permute-start(f32[384,128]{1,0:T(8,128)S(1)} %get-tuple-element.71), channel_id=1, source_target_pairs={{0,6},{1,7},{2,4},{3,5},{4,2},{5,3},{6,0},{7,1},{8,14},{9,15},{10,... | collective-permute-start | bytes 589832 | tf_op jit(solution)/shard_map/ppermute | solution.py:357
  52.3 2.4 %collective-permute-done.14.refs_0_ = f32[384,128]{1,0:T(8,128)S(1)} collective-permute-done((f32[384,128]{1,0:T(8,128)S(1)}, f32[384,128]{1,0:T(8,128)S(1)}, u32[]{:S(2)}, u32[]{:S(2)}) %collective-permute-start.14) | collective-permute-done | bytes 196640 | tf_op jit(solution)/shard_map/ppermute | solution.py:357
  54.7 1.3 %collective-permute-start.19 = (f32[384,128]{1,0:T(8,128)S(1)}, f32[384,128]{1,0:T(8,128)S(1)}, u32[]{:S(2)}, u32[]{:S(2)}) collective-permute-start(f32[384,128]{1,0:T(8,128)S(1)} %get-tuple-element.72), channel_id=1, source_target_pairs={{0,7},{1,6},{2,5},{3,4},{4,3},{5,2},{6,1},{7,0},{8,15},{9,14},{10,... | collective-permute-start | bytes 589832 | tf_op jit(solution)/shard_map/ppermute | solution.py:357
  55.9 0.4 collective-permute-done.15.refs_1_
  56.4 2.7 %collective-permute-done.16.refs_2_ = f32[384,128]{1,0:T(8,128)S(1)} collective-permute-done((f32[384,128]{1,0:T(8,128)S(1)}, f32[384,128]{1,0:T(8,128)S(1)}, u32[]{:S(2)}, u32[]{:S(2)}) %collective-permute-start.16) | collective-permute-done | bytes 196640 | tf_op jit(solution)/shard_map/ppermute | solution.py:357
  59.1 5.7 %collective-permute-done.18.refs_4_ = f32[384,128]{1,0:T(8,128)S(1)} collective-permute-done((f32[384,128]{1,0:T(8,128)S(1)}, f32[384,128]{1,0:T(8,128)S(1)}, u32[]{:S(2)}, u32[]{:S(2)}) %collective-permute-start.18) | collective-permute-done | bytes 196640 | tf_op jit(solution)/shard_map/ppermute | solution.py:357
  64.8 4.1 %collective-permute-done.19.refs_5_ = f32[384,128]{1,0:T(8,128)S(1)} collective-permute-done((f32[384,128]{1,0:T(8,128)S(1)}, f32[384,128]{1,0:T(8,128)S(1)}, u32[]{:S(2)}, u32[]{:S(2)}) %collective-permute-start.19) | collective-permute-done | bytes 196640 | tf_op jit(solution)/shard_map/ppermute | solution.py:357
  68.9 1.2 %shard_map.101 = (f32[256,128]{1,0:T(8,128)S(1)}, f32[256,128]{1,0:T(8,128)S(1)}, f32[64,256]{1,0:T(8,128)S(1)}) custom-call(s32[3]{0:T(128)S(1)} %pad_add_fusion.1.where, s32[1,2]{1,0:T(1,128)} %slot_range.9, s32[4,8]{1,0:T(4,128)S(1)} %pad_add_fusion.offs, f32[384,128]{1,0:T(8,128)S(1)} %collective-permute-done.14.refs_0_, ...), custom_call_target="tpu_custom_call" | custom-call | flops 2097152 | bytes 1900544 | tf_op jit(solution)/shard_map/pallas_call | solution.py:338
  70.1 1.6 %collective-permute-start.21 = (f32[64,256]{1,0:T(8,128)S(1)}, f32[64,256]{1,0:T(8,128)S(1)}, u32[]{:S(2)}, u32[]{:S(2)}) collective-permute-start(f32[64,256]{1,0:T(8,128)S(1)} %get-tuple-element.77), channel_id=1, source_target_pairs={{0,8},{8,0},{16,24},{24,16},{1,9},{9,1},{17,25},{25,17},{2,10},{10... | collective-permute-start | bytes 196616 | tf_op jit(solution)/shard_map/ppermute | solution.py:367
  71.7 1.6 %shard_map.102.own = f32[4,256,128]{2,1,0:T(8,128)S(1)} custom-call(s32[3]{0:T(128)S(1)} %pad_add_fusion.1.where, s32[1,2]{1,0:T(1,128)} %slot_range.9, s32[4,8]{1,0:T(4,128)S(1)} %pad_add_fusion.offs, f32[384,128]{1,0:T(8,128)S(1)} %collective-permute-done.14.refs_0_, f32[384,128]{1,0:T(8,128)S(1)} %collective-permute-done.15.refs_1_, ...), custom_call_target="tpu_custom_call" | custom-call | flops 4194304 | bytes 2097152 | tf_op jit(solution)/shard_map/pallas_call | solution.py:338
  73.3 1.1 %collective-permute-done.21 = f32[64,256]{1,0:T(8,128)S(1)} collective-permute-done((f32[64,256]{1,0:T(8,128)S(1)}, f32[64,256]{1,0:T(8,128)S(1)}, u32[]{:S(2)}, u32[]{:S(2)}) %collective-permute-start.21) | collective-permute-done | bytes 65568 | tf_op jit(solution)/shard_map/ppermute | solution.py:367
  74.4 3.5 %collective-permute-start.22 = (f32[256,128]{1,0:T(8,128)S(1)}, f32[256,128]{1,0:T(8,128)S(1)}, u32[]{:S(2)}, u32[]{:S(2)}) collective-permute-start(f32[256,128]{1,0:T(8,128)S(1)} %get-tuple-element.79), channel_id=1, source_target_pairs={{0,8},{8,16},{16,24},{1,9},{9,17},{17,25},{2,10},{10,18},{18,26},{... | collective-permute-start | bytes 393224 | tf_op jit(solution)/shard_map/ppermute | solution.py:446
  77.9 3.5 %collective-permute-start.24 = (f32[256,128]{1,0:T(8,128)S(1)}, f32[256,128]{1,0:T(8,128)S(1)}, u32[]{:S(2)}, u32[]{:S(2)}) collective-permute-start(f32[256,128]{1,0:T(8,128)S(1)} %get-tuple-element.81), channel_id=1, source_target_pairs={{0,8},{8,16},{16,24},{1,9},{9,17},{17,25},{2,10},{10,18},{18,26},{... | collective-permute-start | bytes 393224 | tf_op jit(solution)/shard_map/ppermute | solution.py:446
  81.5 0.6 shard_map.103
  82.3 1.6 %collective-permute-done.24.above = f32[256,128]{1,0:T(8,128)S(1)} collective-permute-done((f32[256,128]{1,0:T(8,128)S(1)}, f32[256,128]{1,0:T(8,128)S(1)}, u32[]{:S(2)}, u32[]{:S(2)}) %collective-permute-start.24) | collective-permute-done | bytes 131104 | tf_op jit(solution)/shard_map/ppermute | solution.py:446
  83.9 0.6 shard_map.104
  84.5 1.0 collective-permute-start.25
  85.4 1.5 %collective-permute-start.26 = (f32[256,128]{1,0:T(8,128)S(1)}, f32[256,128]{1,0:T(8,128)S(1)}, u32[]{:S(2)}, u32[]{:S(2)}) collective-permute-start(f32[256,128]{1,0:T(8,128)S(1)} %get-tuple-element.83), channel_id=1, source_target_pairs={{0,6},{2,4},{4,2},{6,0},{1,7},{3,5},{5,3},{7,1},{8,14},{10,12},{12... | collective-permute-start | bytes 393224 | tf_op jit(solution)/shard_map/ppermute | solution.py:357
  86.9 9.5 %all_gather.3.refs_4_ = f32[512,256]{1,0:T(8,128)S(1)} all-gather(f32[64,256]{1,0:T(8,128)S(1)} %add.7), channel_id=1, replica_groups=mesh['pair'=4,'half'=2,'col'=2,'core'=2] {'half','col','core'}, dimensions={0}, use_global_device_ids=true | all-gather | bytes 589824 | tf_op jit(solution)/shard_map/all_gather | solution.py:452
  96.4 1.5 %shard_map.105 = (f32[4,256,128]{2,1,0:T(8,128)}, f32[512,256]{1,0:T(8,128)}) custom-call(s32[3]{0:T(128)S(1)} %pad_add_fusion.1.where, f32[256,128]{1,0:T(8,128)S(1)} %collective-permute-done.23.refs_0_, f32[256,128]{1,0:T(8,128)S(1)} %collective-permute-done.25.refs_1_, f32[256,128]{1,0:T(8,128)S(1)} %collective-permute-done.26.refs_2_, ...), custom_call_target="tpu_custom_call" | custom-call | bytes 2097152 | tf_op jit(solution)/shard_map/pallas_call | solution.py:338
  (32 shorter events, 1.1 us)
Async XLA Ops:
  2.7 7.0 %collective-permute-start = (f32[264,128]{1,0:T(8,128)S(1)}, f32[264,128]{1,0:T(8,128)S(1)}, u32[]{:S(2)}, u32[]{:S(2)}) collective-permute-start(f32[264,128]{1,0:T(8,128)S(1)} %get-tuple-element.47), channel_id=1, source_target_pairs={{0,2},{2,0},{4,6},{6,4},{1,3},{3,1},{5,7},{7,5},{8,10},{10,8},{12,... | collective-permute-start | bytes 405512 | tf_op jit(solution)/shard_map/ppermute | solution.py:357
  5.7 7.9 %collective-permute-start.1 = (f32[264,128]{1,0:T(8,128)S(1)}, f32[264,128]{1,0:T(8,128)S(1)}, u32[]{:S(2)}, u32[]{:S(2)}) collective-permute-start(f32[264,128]{1,0:T(8,128)S(1)} %get-tuple-element.48), channel_id=1, source_target_pairs={{0,4},{2,6},{4,0},{6,2},{1,5},{3,7},{5,1},{7,3},{8,12},{10,14},{12... | collective-permute-start | bytes 405512 | tf_op jit(solution)/shard_map/ppermute | solution.py:357
  7.2 6.5 %collective-permute-start.2 = (f32[264,128]{1,0:T(8,128)S(1)}, f32[264,128]{1,0:T(8,128)S(1)}, u32[]{:S(2)}, u32[]{:S(2)}) collective-permute-start(f32[264,128]{1,0:T(8,128)S(1)} %get-tuple-element.49), channel_id=1, source_target_pairs={{0,6},{2,4},{4,2},{6,0},{1,7},{3,5},{5,3},{7,1},{8,14},{10,12},{12... | collective-permute-start | bytes 405512 | tf_op jit(solution)/shard_map/ppermute | solution.py:357
  13.9 1.2 %collective-permute-start.3 = (s32[4,4]{1,0:T(4,128)S(1)}, s32[4,4]{1,0:T(4,128)S(1)}, u32[]{:S(2)}, u32[]{:S(2)}) collective-permute-start(s32[4,4]{1,0:T(4,128)S(1)} %maximum_convert_fusion), channel_id=1, source_target_pairs={{0,1},{1,0},{2,3},{3,2},{4,5},{5,4},{6,7},{7,6},{8,9},{9,8},{10,11... | collective-permute-start | bytes 200 | tf_op jit(solution)/shard_map/ppermute | solution.py:395
  15.2 10.7 %collective-permute-start.6 = (f32[256,256]{1,0:T(8,128)S(1)}, f32[256,256]{1,0:T(8,128)S(1)}, u32[]{:S(2)}, u32[]{:S(2)}) collective-permute-start(f32[256,256]{1,0:T(8,128)S(1)} %get-tuple-element.53), channel_id=1, source_target_pairs={{0,4},{4,0},{1,5},{5,1},{2,6},{6,2},{3,7},{7,3},{8,12},{12,8},{9,1... | collective-permute-start | bytes 786440 | tf_op jit(solution)/shard_map/ppermute | solution.py:403
  17.8 8.1 %collective-permute-start.5 = (f32[256,128]{1,0:T(8,128)S(1)}, f32[256,128]{1,0:T(8,128)S(1)}, u32[]{:S(2)}, u32[]{:S(2)}) collective-permute-start(f32[256,128]{1,0:T(8,128)S(1)} %shard_map.97), channel_id=1, source_target_pairs={{8,0},{16,8},{24,16},{9,1},{17,9},{25,17},{10,2},{18,10},{26,18},{... | collective-permute-start | bytes 393224 | tf_op jit(solution)/shard_map/ppermute | solution.py:401
  19.1 8.7 %collective-permute-start.4 = (f32[256,128]{1,0:T(8,128)S(1)}, f32[256,128]{1,0:T(8,128)S(1)}, u32[]{:S(2)}, u32[]{:S(2)}) collective-permute-start(f32[256,128]{1,0:T(8,128)S(1)} %shard_map.96), channel_id=1, source_target_pairs={{8,0},{16,8},{24,16},{9,1},{17,9},{25,17},{10,2},{18,10},{26,18},{... | collective-permute-start | bytes 393224 | tf_op jit(solution)/shard_map/ppermute | solution.py:401
  29.3 5.4 %collective-permute-start.7 = (f32[256,128]{1,0:T(8,128)S(1)}, f32[256,128]{1,0:T(8,128)S(1)}, u32[]{:S(2)}, u32[]{:S(2)}) collective-permute-start(f32[256,128]{1,0:T(8,128)S(1)} %get-tuple-element.55), channel_id=1, source_target_pairs={{0,4},{1,5},{2,6},{3,7},{4,0},{5,1},{6,2},{7,3},{8,12},{9,13},{10,... | collective-permute-start | bytes 393224 | tf_op jit(solution)/shard_map/ppermute | solution.py:357
  29.9 5.4 %collective-permute-start.8 = (f32[256,128]{1,0:T(8,128)S(1)}, f32[256,128]{1,0:T(8,128)S(1)}, u32[]{:S(2)}, u32[]{:S(2)}) collective-permute-start(f32[256,128]{1,0:T(8,128)S(1)} %get-tuple-element.56), channel_id=1, source_target_pairs={{0,2},{1,3},{2,0},{3,1},{4,6},{5,7},{6,4},{7,5},{8,10},{9,11},{10,... | collective-permute-start | bytes 393224 | tf_op jit(solution)/shard_map/ppermute | solution.py:357
  31.0 7.8 %collective-permute-start.9 = (f32[256,128]{1,0:T(8,128)S(1)}, f32[256,128]{1,0:T(8,128)S(1)}, u32[]{:S(2)}, u32[]{:S(2)}) collective-permute-start(f32[256,128]{1,0:T(8,128)S(1)} %get-tuple-element.57), channel_id=1, source_target_pairs={{0,5},{1,4},{2,7},{3,6},{4,1},{5,0},{6,3},{7,2},{8,13},{9,12},{10,... | collective-permute-start | bytes 393224 | tf_op jit(solution)/shard_map/ppermute | solution.py:357
  31.0 7.8 %collective-permute-start.10 = (f32[256,128]{1,0:T(8,128)S(1)}, f32[256,128]{1,0:T(8,128)S(1)}, u32[]{:S(2)}, u32[]{:S(2)}) collective-permute-start(f32[256,128]{1,0:T(8,128)S(1)} %get-tuple-element.58), channel_id=1, source_target_pairs={{0,3},{1,2},{2,1},{3,0},{4,7},{5,6},{6,5},{7,4},{8,11},{9,10},{10,... | collective-permute-start | bytes 393224 | tf_op jit(solution)/shard_map/ppermute | solution.py:357
  33.1 9.6 %collective-permute-start.11 = (f32[256,128]{1,0:T(8,128)S(1)}, f32[256,128]{1,0:T(8,128)S(1)}, u32[]{:S(2)}, u32[]{:S(2)}) collective-permute-start(f32[256,128]{1,0:T(8,128)S(1)} %get-tuple-element.59), channel_id=1, source_target_pairs={{0,6},{1,7},{2,4},{3,5},{4,2},{5,3},{6,0},{7,1},{8,14},{9,15},{10,... | collective-permute-start | bytes 393224 | tf_op jit(solution)/shard_map/ppermute | solution.py:357
  34.7 8.1 %collective-permute-start.12 = (f32[256,128]{1,0:T(8,128)S(1)}, f32[256,128]{1,0:T(8,128)S(1)}, u32[]{:S(2)}, u32[]{:S(2)}) collective-permute-start(f32[256,128]{1,0:T(8,128)S(1)} %get-tuple-element.60), channel_id=1, source_target_pairs={{0,7},{1,6},{2,5},{3,4},{4,3},{5,2},{6,1},{7,0},{8,15},{9,14},{10,... | collective-permute-start | bytes 393224 | tf_op jit(solution)/shard_map/ppermute | solution.py:357
  35.3 7.5 %copy-start = (f32[2,136,128]{2,1,0:T(8,128)S(1)}, f32[2,136,128]{2,1,0:T(8,128)}, u32[]{:S(2)}) copy-start(f32[2,136,128]{2,1,0:T(8,128)} %constant.19.clone.refs_11_) | copy-start | bytes 417796
  35.3 7.5 %collective-permute-start.13 = (f32[256,128]{1,0:T(8,128)S(1)}, f32[256,128]{1,0:T(8,128)S(1)}, u32[]{:S(2)}, u32[]{:S(2)}) collective-permute-start(f32[256,128]{1,0:T(8,128)S(1)} %get-tuple-element.61), channel_id=1, source_target_pairs={{0,1},{1,0},{2,3},{3,2},{4,5},{5,4},{6,7},{7,6},{8,9},{9,8},{10,11... | collective-permute-start | bytes 393224 | tf_op jit(solution)/shard_map/ppermute | solution.py:357
  47.1 7.6 %collective-permute-start.14 = (f32[384,128]{1,0:T(8,128)S(1)}, f32[384,128]{1,0:T(8,128)S(1)}, u32[]{:S(2)}, u32[]{:S(2)}) collective-permute-start(f32[384,128]{1,0:T(8,128)S(1)} %get-tuple-element.67), channel_id=1, source_target_pairs={{0,4},{1,5},{2,6},{3,7},{4,0},{5,1},{6,2},{7,3},{8,12},{9,13},{10,... | collective-permute-start | bytes 589832 | tf_op jit(solution)/shard_map/ppermute | solution.py:357
  48.6 7.8 %collective-permute-start.15 = (f32[384,128]{1,0:T(8,128)S(1)}, f32[384,128]{1,0:T(8,128)S(1)}, u32[]{:S(2)}, u32[]{:S(2)}) collective-permute-start(f32[384,128]{1,0:T(8,128)S(1)} %get-tuple-element.68), channel_id=1, source_target_pairs={{0,2},{1,3},{2,0},{3,1},{4,6},{5,7},{6,4},{7,5},{8,10},{9,11},{10,... | collective-permute-start | bytes 589832 | tf_op jit(solution)/shard_map/ppermute | solution.py:357
  49.1 10.1 %collective-permute-start.16 = (f32[384,128]{1,0:T(8,128)S(1)}, f32[384,128]{1,0:T(8,128)S(1)}, u32[]{:S(2)}, u32[]{:S(2)}) collective-permute-start(f32[384,128]{1,0:T(8,128)S(1)} %get-tuple-element.69), channel_id=1, source_target_pairs={{0,5},{1,4},{2,7},{3,6},{4,1},{5,0},{6,3},{7,2},{8,13},{9,12},{10,... | collective-permute-start | bytes 589832 | tf_op jit(solution)/shard_map/ppermute | solution.py:357
  50.0 9.1 %collective-permute-start.17 = (f32[384,128]{1,0:T(8,128)S(1)}, f32[384,128]{1,0:T(8,128)S(1)}, u32[]{:S(2)}, u32[]{:S(2)}) collective-permute-start(f32[384,128]{1,0:T(8,128)S(1)} %get-tuple-element.70), channel_id=1, source_target_pairs={{0,3},{1,2},{2,1},{3,0},{4,7},{5,6},{6,5},{7,4},{8,11},{9,10},{10,... | collective-permute-start | bytes 589832 | tf_op jit(solution)/shard_map/ppermute | solution.py:357
  50.9 13.9 %collective-permute-start.18 = (f32[384,128]{1,0:T(8,128)S(1)}, f32[384,128]{1,0:T(8,128)S(1)}, u32[]{:S(2)}, u32[]{:S(2)}) collective-permute-start(f32[384,128]{1,0:T(8,128)S(1)} %get-tuple-element.71), channel_id=1, source_target_pairs={{0,6},{1,7},{2,4},{3,5},{4,2},{5,3},{6,0},{7,1},{8,14},{9,15},{10,... | collective-permute-start | bytes 589832 | tf_op jit(solution)/shard_map/ppermute | solution.py:357
  54.7 14.2 %collective-permute-start.19 = (f32[384,128]{1,0:T(8,128)S(1)}, f32[384,128]{1,0:T(8,128)S(1)}, u32[]{:S(2)}, u32[]{:S(2)}) collective-permute-start(f32[384,128]{1,0:T(8,128)S(1)} %get-tuple-element.72), channel_id=1, source_target_pairs={{0,7},{1,6},{2,5},{3,4},{4,3},{5,2},{6,1},{7,0},{8,15},{9,14},{10,... | collective-permute-start | bytes 589832 | tf_op jit(solution)/shard_map/ppermute | solution.py:357
  56.4 12.6 %collective-permute-start.20 = (f32[384,128]{1,0:T(8,128)S(1)}, f32[384,128]{1,0:T(8,128)S(1)}, u32[]{:S(2)}, u32[]{:S(2)}) collective-permute-start(f32[384,128]{1,0:T(8,128)S(1)} %get-tuple-element.73), channel_id=1, source_target_pairs={{0,1},{1,0},{2,3},{3,2},{4,5},{5,4},{6,7},{7,6},{8,9},{9,8},{10,11... | collective-permute-start | bytes 589832 | tf_op jit(solution)/shard_map/ppermute | solution.py:357
  70.1 4.3 %collective-permute-start.21 = (f32[64,256]{1,0:T(8,128)S(1)}, f32[64,256]{1,0:T(8,128)S(1)}, u32[]{:S(2)}, u32[]{:S(2)}) collective-permute-start(f32[64,256]{1,0:T(8,128)S(1)} %get-tuple-element.77), channel_id=1, source_target_pairs={{0,8},{8,0},{16,24},{24,16},{1,9},{9,1},{17,25},{25,17},{2,10},{10... | collective-permute-start | bytes 196616 | tf_op jit(solution)/shard_map/ppermute | solution.py:367
  74.4 7.1 %collective-permute-start.22 = (f32[256,128]{1,0:T(8,128)S(1)}, f32[256,128]{1,0:T(8,128)S(1)}, u32[]{:S(2)}, u32[]{:S(2)}) collective-permute-start(f32[256,128]{1,0:T(8,128)S(1)} %get-tuple-element.79), channel_id=1, source_target_pairs={{0,8},{8,16},{16,24},{1,9},{9,17},{17,25},{2,10},{10,18},{18,26},{... | collective-permute-start | bytes 393224 | tf_op jit(solution)/shard_map/ppermute | solution.py:446
  77.9 6.0 %collective-permute-start.24 = (f32[256,128]{1,0:T(8,128)S(1)}, f32[256,128]{1,0:T(8,128)S(1)}, u32[]{:S(2)}, u32[]{:S(2)}) collective-permute-start(f32[256,128]{1,0:T(8,128)S(1)} %get-tuple-element.81), channel_id=1, source_target_pairs={{0,8},{8,16},{16,24},{1,9},{9,17},{17,25},{2,10},{10,18},{18,26},{... | collective-permute-start | bytes 393224 | tf_op jit(solution)/shard_map/ppermute | solution.py:446
  81.4 5.5 %collective-permute-start.27 = (f32[64,256]{1,0:T(8,128)S(1)}, f32[64,256]{1,0:T(8,128)S(1)}, u32[]{:S(2)}, u32[]{:S(2)}) collective-permute-start(f32[64,256]{1,0:T(8,128)S(1)} %add.6), channel_id=1, source_target_pairs={{0,16},{8,24},{16,0},{24,8},{1,17},{9,25},{17,1},{25,9},{2,18},{10... | collective-permute-start | bytes 196616 | tf_op jit(solution)/shard_map/ppermute | solution.py:367
  82.1 14.3 %collective-permute-start.23 = (f32[256,128]{1,0:T(8,128)S(1)}, f32[256,128]{1,0:T(8,128)S(1)}, u32[]{:S(2)}, u32[]{:S(2)}) collective-permute-start(f32[256,128]{1,0:T(8,128)S(1)} %get-tuple-element.80), channel_id=1, source_target_pairs={{0,4},{2,6},{4,0},{6,2},{1,5},{3,7},{5,1},{7,3},{8,12},{10,14},{12... | collective-permute-start | bytes 393224 | tf_op jit(solution)/shard_map/ppermute | solution.py:357
  84.5 11.9 %collective-permute-start.25 = (f32[256,128]{1,0:T(8,128)S(1)}, f32[256,128]{1,0:T(8,128)S(1)}, u32[]{:S(2)}, u32[]{:S(2)}) collective-permute-start(f32[256,128]{1,0:T(8,128)S(1)} %get-tuple-element.82), channel_id=1, source_target_pairs={{0,2},{2,0},{4,6},{6,4},{1,3},{3,1},{5,7},{7,5},{8,10},{10,8},{12,... | collective-permute-start | bytes 393224 | tf_op jit(solution)/shard_map/ppermute | solution.py:357
  85.4 11.0 %collective-permute-start.26 = (f32[256,128]{1,0:T(8,128)S(1)}, f32[256,128]{1,0:T(8,128)S(1)}, u32[]{:S(2)}, u32[]{:S(2)}) collective-permute-start(f32[256,128]{1,0:T(8,128)S(1)} %get-tuple-element.83), channel_id=1, source_target_pairs={{0,6},{2,4},{4,2},{6,0},{1,7},{3,5},{5,3},{7,1},{8,14},{10,12},{12... | collective-permute-start | bytes 393224 | tf_op jit(solution)/shard_map/ppermute | solution.py:357

commit v12 on v10

--- a/solution.py
+++ b/solution.py
@@ -298,11 +298,11 @@
 
 
 def add_below_kernel(where, slot_range, offs, *refs):
-    parts, (below, probe_band) = refs[:8], refs[8:]
-    rows, cols = below.shape[1:]
+    parts, (below0, below1, probe_band) = refs[:8], refs[8:]
+    rows, cols = below0.shape
     sums = add_parts(where, slot_range, offs, parts, 2, rows, cols)
-    for side in range(2):
-        below[jnp.bitwise_xor(where[1], side)] = sums[side]
+    below0[...] = jnp.where(where[1] == 0, sums[0], sums[1])
+    below1[...] = jnp.where(where[1] == 0, sums[1], sums[0])
     total = parts[0][rows:]
     for part in parts[1:]:
         total = total + part[rows:]
@@ -312,24 +312,22 @@
 
 
 def add_own_kernel(where, slot_range, offs, *refs):
-    parts, own = refs[:8], refs[8]
+    parts, outs, own = refs[:8], refs[8:12], refs[12]
     rows, cols = own.shape[1:]
     for strip in range(2):
         own[2 * strip], own[2 * strip + 1] = add_parts(where, slot_range, offs, parts, strip, rows, cols)
-
-
-def top_kernel(where, own, above, *outs):
+    for turn, out in zip(FOUR, outs):
+        out[...] = own[jnp.bitwise_xor(2 * where[0] + where[1], turn)]
+
+
+def join_kernel(where, *refs):
+    probe, out, probe_out, sums, sems = refs[8:]
+    copies = fetch([(probe, probe_out)], sems)
     mine = 2 * where[0] + where[1]
-    for turn, out in zip(FOUR, outs):
-        extra = jnp.where(where[0] == turn // 2, above[turn % 2], 0.0)
-        out[...] = own[jnp.bitwise_xor(mine, turn)] + extra
-
-
-def join_kernel(where, *refs):
-    probe, out, probe_out, sems = refs[4:]
-    mine = 2 * where[0] + where[1]
-    pairs = [(ref, out.at[jnp.bitwise_xor(mine, turn)]) for turn, ref in zip(FOUR, refs)]
-    for copy in fetch([(probe, probe_out), *pairs], sems):
+    for at, turn in enumerate(FOUR):
+        sums[turn] = refs[at][...] + refs[4 + at][...]
+        copies += fetch([(sums.at[turn], out.at[jnp.bitwise_xor(mine, turn)])], sems.at[pl.ds(1 + turn, 1)])
+    for copy in copies:
         copy.wait()
 
 
@@ -379,6 +377,11 @@
     return value
 
 
+def down_pairs(pairs, half, turn):
+    places = [(pair, col) for pair in range(pairs - 1) for col in range(2)]
+    return [(4 * pair + 2 * half + col, 4 * (pair + 1) + (col ^ turn)) for pair, col in places]
+
+
 def local(object_field, probe, offsets, slot_range, measured):
     width = probe.shape[-1]
     planes, rows, cols = 4, object_field.shape[2], object_field.shape[3]
@@ -434,27 +437,28 @@
         [(8, rows, cols), (8, rows + 2 * band, cols)],
     )
     got = deal(grad, PLANE)
-    lower_sums, probe_band = call(
+    *lower_sums, probe_band = call(
         add_below_kernel,
-        [shape(2, rows, cols), shape(band, width)],
+        [shape(rows, cols)] * 2 + [shape(band, width)],
         scalars,
         got,
         32 * rows * width,
     )
     probe_band = sum_over(probe_band, "pair", pairs, 0)
-    (sums,) = call(add_own_kernel, [shape(planes, rows, cols)], scalars, got, 64 * rows * width)
-    lower_sums, sums, probe_band = lax.optimization_barrier((lower_sums, sums, probe_band))
-    above = lax.ppermute(lower_sums, "pair", [(k, k + 1) for k in range(pairs - 1)])
-    sums = call(top_kernel, [shape(rows, cols)] * 4, (where,), (sums, above), planes * rows * cols)
+    sums = call(add_own_kernel, [shape(rows, cols)] * 4, scalars, got, 64 * rows * width, [(planes, rows, cols)])
     sums = deal(sums, PLANE[:2])
+    above = []
+    for turn in FOUR:
+        above.append(lax.ppermute(lower_sums[turn % 2], ("pair", *PLANE[:2]), down_pairs(pairs, turn // 2, turn % 2)))
     probe_band = sum_over(probe_band, "pair", pairs, 1)
     probe_grad = lax.all_gather(probe_band, PLANE, axis=0, tiled=True)
     object_grad, probe_grad = call(
         join_kernel,
         [(shape(planes, rows, cols), HBM), (shape(*probe_grad.shape), HBM)],
         (where,),
-        [(x, ANY) for x in (*sums, probe_grad)],
-        0,
+        (*sums, *above, (probe_grad, ANY)),
+        planes * rows * cols,
+        [(planes, rows, cols)],
         copies=5,
     )
     return (object_grad.reshape(object_field.shape), probe_grad.reshape(probe.shape))

time: 97.8 us -> 98.1 us (level); the launches traced: 96.1 us -> 97.8 us
  starting transfers between devices: 32.4 us -> 38 us
  waiting for transfers between devices: 37.3 us -> 32.9 us
    ppermute x1 -> x4, waiting for transfers between devices: 3.46 us -> 0.01 us  [local(): lax.ppermute(lower_sums[turn % 2], ('pair', *PLANE[:2]), down_pairs(pairs...]
    ppermute x1 -> x4, starting transfers between devices: 3.66 us -> 6.65 us  [local(): lax.ppermute(lower_sums[turn % 2], ('pair', *PLANE[:2]), down_pairs(pairs...]
    ppermute x20, starting transfers between devices: 20.8 us -> 23.4 us  [deal(): lax.ppermute(value, axes, [(k, k ^ turn) for k in range(count)])]
    pallas_call x9 -> x8, Pallas kernels: 15.8 us -> 15.4 us  [call(): pl.pallas_call(kernel, out_shape=[x for x, unused in outs], in_specs=[SME...]
  transfers between devices with their start and end apart: 26 -> 29, of which waited for: 15 -> 14; matrix products, arithmetic and copies ran while one was open for 1% -> 1% of each run, Pallas kernels for 5% -> 5%
where the time goes in v12:
time: 98.1 us; the launch traced here: 97.8 us
  starting transfers between devices  38 us (39%)
  waiting for transfers between devices  32.9 us (34%)
  Pallas kernels  15.4 us (16%)
  blocking collectives  10.1 us (10%)
    ppermute x20, waiting for transfers between devices, deal(): lax.ppermute(value, axes, [(k, k ^ turn) for k in range(count)])  25.7 us
    ppermute x20, starting transfers between devices, deal(): lax.ppermute(value, axes, [(k, k ^ turn) for k in range(count)])  23.4 us
    pallas_call x8, Pallas kernels, call(): pl.pallas_call(kernel, out_shape=[x for x, unused in outs], in_specs=[SME...  15.4 us
    all_gather x1, blocking collectives, local(): probe_grad = lax.all_gather(probe_band, PLANE, axis=0, tiled=True)  10.1 us
    ppermute x4, starting transfers between devices, local(): lax.ppermute(lower_sums[turn % 2], ('pair', *PLANE[:2]), down_pairs(pairs...  6.65 us
    ppermute x1, waiting for transfers between devices, local(): below = lax.ppermute(lowest, 'pair', [(k, k - 1) for k in range(1, pairs)])  6.01 us
    ppermute x2, starting transfers between devices, sum_over(): lax.ppermute(value, axis, [(k, k ^ step) for k in range(size)])  4.57 us
  transfers between devices with their start and end apart: 29, of which 14 were waited for; matrix products, arithmetic and copies ran while one was open for 1% of the time, Pallas kernels for 5%

profile of v12, /device:TPU:0, one launch (start us, length us, event | category | flops | bytes accessed | tf_op | source)
XLA Modules:
  0.0 97.8 jit_solution(16944979978432366825)
XLA Ops:
  0.6 0.5 collective-permute-start
  1.2 1.0 collective-permute-done.sibling
  2.2 2.0 %shard_map.95 = (f32[264,128]{1,0:T(8,128)S(1)}, f32[264,128]{1,0:T(8,128)S(1)}, f32[264,128]{1,0:T(8,128)S(1)}, f32[264,128]{1,0:T(8,128)S(1)}, f32[256,256]{1,0:T(8,128)S(1)}) custom-call(s32[3]{0:T(128)S(1)} %pad_add_fusion.where, s32[1,2,2]{2,1,0:T(2,128)} %offsets.1, s32[1,2,2]{2,1,0:T(2,128)S(1)} %collective-permute-done.sibling, ...), custom_call_target="tpu_custom_call" | custom-call | bytes 1851392 | tf_op jit(solution)/shard_map/pallas_call | solution.py:344
  4.2 2.9 %collective-permute-start.1 = (f32[264,128]{1,0:T(8,128)S(1)}, f32[264,128]{1,0:T(8,128)S(1)}, u32[]{:S(2)}, u32[]{:S(2)}) collective-permute-start(f32[264,128]{1,0:T(8,128)S(1)} %get-tuple-element.40), channel_id=1, source_target_pairs={{0,2},{2,0},{4,6},{6,4},{1,3},{3,1},{5,7},{7,5},{8,10},{10,8},{12,... | collective-permute-start | bytes 405512 | tf_op jit(solution)/shard_map/ppermute | solution.py:363
  7.0 1.5 %collective-permute-start.2 = (f32[264,128]{1,0:T(8,128)S(1)}, f32[264,128]{1,0:T(8,128)S(1)}, u32[]{:S(2)}, u32[]{:S(2)}) collective-permute-start(f32[264,128]{1,0:T(8,128)S(1)} %get-tuple-element.41), channel_id=1, source_target_pairs={{0,4},{2,6},{4,0},{6,2},{1,5},{3,7},{5,1},{7,3},{8,12},{10,14},{12... | collective-permute-start | bytes 405512 | tf_op jit(solution)/shard_map/ppermute | solution.py:363
  8.6 2.6 %collective-permute-done.1.refs_1_ = f32[264,128]{1,0:T(8,128)S(1)} collective-permute-done((f32[264,128]{1,0:T(8,128)S(1)}, f32[264,128]{1,0:T(8,128)S(1)}, u32[]{:S(2)}, u32[]{:S(2)}) %collective-permute-start.1) | collective-permute-done | bytes 135200 | tf_op jit(solution)/shard_map/ppermute | solution.py:363
  11.1 4.2 %collective-permute-done.2.refs_0_ = f32[264,128]{1,0:T(8,128)S(1)} collective-permute-done((f32[264,128]{1,0:T(8,128)S(1)}, f32[264,128]{1,0:T(8,128)S(1)}, u32[]{:S(2)}, u32[]{:S(2)}) %collective-permute-start.2) | collective-permute-done | bytes 135200 | tf_op jit(solution)/shard_map/ppermute | solution.py:363
  15.3 0.6 shard_map.96
  15.9 1.3 %collective-permute-start.4 = (f32[2,256,128]{2,1,0:T(8,128)S(1)}, f32[2,256,128]{2,1,0:T(8,128)S(1)}, u32[]{:S(2)}, u32[]{:S(2)}) collective-permute-start(f32[2,256,128]{2,1,0:T(8,128)S(1)} %shard_map.96), channel_id=1, source_target_pairs={{8,0},{16,8},{24,16},{9,1},{17,9},{25,17},{10,2},{18,10},{26,18},{... | collective-permute-start | bytes 786440 | tf_op jit(solution)/shard_map/ppermute | solution.py:407
  17.2 1.6 %collective-permute-start.5 = (f32[256,256]{1,0:T(8,128)S(1)}, f32[256,256]{1,0:T(8,128)S(1)}, u32[]{:S(2)}, u32[]{:S(2)}) collective-permute-start(f32[256,256]{1,0:T(8,128)S(1)} %get-tuple-element.45), channel_id=1, source_target_pairs={{0,4},{4,0},{1,5},{5,1},{2,6},{6,2},{3,7},{7,3},{8,12},{12,8},{9,1... | collective-permute-start | bytes 786440 | tf_op jit(solution)/shard_map/ppermute | solution.py:408
  19.0 6.0 %collective-permute-done.4.refs_4_ = f32[2,256,128]{2,1,0:T(8,128)S(1)} collective-permute-done((f32[2,256,128]{2,1,0:T(8,128)S(1)}, f32[2,256,128]{2,1,0:T(8,128)S(1)}, u32[]{:S(2)}, u32[]{:S(2)}) %collective-permute-start.4) | collective-permute-done | bytes 262176 | tf_op jit(solution)/shard_map/ppermute | solution.py:407
  25.0 1.4 %shard_map.97 = (f32[256,128]{1,0:T(8,128)S(1)}, f32[256,128]{1,0:T(8,128)S(1)}, f32[256,128]{1,0:T(8,128)S(1)}, f32[256,128]{1,0:T(8,128)S(1)}, f32[256,128]{1,...) custom-call(s32[3]{0:T(128)S(1)} %pad_add_fusion.where, ...), custom_call_target="tpu_custom_call" | custom-call | flops 2097152 | bytes 1851392 | tf_op jit(solution)/shard_map/pallas_call | solution.py:344
  26.4 1.6 %collective-permute-start.6 = (f32[256,128]{1,0:T(8,128)S(1)}, f32[256,128]{1,0:T(8,128)S(1)}, u32[]{:S(2)}, u32[]{:S(2)}) collective-permute-start(f32[256,128]{1,0:T(8,128)S(1)} %get-tuple-element.47), channel_id=1, source_target_pairs={{0,4},{1,5},{2,6},{3,7},{4,0},{5,1},{6,2},{7,3},{8,12},{9,13},{10,... | collective-permute-start | bytes 393224 | tf_op jit(solution)/shard_map/ppermute | solution.py:363
  28.1 0.6 collective-permute-start.7
  28.9 1.6 %collective-permute-start.9 = (f32[256,128]{1,0:T(8,128)S(1)}, f32[256,128]{1,0:T(8,128)S(1)}, u32[]{:S(2)}, u32[]{:S(2)}) collective-permute-start(f32[256,128]{1,0:T(8,128)S(1)} %get-tuple-element.50), channel_id=1, source_target_pairs={{0,3},{1,2},{2,1},{3,0},{4,7},{5,6},{6,5},{7,4},{8,11},{9,10},{10,... | collective-permute-start | bytes 393224 | tf_op jit(solution)/shard_map/ppermute | solution.py:363
  30.6 1.6 %collective-permute-start.10 = (f32[256,128]{1,0:T(8,128)S(1)}, f32[256,128]{1,0:T(8,128)S(1)}, u32[]{:S(2)}, u32[]{:S(2)}) collective-permute-start(f32[256,128]{1,0:T(8,128)S(1)} %get-tuple-element.51), channel_id=1, source_target_pairs={{0,6},{1,7},{2,4},{3,5},{4,2},{5,3},{6,0},{7,1},{8,14},{9,15},{10,... | collective-permute-start | bytes 393224 | tf_op jit(solution)/shard_map/ppermute | solution.py:363
  32.1 0.7 collective-permute-start.11
  32.8 1.3 %collective-permute-done.7.refs_1_ = f32[256,128]{1,0:T(8,128)S(1)} collective-permute-done((f32[256,128]{1,0:T(8,128)S(1)}, f32[256,128]{1,0:T(8,128)S(1)}, u32[]{:S(2)}, u32[]{:S(2)}) %collective-permute-start.7) | collective-permute-done | bytes 131104 | tf_op jit(solution)/shard_map/ppermute | solution.py:363
  34.2 2.7 %shard_map.98 = (f32[2,256,256]{2,1,0:T(8,128)S(1)}, f32[256,256]{1,0:T(8,128)S(1)}, bf16[6,512,256]{2,1,0:T(8,128)(2,1)S(1)}) custom-call(s32[3]{0:T(128)S(1)} %pad_add_fusion.where, s32[1,2]{1,0:T(1,128)} %slot_range.9, s32[4,8]{1,0:T(4,128)S(1)} %maximum_convert_fusion.offs, f32[256,256]{1,0:T(8,128)S(1)} %collective-permute-done.5.taken, ...), custom_call_target="tpu_custom_call" | custom-call | flops 201326592 | bytes 5505024 | tf_op jit(solution)/shard_map/pallas_call | solution.py:344
  36.9 2.3 %collective-permute-done.10.refs_4_ = f32[256,128]{1,0:T(8,128)S(1)} collective-permute-done((f32[256,128]{1,0:T(8,128)S(1)}, f32[256,128]{1,0:T(8,128)S(1)}, u32[]{:S(2)}, u32[]{:S(2)}) %collective-permute-start.10) | collective-permute-done | bytes 131104 | tf_op jit(solution)/shard_map/ppermute | solution.py:363
  39.3 1.4 %collective-permute-done.11.refs_5_ = f32[256,128]{1,0:T(8,128)S(1)} collective-permute-done((f32[256,128]{1,0:T(8,128)S(1)}, f32[256,128]{1,0:T(8,128)S(1)}, u32[]{:S(2)}, u32[]{:S(2)}) %collective-permute-start.11) | collective-permute-done | bytes 131104 | tf_op jit(solution)/shard_map/ppermute | solution.py:363
  40.7 4.3 %shard_map.99 = (f32[384,128]{1,0:T(8,128)S(1)}, f32[384,128]{1,0:T(8,128)S(1)}, f32[384,128]{1,0:T(8,128)S(1)}, f32[384,128]{1,0:T(8,128)S(1)}, f32[384,128]{1,...) custom-call(s32[3]{0:T(128)S(1)} %pad_add_fusion.where, ...), custom_call_target="tpu_custom_call" | custom-call | flops 1610612736 | bytes 5120000 | tf_op jit(solution)/shard_map/pallas_call | solution.py:344
  45.0 1.2 %collective-permute-start.13 = (f32[384,128]{1,0:T(8,128)S(1)}, f32[384,128]{1,0:T(8,128)S(1)}, u32[]{:S(2)}, u32[]{:S(2)}) collective-permute-start(f32[384,128]{1,0:T(8,128)S(1)} %get-tuple-element.59), channel_id=1, source_target_pairs={{0,4},{1,5},{2,6},{3,7},{4,0},{5,1},{6,2},{7,3},{8,12},{9,13},{10,... | collective-permute-start | bytes 589832 | tf_op jit(solution)/shard_map/ppermute | solution.py:363
  46.2 1.2 %collective-permute-start.14 = (f32[384,128]{1,0:T(8,128)S(1)}, f32[384,128]{1,0:T(8,128)S(1)}, u32[]{:S(2)}, u32[]{:S(2)}) collective-permute-start(f32[384,128]{1,0:T(8,128)S(1)} %get-tuple-element.60), channel_id=1, source_target_pairs={{0,2},{1,3},{2,0},{3,1},{4,6},{5,7},{6,4},{7,5},{8,10},{9,11},{10,... | collective-permute-start | bytes 589832 | tf_op jit(solution)/shard_map/ppermute | solution.py:363
  47.4 0.8 collective-permute-start.15
  48.2 0.6 collective-permute-start.16
  48.8 1.8 %collective-permute-start.17 = (f32[384,128]{1,0:T(8,128)S(1)}, f32[384,128]{1,0:T(8,128)S(1)}, u32[]{:S(2)}, u32[]{:S(2)}) collective-permute-start(f32[384,128]{1,0:T(8,128)S(1)} %get-tuple-element.63), channel_id=1, source_target_pairs={{0,6},{1,7},{2,4},{3,5},{4,2},{5,3},{6,0},{7,1},{8,14},{9,15},{10,... | collective-permute-start | bytes 589832 | tf_op jit(solution)/shard_map/ppermute | solution.py:363
  50.6 2.1 %collective-permute-done.13.refs_0_ = f32[384,128]{1,0:T(8,128)S(1)} collective-permute-done((f32[384,128]{1,0:T(8,128)S(1)}, f32[384,128]{1,0:T(8,128)S(1)}, u32[]{:S(2)}, u32[]{:S(2)}) %collective-permute-start.13) | collective-permute-done | bytes 196640 | tf_op jit(solution)/shard_map/ppermute | solution.py:363
  52.7 0.3 collective-permute-start.18
  53.0 0.9 collective-permute-done.14.refs_1_
  54.0 0.7 collective-permute-start.19
  54.7 1.5 %collective-permute-done.15.refs_2_ = f32[384,128]{1,0:T(8,128)S(1)} collective-permute-done((f32[384,128]{1,0:T(8,128)S(1)}, f32[384,128]{1,0:T(8,128)S(1)}, u32[]{:S(2)}, u32[]{:S(2)}) %collective-permute-start.15) | collective-permute-done | bytes 196640 | tf_op jit(solution)/shard_map/ppermute | solution.py:363
  56.2 1.3 %collective-permute-done.16.refs_3_ = f32[384,128]{1,0:T(8,128)S(1)} collective-permute-done((f32[384,128]{1,0:T(8,128)S(1)}, f32[384,128]{1,0:T(8,128)S(1)}, u32[]{:S(2)}, u32[]{:S(2)}) %collective-permute-start.16) | collective-permute-done | bytes 196640 | tf_op jit(solution)/shard_map/ppermute | solution.py:363
  57.5 5.1 %collective-permute-done.17.refs_4_ = f32[384,128]{1,0:T(8,128)S(1)} collective-permute-done((f32[384,128]{1,0:T(8,128)S(1)}, f32[384,128]{1,0:T(8,128)S(1)}, u32[]{:S(2)}, u32[]{:S(2)}) %collective-permute-start.17) | collective-permute-done | bytes 196640 | tf_op jit(solution)/shard_map/ppermute | solution.py:363
  62.7 2.8 %collective-permute-done.18.refs_5_ = f32[384,128]{1,0:T(8,128)S(1)} collective-permute-done((f32[384,128]{1,0:T(8,128)S(1)}, f32[384,128]{1,0:T(8,128)S(1)}, u32[]{:S(2)}, u32[]{:S(2)}) %collective-permute-start.18) | collective-permute-done | bytes 196640 | tf_op jit(solution)/shard_map/ppermute | solution.py:363
  65.5 1.2 %shard_map.101 = (f32[256,128]{1,0:T(8,128)S(1)}, f32[256,128]{1,0:T(8,128)S(1)}, f32[64,256]{1,0:T(8,128)S(1)}) custom-call(s32[3]{0:T(128)S(1)} %pad_add_fusion.where, s32[1,2]{1,0:T(1,128)} %slot_range.9, s32[4,8]{1,0:T(4,128)S(1)} %maximum_convert_fusion.offs, f32[384,128]{1,0:T(8,128)S(1)} %collective-permute-done.13.refs_0_, ...), custom_call_target="tpu_custom_call" | custom-call | flops 2097152 | bytes 1900544 | tf_op jit(solution)/shard_map/pallas_call | solution.py:344
  66.7 1.9 %collective-permute-start.27 = (f32[64,256]{1,0:T(8,128)S(1)}, f32[64,256]{1,0:T(8,128)S(1)}, u32[]{:S(2)}, u32[]{:S(2)}) collective-permute-start(f32[64,256]{1,0:T(8,128)S(1)} %get-tuple-element.73), channel_id=1, source_target_pairs={{0,8},{8,0},{16,24},{24,16},{1,9},{9,1},{17,25},{25,17},{2,10},{10... | collective-permute-start | bytes 196616 | tf_op jit(solution)/shard_map/ppermute | solution.py:373
  68.6 1.7 %shard_map.100 = (f32[256,128]{1,0:T(8,128)S(1)}, f32[256,128]{1,0:T(8,128)S(1)}, f32[256,128]{1,0:T(8,128)S(1)}, f32[256,128]{1,0:T(8,128)S(1)}) custom-call(s32[3]{0:T(128)S(1)} %pad_add_fusion.where, s32[1,2]{1,0:T(1,128)} %slot_range.9, s32[4,8]{1,0:T(4,128)S(1)} %maximum_convert_fusion.offs, f32[384,128]{1,0:T(8,128)S(1)} %collective-permute-done.13.refs_0_, ...), custom_call_target="tpu_custom_call" | custom-call | flops 4194304 | bytes 2097152 | tf_op jit(solution)/shard_map/pallas_call | solution.py:344
  70.3 2.0 %collective-permute-start.20 = (f32[256,128]{1,0:T(8,128)S(1)}, f32[256,128]{1,0:T(8,128)S(1)}, u32[]{:S(2)}, u32[]{:S(2)}) collective-permute-start(f32[256,128]{1,0:T(8,128)S(1)} %get-tuple-element.67), channel_id=1, source_target_pairs={{0,4},{2,6},{4,0},{6,2},{1,5},{3,7},{5,1},{7,3},{8,12},{10,14},{12... | collective-permute-start | bytes 393224 | tf_op jit(solution)/shard_map/ppermute | solution.py:363
  72.4 2.7 %collective-permute-start.28 = (f32[64,256]{1,0:T(8,128)S(1)}, f32[64,256]{1,0:T(8,128)S(1)}, u32[]{:S(2)}, u32[]{:S(2)}) collective-permute-start(f32[64,256]{1,0:T(8,128)S(1)} %add.6), channel_id=1, source_target_pairs={{0,16},{8,24},{16,0},{24,8},{1,17},{9,25},{17,1},{25,9},{2,18},{10... | collective-permute-start | bytes 196616 | tf_op jit(solution)/shard_map/ppermute | solution.py:373
  75.1 2.6 %collective-permute-start.26 = (f32[256,128]{1,0:T(8,128)S(1)}, f32[256,128]{1,0:T(8,128)S(1)}, u32[]{:S(2)}, u32[]{:S(2)}) collective-permute-start(f32[256,128]{1,0:T(8,128)S(1)} %get-tuple-element.71), channel_id=1, source_target_pairs={{0,8},{2,10},{8,16},{10,18},{16,24},{18,26},{1,9},{3,11},{9,17},{1... | collective-permute-start | bytes 393224 | tf_op jit(solution)/shard_map/ppermute | solution.py:452
  77.7 0.7 collective-permute-start.23
  78.3 0.2 collective-permute-done.28
  78.6 4.1 %collective-permute-start.22 = (f32[256,128]{1,0:T(8,128)S(1)}, f32[256,128]{1,0:T(8,128)S(1)}, u32[]{:S(2)}, u32[]{:S(2)}) collective-permute-start(f32[256,128]{1,0:T(8,128)S(1)} %get-tuple-element.69), channel_id=1, source_target_pairs={{0,6},{2,4},{4,2},{6,0},{1,7},{3,5},{5,3},{7,1},{8,14},{10,12},{12... | collective-permute-start | bytes 393224 | tf_op jit(solution)/shard_map/ppermute | solution.py:363
  82.7 0.7 collective-permute-start.25
  83.4 2.8 %collective-permute-start.24 = (f32[256,128]{1,0:T(8,128)S(1)}, f32[256,128]{1,0:T(8,128)S(1)}, u32[]{:S(2)}, u32[]{:S(2)}) collective-permute-start(f32[256,128]{1,0:T(8,128)S(1)} %get-tuple-element.72), channel_id=1, source_target_pairs={{0,10},{2,8},{8,18},{10,16},{16,26},{18,24},{1,11},{3,9},{9,19},{1... | collective-permute-start | bytes 393224 | tf_op jit(solution)/shard_map/ppermute | solution.py:452
  86.1 10.1 %all_gather.3.refs_8_ = f32[512,256]{1,0:T(8,128)S(1)} all-gather(f32[64,256]{1,0:T(8,128)S(1)} %add.7), channel_id=1, replica_groups=mesh['pair'=4,'half'=2,'col'=2,'core'=2] {'half','col','core'}, dimensions={0}, use_global_device_ids=true | all-gather | bytes 589824 | tf_op jit(solution)/shard_map/all_gather | solution.py:454
  96.3 1.5 %shard_map.102 = (f32[4,256,128]{2,1,0:T(8,128)}, f32[512,256]{1,0:T(8,128)}) custom-call(s32[3]{0:T(128)S(1)} %pad_add_fusion.where, f32[256,128]{1,0:T(8,128)S(1)} %collective-permute-done.20.refs_0_, f32[256,128]{1,0:T(8,128)S(1)} %collective-permute-done.21.refs_1_, f32[256,128]{1,0:T(8,128)S(1)} %collective-permute-done.22.refs_2_, ...), custom_call_target="tpu_custom_call" | custom-call | flops 131072 | bytes 2621440 | tf_op jit(solution)/shard_map/pallas_call | solution.py:344
  (29 shorter events, 0.8 us)
Async XLA Ops:
  0.6 1.5 %collective-permute-start = (s32[1,2,2]{2,1,0:T(2,128)}, s32[1,2,2]{2,1,0:T(2,128)S(1)}, u32[]{:S(2)}, u32[]{:S(2)}) collective-permute-start(s32[1,2,2]{2,1,0:T(2,128)} %offsets.1), channel_id=1, source_target_pairs={{0,1},{1,0},{2,3},{3,2},{4,5},{5,4},{6,7},{7,6},{8,9},{9,8},{10,11... | collective-permute-start | bytes 56 | tf_op jit(solution)/shard_map/ppermute | solution.py:393
  4.2 7.0 %collective-permute-start.1 = (f32[264,128]{1,0:T(8,128)S(1)}, f32[264,128]{1,0:T(8,128)S(1)}, u32[]{:S(2)}, u32[]{:S(2)}) collective-permute-start(f32[264,128]{1,0:T(8,128)S(1)} %get-tuple-element.40), channel_id=1, source_target_pairs={{0,2},{2,0},{4,6},{6,4},{1,3},{3,1},{5,7},{7,5},{8,10},{10,8},{12,... | collective-permute-start | bytes 405512 | tf_op jit(solution)/shard_map/ppermute | solution.py:363
  7.0 8.3 %collective-permute-start.2 = (f32[264,128]{1,0:T(8,128)S(1)}, f32[264,128]{1,0:T(8,128)S(1)}, u32[]{:S(2)}, u32[]{:S(2)}) collective-permute-start(f32[264,128]{1,0:T(8,128)S(1)} %get-tuple-element.41), channel_id=1, source_target_pairs={{0,4},{2,6},{4,0},{6,2},{1,5},{3,7},{5,1},{7,3},{8,12},{10,14},{12... | collective-permute-start | bytes 405512 | tf_op jit(solution)/shard_map/ppermute | solution.py:363
  8.5 6.8 %collective-permute-start.3 = (f32[264,128]{1,0:T(8,128)S(1)}, f32[264,128]{1,0:T(8,128)S(1)}, u32[]{:S(2)}, u32[]{:S(2)}) collective-permute-start(f32[264,128]{1,0:T(8,128)S(1)} %get-tuple-element.42), channel_id=1, source_target_pairs={{0,6},{2,4},{4,2},{6,0},{1,7},{3,5},{5,3},{7,1},{8,14},{10,12},{12... | collective-permute-start | bytes 405512 | tf_op jit(solution)/shard_map/ppermute | solution.py:363
  15.9 9.1 %collective-permute-start.4 = (f32[2,256,128]{2,1,0:T(8,128)S(1)}, f32[2,256,128]{2,1,0:T(8,128)S(1)}, u32[]{:S(2)}, u32[]{:S(2)}) collective-permute-start(f32[2,256,128]{2,1,0:T(8,128)S(1)} %shard_map.96), channel_id=1, source_target_pairs={{8,0},{16,8},{24,16},{9,1},{17,9},{25,17},{10,2},{18,10},{26,18},{... | collective-permute-start | bytes 786440 | tf_op jit(solution)/shard_map/ppermute | solution.py:407
  17.2 7.8 %collective-permute-start.5 = (f32[256,256]{1,0:T(8,128)S(1)}, f32[256,256]{1,0:T(8,128)S(1)}, u32[]{:S(2)}, u32[]{:S(2)}) collective-permute-start(f32[256,256]{1,0:T(8,128)S(1)} %get-tuple-element.45), channel_id=1, source_target_pairs={{0,4},{4,0},{1,5},{5,1},{2,6},{6,2},{3,7},{7,3},{8,12},{12,8},{9,1... | collective-permute-start | bytes 786440 | tf_op jit(solution)/shard_map/ppermute | solution.py:408
  26.4 5.7 %collective-permute-start.6 = (f32[256,128]{1,0:T(8,128)S(1)}, f32[256,128]{1,0:T(8,128)S(1)}, u32[]{:S(2)}, u32[]{:S(2)}) collective-permute-start(f32[256,128]{1,0:T(8,128)S(1)} %get-tuple-element.47), channel_id=1, source_target_pairs={{0,4},{1,5},{2,6},{3,7},{4,0},{5,1},{6,2},{7,3},{8,12},{9,13},{10,... | collective-permute-start | bytes 393224 | tf_op jit(solution)/shard_map/ppermute | solution.py:363
  28.1 6.1 %collective-permute-start.7 = (f32[256,128]{1,0:T(8,128)S(1)}, f32[256,128]{1,0:T(8,128)S(1)}, u32[]{:S(2)}, u32[]{:S(2)}) collective-permute-start(f32[256,128]{1,0:T(8,128)S(1)} %get-tuple-element.48), channel_id=1, source_target_pairs={{0,2},{1,3},{2,0},{3,1},{4,6},{5,7},{6,4},{7,5},{8,10},{9,11},{10,... | collective-permute-start | bytes 393224 | tf_op jit(solution)/shard_map/ppermute | solution.py:363
  28.9 8.0 %collective-permute-start.8 = (f32[256,128]{1,0:T(8,128)S(1)}, f32[256,128]{1,0:T(8,128)S(1)}, u32[]{:S(2)}, u32[]{:S(2)}) collective-permute-start(f32[256,128]{1,0:T(8,128)S(1)} %get-tuple-element.49), channel_id=1, source_target_pairs={{0,5},{1,4},{2,7},{3,6},{4,1},{5,0},{6,3},{7,2},{8,13},{9,12},{10,... | collective-permute-start | bytes 393224 | tf_op jit(solution)/shard_map/ppermute | solution.py:363
  28.9 8.0 %collective-permute-start.9 = (f32[256,128]{1,0:T(8,128)S(1)}, f32[256,128]{1,0:T(8,128)S(1)}, u32[]{:S(2)}, u32[]{:S(2)}) collective-permute-start(f32[256,128]{1,0:T(8,128)S(1)} %get-tuple-element.50), channel_id=1, source_target_pairs={{0,3},{1,2},{2,1},{3,0},{4,7},{5,6},{6,5},{7,4},{8,11},{9,10},{10,... | collective-permute-start | bytes 393224 | tf_op jit(solution)/shard_map/ppermute | solution.py:363
  30.6 8.7 %collective-permute-start.10 = (f32[256,128]{1,0:T(8,128)S(1)}, f32[256,128]{1,0:T(8,128)S(1)}, u32[]{:S(2)}, u32[]{:S(2)}) collective-permute-start(f32[256,128]{1,0:T(8,128)S(1)} %get-tuple-element.51), channel_id=1, source_target_pairs={{0,6},{1,7},{2,4},{3,5},{4,2},{5,3},{6,0},{7,1},{8,14},{9,15},{10,... | collective-permute-start | bytes 393224 | tf_op jit(solution)/shard_map/ppermute | solution.py:363
  32.1 8.5 %collective-permute-start.11 = (f32[256,128]{1,0:T(8,128)S(1)}, f32[256,128]{1,0:T(8,128)S(1)}, u32[]{:S(2)}, u32[]{:S(2)}) collective-permute-start(f32[256,128]{1,0:T(8,128)S(1)} %get-tuple-element.52), channel_id=1, source_target_pairs={{0,7},{1,6},{2,5},{3,4},{4,3},{5,2},{6,1},{7,0},{8,15},{9,14},{10,... | collective-permute-start | bytes 393224 | tf_op jit(solution)/shard_map/ppermute | solution.py:363
  34.1 6.5 %collective-permute-start.12 = (f32[256,128]{1,0:T(8,128)S(1)}, f32[256,128]{1,0:T(8,128)S(1)}, u32[]{:S(2)}, u32[]{:S(2)}) collective-permute-start(f32[256,128]{1,0:T(8,128)S(1)} %get-tuple-element.53), channel_id=1, source_target_pairs={{0,1},{1,0},{2,3},{3,2},{4,5},{5,4},{6,7},{7,6},{8,9},{9,8},{10,11... | collective-permute-start | bytes 393224 | tf_op jit(solution)/shard_map/ppermute | solution.py:363
  34.2 6.5 %copy-start = (f32[2,136,128]{2,1,0:T(8,128)S(1)}, f32[2,136,128]{2,1,0:T(8,128)}, u32[]{:S(2)}) copy-start(f32[2,136,128]{2,1,0:T(8,128)} %constant.17.clone.refs_11_) | copy-start | bytes 417796
  45.0 7.8 %collective-permute-start.13 = (f32[384,128]{1,0:T(8,128)S(1)}, f32[384,128]{1,0:T(8,128)S(1)}, u32[]{:S(2)}, u32[]{:S(2)}) collective-permute-start(f32[384,128]{1,0:T(8,128)S(1)} %get-tuple-element.59), channel_id=1, source_target_pairs={{0,4},{1,5},{2,6},{3,7},{4,0},{5,1},{6,2},{7,3},{8,12},{9,13},{10,... | collective-permute-start | bytes 589832 | tf_op jit(solution)/shard_map/ppermute | solution.py:363
  46.2 7.8 %collective-permute-start.14 = (f32[384,128]{1,0:T(8,128)S(1)}, f32[384,128]{1,0:T(8,128)S(1)}, u32[]{:S(2)}, u32[]{:S(2)}) collective-permute-start(f32[384,128]{1,0:T(8,128)S(1)} %get-tuple-element.60), channel_id=1, source_target_pairs={{0,2},{1,3},{2,0},{3,1},{4,6},{5,7},{6,4},{7,5},{8,10},{9,11},{10,... | collective-permute-start | bytes 589832 | tf_op jit(solution)/shard_map/ppermute | solution.py:363
  47.4 8.8 %collective-permute-start.15 = (f32[384,128]{1,0:T(8,128)S(1)}, f32[384,128]{1,0:T(8,128)S(1)}, u32[]{:S(2)}, u32[]{:S(2)}) collective-permute-start(f32[384,128]{1,0:T(8,128)S(1)} %get-tuple-element.61), channel_id=1, source_target_pairs={{0,5},{1,4},{2,7},{3,6},{4,1},{5,0},{6,3},{7,2},{8,13},{9,12},{10,... | collective-permute-start | bytes 589832 | tf_op jit(solution)/shard_map/ppermute | solution.py:363
  48.2 9.3 %collective-permute-start.16 = (f32[384,128]{1,0:T(8,128)S(1)}, f32[384,128]{1,0:T(8,128)S(1)}, u32[]{:S(2)}, u32[]{:S(2)}) collective-permute-start(f32[384,128]{1,0:T(8,128)S(1)} %get-tuple-element.62), channel_id=1, source_target_pairs={{0,3},{1,2},{2,1},{3,0},{4,7},{5,6},{6,5},{7,4},{8,11},{9,10},{10,... | collective-permute-start | bytes 589832 | tf_op jit(solution)/shard_map/ppermute | solution.py:363
  48.8 13.9 %collective-permute-start.17 = (f32[384,128]{1,0:T(8,128)S(1)}, f32[384,128]{1,0:T(8,128)S(1)}, u32[]{:S(2)}, u32[]{:S(2)}) collective-permute-start(f32[384,128]{1,0:T(8,128)S(1)} %get-tuple-element.63), channel_id=1, source_target_pairs={{0,6},{1,7},{2,4},{3,5},{4,2},{5,3},{6,0},{7,1},{8,14},{9,15},{10,... | collective-permute-start | bytes 589832 | tf_op jit(solution)/shard_map/ppermute | solution.py:363
  52.7 12.8 %collective-permute-start.18 = (f32[384,128]{1,0:T(8,128)S(1)}, f32[384,128]{1,0:T(8,128)S(1)}, u32[]{:S(2)}, u32[]{:S(2)}) collective-permute-start(f32[384,128]{1,0:T(8,128)S(1)} %get-tuple-element.64), channel_id=1, source_target_pairs={{0,7},{1,6},{2,5},{3,4},{4,3},{5,2},{6,1},{7,0},{8,15},{9,14},{10,... | collective-permute-start | bytes 589832 | tf_op jit(solution)/shard_map/ppermute | solution.py:363
  54.0 11.6 %collective-permute-start.19 = (f32[384,128]{1,0:T(8,128)S(1)}, f32[384,128]{1,0:T(8,128)S(1)}, u32[]{:S(2)}, u32[]{:S(2)}) collective-permute-start(f32[384,128]{1,0:T(8,128)S(1)} %get-tuple-element.65), channel_id=1, source_target_pairs={{0,1},{1,0},{2,3},{3,2},{4,5},{5,4},{6,7},{7,6},{8,9},{9,8},{10,11... | collective-permute-start | bytes 589832 | tf_op jit(solution)/shard_map/ppermute | solution.py:363
  66.7 5.8 %collective-permute-start.27 = (f32[64,256]{1,0:T(8,128)S(1)}, f32[64,256]{1,0:T(8,128)S(1)}, u32[]{:S(2)}, u32[]{:S(2)}) collective-permute-start(f32[64,256]{1,0:T(8,128)S(1)} %get-tuple-element.73), channel_id=1, source_target_pairs={{0,8},{8,0},{16,24},{24,16},{1,9},{9,1},{17,25},{25,17},{2,10},{10... | collective-permute-start | bytes 196616 | tf_op jit(solution)/shard_map/ppermute | solution.py:373
  70.3 12.4 %collective-permute-start.20 = (f32[256,128]{1,0:T(8,128)S(1)}, f32[256,128]{1,0:T(8,128)S(1)}, u32[]{:S(2)}, u32[]{:S(2)}) collective-permute-start(f32[256,128]{1,0:T(8,128)S(1)} %get-tuple-element.67), channel_id=1, source_target_pairs={{0,4},{2,6},{4,0},{6,2},{1,5},{3,7},{5,1},{7,3},{8,12},{10,14},{12... | collective-permute-start | bytes 393224 | tf_op jit(solution)/shard_map/ppermute | solution.py:363
  72.3 11.1 %collective-permute-start.21 = (f32[256,128]{1,0:T(8,128)S(1)}, f32[256,128]{1,0:T(8,128)S(1)}, u32[]{:S(2)}, u32[]{:S(2)}) collective-permute-start(f32[256,128]{1,0:T(8,128)S(1)} %get-tuple-element.68), channel_id=1, source_target_pairs={{0,2},{2,0},{4,6},{6,4},{1,3},{3,1},{5,7},{7,5},{8,10},{10,8},{12,... | collective-permute-start | bytes 393224 | tf_op jit(solution)/shard_map/ppermute | solution.py:363
  72.4 6.1 %collective-permute-start.28 = (f32[64,256]{1,0:T(8,128)S(1)}, f32[64,256]{1,0:T(8,128)S(1)}, u32[]{:S(2)}, u32[]{:S(2)}) collective-permute-start(f32[64,256]{1,0:T(8,128)S(1)} %add.6), channel_id=1, source_target_pairs={{0,16},{8,24},{16,0},{24,8},{1,17},{9,25},{17,1},{25,9},{2,18},{10... | collective-permute-start | bytes 196616 | tf_op jit(solution)/shard_map/ppermute | solution.py:373
  75.1 21.1 %collective-permute-start.26 = (f32[256,128]{1,0:T(8,128)S(1)}, f32[256,128]{1,0:T(8,128)S(1)}, u32[]{:S(2)}, u32[]{:S(2)}) collective-permute-start(f32[256,128]{1,0:T(8,128)S(1)} %get-tuple-element.71), channel_id=1, source_target_pairs={{0,8},{2,10},{8,16},{10,18},{16,24},{18,26},{1,9},{3,11},{9,17},{1... | collective-permute-start | bytes 393224 | tf_op jit(solution)/shard_map/ppermute | solution.py:452
  77.7 18.6 %collective-permute-start.23 = (f32[256,128]{1,0:T(8,128)S(1)}, f32[256,128]{1,0:T(8,128)S(1)}, u32[]{:S(2)}, u32[]{:S(2)}) collective-permute-start(f32[256,128]{1,0:T(8,128)S(1)} %get-tuple-element.71), channel_id=1, source_target_pairs={{4,8},{6,10},{12,16},{14,18},{20,24},{22,26},{5,9},{7,11},{13,17},... | collective-permute-start | bytes 393224 | tf_op jit(solution)/shard_map/ppermute | solution.py:452
  78.6 17.7 %collective-permute-start.22 = (f32[256,128]{1,0:T(8,128)S(1)}, f32[256,128]{1,0:T(8,128)S(1)}, u32[]{:S(2)}, u32[]{:S(2)}) collective-permute-start(f32[256,128]{1,0:T(8,128)S(1)} %get-tuple-element.69), channel_id=1, source_target_pairs={{0,6},{2,4},{4,2},{6,0},{1,7},{3,5},{5,3},{7,1},{8,14},{10,12},{12... | collective-permute-start | bytes 393224 | tf_op jit(solution)/shard_map/ppermute | solution.py:363
  82.7 13.6 %collective-permute-start.25 = (f32[256,128]{1,0:T(8,128)S(1)}, f32[256,128]{1,0:T(8,128)S(1)}, u32[]{:S(2)}, u32[]{:S(2)}) collective-permute-start(f32[256,128]{1,0:T(8,128)S(1)} %get-tuple-element.72), channel_id=1, source_target_pairs={{4,10},{6,8},{12,18},{14,16},{20,26},{22,24},{5,11},{7,9},{13,19},... | collective-permute-start | bytes 393224 | tf_op jit(solution)/shard_map/ppermute | solution.py:452
  83.4 12.9 %collective-permute-start.24 = (f32[256,128]{1,0:T(8,128)S(1)}, f32[256,128]{1,0:T(8,128)S(1)}, u32[]{:S(2)}, u32[]{:S(2)}) collective-permute-start(f32[256,128]{1,0:T(8,128)S(1)} %get-tuple-element.72), channel_id=1, source_target_pairs={{0,10},{2,8},{8,18},{10,16},{16,26},{18,24},{1,11},{3,9},{9,19},{1... | collective-permute-start | bytes 393224 | tf_op jit(solution)/shard_map/ppermute | solution.py:452

commit v13 on v10

--- a/solution.py
+++ b/solution.py
@@ -167,20 +167,20 @@
         copy.wait()
 
 
-def lowest_kernel(where, *refs):
-    gotten, out = dict(zip(FOUR, refs)), refs[4]
-    rows = out.shape[1]
-    for turn in range(2):
-        out[turn] = jnp.where(where[0] == 0, gotten[turn][:rows], gotten[2 + turn][:rows])
+def lowest_kernel(where, first, second, out):
+    rows = out.shape[0]
+    out[...] = jnp.where(where[0] == 0, first[:rows], second[:rows])
 
 
 def pick_kernel(where, slot_range, *refs):
-    gotten, below, outs, (own, parts) = dict(zip(FOUR, refs)), refs[4], refs[5:13], refs[13:]
+    gotten, below, outs, (own, parts) = dict(zip(FOUR, refs)), refs[4:7], refs[7:15], refs[15:]
     rows, cols = outs[0].shape
     half, col, core = where[0], where[1], where[2]
     mine = 2 * half + col
     for turn in range(4):
         own[jnp.bitwise_xor(mine, turn)] = gotten[turn][...]
+    near = jnp.where(half == 0, below[0][:rows], below[1][:rows])
+    below = [jnp.where(col == side, near, below[2][...]) for side in range(2)]
     split_at = slot_range[0, 1 - half]
     row_ids = lax.broadcasted_iota(jnp.int32, (rows, cols), 0).astype(jnp.float32)
     col_ids = (lax.broadcasted_iota(jnp.int32, (rows, cols), 1) + core * cols).astype(jnp.float32)
@@ -194,7 +194,7 @@
         def merged(side, lower=lower, upper_rows=upper_rows):
             second = own[2 + side, :rows]
             top = jnp.where(lower == 1, second, own[side, :rows])
-            bottom = jnp.where(lower == 1, below[jnp.bitwise_xor(col, side)], second)
+            bottom = jnp.where(lower == 1, below[side], second)
             return jnp.where(upper_rows, top, bottom)
 
         parts[place] = jnp.where(left_cols, merged(0), merged(1))
@@ -298,17 +298,16 @@
 
 
 def add_below_kernel(where, slot_range, offs, *refs):
-    parts, (below, probe_band) = refs[:8], refs[8:]
-    rows, cols = below.shape[1:]
+    parts, out = refs[:8], refs[8]
+    cols = out.shape[1]
+    rows = 2 * cols
     sums = add_parts(where, slot_range, offs, parts, 2, rows, cols)
-    for side in range(2):
-        below[jnp.bitwise_xor(where[1], side)] = sums[side]
+    out[:rows] = jnp.where(where[1] == 0, sums[0], sums[1])
+    out[rows : 2 * rows] = jnp.where(where[1] == 0, sums[1], sums[0])
     total = parts[0][rows:]
     for part in parts[1:]:
         total = total + part[rows:]
-    band = probe_band.shape[0]
-    probe_band[:, :cols] = total[:band]
-    probe_band[:, cols:] = total[band:]
+    out[2 * rows :] = total
 
 
 def add_own_kernel(where, slot_range, offs, *refs):
@@ -318,11 +317,30 @@
         own[2 * strip], own[2 * strip + 1] = add_parts(where, slot_range, offs, parts, strip, rows, cols)
 
 
-def top_kernel(where, own, above, *outs):
+def top_kernel(where, own, below, above, *refs):
+    outs, both = refs[:4], refs[4]
     mine = 2 * where[0] + where[1]
+    rows = outs[0].shape[0]
     for turn, out in zip(FOUR, outs):
-        extra = jnp.where(where[0] == turn // 2, above[turn % 2], 0.0)
+        start = rows * (turn % 2)
+        extra = jnp.where((where[0] == turn // 2) & (where[3] > 0), above[start : start + rows], 0.0)
         out[...] = own[jnp.bitwise_xor(mine, turn)] + extra
+    both[0] = below[2 * rows :]
+    both[1] = above[2 * rows :]
+
+
+def band_kernel(where, *refs):
+    parts, out, inside = refs[:-2], refs[-2], refs[-1]
+    count = inside.shape[0]
+    for number in range(count):
+        part = parts[number // parts[0].shape[0]][number % parts[0].shape[0]]
+        inside[lax.rem(where[3] + count - number, count)] = part
+    total = inside[0]
+    for number in range(1, count):
+        total = total + inside[number]
+    band, cols = out.shape[0], total.shape[1]
+    out[:, :cols] = total[:band]
+    out[:, cols:] = total[band:]
 
 
 def join_kernel(where, *refs):
@@ -367,25 +385,13 @@
     ]
 
 
-def sum_over(value, axis, size, first):
-    if size & (size - 1):
-        return value if first else lax.psum(value, axis)
-    step = 1 << first
-    while step < size:
-        value = value + lax.ppermute(value, axis, [(k, k ^ step) for k in range(size)])
-        step *= 2
-        if first == 0:
-            break
-    return value
-
-
 def local(object_field, probe, offsets, slot_range, measured):
     width = probe.shape[-1]
     planes, rows, cols = 4, object_field.shape[2], object_field.shape[3]
     band = width // 4
     pairs = lax.axis_size("pair")
     half, col, core = (lax.axis_index(name) for name in PLANE)
-    where = jnp.stack([half, col, core])
+    where = jnp.stack([half, col, core, lax.axis_index("pair")])
 
     sibling = lax.ppermute(offsets, "core", [(0, 1), (1, 0)])
     offsets, slot_range = (pltpu.with_memory_space_constraint(x, pltpu.HBM) for x in (offsets, slot_range))
@@ -398,18 +404,25 @@
         0,
         copies=5,
     )
-    own = deal(dealt, PLANE[:2])
-    (lowest,) = call(lowest_kernel, [shape(2, rows, cols)], (where,), own, 0)
+    dealt = dict(zip(FOUR, dealt))
+    below = []
+    for to_half in range(2):
+        moves = [(2 * (pair + 1), 2 * pair + to_half) for pair in range(pairs - 1)]
+        below.append(lax.ppermute(dealt[2 * to_half], ("pair", "half"), moves))
+    own = deal([dealt[turn] for turn in FOUR], PLANE[:2])
+    below[0], below[1], *own = lax.optimization_barrier((*below, *own))
+    turned = dict(zip(FOUR, own))
+    (lowest,) = call(lowest_kernel, [shape(rows, cols)], (where,), (turned[1], turned[3]), 0)
     lowest, given = lax.optimization_barrier((lowest, given))
-    below = lax.ppermute(lowest, "pair", [(k, k - 1) for k in range(1, pairs)])
+    below.append(lax.ppermute(lowest, "pair", [(k, k - 1) for k in range(1, pairs)]))
     taken = lax.ppermute(given, "half", [(0, 1), (1, 0)])
-    below, taken = lax.optimization_barrier((below, taken))
+    below[2], taken = lax.optimization_barrier((below[2], taken))
 
     parts = call(
         pick_kernel,
         [shape(rows, cols)] * 8,
         (where, slot_range),
-        (*own, below),
+        (*own, *below),
         32 * rows * width,
         [(planes, rows + 8, cols), (8, rows, cols)],
     )
@@ -434,20 +447,29 @@
         [(8, rows, cols), (8, rows + 2 * band, cols)],
     )
     got = deal(grad, PLANE)
-    lower_sums, probe_band = call(
-        add_below_kernel,
-        [shape(2, rows, cols), shape(band, width)],
-        scalars,
-        got,
-        32 * rows * width,
-    )
-    probe_band = sum_over(probe_band, "pair", pairs, 0)
+    (lower_sums,) = call(add_below_kernel, [shape(2 * rows + 2 * band, cols)], scalars, got, 32 * rows * width)
+    above = lax.ppermute(lower_sums, "pair", [(k, (k + 1) % pairs) for k in range(pairs)])
     (sums,) = call(add_own_kernel, [shape(planes, rows, cols)], scalars, got, 64 * rows * width)
-    lower_sums, sums, probe_band = lax.optimization_barrier((lower_sums, sums, probe_band))
-    above = lax.ppermute(lower_sums, "pair", [(k, k + 1) for k in range(pairs - 1)])
-    sums = call(top_kernel, [shape(rows, cols)] * 4, (where,), (sums, above), planes * rows * cols)
+    *sums, both = call(
+        top_kernel,
+        [shape(rows, cols)] * 4 + [shape(2, 2 * band, cols)],
+        (where,),
+        (sums, lower_sums, above),
+        planes * rows * cols,
+    )
     sums = deal(sums, PLANE[:2])
-    probe_band = sum_over(probe_band, "pair", pairs, 1)
+    if pairs & (pairs - 1) or pairs == 1:
+        bands = [lax.all_gather(both[0], "pair")]
+        bands = [bands[0][(lax.axis_index("pair") - jnp.arange(pairs)) % pairs]]
+    else:
+        bands, step = [both], 2
+        while step < pairs:
+            near = jnp.concatenate(bands) if len(bands) > 1 else bands[0]
+            bands = [near, lax.ppermute(near, "pair", [(k, (k + step) % pairs) for k in range(pairs)])]
+            step *= 2
+    (probe_band,) = call(
+        band_kernel, [shape(band, width)], (where,), bands, pairs * band * width, [(pairs, 2 * band, cols)]
+    )
     probe_grad = lax.all_gather(probe_band, PLANE, axis=0, tiled=True)
     object_grad, probe_grad = call(
         join_kernel,

time: 97.8 us -> 104 us (1.063)
  waiting for transfers between devices: 37.3 us -> 43.8 us
  blocking collectives: 9.32 us -> 10.4 us
    ppermute x4 -> x5, waiting for transfers between devices: 10.7 us -> 18.1 us  [the longest x1 8.2 us: local(): lax.ppermute(lower_sums, 'pair', [(k, (k + 1) % pairs) for k in range(pai...]
    ppermute x4 -> x5, starting transfers between devices: 9.51 us -> 6.45 us  [the longest x1 2.17 us: local(): lax.ppermute(lower_sums, 'pair', [(k, (k + 1) % pairs) for k in range(pai...]
    ppermute x20, starting transfers between devices: 20.8 us -> 22 us  [deal(): lax.ppermute(value, axes, [(k, k ^ turn) for k in range(count)])]
    all_gather x1, blocking collectives: 9.32 us -> 10.4 us  [local(): probe_grad = lax.all_gather(probe_band, PLANE, axis=0, tiled=True)]
    pallas_call x9 -> x10, Pallas kernels: 15.8 us -> 16.4 us  [call(): pl.pallas_call(kernel, out_shape=[x for x, unused in outs], in_specs=[SME...]
  transfers between devices with their start and end apart: 26 -> 27, of which waited for: 15 -> 15; matrix products, arithmetic and copies ran while one was open for 1% -> 0% of each run, Pallas kernels for 5% -> 5%
where the time goes in v13:
time: 104 us; the launch traced here: 103 us
  waiting for transfers between devices  43.8 us (42%)
  starting transfers between devices  31.6 us (30%)
  Pallas kernels  16.4 us (16%)
  blocking collectives  10.4 us (10%)
    ppermute x20, waiting for transfers between devices, deal(): lax.ppermute(value, axes, [(k, k ^ turn) for k in range(count)])  24.8 us
    ppermute x20, starting transfers between devices, deal(): lax.ppermute(value, axes, [(k, k ^ turn) for k in range(count)])  22 us
    pallas_call x10, Pallas kernels, call(): pl.pallas_call(kernel, out_shape=[x for x, unused in outs], in_specs=[SME...  16.4 us
    all_gather x1, blocking collectives, local(): probe_grad = lax.all_gather(probe_band, PLANE, axis=0, tiled=True)  10.4 us
    ppermute x1, waiting for transfers between devices, local(): lax.ppermute(lower_sums, 'pair', [(k, (k + 1) % pairs) for k in range(pai...  8.2 us
    ppermute x1, waiting for transfers between devices, local(): lax.ppermute(lowest, 'pair', [(k, k - 1) for k in range(1, pairs)])  5.88 us
    ppermute x1, waiting for transfers between devices, local(): lax.ppermute(near, 'pair', [(k, (k + step) % pairs) for k in range(pairs)])  3.32 us
    ppermute x1, starting transfers between devices, local(): taken = lax.ppermute(given, 'half', [(0, 1), (1, 0)])  2.55 us
  transfers between devices with their start and end apart: 27, of which 15 were waited for; matrix products, arithmetic and copies ran while one was open for 0% of the time, Pallas kernels for 5%

profile of v13, /device:TPU:0, one launch (start us, length us, event | category | flops | bytes accessed | tf_op | source)
XLA Modules:
  0.0 103.2 jit_solution(16510055649920118667)
XLA Ops:
  1.2 1.0 collective-permute-done.sibling
  2.2 2.0 %shard_map.95 = (f32[264,128]{1,0:T(8,128)S(1)}, f32[264,128]{1,0:T(8,128)S(1)}, f32[264,128]{1,0:T(8,128)S(1)}, f32[264,128]{1,0:T(8,128)S(1)}, f32[256,256]{1,0:T(8,128)S(1)}) custom-call(s32[4]{0:T(128)S(1)} %pad_add_fusion.where, s32[1,2,2]{2,1,0:T(2,128)} %offsets.1, s32[1,2,2]{2,1,0:T(2,128)S(1)} %collective-permute-done.sibling, ...), custom_call_target="tpu_custom_call" | custom-call | bytes 1851392 | tf_op jit(solution)/shard_map/pallas_call | solution.py:364
  4.2 2.9 %collective-permute-start.4 = (f32[264,128]{1,0:T(8,128)S(1)}, f32[264,128]{1,0:T(8,128)S(1)}, u32[]{:S(2)}, u32[]{:S(2)}) collective-permute-start(f32[264,128]{1,0:T(8,128)S(1)} %get-tuple-element.45), channel_id=1, source_target_pairs={{0,2},{2,0},{4,6},{6,4},{1,3},{3,1},{5,7},{7,5},{8,10},{10,8},{12,... | collective-permute-start | bytes 405512 | tf_op jit(solution)/shard_map/ppermute | solution.py:383
  7.0 1.5 %collective-permute-start.5 = (f32[264,128]{1,0:T(8,128)S(1)}, f32[264,128]{1,0:T(8,128)S(1)}, u32[]{:S(2)}, u32[]{:S(2)}) collective-permute-start(f32[264,128]{1,0:T(8,128)S(1)} %get-tuple-element.46), channel_id=1, source_target_pairs={{0,6},{2,4},{4,2},{6,0},{1,7},{3,5},{5,3},{7,1},{8,14},{10,12},{12... | collective-permute-start | bytes 405512 | tf_op jit(solution)/shard_map/ppermute | solution.py:383
  8.5 1.3 %collective-permute-start.1 = (f32[264,128]{1,0:T(8,128)S(1)}, f32[264,128]{1,0:T(8,128)S(1)}, u32[]{:S(2)}, u32[]{:S(2)}) collective-permute-start(f32[264,128]{1,0:T(8,128)S(1)} %get-tuple-element.47.refs_3_), channel_id=1, source_target_pairs={{8,0},{16,8},{24,16},{9,1},{17,9},{25,17},{10,2},{18,10},{26,18},{... | collective-permute-start | bytes 405512 | tf_op jit(solution)/shard_map/ppermute | solution.py:411
  9.9 0.7 collective-permute-start.2
  10.6 0.8 collective-permute-done.4.first.refs_1_
  11.4 3.8 %collective-permute-done.5.second.refs_2_ = f32[264,128]{1,0:T(8,128)S(1)} collective-permute-done((f32[264,128]{1,0:T(8,128)S(1)}, f32[264,128]{1,0:T(8,128)S(1)}, u32[]{:S(2)}, u32[]{:S(2)}) %collective-permute-start.5) | collective-permute-done | bytes 135200 | tf_op jit(solution)/shard_map/ppermute | solution.py:383
  15.2 0.7 collective-permute-done.1.refs_4_
  15.8 2.5 %collective-permute-done.3.refs_0_ = f32[264,128]{1,0:T(8,128)S(1)} collective-permute-done((f32[264,128]{1,0:T(8,128)S(1)}, f32[264,128]{1,0:T(8,128)S(1)}, u32[]{:S(2)}, u32[]{:S(2)}) %collective-permute-start.3) | collective-permute-done | bytes 135200 | tf_op jit(solution)/shard_map/ppermute | solution.py:383
  18.4 0.6 shard_map.96
  19.0 2.5 %collective-permute-start.7 = (f32[256,256]{1,0:T(8,128)S(1)}, f32[256,256]{1,0:T(8,128)S(1)}, u32[]{:S(2)}, u32[]{:S(2)}) collective-permute-start(f32[256,256]{1,0:T(8,128)S(1)} %get-tuple-element.55), channel_id=1, source_target_pairs={{0,4},{4,0},{1,5},{5,1},{2,6},{6,2},{3,7},{7,3},{8,12},{12,8},{9,1... | collective-permute-start | bytes 786440 | tf_op jit(solution)/shard_map/ppermute | solution.py:418
  21.5 1.3 %collective-permute-start.6 = (f32[256,128]{1,0:T(8,128)S(1)}, f32[256,128]{1,0:T(8,128)S(1)}, u32[]{:S(2)}, u32[]{:S(2)}) collective-permute-start(f32[256,128]{1,0:T(8,128)S(1)} %shard_map.96), channel_id=1, source_target_pairs={{8,0},{16,8},{24,16},{9,1},{17,9},{25,17},{10,2},{18,10},{26,18},{... | collective-permute-start | bytes 393224 | tf_op jit(solution)/shard_map/ppermute | solution.py:417
  22.8 5.9 %collective-permute-done.6.refs_6_ = f32[256,128]{1,0:T(8,128)S(1)} collective-permute-done((f32[256,128]{1,0:T(8,128)S(1)}, f32[256,128]{1,0:T(8,128)S(1)}, u32[]{:S(2)}, u32[]{:S(2)}) %collective-permute-start.6) | collective-permute-done | bytes 131104 | tf_op jit(solution)/shard_map/ppermute | solution.py:417
  28.7 1.4 %shard_map.97 = (f32[256,128]{1,0:T(8,128)S(1)}, f32[256,128]{1,0:T(8,128)S(1)}, f32[256,128]{1,0:T(8,128)S(1)}, f32[256,128]{1,0:T(8,128)S(1)}, f32[256,128]{1,...) custom-call(s32[4]{0:T(128)S(1)} %pad_add_fusion.where, ...), custom_call_target="tpu_custom_call" | custom-call | flops 2097152 | bytes 1990656 | tf_op jit(solution)/shard_map/pallas_call | solution.py:364
  30.1 0.9 collective-permute-start.8
  31.0 1.3 %collective-permute-start.9 = (f32[256,128]{1,0:T(8,128)S(1)}, f32[256,128]{1,0:T(8,128)S(1)}, u32[]{:S(2)}, u32[]{:S(2)}) collective-permute-start(f32[256,128]{1,0:T(8,128)S(1)} %get-tuple-element.58), channel_id=1, source_target_pairs={{0,2},{1,3},{2,0},{3,1},{4,6},{5,7},{6,4},{7,5},{8,10},{9,11},{10,... | collective-permute-start | bytes 393224 | tf_op jit(solution)/shard_map/ppermute | solution.py:383
  32.6 1.7 %collective-permute-start.11 = (f32[256,128]{1,0:T(8,128)S(1)}, f32[256,128]{1,0:T(8,128)S(1)}, u32[]{:S(2)}, u32[]{:S(2)}) collective-permute-start(f32[256,128]{1,0:T(8,128)S(1)} %get-tuple-element.60), channel_id=1, source_target_pairs={{0,3},{1,2},{2,1},{3,0},{4,7},{5,6},{6,5},{7,4},{8,11},{9,10},{10,... | collective-permute-start | bytes 393224 | tf_op jit(solution)/shard_map/ppermute | solution.py:383
  34.3 1.5 %collective-permute-start.12 = (f32[256,128]{1,0:T(8,128)S(1)}, f32[256,128]{1,0:T(8,128)S(1)}, u32[]{:S(2)}, u32[]{:S(2)}) collective-permute-start(f32[256,128]{1,0:T(8,128)S(1)} %get-tuple-element.61), channel_id=1, source_target_pairs={{0,6},{1,7},{2,4},{3,5},{4,2},{5,3},{6,0},{7,1},{8,14},{9,15},{10,... | collective-permute-start | bytes 393224 | tf_op jit(solution)/shard_map/ppermute | solution.py:383
  35.8 0.5 collective-permute-start.13
  36.3 1.0 collective-permute-start.14
  37.3 2.7 %shard_map.98 = (f32[2,256,256]{2,1,0:T(8,128)S(1)}, f32[256,256]{1,0:T(8,128)S(1)}, bf16[6,512,256]{2,1,0:T(8,128)(2,1)S(1)}) custom-call(s32[4]{0:T(128)S(1)} %pad_add_fusion.where, s32[1,2]{1,0:T(1,128)} %slot_range.9, s32[4,8]{1,0:T(4,128)S(1)} %maximum_convert_fusion.offs, f32[256,256]{1,0:T(8,128)S(1)} %collective-permute-done.7.taken, ...), custom_call_target="tpu_custom_call" | custom-call | flops 201326592 | bytes 5505024 | tf_op jit(solution)/shard_map/pallas_call | solution.py:364
  40.1 2.8 %collective-permute-done.12.refs_4_ = f32[256,128]{1,0:T(8,128)S(1)} collective-permute-done((f32[256,128]{1,0:T(8,128)S(1)}, f32[256,128]{1,0:T(8,128)S(1)}, u32[]{:S(2)}, u32[]{:S(2)}) %collective-permute-start.12) | collective-permute-done | bytes 131104 | tf_op jit(solution)/shard_map/ppermute | solution.py:383
  42.9 1.3 %collective-permute-done.13.refs_5_ = f32[256,128]{1,0:T(8,128)S(1)} collective-permute-done((f32[256,128]{1,0:T(8,128)S(1)}, f32[256,128]{1,0:T(8,128)S(1)}, u32[]{:S(2)}, u32[]{:S(2)}) %collective-permute-start.13) | collective-permute-done | bytes 131104 | tf_op jit(solution)/shard_map/ppermute | solution.py:383
  44.3 4.3 %shard_map.99 = (f32[384,128]{1,0:T(8,128)S(1)}, f32[384,128]{1,0:T(8,128)S(1)}, f32[384,128]{1,0:T(8,128)S(1)}, f32[384,128]{1,0:T(8,128)S(1)}, f32[384,128]{1,...) custom-call(s32[4]{0:T(128)S(1)} %pad_add_fusion.where, ...), custom_call_target="tpu_custom_call" | custom-call | flops 1610612736 | bytes 5120000 | tf_op jit(solution)/shard_map/pallas_call | solution.py:364
  48.9 1.9 %collective-permute-start.16 = (f32[384,128]{1,0:T(8,128)S(1)}, f32[384,128]{1,0:T(8,128)S(1)}, u32[]{:S(2)}, u32[]{:S(2)}) collective-permute-start(f32[384,128]{1,0:T(8,128)S(1)} %get-tuple-element.70), channel_id=1, source_target_pairs={{0,2},{1,3},{2,0},{3,1},{4,6},{5,7},{6,4},{7,5},{8,10},{9,11},{10,... | collective-permute-start | bytes 589832 | tf_op jit(solution)/shard_map/ppermute | solution.py:383
  50.8 0.9 collective-permute-start.17
  51.7 0.7 collective-permute-start.18
  52.4 1.6 %collective-permute-start.19 = (f32[384,128]{1,0:T(8,128)S(1)}, f32[384,128]{1,0:T(8,128)S(1)}, u32[]{:S(2)}, u32[]{:S(2)}) collective-permute-start(f32[384,128]{1,0:T(8,128)S(1)} %get-tuple-element.73), channel_id=1, source_target_pairs={{0,6},{1,7},{2,4},{3,5},{4,2},{5,3},{6,0},{7,1},{8,14},{9,15},{10,... | collective-permute-start | bytes 589832 | tf_op jit(solution)/shard_map/ppermute | solution.py:383
  54.0 2.3 %collective-permute-done.15.refs_0_ = f32[384,128]{1,0:T(8,128)S(1)} collective-permute-done((f32[384,128]{1,0:T(8,128)S(1)}, f32[384,128]{1,0:T(8,128)S(1)}, u32[]{:S(2)}, u32[]{:S(2)}) %collective-permute-start.15) | collective-permute-done | bytes 196640 | tf_op jit(solution)/shard_map/ppermute | solution.py:383
  56.8 1.3 %collective-permute-start.21 = (f32[384,128]{1,0:T(8,128)S(1)}, f32[384,128]{1,0:T(8,128)S(1)}, u32[]{:S(2)}, u32[]{:S(2)}) collective-permute-start(f32[384,128]{1,0:T(8,128)S(1)} %get-tuple-element.75), channel_id=1, source_target_pairs={{0,1},{1,0},{2,3},{3,2},{4,5},{5,4},{6,7},{7,6},{8,9},{9,8},{10,11... | collective-permute-start | bytes 589832 | tf_op jit(solution)/shard_map/ppermute | solution.py:383
  58.1 1.8 %collective-permute-done.17.refs_2_ = f32[384,128]{1,0:T(8,128)S(1)} collective-permute-done((f32[384,128]{1,0:T(8,128)S(1)}, f32[384,128]{1,0:T(8,128)S(1)}, u32[]{:S(2)}, u32[]{:S(2)}) %collective-permute-start.17) | collective-permute-done | bytes 196640 | tf_op jit(solution)/shard_map/ppermute | solution.py:383
  59.9 0.8 collective-permute-done.18.refs_3_
  60.6 5.6 %collective-permute-done.19.refs_4_ = f32[384,128]{1,0:T(8,128)S(1)} collective-permute-done((f32[384,128]{1,0:T(8,128)S(1)}, f32[384,128]{1,0:T(8,128)S(1)}, u32[]{:S(2)}, u32[]{:S(2)}) %collective-permute-start.19) | collective-permute-done | bytes 196640 | tf_op jit(solution)/shard_map/ppermute | solution.py:383
  66.3 2.9 %collective-permute-done.20.refs_5_ = f32[384,128]{1,0:T(8,128)S(1)} collective-permute-done((f32[384,128]{1,0:T(8,128)S(1)}, f32[384,128]{1,0:T(8,128)S(1)}, u32[]{:S(2)}, u32[]{:S(2)}) %collective-permute-start.20) | collective-permute-done | bytes 196640 | tf_op jit(solution)/shard_map/ppermute | solution.py:383
  69.2 1.2 %shard_map.101.below = f32[640,128]{1,0:T(8,128)S(1)} custom-call(s32[4]{0:T(128)S(1)} %pad_add_fusion.where, s32[1,2]{1,0:T(1,128)} %slot_range.9, s32[4,8]{1,0:T(4,128)S(1)} %maximum_convert_fusion.offs, f32[384,128]{1,0:T(8,128)S(1)} %collective-permute-done.15.refs_0_, f32[384,128]{1,0:T(8,128)S(1)} %collective-permute-done.16.refs_1_, ...), custom_call_target="tpu_custom_call" | custom-call | flops 2097152 | bytes 1900544 | tf_op jit(solution)/shard_map/pallas_call | solution.py:364
  70.3 2.2 %collective-permute-start.22 = (f32[640,128]{1,0:T(8,128)S(1)}, f32[640,128]{1,0:T(8,128)S(1)}, u32[]{:S(2)}, u32[]{:S(2)}) collective-permute-start(f32[640,128]{1,0:T(8,128)S(1)} %shard_map.101.below), channel_id=1, source_target_pairs={{0,8},{8,16},{16,24},{24,0},{1,9},{9,17},{17,25},{25,1},{2,10},{10... | collective-permute-start | bytes 983048 | tf_op jit(solution)/shard_map/ppermute | solution.py:451
  72.5 1.6 %shard_map.100.own = f32[4,256,128]{2,1,0:T(8,128)S(1)} custom-call(s32[4]{0:T(128)S(1)} %pad_add_fusion.where, s32[1,2]{1,0:T(1,128)} %slot_range.9, s32[4,8]{1,0:T(4,128)S(1)} %maximum_convert_fusion.offs, f32[384,128]{1,0:T(8,128)S(1)} %collective-permute-done.15.refs_0_, f32[384,128]{1,0:T(8,128)S(1)} %collective-permute-done.16.refs_1_, ...), custom_call_target="tpu_custom_call" | custom-call | flops 4194304 | bytes 2097152 | tf_op jit(solution)/shard_map/pallas_call | solution.py:364
  74.1 8.2 %collective-permute-done.22.above = f32[640,128]{1,0:T(8,128)S(1)} collective-permute-done((f32[640,128]{1,0:T(8,128)S(1)}, f32[640,128]{1,0:T(8,128)S(1)}, u32[]{:S(2)}, u32[]{:S(2)}) %collective-permute-start.22) | collective-permute-done | bytes 327712 | tf_op jit(solution)/shard_map/ppermute | solution.py:451
  82.3 0.6 shard_map.102
  82.9 1.0 %collective-permute-start.26 = (f32[2,128,128]{2,1,0:T(8,128)S(1)}, f32[2,128,128]{2,1,0:T(8,128)S(1)}, u32[]{:S(2)}, u32[]{:S(2)}) collective-permute-start(f32[2,128,128]{2,1,0:T(8,128)S(1)} %get-tuple-element.81.refs_0_), channel_id=1, source_target_pairs={{0,16},{8,24},{16,0},{24,8},{1,17},{9,25},{17,1},{25,9},{2,18},{10... | collective-permute-start | bytes 393224 | tf_op jit(solution)/shard_map/ppermute | solution.py:468
  83.9 1.2 %collective-permute-start.23 = (f32[256,128]{1,0:T(8,128)S(1)}, f32[256,128]{1,0:T(8,128)S(1)}, u32[]{:S(2)}, u32[]{:S(2)}) collective-permute-start(f32[256,128]{1,0:T(8,128)S(1)} %get-tuple-element.77), channel_id=1, source_target_pairs={{0,4},{2,6},{4,0},{6,2},{1,5},{3,7},{5,1},{7,3},{8,12},{10,14},{12... | collective-permute-start | bytes 393224 | tf_op jit(solution)/shard_map/ppermute | solution.py:383
  85.1 1.4 %collective-permute-start.24 = (f32[256,128]{1,0:T(8,128)S(1)}, f32[256,128]{1,0:T(8,128)S(1)}, u32[]{:S(2)}, u32[]{:S(2)}) collective-permute-start(f32[256,128]{1,0:T(8,128)S(1)} %get-tuple-element.78), channel_id=1, source_target_pairs={{0,2},{2,0},{4,6},{6,4},{1,3},{3,1},{5,7},{7,5},{8,10},{10,8},{12,... | collective-permute-start | bytes 393224 | tf_op jit(solution)/shard_map/ppermute | solution.py:383
  86.5 0.9 collective-permute-start.25
  87.4 3.3 %collective-permute-done.26.refs_1_ = f32[2,128,128]{2,1,0:T(8,128)S(1)} collective-permute-done((f32[2,128,128]{2,1,0:T(8,128)S(1)}, f32[2,128,128]{2,1,0:T(8,128)S(1)}, u32[]{:S(2)}, u32[]{:S(2)}) %collective-permute-start.26) | collective-permute-done | bytes 131104 | tf_op jit(solution)/shard_map/ppermute | solution.py:468
  90.7 0.6 shard_map.103
  91.3 10.4 %all_gather.3.refs_4_ = f32[512,256]{1,0:T(8,128)S(1)} all-gather(f32[64,256]{1,0:T(8,128)S(1)} %shard_map.103), channel_id=1, replica_groups=mesh['pair'=4,'half'=2,'col'=2,'core'=2] {'half','col','core'}, dimensions={0}, use_global_device_ids=true | all-gather | bytes 589824 | tf_op jit(solution)/shard_map/all_gather | solution.py:473
  101.7 1.5 %shard_map.104 = (f32[4,256,128]{2,1,0:T(8,128)}, f32[512,256]{1,0:T(8,128)}) custom-call(s32[4]{0:T(128)S(1)} %pad_add_fusion.where, f32[256,128]{1,0:T(8,128)S(1)} %collective-permute-done.23.refs_0_, f32[256,128]{1,0:T(8,128)S(1)} %collective-permute-done.24.refs_1_, f32[256,128]{1,0:T(8,128)S(1)} %collective-permute-done.25.refs_2_, ...), custom_call_target="tpu_custom_call" | custom-call | bytes 2097152 | tf_op jit(solution)/shard_map/pallas_call | solution.py:364
  (23 shorter events, 1.8 us)
Async XLA Ops:
  0.6 1.5 %collective-permute-start = (s32[1,2,2]{2,1,0:T(2,128)}, s32[1,2,2]{2,1,0:T(2,128)S(1)}, u32[]{:S(2)}, u32[]{:S(2)}) collective-permute-start(s32[1,2,2]{2,1,0:T(2,128)} %offsets.1), channel_id=1, source_target_pairs={{0,1},{1,0},{2,3},{3,2},{4,5},{5,4},{6,7},{7,6},{8,9},{9,8},{10,11... | collective-permute-start | bytes 56 | tf_op jit(solution)/shard_map/ppermute | solution.py:396
  4.2 7.2 %collective-permute-start.4 = (f32[264,128]{1,0:T(8,128)S(1)}, f32[264,128]{1,0:T(8,128)S(1)}, u32[]{:S(2)}, u32[]{:S(2)}) collective-permute-start(f32[264,128]{1,0:T(8,128)S(1)} %get-tuple-element.45), channel_id=1, source_target_pairs={{0,2},{2,0},{4,6},{6,4},{1,3},{3,1},{5,7},{7,5},{8,10},{10,8},{12,... | collective-permute-start | bytes 405512 | tf_op jit(solution)/shard_map/ppermute | solution.py:383
  7.0 8.1 %collective-permute-start.5 = (f32[264,128]{1,0:T(8,128)S(1)}, f32[264,128]{1,0:T(8,128)S(1)}, u32[]{:S(2)}, u32[]{:S(2)}) collective-permute-start(f32[264,128]{1,0:T(8,128)S(1)} %get-tuple-element.46), channel_id=1, source_target_pairs={{0,6},{2,4},{4,2},{6,0},{1,7},{3,5},{5,3},{7,1},{8,14},{10,12},{12... | collective-permute-start | bytes 405512 | tf_op jit(solution)/shard_map/ppermute | solution.py:383
  8.5 7.3 %collective-permute-start.1 = (f32[264,128]{1,0:T(8,128)S(1)}, f32[264,128]{1,0:T(8,128)S(1)}, u32[]{:S(2)}, u32[]{:S(2)}) collective-permute-start(f32[264,128]{1,0:T(8,128)S(1)} %get-tuple-element.47.refs_3_), channel_id=1, source_target_pairs={{8,0},{16,8},{24,16},{9,1},{17,9},{25,17},{10,2},{18,10},{26,18},{... | collective-permute-start | bytes 405512 | tf_op jit(solution)/shard_map/ppermute | solution.py:411
  9.8 8.6 %collective-permute-start.3 = (f32[264,128]{1,0:T(8,128)S(1)}, f32[264,128]{1,0:T(8,128)S(1)}, u32[]{:S(2)}, u32[]{:S(2)}) collective-permute-start(f32[264,128]{1,0:T(8,128)S(1)} %get-tuple-element.44), channel_id=1, source_target_pairs={{0,4},{2,6},{4,0},{6,2},{1,5},{3,7},{5,1},{7,3},{8,12},{10,14},{12... | collective-permute-start | bytes 405512 | tf_op jit(solution)/shard_map/ppermute | solution.py:383
  9.9 8.5 %collective-permute-start.2 = (f32[264,128]{1,0:T(8,128)S(1)}, f32[264,128]{1,0:T(8,128)S(1)}, u32[]{:S(2)}, u32[]{:S(2)}) collective-permute-start(f32[264,128]{1,0:T(8,128)S(1)} %get-tuple-element.44), channel_id=1, source_target_pairs={{8,4},{16,12},{24,20},{9,5},{17,13},{25,21},{10,6},{18,14},{26,22}... | collective-permute-start | bytes 405512 | tf_op jit(solution)/shard_map/ppermute | solution.py:411
  19.0 9.7 %collective-permute-start.7 = (f32[256,256]{1,0:T(8,128)S(1)}, f32[256,256]{1,0:T(8,128)S(1)}, u32[]{:S(2)}, u32[]{:S(2)}) collective-permute-start(f32[256,256]{1,0:T(8,128)S(1)} %get-tuple-element.55), channel_id=1, source_target_pairs={{0,4},{4,0},{1,5},{5,1},{2,6},{6,2},{3,7},{7,3},{8,12},{12,8},{9,1... | collective-permute-start | bytes 786440 | tf_op jit(solution)/shard_map/ppermute | solution.py:418
  21.5 7.2 %collective-permute-start.6 = (f32[256,128]{1,0:T(8,128)S(1)}, f32[256,128]{1,0:T(8,128)S(1)}, u32[]{:S(2)}, u32[]{:S(2)}) collective-permute-start(f32[256,128]{1,0:T(8,128)S(1)} %shard_map.96), channel_id=1, source_target_pairs={{8,0},{16,8},{24,16},{9,1},{17,9},{25,17},{10,2},{18,10},{26,18},{... | collective-permute-start | bytes 393224 | tf_op jit(solution)/shard_map/ppermute | solution.py:417
  30.1 5.7 %collective-permute-start.8 = (f32[256,128]{1,0:T(8,128)S(1)}, f32[256,128]{1,0:T(8,128)S(1)}, u32[]{:S(2)}, u32[]{:S(2)}) collective-permute-start(f32[256,128]{1,0:T(8,128)S(1)} %get-tuple-element.57), channel_id=1, source_target_pairs={{0,4},{1,5},{2,6},{3,7},{4,0},{5,1},{6,2},{7,3},{8,12},{9,13},{10,... | collective-permute-start | bytes 393224 | tf_op jit(solution)/shard_map/ppermute | solution.py:383
  31.0 5.4 %collective-permute-start.9 = (f32[256,128]{1,0:T(8,128)S(1)}, f32[256,128]{1,0:T(8,128)S(1)}, u32[]{:S(2)}, u32[]{:S(2)}) collective-permute-start(f32[256,128]{1,0:T(8,128)S(1)} %get-tuple-element.58), channel_id=1, source_target_pairs={{0,2},{1,3},{2,0},{3,1},{4,6},{5,7},{6,4},{7,5},{8,10},{9,11},{10,... | collective-permute-start | bytes 393224 | tf_op jit(solution)/shard_map/ppermute | solution.py:383
  32.5 7.6 %collective-permute-start.10 = (f32[256,128]{1,0:T(8,128)S(1)}, f32[256,128]{1,0:T(8,128)S(1)}, u32[]{:S(2)}, u32[]{:S(2)}) collective-permute-start(f32[256,128]{1,0:T(8,128)S(1)} %get-tuple-element.59), channel_id=1, source_target_pairs={{0,5},{1,4},{2,7},{3,6},{4,1},{5,0},{6,3},{7,2},{8,13},{9,12},{10,... | collective-permute-start | bytes 393224 | tf_op jit(solution)/shard_map/ppermute | solution.py:383
  32.6 7.5 %collective-permute-start.11 = (f32[256,128]{1,0:T(8,128)S(1)}, f32[256,128]{1,0:T(8,128)S(1)}, u32[]{:S(2)}, u32[]{:S(2)}) collective-permute-start(f32[256,128]{1,0:T(8,128)S(1)} %get-tuple-element.60), channel_id=1, source_target_pairs={{0,3},{1,2},{2,1},{3,0},{4,7},{5,6},{6,5},{7,4},{8,11},{9,10},{10,... | collective-permute-start | bytes 393224 | tf_op jit(solution)/shard_map/ppermute | solution.py:383
  34.3 8.6 %collective-permute-start.12 = (f32[256,128]{1,0:T(8,128)S(1)}, f32[256,128]{1,0:T(8,128)S(1)}, u32[]{:S(2)}, u32[]{:S(2)}) collective-permute-start(f32[256,128]{1,0:T(8,128)S(1)} %get-tuple-element.61), channel_id=1, source_target_pairs={{0,6},{1,7},{2,4},{3,5},{4,2},{5,3},{6,0},{7,1},{8,14},{9,15},{10,... | collective-permute-start | bytes 393224 | tf_op jit(solution)/shard_map/ppermute | solution.py:383
  35.8 8.5 %collective-permute-start.13 = (f32[256,128]{1,0:T(8,128)S(1)}, f32[256,128]{1,0:T(8,128)S(1)}, u32[]{:S(2)}, u32[]{:S(2)}) collective-permute-start(f32[256,128]{1,0:T(8,128)S(1)} %get-tuple-element.62), channel_id=1, source_target_pairs={{0,7},{1,6},{2,5},{3,4},{4,3},{5,2},{6,1},{7,0},{8,15},{9,14},{10,... | collective-permute-start | bytes 393224 | tf_op jit(solution)/shard_map/ppermute | solution.py:383
  36.3 7.9 %collective-permute-start.14 = (f32[256,128]{1,0:T(8,128)S(1)}, f32[256,128]{1,0:T(8,128)S(1)}, u32[]{:S(2)}, u32[]{:S(2)}) collective-permute-start(f32[256,128]{1,0:T(8,128)S(1)} %get-tuple-element.63), channel_id=1, source_target_pairs={{0,1},{1,0},{2,3},{3,2},{4,5},{5,4},{6,7},{7,6},{8,9},{9,8},{10,11... | collective-permute-start | bytes 393224 | tf_op jit(solution)/shard_map/ppermute | solution.py:383
  37.3 6.9 %copy-start = (f32[2,136,128]{2,1,0:T(8,128)S(1)}, f32[2,136,128]{2,1,0:T(8,128)}, u32[]{:S(2)}) copy-start(f32[2,136,128]{2,1,0:T(8,128)} %constant.21.clone.refs_11_) | copy-start | bytes 417796
  48.6 7.8 %collective-permute-start.15 = (f32[384,128]{1,0:T(8,128)S(1)}, f32[384,128]{1,0:T(8,128)S(1)}, u32[]{:S(2)}, u32[]{:S(2)}) collective-permute-start(f32[384,128]{1,0:T(8,128)S(1)} %get-tuple-element.69), channel_id=1, source_target_pairs={{0,4},{1,5},{2,6},{3,7},{4,0},{5,1},{6,2},{7,3},{8,12},{9,13},{10,... | collective-permute-start | bytes 589832 | tf_op jit(solution)/shard_map/ppermute | solution.py:383
  48.9 7.9 %collective-permute-start.16 = (f32[384,128]{1,0:T(8,128)S(1)}, f32[384,128]{1,0:T(8,128)S(1)}, u32[]{:S(2)}, u32[]{:S(2)}) collective-permute-start(f32[384,128]{1,0:T(8,128)S(1)} %get-tuple-element.70), channel_id=1, source_target_pairs={{0,2},{1,3},{2,0},{3,1},{4,6},{5,7},{6,4},{7,5},{8,10},{9,11},{10,... | collective-permute-start | bytes 589832 | tf_op jit(solution)/shard_map/ppermute | solution.py:383
  50.8 9.1 %collective-permute-start.17 = (f32[384,128]{1,0:T(8,128)S(1)}, f32[384,128]{1,0:T(8,128)S(1)}, u32[]{:S(2)}, u32[]{:S(2)}) collective-permute-start(f32[384,128]{1,0:T(8,128)S(1)} %get-tuple-element.71), channel_id=1, source_target_pairs={{0,5},{1,4},{2,7},{3,6},{4,1},{5,0},{6,3},{7,2},{8,13},{9,12},{10,... | collective-permute-start | bytes 589832 | tf_op jit(solution)/shard_map/ppermute | solution.py:383
  51.7 8.9 %collective-permute-start.18 = (f32[384,128]{1,0:T(8,128)S(1)}, f32[384,128]{1,0:T(8,128)S(1)}, u32[]{:S(2)}, u32[]{:S(2)}) collective-permute-start(f32[384,128]{1,0:T(8,128)S(1)} %get-tuple-element.72), channel_id=1, source_target_pairs={{0,3},{1,2},{2,1},{3,0},{4,7},{5,6},{6,5},{7,4},{8,11},{9,10},{10,... | collective-permute-start | bytes 589832 | tf_op jit(solution)/shard_map/ppermute | solution.py:383
  52.4 13.8 %collective-permute-start.19 = (f32[384,128]{1,0:T(8,128)S(1)}, f32[384,128]{1,0:T(8,128)S(1)}, u32[]{:S(2)}, u32[]{:S(2)}) collective-permute-start(f32[384,128]{1,0:T(8,128)S(1)} %get-tuple-element.73), channel_id=1, source_target_pairs={{0,6},{1,7},{2,4},{3,5},{4,2},{5,3},{6,0},{7,1},{8,14},{9,15},{10,... | collective-permute-start | bytes 589832 | tf_op jit(solution)/shard_map/ppermute | solution.py:383
  56.3 12.9 %collective-permute-start.20 = (f32[384,128]{1,0:T(8,128)S(1)}, f32[384,128]{1,0:T(8,128)S(1)}, u32[]{:S(2)}, u32[]{:S(2)}) collective-permute-start(f32[384,128]{1,0:T(8,128)S(1)} %get-tuple-element.74), channel_id=1, source_target_pairs={{0,7},{1,6},{2,5},{3,4},{4,3},{5,2},{6,1},{7,0},{8,15},{9,14},{10,... | collective-permute-start | bytes 589832 | tf_op jit(solution)/shard_map/ppermute | solution.py:383
  56.8 12.4 %collective-permute-start.21 = (f32[384,128]{1,0:T(8,128)S(1)}, f32[384,128]{1,0:T(8,128)S(1)}, u32[]{:S(2)}, u32[]{:S(2)}) collective-permute-start(f32[384,128]{1,0:T(8,128)S(1)} %get-tuple-element.75), channel_id=1, source_target_pairs={{0,1},{1,0},{2,3},{3,2},{4,5},{5,4},{6,7},{7,6},{8,9},{9,8},{10,11... | collective-permute-start | bytes 589832 | tf_op jit(solution)/shard_map/ppermute | solution.py:383
  70.3 11.9 %collective-permute-start.22 = (f32[640,128]{1,0:T(8,128)S(1)}, f32[640,128]{1,0:T(8,128)S(1)}, u32[]{:S(2)}, u32[]{:S(2)}) collective-permute-start(f32[640,128]{1,0:T(8,128)S(1)} %shard_map.101.below), channel_id=1, source_target_pairs={{0,8},{8,16},{16,24},{24,0},{1,9},{9,17},{17,25},{25,1},{2,10},{10... | collective-permute-start | bytes 983048 | tf_op jit(solution)/shard_map/ppermute | solution.py:451
  82.9 7.9 %collective-permute-start.26 = (f32[2,128,128]{2,1,0:T(8,128)S(1)}, f32[2,128,128]{2,1,0:T(8,128)S(1)}, u32[]{:S(2)}, u32[]{:S(2)}) collective-permute-start(f32[2,128,128]{2,1,0:T(8,128)S(1)} %get-tuple-element.81.refs_0_), channel_id=1, source_target_pairs={{0,16},{8,24},{16,0},{24,8},{1,17},{9,25},{17,1},{25,9},{2,18},{10... | collective-permute-start | bytes 393224 | tf_op jit(solution)/shard_map/ppermute | solution.py:468
  83.9 17.8 %collective-permute-start.23 = (f32[256,128]{1,0:T(8,128)S(1)}, f32[256,128]{1,0:T(8,128)S(1)}, u32[]{:S(2)}, u32[]{:S(2)}) collective-permute-start(f32[256,128]{1,0:T(8,128)S(1)} %get-tuple-element.77), channel_id=1, source_target_pairs={{0,4},{2,6},{4,0},{6,2},{1,5},{3,7},{5,1},{7,3},{8,12},{10,14},{12... | collective-permute-start | bytes 393224 | tf_op jit(solution)/shard_map/ppermute | solution.py:383
  85.1 16.6 %collective-permute-start.24 = (f32[256,128]{1,0:T(8,128)S(1)}, f32[256,128]{1,0:T(8,128)S(1)}, u32[]{:S(2)}, u32[]{:S(2)}) collective-permute-start(f32[256,128]{1,0:T(8,128)S(1)} %get-tuple-element.78), channel_id=1, source_target_pairs={{0,2},{2,0},{4,6},{6,4},{1,3},{3,1},{5,7},{7,5},{8,10},{10,8},{12,... | collective-permute-start | bytes 393224 | tf_op jit(solution)/shard_map/ppermute | solution.py:383
  86.5 15.2 %collective-permute-start.25 = (f32[256,128]{1,0:T(8,128)S(1)}, f32[256,128]{1,0:T(8,128)S(1)}, u32[]{:S(2)}, u32[]{:S(2)}) collective-permute-start(f32[256,128]{1,0:T(8,128)S(1)} %get-tuple-element.79), channel_id=1, source_target_pairs={{0,6},{2,4},{4,2},{6,0},{1,7},{3,5},{5,3},{7,1},{8,14},{10,12},{12... | collective-permute-start | bytes 393224 | tf_op jit(solution)/shard_map/ppermute | solution.py:383

commit v14 on v10

--- a/solution.py
+++ b/solution.py
@@ -12,7 +12,7 @@
 
 GRAD_WEIGHT = 0.0625
 PLANE = ("half", "col", "core")
-EIGHT, FOUR = (4, 2, 5, 3, 6, 7, 1, 0), (2, 1, 3, 0)
+EIGHT, BACK, FOUR = (4, 2, 5, 3, 6, 7, 1, 0), (1, 4, 2, 5, 3, 6, 7, 0), (2, 1, 3, 0)
 VMEM_LIMIT = 24 * 1024 * 1024
 
 
@@ -148,19 +148,14 @@
     return copies
 
 
-def deal_kernel(where, offsets, sibling, block, measured, *refs):
+def deal_kernel(where, offsets, block, measured, *refs):
     outs, given, sems = refs[:4], refs[4], refs[5]
-    mine, core = 2 * where[0] + where[1], where[2]
+    mine = 2 * where[0] + where[1]
     rows, cols = block.shape[1:]
     pairs = [(block.at[jnp.bitwise_xor(mine, turn)], out.at[pl.ds(0, rows)]) for turn, out in zip(FOUR, outs)]
     copies = fetch([*pairs, (measured.at[0, 1 - where[0]], given)], sems)
-    lines = []
-    for holder in range(2):
-        for slot in range(2):
-            for axis in range(2):
-                value = jnp.where(core == holder, offsets[0, slot, axis], sibling[0, slot, axis])
-                lines.append(jnp.full((1, cols), value, jnp.int32))
-    lines = jnp.concatenate(lines, axis=0).astype(jnp.float32)
+    lines = [jnp.full((1, cols), offsets[0, slot, axis], jnp.int32) for slot in range(2) for axis in range(2)]
+    lines = jnp.concatenate(lines * 2, axis=0).astype(jnp.float32)
     for out in outs:
         out[rows:] = lines
     for copy in copies:
@@ -174,26 +169,24 @@
         out[turn] = jnp.where(where[0] == 0, gotten[turn][:rows], gotten[2 + turn][:rows])
 
 
-def pick_kernel(where, slot_range, *refs):
+def pick_kernel(where, slot_range, offs, *refs):
     gotten, below, outs, (own, parts) = dict(zip(FOUR, refs)), refs[4], refs[5:13], refs[13:]
     rows, cols = outs[0].shape
     half, col, core = where[0], where[1], where[2]
     mine = 2 * half + col
     for turn in range(4):
-        own[jnp.bitwise_xor(mine, turn)] = gotten[turn][...]
+        own[jnp.bitwise_xor(mine, turn)] = gotten[turn][:rows]
     split_at = slot_range[0, 1 - half]
-    row_ids = lax.broadcasted_iota(jnp.int32, (rows, cols), 0).astype(jnp.float32)
-    col_ids = (lax.broadcasted_iota(jnp.int32, (rows, cols), 1) + core * cols).astype(jnp.float32)
+    row_ids = lax.broadcasted_iota(jnp.int32, (rows, cols), 0)
+    col_ids = lax.broadcasted_iota(jnp.int32, (rows, cols), 1) + core * cols
     for place, slot in enumerate(receivers()):
-        lower = jnp.where(slot >= split_at, 1, 0)
-        at = rows + 2 * (slot % 4)
-        offs = own[2 * lower + slot // 4, at : at + 2]
-        upper_rows = row_ids >= offs[0:1]
-        left_cols = col_ids >= offs[1:2]
+        lower, row_at, col_at = slot_place(offs, mine, split_at, slot)
+        upper_rows = row_ids >= row_at
+        left_cols = col_ids >= col_at
 
         def merged(side, lower=lower, upper_rows=upper_rows):
-            second = own[2 + side, :rows]
-            top = jnp.where(lower == 1, second, own[side, :rows])
+            second = own[2 + side]
+            top = jnp.where(lower == 1, second, own[side])
             bottom = jnp.where(lower == 1, below[jnp.bitwise_xor(col, side)], second)
             return jnp.where(upper_rows, top, bottom)
 
@@ -230,7 +223,7 @@
 
 def position_kernel(where, slot_range, offs, *refs):
     gotten, (probe, target, tabs, factors) = dict(zip(EIGHT, refs)), refs[8:12]
-    outs, patch, grad = refs[12:20], refs[20], refs[21]
+    outs, keep, (patch, grad, bands) = refs[12:20], refs[20], refs[21:]
     half, col, core = where[0], where[1], where[2]
     mine = 2 * half + col
     flat = 2 * mine + core
@@ -244,8 +237,8 @@
         return jnp.concatenate([patch[2 * plane], patch[2 * plane + 1]], axis=1)
 
     def store(plane, value):
-        grad[2 * plane, :width] = value[:, :lanes]
-        grad[2 * plane + 1, :width] = value[:, lanes:]
+        grad[2 * plane] = value[:, :lanes]
+        grad[2 * plane + 1] = value[:, lanes:]
 
     wave_re, wave_im = probe[0], probe[1]
     o0_re, o0_im, o1_re, o1_im = load(0), load(2), load(1), load(3)
@@ -273,10 +266,22 @@
         value = roll(value, back_row, back_col)
         for step in range(4):
             rows = value[step * band : (step + 1) * band]
-            grad[4 * part + step, width : width + band] = rows[:, :lanes]
-            grad[4 * part + step, width + band :] = rows[:, lanes:]
-    for turn, out in zip(EIGHT, outs):
-        out[...] = grad[jnp.bitwise_xor(flat, turn)]
+            bands[4 * part + step, :band] = rows[:, :lanes]
+            bands[4 * part + step, band:] = rows[:, lanes:]
+    for turn, out in zip(BACK, outs):
+        out[:width] = grad[jnp.bitwise_xor(flat, turn)]
+    for part in range(4):
+        keep[part] = bands[2 * part + core]
+        start = width + 2 * band * part
+        outs[0][start : start + 2 * band] = bands[2 * part + 1 - core]
+
+
+def pair_kernel(where, keep, got, *outs):
+    band = keep.shape[1]
+    first = got.shape[0] - 4 * band
+    for turn, out in zip(FOUR, outs):
+        part = jnp.bitwise_xor(2 * where[0] + where[1], turn)
+        out[...] = keep[part] + got[pl.ds(pl.multiple_of(first + band * part, band), band)]
 
 
 def add_parts(where, slot_range, offs, parts, strip, rows, cols):
@@ -285,7 +290,7 @@
     row_ids = lax.broadcasted_iota(jnp.int32, (rows, cols), 0)
     col_ids = lax.broadcasted_iota(jnp.int32, (rows, cols), 1) + core * cols
     sums = [jnp.zeros((rows, cols), jnp.float32)] * 2
-    for turn, part in zip(EIGHT, parts):
+    for turn, part in zip(BACK, parts):
         flat = jnp.bitwise_xor(2 * mine + core, turn)
         slot = slot_of(flat // 4, (flat // 2) % 2, flat % 2)
         lower, row_at, col_at = slot_place(offs, mine, slot_range[0, 1 - half], slot)
@@ -298,14 +303,12 @@
 
 
 def add_below_kernel(where, slot_range, offs, *refs):
-    parts, (below, probe_band) = refs[:8], refs[8:]
+    parts, quarters, (below, probe_band) = refs[:8], refs[8:12], refs[12:]
     rows, cols = below.shape[1:]
     sums = add_parts(where, slot_range, offs, parts, 2, rows, cols)
     for side in range(2):
         below[jnp.bitwise_xor(where[1], side)] = sums[side]
-    total = parts[0][rows:]
-    for part in parts[1:]:
-        total = total + part[rows:]
+    total = (quarters[0][...] + quarters[1][...]) + (quarters[2][...] + quarters[3][...])
     band = probe_band.shape[0]
     probe_band[:, :cols] = total[:band]
     probe_band[:, cols:] = total[band:]
@@ -358,11 +361,9 @@
     return jax.ShapeDtypeStruct(dims, jnp.float32)
 
 
-def deal(values, axes):
-    count = len(values)
-    order = EIGHT if count == 8 else FOUR
+def deal(values, axes, order):
     return [
-        lax.ppermute(value, axes, [(k, k ^ turn) for k in range(count)]) if turn else value
+        lax.ppermute(value, axes, [(k, k ^ turn) for k in range(len(order))]) if turn else value
         for turn, value in zip(order, values)
     ]
 
@@ -387,34 +388,36 @@
     half, col, core = (lax.axis_index(name) for name in PLANE)
     where = jnp.stack([half, col, core])
 
-    sibling = lax.ppermute(offsets, "core", [(0, 1), (1, 0)])
     offsets, slot_range = (pltpu.with_memory_space_constraint(x, pltpu.HBM) for x in (offsets, slot_range))
     block = object_field.reshape(planes, rows, cols)
     *dealt, given = call(
         deal_kernel,
         [shape(rows + 8, cols)] * 4 + [shape(width, width)],
-        (where, offsets, sibling),
+        (where, offsets),
         ((block, HBM), (measured, HBM)),
         0,
         copies=5,
     )
-    own = deal(dealt, PLANE[:2])
+    own = deal(dealt, PLANE[:2], FOUR)
     (lowest,) = call(lowest_kernel, [shape(2, rows, cols)], (where,), own, 0)
     lowest, given = lax.optimization_barrier((lowest, given))
     below = lax.ppermute(lowest, "pair", [(k, k - 1) for k in range(1, pairs)])
     taken = lax.ppermute(given, "half", [(0, 1), (1, 0)])
     below, taken = lax.optimization_barrier((below, taken))
 
+    turned = dict(zip(FOUR, own))
+    offs = jnp.stack([turned[turn][rows : rows + 4, 0] for turn in range(4)]).astype(jnp.int32)
+    others = lax.ppermute(offs, "core", [(0, 1), (1, 0)])
+    offs = jnp.concatenate([jnp.where(core == 0, offs, others), jnp.where(core == 0, others, offs)], axis=1)
+    scalars = (where, slot_range, offs)
     parts = call(
         pick_kernel,
         [shape(rows, cols)] * 8,
-        (where, slot_range),
+        scalars,
         (*own, below),
         32 * rows * width,
-        [(planes, rows + 8, cols), (8, rows, cols)],
-    )
-    offs = [own[FOUR.index(turn)][rows:, 0] for turn in range(4)]
-    scalars = (where, slot_range, jnp.stack(offs).astype(jnp.int32))
+        [(planes, rows, cols), (8, rows, cols)],
+    )
     tabs, factors, order = (jnp.asarray(table) for table in tables(width))
     probe, target, tabs = call(
         ready_kernel,
@@ -425,20 +428,21 @@
         [(width, width), pltpu.VMEM(order.shape, order.dtype)],
         copies=4,
     )
-    grad = call(
+    *grad, keep = call(
         position_kernel,
-        [shape(rows + 2 * band, cols)] * 8,
+        [shape(rows + 8 * band, cols)] + [shape(rows, cols)] * 7 + [shape(4, 2 * band, cols)],
         scalars,
-        (*deal(parts, PLANE), probe, target, tabs, factors),
+        (*deal(parts, PLANE, EIGHT), probe, target, tabs, factors),
         8 * 12 * width**3,
-        [(8, rows, cols), (8, rows + 2 * band, cols)],
-    )
-    got = deal(grad, PLANE)
+        [(8, rows, cols)] * 2 + [(8, 2 * band, cols)],
+    )
+    got = deal(grad, PLANE, BACK)
+    quarters = call(pair_kernel, [shape(2 * band, cols)] * 4, (where,), (keep, got[0]), 4 * band * width)
     lower_sums, probe_band = call(
         add_below_kernel,
         [shape(2, rows, cols), shape(band, width)],
         scalars,
-        got,
+        (*got, *deal(quarters, PLANE[:2], FOUR)),
         32 * rows * width,
     )
     probe_band = sum_over(probe_band, "pair", pairs, 0)
@@ -446,7 +450,7 @@
     lower_sums, sums, probe_band = lax.optimization_barrier((lower_sums, sums, probe_band))
     above = lax.ppermute(lower_sums, "pair", [(k, k + 1) for k in range(pairs - 1)])
     sums = call(top_kernel, [shape(rows, cols)] * 4, (where,), (sums, above), planes * rows * cols)
-    sums = deal(sums, PLANE[:2])
+    sums = deal(sums, PLANE[:2], FOUR)
     probe_band = sum_over(probe_band, "pair", pairs, 1)
     probe_grad = lax.all_gather(probe_band, PLANE, axis=0, tiled=True)
     object_grad, probe_grad = call(

time: 97.8 us -> 94.9 us (0.970)
  waiting for transfers between devices: 37.3 us -> 31 us
  starting transfers between devices: 32.4 us -> 34.5 us
    ppermute x21 -> x24, waiting for transfers between devices: 26.7 us -> 20.5 us  [the longest x23 20.5 us: deal(): lax.ppermute(value, axes, [(k, k ^ turn) for k in range(len(order))])]
    ppermute x21 -> x24, starting transfers between devices: 21.3 us -> 23.3 us  [the longest x23 23.3 us: deal(): lax.ppermute(value, axes, [(k, k ^ turn) for k in range(len(order))])]
    ppermute x1, waiting for transfers between devices: 6.01 us -> 7.62 us  [local(): below = lax.ppermute(lowest, 'pair', [(k, k - 1) for k in range(1, pairs)])]
    ppermute x1, waiting for transfers between devices: 3.46 us -> 1.92 us  [local(): lax.ppermute(lower_sums, 'pair', [(k, k + 1) for k in range(pairs - 1)])]
    pallas_call x9 -> x10, Pallas kernels: 15.8 us -> 16.4 us  [call(): pl.pallas_call(kernel, out_shape=[x for x, unused in outs], in_specs=[SME...]
  transfers between devices with their start and end apart: 26 -> 29, of which waited for: 15 -> 13; matrix products, arithmetic and copies ran while one was open for 1% -> 0% of each run, Pallas kernels for 5% -> 6%
where the time goes in v14:
time: 94.9 us; the launch traced here: 93.2 us
  starting transfers between devices  34.5 us (36%)
  waiting for transfers between devices  31 us (33%)
  Pallas kernels  16.4 us (17%)
  blocking collectives  9.92 us (10%)
    ppermute x23, starting transfers between devices, deal(): lax.ppermute(value, axes, [(k, k ^ turn) for k in range(len(order))])  23.3 us
    ppermute x23, waiting for transfers between devices, deal(): lax.ppermute(value, axes, [(k, k ^ turn) for k in range(len(order))])  20.5 us
    pallas_call x10, Pallas kernels, call(): pl.pallas_call(kernel, out_shape=[x for x, unused in outs], in_specs=[SME...  16.4 us
    all_gather x1, blocking collectives, local(): probe_grad = lax.all_gather(probe_band, PLANE, axis=0, tiled=True)  9.92 us
    ppermute x1, waiting for transfers between devices, local(): below = lax.ppermute(lowest, 'pair', [(k, k - 1) for k in range(1, pairs)])  7.62 us
    ppermute x2, starting transfers between devices, sum_over(): lax.ppermute(value, axis, [(k, k ^ step) for k in range(size)])  4.55 us
    ppermute x1, starting transfers between devices, local(): lax.ppermute(lower_sums, 'pair', [(k, k + 1) for k in range(pairs - 1)])  3.75 us
    ppermute x1, waiting for transfers between devices, local(): lax.ppermute(lower_sums, 'pair', [(k, k + 1) for k in range(pairs - 1)])  1.92 us
  transfers between devices with their start and end apart: 29, of which 13 were waited for; matrix products, arithmetic and copies ran while one was open for 0% of the time, Pallas kernels for 6%

profile of v14, /device:TPU:0, one launch (start us, length us, event | category | flops | bytes accessed | tf_op | source)
XLA Modules:
  0.0 93.2 jit_solution(101671441853746547)
XLA Ops:
  0.7 2.0 %shard_map.95 = (f32[264,128]{1,0:T(8,128)S(1)}, f32[264,128]{1,0:T(8,128)S(1)}, f32[264,128]{1,0:T(8,128)S(1)}, f32[264,128]{1,0:T(8,128)S(1)}, f32[256,256]{1,0:T(8,128)S(1)}) custom-call(s32[3]{0:T(128)S(1)} %pad_add_fusion.1.where, s32[1,2,2]{2,1,0:T(2,128)} %offsets.1, f32[4,256,128]{2,1,0:T(8,128)} %bitcast.10, f32[1,2,256,256]{3,2,1,0:T(8,128)} %measured.3), custom_call_target="tpu_custom_call" | custom-call | bytes 1851392 | tf_op jit(solution)/shard_map/pallas_call | solution.py:349
  2.7 3.0 %collective-permute-start = (f32[264,128]{1,0:T(8,128)S(1)}, f32[264,128]{1,0:T(8,128)S(1)}, u32[]{:S(2)}, u32[]{:S(2)}) collective-permute-start(f32[264,128]{1,0:T(8,128)S(1)} %get-tuple-element.47), channel_id=1, source_target_pairs={{0,2},{2,0},{4,6},{6,4},{1,3},{3,1},{5,7},{7,5},{8,10},{10,8},{12,... | collective-permute-start | bytes 405512 | tf_op jit(solution)/shard_map/ppermute | solution.py:366
  5.7 1.5 %collective-permute-start.1 = (f32[264,128]{1,0:T(8,128)S(1)}, f32[264,128]{1,0:T(8,128)S(1)}, u32[]{:S(2)}, u32[]{:S(2)}) collective-permute-start(f32[264,128]{1,0:T(8,128)S(1)} %get-tuple-element.48), channel_id=1, source_target_pairs={{0,4},{2,6},{4,0},{6,2},{1,5},{3,7},{5,1},{7,3},{8,12},{10,14},{12... | collective-permute-start | bytes 405512 | tf_op jit(solution)/shard_map/ppermute | solution.py:366
  7.3 2.3 %collective-permute-done.refs_1_ = f32[264,128]{1,0:T(8,128)S(1)} collective-permute-done((f32[264,128]{1,0:T(8,128)S(1)}, f32[264,128]{1,0:T(8,128)S(1)}, u32[]{:S(2)}, u32[]{:S(2)}) %collective-permute-start) | collective-permute-done | bytes 135200 | tf_op jit(solution)/shard_map/ppermute | solution.py:366
  9.8 3.8 %collective-permute-done.1.refs_0_ = f32[264,128]{1,0:T(8,128)S(1)} collective-permute-done((f32[264,128]{1,0:T(8,128)S(1)}, f32[264,128]{1,0:T(8,128)S(1)}, u32[]{:S(2)}, u32[]{:S(2)}) %collective-permute-start.1) | collective-permute-done | bytes 135200 | tf_op jit(solution)/shard_map/ppermute | solution.py:366
  14.0 0.6 shard_map.96
  14.5 1.3 %collective-permute-start.4 = (f32[2,256,128]{2,1,0:T(8,128)S(1)}, f32[2,256,128]{2,1,0:T(8,128)S(1)}, u32[]{:S(2)}, u32[]{:S(2)}) collective-permute-start(f32[2,256,128]{2,1,0:T(8,128)S(1)} %shard_map.96), channel_id=1, source_target_pairs={{8,0},{16,8},{24,16},{9,1},{17,9},{25,17},{10,2},{18,10},{26,18},{... | collective-permute-start | bytes 786440 | tf_op jit(solution)/shard_map/ppermute | solution.py:404
  15.8 1.6 %collective-permute-start.5 = (f32[256,256]{1,0:T(8,128)S(1)}, f32[256,256]{1,0:T(8,128)S(1)}, u32[]{:S(2)}, u32[]{:S(2)}) collective-permute-start(f32[256,256]{1,0:T(8,128)S(1)} %get-tuple-element.52), channel_id=1, source_target_pairs={{0,4},{4,0},{1,5},{5,1},{2,6},{6,2},{3,7},{7,3},{8,12},{12,8},{9,1... | collective-permute-start | bytes 786440 | tf_op jit(solution)/shard_map/ppermute | solution.py:405
  17.5 7.6 %collective-permute-done.4.refs_4_ = f32[2,256,128]{2,1,0:T(8,128)S(1)} collective-permute-done((f32[2,256,128]{2,1,0:T(8,128)S(1)}, f32[2,256,128]{2,1,0:T(8,128)S(1)}, u32[]{:S(2)}, u32[]{:S(2)}) %collective-permute-start.4) | collective-permute-done | bytes 262176 | tf_op jit(solution)/shard_map/ppermute | solution.py:404
  25.1 1.4 %shard_map.97 = (f32[256,128]{1,0:T(8,128)S(1)}, f32[256,128]{1,0:T(8,128)S(1)}, f32[256,128]{1,0:T(8,128)S(1)}, f32[256,128]{1,0:T(8,128)S(1)}, f32[256,128]{1,...) custom-call(s32[3]{0:T(128)S(1)} %pad_add_fusion.1.where, ...), custom_call_target="tpu_custom_call" | custom-call | flops 2097152 | bytes 1851392 | tf_op jit(solution)/shard_map/pallas_call | solution.py:349
  26.6 1.6 %collective-permute-start.6 = (f32[256,128]{1,0:T(8,128)S(1)}, f32[256,128]{1,0:T(8,128)S(1)}, u32[]{:S(2)}, u32[]{:S(2)}) collective-permute-start(f32[256,128]{1,0:T(8,128)S(1)} %get-tuple-element.54), channel_id=1, source_target_pairs={{0,4},{1,5},{2,6},{3,7},{4,0},{5,1},{6,2},{7,3},{8,12},{9,13},{10,... | collective-permute-start | bytes 393224 | tf_op jit(solution)/shard_map/ppermute | solution.py:366
  28.2 0.5 collective-permute-start.7
  28.7 1.7 %collective-permute-start.9 = (f32[256,128]{1,0:T(8,128)S(1)}, f32[256,128]{1,0:T(8,128)S(1)}, u32[]{:S(2)}, u32[]{:S(2)}) collective-permute-start(f32[256,128]{1,0:T(8,128)S(1)} %get-tuple-element.57), channel_id=1, source_target_pairs={{0,3},{1,2},{2,1},{3,0},{4,7},{5,6},{6,5},{7,4},{8,11},{9,10},{10,... | collective-permute-start | bytes 393224 | tf_op jit(solution)/shard_map/ppermute | solution.py:366
  30.4 1.5 %collective-permute-start.10 = (f32[256,128]{1,0:T(8,128)S(1)}, f32[256,128]{1,0:T(8,128)S(1)}, u32[]{:S(2)}, u32[]{:S(2)}) collective-permute-start(f32[256,128]{1,0:T(8,128)S(1)} %get-tuple-element.58), channel_id=1, source_target_pairs={{0,6},{1,7},{2,4},{3,5},{4,2},{5,3},{6,0},{7,1},{8,14},{9,15},{10,... | collective-permute-start | bytes 393224 | tf_op jit(solution)/shard_map/ppermute | solution.py:366
  31.9 0.7 collective-permute-start.11
  32.6 2.0 %collective-permute-done.7.refs_1_ = f32[256,128]{1,0:T(8,128)S(1)} collective-permute-done((f32[256,128]{1,0:T(8,128)S(1)}, f32[256,128]{1,0:T(8,128)S(1)}, u32[]{:S(2)}, u32[]{:S(2)}) %collective-permute-start.7) | collective-permute-done | bytes 131104 | tf_op jit(solution)/shard_map/ppermute | solution.py:366
  34.6 2.7 %shard_map.98 = (f32[2,256,256]{2,1,0:T(8,128)S(1)}, f32[256,256]{1,0:T(8,128)S(1)}, bf16[6,512,256]{2,1,0:T(8,128)(2,1)S(1)}) custom-call(s32[3]{0:T(128)S(1)} %pad_add_fusion.1.where, s32[1,2]{1,0:T(1,128)} %slot_range.9, s32[4,8]{1,0:T(4,128)S(1)} %pad_add_fusion.offs, f32[256,256]{1,0:T(8,128)S(1)} %collective-permute-done.5.taken, ...), custom_call_target="tpu_custom_call" | custom-call | flops 201326592 | bytes 5505024 | tf_op jit(solution)/shard_map/pallas_call | solution.py:349
  37.3 1.9 %collective-permute-done.10.refs_4_ = f32[256,128]{1,0:T(8,128)S(1)} collective-permute-done((f32[256,128]{1,0:T(8,128)S(1)}, f32[256,128]{1,0:T(8,128)S(1)}, u32[]{:S(2)}, u32[]{:S(2)}) %collective-permute-start.10) | collective-permute-done | bytes 131104 | tf_op jit(solution)/shard_map/ppermute | solution.py:366
  39.2 1.9 %collective-permute-done.11.refs_5_ = f32[256,128]{1,0:T(8,128)S(1)} collective-permute-done((f32[256,128]{1,0:T(8,128)S(1)}, f32[256,128]{1,0:T(8,128)S(1)}, u32[]{:S(2)}, u32[]{:S(2)}) %collective-permute-start.11) | collective-permute-done | bytes 131104 | tf_op jit(solution)/shard_map/ppermute | solution.py:366
  41.1 4.3 %shard_map.99 = (f32[768,128]{1,0:T(8,128)S(1)}, f32[256,128]{1,0:T(8,128)S(1)}, f32[256,128]{1,0:T(8,128)S(1)}, f32[256,128]{1,0:T(8,128)S(1)}, f32[256,128]{1,...) custom-call(s32[3]{0:T(128)S(1)} %pad_add_fusion.1.where, ...), custom_call_target="tpu_custom_call" | custom-call | flops 1610612736 | bytes 5120000 | tf_op jit(solution)/shard_map/pallas_call | solution.py:349
  45.3 0.4 collective-permute-start.13
  45.7 1.5 %collective-permute-start.14 = (f32[256,128]{1,0:T(8,128)S(1)}, f32[256,128]{1,0:T(8,128)S(1)}, u32[]{:S(2)}, u32[]{:S(2)}) collective-permute-start(f32[256,128]{1,0:T(8,128)S(1)} %get-tuple-element.67), channel_id=1, source_target_pairs={{0,4},{1,5},{2,6},{3,7},{4,0},{5,1},{6,2},{7,3},{8,12},{9,13},{10,... | collective-permute-start | bytes 393224 | tf_op jit(solution)/shard_map/ppermute | solution.py:366
  47.2 0.6 collective-permute-start.15
  47.7 0.2 collective-permute-start.16
  47.9 1.5 %collective-permute-start.17 = (f32[256,128]{1,0:T(8,128)S(1)}, f32[256,128]{1,0:T(8,128)S(1)}, u32[]{:S(2)}, u32[]{:S(2)}) collective-permute-start(f32[256,128]{1,0:T(8,128)S(1)} %get-tuple-element.70), channel_id=1, source_target_pairs={{0,3},{1,2},{2,1},{3,0},{4,7},{5,6},{6,5},{7,4},{8,11},{9,10},{10,... | collective-permute-start | bytes 393224 | tf_op jit(solution)/shard_map/ppermute | solution.py:366
  49.5 2.3 %collective-permute-done.14.refs_1_ = f32[256,128]{1,0:T(8,128)S(1)} collective-permute-done((f32[256,128]{1,0:T(8,128)S(1)}, f32[256,128]{1,0:T(8,128)S(1)}, u32[]{:S(2)}, u32[]{:S(2)}) %collective-permute-start.14) | collective-permute-done | bytes 131104 | tf_op jit(solution)/shard_map/ppermute | solution.py:366
  51.8 1.5 %collective-permute-start.18 = (f32[256,128]{1,0:T(8,128)S(1)}, f32[256,128]{1,0:T(8,128)S(1)}, u32[]{:S(2)}, u32[]{:S(2)}) collective-permute-start(f32[256,128]{1,0:T(8,128)S(1)} %get-tuple-element.71), channel_id=1, source_target_pairs={{0,6},{1,7},{2,4},{3,5},{4,2},{5,3},{6,0},{7,1},{8,14},{9,15},{10,... | collective-permute-start | bytes 393224 | tf_op jit(solution)/shard_map/ppermute | solution.py:366
  53.3 0.6 shard_map.100
  53.9 0.9 collective-permute-start.20
  54.8 1.2 %collective-permute-start.21 = (f32[128,128]{1,0:T(8,128)S(1)}, f32[128,128]{1,0:T(8,128)S(1)}, u32[]{:S(2)}, u32[]{:S(2)}) collective-permute-start(f32[128,128]{1,0:T(8,128)S(1)} %get-tuple-element.76), channel_id=1, source_target_pairs={{0,2},{2,0},{4,6},{6,4},{1,3},{3,1},{5,7},{7,5},{8,10},{10,8},{12,... | collective-permute-start | bytes 196616 | tf_op jit(solution)/shard_map/ppermute | solution.py:366
  56.0 1.5 %collective-permute-start.22 = (f32[128,128]{1,0:T(8,128)S(1)}, f32[128,128]{1,0:T(8,128)S(1)}, u32[]{:S(2)}, u32[]{:S(2)}) collective-permute-start(f32[128,128]{1,0:T(8,128)S(1)} %get-tuple-element.77), channel_id=1, source_target_pairs={{0,6},{2,4},{4,2},{6,0},{1,7},{3,5},{5,3},{7,1},{8,14},{10,12},{12... | collective-permute-start | bytes 196616 | tf_op jit(solution)/shard_map/ppermute | solution.py:366
  57.5 1.6 %collective-permute-done.18.refs_5_ = f32[256,128]{1,0:T(8,128)S(1)} collective-permute-done((f32[256,128]{1,0:T(8,128)S(1)}, f32[256,128]{1,0:T(8,128)S(1)}, u32[]{:S(2)}, u32[]{:S(2)}) %collective-permute-start.18) | collective-permute-done | bytes 131104 | tf_op jit(solution)/shard_map/ppermute | solution.py:366
  59.1 1.0 %collective-permute-done.19.refs_6_ = f32[256,128]{1,0:T(8,128)S(1)} collective-permute-done((f32[256,128]{1,0:T(8,128)S(1)}, f32[256,128]{1,0:T(8,128)S(1)}, u32[]{:S(2)}, u32[]{:S(2)}) %collective-permute-start.19) | collective-permute-done | bytes 131104 | tf_op jit(solution)/shard_map/ppermute | solution.py:366
  60.1 2.9 %collective-permute-done.20.refs_8_ = f32[128,128]{1,0:T(8,128)S(1)} collective-permute-done((f32[128,128]{1,0:T(8,128)S(1)}, f32[128,128]{1,0:T(8,128)S(1)}, u32[]{:S(2)}, u32[]{:S(2)}) %collective-permute-start.20) | collective-permute-done | bytes 65568 | tf_op jit(solution)/shard_map/ppermute | solution.py:366
  63.0 0.8 collective-permute-done.22.refs_10_
  63.8 1.1 %shard_map.101 = (f32[2,256,128]{2,1,0:T(8,128)S(1)}, f32[64,256]{1,0:T(8,128)S(1)}) custom-call(s32[3]{0:T(128)S(1)} %pad_add_fusion.1.where, s32[1,2]{1,0:T(1,128)} %slot_range.9, s32[4,8]{1,0:T(4,128)S(1)} %pad_add_fusion.offs, f32[768,128]{1,0:T(8,128)S(1)} %collective-permute-done.13.got.refs_0_, f32[256,128]{1,0:T(8,128)S(1)} %collective-permute-done.14.refs_1_, ...), custom_call_target="tpu_custom_call" | custom-call | flops 2097152 | bytes 1900544 | tf_op jit(solution)/shard_map/pallas_call | solution.py:349
  64.9 1.9 %collective-permute-start.23 = (f32[64,256]{1,0:T(8,128)S(1)}, f32[64,256]{1,0:T(8,128)S(1)}, u32[]{:S(2)}, u32[]{:S(2)}) collective-permute-start(f32[64,256]{1,0:T(8,128)S(1)} %get-tuple-element.80), channel_id=1, source_target_pairs={{0,8},{8,0},{16,24},{24,16},{1,9},{9,1},{17,25},{25,17},{2,10},{10... | collective-permute-start | bytes 196616 | tf_op jit(solution)/shard_map/ppermute | solution.py:376
  66.8 1.6 %shard_map.102.own = f32[4,256,128]{2,1,0:T(8,128)S(1)} custom-call(s32[3]{0:T(128)S(1)} %pad_add_fusion.1.where, s32[1,2]{1,0:T(1,128)} %slot_range.9, s32[4,8]{1,0:T(4,128)S(1)} %pad_add_fusion.offs, f32[768,128]{1,0:T(8,128)S(1)} %collective-permute-done.13.got.refs_0_, f32[256,128]{1,0:T(8,128)S(1)} %collective-permute-done.14.refs_1_, ...), custom_call_target="tpu_custom_call" | custom-call | flops 4194304 | bytes 1835008 | tf_op jit(solution)/shard_map/pallas_call | solution.py:349
  68.3 0.9 collective-permute-done.23
  69.2 3.8 %collective-permute-start.24 = (f32[2,256,128]{2,1,0:T(8,128)S(1)}, f32[2,256,128]{2,1,0:T(8,128)S(1)}, u32[]{:S(2)}, u32[]{:S(2)}) collective-permute-start(f32[2,256,128]{2,1,0:T(8,128)S(1)} %get-tuple-element.82), channel_id=1, source_target_pairs={{0,8},{8,16},{16,24},{1,9},{9,17},{17,25},{2,10},{10,18},{18,26},{... | collective-permute-start | bytes 786440 | tf_op jit(solution)/shard_map/ppermute | solution.py:451
  73.0 2.7 %collective-permute-start.28 = (f32[64,256]{1,0:T(8,128)S(1)}, f32[64,256]{1,0:T(8,128)S(1)}, u32[]{:S(2)}, u32[]{:S(2)}) collective-permute-start(f32[64,256]{1,0:T(8,128)S(1)} %add.6), channel_id=1, source_target_pairs={{0,16},{8,24},{16,0},{24,8},{1,17},{9,25},{17,1},{25,9},{2,18},{10... | collective-permute-start | bytes 196616 | tf_op jit(solution)/shard_map/ppermute | solution.py:376
  75.6 1.9 %collective-permute-done.24.above = f32[2,256,128]{2,1,0:T(8,128)S(1)} collective-permute-done((f32[2,256,128]{2,1,0:T(8,128)S(1)}, f32[2,256,128]{2,1,0:T(8,128)S(1)}, u32[]{:S(2)}, u32[]{:S(2)}) %collective-permute-start.24) | collective-permute-done | bytes 262176 | tf_op jit(solution)/shard_map/ppermute | solution.py:451
  77.6 0.6 shard_map.103
  78.2 1.4 %collective-permute-start.25 = (f32[256,128]{1,0:T(8,128)S(1)}, f32[256,128]{1,0:T(8,128)S(1)}, u32[]{:S(2)}, u32[]{:S(2)}) collective-permute-start(f32[256,128]{1,0:T(8,128)S(1)} %get-tuple-element.83), channel_id=1, source_target_pairs={{0,4},{2,6},{4,0},{6,2},{1,5},{3,7},{5,1},{7,3},{8,12},{10,14},{12... | collective-permute-start | bytes 393224 | tf_op jit(solution)/shard_map/ppermute | solution.py:366
  79.5 0.7 collective-permute-start.26
  80.2 1.5 %collective-permute-start.27 = (f32[256,128]{1,0:T(8,128)S(1)}, f32[256,128]{1,0:T(8,128)S(1)}, u32[]{:S(2)}, u32[]{:S(2)}) collective-permute-start(f32[256,128]{1,0:T(8,128)S(1)} %get-tuple-element.85), channel_id=1, source_target_pairs={{0,6},{2,4},{4,2},{6,0},{1,7},{3,5},{5,3},{7,1},{8,14},{10,12},{12... | collective-permute-start | bytes 393224 | tf_op jit(solution)/shard_map/ppermute | solution.py:366
  81.7 9.9 %all_gather.3.refs_4_ = f32[512,256]{1,0:T(8,128)S(1)} all-gather(f32[64,256]{1,0:T(8,128)S(1)} %add.7), channel_id=1, replica_groups=mesh['pair'=4,'half'=2,'col'=2,'core'=2] {'half','col','core'}, dimensions={0}, use_global_device_ids=true | all-gather | bytes 589824 | tf_op jit(solution)/shard_map/all_gather | solution.py:455
  91.7 1.5 %shard_map.104 = (f32[4,256,128]{2,1,0:T(8,128)}, f32[512,256]{1,0:T(8,128)}) custom-call(s32[3]{0:T(128)S(1)} %pad_add_fusion.1.where, f32[256,128]{1,0:T(8,128)S(1)} %collective-permute-done.25.refs_0_, f32[256,128]{1,0:T(8,128)S(1)} %collective-permute-done.26.refs_1_, f32[256,128]{1,0:T(8,128)S(1)} %collective-permute-done.27.refs_2_, ...), custom_call_target="tpu_custom_call" | custom-call | bytes 2097152 | tf_op jit(solution)/shard_map/pallas_call | solution.py:349
  (33 shorter events, 0.8 us)
Async XLA Ops:
  2.7 7.0 %collective-permute-start = (f32[264,128]{1,0:T(8,128)S(1)}, f32[264,128]{1,0:T(8,128)S(1)}, u32[]{:S(2)}, u32[]{:S(2)}) collective-permute-start(f32[264,128]{1,0:T(8,128)S(1)} %get-tuple-element.47), channel_id=1, source_target_pairs={{0,2},{2,0},{4,6},{6,4},{1,3},{3,1},{5,7},{7,5},{8,10},{10,8},{12,... | collective-permute-start | bytes 405512 | tf_op jit(solution)/shard_map/ppermute | solution.py:366
  5.7 7.9 %collective-permute-start.1 = (f32[264,128]{1,0:T(8,128)S(1)}, f32[264,128]{1,0:T(8,128)S(1)}, u32[]{:S(2)}, u32[]{:S(2)}) collective-permute-start(f32[264,128]{1,0:T(8,128)S(1)} %get-tuple-element.48), channel_id=1, source_target_pairs={{0,4},{2,6},{4,0},{6,2},{1,5},{3,7},{5,1},{7,3},{8,12},{10,14},{12... | collective-permute-start | bytes 405512 | tf_op jit(solution)/shard_map/ppermute | solution.py:366
  7.2 6.5 %collective-permute-start.2 = (f32[264,128]{1,0:T(8,128)S(1)}, f32[264,128]{1,0:T(8,128)S(1)}, u32[]{:S(2)}, u32[]{:S(2)}) collective-permute-start(f32[264,128]{1,0:T(8,128)S(1)} %get-tuple-element.49), channel_id=1, source_target_pairs={{0,6},{2,4},{4,2},{6,0},{1,7},{3,5},{5,3},{7,1},{8,14},{10,12},{12... | collective-permute-start | bytes 405512 | tf_op jit(solution)/shard_map/ppermute | solution.py:366
  13.9 3.5 %collective-permute-start.3 = (s32[4,4]{1,0:T(4,128)S(1)}, s32[4,4]{1,0:T(4,128)S(1)}, u32[]{:S(2)}, u32[]{:S(2)}) collective-permute-start(s32[4,4]{1,0:T(4,128)S(1)} %maximum_convert_fusion), channel_id=1, source_target_pairs={{0,1},{1,0},{2,3},{3,2},{4,5},{5,4},{6,7},{7,6},{8,9},{9,8},{10,11... | collective-permute-start | bytes 200 | tf_op jit(solution)/shard_map/ppermute | solution.py:410
  14.5 10.6 %collective-permute-start.4 = (f32[2,256,128]{2,1,0:T(8,128)S(1)}, f32[2,256,128]{2,1,0:T(8,128)S(1)}, u32[]{:S(2)}, u32[]{:S(2)}) collective-permute-start(f32[2,256,128]{2,1,0:T(8,128)S(1)} %shard_map.96), channel_id=1, source_target_pairs={{8,0},{16,8},{24,16},{9,1},{17,9},{25,17},{10,2},{18,10},{26,18},{... | collective-permute-start | bytes 786440 | tf_op jit(solution)/shard_map/ppermute | solution.py:404
  15.8 9.3 %collective-permute-start.5 = (f32[256,256]{1,0:T(8,128)S(1)}, f32[256,256]{1,0:T(8,128)S(1)}, u32[]{:S(2)}, u32[]{:S(2)}) collective-permute-start(f32[256,256]{1,0:T(8,128)S(1)} %get-tuple-element.52), channel_id=1, source_target_pairs={{0,4},{4,0},{1,5},{5,1},{2,6},{6,2},{3,7},{7,3},{8,12},{12,8},{9,1... | collective-permute-start | bytes 786440 | tf_op jit(solution)/shard_map/ppermute | solution.py:405
  26.6 5.3 %collective-permute-start.6 = (f32[256,128]{1,0:T(8,128)S(1)}, f32[256,128]{1,0:T(8,128)S(1)}, u32[]{:S(2)}, u32[]{:S(2)}) collective-permute-start(f32[256,128]{1,0:T(8,128)S(1)} %get-tuple-element.54), channel_id=1, source_target_pairs={{0,4},{1,5},{2,6},{3,7},{4,0},{5,1},{6,2},{7,3},{8,12},{9,13},{10,... | collective-permute-start | bytes 393224 | tf_op jit(solution)/shard_map/ppermute | solution.py:366
  28.2 6.4 %collective-permute-start.7 = (f32[256,128]{1,0:T(8,128)S(1)}, f32[256,128]{1,0:T(8,128)S(1)}, u32[]{:S(2)}, u32[]{:S(2)}) collective-permute-start(f32[256,128]{1,0:T(8,128)S(1)} %get-tuple-element.55), channel_id=1, source_target_pairs={{0,2},{1,3},{2,0},{3,1},{4,6},{5,7},{6,4},{7,5},{8,10},{9,11},{10,... | collective-permute-start | bytes 393224 | tf_op jit(solution)/shard_map/ppermute | solution.py:366
  28.7 8.6 %collective-permute-start.8 = (f32[256,128]{1,0:T(8,128)S(1)}, f32[256,128]{1,0:T(8,128)S(1)}, u32[]{:S(2)}, u32[]{:S(2)}) collective-permute-start(f32[256,128]{1,0:T(8,128)S(1)} %get-tuple-element.56), channel_id=1, source_target_pairs={{0,5},{1,4},{2,7},{3,6},{4,1},{5,0},{6,3},{7,2},{8,13},{9,12},{10,... | collective-permute-start | bytes 393224 | tf_op jit(solution)/shard_map/ppermute | solution.py:366
  28.7 8.6 %collective-permute-start.9 = (f32[256,128]{1,0:T(8,128)S(1)}, f32[256,128]{1,0:T(8,128)S(1)}, u32[]{:S(2)}, u32[]{:S(2)}) collective-permute-start(f32[256,128]{1,0:T(8,128)S(1)} %get-tuple-element.57), channel_id=1, source_target_pairs={{0,3},{1,2},{2,1},{3,0},{4,7},{5,6},{6,5},{7,4},{8,11},{9,10},{10,... | collective-permute-start | bytes 393224 | tf_op jit(solution)/shard_map/ppermute | solution.py:366
  30.4 8.7 %collective-permute-start.10 = (f32[256,128]{1,0:T(8,128)S(1)}, f32[256,128]{1,0:T(8,128)S(1)}, u32[]{:S(2)}, u32[]{:S(2)}) collective-permute-start(f32[256,128]{1,0:T(8,128)S(1)} %get-tuple-element.58), channel_id=1, source_target_pairs={{0,6},{1,7},{2,4},{3,5},{4,2},{5,3},{6,0},{7,1},{8,14},{9,15},{10,... | collective-permute-start | bytes 393224 | tf_op jit(solution)/shard_map/ppermute | solution.py:366
  31.9 9.1 %collective-permute-start.11 = (f32[256,128]{1,0:T(8,128)S(1)}, f32[256,128]{1,0:T(8,128)S(1)}, u32[]{:S(2)}, u32[]{:S(2)}) collective-permute-start(f32[256,128]{1,0:T(8,128)S(1)} %get-tuple-element.59), channel_id=1, source_target_pairs={{0,7},{1,6},{2,5},{3,4},{4,3},{5,2},{6,1},{7,0},{8,15},{9,14},{10,... | collective-permute-start | bytes 393224 | tf_op jit(solution)/shard_map/ppermute | solution.py:366
  34.5 6.5 %copy-start = (f32[2,136,128]{2,1,0:T(8,128)S(1)}, f32[2,136,128]{2,1,0:T(8,128)}, u32[]{:S(2)}) copy-start(f32[2,136,128]{2,1,0:T(8,128)} %constant.19.clone.refs_11_) | copy-start | bytes 417796
  34.6 6.5 %collective-permute-start.12 = (f32[256,128]{1,0:T(8,128)S(1)}, f32[256,128]{1,0:T(8,128)S(1)}, u32[]{:S(2)}, u32[]{:S(2)}) collective-permute-start(f32[256,128]{1,0:T(8,128)S(1)} %get-tuple-element.60), channel_id=1, source_target_pairs={{0,1},{1,0},{2,3},{3,2},{4,5},{5,4},{6,7},{7,6},{8,9},{9,8},{10,11... | collective-permute-start | bytes 393224 | tf_op jit(solution)/shard_map/ppermute | solution.py:366
  45.3 8.0 %collective-permute-start.13 = (f32[768,128]{1,0:T(8,128)S(1)}, f32[768,128]{1,0:T(8,128)S(1)}, u32[]{:S(2)}, u32[]{:S(2)}) collective-permute-start(f32[768,128]{1,0:T(8,128)S(1)} %get-tuple-element.66), channel_id=1, source_target_pairs={{0,1},{1,0},{2,3},{3,2},{4,5},{5,4},{6,7},{7,6},{8,9},{9,8},{10,11... | collective-permute-start | bytes 1179656 | tf_op jit(solution)/shard_map/ppermute | solution.py:366
  45.7 6.1 %collective-permute-start.14 = (f32[256,128]{1,0:T(8,128)S(1)}, f32[256,128]{1,0:T(8,128)S(1)}, u32[]{:S(2)}, u32[]{:S(2)}) collective-permute-start(f32[256,128]{1,0:T(8,128)S(1)} %get-tuple-element.67), channel_id=1, source_target_pairs={{0,4},{1,5},{2,6},{3,7},{4,0},{5,1},{6,2},{7,3},{8,12},{9,13},{10,... | collective-permute-start | bytes 393224 | tf_op jit(solution)/shard_map/ppermute | solution.py:366
  47.2 6.7 %collective-permute-start.15 = (f32[256,128]{1,0:T(8,128)S(1)}, f32[256,128]{1,0:T(8,128)S(1)}, u32[]{:S(2)}, u32[]{:S(2)}) collective-permute-start(f32[256,128]{1,0:T(8,128)S(1)} %get-tuple-element.68), channel_id=1, source_target_pairs={{0,2},{1,3},{2,0},{3,1},{4,6},{5,7},{6,4},{7,5},{8,10},{9,11},{10,... | collective-permute-start | bytes 393224 | tf_op jit(solution)/shard_map/ppermute | solution.py:366
  47.7 7.1 %collective-permute-start.16 = (f32[256,128]{1,0:T(8,128)S(1)}, f32[256,128]{1,0:T(8,128)S(1)}, u32[]{:S(2)}, u32[]{:S(2)}) collective-permute-start(f32[256,128]{1,0:T(8,128)S(1)} %get-tuple-element.69), channel_id=1, source_target_pairs={{0,5},{1,4},{2,7},{3,6},{4,1},{5,0},{6,3},{7,2},{8,13},{9,12},{10,... | collective-permute-start | bytes 393224 | tf_op jit(solution)/shard_map/ppermute | solution.py:366
  47.9 8.0 %collective-permute-start.17 = (f32[256,128]{1,0:T(8,128)S(1)}, f32[256,128]{1,0:T(8,128)S(1)}, u32[]{:S(2)}, u32[]{:S(2)}) collective-permute-start(f32[256,128]{1,0:T(8,128)S(1)} %get-tuple-element.70), channel_id=1, source_target_pairs={{0,3},{1,2},{2,1},{3,0},{4,7},{5,6},{6,5},{7,4},{8,11},{9,10},{10,... | collective-permute-start | bytes 393224 | tf_op jit(solution)/shard_map/ppermute | solution.py:366
  51.8 7.3 %collective-permute-start.18 = (f32[256,128]{1,0:T(8,128)S(1)}, f32[256,128]{1,0:T(8,128)S(1)}, u32[]{:S(2)}, u32[]{:S(2)}) collective-permute-start(f32[256,128]{1,0:T(8,128)S(1)} %get-tuple-element.71), channel_id=1, source_target_pairs={{0,6},{1,7},{2,4},{3,5},{4,2},{5,3},{6,0},{7,1},{8,14},{9,15},{10,... | collective-permute-start | bytes 393224 | tf_op jit(solution)/shard_map/ppermute | solution.py:366
  53.3 6.8 %collective-permute-start.19 = (f32[256,128]{1,0:T(8,128)S(1)}, f32[256,128]{1,0:T(8,128)S(1)}, u32[]{:S(2)}, u32[]{:S(2)}) collective-permute-start(f32[256,128]{1,0:T(8,128)S(1)} %get-tuple-element.72), channel_id=1, source_target_pairs={{0,7},{1,6},{2,5},{3,4},{4,3},{5,2},{6,1},{7,0},{8,15},{9,14},{10,... | collective-permute-start | bytes 393224 | tf_op jit(solution)/shard_map/ppermute | solution.py:366
  53.9 9.0 %collective-permute-start.20 = (f32[128,128]{1,0:T(8,128)S(1)}, f32[128,128]{1,0:T(8,128)S(1)}, u32[]{:S(2)}, u32[]{:S(2)}) collective-permute-start(f32[128,128]{1,0:T(8,128)S(1)} %get-tuple-element.75), channel_id=1, source_target_pairs={{0,4},{2,6},{4,0},{6,2},{1,5},{3,7},{5,1},{7,3},{8,12},{10,14},{12... | collective-permute-start | bytes 196616 | tf_op jit(solution)/shard_map/ppermute | solution.py:366
  54.8 8.2 %collective-permute-start.21 = (f32[128,128]{1,0:T(8,128)S(1)}, f32[128,128]{1,0:T(8,128)S(1)}, u32[]{:S(2)}, u32[]{:S(2)}) collective-permute-start(f32[128,128]{1,0:T(8,128)S(1)} %get-tuple-element.76), channel_id=1, source_target_pairs={{0,2},{2,0},{4,6},{6,4},{1,3},{3,1},{5,7},{7,5},{8,10},{10,8},{12,... | collective-permute-start | bytes 196616 | tf_op jit(solution)/shard_map/ppermute | solution.py:366
  56.0 7.8 %collective-permute-start.22 = (f32[128,128]{1,0:T(8,128)S(1)}, f32[128,128]{1,0:T(8,128)S(1)}, u32[]{:S(2)}, u32[]{:S(2)}) collective-permute-start(f32[128,128]{1,0:T(8,128)S(1)} %get-tuple-element.77), channel_id=1, source_target_pairs={{0,6},{2,4},{4,2},{6,0},{1,7},{3,5},{5,3},{7,1},{8,14},{10,12},{12... | collective-permute-start | bytes 196616 | tf_op jit(solution)/shard_map/ppermute | solution.py:366
  64.9 4.3 %collective-permute-start.23 = (f32[64,256]{1,0:T(8,128)S(1)}, f32[64,256]{1,0:T(8,128)S(1)}, u32[]{:S(2)}, u32[]{:S(2)}) collective-permute-start(f32[64,256]{1,0:T(8,128)S(1)} %get-tuple-element.80), channel_id=1, source_target_pairs={{0,8},{8,0},{16,24},{24,16},{1,9},{9,1},{17,25},{25,17},{2,10},{10... | collective-permute-start | bytes 196616 | tf_op jit(solution)/shard_map/ppermute | solution.py:376
  69.2 8.3 %collective-permute-start.24 = (f32[2,256,128]{2,1,0:T(8,128)S(1)}, f32[2,256,128]{2,1,0:T(8,128)S(1)}, u32[]{:S(2)}, u32[]{:S(2)}) collective-permute-start(f32[2,256,128]{2,1,0:T(8,128)S(1)} %get-tuple-element.82), channel_id=1, source_target_pairs={{0,8},{8,16},{16,24},{1,9},{9,17},{17,25},{2,10},{10,18},{18,26},{... | collective-permute-start | bytes 786440 | tf_op jit(solution)/shard_map/ppermute | solution.py:451
  73.0 8.7 %collective-permute-start.28 = (f32[64,256]{1,0:T(8,128)S(1)}, f32[64,256]{1,0:T(8,128)S(1)}, u32[]{:S(2)}, u32[]{:S(2)}) collective-permute-start(f32[64,256]{1,0:T(8,128)S(1)} %add.6), channel_id=1, source_target_pairs={{0,16},{8,24},{16,0},{24,8},{1,17},{9,25},{17,1},{25,9},{2,18},{10... | collective-permute-start | bytes 196616 | tf_op jit(solution)/shard_map/ppermute | solution.py:376
  78.2 13.5 %collective-permute-start.25 = (f32[256,128]{1,0:T(8,128)S(1)}, f32[256,128]{1,0:T(8,128)S(1)}, u32[]{:S(2)}, u32[]{:S(2)}) collective-permute-start(f32[256,128]{1,0:T(8,128)S(1)} %get-tuple-element.83), channel_id=1, source_target_pairs={{0,4},{2,6},{4,0},{6,2},{1,5},{3,7},{5,1},{7,3},{8,12},{10,14},{12... | collective-permute-start | bytes 393224 | tf_op jit(solution)/shard_map/ppermute | solution.py:366
  79.5 12.1 %collective-permute-start.26 = (f32[256,128]{1,0:T(8,128)S(1)}, f32[256,128]{1,0:T(8,128)S(1)}, u32[]{:S(2)}, u32[]{:S(2)}) collective-permute-start(f32[256,128]{1,0:T(8,128)S(1)} %get-tuple-element.84), channel_id=1, source_target_pairs={{0,2},{2,0},{4,6},{6,4},{1,3},{3,1},{5,7},{7,5},{8,10},{10,8},{12,... | collective-permute-start | bytes 393224 | tf_op jit(solution)/shard_map/ppermute | solution.py:366
  80.2 11.4 %collective-permute-start.27 = (f32[256,128]{1,0:T(8,128)S(1)}, f32[256,128]{1,0:T(8,128)S(1)}, u32[]{:S(2)}, u32[]{:S(2)}) collective-permute-start(f32[256,128]{1,0:T(8,128)S(1)} %get-tuple-element.85), channel_id=1, source_target_pairs={{0,6},{2,4},{4,2},{6,0},{1,7},{3,5},{5,3},{7,1},{8,14},{10,12},{12... | collective-permute-start | bytes 393224 | tf_op jit(solution)/shard_map/ppermute | solution.py:366

commit v15 on v14

--- a/solution.py
+++ b/solution.py
@@ -368,15 +368,11 @@
     ]
 
 
-def sum_over(value, axis, size, first):
-    if size & (size - 1):
-        return value if first else lax.psum(value, axis)
-    step = 1 << first
+def sum_over(value, axis, size):
+    step = 2
     while step < size:
         value = value + lax.ppermute(value, axis, [(k, k ^ step) for k in range(size)])
         step *= 2
-        if first == 0:
-            break
     return value
 
 
@@ -445,13 +441,18 @@
         (*got, *deal(quarters, PLANE[:2], FOUR)),
         32 * rows * width,
     )
-    probe_band = sum_over(probe_band, "pair", pairs, 0)
+    above = lax.ppermute(lower_sums, "pair", [(k, k + 1) for k in range(pairs - 1)])
+    doubling = pairs > 1 and pairs & (pairs - 1) == 0
+    if doubling:
+        near = lax.ppermute(probe_band, "pair", [(k, k ^ 1) for k in range(pairs)])
     (sums,) = call(add_own_kernel, [shape(planes, rows, cols)], scalars, got, 64 * rows * width)
-    lower_sums, sums, probe_band = lax.optimization_barrier((lower_sums, sums, probe_band))
-    above = lax.ppermute(lower_sums, "pair", [(k, k + 1) for k in range(pairs - 1)])
     sums = call(top_kernel, [shape(rows, cols)] * 4, (where,), (sums, above), planes * rows * cols)
+    if doubling:
+        *sums, near = lax.optimization_barrier((*sums, near))
+        probe_band = sum_over(probe_band + near, "pair", pairs)
+    else:
+        probe_band = lax.psum(probe_band, "pair")
     sums = deal(sums, PLANE[:2], FOUR)
-    probe_band = sum_over(probe_band, "pair", pairs, 1)
     probe_grad = lax.all_gather(probe_band, PLANE, axis=0, tiled=True)
     object_grad, probe_grad = call(
         join_kernel,

time: 94.9 us -> 93.3 us (0.983); the launches traced: 93.2 us -> 93 us
    ppermute x2 -> x1, starting transfers between devices: 4.55 us -> 2.77 us  [sum_over(): lax.ppermute(value, axis, [(k, k ^ step) for k in range(size)])]
    ppermute x0 -> x1, starting transfers between devices: none -> 1.64 us  [local(): near = lax.ppermute(probe_band, 'pair', [(k, k ^ 1) for k in range(pairs)])]
where the time goes in v15:
time: 93.3 us; the launch traced here: 93 us
  starting transfers between devices  34.3 us (37%)
  waiting for transfers between devices  30.8 us (33%)
  Pallas kernels  16.3 us (17%)
  blocking collectives  10.1 us (11%)
    ppermute x23, starting transfers between devices, deal(): lax.ppermute(value, axes, [(k, k ^ turn) for k in range(len(order))])  23.2 us
    ppermute x23, waiting for transfers between devices, deal(): lax.ppermute(value, axes, [(k, k ^ turn) for k in range(len(order))])  20.5 us
    pallas_call x10, Pallas kernels, call(): pl.pallas_call(kernel, out_shape=[x for x, unused in outs], in_specs=[SME...  16.3 us
    all_gather x1, blocking collectives, local(): probe_grad = lax.all_gather(probe_band, PLANE, axis=0, tiled=True)  10.1 us
    ppermute x1, waiting for transfers between devices, local(): below = lax.ppermute(lowest, 'pair', [(k, k - 1) for k in range(1, pairs)])  7.62 us
    ppermute x1, starting transfers between devices, local(): lax.ppermute(lower_sums, 'pair', [(k, k + 1) for k in range(pairs - 1)])  3.75 us
    ppermute x1, starting transfers between devices, sum_over(): lax.ppermute(value, axis, [(k, k ^ step) for k in range(size)])  2.77 us
    ppermute x1, waiting for transfers between devices, local(): lax.ppermute(lower_sums, 'pair', [(k, k + 1) for k in range(pairs - 1)])  2.52 us
  transfers between devices with their start and end apart: 29, of which 13 were waited for; matrix products, arithmetic and copies ran while one was open for 0% of the time, Pallas kernels for 6%

profile of v15, /device:TPU:0, one launch (start us, length us, event | category | flops | bytes accessed | tf_op | source)
XLA Modules:
  0.0 93.0 jit_solution(11933961851170546871)
XLA Ops:
  0.7 2.0 %shard_map.95 = (f32[264,128]{1,0:T(8,128)S(1)}, f32[264,128]{1,0:T(8,128)S(1)}, f32[264,128]{1,0:T(8,128)S(1)}, f32[264,128]{1,0:T(8,128)S(1)}, f32[256,256]{1,0:T(8,128)S(1)}) custom-call(s32[3]{0:T(128)S(1)} %pad_add_fusion.1.where, s32[1,2,2]{2,1,0:T(2,128)} %offsets.1, f32[4,256,128]{2,1,0:T(8,128)} %bitcast.10, f32[1,2,256,256]{3,2,1,0:T(8,128)} %measured.3), custom_call_target="tpu_custom_call" | custom-call | bytes 1851392 | tf_op jit(solution)/shard_map/pallas_call | solution.py:349
  2.7 3.0 %collective-permute-start = (f32[264,128]{1,0:T(8,128)S(1)}, f32[264,128]{1,0:T(8,128)S(1)}, u32[]{:S(2)}, u32[]{:S(2)}) collective-permute-start(f32[264,128]{1,0:T(8,128)S(1)} %get-tuple-element.49), channel_id=1, source_target_pairs={{0,2},{2,0},{4,6},{6,4},{1,3},{3,1},{5,7},{7,5},{8,10},{10,8},{12,... | collective-permute-start | bytes 405512 | tf_op jit(solution)/shard_map/ppermute | solution.py:366
  5.7 1.5 %collective-permute-start.1 = (f32[264,128]{1,0:T(8,128)S(1)}, f32[264,128]{1,0:T(8,128)S(1)}, u32[]{:S(2)}, u32[]{:S(2)}) collective-permute-start(f32[264,128]{1,0:T(8,128)S(1)} %get-tuple-element.50), channel_id=1, source_target_pairs={{0,4},{2,6},{4,0},{6,2},{1,5},{3,7},{5,1},{7,3},{8,12},{10,14},{12... | collective-permute-start | bytes 405512 | tf_op jit(solution)/shard_map/ppermute | solution.py:366
  7.3 2.3 %collective-permute-done.refs_1_ = f32[264,128]{1,0:T(8,128)S(1)} collective-permute-done((f32[264,128]{1,0:T(8,128)S(1)}, f32[264,128]{1,0:T(8,128)S(1)}, u32[]{:S(2)}, u32[]{:S(2)}) %collective-permute-start) | collective-permute-done | bytes 135200 | tf_op jit(solution)/shard_map/ppermute | solution.py:366
  9.8 3.8 %collective-permute-done.1.refs_0_ = f32[264,128]{1,0:T(8,128)S(1)} collective-permute-done((f32[264,128]{1,0:T(8,128)S(1)}, f32[264,128]{1,0:T(8,128)S(1)}, u32[]{:S(2)}, u32[]{:S(2)}) %collective-permute-start.1) | collective-permute-done | bytes 135200 | tf_op jit(solution)/shard_map/ppermute | solution.py:366
  13.7 0.1 slice_reduce_fusion
  14.0 0.6 shard_map.96
  14.5 1.3 %collective-permute-start.4 = (f32[2,256,128]{2,1,0:T(8,128)S(1)}, f32[2,256,128]{2,1,0:T(8,128)S(1)}, u32[]{:S(2)}, u32[]{:S(2)}) collective-permute-start(f32[2,256,128]{2,1,0:T(8,128)S(1)} %shard_map.96), channel_id=1, source_target_pairs={{8,0},{16,8},{24,16},{9,1},{17,9},{25,17},{10,2},{18,10},{26,18},{... | collective-permute-start | bytes 786440 | tf_op jit(solution)/shard_map/ppermute | solution.py:400
  15.8 1.6 %collective-permute-start.5 = (f32[256,256]{1,0:T(8,128)S(1)}, f32[256,256]{1,0:T(8,128)S(1)}, u32[]{:S(2)}, u32[]{:S(2)}) collective-permute-start(f32[256,256]{1,0:T(8,128)S(1)} %get-tuple-element.54), channel_id=1, source_target_pairs={{0,4},{4,0},{1,5},{5,1},{2,6},{6,2},{3,7},{7,3},{8,12},{12,8},{9,1... | collective-permute-start | bytes 786440 | tf_op jit(solution)/shard_map/ppermute | solution.py:401
  17.5 7.6 %collective-permute-done.4.refs_4_ = f32[2,256,128]{2,1,0:T(8,128)S(1)} collective-permute-done((f32[2,256,128]{2,1,0:T(8,128)S(1)}, f32[2,256,128]{2,1,0:T(8,128)S(1)}, u32[]{:S(2)}, u32[]{:S(2)}) %collective-permute-start.4) | collective-permute-done | bytes 262176 | tf_op jit(solution)/shard_map/ppermute | solution.py:400
  25.1 1.4 %shard_map.97 = (f32[256,128]{1,0:T(8,128)S(1)}, f32[256,128]{1,0:T(8,128)S(1)}, f32[256,128]{1,0:T(8,128)S(1)}, f32[256,128]{1,0:T(8,128)S(1)}, f32[256,128]{1,...) custom-call(s32[3]{0:T(128)S(1)} %pad_add_fusion.1.where, ...), custom_call_target="tpu_custom_call" | custom-call | flops 2097152 | bytes 1851392 | tf_op jit(solution)/shard_map/pallas_call | solution.py:349
  26.6 1.6 %collective-permute-start.6 = (f32[256,128]{1,0:T(8,128)S(1)}, f32[256,128]{1,0:T(8,128)S(1)}, u32[]{:S(2)}, u32[]{:S(2)}) collective-permute-start(f32[256,128]{1,0:T(8,128)S(1)} %get-tuple-element.56), channel_id=1, source_target_pairs={{0,4},{1,5},{2,6},{3,7},{4,0},{5,1},{6,2},{7,3},{8,12},{9,13},{10,... | collective-permute-start | bytes 393224 | tf_op jit(solution)/shard_map/ppermute | solution.py:366
  28.2 0.5 collective-permute-start.7
  28.7 1.7 %collective-permute-start.9 = (f32[256,128]{1,0:T(8,128)S(1)}, f32[256,128]{1,0:T(8,128)S(1)}, u32[]{:S(2)}, u32[]{:S(2)}) collective-permute-start(f32[256,128]{1,0:T(8,128)S(1)} %get-tuple-element.59), channel_id=1, source_target_pairs={{0,3},{1,2},{2,1},{3,0},{4,7},{5,6},{6,5},{7,4},{8,11},{9,10},{10,... | collective-permute-start | bytes 393224 | tf_op jit(solution)/shard_map/ppermute | solution.py:366
  30.4 1.5 %collective-permute-start.10 = (f32[256,128]{1,0:T(8,128)S(1)}, f32[256,128]{1,0:T(8,128)S(1)}, u32[]{:S(2)}, u32[]{:S(2)}) collective-permute-start(f32[256,128]{1,0:T(8,128)S(1)} %get-tuple-element.60), channel_id=1, source_target_pairs={{0,6},{1,7},{2,4},{3,5},{4,2},{5,3},{6,0},{7,1},{8,14},{9,15},{10,... | collective-permute-start | bytes 393224 | tf_op jit(solution)/shard_map/ppermute | solution.py:366
  31.9 0.7 collective-permute-start.11
  32.6 2.0 %collective-permute-done.7.refs_1_ = f32[256,128]{1,0:T(8,128)S(1)} collective-permute-done((f32[256,128]{1,0:T(8,128)S(1)}, f32[256,128]{1,0:T(8,128)S(1)}, u32[]{:S(2)}, u32[]{:S(2)}) %collective-permute-start.7) | collective-permute-done | bytes 131104 | tf_op jit(solution)/shard_map/ppermute | solution.py:366
  34.6 2.7 %shard_map.98 = (f32[2,256,256]{2,1,0:T(8,128)S(1)}, f32[256,256]{1,0:T(8,128)S(1)}, bf16[6,512,256]{2,1,0:T(8,128)(2,1)S(1)}) custom-call(s32[3]{0:T(128)S(1)} %pad_add_fusion.1.where, s32[1,2]{1,0:T(1,128)} %slot_range.9, s32[4,8]{1,0:T(4,128)S(1)} %pad_add_fusion.offs, f32[256,256]{1,0:T(8,128)S(1)} %collective-permute-done.5.taken, ...), custom_call_target="tpu_custom_call" | custom-call | flops 201326592 | bytes 5505024 | tf_op jit(solution)/shard_map/pallas_call | solution.py:349
  37.3 1.9 %collective-permute-done.10.refs_4_ = f32[256,128]{1,0:T(8,128)S(1)} collective-permute-done((f32[256,128]{1,0:T(8,128)S(1)}, f32[256,128]{1,0:T(8,128)S(1)}, u32[]{:S(2)}, u32[]{:S(2)}) %collective-permute-start.10) | collective-permute-done | bytes 131104 | tf_op jit(solution)/shard_map/ppermute | solution.py:366
  39.2 1.9 %collective-permute-done.11.refs_5_ = f32[256,128]{1,0:T(8,128)S(1)} collective-permute-done((f32[256,128]{1,0:T(8,128)S(1)}, f32[256,128]{1,0:T(8,128)S(1)}, u32[]{:S(2)}, u32[]{:S(2)}) %collective-permute-start.11) | collective-permute-done | bytes 131104 | tf_op jit(solution)/shard_map/ppermute | solution.py:366
  41.1 4.3 %shard_map.99 = (f32[768,128]{1,0:T(8,128)S(1)}, f32[256,128]{1,0:T(8,128)S(1)}, f32[256,128]{1,0:T(8,128)S(1)}, f32[256,128]{1,0:T(8,128)S(1)}, f32[256,128]{1,...) custom-call(s32[3]{0:T(128)S(1)} %pad_add_fusion.1.where, ...), custom_call_target="tpu_custom_call" | custom-call | flops 1610612736 | bytes 5120000 | tf_op jit(solution)/shard_map/pallas_call | solution.py:349
  45.3 0.4 collective-permute-start.13
  45.7 1.5 %collective-permute-start.14 = (f32[256,128]{1,0:T(8,128)S(1)}, f32[256,128]{1,0:T(8,128)S(1)}, u32[]{:S(2)}, u32[]{:S(2)}) collective-permute-start(f32[256,128]{1,0:T(8,128)S(1)} %get-tuple-element.69), channel_id=1, source_target_pairs={{0,4},{1,5},{2,6},{3,7},{4,0},{5,1},{6,2},{7,3},{8,12},{9,13},{10,... | collective-permute-start | bytes 393224 | tf_op jit(solution)/shard_map/ppermute | solution.py:366
  47.2 0.6 collective-permute-start.15
  47.7 0.2 collective-permute-start.16
  47.9 1.5 %collective-permute-start.17 = (f32[256,128]{1,0:T(8,128)S(1)}, f32[256,128]{1,0:T(8,128)S(1)}, u32[]{:S(2)}, u32[]{:S(2)}) collective-permute-start(f32[256,128]{1,0:T(8,128)S(1)} %get-tuple-element.72), channel_id=1, source_target_pairs={{0,3},{1,2},{2,1},{3,0},{4,7},{5,6},{6,5},{7,4},{8,11},{9,10},{10,... | collective-permute-start | bytes 393224 | tf_op jit(solution)/shard_map/ppermute | solution.py:366
  49.5 2.3 %collective-permute-done.14.refs_1_ = f32[256,128]{1,0:T(8,128)S(1)} collective-permute-done((f32[256,128]{1,0:T(8,128)S(1)}, f32[256,128]{1,0:T(8,128)S(1)}, u32[]{:S(2)}, u32[]{:S(2)}) %collective-permute-start.14) | collective-permute-done | bytes 131104 | tf_op jit(solution)/shard_map/ppermute | solution.py:366
  51.8 1.5 %collective-permute-start.18 = (f32[256,128]{1,0:T(8,128)S(1)}, f32[256,128]{1,0:T(8,128)S(1)}, u32[]{:S(2)}, u32[]{:S(2)}) collective-permute-start(f32[256,128]{1,0:T(8,128)S(1)} %get-tuple-element.73), channel_id=1, source_target_pairs={{0,6},{1,7},{2,4},{3,5},{4,2},{5,3},{6,0},{7,1},{8,14},{9,15},{10,... | collective-permute-start | bytes 393224 | tf_op jit(solution)/shard_map/ppermute | solution.py:366
  53.3 0.6 shard_map.101
  53.9 0.9 collective-permute-start.20
  54.8 1.2 %collective-permute-start.21 = (f32[128,128]{1,0:T(8,128)S(1)}, f32[128,128]{1,0:T(8,128)S(1)}, u32[]{:S(2)}, u32[]{:S(2)}) collective-permute-start(f32[128,128]{1,0:T(8,128)S(1)} %get-tuple-element.78), channel_id=1, source_target_pairs={{0,2},{2,0},{4,6},{6,4},{1,3},{3,1},{5,7},{7,5},{8,10},{10,8},{12,... | collective-permute-start | bytes 196616 | tf_op jit(solution)/shard_map/ppermute | solution.py:366
  56.0 1.5 %collective-permute-start.22 = (f32[128,128]{1,0:T(8,128)S(1)}, f32[128,128]{1,0:T(8,128)S(1)}, u32[]{:S(2)}, u32[]{:S(2)}) collective-permute-start(f32[128,128]{1,0:T(8,128)S(1)} %get-tuple-element.79), channel_id=1, source_target_pairs={{0,6},{2,4},{4,2},{6,0},{1,7},{3,5},{5,3},{7,1},{8,14},{10,12},{12... | collective-permute-start | bytes 196616 | tf_op jit(solution)/shard_map/ppermute | solution.py:366
  57.5 1.6 %collective-permute-done.18.refs_5_ = f32[256,128]{1,0:T(8,128)S(1)} collective-permute-done((f32[256,128]{1,0:T(8,128)S(1)}, f32[256,128]{1,0:T(8,128)S(1)}, u32[]{:S(2)}, u32[]{:S(2)}) %collective-permute-start.18) | collective-permute-done | bytes 131104 | tf_op jit(solution)/shard_map/ppermute | solution.py:366
  59.1 1.0 %collective-permute-done.19.refs_6_ = f32[256,128]{1,0:T(8,128)S(1)} collective-permute-done((f32[256,128]{1,0:T(8,128)S(1)}, f32[256,128]{1,0:T(8,128)S(1)}, u32[]{:S(2)}, u32[]{:S(2)}) %collective-permute-start.19) | collective-permute-done | bytes 131104 | tf_op jit(solution)/shard_map/ppermute | solution.py:366
  60.1 2.9 %collective-permute-done.20.refs_8_ = f32[128,128]{1,0:T(8,128)S(1)} collective-permute-done((f32[128,128]{1,0:T(8,128)S(1)}, f32[128,128]{1,0:T(8,128)S(1)}, u32[]{:S(2)}, u32[]{:S(2)}) %collective-permute-start.20) | collective-permute-done | bytes 65568 | tf_op jit(solution)/shard_map/ppermute | solution.py:366
  63.0 0.8 collective-permute-done.22.refs_10_
  63.8 1.1 %shard_map.102 = (f32[2,256,128]{2,1,0:T(8,128)S(1)}, f32[64,256]{1,0:T(8,128)S(1)}) custom-call(s32[3]{0:T(128)S(1)} %pad_add_fusion.1.where, s32[1,2]{1,0:T(1,128)} %slot_range.9, s32[4,8]{1,0:T(4,128)S(1)} %pad_add_fusion.offs, f32[768,128]{1,0:T(8,128)S(1)} %collective-permute-done.13.refs_0_.got, f32[256,128]{1,0:T(8,128)S(1)} %collective-permute-done.14.refs_1_, ...), custom_call_target="tpu_custom_call" | custom-call | flops 2097152 | bytes 1900544 | tf_op jit(solution)/shard_map/pallas_call | solution.py:349
  64.9 3.8 %collective-permute-start.23 = (f32[2,256,128]{2,1,0:T(8,128)S(1)}, f32[2,256,128]{2,1,0:T(8,128)S(1)}, u32[]{:S(2)}, u32[]{:S(2)}) collective-permute-start(f32[2,256,128]{2,1,0:T(8,128)S(1)} %get-tuple-element.81), channel_id=1, source_target_pairs={{0,8},{8,16},{16,24},{1,9},{9,17},{17,25},{2,10},{10,18},{18,26},{... | collective-permute-start | bytes 786440 | tf_op jit(solution)/shard_map/ppermute | solution.py:444
  68.6 1.6 %collective-permute-start.24 = (f32[64,256]{1,0:T(8,128)S(1)}, f32[64,256]{1,0:T(8,128)S(1)}, u32[]{:S(2)}, u32[]{:S(2)}) collective-permute-start(f32[64,256]{1,0:T(8,128)S(1)} %get-tuple-element.86), channel_id=1, source_target_pairs={{0,8},{8,0},{16,24},{24,16},{1,9},{9,1},{17,25},{25,17},{2,10},{10... | collective-permute-start | bytes 196616 | tf_op jit(solution)/shard_map/ppermute | solution.py:447
  70.3 1.6 %shard_map.100.own = f32[4,256,128]{2,1,0:T(8,128)S(1)} custom-call(s32[3]{0:T(128)S(1)} %pad_add_fusion.1.where, s32[1,2]{1,0:T(1,128)} %slot_range.9, s32[4,8]{1,0:T(4,128)S(1)} %pad_add_fusion.offs, f32[768,128]{1,0:T(8,128)S(1)} %collective-permute-done.13.refs_0_.got, f32[256,128]{1,0:T(8,128)S(1)} %collective-permute-done.14.refs_1_, ...), custom_call_target="tpu_custom_call" | custom-call | flops 4194304 | bytes 1835008 | tf_op jit(solution)/shard_map/pallas_call | solution.py:349
  71.8 2.5 %collective-permute-done.23.above = f32[2,256,128]{2,1,0:T(8,128)S(1)} collective-permute-done((f32[2,256,128]{2,1,0:T(8,128)S(1)}, f32[2,256,128]{2,1,0:T(8,128)S(1)}, u32[]{:S(2)}, u32[]{:S(2)}) %collective-permute-start.23) | collective-permute-done | bytes 262176 | tf_op jit(solution)/shard_map/ppermute | solution.py:444
  74.4 0.6 shard_map.103
  75.1 2.8 %collective-permute-start.28 = (f32[64,256]{1,0:T(8,128)S(1)}, f32[64,256]{1,0:T(8,128)S(1)}, u32[]{:S(2)}, u32[]{:S(2)}) collective-permute-start(f32[64,256]{1,0:T(8,128)S(1)} %add.6), channel_id=1, source_target_pairs={{0,16},{8,24},{16,0},{24,8},{1,17},{9,25},{17,1},{25,9},{2,18},{10... | collective-permute-start | bytes 196616 | tf_op jit(solution)/shard_map/ppermute | solution.py:374
  77.8 1.3 %collective-permute-start.25 = (f32[256,128]{1,0:T(8,128)S(1)}, f32[256,128]{1,0:T(8,128)S(1)}, u32[]{:S(2)}, u32[]{:S(2)}) collective-permute-start(f32[256,128]{1,0:T(8,128)S(1)} %get-tuple-element.87), channel_id=1, source_target_pairs={{0,4},{2,6},{4,0},{6,2},{1,5},{3,7},{5,1},{7,3},{8,12},{10,14},{12... | collective-permute-start | bytes 393224 | tf_op jit(solution)/shard_map/ppermute | solution.py:366
  79.1 0.7 collective-permute-start.26
  79.9 1.5 %collective-permute-start.27 = (f32[256,128]{1,0:T(8,128)S(1)}, f32[256,128]{1,0:T(8,128)S(1)}, u32[]{:S(2)}, u32[]{:S(2)}) collective-permute-start(f32[256,128]{1,0:T(8,128)S(1)} %get-tuple-element.89), channel_id=1, source_target_pairs={{0,6},{2,4},{4,2},{6,0},{1,7},{3,5},{5,3},{7,1},{8,14},{10,12},{12... | collective-permute-start | bytes 393224 | tf_op jit(solution)/shard_map/ppermute | solution.py:366
  81.4 10.1 %all_gather.3.refs_4_ = f32[512,256]{1,0:T(8,128)S(1)} all-gather(f32[64,256]{1,0:T(8,128)S(1)} %add.7), channel_id=1, replica_groups=mesh['pair'=4,'half'=2,'col'=2,'core'=2] {'half','col','core'}, dimensions={0}, use_global_device_ids=true | all-gather | bytes 589824 | tf_op jit(solution)/shard_map/all_gather | solution.py:456
  91.5 1.5 %shard_map.104 = (f32[4,256,128]{2,1,0:T(8,128)}, f32[512,256]{1,0:T(8,128)}) custom-call(s32[3]{0:T(128)S(1)} %pad_add_fusion.1.where, f32[256,128]{1,0:T(8,128)S(1)} %collective-permute-done.25.refs_0_, f32[256,128]{1,0:T(8,128)S(1)} %collective-permute-done.26.refs_1_, f32[256,128]{1,0:T(8,128)S(1)} %collective-permute-done.27.refs_2_, ...), custom_call_target="tpu_custom_call" | custom-call | bytes 2097152 | tf_op jit(solution)/shard_map/pallas_call | solution.py:349
  (33 shorter events, 0.8 us)
Async XLA Ops:
  2.7 7.0 %collective-permute-start = (f32[264,128]{1,0:T(8,128)S(1)}, f32[264,128]{1,0:T(8,128)S(1)}, u32[]{:S(2)}, u32[]{:S(2)}) collective-permute-start(f32[264,128]{1,0:T(8,128)S(1)} %get-tuple-element.49), channel_id=1, source_target_pairs={{0,2},{2,0},{4,6},{6,4},{1,3},{3,1},{5,7},{7,5},{8,10},{10,8},{12,... | collective-permute-start | bytes 405512 | tf_op jit(solution)/shard_map/ppermute | solution.py:366
  5.7 7.9 %collective-permute-start.1 = (f32[264,128]{1,0:T(8,128)S(1)}, f32[264,128]{1,0:T(8,128)S(1)}, u32[]{:S(2)}, u32[]{:S(2)}) collective-permute-start(f32[264,128]{1,0:T(8,128)S(1)} %get-tuple-element.50), channel_id=1, source_target_pairs={{0,4},{2,6},{4,0},{6,2},{1,5},{3,7},{5,1},{7,3},{8,12},{10,14},{12... | collective-permute-start | bytes 405512 | tf_op jit(solution)/shard_map/ppermute | solution.py:366
  7.2 6.5 %collective-permute-start.2 = (f32[264,128]{1,0:T(8,128)S(1)}, f32[264,128]{1,0:T(8,128)S(1)}, u32[]{:S(2)}, u32[]{:S(2)}) collective-permute-start(f32[264,128]{1,0:T(8,128)S(1)} %get-tuple-element.51), channel_id=1, source_target_pairs={{0,6},{2,4},{4,2},{6,0},{1,7},{3,5},{5,3},{7,1},{8,14},{10,12},{12... | collective-permute-start | bytes 405512 | tf_op jit(solution)/shard_map/ppermute | solution.py:366
  13.9 3.5 %collective-permute-start.3 = (s32[4,4]{1,0:T(4,128)S(1)}, s32[4,4]{1,0:T(4,128)S(1)}, u32[]{:S(2)}, u32[]{:S(2)}) collective-permute-start(s32[4,4]{1,0:T(4,128)S(1)} %maximum_convert_fusion), channel_id=1, source_target_pairs={{0,1},{1,0},{2,3},{3,2},{4,5},{5,4},{6,7},{7,6},{8,9},{9,8},{10,11... | collective-permute-start | bytes 200 | tf_op jit(solution)/shard_map/ppermute | solution.py:406
  14.5 10.6 %collective-permute-start.4 = (f32[2,256,128]{2,1,0:T(8,128)S(1)}, f32[2,256,128]{2,1,0:T(8,128)S(1)}, u32[]{:S(2)}, u32[]{:S(2)}) collective-permute-start(f32[2,256,128]{2,1,0:T(8,128)S(1)} %shard_map.96), channel_id=1, source_target_pairs={{8,0},{16,8},{24,16},{9,1},{17,9},{25,17},{10,2},{18,10},{26,18},{... | collective-permute-start | bytes 786440 | tf_op jit(solution)/shard_map/ppermute | solution.py:400
  15.8 9.3 %collective-permute-start.5 = (f32[256,256]{1,0:T(8,128)S(1)}, f32[256,256]{1,0:T(8,128)S(1)}, u32[]{:S(2)}, u32[]{:S(2)}) collective-permute-start(f32[256,256]{1,0:T(8,128)S(1)} %get-tuple-element.54), channel_id=1, source_target_pairs={{0,4},{4,0},{1,5},{5,1},{2,6},{6,2},{3,7},{7,3},{8,12},{12,8},{9,1... | collective-permute-start | bytes 786440 | tf_op jit(solution)/shard_map/ppermute | solution.py:401
  26.6 5.3 %collective-permute-start.6 = (f32[256,128]{1,0:T(8,128)S(1)}, f32[256,128]{1,0:T(8,128)S(1)}, u32[]{:S(2)}, u32[]{:S(2)}) collective-permute-start(f32[256,128]{1,0:T(8,128)S(1)} %get-tuple-element.56), channel_id=1, source_target_pairs={{0,4},{1,5},{2,6},{3,7},{4,0},{5,1},{6,2},{7,3},{8,12},{9,13},{10,... | collective-permute-start | bytes 393224 | tf_op jit(solution)/shard_map/ppermute | solution.py:366
  28.2 6.4 %collective-permute-start.7 = (f32[256,128]{1,0:T(8,128)S(1)}, f32[256,128]{1,0:T(8,128)S(1)}, u32[]{:S(2)}, u32[]{:S(2)}) collective-permute-start(f32[256,128]{1,0:T(8,128)S(1)} %get-tuple-element.57), channel_id=1, source_target_pairs={{0,2},{1,3},{2,0},{3,1},{4,6},{5,7},{6,4},{7,5},{8,10},{9,11},{10,... | collective-permute-start | bytes 393224 | tf_op jit(solution)/shard_map/ppermute | solution.py:366
  28.7 8.6 %collective-permute-start.8 = (f32[256,128]{1,0:T(8,128)S(1)}, f32[256,128]{1,0:T(8,128)S(1)}, u32[]{:S(2)}, u32[]{:S(2)}) collective-permute-start(f32[256,128]{1,0:T(8,128)S(1)} %get-tuple-element.58), channel_id=1, source_target_pairs={{0,5},{1,4},{2,7},{3,6},{4,1},{5,0},{6,3},{7,2},{8,13},{9,12},{10,... | collective-permute-start | bytes 393224 | tf_op jit(solution)/shard_map/ppermute | solution.py:366
  28.7 8.6 %collective-permute-start.9 = (f32[256,128]{1,0:T(8,128)S(1)}, f32[256,128]{1,0:T(8,128)S(1)}, u32[]{:S(2)}, u32[]{:S(2)}) collective-permute-start(f32[256,128]{1,0:T(8,128)S(1)} %get-tuple-element.59), channel_id=1, source_target_pairs={{0,3},{1,2},{2,1},{3,0},{4,7},{5,6},{6,5},{7,4},{8,11},{9,10},{10,... | collective-permute-start | bytes 393224 | tf_op jit(solution)/shard_map/ppermute | solution.py:366
  30.4 8.7 %collective-permute-start.10 = (f32[256,128]{1,0:T(8,128)S(1)}, f32[256,128]{1,0:T(8,128)S(1)}, u32[]{:S(2)}, u32[]{:S(2)}) collective-permute-start(f32[256,128]{1,0:T(8,128)S(1)} %get-tuple-element.60), channel_id=1, source_target_pairs={{0,6},{1,7},{2,4},{3,5},{4,2},{5,3},{6,0},{7,1},{8,14},{9,15},{10,... | collective-permute-start | bytes 393224 | tf_op jit(solution)/shard_map/ppermute | solution.py:366
  31.9 9.1 %collective-permute-start.11 = (f32[256,128]{1,0:T(8,128)S(1)}, f32[256,128]{1,0:T(8,128)S(1)}, u32[]{:S(2)}, u32[]{:S(2)}) collective-permute-start(f32[256,128]{1,0:T(8,128)S(1)} %get-tuple-element.61), channel_id=1, source_target_pairs={{0,7},{1,6},{2,5},{3,4},{4,3},{5,2},{6,1},{7,0},{8,15},{9,14},{10,... | collective-permute-start | bytes 393224 | tf_op jit(solution)/shard_map/ppermute | solution.py:366
  34.5 6.5 %copy-start = (f32[2,136,128]{2,1,0:T(8,128)S(1)}, f32[2,136,128]{2,1,0:T(8,128)}, u32[]{:S(2)}) copy-start(f32[2,136,128]{2,1,0:T(8,128)} %constant.19.clone.refs_11_) | copy-start | bytes 417796
  34.6 6.5 %collective-permute-start.12 = (f32[256,128]{1,0:T(8,128)S(1)}, f32[256,128]{1,0:T(8,128)S(1)}, u32[]{:S(2)}, u32[]{:S(2)}) collective-permute-start(f32[256,128]{1,0:T(8,128)S(1)} %get-tuple-element.62), channel_id=1, source_target_pairs={{0,1},{1,0},{2,3},{3,2},{4,5},{5,4},{6,7},{7,6},{8,9},{9,8},{10,11... | collective-permute-start | bytes 393224 | tf_op jit(solution)/shard_map/ppermute | solution.py:366
  45.3 8.0 %collective-permute-start.13 = (f32[768,128]{1,0:T(8,128)S(1)}, f32[768,128]{1,0:T(8,128)S(1)}, u32[]{:S(2)}, u32[]{:S(2)}) collective-permute-start(f32[768,128]{1,0:T(8,128)S(1)} %get-tuple-element.68), channel_id=1, source_target_pairs={{0,1},{1,0},{2,3},{3,2},{4,5},{5,4},{6,7},{7,6},{8,9},{9,8},{10,11... | collective-permute-start | bytes 1179656 | tf_op jit(solution)/shard_map/ppermute | solution.py:366
  45.7 6.1 %collective-permute-start.14 = (f32[256,128]{1,0:T(8,128)S(1)}, f32[256,128]{1,0:T(8,128)S(1)}, u32[]{:S(2)}, u32[]{:S(2)}) collective-permute-start(f32[256,128]{1,0:T(8,128)S(1)} %get-tuple-element.69), channel_id=1, source_target_pairs={{0,4},{1,5},{2,6},{3,7},{4,0},{5,1},{6,2},{7,3},{8,12},{9,13},{10,... | collective-permute-start | bytes 393224 | tf_op jit(solution)/shard_map/ppermute | solution.py:366
  47.2 6.7 %collective-permute-start.15 = (f32[256,128]{1,0:T(8,128)S(1)}, f32[256,128]{1,0:T(8,128)S(1)}, u32[]{:S(2)}, u32[]{:S(2)}) collective-permute-start(f32[256,128]{1,0:T(8,128)S(1)} %get-tuple-element.70), channel_id=1, source_target_pairs={{0,2},{1,3},{2,0},{3,1},{4,6},{5,7},{6,4},{7,5},{8,10},{9,11},{10,... | collective-permute-start | bytes 393224 | tf_op jit(solution)/shard_map/ppermute | solution.py:366
  47.7 7.1 %collective-permute-start.16 = (f32[256,128]{1,0:T(8,128)S(1)}, f32[256,128]{1,0:T(8,128)S(1)}, u32[]{:S(2)}, u32[]{:S(2)}) collective-permute-start(f32[256,128]{1,0:T(8,128)S(1)} %get-tuple-element.71), channel_id=1, source_target_pairs={{0,5},{1,4},{2,7},{3,6},{4,1},{5,0},{6,3},{7,2},{8,13},{9,12},{10,... | collective-permute-start | bytes 393224 | tf_op jit(solution)/shard_map/ppermute | solution.py:366
  47.9 8.0 %collective-permute-start.17 = (f32[256,128]{1,0:T(8,128)S(1)}, f32[256,128]{1,0:T(8,128)S(1)}, u32[]{:S(2)}, u32[]{:S(2)}) collective-permute-start(f32[256,128]{1,0:T(8,128)S(1)} %get-tuple-element.72), channel_id=1, source_target_pairs={{0,3},{1,2},{2,1},{3,0},{4,7},{5,6},{6,5},{7,4},{8,11},{9,10},{10,... | collective-permute-start | bytes 393224 | tf_op jit(solution)/shard_map/ppermute | solution.py:366
  51.8 7.3 %collective-permute-start.18 = (f32[256,128]{1,0:T(8,128)S(1)}, f32[256,128]{1,0:T(8,128)S(1)}, u32[]{:S(2)}, u32[]{:S(2)}) collective-permute-start(f32[256,128]{1,0:T(8,128)S(1)} %get-tuple-element.73), channel_id=1, source_target_pairs={{0,6},{1,7},{2,4},{3,5},{4,2},{5,3},{6,0},{7,1},{8,14},{9,15},{10,... | collective-permute-start | bytes 393224 | tf_op jit(solution)/shard_map/ppermute | solution.py:366
  53.3 6.8 %collective-permute-start.19 = (f32[256,128]{1,0:T(8,128)S(1)}, f32[256,128]{1,0:T(8,128)S(1)}, u32[]{:S(2)}, u32[]{:S(2)}) collective-permute-start(f32[256,128]{1,0:T(8,128)S(1)} %get-tuple-element.74), channel_id=1, source_target_pairs={{0,7},{1,6},{2,5},{3,4},{4,3},{5,2},{6,1},{7,0},{8,15},{9,14},{10,... | collective-permute-start | bytes 393224 | tf_op jit(solution)/shard_map/ppermute | solution.py:366
  53.9 9.0 %collective-permute-start.20 = (f32[128,128]{1,0:T(8,128)S(1)}, f32[128,128]{1,0:T(8,128)S(1)}, u32[]{:S(2)}, u32[]{:S(2)}) collective-permute-start(f32[128,128]{1,0:T(8,128)S(1)} %get-tuple-element.77), channel_id=1, source_target_pairs={{0,4},{2,6},{4,0},{6,2},{1,5},{3,7},{5,1},{7,3},{8,12},{10,14},{12... | collective-permute-start | bytes 196616 | tf_op jit(solution)/shard_map/ppermute | solution.py:366
  54.8 8.2 %collective-permute-start.21 = (f32[128,128]{1,0:T(8,128)S(1)}, f32[128,128]{1,0:T(8,128)S(1)}, u32[]{:S(2)}, u32[]{:S(2)}) collective-permute-start(f32[128,128]{1,0:T(8,128)S(1)} %get-tuple-element.78), channel_id=1, source_target_pairs={{0,2},{2,0},{4,6},{6,4},{1,3},{3,1},{5,7},{7,5},{8,10},{10,8},{12,... | collective-permute-start | bytes 196616 | tf_op jit(solution)/shard_map/ppermute | solution.py:366
  56.0 7.8 %collective-permute-start.22 = (f32[128,128]{1,0:T(8,128)S(1)}, f32[128,128]{1,0:T(8,128)S(1)}, u32[]{:S(2)}, u32[]{:S(2)}) collective-permute-start(f32[128,128]{1,0:T(8,128)S(1)} %get-tuple-element.79), channel_id=1, source_target_pairs={{0,6},{2,4},{4,2},{6,0},{1,7},{3,5},{5,3},{7,1},{8,14},{10,12},{12... | collective-permute-start | bytes 196616 | tf_op jit(solution)/shard_map/ppermute | solution.py:366
  64.9 9.5 %collective-permute-start.23 = (f32[2,256,128]{2,1,0:T(8,128)S(1)}, f32[2,256,128]{2,1,0:T(8,128)S(1)}, u32[]{:S(2)}, u32[]{:S(2)}) collective-permute-start(f32[2,256,128]{2,1,0:T(8,128)S(1)} %get-tuple-element.81), channel_id=1, source_target_pairs={{0,8},{8,16},{16,24},{1,9},{9,17},{17,25},{2,10},{10,18},{18,26},{... | collective-permute-start | bytes 786440 | tf_op jit(solution)/shard_map/ppermute | solution.py:444
  68.6 6.4 %collective-permute-start.24 = (f32[64,256]{1,0:T(8,128)S(1)}, f32[64,256]{1,0:T(8,128)S(1)}, u32[]{:S(2)}, u32[]{:S(2)}) collective-permute-start(f32[64,256]{1,0:T(8,128)S(1)} %get-tuple-element.86), channel_id=1, source_target_pairs={{0,8},{8,0},{16,24},{24,16},{1,9},{9,1},{17,25},{25,17},{2,10},{10... | collective-permute-start | bytes 196616 | tf_op jit(solution)/shard_map/ppermute | solution.py:447
  75.1 6.3 %collective-permute-start.28 = (f32[64,256]{1,0:T(8,128)S(1)}, f32[64,256]{1,0:T(8,128)S(1)}, u32[]{:S(2)}, u32[]{:S(2)}) collective-permute-start(f32[64,256]{1,0:T(8,128)S(1)} %add.6), channel_id=1, source_target_pairs={{0,16},{8,24},{16,0},{24,8},{1,17},{9,25},{17,1},{25,9},{2,18},{10... | collective-permute-start | bytes 196616 | tf_op jit(solution)/shard_map/ppermute | solution.py:374
  77.8 13.6 %collective-permute-start.25 = (f32[256,128]{1,0:T(8,128)S(1)}, f32[256,128]{1,0:T(8,128)S(1)}, u32[]{:S(2)}, u32[]{:S(2)}) collective-permute-start(f32[256,128]{1,0:T(8,128)S(1)} %get-tuple-element.87), channel_id=1, source_target_pairs={{0,4},{2,6},{4,0},{6,2},{1,5},{3,7},{5,1},{7,3},{8,12},{10,14},{12... | collective-permute-start | bytes 393224 | tf_op jit(solution)/shard_map/ppermute | solution.py:366
  79.1 12.3 %collective-permute-start.26 = (f32[256,128]{1,0:T(8,128)S(1)}, f32[256,128]{1,0:T(8,128)S(1)}, u32[]{:S(2)}, u32[]{:S(2)}) collective-permute-start(f32[256,128]{1,0:T(8,128)S(1)} %get-tuple-element.88), channel_id=1, source_target_pairs={{0,2},{2,0},{4,6},{6,4},{1,3},{3,1},{5,7},{7,5},{8,10},{10,8},{12,... | collective-permute-start | bytes 393224 | tf_op jit(solution)/shard_map/ppermute | solution.py:366
  79.9 11.6 %collective-permute-start.27 = (f32[256,128]{1,0:T(8,128)S(1)}, f32[256,128]{1,0:T(8,128)S(1)}, u32[]{:S(2)}, u32[]{:S(2)}) collective-permute-start(f32[256,128]{1,0:T(8,128)S(1)} %get-tuple-element.89), channel_id=1, source_target_pairs={{0,6},{2,4},{4,2},{6,0},{1,7},{3,5},{5,3},{7,1},{8,14},{10,12},{12... | collective-permute-start | bytes 393224 | tf_op jit(solution)/shard_map/ppermute | solution.py:366

commit v16 on v15

--- a/solution.py
+++ b/solution.py
@@ -303,15 +303,19 @@
 
 
 def add_below_kernel(where, slot_range, offs, *refs):
-    parts, quarters, (below, probe_band) = refs[:8], refs[8:12], refs[12:]
+    parts, below = refs[:8], refs[8]
     rows, cols = below.shape[1:]
     sums = add_parts(where, slot_range, offs, parts, 2, rows, cols)
     for side in range(2):
         below[jnp.bitwise_xor(where[1], side)] = sums[side]
+
+
+def band_kernel(*refs):
+    quarters, out = refs[:4], refs[4]
     total = (quarters[0][...] + quarters[1][...]) + (quarters[2][...] + quarters[3][...])
-    band = probe_band.shape[0]
-    probe_band[:, :cols] = total[:band]
-    probe_band[:, cols:] = total[band:]
+    band, cols = out.shape[0], total.shape[1]
+    out[:, :cols] = total[:band]
+    out[:, cols:] = total[band:]
 
 
 def add_own_kernel(where, slot_range, offs, *refs):
@@ -434,18 +438,15 @@
     )
     got = deal(grad, PLANE, BACK)
     quarters = call(pair_kernel, [shape(2 * band, cols)] * 4, (where,), (keep, got[0]), 4 * band * width)
-    lower_sums, probe_band = call(
-        add_below_kernel,
-        [shape(2, rows, cols), shape(band, width)],
-        scalars,
-        (*got, *deal(quarters, PLANE[:2], FOUR)),
-        32 * rows * width,
-    )
+    *got, last = lax.optimization_barrier((*got, quarters[-1]))
+    quarters = [*quarters[:-1], last]
+    (lower_sums,) = call(add_below_kernel, [shape(2, rows, cols)], scalars, got, 32 * rows * width)
     above = lax.ppermute(lower_sums, "pair", [(k, k + 1) for k in range(pairs - 1)])
+    (sums,) = call(add_own_kernel, [shape(planes, rows, cols)], scalars, got, 64 * rows * width)
+    (probe_band,) = call(band_kernel, [shape(band, width)], (), deal(quarters, PLANE[:2], FOUR), 4 * band * width)
     doubling = pairs > 1 and pairs & (pairs - 1) == 0
     if doubling:
         near = lax.ppermute(probe_band, "pair", [(k, k ^ 1) for k in range(pairs)])
-    (sums,) = call(add_own_kernel, [shape(planes, rows, cols)], scalars, got, 64 * rows * width)
     sums = call(top_kernel, [shape(rows, cols)] * 4, (where,), (sums, above), planes * rows * cols)
     if doubling:
         *sums, near = lax.optimization_barrier((*sums, near))

time: 93.3 us -> 94.5 us (1.013)
  waiting for transfers between devices: 30.8 us -> 32.1 us
    ppermute x23, waiting for transfers between devices: 20.5 us -> 24 us  [deal(): lax.ppermute(value, axes, [(k, k ^ turn) for k in range(len(order))])]
    ppermute x1, waiting for transfers between devices: 2.52 us -> 0.01 us  [local(): lax.ppermute(lower_sums, 'pair', [(k, k + 1) for k in range(pairs - 1)])]
    pallas_call x10 -> x11, Pallas kernels: 16.3 us -> 16.4 us  [call(): pl.pallas_call(kernel, out_shape=[x for x, unused in outs], in_specs=[SME...]
  transfers between devices with their start and end apart: 29 -> 29, of which waited for: 13 -> 14; matrix products, arithmetic and copies ran while one was open for 0% -> 0% of each run, Pallas kernels for 6% -> 6%
where the time goes in v16:
time: 94.5 us; the launch traced here: 94.2 us
  starting transfers between devices  34.2 us (36%)
  waiting for transfers between devices  32.1 us (34%)
  Pallas kernels  16.4 us (17%)
  blocking collectives  10.1 us (11%)
    ppermute x23, waiting for transfers between devices, deal(): lax.ppermute(value, axes, [(k, k ^ turn) for k in range(len(order))])  24 us
    ppermute x23, starting transfers between devices, deal(): lax.ppermute(value, axes, [(k, k ^ turn) for k in range(len(order))])  23.2 us
    pallas_call x11, Pallas kernels, call(): pl.pallas_call(kernel, out_shape=[x for x, unused in outs], in_specs=[SME...  16.4 us
    all_gather x1, blocking collectives, local(): probe_grad = lax.all_gather(probe_band, PLANE, axis=0, tiled=True)  10.1 us
    ppermute x1, waiting for transfers between devices, local(): below = lax.ppermute(lowest, 'pair', [(k, k - 1) for k in range(1, pairs)])  7.62 us
    ppermute x1, starting transfers between devices, local(): lax.ppermute(lower_sums, 'pair', [(k, k + 1) for k in range(pairs - 1)])  3.77 us
    ppermute x1, starting transfers between devices, sum_over(): lax.ppermute(value, axis, [(k, k ^ step) for k in range(size)])  2.63 us
  transfers between devices with their start and end apart: 29, of which 14 were waited for; matrix products, arithmetic and copies ran while one was open for 0% of the time, Pallas kernels for 6%

profile of v16, /device:TPU:0, one launch (start us, length us, event | category | flops | bytes accessed | tf_op | source)
XLA Modules:
  0.0 94.2 jit_solution(7309069088570529678)
XLA Ops:
  0.7 2.0 %shard_map.95 = (f32[264,128]{1,0:T(8,128)S(1)}, f32[264,128]{1,0:T(8,128)S(1)}, f32[264,128]{1,0:T(8,128)S(1)}, f32[264,128]{1,0:T(8,128)S(1)}, f32[256,256]{1,0:T(8,128)S(1)}) custom-call(s32[3]{0:T(128)S(1)} %pad_add_fusion.1.where, s32[1,2,2]{2,1,0:T(2,128)} %offsets.1, f32[4,256,128]{2,1,0:T(8,128)} %bitcast.10, f32[1,2,256,256]{3,2,1,0:T(8,128)} %measured.3), custom_call_target="tpu_custom_call" | custom-call | bytes 1851392 | tf_op jit(solution)/shard_map/pallas_call | solution.py:353
  2.7 3.0 %collective-permute-start = (f32[264,128]{1,0:T(8,128)S(1)}, f32[264,128]{1,0:T(8,128)S(1)}, u32[]{:S(2)}, u32[]{:S(2)}) collective-permute-start(f32[264,128]{1,0:T(8,128)S(1)} %get-tuple-element.56), channel_id=1, source_target_pairs={{0,2},{2,0},{4,6},{6,4},{1,3},{3,1},{5,7},{7,5},{8,10},{10,8},{12,... | collective-permute-start | bytes 405512 | tf_op jit(solution)/shard_map/ppermute | solution.py:370
  5.7 1.5 %collective-permute-start.1 = (f32[264,128]{1,0:T(8,128)S(1)}, f32[264,128]{1,0:T(8,128)S(1)}, u32[]{:S(2)}, u32[]{:S(2)}) collective-permute-start(f32[264,128]{1,0:T(8,128)S(1)} %get-tuple-element.57), channel_id=1, source_target_pairs={{0,4},{2,6},{4,0},{6,2},{1,5},{3,7},{5,1},{7,3},{8,12},{10,14},{12... | collective-permute-start | bytes 405512 | tf_op jit(solution)/shard_map/ppermute | solution.py:370
  7.3 2.3 %collective-permute-done.refs_1_ = f32[264,128]{1,0:T(8,128)S(1)} collective-permute-done((f32[264,128]{1,0:T(8,128)S(1)}, f32[264,128]{1,0:T(8,128)S(1)}, u32[]{:S(2)}, u32[]{:S(2)}) %collective-permute-start) | collective-permute-done | bytes 135200 | tf_op jit(solution)/shard_map/ppermute | solution.py:370
  9.8 3.8 %collective-permute-done.1.refs_0_ = f32[264,128]{1,0:T(8,128)S(1)} collective-permute-done((f32[264,128]{1,0:T(8,128)S(1)}, f32[264,128]{1,0:T(8,128)S(1)}, u32[]{:S(2)}, u32[]{:S(2)}) %collective-permute-start.1) | collective-permute-done | bytes 135200 | tf_op jit(solution)/shard_map/ppermute | solution.py:370
  14.0 0.6 shard_map.96
  14.5 1.3 %collective-permute-start.4 = (f32[2,256,128]{2,1,0:T(8,128)S(1)}, f32[2,256,128]{2,1,0:T(8,128)S(1)}, u32[]{:S(2)}, u32[]{:S(2)}) collective-permute-start(f32[2,256,128]{2,1,0:T(8,128)S(1)} %shard_map.96), channel_id=1, source_target_pairs={{8,0},{16,8},{24,16},{9,1},{17,9},{25,17},{10,2},{18,10},{26,18},{... | collective-permute-start | bytes 786440 | tf_op jit(solution)/shard_map/ppermute | solution.py:404
  15.8 1.6 %collective-permute-start.5 = (f32[256,256]{1,0:T(8,128)S(1)}, f32[256,256]{1,0:T(8,128)S(1)}, u32[]{:S(2)}, u32[]{:S(2)}) collective-permute-start(f32[256,256]{1,0:T(8,128)S(1)} %get-tuple-element.61), channel_id=1, source_target_pairs={{0,4},{4,0},{1,5},{5,1},{2,6},{6,2},{3,7},{7,3},{8,12},{12,8},{9,1... | collective-permute-start | bytes 786440 | tf_op jit(solution)/shard_map/ppermute | solution.py:405
  17.5 7.6 %collective-permute-done.4.refs_4_ = f32[2,256,128]{2,1,0:T(8,128)S(1)} collective-permute-done((f32[2,256,128]{2,1,0:T(8,128)S(1)}, f32[2,256,128]{2,1,0:T(8,128)S(1)}, u32[]{:S(2)}, u32[]{:S(2)}) %collective-permute-start.4) | collective-permute-done | bytes 262176 | tf_op jit(solution)/shard_map/ppermute | solution.py:404
  25.1 1.4 %shard_map.97 = (f32[256,128]{1,0:T(8,128)S(1)}, f32[256,128]{1,0:T(8,128)S(1)}, f32[256,128]{1,0:T(8,128)S(1)}, f32[256,128]{1,0:T(8,128)S(1)}, f32[256,128]{1,...) custom-call(s32[3]{0:T(128)S(1)} %pad_add_fusion.1.where, ...), custom_call_target="tpu_custom_call" | custom-call | flops 2097152 | bytes 1851392 | tf_op jit(solution)/shard_map/pallas_call | solution.py:353
  26.6 1.6 %collective-permute-start.6 = (f32[256,128]{1,0:T(8,128)S(1)}, f32[256,128]{1,0:T(8,128)S(1)}, u32[]{:S(2)}, u32[]{:S(2)}) collective-permute-start(f32[256,128]{1,0:T(8,128)S(1)} %get-tuple-element.63), channel_id=1, source_target_pairs={{0,4},{1,5},{2,6},{3,7},{4,0},{5,1},{6,2},{7,3},{8,12},{9,13},{10,... | collective-permute-start | bytes 393224 | tf_op jit(solution)/shard_map/ppermute | solution.py:370
  28.2 0.5 collective-permute-start.7
  28.7 1.7 %collective-permute-start.9 = (f32[256,128]{1,0:T(8,128)S(1)}, f32[256,128]{1,0:T(8,128)S(1)}, u32[]{:S(2)}, u32[]{:S(2)}) collective-permute-start(f32[256,128]{1,0:T(8,128)S(1)} %get-tuple-element.66), channel_id=1, source_target_pairs={{0,3},{1,2},{2,1},{3,0},{4,7},{5,6},{6,5},{7,4},{8,11},{9,10},{10,... | collective-permute-start | bytes 393224 | tf_op jit(solution)/shard_map/ppermute | solution.py:370
  30.4 1.5 %collective-permute-start.10 = (f32[256,128]{1,0:T(8,128)S(1)}, f32[256,128]{1,0:T(8,128)S(1)}, u32[]{:S(2)}, u32[]{:S(2)}) collective-permute-start(f32[256,128]{1,0:T(8,128)S(1)} %get-tuple-element.67), channel_id=1, source_target_pairs={{0,6},{1,7},{2,4},{3,5},{4,2},{5,3},{6,0},{7,1},{8,14},{9,15},{10,... | collective-permute-start | bytes 393224 | tf_op jit(solution)/shard_map/ppermute | solution.py:370
  31.9 0.7 collective-permute-start.11
  32.6 2.0 %collective-permute-done.7.refs_1_ = f32[256,128]{1,0:T(8,128)S(1)} collective-permute-done((f32[256,128]{1,0:T(8,128)S(1)}, f32[256,128]{1,0:T(8,128)S(1)}, u32[]{:S(2)}, u32[]{:S(2)}) %collective-permute-start.7) | collective-permute-done | bytes 131104 | tf_op jit(solution)/shard_map/ppermute | solution.py:370
  34.6 2.7 %shard_map.98 = (f32[2,256,256]{2,1,0:T(8,128)S(1)}, f32[256,256]{1,0:T(8,128)S(1)}, bf16[6,512,256]{2,1,0:T(8,128)(2,1)S(1)}) custom-call(s32[3]{0:T(128)S(1)} %pad_add_fusion.1.where, s32[1,2]{1,0:T(1,128)} %slot_range.9, s32[4,8]{1,0:T(4,128)S(1)} %pad_add_fusion.offs, f32[256,256]{1,0:T(8,128)S(1)} %collective-permute-done.5.taken, ...), custom_call_target="tpu_custom_call" | custom-call | flops 201326592 | bytes 5505024 | tf_op jit(solution)/shard_map/pallas_call | solution.py:353
  37.3 1.9 %collective-permute-done.10.refs_4_ = f32[256,128]{1,0:T(8,128)S(1)} collective-permute-done((f32[256,128]{1,0:T(8,128)S(1)}, f32[256,128]{1,0:T(8,128)S(1)}, u32[]{:S(2)}, u32[]{:S(2)}) %collective-permute-start.10) | collective-permute-done | bytes 131104 | tf_op jit(solution)/shard_map/ppermute | solution.py:370
  39.2 1.9 %collective-permute-done.11.refs_5_ = f32[256,128]{1,0:T(8,128)S(1)} collective-permute-done((f32[256,128]{1,0:T(8,128)S(1)}, f32[256,128]{1,0:T(8,128)S(1)}, u32[]{:S(2)}, u32[]{:S(2)}) %collective-permute-start.11) | collective-permute-done | bytes 131104 | tf_op jit(solution)/shard_map/ppermute | solution.py:370
  41.1 4.3 %shard_map.99 = (f32[768,128]{1,0:T(8,128)S(1)}, f32[256,128]{1,0:T(8,128)S(1)}, f32[256,128]{1,0:T(8,128)S(1)}, f32[256,128]{1,0:T(8,128)S(1)}, f32[256,128]{1,...) custom-call(s32[3]{0:T(128)S(1)} %pad_add_fusion.1.where, ...), custom_call_target="tpu_custom_call" | custom-call | flops 1610612736 | bytes 5120000 | tf_op jit(solution)/shard_map/pallas_call | solution.py:353
  45.3 0.4 collective-permute-start.13
  45.7 1.5 %collective-permute-start.14 = (f32[256,128]{1,0:T(8,128)S(1)}, f32[256,128]{1,0:T(8,128)S(1)}, u32[]{:S(2)}, u32[]{:S(2)}) collective-permute-start(f32[256,128]{1,0:T(8,128)S(1)} %get-tuple-element.76), channel_id=1, source_target_pairs={{0,4},{1,5},{2,6},{3,7},{4,0},{5,1},{6,2},{7,3},{8,12},{9,13},{10,... | collective-permute-start | bytes 393224 | tf_op jit(solution)/shard_map/ppermute | solution.py:370
  47.2 0.6 collective-permute-start.15
  47.9 1.5 %collective-permute-start.17 = (f32[256,128]{1,0:T(8,128)S(1)}, f32[256,128]{1,0:T(8,128)S(1)}, u32[]{:S(2)}, u32[]{:S(2)}) collective-permute-start(f32[256,128]{1,0:T(8,128)S(1)} %get-tuple-element.79), channel_id=1, source_target_pairs={{0,3},{1,2},{2,1},{3,0},{4,7},{5,6},{6,5},{7,4},{8,11},{9,10},{10,... | collective-permute-start | bytes 393224 | tf_op jit(solution)/shard_map/ppermute | solution.py:370
  49.5 2.3 %collective-permute-done.14.refs_1_ = f32[256,128]{1,0:T(8,128)S(1)} collective-permute-done((f32[256,128]{1,0:T(8,128)S(1)}, f32[256,128]{1,0:T(8,128)S(1)}, u32[]{:S(2)}, u32[]{:S(2)}) %collective-permute-start.14) | collective-permute-done | bytes 131104 | tf_op jit(solution)/shard_map/ppermute | solution.py:370
  51.8 1.5 %collective-permute-start.18 = (f32[256,128]{1,0:T(8,128)S(1)}, f32[256,128]{1,0:T(8,128)S(1)}, u32[]{:S(2)}, u32[]{:S(2)}) collective-permute-start(f32[256,128]{1,0:T(8,128)S(1)} %get-tuple-element.80), channel_id=1, source_target_pairs={{0,6},{1,7},{2,4},{3,5},{4,2},{5,3},{6,0},{7,1},{8,14},{9,15},{10,... | collective-permute-start | bytes 393224 | tf_op jit(solution)/shard_map/ppermute | solution.py:370
  53.3 0.6 shard_map.100
  53.9 0.3 collective-permute-done.17.refs_4_
  54.3 4.7 %collective-permute-done.18.refs_5_ = f32[256,128]{1,0:T(8,128)S(1)} collective-permute-done((f32[256,128]{1,0:T(8,128)S(1)}, f32[256,128]{1,0:T(8,128)S(1)}, u32[]{:S(2)}, u32[]{:S(2)}) %collective-permute-start.18) | collective-permute-done | bytes 131104 | tf_op jit(solution)/shard_map/ppermute | solution.py:370
  59.0 1.0 %collective-permute-done.19.refs_6_ = f32[256,128]{1,0:T(8,128)S(1)} collective-permute-done((f32[256,128]{1,0:T(8,128)S(1)}, f32[256,128]{1,0:T(8,128)S(1)}, u32[]{:S(2)}, u32[]{:S(2)}) %collective-permute-start.19) | collective-permute-done | bytes 131104 | tf_op jit(solution)/shard_map/ppermute | solution.py:370
  60.0 1.1 %shard_map.102 = f32[2,256,128]{2,1,0:T(8,128)S(1)} custom-call(s32[3]{0:T(128)S(1)} %pad_add_fusion.1.where, s32[1,2]{1,0:T(1,128)} %slot_range.9, s32[4,8]{1,0:T(4,128)S(1)} %pad_add_fusion.offs, f32[768,128]{1,0:T(8,128)S(1)} %collective-permute-done.13.got.refs_0_, f32[256,128]{1,0:T(8,128)S(1)} %collective-permute-done.14.refs_1_, ...), custom_call_target="tpu_custom_call" | custom-call | flops 2097152 | bytes 1572864 | tf_op jit(solution)/shard_map/pallas_call | solution.py:353
  61.1 3.8 %collective-permute-start.20 = (f32[2,256,128]{2,1,0:T(8,128)S(1)}, f32[2,256,128]{2,1,0:T(8,128)S(1)}, u32[]{:S(2)}, u32[]{:S(2)}) collective-permute-start(f32[2,256,128]{2,1,0:T(8,128)S(1)} %shard_map.102), channel_id=1, source_target_pairs={{0,8},{8,16},{16,24},{1,9},{9,17},{17,25},{2,10},{10,18},{18,26},{... | collective-permute-start | bytes 786440 | tf_op jit(solution)/shard_map/ppermute | solution.py:444
  64.9 0.9 collective-permute-start.21
  65.8 1.1 %collective-permute-start.22 = (f32[128,128]{1,0:T(8,128)S(1)}, f32[128,128]{1,0:T(8,128)S(1)}, u32[]{:S(2)}, u32[]{:S(2)}) collective-permute-start(f32[128,128]{1,0:T(8,128)S(1)} %get-tuple-element.98), channel_id=1, source_target_pairs={{0,2},{2,0},{4,6},{6,4},{1,3},{3,1},{5,7},{7,5},{8,10},{10,8},{12,... | collective-permute-start | bytes 196616 | tf_op jit(solution)/shard_map/ppermute | solution.py:370
  66.9 1.5 %collective-permute-start.23 = (f32[128,128]{1,0:T(8,128)S(1)}, f32[128,128]{1,0:T(8,128)S(1)}, u32[]{:S(2)}, u32[]{:S(2)}) collective-permute-start(f32[128,128]{1,0:T(8,128)S(1)} %get-tuple-element.99), channel_id=1, source_target_pairs={{0,6},{2,4},{4,2},{6,0},{1,7},{3,5},{5,3},{7,1},{8,14},{10,12},{12... | collective-permute-start | bytes 196616 | tf_op jit(solution)/shard_map/ppermute | solution.py:370
  68.4 0.9 %collective-permute-done.21.refs_0_ = f32[128,128]{1,0:T(8,128)S(1)} collective-permute-done((f32[128,128]{1,0:T(8,128)S(1)}, f32[128,128]{1,0:T(8,128)S(1)}, u32[]{:S(2)}, u32[]{:S(2)}) %collective-permute-start.21) | collective-permute-done | bytes 65568 | tf_op jit(solution)/shard_map/ppermute | solution.py:370
  69.4 1.3 %collective-permute-done.22.refs_1_ = f32[128,128]{1,0:T(8,128)S(1)} collective-permute-done((f32[128,128]{1,0:T(8,128)S(1)}, f32[128,128]{1,0:T(8,128)S(1)}, u32[]{:S(2)}, u32[]{:S(2)}) %collective-permute-start.22) | collective-permute-done | bytes 65568 | tf_op jit(solution)/shard_map/ppermute | solution.py:370
  70.7 1.4 %collective-permute-done.23.refs_2_ = f32[128,128]{1,0:T(8,128)S(1)} collective-permute-done((f32[128,128]{1,0:T(8,128)S(1)}, f32[128,128]{1,0:T(8,128)S(1)}, u32[]{:S(2)}, u32[]{:S(2)}) %collective-permute-start.23) | collective-permute-done | bytes 65568 | tf_op jit(solution)/shard_map/ppermute | solution.py:370
  72.1 1.6 %collective-permute-start.24 = (f32[64,256]{1,0:T(8,128)S(1)}, f32[64,256]{1,0:T(8,128)S(1)}, u32[]{:S(2)}, u32[]{:S(2)}) collective-permute-start(f32[64,256]{1,0:T(8,128)S(1)} %shard_map.104), channel_id=1, source_target_pairs={{0,8},{8,0},{16,24},{24,16},{1,9},{9,1},{17,25},{25,17},{2,10},{10... | collective-permute-start | bytes 196616 | tf_op jit(solution)/shard_map/ppermute | solution.py:449
  73.7 1.6 %shard_map.101.own = f32[4,256,128]{2,1,0:T(8,128)S(1)} custom-call(s32[3]{0:T(128)S(1)} %pad_add_fusion.1.where, s32[1,2]{1,0:T(1,128)} %slot_range.9, s32[4,8]{1,0:T(4,128)S(1)} %pad_add_fusion.offs, f32[768,128]{1,0:T(8,128)S(1)} %collective-permute-done.13.got.refs_0_, f32[256,128]{1,0:T(8,128)S(1)} %collective-permute-done.14.refs_1_, ...), custom_call_target="tpu_custom_call" | custom-call | flops 4194304 | bytes 1835008 | tf_op jit(solution)/shard_map/pallas_call | solution.py:353
  75.3 0.6 shard_map.103
  75.9 0.5 collective-permute-done.24
  76.5 2.6 %collective-permute-start.28 = (f32[64,256]{1,0:T(8,128)S(1)}, f32[64,256]{1,0:T(8,128)S(1)}, u32[]{:S(2)}, u32[]{:S(2)}) collective-permute-start(f32[64,256]{1,0:T(8,128)S(1)} %add.6), channel_id=1, source_target_pairs={{0,16},{8,24},{16,0},{24,8},{1,17},{9,25},{17,1},{25,9},{2,18},{10... | collective-permute-start | bytes 196616 | tf_op jit(solution)/shard_map/ppermute | solution.py:378
  79.1 1.7 %collective-permute-start.25 = (f32[256,128]{1,0:T(8,128)S(1)}, f32[256,128]{1,0:T(8,128)S(1)}, u32[]{:S(2)}, u32[]{:S(2)}) collective-permute-start(f32[256,128]{1,0:T(8,128)S(1)} %get-tuple-element.101), channel_id=1, source_target_pairs={{0,4},{2,6},{4,0},{6,2},{1,5},{3,7},{5,1},{7,3},{8,12},{10,14},{12... | collective-permute-start | bytes 393224 | tf_op jit(solution)/shard_map/ppermute | solution.py:370
  80.8 0.3 collective-permute-start.26
  81.2 1.4 %collective-permute-start.27 = (f32[256,128]{1,0:T(8,128)S(1)}, f32[256,128]{1,0:T(8,128)S(1)}, u32[]{:S(2)}, u32[]{:S(2)}) collective-permute-start(f32[256,128]{1,0:T(8,128)S(1)} %get-tuple-element.103), channel_id=1, source_target_pairs={{0,6},{2,4},{4,2},{6,0},{1,7},{3,5},{5,3},{7,1},{8,14},{10,12},{12... | collective-permute-start | bytes 393224 | tf_op jit(solution)/shard_map/ppermute | solution.py:370
  82.6 10.1 %all_gather.3.refs_4_ = f32[512,256]{1,0:T(8,128)S(1)} all-gather(f32[64,256]{1,0:T(8,128)S(1)} %add.7), channel_id=1, replica_groups=mesh['pair'=4,'half'=2,'col'=2,'core'=2] {'half','col','core'}, dimensions={0}, use_global_device_ids=true | all-gather | bytes 589824 | tf_op jit(solution)/shard_map/all_gather | solution.py:457
  92.7 1.5 %shard_map.105 = (f32[4,256,128]{2,1,0:T(8,128)}, f32[512,256]{1,0:T(8,128)}) custom-call(s32[3]{0:T(128)S(1)} %pad_add_fusion.1.where, f32[256,128]{1,0:T(8,128)S(1)} %collective-permute-done.25.refs_0_, f32[256,128]{1,0:T(8,128)S(1)} %collective-permute-done.26.refs_1_, f32[256,128]{1,0:T(8,128)S(1)} %collective-permute-done.27.refs_2_, ...), custom_call_target="tpu_custom_call" | custom-call | bytes 2097152 | tf_op jit(solution)/shard_map/pallas_call | solution.py:353
  (34 shorter events, 1.0 us)
Async XLA Ops:
  2.7 7.0 %collective-permute-start = (f32[264,128]{1,0:T(8,128)S(1)}, f32[264,128]{1,0:T(8,128)S(1)}, u32[]{:S(2)}, u32[]{:S(2)}) collective-permute-start(f32[264,128]{1,0:T(8,128)S(1)} %get-tuple-element.56), channel_id=1, source_target_pairs={{0,2},{2,0},{4,6},{6,4},{1,3},{3,1},{5,7},{7,5},{8,10},{10,8},{12,... | collective-permute-start | bytes 405512 | tf_op jit(solution)/shard_map/ppermute | solution.py:370
  5.7 7.9 %collective-permute-start.1 = (f32[264,128]{1,0:T(8,128)S(1)}, f32[264,128]{1,0:T(8,128)S(1)}, u32[]{:S(2)}, u32[]{:S(2)}) collective-permute-start(f32[264,128]{1,0:T(8,128)S(1)} %get-tuple-element.57), channel_id=1, source_target_pairs={{0,4},{2,6},{4,0},{6,2},{1,5},{3,7},{5,1},{7,3},{8,12},{10,14},{12... | collective-permute-start | bytes 405512 | tf_op jit(solution)/shard_map/ppermute | solution.py:370
  7.2 6.5 %collective-permute-start.2 = (f32[264,128]{1,0:T(8,128)S(1)}, f32[264,128]{1,0:T(8,128)S(1)}, u32[]{:S(2)}, u32[]{:S(2)}) collective-permute-start(f32[264,128]{1,0:T(8,128)S(1)} %get-tuple-element.58), channel_id=1, source_target_pairs={{0,6},{2,4},{4,2},{6,0},{1,7},{3,5},{5,3},{7,1},{8,14},{10,12},{12... | collective-permute-start | bytes 405512 | tf_op jit(solution)/shard_map/ppermute | solution.py:370
  13.9 3.5 %collective-permute-start.3 = (s32[4,4]{1,0:T(4,128)S(1)}, s32[4,4]{1,0:T(4,128)S(1)}, u32[]{:S(2)}, u32[]{:S(2)}) collective-permute-start(s32[4,4]{1,0:T(4,128)S(1)} %maximum_convert_fusion), channel_id=1, source_target_pairs={{0,1},{1,0},{2,3},{3,2},{4,5},{5,4},{6,7},{7,6},{8,9},{9,8},{10,11... | collective-permute-start | bytes 200 | tf_op jit(solution)/shard_map/ppermute | solution.py:410
  14.5 10.6 %collective-permute-start.4 = (f32[2,256,128]{2,1,0:T(8,128)S(1)}, f32[2,256,128]{2,1,0:T(8,128)S(1)}, u32[]{:S(2)}, u32[]{:S(2)}) collective-permute-start(f32[2,256,128]{2,1,0:T(8,128)S(1)} %shard_map.96), channel_id=1, source_target_pairs={{8,0},{16,8},{24,16},{9,1},{17,9},{25,17},{10,2},{18,10},{26,18},{... | collective-permute-start | bytes 786440 | tf_op jit(solution)/shard_map/ppermute | solution.py:404
  15.8 9.3 %collective-permute-start.5 = (f32[256,256]{1,0:T(8,128)S(1)}, f32[256,256]{1,0:T(8,128)S(1)}, u32[]{:S(2)}, u32[]{:S(2)}) collective-permute-start(f32[256,256]{1,0:T(8,128)S(1)} %get-tuple-element.61), channel_id=1, source_target_pairs={{0,4},{4,0},{1,5},{5,1},{2,6},{6,2},{3,7},{7,3},{8,12},{12,8},{9,1... | collective-permute-start | bytes 786440 | tf_op jit(solution)/shard_map/ppermute | solution.py:405
  26.6 5.3 %collective-permute-start.6 = (f32[256,128]{1,0:T(8,128)S(1)}, f32[256,128]{1,0:T(8,128)S(1)}, u32[]{:S(2)}, u32[]{:S(2)}) collective-permute-start(f32[256,128]{1,0:T(8,128)S(1)} %get-tuple-element.63), channel_id=1, source_target_pairs={{0,4},{1,5},{2,6},{3,7},{4,0},{5,1},{6,2},{7,3},{8,12},{9,13},{10,... | collective-permute-start | bytes 393224 | tf_op jit(solution)/shard_map/ppermute | solution.py:370
  28.2 6.4 %collective-permute-start.7 = (f32[256,128]{1,0:T(8,128)S(1)}, f32[256,128]{1,0:T(8,128)S(1)}, u32[]{:S(2)}, u32[]{:S(2)}) collective-permute-start(f32[256,128]{1,0:T(8,128)S(1)} %get-tuple-element.64), channel_id=1, source_target_pairs={{0,2},{1,3},{2,0},{3,1},{4,6},{5,7},{6,4},{7,5},{8,10},{9,11},{10,... | collective-permute-start | bytes 393224 | tf_op jit(solution)/shard_map/ppermute | solution.py:370
  28.7 8.6 %collective-permute-start.8 = (f32[256,128]{1,0:T(8,128)S(1)}, f32[256,128]{1,0:T(8,128)S(1)}, u32[]{:S(2)}, u32[]{:S(2)}) collective-permute-start(f32[256,128]{1,0:T(8,128)S(1)} %get-tuple-element.65), channel_id=1, source_target_pairs={{0,5},{1,4},{2,7},{3,6},{4,1},{5,0},{6,3},{7,2},{8,13},{9,12},{10,... | collective-permute-start | bytes 393224 | tf_op jit(solution)/shard_map/ppermute | solution.py:370
  28.7 8.6 %collective-permute-start.9 = (f32[256,128]{1,0:T(8,128)S(1)}, f32[256,128]{1,0:T(8,128)S(1)}, u32[]{:S(2)}, u32[]{:S(2)}) collective-permute-start(f32[256,128]{1,0:T(8,128)S(1)} %get-tuple-element.66), channel_id=1, source_target_pairs={{0,3},{1,2},{2,1},{3,0},{4,7},{5,6},{6,5},{7,4},{8,11},{9,10},{10,... | collective-permute-start | bytes 393224 | tf_op jit(solution)/shard_map/ppermute | solution.py:370
  30.4 8.7 %collective-permute-start.10 = (f32[256,128]{1,0:T(8,128)S(1)}, f32[256,128]{1,0:T(8,128)S(1)}, u32[]{:S(2)}, u32[]{:S(2)}) collective-permute-start(f32[256,128]{1,0:T(8,128)S(1)} %get-tuple-element.67), channel_id=1, source_target_pairs={{0,6},{1,7},{2,4},{3,5},{4,2},{5,3},{6,0},{7,1},{8,14},{9,15},{10,... | collective-permute-start | bytes 393224 | tf_op jit(solution)/shard_map/ppermute | solution.py:370
  31.9 9.1 %collective-permute-start.11 = (f32[256,128]{1,0:T(8,128)S(1)}, f32[256,128]{1,0:T(8,128)S(1)}, u32[]{:S(2)}, u32[]{:S(2)}) collective-permute-start(f32[256,128]{1,0:T(8,128)S(1)} %get-tuple-element.68), channel_id=1, source_target_pairs={{0,7},{1,6},{2,5},{3,4},{4,3},{5,2},{6,1},{7,0},{8,15},{9,14},{10,... | collective-permute-start | bytes 393224 | tf_op jit(solution)/shard_map/ppermute | solution.py:370
  34.5 6.5 %copy-start = (f32[2,136,128]{2,1,0:T(8,128)S(1)}, f32[2,136,128]{2,1,0:T(8,128)}, u32[]{:S(2)}) copy-start(f32[2,136,128]{2,1,0:T(8,128)} %constant.19.clone.refs_11_) | copy-start | bytes 417796
  34.6 6.5 %collective-permute-start.12 = (f32[256,128]{1,0:T(8,128)S(1)}, f32[256,128]{1,0:T(8,128)S(1)}, u32[]{:S(2)}, u32[]{:S(2)}) collective-permute-start(f32[256,128]{1,0:T(8,128)S(1)} %get-tuple-element.69), channel_id=1, source_target_pairs={{0,1},{1,0},{2,3},{3,2},{4,5},{5,4},{6,7},{7,6},{8,9},{9,8},{10,11... | collective-permute-start | bytes 393224 | tf_op jit(solution)/shard_map/ppermute | solution.py:370
  45.3 8.0 %collective-permute-start.13 = (f32[768,128]{1,0:T(8,128)S(1)}, f32[768,128]{1,0:T(8,128)S(1)}, u32[]{:S(2)}, u32[]{:S(2)}) collective-permute-start(f32[768,128]{1,0:T(8,128)S(1)} %get-tuple-element.75), channel_id=1, source_target_pairs={{0,1},{1,0},{2,3},{3,2},{4,5},{5,4},{6,7},{7,6},{8,9},{9,8},{10,11... | collective-permute-start | bytes 1179656 | tf_op jit(solution)/shard_map/ppermute | solution.py:370
  45.7 6.1 %collective-permute-start.14 = (f32[256,128]{1,0:T(8,128)S(1)}, f32[256,128]{1,0:T(8,128)S(1)}, u32[]{:S(2)}, u32[]{:S(2)}) collective-permute-start(f32[256,128]{1,0:T(8,128)S(1)} %get-tuple-element.76), channel_id=1, source_target_pairs={{0,4},{1,5},{2,6},{3,7},{4,0},{5,1},{6,2},{7,3},{8,12},{9,13},{10,... | collective-permute-start | bytes 393224 | tf_op jit(solution)/shard_map/ppermute | solution.py:370
  47.2 6.7 %collective-permute-start.15 = (f32[256,128]{1,0:T(8,128)S(1)}, f32[256,128]{1,0:T(8,128)S(1)}, u32[]{:S(2)}, u32[]{:S(2)}) collective-permute-start(f32[256,128]{1,0:T(8,128)S(1)} %get-tuple-element.77), channel_id=1, source_target_pairs={{0,2},{1,3},{2,0},{3,1},{4,6},{5,7},{6,4},{7,5},{8,10},{9,11},{10,... | collective-permute-start | bytes 393224 | tf_op jit(solution)/shard_map/ppermute | solution.py:370
  47.7 6.2 %collective-permute-start.16 = (f32[256,128]{1,0:T(8,128)S(1)}, f32[256,128]{1,0:T(8,128)S(1)}, u32[]{:S(2)}, u32[]{:S(2)}) collective-permute-start(f32[256,128]{1,0:T(8,128)S(1)} %get-tuple-element.78), channel_id=1, source_target_pairs={{0,5},{1,4},{2,7},{3,6},{4,1},{5,0},{6,3},{7,2},{8,13},{9,12},{10,... | collective-permute-start | bytes 393224 | tf_op jit(solution)/shard_map/ppermute | solution.py:370
  47.9 6.3 %collective-permute-start.17 = (f32[256,128]{1,0:T(8,128)S(1)}, f32[256,128]{1,0:T(8,128)S(1)}, u32[]{:S(2)}, u32[]{:S(2)}) collective-permute-start(f32[256,128]{1,0:T(8,128)S(1)} %get-tuple-element.79), channel_id=1, source_target_pairs={{0,3},{1,2},{2,1},{3,0},{4,7},{5,6},{6,5},{7,4},{8,11},{9,10},{10,... | collective-permute-start | bytes 393224 | tf_op jit(solution)/shard_map/ppermute | solution.py:370
  51.8 7.2 %collective-permute-start.18 = (f32[256,128]{1,0:T(8,128)S(1)}, f32[256,128]{1,0:T(8,128)S(1)}, u32[]{:S(2)}, u32[]{:S(2)}) collective-permute-start(f32[256,128]{1,0:T(8,128)S(1)} %get-tuple-element.80), channel_id=1, source_target_pairs={{0,6},{1,7},{2,4},{3,5},{4,2},{5,3},{6,0},{7,1},{8,14},{9,15},{10,... | collective-permute-start | bytes 393224 | tf_op jit(solution)/shard_map/ppermute | solution.py:370
  53.3 6.7 %collective-permute-start.19 = (f32[256,128]{1,0:T(8,128)S(1)}, f32[256,128]{1,0:T(8,128)S(1)}, u32[]{:S(2)}, u32[]{:S(2)}) collective-permute-start(f32[256,128]{1,0:T(8,128)S(1)} %get-tuple-element.81), channel_id=1, source_target_pairs={{0,7},{1,6},{2,5},{3,4},{4,3},{5,2},{6,1},{7,0},{8,15},{9,14},{10,... | collective-permute-start | bytes 393224 | tf_op jit(solution)/shard_map/ppermute | solution.py:370
  61.1 14.2 %collective-permute-start.20 = (f32[2,256,128]{2,1,0:T(8,128)S(1)}, f32[2,256,128]{2,1,0:T(8,128)S(1)}, u32[]{:S(2)}, u32[]{:S(2)}) collective-permute-start(f32[2,256,128]{2,1,0:T(8,128)S(1)} %shard_map.102), channel_id=1, source_target_pairs={{0,8},{8,16},{16,24},{1,9},{9,17},{17,25},{2,10},{10,18},{18,26},{... | collective-permute-start | bytes 786440 | tf_op jit(solution)/shard_map/ppermute | solution.py:444
  64.9 4.5 %collective-permute-start.21 = (f32[128,128]{1,0:T(8,128)S(1)}, f32[128,128]{1,0:T(8,128)S(1)}, u32[]{:S(2)}, u32[]{:S(2)}) collective-permute-start(f32[128,128]{1,0:T(8,128)S(1)} %get-tuple-element.97), channel_id=1, source_target_pairs={{0,4},{2,6},{4,0},{6,2},{1,5},{3,7},{5,1},{7,3},{8,12},{10,14},{12... | collective-permute-start | bytes 196616 | tf_op jit(solution)/shard_map/ppermute | solution.py:370
  65.8 4.9 %collective-permute-start.22 = (f32[128,128]{1,0:T(8,128)S(1)}, f32[128,128]{1,0:T(8,128)S(1)}, u32[]{:S(2)}, u32[]{:S(2)}) collective-permute-start(f32[128,128]{1,0:T(8,128)S(1)} %get-tuple-element.98), channel_id=1, source_target_pairs={{0,2},{2,0},{4,6},{6,4},{1,3},{3,1},{5,7},{7,5},{8,10},{10,8},{12,... | collective-permute-start | bytes 196616 | tf_op jit(solution)/shard_map/ppermute | solution.py:370
  66.9 5.2 %collective-permute-start.23 = (f32[128,128]{1,0:T(8,128)S(1)}, f32[128,128]{1,0:T(8,128)S(1)}, u32[]{:S(2)}, u32[]{:S(2)}) collective-permute-start(f32[128,128]{1,0:T(8,128)S(1)} %get-tuple-element.99), channel_id=1, source_target_pairs={{0,6},{2,4},{4,2},{6,0},{1,7},{3,5},{5,3},{7,1},{8,14},{10,12},{12... | collective-permute-start | bytes 196616 | tf_op jit(solution)/shard_map/ppermute | solution.py:370
  72.1 4.3 %collective-permute-start.24 = (f32[64,256]{1,0:T(8,128)S(1)}, f32[64,256]{1,0:T(8,128)S(1)}, u32[]{:S(2)}, u32[]{:S(2)}) collective-permute-start(f32[64,256]{1,0:T(8,128)S(1)} %shard_map.104), channel_id=1, source_target_pairs={{0,8},{8,0},{16,24},{24,16},{1,9},{9,1},{17,25},{25,17},{2,10},{10... | collective-permute-start | bytes 196616 | tf_op jit(solution)/shard_map/ppermute | solution.py:449
  76.5 6.1 %collective-permute-start.28 = (f32[64,256]{1,0:T(8,128)S(1)}, f32[64,256]{1,0:T(8,128)S(1)}, u32[]{:S(2)}, u32[]{:S(2)}) collective-permute-start(f32[64,256]{1,0:T(8,128)S(1)} %add.6), channel_id=1, source_target_pairs={{0,16},{8,24},{16,0},{24,8},{1,17},{9,25},{17,1},{25,9},{2,18},{10... | collective-permute-start | bytes 196616 | tf_op jit(solution)/shard_map/ppermute | solution.py:378
  79.1 13.6 %collective-permute-start.25 = (f32[256,128]{1,0:T(8,128)S(1)}, f32[256,128]{1,0:T(8,128)S(1)}, u32[]{:S(2)}, u32[]{:S(2)}) collective-permute-start(f32[256,128]{1,0:T(8,128)S(1)} %get-tuple-element.101), channel_id=1, source_target_pairs={{0,4},{2,6},{4,0},{6,2},{1,5},{3,7},{5,1},{7,3},{8,12},{10,14},{12... | collective-permute-start | bytes 393224 | tf_op jit(solution)/shard_map/ppermute | solution.py:370
  80.8 11.9 %collective-permute-start.26 = (f32[256,128]{1,0:T(8,128)S(1)}, f32[256,128]{1,0:T(8,128)S(1)}, u32[]{:S(2)}, u32[]{:S(2)}) collective-permute-start(f32[256,128]{1,0:T(8,128)S(1)} %get-tuple-element.102), channel_id=1, source_target_pairs={{0,2},{2,0},{4,6},{6,4},{1,3},{3,1},{5,7},{7,5},{8,10},{10,8},{12,... | collective-permute-start | bytes 393224 | tf_op jit(solution)/shard_map/ppermute | solution.py:370
  81.2 11.5 %collective-permute-start.27 = (f32[256,128]{1,0:T(8,128)S(1)}, f32[256,128]{1,0:T(8,128)S(1)}, u32[]{:S(2)}, u32[]{:S(2)}) collective-permute-start(f32[256,128]{1,0:T(8,128)S(1)} %get-tuple-element.103), channel_id=1, source_target_pairs={{0,6},{2,4},{4,2},{6,0},{1,7},{3,5},{5,3},{7,1},{8,14},{10,12},{12... | collective-permute-start | bytes 393224 | tf_op jit(solution)/shard_map/ppermute | solution.py:370

commit v17 on v15

--- a/solution.py
+++ b/solution.py
@@ -141,6 +141,10 @@
     return lower, offs[holder, at], offs[holder, at + 1]
 
 
+def here():
+    return tuple(lax.axis_index(name) for name in PLANE)
+
+
 def fetch(pairs, sems):
     copies = [pltpu.make_async_copy(source, into, sems.at[k]) for k, (source, into) in enumerate(pairs)]
     for copy in copies:
@@ -148,31 +152,34 @@
     return copies
 
 
-def deal_kernel(where, offsets, block, measured, *refs):
-    outs, given, sems = refs[:4], refs[4], refs[5]
-    mine = 2 * where[0] + where[1]
+def deal_kernel(block, measured, offsets_from, *refs):
+    outs, given, offsets, sems = refs[:4], refs[4], refs[5], refs[6]
+    half, col, unused = here()
+    mine = 2 * half + col
     rows, cols = block.shape[1:]
     pairs = [(block.at[jnp.bitwise_xor(mine, turn)], out.at[pl.ds(0, rows)]) for turn, out in zip(FOUR, outs)]
-    copies = fetch([*pairs, (measured.at[0, 1 - where[0]], given)], sems)
+    copies = fetch([(offsets_from, offsets), *pairs, (measured.at[0, 1 - half], given)], sems)
+    copies[0].wait()
     lines = [jnp.full((1, cols), offsets[0, slot, axis], jnp.int32) for slot in range(2) for axis in range(2)]
     lines = jnp.concatenate(lines * 2, axis=0).astype(jnp.float32)
     for out in outs:
         out[rows:] = lines
-    for copy in copies:
+    for copy in copies[1:]:
         copy.wait()
 
 
-def lowest_kernel(where, *refs):
+def lowest_kernel(*refs):
     gotten, out = dict(zip(FOUR, refs)), refs[4]
     rows = out.shape[1]
+    half = here()[0]
     for turn in range(2):
-        out[turn] = jnp.where(where[0] == 0, gotten[turn][:rows], gotten[2 + turn][:rows])
-
-
-def pick_kernel(where, slot_range, offs, *refs):
+        out[turn] = jnp.where(half == 0, gotten[turn][:rows], gotten[2 + turn][:rows])
+
+
+def pick_kernel(slot_range, offs, *refs):
     gotten, below, outs, (own, parts) = dict(zip(FOUR, refs)), refs[4], refs[5:13], refs[13:]
     rows, cols = outs[0].shape
-    half, col, core = where[0], where[1], where[2]
+    half, col, core = here()
     mine = 2 * half + col
     for turn in range(4):
         own[jnp.bitwise_xor(mine, turn)] = gotten[turn][:rows]
@@ -199,8 +206,8 @@
     return pltpu.roll(pltpu.roll(value, rows, 0), cols, 1)
 
 
-def ready_kernel(where, slot_range, offs, taken, probe_from, measured, tabs_from, order_from, probe, target, tabs, kept, order, sems):
-    half, col, core = where[0], where[1], where[2]
+def ready_kernel(slot_range, offs, taken, probe_from, measured, tabs_from, order_from, probe, target, tabs, kept, order, sems):
+    half, col, core = here()
     probe_copy, kept_copy, order_copy, tabs_copy = fetch(
         [(probe_from, probe), (measured.at[0, half], kept), (order_from, order), (tabs_from, tabs)], sems
     )
@@ -221,10 +228,10 @@
     tabs_copy.wait()
 
 
-def position_kernel(where, slot_range, offs, *refs):
+def position_kernel(slot_range, offs, *refs):
     gotten, (probe, target, tabs, factors) = dict(zip(EIGHT, refs)), refs[8:12]
     outs, keep, (patch, grad, bands) = refs[12:20], refs[20], refs[21:]
-    half, col, core = where[0], where[1], where[2]
+    half, col, core = here()
     mine = 2 * half + col
     flat = 2 * mine + core
     unused, row_at, col_at = slot_place(offs, mine, slot_range[0, 1 - half], slot_of(half, col, core))
@@ -276,16 +283,17 @@
         outs[0][start : start + 2 * band] = bands[2 * part + 1 - core]
 
 
-def pair_kernel(where, keep, got, *outs):
+def pair_kernel(keep, got, *outs):
     band = keep.shape[1]
+    half, col, unused = here()
     first = got.shape[0] - 4 * band
     for turn, out in zip(FOUR, outs):
-        part = jnp.bitwise_xor(2 * where[0] + where[1], turn)
+        part = jnp.bitwise_xor(2 * half + col, turn)
         out[...] = keep[part] + got[pl.ds(pl.multiple_of(first + band * part, band), band)]
 
 
-def add_parts(where, slot_range, offs, parts, strip, rows, cols):
-    half, col, core = where[0], where[1], where[2]
+def add_parts(slot_range, offs, parts, strip, rows, cols):
+    half, col, core = here()
     mine = 2 * half + col
     row_ids = lax.broadcasted_iota(jnp.int32, (rows, cols), 0)
     col_ids = lax.broadcasted_iota(jnp.int32, (rows, cols), 1) + core * cols
@@ -302,35 +310,38 @@
     return sums
 
 
-def add_below_kernel(where, slot_range, offs, *refs):
+def add_below_kernel(slot_range, offs, *refs):
     parts, quarters, (below, probe_band) = refs[:8], refs[8:12], refs[12:]
     rows, cols = below.shape[1:]
-    sums = add_parts(where, slot_range, offs, parts, 2, rows, cols)
+    sums = add_parts(slot_range, offs, parts, 2, rows, cols)
+    col = here()[1]
     for side in range(2):
-        below[jnp.bitwise_xor(where[1], side)] = sums[side]
+        below[jnp.bitwise_xor(col, side)] = sums[side]
     total = (quarters[0][...] + quarters[1][...]) + (quarters[2][...] + quarters[3][...])
     band = probe_band.shape[0]
     probe_band[:, :cols] = total[:band]
     probe_band[:, cols:] = total[band:]
 
 
-def add_own_kernel(where, slot_range, offs, *refs):
+def add_own_kernel(slot_range, offs, *refs):
     parts, own = refs[:8], refs[8]
     rows, cols = own.shape[1:]
     for strip in range(2):
-        own[2 * strip], own[2 * strip + 1] = add_parts(where, slot_range, offs, parts, strip, rows, cols)
-
-
-def top_kernel(where, own, above, *outs):
-    mine = 2 * where[0] + where[1]
+        own[2 * strip], own[2 * strip + 1] = add_parts(slot_range, offs, parts, strip, rows, cols)
+
+
+def top_kernel(own, above, *outs):
+    half, col, unused = here()
+    mine = 2 * half + col
     for turn, out in zip(FOUR, outs):
-        extra = jnp.where(where[0] == turn // 2, above[turn % 2], 0.0)
+        extra = jnp.where(half == turn // 2, above[turn % 2], 0.0)
         out[...] = own[jnp.bitwise_xor(mine, turn)] + extra
 
 
-def join_kernel(where, *refs):
+def join_kernel(*refs):
     probe, out, probe_out, sems = refs[4:]
-    mine = 2 * where[0] + where[1]
+    half, col, unused = here()
+    mine = 2 * half + col
     pairs = [(ref, out.at[jnp.bitwise_xor(mine, turn)]) for turn, ref in zip(FOUR, refs)]
     for copy in fetch([(probe, probe_out), *pairs], sems):
         copy.wait()
@@ -382,20 +393,20 @@
     band = width // 4
     pairs = lax.axis_size("pair")
     half, col, core = (lax.axis_index(name) for name in PLANE)
-    where = jnp.stack([half, col, core])
 
     offsets, slot_range = (pltpu.with_memory_space_constraint(x, pltpu.HBM) for x in (offsets, slot_range))
     block = object_field.reshape(planes, rows, cols)
     *dealt, given = call(
         deal_kernel,
         [shape(rows + 8, cols)] * 4 + [shape(width, width)],
-        (where, offsets),
-        ((block, HBM), (measured, HBM)),
+        (),
+        ((block, HBM), (measured, HBM), (offsets, HBM)),
         0,
-        copies=5,
+        [pltpu.SMEM(offsets.shape, offsets.dtype)],
+        copies=6,
     )
     own = deal(dealt, PLANE[:2], FOUR)
-    (lowest,) = call(lowest_kernel, [shape(2, rows, cols)], (where,), own, 0)
+    (lowest,) = call(lowest_kernel, [shape(2, rows, cols)], (), own, 0)
     lowest, given = lax.optimization_barrier((lowest, given))
     below = lax.ppermute(lowest, "pair", [(k, k - 1) for k in range(1, pairs)])
     taken = lax.ppermute(given, "half", [(0, 1), (1, 0)])
@@ -405,7 +416,7 @@
     offs = jnp.stack([turned[turn][rows : rows + 4, 0] for turn in range(4)]).astype(jnp.int32)
     others = lax.ppermute(offs, "core", [(0, 1), (1, 0)])
     offs = jnp.concatenate([jnp.where(core == 0, offs, others), jnp.where(core == 0, others, offs)], axis=1)
-    scalars = (where, slot_range, offs)
+    scalars = (slot_range, offs)
     parts = call(
         pick_kernel,
         [shape(rows, cols)] * 8,
@@ -433,7 +444,7 @@
         [(8, rows, cols)] * 2 + [(8, 2 * band, cols)],
     )
     got = deal(grad, PLANE, BACK)
-    quarters = call(pair_kernel, [shape(2 * band, cols)] * 4, (where,), (keep, got[0]), 4 * band * width)
+    quarters = call(pair_kernel, [shape(2 * band, cols)] * 4, (), (keep, got[0]), 4 * band * width)
     lower_sums, probe_band = call(
         add_below_kernel,
         [shape(2, rows, cols), shape(band, width)],
@@ -446,7 +457,7 @@
     if doubling:
         near = lax.ppermute(probe_band, "pair", [(k, k ^ 1) for k in range(pairs)])
     (sums,) = call(add_own_kernel, [shape(planes, rows, cols)], scalars, got, 64 * rows * width)
-    sums = call(top_kernel, [shape(rows, cols)] * 4, (where,), (sums, above), planes * rows * cols)
+    sums = call(top_kernel, [shape(rows, cols)] * 4, (), (sums, above), planes * rows * cols)
     if doubling:
         *sums, near = lax.optimization_barrier((*sums, near))
         probe_band = sum_over(probe_band + near, "pair", pairs)
@@ -457,7 +468,7 @@
     object_grad, probe_grad = call(
         join_kernel,
         [(shape(planes, rows, cols), HBM), (shape(*probe_grad.shape), HBM)],
-        (where,),
+        (),
         [(x, ANY) for x in (*sums, probe_grad)],
         0,
         copies=5,

time: 93.3 us -> 91.4 us (0.980)
  Pallas kernels: 16.3 us -> 13.5 us
  waiting for transfers between devices: 30.8 us -> 32 us
    pallas_call x10, Pallas kernels: 16.3 us -> 13.5 us  [call(): pl.pallas_call(kernel, out_shape=[x for x, unused in outs], in_specs=[SME...]
  transfers between devices with their start and end apart: 29 -> 29, of which waited for: 13 -> 14; matrix products, arithmetic and copies ran while one was open for 0% -> 0% of each run, Pallas kernels for 6% -> 5%
where the time goes in v17:
time: 91.4 us; the launch traced here: 91.1 us
  starting transfers between devices  34.1 us (37%)
  waiting for transfers between devices  32 us (35%)
  Pallas kernels  13.5 us (15%)
  blocking collectives  10.2 us (11%)
    ppermute x23, starting transfers between devices, deal(): lax.ppermute(value, axes, [(k, k ^ turn) for k in range(len(order))])  23.1 us
    ppermute x23, waiting for transfers between devices, deal(): lax.ppermute(value, axes, [(k, k ^ turn) for k in range(len(order))])  21.2 us
    pallas_call x10, Pallas kernels, call(): pl.pallas_call(kernel, out_shape=[x for x, unused in outs], in_specs=[SME...  13.5 us
    all_gather x1, blocking collectives, local(): probe_grad = lax.all_gather(probe_band, PLANE, axis=0, tiled=True)  10.2 us
    ppermute x1, waiting for transfers between devices, local(): below = lax.ppermute(lowest, 'pair', [(k, k - 1) for k in range(1, pairs)])  7.62 us
    ppermute x1, starting transfers between devices, local(): lax.ppermute(lower_sums, 'pair', [(k, k + 1) for k in range(pairs - 1)])  3.73 us
    ppermute x1, starting transfers between devices, sum_over(): lax.ppermute(value, axis, [(k, k ^ step) for k in range(size)])  2.68 us
    ppermute x1, waiting for transfers between devices, local(): lax.ppermute(lower_sums, 'pair', [(k, k + 1) for k in range(pairs - 1)])  2.56 us
  transfers between devices with their start and end apart: 29, of which 14 were waited for; matrix products, arithmetic and copies ran while one was open for 0% of the time, Pallas kernels for 5%

profile of v17, /device:TPU:0, one launch (start us, length us, event | category | flops | bytes accessed | tf_op | source)
XLA Modules:
  0.0 91.1 jit_solution(11491213167067887939)
XLA Ops:
  0.6 1.3 %shard_map.95 = (f32[264,128]{1,0:T(8,128)S(1)}, f32[264,128]{1,0:T(8,128)S(1)}, f32[264,128]{1,0:T(8,128)S(1)}, f32[264,128]{1,0:T(8,128)S(1)}, f32[256,256]{1,0:T(8,128)S(1)}) custom-call(f32[4,256,128]{2,1,0:T(8,128)} %bitcast.7, f32[1,2,256,256]{3,2,1,0:T(8,128)} %measured.3, s32[1,2,2]{2,1,0:T(2,128)} %offsets_from.1), custom_call_target="tpu_custom_call" | custom-call | bytes 1851408 | tf_op jit(solution)/shard_map/pallas_call | solution.py:360
  1.9 3.0 %collective-permute-start = (f32[264,128]{1,0:T(8,128)S(1)}, f32[264,128]{1,0:T(8,128)S(1)}, u32[]{:S(2)}, u32[]{:S(2)}) collective-permute-start(f32[264,128]{1,0:T(8,128)S(1)} %get-tuple-element.49), channel_id=1, source_target_pairs={{0,2},{2,0},{4,6},{6,4},{1,3},{3,1},{5,7},{7,5},{8,10},{10,8},{12,... | collective-permute-start | bytes 405512 | tf_op jit(solution)/shard_map/ppermute | solution.py:377
  4.9 1.5 %collective-permute-start.1 = (f32[264,128]{1,0:T(8,128)S(1)}, f32[264,128]{1,0:T(8,128)S(1)}, u32[]{:S(2)}, u32[]{:S(2)}) collective-permute-start(f32[264,128]{1,0:T(8,128)S(1)} %get-tuple-element.50), channel_id=1, source_target_pairs={{0,4},{2,6},{4,0},{6,2},{1,5},{3,7},{5,1},{7,3},{8,12},{10,14},{12... | collective-permute-start | bytes 405512 | tf_op jit(solution)/shard_map/ppermute | solution.py:377
  6.5 0.1 slice_reduce_fusion.3
  6.6 2.3 %collective-permute-done.refs_1_ = f32[264,128]{1,0:T(8,128)S(1)} collective-permute-done((f32[264,128]{1,0:T(8,128)S(1)}, f32[264,128]{1,0:T(8,128)S(1)}, u32[]{:S(2)}, u32[]{:S(2)}) %collective-permute-start) | collective-permute-done | bytes 135200 | tf_op jit(solution)/shard_map/ppermute | solution.py:377
  9.0 3.8 %collective-permute-done.1.refs_0_ = f32[264,128]{1,0:T(8,128)S(1)} collective-permute-done((f32[264,128]{1,0:T(8,128)S(1)}, f32[264,128]{1,0:T(8,128)S(1)}, u32[]{:S(2)}, u32[]{:S(2)}) %collective-permute-start.1) | collective-permute-done | bytes 135200 | tf_op jit(solution)/shard_map/ppermute | solution.py:377
  13.0 0.1 slice_reduce_fusion
  13.2 1.3 %collective-permute-start.4 = (f32[2,256,128]{2,1,0:T(8,128)S(1)}, f32[2,256,128]{2,1,0:T(8,128)S(1)}, u32[]{:S(2)}, u32[]{:S(2)}) collective-permute-start(f32[2,256,128]{2,1,0:T(8,128)S(1)} %shard_map.96), channel_id=1, source_target_pairs={{8,0},{16,8},{24,16},{9,1},{17,9},{25,17},{10,2},{18,10},{26,18},{... | collective-permute-start | bytes 786440 | tf_op jit(solution)/shard_map/ppermute | solution.py:411
  14.5 1.6 %collective-permute-start.5 = (f32[256,256]{1,0:T(8,128)S(1)}, f32[256,256]{1,0:T(8,128)S(1)}, u32[]{:S(2)}, u32[]{:S(2)}) collective-permute-start(f32[256,256]{1,0:T(8,128)S(1)} %get-tuple-element.54), channel_id=1, source_target_pairs={{0,4},{4,0},{1,5},{5,1},{2,6},{6,2},{3,7},{7,3},{8,12},{12,8},{9,1... | collective-permute-start | bytes 786440 | tf_op jit(solution)/shard_map/ppermute | solution.py:412
  16.2 7.6 %collective-permute-done.4.refs_4_ = f32[2,256,128]{2,1,0:T(8,128)S(1)} collective-permute-done((f32[2,256,128]{2,1,0:T(8,128)S(1)}, f32[2,256,128]{2,1,0:T(8,128)S(1)}, u32[]{:S(2)}, u32[]{:S(2)}) %collective-permute-start.4) | collective-permute-done | bytes 262176 | tf_op jit(solution)/shard_map/ppermute | solution.py:411
  23.8 1.4 %shard_map.97 = (f32[256,128]{1,0:T(8,128)S(1)}, f32[256,128]{1,0:T(8,128)S(1)}, f32[256,128]{1,0:T(8,128)S(1)}, f32[256,128]{1,0:T(8,128)S(1)}, f32[256,128]{1,...) custom-call(s32[1,2]{1,0:T(1,128)} %slot_range.9, ...), custom_call_target="tpu_custom_call" | custom-call | flops 2097152 | bytes 1851392 | tf_op jit(solution)/shard_map/pallas_call | solution.py:360
  25.3 1.6 %collective-permute-start.6 = (f32[256,128]{1,0:T(8,128)S(1)}, f32[256,128]{1,0:T(8,128)S(1)}, u32[]{:S(2)}, u32[]{:S(2)}) collective-permute-start(f32[256,128]{1,0:T(8,128)S(1)} %get-tuple-element.56), channel_id=1, source_target_pairs={{0,4},{1,5},{2,6},{3,7},{4,0},{5,1},{6,2},{7,3},{8,12},{9,13},{10,... | collective-permute-start | bytes 393224 | tf_op jit(solution)/shard_map/ppermute | solution.py:377
  26.8 0.5 collective-permute-start.7
  27.4 1.7 %collective-permute-start.9 = (f32[256,128]{1,0:T(8,128)S(1)}, f32[256,128]{1,0:T(8,128)S(1)}, u32[]{:S(2)}, u32[]{:S(2)}) collective-permute-start(f32[256,128]{1,0:T(8,128)S(1)} %get-tuple-element.59), channel_id=1, source_target_pairs={{0,3},{1,2},{2,1},{3,0},{4,7},{5,6},{6,5},{7,4},{8,11},{9,10},{10,... | collective-permute-start | bytes 393224 | tf_op jit(solution)/shard_map/ppermute | solution.py:377
  29.1 1.5 %collective-permute-start.10 = (f32[256,128]{1,0:T(8,128)S(1)}, f32[256,128]{1,0:T(8,128)S(1)}, u32[]{:S(2)}, u32[]{:S(2)}) collective-permute-start(f32[256,128]{1,0:T(8,128)S(1)} %get-tuple-element.60), channel_id=1, source_target_pairs={{0,6},{1,7},{2,4},{3,5},{4,2},{5,3},{6,0},{7,1},{8,14},{9,15},{10,... | collective-permute-start | bytes 393224 | tf_op jit(solution)/shard_map/ppermute | solution.py:377
  30.6 0.7 collective-permute-start.11
  31.2 2.0 %collective-permute-done.7.refs_1_ = f32[256,128]{1,0:T(8,128)S(1)} collective-permute-done((f32[256,128]{1,0:T(8,128)S(1)}, f32[256,128]{1,0:T(8,128)S(1)}, u32[]{:S(2)}, u32[]{:S(2)}) %collective-permute-start.7) | collective-permute-done | bytes 131104 | tf_op jit(solution)/shard_map/ppermute | solution.py:377
  33.2 2.7 %shard_map.98 = (f32[2,256,256]{2,1,0:T(8,128)S(1)}, f32[256,256]{1,0:T(8,128)S(1)}, bf16[6,512,256]{2,1,0:T(8,128)(2,1)S(1)}) custom-call(s32[1,2]{1,0:T(1,128)} %slot_range.9, s32[4,8]{1,0:T(4,128)S(1)} %pad_add_fusion.offs, f32[256,256]{1,0:T(8,128)S(1)} %collective-permute-done.5.taken, f32[2,256,256]{2,1,0:T(8,128)} %probe_from.1, ...), custom_call_target="tpu_custom_call" | custom-call | flops 201326592 | bytes 5505024 | tf_op jit(solution)/shard_map/pallas_call | solution.py:360
  36.0 1.9 %collective-permute-done.10.refs_4_ = f32[256,128]{1,0:T(8,128)S(1)} collective-permute-done((f32[256,128]{1,0:T(8,128)S(1)}, f32[256,128]{1,0:T(8,128)S(1)}, u32[]{:S(2)}, u32[]{:S(2)}) %collective-permute-start.10) | collective-permute-done | bytes 131104 | tf_op jit(solution)/shard_map/ppermute | solution.py:377
  37.8 1.9 %collective-permute-done.11.refs_5_ = f32[256,128]{1,0:T(8,128)S(1)} collective-permute-done((f32[256,128]{1,0:T(8,128)S(1)}, f32[256,128]{1,0:T(8,128)S(1)}, u32[]{:S(2)}, u32[]{:S(2)}) %collective-permute-start.11) | collective-permute-done | bytes 131104 | tf_op jit(solution)/shard_map/ppermute | solution.py:377
  39.7 4.3 %shard_map.99 = (f32[768,128]{1,0:T(8,128)S(1)}, f32[256,128]{1,0:T(8,128)S(1)}, f32[256,128]{1,0:T(8,128)S(1)}, f32[256,128]{1,0:T(8,128)S(1)}, f32[256,128]{1,...) custom-call(s32[1,2]{1,0:T(1,128)} %slot_range.9, ...), custom_call_target="tpu_custom_call" | custom-call | flops 1610612736 | bytes 5120000 | tf_op jit(solution)/shard_map/pallas_call | solution.py:360
  44.0 0.4 collective-permute-start.13
  44.4 1.5 %collective-permute-start.14 = (f32[256,128]{1,0:T(8,128)S(1)}, f32[256,128]{1,0:T(8,128)S(1)}, u32[]{:S(2)}, u32[]{:S(2)}) collective-permute-start(f32[256,128]{1,0:T(8,128)S(1)} %get-tuple-element.69), channel_id=1, source_target_pairs={{0,4},{1,5},{2,6},{3,7},{4,0},{5,1},{6,2},{7,3},{8,12},{9,13},{10,... | collective-permute-start | bytes 393224 | tf_op jit(solution)/shard_map/ppermute | solution.py:377
  45.8 0.6 collective-permute-start.15
  46.4 0.2 collective-permute-start.16
  46.6 1.5 %collective-permute-start.17 = (f32[256,128]{1,0:T(8,128)S(1)}, f32[256,128]{1,0:T(8,128)S(1)}, u32[]{:S(2)}, u32[]{:S(2)}) collective-permute-start(f32[256,128]{1,0:T(8,128)S(1)} %get-tuple-element.72), channel_id=1, source_target_pairs={{0,3},{1,2},{2,1},{3,0},{4,7},{5,6},{6,5},{7,4},{8,11},{9,10},{10,... | collective-permute-start | bytes 393224 | tf_op jit(solution)/shard_map/ppermute | solution.py:377
  48.1 2.4 %collective-permute-done.14.refs_1_ = f32[256,128]{1,0:T(8,128)S(1)} collective-permute-done((f32[256,128]{1,0:T(8,128)S(1)}, f32[256,128]{1,0:T(8,128)S(1)}, u32[]{:S(2)}, u32[]{:S(2)}) %collective-permute-start.14) | collective-permute-done | bytes 131104 | tf_op jit(solution)/shard_map/ppermute | solution.py:377
  50.5 1.5 %collective-permute-start.18 = (f32[256,128]{1,0:T(8,128)S(1)}, f32[256,128]{1,0:T(8,128)S(1)}, u32[]{:S(2)}, u32[]{:S(2)}) collective-permute-start(f32[256,128]{1,0:T(8,128)S(1)} %get-tuple-element.73), channel_id=1, source_target_pairs={{0,6},{1,7},{2,4},{3,5},{4,2},{5,3},{6,0},{7,1},{8,14},{9,15},{10,... | collective-permute-start | bytes 393224 | tf_op jit(solution)/shard_map/ppermute | solution.py:377
  52.0 0.2 collective-permute-done.15.refs_2_
  52.2 0.7 collective-permute-start.20
  52.9 1.2 %collective-permute-start.21 = (f32[128,128]{1,0:T(8,128)S(1)}, f32[128,128]{1,0:T(8,128)S(1)}, u32[]{:S(2)}, u32[]{:S(2)}) collective-permute-start(f32[128,128]{1,0:T(8,128)S(1)} %get-tuple-element.78), channel_id=1, source_target_pairs={{0,2},{2,0},{4,6},{6,4},{1,3},{3,1},{5,7},{7,5},{8,10},{10,8},{12,... | collective-permute-start | bytes 196616 | tf_op jit(solution)/shard_map/ppermute | solution.py:377
  54.1 1.6 %collective-permute-start.22 = (f32[128,128]{1,0:T(8,128)S(1)}, f32[128,128]{1,0:T(8,128)S(1)}, u32[]{:S(2)}, u32[]{:S(2)}) collective-permute-start(f32[128,128]{1,0:T(8,128)S(1)} %get-tuple-element.79), channel_id=1, source_target_pairs={{0,6},{2,4},{4,2},{6,0},{1,7},{3,5},{5,3},{7,1},{8,14},{10,12},{12... | collective-permute-start | bytes 196616 | tf_op jit(solution)/shard_map/ppermute | solution.py:377
  55.7 2.1 %collective-permute-done.18.refs_5_ = f32[256,128]{1,0:T(8,128)S(1)} collective-permute-done((f32[256,128]{1,0:T(8,128)S(1)}, f32[256,128]{1,0:T(8,128)S(1)}, u32[]{:S(2)}, u32[]{:S(2)}) %collective-permute-start.18) | collective-permute-done | bytes 131104 | tf_op jit(solution)/shard_map/ppermute | solution.py:377
  57.8 0.9 collective-permute-done.19.refs_6_
  58.7 2.9 %collective-permute-done.20.refs_8_ = f32[128,128]{1,0:T(8,128)S(1)} collective-permute-done((f32[128,128]{1,0:T(8,128)S(1)}, f32[128,128]{1,0:T(8,128)S(1)}, u32[]{:S(2)}, u32[]{:S(2)}) %collective-permute-start.20) | collective-permute-done | bytes 65568 | tf_op jit(solution)/shard_map/ppermute | solution.py:377
  61.7 0.8 collective-permute-done.22.refs_10_
  62.4 1.1 %shard_map.102 = (f32[2,256,128]{2,1,0:T(8,128)S(1)}, f32[64,256]{1,0:T(8,128)S(1)}) custom-call(s32[1,2]{1,0:T(1,128)} %slot_range.9, s32[4,8]{1,0:T(4,128)S(1)} %pad_add_fusion.offs, f32[768,128]{1,0:T(8,128)S(1)} %collective-permute-done.13.refs_0_.got, f32[256,128]{1,0:T(8,128)S(1)} %collective-permute-done.14.refs_1_, ...), custom_call_target="tpu_custom_call" | custom-call | flops 2097152 | bytes 1900544 | tf_op jit(solution)/shard_map/pallas_call | solution.py:360
  63.5 3.7 %collective-permute-start.23 = (f32[2,256,128]{2,1,0:T(8,128)S(1)}, f32[2,256,128]{2,1,0:T(8,128)S(1)}, u32[]{:S(2)}, u32[]{:S(2)}) collective-permute-start(f32[2,256,128]{2,1,0:T(8,128)S(1)} %get-tuple-element.81), channel_id=1, source_target_pairs={{0,8},{8,16},{16,24},{1,9},{9,17},{17,25},{2,10},{10,18},{18,26},{... | collective-permute-start | bytes 786440 | tf_op jit(solution)/shard_map/ppermute | solution.py:455
  67.3 1.6 %collective-permute-start.24 = (f32[64,256]{1,0:T(8,128)S(1)}, f32[64,256]{1,0:T(8,128)S(1)}, u32[]{:S(2)}, u32[]{:S(2)}) collective-permute-start(f32[64,256]{1,0:T(8,128)S(1)} %get-tuple-element.86), channel_id=1, source_target_pairs={{0,8},{8,0},{16,24},{24,16},{1,9},{9,1},{17,25},{25,17},{2,10},{10... | collective-permute-start | bytes 196616 | tf_op jit(solution)/shard_map/ppermute | solution.py:458
  68.9 1.5 %shard_map.100.own = f32[4,256,128]{2,1,0:T(8,128)S(1)} custom-call(s32[1,2]{1,0:T(1,128)} %slot_range.9, s32[4,8]{1,0:T(4,128)S(1)} %pad_add_fusion.offs, f32[768,128]{1,0:T(8,128)S(1)} %collective-permute-done.13.refs_0_.got, f32[256,128]{1,0:T(8,128)S(1)} %collective-permute-done.14.refs_1_, f32[256,128]{1,0:T(8,128)S(1)} %collective-permute-done.15.refs_2_, ...), custom_call_target="tpu_custom_call" | custom-call | flops 4194304 | bytes 1835008 | tf_op jit(solution)/shard_map/pallas_call | solution.py:360
  70.5 2.6 %collective-permute-done.23.above = f32[2,256,128]{2,1,0:T(8,128)S(1)} collective-permute-done((f32[2,256,128]{2,1,0:T(8,128)S(1)}, f32[2,256,128]{2,1,0:T(8,128)S(1)}, u32[]{:S(2)}, u32[]{:S(2)}) %collective-permute-start.23) | collective-permute-done | bytes 262176 | tf_op jit(solution)/shard_map/ppermute | solution.py:455
  73.1 0.6 collective-permute-done.24
  73.7 2.7 %collective-permute-start.28 = (f32[64,256]{1,0:T(8,128)S(1)}, f32[64,256]{1,0:T(8,128)S(1)}, u32[]{:S(2)}, u32[]{:S(2)}) collective-permute-start(f32[64,256]{1,0:T(8,128)S(1)} %add.6), channel_id=1, source_target_pairs={{0,16},{8,24},{16,0},{24,8},{1,17},{9,25},{17,1},{25,9},{2,18},{10... | collective-permute-start | bytes 196616 | tf_op jit(solution)/shard_map/ppermute | solution.py:385
  76.4 1.3 %collective-permute-start.25 = (f32[256,128]{1,0:T(8,128)S(1)}, f32[256,128]{1,0:T(8,128)S(1)}, u32[]{:S(2)}, u32[]{:S(2)}) collective-permute-start(f32[256,128]{1,0:T(8,128)S(1)} %get-tuple-element.87), channel_id=1, source_target_pairs={{0,4},{2,6},{4,0},{6,2},{1,5},{3,7},{5,1},{7,3},{8,12},{10,14},{12... | collective-permute-start | bytes 393224 | tf_op jit(solution)/shard_map/ppermute | solution.py:377
  77.7 0.7 collective-permute-start.26
  78.4 1.5 %collective-permute-start.27 = (f32[256,128]{1,0:T(8,128)S(1)}, f32[256,128]{1,0:T(8,128)S(1)}, u32[]{:S(2)}, u32[]{:S(2)}) collective-permute-start(f32[256,128]{1,0:T(8,128)S(1)} %get-tuple-element.89), channel_id=1, source_target_pairs={{0,6},{2,4},{4,2},{6,0},{1,7},{3,5},{5,3},{7,1},{8,14},{10,12},{12... | collective-permute-start | bytes 393224 | tf_op jit(solution)/shard_map/ppermute | solution.py:377
  79.9 10.2 %all_gather.3.refs_4_ = f32[512,256]{1,0:T(8,128)S(1)} all-gather(f32[64,256]{1,0:T(8,128)S(1)} %add.7), channel_id=1, replica_groups=mesh['pair'=4,'half'=2,'col'=2,'core'=2] {'half','col','core'}, dimensions={0}, use_global_device_ids=true | all-gather | bytes 589824 | tf_op jit(solution)/shard_map/all_gather | solution.py:467
  90.1 1.0 %shard_map.104 = (f32[4,256,128]{2,1,0:T(8,128)}, f32[512,256]{1,0:T(8,128)}) custom-call(f32[256,128]{1,0:T(8,128)S(1)} %collective-permute-done.25.refs_0_, f32[256,128]{1,0:T(8,128)S(1)} %collective-permute-done.26.refs_1_, f32[256,128]{1,0:T(8,128)S(1)} %collective-permute-done.27.refs_2_, f32[256,128]{1,0:T(8,128)S(1)} %get-tuple-element.90.refs_3_, ...), custom_call_target="tpu_custom_call" | custom-call | bytes 2097152 | tf_op jit(solution)/shard_map/pallas_call | solution.py:360
  (32 shorter events, 0.6 us)
Async XLA Ops:
  1.9 7.0 %collective-permute-start = (f32[264,128]{1,0:T(8,128)S(1)}, f32[264,128]{1,0:T(8,128)S(1)}, u32[]{:S(2)}, u32[]{:S(2)}) collective-permute-start(f32[264,128]{1,0:T(8,128)S(1)} %get-tuple-element.49), channel_id=1, source_target_pairs={{0,2},{2,0},{4,6},{6,4},{1,3},{3,1},{5,7},{7,5},{8,10},{10,8},{12,... | collective-permute-start | bytes 405512 | tf_op jit(solution)/shard_map/ppermute | solution.py:377
  4.9 7.9 %collective-permute-start.1 = (f32[264,128]{1,0:T(8,128)S(1)}, f32[264,128]{1,0:T(8,128)S(1)}, u32[]{:S(2)}, u32[]{:S(2)}) collective-permute-start(f32[264,128]{1,0:T(8,128)S(1)} %get-tuple-element.50), channel_id=1, source_target_pairs={{0,4},{2,6},{4,0},{6,2},{1,5},{3,7},{5,1},{7,3},{8,12},{10,14},{12... | collective-permute-start | bytes 405512 | tf_op jit(solution)/shard_map/ppermute | solution.py:377
  6.4 6.5 %collective-permute-start.2 = (f32[264,128]{1,0:T(8,128)S(1)}, f32[264,128]{1,0:T(8,128)S(1)}, u32[]{:S(2)}, u32[]{:S(2)}) collective-permute-start(f32[264,128]{1,0:T(8,128)S(1)} %get-tuple-element.51), channel_id=1, source_target_pairs={{0,6},{2,4},{4,2},{6,0},{1,7},{3,5},{5,3},{7,1},{8,14},{10,12},{12... | collective-permute-start | bytes 405512 | tf_op jit(solution)/shard_map/ppermute | solution.py:377
  13.1 3.0 %collective-permute-start.3 = (s32[4,4]{1,0:T(4,128)S(1)}, s32[4,4]{1,0:T(4,128)S(1)}, u32[]{:S(2)}, u32[]{:S(2)}) collective-permute-start(s32[4,4]{1,0:T(4,128)S(1)} %maximum_convert_fusion), channel_id=1, source_target_pairs={{0,1},{1,0},{2,3},{3,2},{4,5},{5,4},{6,7},{7,6},{8,9},{9,8},{10,11... | collective-permute-start | bytes 200 | tf_op jit(solution)/shard_map/ppermute | solution.py:417
  13.2 10.6 %collective-permute-start.4 = (f32[2,256,128]{2,1,0:T(8,128)S(1)}, f32[2,256,128]{2,1,0:T(8,128)S(1)}, u32[]{:S(2)}, u32[]{:S(2)}) collective-permute-start(f32[2,256,128]{2,1,0:T(8,128)S(1)} %shard_map.96), channel_id=1, source_target_pairs={{8,0},{16,8},{24,16},{9,1},{17,9},{25,17},{10,2},{18,10},{26,18},{... | collective-permute-start | bytes 786440 | tf_op jit(solution)/shard_map/ppermute | solution.py:411
  14.5 9.3 %collective-permute-start.5 = (f32[256,256]{1,0:T(8,128)S(1)}, f32[256,256]{1,0:T(8,128)S(1)}, u32[]{:S(2)}, u32[]{:S(2)}) collective-permute-start(f32[256,256]{1,0:T(8,128)S(1)} %get-tuple-element.54), channel_id=1, source_target_pairs={{0,4},{4,0},{1,5},{5,1},{2,6},{6,2},{3,7},{7,3},{8,12},{12,8},{9,1... | collective-permute-start | bytes 786440 | tf_op jit(solution)/shard_map/ppermute | solution.py:412
  25.3 5.3 %collective-permute-start.6 = (f32[256,128]{1,0:T(8,128)S(1)}, f32[256,128]{1,0:T(8,128)S(1)}, u32[]{:S(2)}, u32[]{:S(2)}) collective-permute-start(f32[256,128]{1,0:T(8,128)S(1)} %get-tuple-element.56), channel_id=1, source_target_pairs={{0,4},{1,5},{2,6},{3,7},{4,0},{5,1},{6,2},{7,3},{8,12},{9,13},{10,... | collective-permute-start | bytes 393224 | tf_op jit(solution)/shard_map/ppermute | solution.py:377
  26.8 6.4 %collective-permute-start.7 = (f32[256,128]{1,0:T(8,128)S(1)}, f32[256,128]{1,0:T(8,128)S(1)}, u32[]{:S(2)}, u32[]{:S(2)}) collective-permute-start(f32[256,128]{1,0:T(8,128)S(1)} %get-tuple-element.57), channel_id=1, source_target_pairs={{0,2},{1,3},{2,0},{3,1},{4,6},{5,7},{6,4},{7,5},{8,10},{9,11},{10,... | collective-permute-start | bytes 393224 | tf_op jit(solution)/shard_map/ppermute | solution.py:377
  27.4 8.6 %collective-permute-start.8 = (f32[256,128]{1,0:T(8,128)S(1)}, f32[256,128]{1,0:T(8,128)S(1)}, u32[]{:S(2)}, u32[]{:S(2)}) collective-permute-start(f32[256,128]{1,0:T(8,128)S(1)} %get-tuple-element.58), channel_id=1, source_target_pairs={{0,5},{1,4},{2,7},{3,6},{4,1},{5,0},{6,3},{7,2},{8,13},{9,12},{10,... | collective-permute-start | bytes 393224 | tf_op jit(solution)/shard_map/ppermute | solution.py:377
  27.4 8.6 %collective-permute-start.9 = (f32[256,128]{1,0:T(8,128)S(1)}, f32[256,128]{1,0:T(8,128)S(1)}, u32[]{:S(2)}, u32[]{:S(2)}) collective-permute-start(f32[256,128]{1,0:T(8,128)S(1)} %get-tuple-element.59), channel_id=1, source_target_pairs={{0,3},{1,2},{2,1},{3,0},{4,7},{5,6},{6,5},{7,4},{8,11},{9,10},{10,... | collective-permute-start | bytes 393224 | tf_op jit(solution)/shard_map/ppermute | solution.py:377
  29.1 8.7 %collective-permute-start.10 = (f32[256,128]{1,0:T(8,128)S(1)}, f32[256,128]{1,0:T(8,128)S(1)}, u32[]{:S(2)}, u32[]{:S(2)}) collective-permute-start(f32[256,128]{1,0:T(8,128)S(1)} %get-tuple-element.60), channel_id=1, source_target_pairs={{0,6},{1,7},{2,4},{3,5},{4,2},{5,3},{6,0},{7,1},{8,14},{9,15},{10,... | collective-permute-start | bytes 393224 | tf_op jit(solution)/shard_map/ppermute | solution.py:377
  30.6 9.1 %collective-permute-start.11 = (f32[256,128]{1,0:T(8,128)S(1)}, f32[256,128]{1,0:T(8,128)S(1)}, u32[]{:S(2)}, u32[]{:S(2)}) collective-permute-start(f32[256,128]{1,0:T(8,128)S(1)} %get-tuple-element.61), channel_id=1, source_target_pairs={{0,7},{1,6},{2,5},{3,4},{4,3},{5,2},{6,1},{7,0},{8,15},{9,14},{10,... | collective-permute-start | bytes 393224 | tf_op jit(solution)/shard_map/ppermute | solution.py:377
  33.2 6.5 %copy-start = (f32[2,136,128]{2,1,0:T(8,128)S(1)}, f32[2,136,128]{2,1,0:T(8,128)}, u32[]{:S(2)}) copy-start(f32[2,136,128]{2,1,0:T(8,128)} %constant.13.clone.refs_11_) | copy-start | bytes 417796
  33.2 6.5 %collective-permute-start.12 = (f32[256,128]{1,0:T(8,128)S(1)}, f32[256,128]{1,0:T(8,128)S(1)}, u32[]{:S(2)}, u32[]{:S(2)}) collective-permute-start(f32[256,128]{1,0:T(8,128)S(1)} %get-tuple-element.62), channel_id=1, source_target_pairs={{0,1},{1,0},{2,3},{3,2},{4,5},{5,4},{6,7},{7,6},{8,9},{9,8},{10,11... | collective-permute-start | bytes 393224 | tf_op jit(solution)/shard_map/ppermute | solution.py:377
  44.0 8.0 %collective-permute-start.13 = (f32[768,128]{1,0:T(8,128)S(1)}, f32[768,128]{1,0:T(8,128)S(1)}, u32[]{:S(2)}, u32[]{:S(2)}) collective-permute-start(f32[768,128]{1,0:T(8,128)S(1)} %get-tuple-element.68), channel_id=1, source_target_pairs={{0,1},{1,0},{2,3},{3,2},{4,5},{5,4},{6,7},{7,6},{8,9},{9,8},{10,11... | collective-permute-start | bytes 1179656 | tf_op jit(solution)/shard_map/ppermute | solution.py:377
  44.4 6.1 %collective-permute-start.14 = (f32[256,128]{1,0:T(8,128)S(1)}, f32[256,128]{1,0:T(8,128)S(1)}, u32[]{:S(2)}, u32[]{:S(2)}) collective-permute-start(f32[256,128]{1,0:T(8,128)S(1)} %get-tuple-element.69), channel_id=1, source_target_pairs={{0,4},{1,5},{2,6},{3,7},{4,0},{5,1},{6,2},{7,3},{8,12},{9,13},{10,... | collective-permute-start | bytes 393224 | tf_op jit(solution)/shard_map/ppermute | solution.py:377
  45.8 6.4 %collective-permute-start.15 = (f32[256,128]{1,0:T(8,128)S(1)}, f32[256,128]{1,0:T(8,128)S(1)}, u32[]{:S(2)}, u32[]{:S(2)}) collective-permute-start(f32[256,128]{1,0:T(8,128)S(1)} %get-tuple-element.70), channel_id=1, source_target_pairs={{0,2},{1,3},{2,0},{3,1},{4,6},{5,7},{6,4},{7,5},{8,10},{9,11},{10,... | collective-permute-start | bytes 393224 | tf_op jit(solution)/shard_map/ppermute | solution.py:377
  46.4 6.5 %collective-permute-start.16 = (f32[256,128]{1,0:T(8,128)S(1)}, f32[256,128]{1,0:T(8,128)S(1)}, u32[]{:S(2)}, u32[]{:S(2)}) collective-permute-start(f32[256,128]{1,0:T(8,128)S(1)} %get-tuple-element.71), channel_id=1, source_target_pairs={{0,5},{1,4},{2,7},{3,6},{4,1},{5,0},{6,3},{7,2},{8,13},{9,12},{10,... | collective-permute-start | bytes 393224 | tf_op jit(solution)/shard_map/ppermute | solution.py:377
  46.6 7.5 %collective-permute-start.17 = (f32[256,128]{1,0:T(8,128)S(1)}, f32[256,128]{1,0:T(8,128)S(1)}, u32[]{:S(2)}, u32[]{:S(2)}) collective-permute-start(f32[256,128]{1,0:T(8,128)S(1)} %get-tuple-element.72), channel_id=1, source_target_pairs={{0,3},{1,2},{2,1},{3,0},{4,7},{5,6},{6,5},{7,4},{8,11},{9,10},{10,... | collective-permute-start | bytes 393224 | tf_op jit(solution)/shard_map/ppermute | solution.py:377
  50.5 7.3 %collective-permute-start.18 = (f32[256,128]{1,0:T(8,128)S(1)}, f32[256,128]{1,0:T(8,128)S(1)}, u32[]{:S(2)}, u32[]{:S(2)}) collective-permute-start(f32[256,128]{1,0:T(8,128)S(1)} %get-tuple-element.73), channel_id=1, source_target_pairs={{0,6},{1,7},{2,4},{3,5},{4,2},{5,3},{6,0},{7,1},{8,14},{9,15},{10,... | collective-permute-start | bytes 393224 | tf_op jit(solution)/shard_map/ppermute | solution.py:377
  51.9 6.8 %collective-permute-start.19 = (f32[256,128]{1,0:T(8,128)S(1)}, f32[256,128]{1,0:T(8,128)S(1)}, u32[]{:S(2)}, u32[]{:S(2)}) collective-permute-start(f32[256,128]{1,0:T(8,128)S(1)} %get-tuple-element.74), channel_id=1, source_target_pairs={{0,7},{1,6},{2,5},{3,4},{4,3},{5,2},{6,1},{7,0},{8,15},{9,14},{10,... | collective-permute-start | bytes 393224 | tf_op jit(solution)/shard_map/ppermute | solution.py:377
  52.2 9.4 %collective-permute-start.20 = (f32[128,128]{1,0:T(8,128)S(1)}, f32[128,128]{1,0:T(8,128)S(1)}, u32[]{:S(2)}, u32[]{:S(2)}) collective-permute-start(f32[128,128]{1,0:T(8,128)S(1)} %get-tuple-element.77), channel_id=1, source_target_pairs={{0,4},{2,6},{4,0},{6,2},{1,5},{3,7},{5,1},{7,3},{8,12},{10,14},{12... | collective-permute-start | bytes 196616 | tf_op jit(solution)/shard_map/ppermute | solution.py:377
  52.9 8.7 %collective-permute-start.21 = (f32[128,128]{1,0:T(8,128)S(1)}, f32[128,128]{1,0:T(8,128)S(1)}, u32[]{:S(2)}, u32[]{:S(2)}) collective-permute-start(f32[128,128]{1,0:T(8,128)S(1)} %get-tuple-element.78), channel_id=1, source_target_pairs={{0,2},{2,0},{4,6},{6,4},{1,3},{3,1},{5,7},{7,5},{8,10},{10,8},{12,... | collective-permute-start | bytes 196616 | tf_op jit(solution)/shard_map/ppermute | solution.py:377
  54.1 8.3 %collective-permute-start.22 = (f32[128,128]{1,0:T(8,128)S(1)}, f32[128,128]{1,0:T(8,128)S(1)}, u32[]{:S(2)}, u32[]{:S(2)}) collective-permute-start(f32[128,128]{1,0:T(8,128)S(1)} %get-tuple-element.79), channel_id=1, source_target_pairs={{0,6},{2,4},{4,2},{6,0},{1,7},{3,5},{5,3},{7,1},{8,14},{10,12},{12... | collective-permute-start | bytes 196616 | tf_op jit(solution)/shard_map/ppermute | solution.py:377
  63.5 9.5 %collective-permute-start.23 = (f32[2,256,128]{2,1,0:T(8,128)S(1)}, f32[2,256,128]{2,1,0:T(8,128)S(1)}, u32[]{:S(2)}, u32[]{:S(2)}) collective-permute-start(f32[2,256,128]{2,1,0:T(8,128)S(1)} %get-tuple-element.81), channel_id=1, source_target_pairs={{0,8},{8,16},{16,24},{1,9},{9,17},{17,25},{2,10},{10,18},{18,26},{... | collective-permute-start | bytes 786440 | tf_op jit(solution)/shard_map/ppermute | solution.py:455
  67.3 6.4 %collective-permute-start.24 = (f32[64,256]{1,0:T(8,128)S(1)}, f32[64,256]{1,0:T(8,128)S(1)}, u32[]{:S(2)}, u32[]{:S(2)}) collective-permute-start(f32[64,256]{1,0:T(8,128)S(1)} %get-tuple-element.86), channel_id=1, source_target_pairs={{0,8},{8,0},{16,24},{24,16},{1,9},{9,1},{17,25},{25,17},{2,10},{10... | collective-permute-start | bytes 196616 | tf_op jit(solution)/shard_map/ppermute | solution.py:458
  73.7 6.2 %collective-permute-start.28 = (f32[64,256]{1,0:T(8,128)S(1)}, f32[64,256]{1,0:T(8,128)S(1)}, u32[]{:S(2)}, u32[]{:S(2)}) collective-permute-start(f32[64,256]{1,0:T(8,128)S(1)} %add.6), channel_id=1, source_target_pairs={{0,16},{8,24},{16,0},{24,8},{1,17},{9,25},{17,1},{25,9},{2,18},{10... | collective-permute-start | bytes 196616 | tf_op jit(solution)/shard_map/ppermute | solution.py:385
  76.4 13.7 %collective-permute-start.25 = (f32[256,128]{1,0:T(8,128)S(1)}, f32[256,128]{1,0:T(8,128)S(1)}, u32[]{:S(2)}, u32[]{:S(2)}) collective-permute-start(f32[256,128]{1,0:T(8,128)S(1)} %get-tuple-element.87), channel_id=1, source_target_pairs={{0,4},{2,6},{4,0},{6,2},{1,5},{3,7},{5,1},{7,3},{8,12},{10,14},{12... | collective-permute-start | bytes 393224 | tf_op jit(solution)/shard_map/ppermute | solution.py:377
  77.7 12.4 %collective-permute-start.26 = (f32[256,128]{1,0:T(8,128)S(1)}, f32[256,128]{1,0:T(8,128)S(1)}, u32[]{:S(2)}, u32[]{:S(2)}) collective-permute-start(f32[256,128]{1,0:T(8,128)S(1)} %get-tuple-element.88), channel_id=1, source_target_pairs={{0,2},{2,0},{4,6},{6,4},{1,3},{3,1},{5,7},{7,5},{8,10},{10,8},{12,... | collective-permute-start | bytes 393224 | tf_op jit(solution)/shard_map/ppermute | solution.py:377
  78.4 11.7 %collective-permute-start.27 = (f32[256,128]{1,0:T(8,128)S(1)}, f32[256,128]{1,0:T(8,128)S(1)}, u32[]{:S(2)}, u32[]{:S(2)}) collective-permute-start(f32[256,128]{1,0:T(8,128)S(1)} %get-tuple-element.89), channel_id=1, source_target_pairs={{0,6},{2,4},{4,2},{6,0},{1,7},{3,5},{5,3},{7,1},{8,14},{10,12},{12... | collective-permute-start | bytes 393224 | tf_op jit(solution)/shard_map/ppermute | solution.py:377

commit v18 on v17

--- a/solution.py
+++ b/solution.py
@@ -135,8 +135,8 @@
     return [slot_of(half, col, core) for half in range(2) for col in range(2) for core in range(2)]
 
 
-def slot_place(offs, mine, split_at, slot):
-    lower = jnp.where(slot >= split_at, 1, 0)
+def slot_place(offs, mine, slot):
+    lower = jnp.where(slot >= offs[4, 0], 1, 0)
     holder, at = jnp.bitwise_xor(2 * lower + slot // 4, mine), 2 * (slot % 4)
     return lower, offs[holder, at], offs[holder, at + 1]
 
@@ -176,18 +176,17 @@
         out[turn] = jnp.where(half == 0, gotten[turn][:rows], gotten[2 + turn][:rows])
 
 
-def pick_kernel(slot_range, offs, *refs):
+def pick_kernel(offs, *refs):
     gotten, below, outs, (own, parts) = dict(zip(FOUR, refs)), refs[4], refs[5:13], refs[13:]
     rows, cols = outs[0].shape
     half, col, core = here()
     mine = 2 * half + col
     for turn in range(4):
         own[jnp.bitwise_xor(mine, turn)] = gotten[turn][:rows]
-    split_at = slot_range[0, 1 - half]
     row_ids = lax.broadcasted_iota(jnp.int32, (rows, cols), 0)
     col_ids = lax.broadcasted_iota(jnp.int32, (rows, cols), 1) + core * cols
     for place, slot in enumerate(receivers()):
-        lower, row_at, col_at = slot_place(offs, mine, split_at, slot)
+        lower, row_at, col_at = slot_place(offs, mine, slot)
         upper_rows = row_ids >= row_at
         left_cols = col_ids >= col_at
 
@@ -206,13 +205,13 @@
     return pltpu.roll(pltpu.roll(value, rows, 0), cols, 1)
 
 
-def ready_kernel(slot_range, offs, taken, probe_from, measured, tabs_from, order_from, probe, target, tabs, kept, order, sems):
+def ready_kernel(offs, taken, probe_from, measured, tabs_from, order_from, probe, target, tabs, kept, order, sems):
     half, col, core = here()
     probe_copy, kept_copy, order_copy, tabs_copy = fetch(
         [(probe_from, probe), (measured.at[0, half], kept), (order_from, order), (tabs_from, tabs)], sems
     )
     slot = slot_of(half, col, core)
-    lower, row_at, col_at = slot_place(offs, 2 * half + col, slot_range[0, 1 - half], slot)
+    lower, row_at, col_at = slot_place(offs, 2 * half + col, slot)
     probe_copy.wait()
     for part in range(2):
         probe[part] = roll(probe[part], row_at, col_at)
@@ -228,13 +227,13 @@
     tabs_copy.wait()
 
 
-def position_kernel(slot_range, offs, *refs):
+def position_kernel(offs, *refs):
     gotten, (probe, target, tabs, factors) = dict(zip(EIGHT, refs)), refs[8:12]
     outs, keep, (patch, grad, bands) = refs[12:20], refs[20], refs[21:]
     half, col, core = here()
     mine = 2 * half + col
     flat = 2 * mine + core
-    unused, row_at, col_at = slot_place(offs, mine, slot_range[0, 1 - half], slot_of(half, col, core))
+    unused, row_at, col_at = slot_place(offs, mine, slot_of(half, col, core))
     width = probe.shape[-1]
     lanes, band = width // 2, width // 4
     for turn in range(8):
@@ -292,7 +291,7 @@
         out[...] = keep[part] + got[pl.ds(pl.multiple_of(first + band * part, band), band)]
 
 
-def add_parts(slot_range, offs, parts, strip, rows, cols):
+def add_parts(offs, parts, strip, rows, cols):
     half, col, core = here()
     mine = 2 * half + col
     row_ids = lax.broadcasted_iota(jnp.int32, (rows, cols), 0)
@@ -301,7 +300,7 @@
     for turn, part in zip(BACK, parts):
         flat = jnp.bitwise_xor(2 * mine + core, turn)
         slot = slot_of(flat // 4, (flat // 2) % 2, flat % 2)
-        lower, row_at, col_at = slot_place(offs, mine, slot_range[0, 1 - half], slot)
+        lower, row_at, col_at = slot_place(offs, mine, slot)
         first = jnp.where(strip == lower, row_at, jnp.where(strip == lower + 1, 0, rows))
         last = jnp.where(strip == lower, rows, jnp.where(strip == lower + 1, row_at, 0))
         value = jnp.where((row_ids >= first) & (row_ids < last), part[:rows], 0.0)
@@ -310,10 +309,10 @@
     return sums
 
 
-def add_below_kernel(slot_range, offs, *refs):
+def add_below_kernel(offs, *refs):
     parts, quarters, (below, probe_band) = refs[:8], refs[8:12], refs[12:]
     rows, cols = below.shape[1:]
-    sums = add_parts(slot_range, offs, parts, 2, rows, cols)
+    sums = add_parts(offs, parts, 2, rows, cols)
     col = here()[1]
     for side in range(2):
         below[jnp.bitwise_xor(col, side)] = sums[side]
@@ -323,11 +322,11 @@
     probe_band[:, cols:] = total[band:]
 
 
-def add_own_kernel(slot_range, offs, *refs):
+def add_own_kernel(offs, *refs):
     parts, own = refs[:8], refs[8]
     rows, cols = own.shape[1:]
     for strip in range(2):
-        own[2 * strip], own[2 * strip + 1] = add_parts(slot_range, offs, parts, strip, rows, cols)
+        own[2 * strip], own[2 * strip + 1] = add_parts(offs, parts, strip, rows, cols)
 
 
 def top_kernel(own, above, *outs):
@@ -394,7 +393,6 @@
     pairs = lax.axis_size("pair")
     half, col, core = (lax.axis_index(name) for name in PLANE)
 
-    offsets, slot_range = (pltpu.with_memory_space_constraint(x, pltpu.HBM) for x in (offsets, slot_range))
     block = object_field.reshape(planes, rows, cols)
     *dealt, given = call(
         deal_kernel,
@@ -416,7 +414,9 @@
     offs = jnp.stack([turned[turn][rows : rows + 4, 0] for turn in range(4)]).astype(jnp.int32)
     others = lax.ppermute(offs, "core", [(0, 1), (1, 0)])
     offs = jnp.concatenate([jnp.where(core == 0, offs, others), jnp.where(core == 0, others, offs)], axis=1)
-    scalars = (slot_range, offs)
+    split_at = jnp.where(half == 0, slot_range[0, 1], slot_range[0, 0])
+    offs = jnp.concatenate([offs, jnp.full((1, offs.shape[1]), split_at, jnp.int32)], axis=0)
+    scalars = (offs,)
     parts = call(
         pick_kernel,
         [shape(rows, cols)] * 8,

time: 91.4 us -> 91.1 us (level)
  waiting for transfers between devices: 32 us -> 29.7 us
  local copies, waits for them, and re-layouts: 0.46 us -> 1.79 us
  between operations: 0.76 us -> 2.06 us
    ppermute x23, waiting for transfers between devices: 21.2 us -> 18.8 us  [deal(): lax.ppermute(value, axes, [(k, k ^ turn) for k in range(len(order))])]
    slice x0 -> x1, local copies, waits for them, and re-layouts: none -> 1.31 us  [local(): split_at = jnp.where(half == 0, slot_range[0, 1], slot_range[0, 0])]
  transfers between devices with their start and end apart: 29 -> 29, of which waited for: 14 -> 13; matrix products, arithmetic and copies ran while one was open for 0% -> 2% of each run, Pallas kernels for 5% -> 5%
where the time goes in v18:
time: 91.1 us; the launch traced here: 90.9 us
  starting transfers between devices  34.1 us (37%)
  waiting for transfers between devices  29.7 us (33%)
  Pallas kernels  13 us (14%)
  blocking collectives  10.2 us (11%)
  between operations  2.06 us (2%)
  local copies, waits for them, and re-layouts  1.79 us (2%)
    ppermute x23, starting transfers between devices, deal(): lax.ppermute(value, axes, [(k, k ^ turn) for k in range(len(order))])  23.1 us
    ppermute x23, waiting for transfers between devices, deal(): lax.ppermute(value, axes, [(k, k ^ turn) for k in range(len(order))])  18.8 us
    pallas_call x10, Pallas kernels, call(): pl.pallas_call(kernel, out_shape=[x for x, unused in outs], in_specs=[SME...  13 us
    all_gather x1, blocking collectives, local(): probe_grad = lax.all_gather(probe_band, PLANE, axis=0, tiled=True)  10.2 us
    ppermute x1, waiting for transfers between devices, local(): below = lax.ppermute(lowest, 'pair', [(k, k - 1) for k in range(1, pairs)])  7.61 us
    ppermute x1, starting transfers between devices, local(): lax.ppermute(lower_sums, 'pair', [(k, k + 1) for k in range(pairs - 1)])  3.73 us
    ppermute x1, starting transfers between devices, sum_over(): lax.ppermute(value, axis, [(k, k ^ step) for k in range(size)])  2.68 us
    ppermute x1, waiting for transfers between devices, local(): lax.ppermute(lower_sums, 'pair', [(k, k + 1) for k in range(pairs - 1)])  2.63 us
  transfers between devices with their start and end apart: 29, of which 13 were waited for; matrix products, arithmetic and copies ran while one was open for 2% of the time, Pallas kernels for 5%

profile of v18, /device:TPU:0, one launch (start us, length us, event | category | flops | bytes accessed | tf_op | source)
XLA Modules:
  0.0 90.9 jit_solution(16874661522716605787)
XLA Ops:
  0.6 1.3 %shard_map.95 = (f32[264,128]{1,0:T(8,128)S(1)}, f32[264,128]{1,0:T(8,128)S(1)}, f32[264,128]{1,0:T(8,128)S(1)}, f32[264,128]{1,0:T(8,128)S(1)}, f32[256,256]{1,0:T(8,128)S(1)}) custom-call(f32[4,256,128]{2,1,0:T(8,128)} %bitcast.9, f32[1,2,256,256]{3,2,1,0:T(8,128)} %measured.3, s32[1,2,2]{2,1,0:T(2,128)} %offsets_from.1), custom_call_target="tpu_custom_call" | custom-call | bytes 1851408 | tf_op jit(solution)/shard_map/pallas_call | solution.py:359
  1.9 3.0 %collective-permute-start = (f32[264,128]{1,0:T(8,128)S(1)}, f32[264,128]{1,0:T(8,128)S(1)}, u32[]{:S(2)}, u32[]{:S(2)}) collective-permute-start(f32[264,128]{1,0:T(8,128)S(1)} %get-tuple-element.49), channel_id=1, source_target_pairs={{0,2},{2,0},{4,6},{6,4},{1,3},{3,1},{5,7},{7,5},{8,10},{10,8},{12,... | collective-permute-start | bytes 405512 | tf_op jit(solution)/shard_map/ppermute | solution.py:376
  4.9 1.5 %collective-permute-start.1 = (f32[264,128]{1,0:T(8,128)S(1)}, f32[264,128]{1,0:T(8,128)S(1)}, u32[]{:S(2)}, u32[]{:S(2)}) collective-permute-start(f32[264,128]{1,0:T(8,128)S(1)} %get-tuple-element.50), channel_id=1, source_target_pairs={{0,4},{2,6},{4,0},{6,2},{1,5},{3,7},{5,1},{7,3},{8,12},{10,14},{12... | collective-permute-start | bytes 405512 | tf_op jit(solution)/shard_map/ppermute | solution.py:376
  6.6 1.3 %fusion = (s32[1,1]{1,0:T(1,128)}, s32[1,1]{1,0:T(1,128)}) fusion(s32[1,2]{1,0:T(1,128)} %param.11), kind=kLoop, calls=%fused_computation.8 | loop fusion | bytes 16 | tf_op jit(solution)/shard_map/slice | solution.py:417
  9.2 0.1 slice_reduce_fusion.2
  9.3 3.5 %collective-permute-done.1.refs_0_ = f32[264,128]{1,0:T(8,128)S(1)} collective-permute-done((f32[264,128]{1,0:T(8,128)S(1)}, f32[264,128]{1,0:T(8,128)S(1)}, u32[]{:S(2)}, u32[]{:S(2)}) %collective-permute-start.1) | collective-permute-done | bytes 135200 | tf_op jit(solution)/shard_map/ppermute | solution.py:376
  13.0 0.1 slice_reduce_fusion
  13.2 1.3 %collective-permute-start.4 = (f32[2,256,128]{2,1,0:T(8,128)S(1)}, f32[2,256,128]{2,1,0:T(8,128)S(1)}, u32[]{:S(2)}, u32[]{:S(2)}) collective-permute-start(f32[2,256,128]{2,1,0:T(8,128)S(1)} %shard_map.96), channel_id=1, source_target_pairs={{8,0},{16,8},{24,16},{9,1},{17,9},{25,17},{10,2},{18,10},{26,18},{... | collective-permute-start | bytes 786440 | tf_op jit(solution)/shard_map/ppermute | solution.py:409
  14.5 1.6 %collective-permute-start.5 = (f32[256,256]{1,0:T(8,128)S(1)}, f32[256,256]{1,0:T(8,128)S(1)}, u32[]{:S(2)}, u32[]{:S(2)}) collective-permute-start(f32[256,256]{1,0:T(8,128)S(1)} %get-tuple-element.54), channel_id=1, source_target_pairs={{0,4},{4,0},{1,5},{5,1},{2,6},{6,2},{3,7},{7,3},{8,12},{12,8},{9,1... | collective-permute-start | bytes 786440 | tf_op jit(solution)/shard_map/ppermute | solution.py:410
  16.2 7.6 %collective-permute-done.4.refs_4_ = f32[2,256,128]{2,1,0:T(8,128)S(1)} collective-permute-done((f32[2,256,128]{2,1,0:T(8,128)S(1)}, f32[2,256,128]{2,1,0:T(8,128)S(1)}, u32[]{:S(2)}, u32[]{:S(2)}) %collective-permute-start.4) | collective-permute-done | bytes 262176 | tf_op jit(solution)/shard_map/ppermute | solution.py:409
  23.8 1.3 %shard_map.97 = (f32[256,128]{1,0:T(8,128)S(1)}, f32[256,128]{1,0:T(8,128)S(1)}, f32[256,128]{1,0:T(8,128)S(1)}, f32[256,128]{1,0:T(8,128)S(1)}, f32[256,128]{1,...) custom-call(s32[5,8]{1,0:T(8,128)S(1)} %concatenate.7.offs, ...), custom_call_target="tpu_custom_call" | custom-call | flops 2097152 | bytes 1851392 | tf_op jit(solution)/shard_map/pallas_call | solution.py:359
  25.2 1.6 %collective-permute-start.6 = (f32[256,128]{1,0:T(8,128)S(1)}, f32[256,128]{1,0:T(8,128)S(1)}, u32[]{:S(2)}, u32[]{:S(2)}) collective-permute-start(f32[256,128]{1,0:T(8,128)S(1)} %get-tuple-element.56), channel_id=1, source_target_pairs={{0,4},{1,5},{2,6},{3,7},{4,0},{5,1},{6,2},{7,3},{8,12},{9,13},{10,... | collective-permute-start | bytes 393224 | tf_op jit(solution)/shard_map/ppermute | solution.py:376
  26.8 0.5 collective-permute-start.7
  27.3 1.7 %collective-permute-start.9 = (f32[256,128]{1,0:T(8,128)S(1)}, f32[256,128]{1,0:T(8,128)S(1)}, u32[]{:S(2)}, u32[]{:S(2)}) collective-permute-start(f32[256,128]{1,0:T(8,128)S(1)} %get-tuple-element.59), channel_id=1, source_target_pairs={{0,3},{1,2},{2,1},{3,0},{4,7},{5,6},{6,5},{7,4},{8,11},{9,10},{10,... | collective-permute-start | bytes 393224 | tf_op jit(solution)/shard_map/ppermute | solution.py:376
  29.0 1.5 %collective-permute-start.10 = (f32[256,128]{1,0:T(8,128)S(1)}, f32[256,128]{1,0:T(8,128)S(1)}, u32[]{:S(2)}, u32[]{:S(2)}) collective-permute-start(f32[256,128]{1,0:T(8,128)S(1)} %get-tuple-element.60), channel_id=1, source_target_pairs={{0,6},{1,7},{2,4},{3,5},{4,2},{5,3},{6,0},{7,1},{8,14},{9,15},{10,... | collective-permute-start | bytes 393224 | tf_op jit(solution)/shard_map/ppermute | solution.py:376
  30.5 0.7 collective-permute-start.11
  31.2 2.0 %collective-permute-done.7.refs_1_ = f32[256,128]{1,0:T(8,128)S(1)} collective-permute-done((f32[256,128]{1,0:T(8,128)S(1)}, f32[256,128]{1,0:T(8,128)S(1)}, u32[]{:S(2)}, u32[]{:S(2)}) %collective-permute-start.7) | collective-permute-done | bytes 131104 | tf_op jit(solution)/shard_map/ppermute | solution.py:376
  33.1 2.5 %shard_map.98 = (f32[2,256,256]{2,1,0:T(8,128)S(1)}, f32[256,256]{1,0:T(8,128)S(1)}, bf16[6,512,256]{2,1,0:T(8,128)(2,1)S(1)}) custom-call(s32[5,8]{1,0:T(8,128)S(1)} %concatenate.7.offs, f32[256,256]{1,0:T(8,128)S(1)} %collective-permute-done.5.taken, f32[2,256,256]{2,1,0:T(8,128)} %probe_from.1, f32[1,2,256,256]{3,2,1,0:T(8,128)} %measured.3, ...), custom_call_target="tpu_custom_call" | custom-call | flops 201326592 | bytes 5505024 | tf_op jit(solution)/shard_map/pallas_call | solution.py:359
  35.7 2.1 %collective-permute-done.10.refs_4_ = f32[256,128]{1,0:T(8,128)S(1)} collective-permute-done((f32[256,128]{1,0:T(8,128)S(1)}, f32[256,128]{1,0:T(8,128)S(1)}, u32[]{:S(2)}, u32[]{:S(2)}) %collective-permute-start.10) | collective-permute-done | bytes 131104 | tf_op jit(solution)/shard_map/ppermute | solution.py:376
  37.8 1.9 %collective-permute-done.11.refs_5_ = f32[256,128]{1,0:T(8,128)S(1)} collective-permute-done((f32[256,128]{1,0:T(8,128)S(1)}, f32[256,128]{1,0:T(8,128)S(1)}, u32[]{:S(2)}, u32[]{:S(2)}) %collective-permute-start.11) | collective-permute-done | bytes 131104 | tf_op jit(solution)/shard_map/ppermute | solution.py:376
  39.6 4.2 %shard_map.99 = (f32[768,128]{1,0:T(8,128)S(1)}, f32[256,128]{1,0:T(8,128)S(1)}, f32[256,128]{1,0:T(8,128)S(1)}, f32[256,128]{1,0:T(8,128)S(1)}, f32[256,128]{1,...) custom-call(s32[5,8]{1,0:T(8,128)S(1)} %concatenate.7.offs, ...), custom_call_target="tpu_custom_call" | custom-call | flops 1610612736 | bytes 5120000 | tf_op jit(solution)/shard_map/pallas_call | solution.py:359
  43.9 0.4 collective-permute-start.13
  44.2 1.5 %collective-permute-start.14 = (f32[256,128]{1,0:T(8,128)S(1)}, f32[256,128]{1,0:T(8,128)S(1)}, u32[]{:S(2)}, u32[]{:S(2)}) collective-permute-start(f32[256,128]{1,0:T(8,128)S(1)} %get-tuple-element.69), channel_id=1, source_target_pairs={{0,4},{1,5},{2,6},{3,7},{4,0},{5,1},{6,2},{7,3},{8,12},{9,13},{10,... | collective-permute-start | bytes 393224 | tf_op jit(solution)/shard_map/ppermute | solution.py:376
  45.7 0.6 collective-permute-start.15
  46.3 0.2 collective-permute-start.16
  46.5 1.5 %collective-permute-start.17 = (f32[256,128]{1,0:T(8,128)S(1)}, f32[256,128]{1,0:T(8,128)S(1)}, u32[]{:S(2)}, u32[]{:S(2)}) collective-permute-start(f32[256,128]{1,0:T(8,128)S(1)} %get-tuple-element.72), channel_id=1, source_target_pairs={{0,3},{1,2},{2,1},{3,0},{4,7},{5,6},{6,5},{7,4},{8,11},{9,10},{10,... | collective-permute-start | bytes 393224 | tf_op jit(solution)/shard_map/ppermute | solution.py:376
  48.0 2.4 %collective-permute-done.14.refs_1_ = f32[256,128]{1,0:T(8,128)S(1)} collective-permute-done((f32[256,128]{1,0:T(8,128)S(1)}, f32[256,128]{1,0:T(8,128)S(1)}, u32[]{:S(2)}, u32[]{:S(2)}) %collective-permute-start.14) | collective-permute-done | bytes 131104 | tf_op jit(solution)/shard_map/ppermute | solution.py:376
  50.3 1.5 %collective-permute-start.18 = (f32[256,128]{1,0:T(8,128)S(1)}, f32[256,128]{1,0:T(8,128)S(1)}, u32[]{:S(2)}, u32[]{:S(2)}) collective-permute-start(f32[256,128]{1,0:T(8,128)S(1)} %get-tuple-element.73), channel_id=1, source_target_pairs={{0,6},{1,7},{2,4},{3,5},{4,2},{5,3},{6,0},{7,1},{8,14},{9,15},{10,... | collective-permute-start | bytes 393224 | tf_op jit(solution)/shard_map/ppermute | solution.py:376
  51.9 0.2 collective-permute-done.15.refs_2_
  52.1 0.7 collective-permute-start.20
  52.8 1.2 %collective-permute-start.21 = (f32[128,128]{1,0:T(8,128)S(1)}, f32[128,128]{1,0:T(8,128)S(1)}, u32[]{:S(2)}, u32[]{:S(2)}) collective-permute-start(f32[128,128]{1,0:T(8,128)S(1)} %get-tuple-element.78), channel_id=1, source_target_pairs={{0,2},{2,0},{4,6},{6,4},{1,3},{3,1},{5,7},{7,5},{8,10},{10,8},{12,... | collective-permute-start | bytes 196616 | tf_op jit(solution)/shard_map/ppermute | solution.py:376
  54.0 1.6 %collective-permute-start.22 = (f32[128,128]{1,0:T(8,128)S(1)}, f32[128,128]{1,0:T(8,128)S(1)}, u32[]{:S(2)}, u32[]{:S(2)}) collective-permute-start(f32[128,128]{1,0:T(8,128)S(1)} %get-tuple-element.79), channel_id=1, source_target_pairs={{0,6},{2,4},{4,2},{6,0},{1,7},{3,5},{5,3},{7,1},{8,14},{10,12},{12... | collective-permute-start | bytes 196616 | tf_op jit(solution)/shard_map/ppermute | solution.py:376
  55.6 2.1 %collective-permute-done.18.refs_5_ = f32[256,128]{1,0:T(8,128)S(1)} collective-permute-done((f32[256,128]{1,0:T(8,128)S(1)}, f32[256,128]{1,0:T(8,128)S(1)}, u32[]{:S(2)}, u32[]{:S(2)}) %collective-permute-start.18) | collective-permute-done | bytes 131104 | tf_op jit(solution)/shard_map/ppermute | solution.py:376
  57.7 0.9 collective-permute-done.19.refs_6_
  58.6 2.9 %collective-permute-done.20.refs_8_ = f32[128,128]{1,0:T(8,128)S(1)} collective-permute-done((f32[128,128]{1,0:T(8,128)S(1)}, f32[128,128]{1,0:T(8,128)S(1)}, u32[]{:S(2)}, u32[]{:S(2)}) %collective-permute-start.20) | collective-permute-done | bytes 65568 | tf_op jit(solution)/shard_map/ppermute | solution.py:376
  61.5 0.8 collective-permute-done.22.refs_10_
  62.3 1.0 %shard_map.102 = (f32[2,256,128]{2,1,0:T(8,128)S(1)}, f32[64,256]{1,0:T(8,128)S(1)}) custom-call(s32[5,8]{1,0:T(8,128)S(1)} %concatenate.7.offs, f32[768,128]{1,0:T(8,128)S(1)} %collective-permute-done.13.refs_0_.got, f32[256,128]{1,0:T(8,128)S(1)} %collective-permute-done.14.refs_1_, f32[256,128]{1,0:T(8,128)S(1)} %collective-permute-done.15.refs_2_, ...), custom_call_target="tpu_custom_call" | custom-call | flops 2097152 | bytes 1900544 | tf_op jit(solution)/shard_map/pallas_call | solution.py:359
  63.3 3.7 %collective-permute-start.23 = (f32[2,256,128]{2,1,0:T(8,128)S(1)}, f32[2,256,128]{2,1,0:T(8,128)S(1)}, u32[]{:S(2)}, u32[]{:S(2)}) collective-permute-start(f32[2,256,128]{2,1,0:T(8,128)S(1)} %get-tuple-element.81), channel_id=1, source_target_pairs={{0,8},{8,16},{16,24},{1,9},{9,17},{17,25},{2,10},{10,18},{18,26},{... | collective-permute-start | bytes 786440 | tf_op jit(solution)/shard_map/ppermute | solution.py:455
  67.1 1.6 %collective-permute-start.24 = (f32[64,256]{1,0:T(8,128)S(1)}, f32[64,256]{1,0:T(8,128)S(1)}, u32[]{:S(2)}, u32[]{:S(2)}) collective-permute-start(f32[64,256]{1,0:T(8,128)S(1)} %get-tuple-element.86), channel_id=1, source_target_pairs={{0,8},{8,0},{16,24},{24,16},{1,9},{9,1},{17,25},{25,17},{2,10},{10... | collective-permute-start | bytes 196616 | tf_op jit(solution)/shard_map/ppermute | solution.py:458
  68.7 1.5 %shard_map.100.own = f32[4,256,128]{2,1,0:T(8,128)S(1)} custom-call(s32[5,8]{1,0:T(8,128)S(1)} %concatenate.7.offs, f32[768,128]{1,0:T(8,128)S(1)} %collective-permute-done.13.refs_0_.got, f32[256,128]{1,0:T(8,128)S(1)} %collective-permute-done.14.refs_1_, f32[256,128]{1,0:T(8,128)S(1)} %collective-permute-done.15.refs_2_, ...), custom_call_target="tpu_custom_call" | custom-call | flops 4194304 | bytes 1835008 | tf_op jit(solution)/shard_map/pallas_call | solution.py:359
  70.2 2.6 %collective-permute-done.23.above = f32[2,256,128]{2,1,0:T(8,128)S(1)} collective-permute-done((f32[2,256,128]{2,1,0:T(8,128)S(1)}, f32[2,256,128]{2,1,0:T(8,128)S(1)}, u32[]{:S(2)}, u32[]{:S(2)}) %collective-permute-start.23) | collective-permute-done | bytes 262176 | tf_op jit(solution)/shard_map/ppermute | solution.py:455
  72.9 0.6 collective-permute-done.24
  73.5 2.7 %collective-permute-start.28 = (f32[64,256]{1,0:T(8,128)S(1)}, f32[64,256]{1,0:T(8,128)S(1)}, u32[]{:S(2)}, u32[]{:S(2)}) collective-permute-start(f32[64,256]{1,0:T(8,128)S(1)} %add.8), channel_id=1, source_target_pairs={{0,16},{8,24},{16,0},{24,8},{1,17},{9,25},{17,1},{25,9},{2,18},{10... | collective-permute-start | bytes 196616 | tf_op jit(solution)/shard_map/ppermute | solution.py:384
  76.2 1.3 %collective-permute-start.25 = (f32[256,128]{1,0:T(8,128)S(1)}, f32[256,128]{1,0:T(8,128)S(1)}, u32[]{:S(2)}, u32[]{:S(2)}) collective-permute-start(f32[256,128]{1,0:T(8,128)S(1)} %get-tuple-element.87), channel_id=1, source_target_pairs={{0,4},{2,6},{4,0},{6,2},{1,5},{3,7},{5,1},{7,3},{8,12},{10,14},{12... | collective-permute-start | bytes 393224 | tf_op jit(solution)/shard_map/ppermute | solution.py:376
  77.5 0.7 collective-permute-start.26
  78.2 1.5 %collective-permute-start.27 = (f32[256,128]{1,0:T(8,128)S(1)}, f32[256,128]{1,0:T(8,128)S(1)}, u32[]{:S(2)}, u32[]{:S(2)}) collective-permute-start(f32[256,128]{1,0:T(8,128)S(1)} %get-tuple-element.89), channel_id=1, source_target_pairs={{0,6},{2,4},{4,2},{6,0},{1,7},{3,5},{5,3},{7,1},{8,14},{10,12},{12... | collective-permute-start | bytes 393224 | tf_op jit(solution)/shard_map/ppermute | solution.py:376
  79.7 10.2 %all_gather.3.refs_4_ = f32[512,256]{1,0:T(8,128)S(1)} all-gather(f32[64,256]{1,0:T(8,128)S(1)} %add.9), channel_id=1, replica_groups=mesh['pair'=4,'half'=2,'col'=2,'core'=2] {'half','col','core'}, dimensions={0}, use_global_device_ids=true | all-gather | bytes 589824 | tf_op jit(solution)/shard_map/all_gather | solution.py:467
  89.9 1.0 %shard_map.104 = (f32[4,256,128]{2,1,0:T(8,128)}, f32[512,256]{1,0:T(8,128)}) custom-call(f32[256,128]{1,0:T(8,128)S(1)} %collective-permute-done.25.refs_0_, f32[256,128]{1,0:T(8,128)S(1)} %collective-permute-done.26.refs_1_, f32[256,128]{1,0:T(8,128)S(1)} %collective-permute-done.27.refs_2_, f32[256,128]{1,0:T(8,128)S(1)} %get-tuple-element.90.refs_3_, ...), custom_call_target="tpu_custom_call" | custom-call | bytes 2097152 | tf_op jit(solution)/shard_map/pallas_call | solution.py:359
  (34 shorter events, 0.6 us)
Async XLA Ops:
  1.9 7.3 %collective-permute-start = (f32[264,128]{1,0:T(8,128)S(1)}, f32[264,128]{1,0:T(8,128)S(1)}, u32[]{:S(2)}, u32[]{:S(2)}) collective-permute-start(f32[264,128]{1,0:T(8,128)S(1)} %get-tuple-element.49), channel_id=1, source_target_pairs={{0,2},{2,0},{4,6},{6,4},{1,3},{3,1},{5,7},{7,5},{8,10},{10,8},{12,... | collective-permute-start | bytes 405512 | tf_op jit(solution)/shard_map/ppermute | solution.py:376
  4.9 7.9 %collective-permute-start.1 = (f32[264,128]{1,0:T(8,128)S(1)}, f32[264,128]{1,0:T(8,128)S(1)}, u32[]{:S(2)}, u32[]{:S(2)}) collective-permute-start(f32[264,128]{1,0:T(8,128)S(1)} %get-tuple-element.50), channel_id=1, source_target_pairs={{0,4},{2,6},{4,0},{6,2},{1,5},{3,7},{5,1},{7,3},{8,12},{10,14},{12... | collective-permute-start | bytes 405512 | tf_op jit(solution)/shard_map/ppermute | solution.py:376
  6.4 6.5 %collective-permute-start.2 = (f32[264,128]{1,0:T(8,128)S(1)}, f32[264,128]{1,0:T(8,128)S(1)}, u32[]{:S(2)}, u32[]{:S(2)}) collective-permute-start(f32[264,128]{1,0:T(8,128)S(1)} %get-tuple-element.51), channel_id=1, source_target_pairs={{0,6},{2,4},{4,2},{6,0},{1,7},{3,5},{5,3},{7,1},{8,14},{10,12},{12... | collective-permute-start | bytes 405512 | tf_op jit(solution)/shard_map/ppermute | solution.py:376
  13.1 3.0 %collective-permute-start.3 = (s32[4,4]{1,0:T(4,128)S(1)}, s32[4,4]{1,0:T(4,128)S(1)}, u32[]{:S(2)}, u32[]{:S(2)}) collective-permute-start(s32[4,4]{1,0:T(4,128)S(1)} %maximum_convert_fusion), channel_id=1, source_target_pairs={{0,1},{1,0},{2,3},{3,2},{4,5},{5,4},{6,7},{7,6},{8,9},{9,8},{10,11... | collective-permute-start | bytes 200 | tf_op jit(solution)/shard_map/ppermute | solution.py:415
  13.2 10.6 %collective-permute-start.4 = (f32[2,256,128]{2,1,0:T(8,128)S(1)}, f32[2,256,128]{2,1,0:T(8,128)S(1)}, u32[]{:S(2)}, u32[]{:S(2)}) collective-permute-start(f32[2,256,128]{2,1,0:T(8,128)S(1)} %shard_map.96), channel_id=1, source_target_pairs={{8,0},{16,8},{24,16},{9,1},{17,9},{25,17},{10,2},{18,10},{26,18},{... | collective-permute-start | bytes 786440 | tf_op jit(solution)/shard_map/ppermute | solution.py:409
  14.5 9.3 %collective-permute-start.5 = (f32[256,256]{1,0:T(8,128)S(1)}, f32[256,256]{1,0:T(8,128)S(1)}, u32[]{:S(2)}, u32[]{:S(2)}) collective-permute-start(f32[256,256]{1,0:T(8,128)S(1)} %get-tuple-element.54), channel_id=1, source_target_pairs={{0,4},{4,0},{1,5},{5,1},{2,6},{6,2},{3,7},{7,3},{8,12},{12,8},{9,1... | collective-permute-start | bytes 786440 | tf_op jit(solution)/shard_map/ppermute | solution.py:410
  25.2 5.3 %collective-permute-start.6 = (f32[256,128]{1,0:T(8,128)S(1)}, f32[256,128]{1,0:T(8,128)S(1)}, u32[]{:S(2)}, u32[]{:S(2)}) collective-permute-start(f32[256,128]{1,0:T(8,128)S(1)} %get-tuple-element.56), channel_id=1, source_target_pairs={{0,4},{1,5},{2,6},{3,7},{4,0},{5,1},{6,2},{7,3},{8,12},{9,13},{10,... | collective-permute-start | bytes 393224 | tf_op jit(solution)/shard_map/ppermute | solution.py:376
  26.8 6.4 %collective-permute-start.7 = (f32[256,128]{1,0:T(8,128)S(1)}, f32[256,128]{1,0:T(8,128)S(1)}, u32[]{:S(2)}, u32[]{:S(2)}) collective-permute-start(f32[256,128]{1,0:T(8,128)S(1)} %get-tuple-element.57), channel_id=1, source_target_pairs={{0,2},{1,3},{2,0},{3,1},{4,6},{5,7},{6,4},{7,5},{8,10},{9,11},{10,... | collective-permute-start | bytes 393224 | tf_op jit(solution)/shard_map/ppermute | solution.py:376
  27.3 8.4 %collective-permute-start.8 = (f32[256,128]{1,0:T(8,128)S(1)}, f32[256,128]{1,0:T(8,128)S(1)}, u32[]{:S(2)}, u32[]{:S(2)}) collective-permute-start(f32[256,128]{1,0:T(8,128)S(1)} %get-tuple-element.58), channel_id=1, source_target_pairs={{0,5},{1,4},{2,7},{3,6},{4,1},{5,0},{6,3},{7,2},{8,13},{9,12},{10,... | collective-permute-start | bytes 393224 | tf_op jit(solution)/shard_map/ppermute | solution.py:376
  27.3 8.4 %collective-permute-start.9 = (f32[256,128]{1,0:T(8,128)S(1)}, f32[256,128]{1,0:T(8,128)S(1)}, u32[]{:S(2)}, u32[]{:S(2)}) collective-permute-start(f32[256,128]{1,0:T(8,128)S(1)} %get-tuple-element.59), channel_id=1, source_target_pairs={{0,3},{1,2},{2,1},{3,0},{4,7},{5,6},{6,5},{7,4},{8,11},{9,10},{10,... | collective-permute-start | bytes 393224 | tf_op jit(solution)/shard_map/ppermute | solution.py:376
  29.0 8.7 %collective-permute-start.10 = (f32[256,128]{1,0:T(8,128)S(1)}, f32[256,128]{1,0:T(8,128)S(1)}, u32[]{:S(2)}, u32[]{:S(2)}) collective-permute-start(f32[256,128]{1,0:T(8,128)S(1)} %get-tuple-element.60), channel_id=1, source_target_pairs={{0,6},{1,7},{2,4},{3,5},{4,2},{5,3},{6,0},{7,1},{8,14},{9,15},{10,... | collective-permute-start | bytes 393224 | tf_op jit(solution)/shard_map/ppermute | solution.py:376
  30.5 9.1 %collective-permute-start.11 = (f32[256,128]{1,0:T(8,128)S(1)}, f32[256,128]{1,0:T(8,128)S(1)}, u32[]{:S(2)}, u32[]{:S(2)}) collective-permute-start(f32[256,128]{1,0:T(8,128)S(1)} %get-tuple-element.61), channel_id=1, source_target_pairs={{0,7},{1,6},{2,5},{3,4},{4,3},{5,2},{6,1},{7,0},{8,15},{9,14},{10,... | collective-permute-start | bytes 393224 | tf_op jit(solution)/shard_map/ppermute | solution.py:376
  33.1 6.5 %copy-start = (f32[2,136,128]{2,1,0:T(8,128)S(1)}, f32[2,136,128]{2,1,0:T(8,128)}, u32[]{:S(2)}) copy-start(f32[2,136,128]{2,1,0:T(8,128)} %constant.17.clone.refs_11_) | copy-start | bytes 417796
  33.1 6.5 %collective-permute-start.12 = (f32[256,128]{1,0:T(8,128)S(1)}, f32[256,128]{1,0:T(8,128)S(1)}, u32[]{:S(2)}, u32[]{:S(2)}) collective-permute-start(f32[256,128]{1,0:T(8,128)S(1)} %get-tuple-element.62), channel_id=1, source_target_pairs={{0,1},{1,0},{2,3},{3,2},{4,5},{5,4},{6,7},{7,6},{8,9},{9,8},{10,11... | collective-permute-start | bytes 393224 | tf_op jit(solution)/shard_map/ppermute | solution.py:376
  43.9 8.0 %collective-permute-start.13 = (f32[768,128]{1,0:T(8,128)S(1)}, f32[768,128]{1,0:T(8,128)S(1)}, u32[]{:S(2)}, u32[]{:S(2)}) collective-permute-start(f32[768,128]{1,0:T(8,128)S(1)} %get-tuple-element.68), channel_id=1, source_target_pairs={{0,1},{1,0},{2,3},{3,2},{4,5},{5,4},{6,7},{7,6},{8,9},{9,8},{10,11... | collective-permute-start | bytes 1179656 | tf_op jit(solution)/shard_map/ppermute | solution.py:376
  44.2 6.1 %collective-permute-start.14 = (f32[256,128]{1,0:T(8,128)S(1)}, f32[256,128]{1,0:T(8,128)S(1)}, u32[]{:S(2)}, u32[]{:S(2)}) collective-permute-start(f32[256,128]{1,0:T(8,128)S(1)} %get-tuple-element.69), channel_id=1, source_target_pairs={{0,4},{1,5},{2,6},{3,7},{4,0},{5,1},{6,2},{7,3},{8,12},{9,13},{10,... | collective-permute-start | bytes 393224 | tf_op jit(solution)/shard_map/ppermute | solution.py:376
  45.7 6.4 %collective-permute-start.15 = (f32[256,128]{1,0:T(8,128)S(1)}, f32[256,128]{1,0:T(8,128)S(1)}, u32[]{:S(2)}, u32[]{:S(2)}) collective-permute-start(f32[256,128]{1,0:T(8,128)S(1)} %get-tuple-element.70), channel_id=1, source_target_pairs={{0,2},{1,3},{2,0},{3,1},{4,6},{5,7},{6,4},{7,5},{8,10},{9,11},{10,... | collective-permute-start | bytes 393224 | tf_op jit(solution)/shard_map/ppermute | solution.py:376
  46.3 6.5 %collective-permute-start.16 = (f32[256,128]{1,0:T(8,128)S(1)}, f32[256,128]{1,0:T(8,128)S(1)}, u32[]{:S(2)}, u32[]{:S(2)}) collective-permute-start(f32[256,128]{1,0:T(8,128)S(1)} %get-tuple-element.71), channel_id=1, source_target_pairs={{0,5},{1,4},{2,7},{3,6},{4,1},{5,0},{6,3},{7,2},{8,13},{9,12},{10,... | collective-permute-start | bytes 393224 | tf_op jit(solution)/shard_map/ppermute | solution.py:376
  46.5 7.5 %collective-permute-start.17 = (f32[256,128]{1,0:T(8,128)S(1)}, f32[256,128]{1,0:T(8,128)S(1)}, u32[]{:S(2)}, u32[]{:S(2)}) collective-permute-start(f32[256,128]{1,0:T(8,128)S(1)} %get-tuple-element.72), channel_id=1, source_target_pairs={{0,3},{1,2},{2,1},{3,0},{4,7},{5,6},{6,5},{7,4},{8,11},{9,10},{10,... | collective-permute-start | bytes 393224 | tf_op jit(solution)/shard_map/ppermute | solution.py:376
  50.3 7.3 %collective-permute-start.18 = (f32[256,128]{1,0:T(8,128)S(1)}, f32[256,128]{1,0:T(8,128)S(1)}, u32[]{:S(2)}, u32[]{:S(2)}) collective-permute-start(f32[256,128]{1,0:T(8,128)S(1)} %get-tuple-element.73), channel_id=1, source_target_pairs={{0,6},{1,7},{2,4},{3,5},{4,2},{5,3},{6,0},{7,1},{8,14},{9,15},{10,... | collective-permute-start | bytes 393224 | tf_op jit(solution)/shard_map/ppermute | solution.py:376
  51.8 6.8 %collective-permute-start.19 = (f32[256,128]{1,0:T(8,128)S(1)}, f32[256,128]{1,0:T(8,128)S(1)}, u32[]{:S(2)}, u32[]{:S(2)}) collective-permute-start(f32[256,128]{1,0:T(8,128)S(1)} %get-tuple-element.74), channel_id=1, source_target_pairs={{0,7},{1,6},{2,5},{3,4},{4,3},{5,2},{6,1},{7,0},{8,15},{9,14},{10,... | collective-permute-start | bytes 393224 | tf_op jit(solution)/shard_map/ppermute | solution.py:376
  52.1 9.4 %collective-permute-start.20 = (f32[128,128]{1,0:T(8,128)S(1)}, f32[128,128]{1,0:T(8,128)S(1)}, u32[]{:S(2)}, u32[]{:S(2)}) collective-permute-start(f32[128,128]{1,0:T(8,128)S(1)} %get-tuple-element.77), channel_id=1, source_target_pairs={{0,4},{2,6},{4,0},{6,2},{1,5},{3,7},{5,1},{7,3},{8,12},{10,14},{12... | collective-permute-start | bytes 196616 | tf_op jit(solution)/shard_map/ppermute | solution.py:376
  52.8 8.7 %collective-permute-start.21 = (f32[128,128]{1,0:T(8,128)S(1)}, f32[128,128]{1,0:T(8,128)S(1)}, u32[]{:S(2)}, u32[]{:S(2)}) collective-permute-start(f32[128,128]{1,0:T(8,128)S(1)} %get-tuple-element.78), channel_id=1, source_target_pairs={{0,2},{2,0},{4,6},{6,4},{1,3},{3,1},{5,7},{7,5},{8,10},{10,8},{12,... | collective-permute-start | bytes 196616 | tf_op jit(solution)/shard_map/ppermute | solution.py:376
  54.0 8.3 %collective-permute-start.22 = (f32[128,128]{1,0:T(8,128)S(1)}, f32[128,128]{1,0:T(8,128)S(1)}, u32[]{:S(2)}, u32[]{:S(2)}) collective-permute-start(f32[128,128]{1,0:T(8,128)S(1)} %get-tuple-element.79), channel_id=1, source_target_pairs={{0,6},{2,4},{4,2},{6,0},{1,7},{3,5},{5,3},{7,1},{8,14},{10,12},{12... | collective-permute-start | bytes 196616 | tf_op jit(solution)/shard_map/ppermute | solution.py:376
  63.3 9.5 %collective-permute-start.23 = (f32[2,256,128]{2,1,0:T(8,128)S(1)}, f32[2,256,128]{2,1,0:T(8,128)S(1)}, u32[]{:S(2)}, u32[]{:S(2)}) collective-permute-start(f32[2,256,128]{2,1,0:T(8,128)S(1)} %get-tuple-element.81), channel_id=1, source_target_pairs={{0,8},{8,16},{16,24},{1,9},{9,17},{17,25},{2,10},{10,18},{18,26},{... | collective-permute-start | bytes 786440 | tf_op jit(solution)/shard_map/ppermute | solution.py:455
  67.1 6.4 %collective-permute-start.24 = (f32[64,256]{1,0:T(8,128)S(1)}, f32[64,256]{1,0:T(8,128)S(1)}, u32[]{:S(2)}, u32[]{:S(2)}) collective-permute-start(f32[64,256]{1,0:T(8,128)S(1)} %get-tuple-element.86), channel_id=1, source_target_pairs={{0,8},{8,0},{16,24},{24,16},{1,9},{9,1},{17,25},{25,17},{2,10},{10... | collective-permute-start | bytes 196616 | tf_op jit(solution)/shard_map/ppermute | solution.py:458
  73.5 6.2 %collective-permute-start.28 = (f32[64,256]{1,0:T(8,128)S(1)}, f32[64,256]{1,0:T(8,128)S(1)}, u32[]{:S(2)}, u32[]{:S(2)}) collective-permute-start(f32[64,256]{1,0:T(8,128)S(1)} %add.8), channel_id=1, source_target_pairs={{0,16},{8,24},{16,0},{24,8},{1,17},{9,25},{17,1},{25,9},{2,18},{10... | collective-permute-start | bytes 196616 | tf_op jit(solution)/shard_map/ppermute | solution.py:384
  76.2 13.7 %collective-permute-start.25 = (f32[256,128]{1,0:T(8,128)S(1)}, f32[256,128]{1,0:T(8,128)S(1)}, u32[]{:S(2)}, u32[]{:S(2)}) collective-permute-start(f32[256,128]{1,0:T(8,128)S(1)} %get-tuple-element.87), channel_id=1, source_target_pairs={{0,4},{2,6},{4,0},{6,2},{1,5},{3,7},{5,1},{7,3},{8,12},{10,14},{12... | collective-permute-start | bytes 393224 | tf_op jit(solution)/shard_map/ppermute | solution.py:376
  77.5 12.4 %collective-permute-start.26 = (f32[256,128]{1,0:T(8,128)S(1)}, f32[256,128]{1,0:T(8,128)S(1)}, u32[]{:S(2)}, u32[]{:S(2)}) collective-permute-start(f32[256,128]{1,0:T(8,128)S(1)} %get-tuple-element.88), channel_id=1, source_target_pairs={{0,2},{2,0},{4,6},{6,4},{1,3},{3,1},{5,7},{7,5},{8,10},{10,8},{12,... | collective-permute-start | bytes 393224 | tf_op jit(solution)/shard_map/ppermute | solution.py:376
  78.2 11.7 %collective-permute-start.27 = (f32[256,128]{1,0:T(8,128)S(1)}, f32[256,128]{1,0:T(8,128)S(1)}, u32[]{:S(2)}, u32[]{:S(2)}) collective-permute-start(f32[256,128]{1,0:T(8,128)S(1)} %get-tuple-element.89), channel_id=1, source_target_pairs={{0,6},{2,4},{4,2},{6,0},{1,7},{3,5},{5,3},{7,1},{8,14},{10,12},{12... | collective-permute-start | bytes 393224 | tf_op jit(solution)/shard_map/ppermute | solution.py:376

commit v19 on v18

--- a/solution.py
+++ b/solution.py
@@ -12,7 +12,7 @@
 
 GRAD_WEIGHT = 0.0625
 PLANE = ("half", "col", "core")
-EIGHT, BACK, FOUR = (4, 2, 5, 3, 6, 7, 1, 0), (1, 4, 2, 5, 3, 6, 7, 0), (2, 1, 3, 0)
+EIGHT, BACK, FOUR = (2, 4, 3, 5, 6, 7, 1, 0), (1, 4, 2, 5, 3, 6, 7, 0), (2, 1, 3, 0)
 VMEM_LIMIT = 24 * 1024 * 1024
 
 
@@ -408,7 +408,6 @@
     lowest, given = lax.optimization_barrier((lowest, given))
     below = lax.ppermute(lowest, "pair", [(k, k - 1) for k in range(1, pairs)])
     taken = lax.ppermute(given, "half", [(0, 1), (1, 0)])
-    below, taken = lax.optimization_barrier((below, taken))
 
     turned = dict(zip(FOUR, own))
     offs = jnp.stack([turned[turn][rows : rows + 4, 0] for turn in range(4)]).astype(jnp.int32)

time: 91.1 us -> 89.5 us (0.982)
  blocking collectives: 10.2 us -> 8.82 us
    ppermute x23, waiting for transfers between devices: 18.8 us -> 17.2 us  [deal(): lax.ppermute(value, axes, [(k, k ^ turn) for k in range(len(order))])]
    all_gather x1, blocking collectives: 10.2 us -> 8.82 us  [local(): probe_grad = lax.all_gather(probe_band, PLANE, axis=0, tiled=True)]
    ppermute x23, starting transfers between devices: 23.1 us -> 24.3 us  [deal(): lax.ppermute(value, axes, [(k, k ^ turn) for k in range(len(order))])]
  transfers between devices with their start and end apart: 29 -> 29, of which waited for: 13 -> 13; matrix products, arithmetic and copies ran while one was open for 2% -> 2% of each run, Pallas kernels for 5% -> 6%
where the time goes in v19:
time: 89.5 us; the launch traced here: 89.2 us
  starting transfers between devices  34.5 us (39%)
  waiting for transfers between devices  28.9 us (32%)
  Pallas kernels  13 us (15%)
  blocking collectives  8.82 us (10%)
  between operations  2.06 us (2%)
  local copies, waits for them, and re-layouts  1.79 us (2%)
    ppermute x23, starting transfers between devices, deal(): lax.ppermute(value, axes, [(k, k ^ turn) for k in range(len(order))])  24.3 us
    ppermute x23, waiting for transfers between devices, deal(): lax.ppermute(value, axes, [(k, k ^ turn) for k in range(len(order))])  17.2 us
    pallas_call x10, Pallas kernels, call(): pl.pallas_call(kernel, out_shape=[x for x, unused in outs], in_specs=[SME...  13 us
    all_gather x1, blocking collectives, local(): probe_grad = lax.all_gather(probe_band, PLANE, axis=0, tiled=True)  8.82 us
    ppermute x1, waiting for transfers between devices, local(): below = lax.ppermute(lowest, 'pair', [(k, k - 1) for k in range(1, pairs)])  7.61 us
    ppermute x1, starting transfers between devices, local(): lax.ppermute(lower_sums, 'pair', [(k, k + 1) for k in range(pairs - 1)])  3.49 us
    ppermute x1, waiting for transfers between devices, local(): lax.ppermute(lower_sums, 'pair', [(k, k + 1) for k in range(pairs - 1)])  3.18 us
    ppermute x1, starting transfers between devices, sum_over(): lax.ppermute(value, axis, [(k, k ^ step) for k in range(size)])  2.21 us
  transfers between devices with their start and end apart: 29, of which 13 were waited for; matrix products, arithmetic and copies ran while one was open for 2% of the time, Pallas kernels for 6%

profile of v19, /device:TPU:0, one launch (start us, length us, event | category | flops | bytes accessed | tf_op | source)
XLA Modules:
  0.0 89.2 jit_solution(11466915280098267571)
XLA Ops:
  0.6 1.3 %shard_map.95 = (f32[264,128]{1,0:T(8,128)S(1)}, f32[264,128]{1,0:T(8,128)S(1)}, f32[264,128]{1,0:T(8,128)S(1)}, f32[264,128]{1,0:T(8,128)S(1)}, f32[256,256]{1,0:T(8,128)S(1)}) custom-call(f32[4,256,128]{2,1,0:T(8,128)} %bitcast.9, f32[1,2,256,256]{3,2,1,0:T(8,128)} %measured.3, s32[1,2,2]{2,1,0:T(2,128)} %offsets_from.1), custom_call_target="tpu_custom_call" | custom-call | bytes 1851408 | tf_op jit(solution)/shard_map/pallas_call | solution.py:359
  1.9 3.0 %collective-permute-start = (f32[264,128]{1,0:T(8,128)S(1)}, f32[264,128]{1,0:T(8,128)S(1)}, u32[]{:S(2)}, u32[]{:S(2)}) collective-permute-start(f32[264,128]{1,0:T(8,128)S(1)} %get-tuple-element.47), channel_id=1, source_target_pairs={{0,2},{2,0},{4,6},{6,4},{1,3},{3,1},{5,7},{7,5},{8,10},{10,8},{12,... | collective-permute-start | bytes 405512 | tf_op jit(solution)/shard_map/ppermute | solution.py:376
  4.9 1.5 %collective-permute-start.1 = (f32[264,128]{1,0:T(8,128)S(1)}, f32[264,128]{1,0:T(8,128)S(1)}, u32[]{:S(2)}, u32[]{:S(2)}) collective-permute-start(f32[264,128]{1,0:T(8,128)S(1)} %get-tuple-element.48), channel_id=1, source_target_pairs={{0,4},{2,6},{4,0},{6,2},{1,5},{3,7},{5,1},{7,3},{8,12},{10,14},{12... | collective-permute-start | bytes 405512 | tf_op jit(solution)/shard_map/ppermute | solution.py:376
  6.6 1.3 %fusion = (s32[1,1]{1,0:T(1,128)}, s32[1,1]{1,0:T(1,128)}) fusion(s32[1,2]{1,0:T(1,128)} %param.11), kind=kLoop, calls=%fused_computation.8 | loop fusion | bytes 16 | tf_op jit(solution)/shard_map/slice | solution.py:416
  9.2 0.1 slice_reduce_fusion.2
  9.3 3.5 %collective-permute-done.1.refs_0_ = f32[264,128]{1,0:T(8,128)S(1)} collective-permute-done((f32[264,128]{1,0:T(8,128)S(1)}, f32[264,128]{1,0:T(8,128)S(1)}, u32[]{:S(2)}, u32[]{:S(2)}) %collective-permute-start.1) | collective-permute-done | bytes 135200 | tf_op jit(solution)/shard_map/ppermute | solution.py:376
  13.0 0.1 slice_reduce_fusion
  13.2 1.3 %collective-permute-start.4 = (f32[2,256,128]{2,1,0:T(8,128)S(1)}, f32[2,256,128]{2,1,0:T(8,128)S(1)}, u32[]{:S(2)}, u32[]{:S(2)}) collective-permute-start(f32[2,256,128]{2,1,0:T(8,128)S(1)} %shard_map.96), channel_id=1, source_target_pairs={{8,0},{16,8},{24,16},{9,1},{17,9},{25,17},{10,2},{18,10},{26,18},{... | collective-permute-start | bytes 786440 | tf_op jit(solution)/shard_map/ppermute | solution.py:409
  14.5 1.6 %collective-permute-start.12 = (f32[256,256]{1,0:T(8,128)S(1)}, f32[256,256]{1,0:T(8,128)S(1)}, u32[]{:S(2)}, u32[]{:S(2)}) collective-permute-start(f32[256,256]{1,0:T(8,128)S(1)} %get-tuple-element.60), channel_id=1, source_target_pairs={{0,4},{4,0},{1,5},{5,1},{2,6},{6,2},{3,7},{7,3},{8,12},{12,8},{9,1... | collective-permute-start | bytes 786440 | tf_op jit(solution)/shard_map/ppermute | solution.py:410
  16.2 7.6 %collective-permute-done.4.refs_4_ = f32[2,256,128]{2,1,0:T(8,128)S(1)} collective-permute-done((f32[2,256,128]{2,1,0:T(8,128)S(1)}, f32[2,256,128]{2,1,0:T(8,128)S(1)}, u32[]{:S(2)}, u32[]{:S(2)}) %collective-permute-start.4) | collective-permute-done | bytes 262176 | tf_op jit(solution)/shard_map/ppermute | solution.py:409
  23.8 1.3 %shard_map.97 = (f32[256,128]{1,0:T(8,128)S(1)}, f32[256,128]{1,0:T(8,128)S(1)}, f32[256,128]{1,0:T(8,128)S(1)}, f32[256,128]{1,0:T(8,128)S(1)}, f32[256,128]{1,...) custom-call(s32[5,8]{1,0:T(8,128)S(1)} %concatenate.7.offs, ...), custom_call_target="tpu_custom_call" | custom-call | flops 2097152 | bytes 1851392 | tf_op jit(solution)/shard_map/pallas_call | solution.py:359
  25.2 1.2 %collective-permute-start.5 = (f32[256,128]{1,0:T(8,128)S(1)}, f32[256,128]{1,0:T(8,128)S(1)}, u32[]{:S(2)}, u32[]{:S(2)}) collective-permute-start(f32[256,128]{1,0:T(8,128)S(1)} %get-tuple-element.52), channel_id=1, source_target_pairs={{0,2},{1,3},{2,0},{3,1},{4,6},{5,7},{6,4},{7,5},{8,10},{9,11},{10,... | collective-permute-start | bytes 393224 | tf_op jit(solution)/shard_map/ppermute | solution.py:376
  26.4 0.9 %collective-permute-start.6 = (f32[256,128]{1,0:T(8,128)S(1)}, f32[256,128]{1,0:T(8,128)S(1)}, u32[]{:S(2)}, u32[]{:S(2)}) collective-permute-start(f32[256,128]{1,0:T(8,128)S(1)} %get-tuple-element.53), channel_id=1, source_target_pairs={{0,4},{1,5},{2,6},{3,7},{4,0},{5,1},{6,2},{7,3},{8,12},{9,13},{10,... | collective-permute-start | bytes 393224 | tf_op jit(solution)/shard_map/ppermute | solution.py:376
  27.3 0.2 collective-permute-start.7
  27.5 1.5 %collective-permute-start.8 = (f32[256,128]{1,0:T(8,128)S(1)}, f32[256,128]{1,0:T(8,128)S(1)}, u32[]{:S(2)}, u32[]{:S(2)}) collective-permute-start(f32[256,128]{1,0:T(8,128)S(1)} %get-tuple-element.55), channel_id=1, source_target_pairs={{0,5},{1,4},{2,7},{3,6},{4,1},{5,0},{6,3},{7,2},{8,13},{9,12},{10,... | collective-permute-start | bytes 393224 | tf_op jit(solution)/shard_map/ppermute | solution.py:376
  29.0 1.5 %collective-permute-start.9 = (f32[256,128]{1,0:T(8,128)S(1)}, f32[256,128]{1,0:T(8,128)S(1)}, u32[]{:S(2)}, u32[]{:S(2)}) collective-permute-start(f32[256,128]{1,0:T(8,128)S(1)} %get-tuple-element.56), channel_id=1, source_target_pairs={{0,6},{1,7},{2,4},{3,5},{4,2},{5,3},{6,0},{7,1},{8,14},{9,15},{10,... | collective-permute-start | bytes 393224 | tf_op jit(solution)/shard_map/ppermute | solution.py:376
  30.5 0.7 collective-permute-start.10
  31.2 1.0 %collective-permute-done.6.refs_1_ = f32[256,128]{1,0:T(8,128)S(1)} collective-permute-done((f32[256,128]{1,0:T(8,128)S(1)}, f32[256,128]{1,0:T(8,128)S(1)}, u32[]{:S(2)}, u32[]{:S(2)}) %collective-permute-start.6) | collective-permute-done | bytes 131104 | tf_op jit(solution)/shard_map/ppermute | solution.py:376
  32.2 2.5 %shard_map.98 = (f32[2,256,256]{2,1,0:T(8,128)S(1)}, f32[256,256]{1,0:T(8,128)S(1)}, bf16[6,512,256]{2,1,0:T(8,128)(2,1)S(1)}) custom-call(s32[5,8]{1,0:T(8,128)S(1)} %concatenate.7.offs, f32[256,256]{1,0:T(8,128)S(1)} %collective-permute-done.12.taken, f32[2,256,256]{2,1,0:T(8,128)} %probe_from.1, f32[1,2,256,256]{3,2,1,0:T(8,128)} %measured.3, ...), custom_call_target="tpu_custom_call" | custom-call | flops 201326592 | bytes 5505024 | tf_op jit(solution)/shard_map/pallas_call | solution.py:359
  34.7 3.5 %collective-permute-done.8.refs_3_ = f32[256,128]{1,0:T(8,128)S(1)} collective-permute-done((f32[256,128]{1,0:T(8,128)S(1)}, f32[256,128]{1,0:T(8,128)S(1)}, u32[]{:S(2)}, u32[]{:S(2)}) %collective-permute-start.8) | collective-permute-done | bytes 131104 | tf_op jit(solution)/shard_map/ppermute | solution.py:376
  38.3 1.0 %collective-permute-done.10.refs_5_ = f32[256,128]{1,0:T(8,128)S(1)} collective-permute-done((f32[256,128]{1,0:T(8,128)S(1)}, f32[256,128]{1,0:T(8,128)S(1)}, u32[]{:S(2)}, u32[]{:S(2)}) %collective-permute-start.10) | collective-permute-done | bytes 131104 | tf_op jit(solution)/shard_map/ppermute | solution.py:376
  39.3 4.2 %shard_map.99 = (f32[768,128]{1,0:T(8,128)S(1)}, f32[256,128]{1,0:T(8,128)S(1)}, f32[256,128]{1,0:T(8,128)S(1)}, f32[256,128]{1,0:T(8,128)S(1)}, f32[256,128]{1,...) custom-call(s32[5,8]{1,0:T(8,128)S(1)} %concatenate.7.offs, ...), custom_call_target="tpu_custom_call" | custom-call | flops 1610612736 | bytes 5120000 | tf_op jit(solution)/shard_map/pallas_call | solution.py:359
  43.5 0.4 collective-permute-start.13
  43.9 1.0 %collective-permute-start.14 = (f32[256,128]{1,0:T(8,128)S(1)}, f32[256,128]{1,0:T(8,128)S(1)}, u32[]{:S(2)}, u32[]{:S(2)}) collective-permute-start(f32[256,128]{1,0:T(8,128)S(1)} %get-tuple-element.65), channel_id=1, source_target_pairs={{0,4},{1,5},{2,6},{3,7},{4,0},{5,1},{6,2},{7,3},{8,12},{9,13},{10,... | collective-permute-start | bytes 393224 | tf_op jit(solution)/shard_map/ppermute | solution.py:376
  44.8 1.5 %collective-permute-start.15 = (f32[256,128]{1,0:T(8,128)S(1)}, f32[256,128]{1,0:T(8,128)S(1)}, u32[]{:S(2)}, u32[]{:S(2)}) collective-permute-start(f32[256,128]{1,0:T(8,128)S(1)} %get-tuple-element.66), channel_id=1, source_target_pairs={{0,2},{1,3},{2,0},{3,1},{4,6},{5,7},{6,4},{7,5},{8,10},{9,11},{10,... | collective-permute-start | bytes 393224 | tf_op jit(solution)/shard_map/ppermute | solution.py:376
  46.3 1.3 %collective-permute-start.17 = (f32[256,128]{1,0:T(8,128)S(1)}, f32[256,128]{1,0:T(8,128)S(1)}, u32[]{:S(2)}, u32[]{:S(2)}) collective-permute-start(f32[256,128]{1,0:T(8,128)S(1)} %get-tuple-element.68), channel_id=1, source_target_pairs={{0,3},{1,2},{2,1},{3,0},{4,7},{5,6},{6,5},{7,4},{8,11},{9,10},{10,... | collective-permute-start | bytes 393224 | tf_op jit(solution)/shard_map/ppermute | solution.py:376
  47.6 1.9 %collective-permute-done.14.refs_1_ = f32[256,128]{1,0:T(8,128)S(1)} collective-permute-done((f32[256,128]{1,0:T(8,128)S(1)}, f32[256,128]{1,0:T(8,128)S(1)}, u32[]{:S(2)}, u32[]{:S(2)}) %collective-permute-start.14) | collective-permute-done | bytes 131104 | tf_op jit(solution)/shard_map/ppermute | solution.py:376
  49.5 2.5 %collective-permute-start.18 = (f32[256,128]{1,0:T(8,128)S(1)}, f32[256,128]{1,0:T(8,128)S(1)}, u32[]{:S(2)}, u32[]{:S(2)}) collective-permute-start(f32[256,128]{1,0:T(8,128)S(1)} %get-tuple-element.69), channel_id=1, source_target_pairs={{0,6},{1,7},{2,4},{3,5},{4,2},{5,3},{6,0},{7,1},{8,14},{9,15},{10,... | collective-permute-start | bytes 393224 | tf_op jit(solution)/shard_map/ppermute | solution.py:376
  52.1 0.6 collective-permute-start.20
  52.7 0.7 collective-permute-start.21
  53.4 2.3 %collective-permute-start.22 = (f32[128,128]{1,0:T(8,128)S(1)}, f32[128,128]{1,0:T(8,128)S(1)}, u32[]{:S(2)}, u32[]{:S(2)}) collective-permute-start(f32[128,128]{1,0:T(8,128)S(1)} %get-tuple-element.75), channel_id=1, source_target_pairs={{0,6},{2,4},{4,2},{6,0},{1,7},{3,5},{5,3},{7,1},{8,14},{10,12},{12... | collective-permute-start | bytes 196616 | tf_op jit(solution)/shard_map/ppermute | solution.py:376
  55.7 0.9 collective-permute-done.18.refs_5_
  56.6 2.4 %collective-permute-done.19.refs_6_ = f32[256,128]{1,0:T(8,128)S(1)} collective-permute-done((f32[256,128]{1,0:T(8,128)S(1)}, f32[256,128]{1,0:T(8,128)S(1)}, u32[]{:S(2)}, u32[]{:S(2)}) %collective-permute-start.19) | collective-permute-done | bytes 131104 | tf_op jit(solution)/shard_map/ppermute | solution.py:376
  58.9 1.7 %collective-permute-done.20.refs_8_ = f32[128,128]{1,0:T(8,128)S(1)} collective-permute-done((f32[128,128]{1,0:T(8,128)S(1)}, f32[128,128]{1,0:T(8,128)S(1)}, u32[]{:S(2)}, u32[]{:S(2)}) %collective-permute-start.20) | collective-permute-done | bytes 65568 | tf_op jit(solution)/shard_map/ppermute | solution.py:376
  60.6 1.3 %collective-permute-done.22.refs_10_ = f32[128,128]{1,0:T(8,128)S(1)} collective-permute-done((f32[128,128]{1,0:T(8,128)S(1)}, f32[128,128]{1,0:T(8,128)S(1)}, u32[]{:S(2)}, u32[]{:S(2)}) %collective-permute-start.22) | collective-permute-done | bytes 65568 | tf_op jit(solution)/shard_map/ppermute | solution.py:376
  61.9 1.0 %shard_map.102 = (f32[2,256,128]{2,1,0:T(8,128)S(1)}, f32[64,256]{1,0:T(8,128)S(1)}) custom-call(s32[5,8]{1,0:T(8,128)S(1)} %concatenate.7.offs, f32[768,128]{1,0:T(8,128)S(1)} %collective-permute-done.13.refs_0_.got, f32[256,128]{1,0:T(8,128)S(1)} %collective-permute-done.14.refs_1_, f32[256,128]{1,0:T(8,128)S(1)} %collective-permute-done.15.refs_2_, ...), custom_call_target="tpu_custom_call" | custom-call | flops 2097152 | bytes 1900544 | tf_op jit(solution)/shard_map/pallas_call | solution.py:359
  62.9 3.5 %collective-permute-start.23 = (f32[2,256,128]{2,1,0:T(8,128)S(1)}, f32[2,256,128]{2,1,0:T(8,128)S(1)}, u32[]{:S(2)}, u32[]{:S(2)}) collective-permute-start(f32[2,256,128]{2,1,0:T(8,128)S(1)} %get-tuple-element.77), channel_id=1, source_target_pairs={{0,8},{8,16},{16,24},{1,9},{9,17},{17,25},{2,10},{10,18},{18,26},{... | collective-permute-start | bytes 786440 | tf_op jit(solution)/shard_map/ppermute | solution.py:454
  66.4 1.6 %collective-permute-start.24 = (f32[64,256]{1,0:T(8,128)S(1)}, f32[64,256]{1,0:T(8,128)S(1)}, u32[]{:S(2)}, u32[]{:S(2)}) collective-permute-start(f32[64,256]{1,0:T(8,128)S(1)} %get-tuple-element.82), channel_id=1, source_target_pairs={{0,8},{8,0},{16,24},{24,16},{1,9},{9,1},{17,25},{25,17},{2,10},{10... | collective-permute-start | bytes 196616 | tf_op jit(solution)/shard_map/ppermute | solution.py:457
  68.1 1.5 %shard_map.100.own = f32[4,256,128]{2,1,0:T(8,128)S(1)} custom-call(s32[5,8]{1,0:T(8,128)S(1)} %concatenate.7.offs, f32[768,128]{1,0:T(8,128)S(1)} %collective-permute-done.13.refs_0_.got, f32[256,128]{1,0:T(8,128)S(1)} %collective-permute-done.14.refs_1_, f32[256,128]{1,0:T(8,128)S(1)} %collective-permute-done.15.refs_2_, ...), custom_call_target="tpu_custom_call" | custom-call | flops 4194304 | bytes 1835008 | tf_op jit(solution)/shard_map/pallas_call | solution.py:359
  69.6 3.2 %collective-permute-done.23.above = f32[2,256,128]{2,1,0:T(8,128)S(1)} collective-permute-done((f32[2,256,128]{2,1,0:T(8,128)S(1)}, f32[2,256,128]{2,1,0:T(8,128)S(1)}, u32[]{:S(2)}, u32[]{:S(2)}) %collective-permute-start.23) | collective-permute-done | bytes 262176 | tf_op jit(solution)/shard_map/ppermute | solution.py:454
  72.8 0.6 collective-permute-done.24
  73.5 2.2 %collective-permute-start.28 = (f32[64,256]{1,0:T(8,128)S(1)}, f32[64,256]{1,0:T(8,128)S(1)}, u32[]{:S(2)}, u32[]{:S(2)}) collective-permute-start(f32[64,256]{1,0:T(8,128)S(1)} %add.8), channel_id=1, source_target_pairs={{0,16},{8,24},{16,0},{24,8},{1,17},{9,25},{17,1},{25,9},{2,18},{10... | collective-permute-start | bytes 196616 | tf_op jit(solution)/shard_map/ppermute | solution.py:384
  75.7 0.4 collective-permute-start.25
  76.1 1.3 %collective-permute-start.26 = (f32[256,128]{1,0:T(8,128)S(1)}, f32[256,128]{1,0:T(8,128)S(1)}, u32[]{:S(2)}, u32[]{:S(2)}) collective-permute-start(f32[256,128]{1,0:T(8,128)S(1)} %get-tuple-element.84), channel_id=1, source_target_pairs={{0,2},{2,0},{4,6},{6,4},{1,3},{3,1},{5,7},{7,5},{8,10},{10,8},{12,... | collective-permute-start | bytes 393224 | tf_op jit(solution)/shard_map/ppermute | solution.py:376
  77.4 1.8 %collective-permute-start.27 = (f32[256,128]{1,0:T(8,128)S(1)}, f32[256,128]{1,0:T(8,128)S(1)}, u32[]{:S(2)}, u32[]{:S(2)}) collective-permute-start(f32[256,128]{1,0:T(8,128)S(1)} %get-tuple-element.85), channel_id=1, source_target_pairs={{0,6},{2,4},{4,2},{6,0},{1,7},{3,5},{5,3},{7,1},{8,14},{10,12},{12... | collective-permute-start | bytes 393224 | tf_op jit(solution)/shard_map/ppermute | solution.py:376
  79.1 0.2 collective-permute-done.28
  79.4 8.8 %all_gather.3.refs_4_ = f32[512,256]{1,0:T(8,128)S(1)} all-gather(f32[64,256]{1,0:T(8,128)S(1)} %add.9), channel_id=1, replica_groups=mesh['pair'=4,'half'=2,'col'=2,'core'=2] {'half','col','core'}, dimensions={0}, use_global_device_ids=true | all-gather | bytes 589824 | tf_op jit(solution)/shard_map/all_gather | solution.py:466
  88.2 1.0 %shard_map.104 = (f32[4,256,128]{2,1,0:T(8,128)}, f32[512,256]{1,0:T(8,128)}) custom-call(f32[256,128]{1,0:T(8,128)S(1)} %collective-permute-done.25.refs_0_, f32[256,128]{1,0:T(8,128)S(1)} %collective-permute-done.26.refs_1_, f32[256,128]{1,0:T(8,128)S(1)} %collective-permute-done.27.refs_2_, f32[256,128]{1,0:T(8,128)S(1)} %get-tuple-element.86.refs_3_, ...), custom_call_target="tpu_custom_call" | custom-call | bytes 2097152 | tf_op jit(solution)/shard_map/pallas_call | solution.py:359
  (34 shorter events, 0.6 us)
Async XLA Ops:
  1.9 7.3 %collective-permute-start = (f32[264,128]{1,0:T(8,128)S(1)}, f32[264,128]{1,0:T(8,128)S(1)}, u32[]{:S(2)}, u32[]{:S(2)}) collective-permute-start(f32[264,128]{1,0:T(8,128)S(1)} %get-tuple-element.47), channel_id=1, source_target_pairs={{0,2},{2,0},{4,6},{6,4},{1,3},{3,1},{5,7},{7,5},{8,10},{10,8},{12,... | collective-permute-start | bytes 405512 | tf_op jit(solution)/shard_map/ppermute | solution.py:376
  4.9 7.9 %collective-permute-start.1 = (f32[264,128]{1,0:T(8,128)S(1)}, f32[264,128]{1,0:T(8,128)S(1)}, u32[]{:S(2)}, u32[]{:S(2)}) collective-permute-start(f32[264,128]{1,0:T(8,128)S(1)} %get-tuple-element.48), channel_id=1, source_target_pairs={{0,4},{2,6},{4,0},{6,2},{1,5},{3,7},{5,1},{7,3},{8,12},{10,14},{12... | collective-permute-start | bytes 405512 | tf_op jit(solution)/shard_map/ppermute | solution.py:376
  6.4 6.5 %collective-permute-start.2 = (f32[264,128]{1,0:T(8,128)S(1)}, f32[264,128]{1,0:T(8,128)S(1)}, u32[]{:S(2)}, u32[]{:S(2)}) collective-permute-start(f32[264,128]{1,0:T(8,128)S(1)} %get-tuple-element.49), channel_id=1, source_target_pairs={{0,6},{2,4},{4,2},{6,0},{1,7},{3,5},{5,3},{7,1},{8,14},{10,12},{12... | collective-permute-start | bytes 405512 | tf_op jit(solution)/shard_map/ppermute | solution.py:376
  13.1 3.0 %collective-permute-start.3 = (s32[4,4]{1,0:T(4,128)S(1)}, s32[4,4]{1,0:T(4,128)S(1)}, u32[]{:S(2)}, u32[]{:S(2)}) collective-permute-start(s32[4,4]{1,0:T(4,128)S(1)} %maximum_convert_fusion), channel_id=1, source_target_pairs={{0,1},{1,0},{2,3},{3,2},{4,5},{5,4},{6,7},{7,6},{8,9},{9,8},{10,11... | collective-permute-start | bytes 200 | tf_op jit(solution)/shard_map/ppermute | solution.py:414
  13.2 10.6 %collective-permute-start.4 = (f32[2,256,128]{2,1,0:T(8,128)S(1)}, f32[2,256,128]{2,1,0:T(8,128)S(1)}, u32[]{:S(2)}, u32[]{:S(2)}) collective-permute-start(f32[2,256,128]{2,1,0:T(8,128)S(1)} %shard_map.96), channel_id=1, source_target_pairs={{8,0},{16,8},{24,16},{9,1},{17,9},{25,17},{10,2},{18,10},{26,18},{... | collective-permute-start | bytes 786440 | tf_op jit(solution)/shard_map/ppermute | solution.py:409
  14.5 14.5 %collective-permute-start.12 = (f32[256,256]{1,0:T(8,128)S(1)}, f32[256,256]{1,0:T(8,128)S(1)}, u32[]{:S(2)}, u32[]{:S(2)}) collective-permute-start(f32[256,256]{1,0:T(8,128)S(1)} %get-tuple-element.60), channel_id=1, source_target_pairs={{0,4},{4,0},{1,5},{5,1},{2,6},{6,2},{3,7},{7,3},{8,12},{12,8},{9,1... | collective-permute-start | bytes 786440 | tf_op jit(solution)/shard_map/ppermute | solution.py:410
  25.2 5.3 %collective-permute-start.5 = (f32[256,128]{1,0:T(8,128)S(1)}, f32[256,128]{1,0:T(8,128)S(1)}, u32[]{:S(2)}, u32[]{:S(2)}) collective-permute-start(f32[256,128]{1,0:T(8,128)S(1)} %get-tuple-element.52), channel_id=1, source_target_pairs={{0,2},{1,3},{2,0},{3,1},{4,6},{5,7},{6,4},{7,5},{8,10},{9,11},{10,... | collective-permute-start | bytes 393224 | tf_op jit(solution)/shard_map/ppermute | solution.py:376
  26.4 5.8 %collective-permute-start.6 = (f32[256,128]{1,0:T(8,128)S(1)}, f32[256,128]{1,0:T(8,128)S(1)}, u32[]{:S(2)}, u32[]{:S(2)}) collective-permute-start(f32[256,128]{1,0:T(8,128)S(1)} %get-tuple-element.53), channel_id=1, source_target_pairs={{0,4},{1,5},{2,6},{3,7},{4,0},{5,1},{6,2},{7,3},{8,12},{9,13},{10,... | collective-permute-start | bytes 393224 | tf_op jit(solution)/shard_map/ppermute | solution.py:376
  27.3 7.4 %collective-permute-start.7 = (f32[256,128]{1,0:T(8,128)S(1)}, f32[256,128]{1,0:T(8,128)S(1)}, u32[]{:S(2)}, u32[]{:S(2)}) collective-permute-start(f32[256,128]{1,0:T(8,128)S(1)} %get-tuple-element.54), channel_id=1, source_target_pairs={{0,3},{1,2},{2,1},{3,0},{4,7},{5,6},{6,5},{7,4},{8,11},{9,10},{10,... | collective-permute-start | bytes 393224 | tf_op jit(solution)/shard_map/ppermute | solution.py:376
  27.5 10.7 %collective-permute-start.8 = (f32[256,128]{1,0:T(8,128)S(1)}, f32[256,128]{1,0:T(8,128)S(1)}, u32[]{:S(2)}, u32[]{:S(2)}) collective-permute-start(f32[256,128]{1,0:T(8,128)S(1)} %get-tuple-element.55), channel_id=1, source_target_pairs={{0,5},{1,4},{2,7},{3,6},{4,1},{5,0},{6,3},{7,2},{8,13},{9,12},{10,... | collective-permute-start | bytes 393224 | tf_op jit(solution)/shard_map/ppermute | solution.py:376
  29.0 9.2 %collective-permute-start.9 = (f32[256,128]{1,0:T(8,128)S(1)}, f32[256,128]{1,0:T(8,128)S(1)}, u32[]{:S(2)}, u32[]{:S(2)}) collective-permute-start(f32[256,128]{1,0:T(8,128)S(1)} %get-tuple-element.56), channel_id=1, source_target_pairs={{0,6},{1,7},{2,4},{3,5},{4,2},{5,3},{6,0},{7,1},{8,14},{9,15},{10,... | collective-permute-start | bytes 393224 | tf_op jit(solution)/shard_map/ppermute | solution.py:376
  30.5 8.7 %collective-permute-start.10 = (f32[256,128]{1,0:T(8,128)S(1)}, f32[256,128]{1,0:T(8,128)S(1)}, u32[]{:S(2)}, u32[]{:S(2)}) collective-permute-start(f32[256,128]{1,0:T(8,128)S(1)} %get-tuple-element.57), channel_id=1, source_target_pairs={{0,7},{1,6},{2,5},{3,4},{4,3},{5,2},{6,1},{7,0},{8,15},{9,14},{10,... | collective-permute-start | bytes 393224 | tf_op jit(solution)/shard_map/ppermute | solution.py:376
  32.2 7.1 %copy-start = (f32[2,136,128]{2,1,0:T(8,128)S(1)}, f32[2,136,128]{2,1,0:T(8,128)}, u32[]{:S(2)}) copy-start(f32[2,136,128]{2,1,0:T(8,128)} %constant.17.clone.refs_11_) | copy-start | bytes 417796
  32.2 7.1 %collective-permute-start.11 = (f32[256,128]{1,0:T(8,128)S(1)}, f32[256,128]{1,0:T(8,128)S(1)}, u32[]{:S(2)}, u32[]{:S(2)}) collective-permute-start(f32[256,128]{1,0:T(8,128)S(1)} %get-tuple-element.58), channel_id=1, source_target_pairs={{0,1},{1,0},{2,3},{3,2},{4,5},{5,4},{6,7},{7,6},{8,9},{9,8},{10,11... | collective-permute-start | bytes 393224 | tf_op jit(solution)/shard_map/ppermute | solution.py:376
  43.5 8.6 %collective-permute-start.13 = (f32[768,128]{1,0:T(8,128)S(1)}, f32[768,128]{1,0:T(8,128)S(1)}, u32[]{:S(2)}, u32[]{:S(2)}) collective-permute-start(f32[768,128]{1,0:T(8,128)S(1)} %get-tuple-element.64), channel_id=1, source_target_pairs={{0,1},{1,0},{2,3},{3,2},{4,5},{5,4},{6,7},{7,6},{8,9},{9,8},{10,11... | collective-permute-start | bytes 1179656 | tf_op jit(solution)/shard_map/ppermute | solution.py:376
  43.9 5.7 %collective-permute-start.14 = (f32[256,128]{1,0:T(8,128)S(1)}, f32[256,128]{1,0:T(8,128)S(1)}, u32[]{:S(2)}, u32[]{:S(2)}) collective-permute-start(f32[256,128]{1,0:T(8,128)S(1)} %get-tuple-element.65), channel_id=1, source_target_pairs={{0,4},{1,5},{2,6},{3,7},{4,0},{5,1},{6,2},{7,3},{8,12},{9,13},{10,... | collective-permute-start | bytes 393224 | tf_op jit(solution)/shard_map/ppermute | solution.py:376
  44.8 7.3 %collective-permute-start.15 = (f32[256,128]{1,0:T(8,128)S(1)}, f32[256,128]{1,0:T(8,128)S(1)}, u32[]{:S(2)}, u32[]{:S(2)}) collective-permute-start(f32[256,128]{1,0:T(8,128)S(1)} %get-tuple-element.66), channel_id=1, source_target_pairs={{0,2},{1,3},{2,0},{3,1},{4,6},{5,7},{6,4},{7,5},{8,10},{9,11},{10,... | collective-permute-start | bytes 393224 | tf_op jit(solution)/shard_map/ppermute | solution.py:376
  46.3 6.4 %collective-permute-start.16 = (f32[256,128]{1,0:T(8,128)S(1)}, f32[256,128]{1,0:T(8,128)S(1)}, u32[]{:S(2)}, u32[]{:S(2)}) collective-permute-start(f32[256,128]{1,0:T(8,128)S(1)} %get-tuple-element.67), channel_id=1, source_target_pairs={{0,5},{1,4},{2,7},{3,6},{4,1},{5,0},{6,3},{7,2},{8,13},{9,12},{10,... | collective-permute-start | bytes 393224 | tf_op jit(solution)/shard_map/ppermute | solution.py:376
  46.3 7.1 %collective-permute-start.17 = (f32[256,128]{1,0:T(8,128)S(1)}, f32[256,128]{1,0:T(8,128)S(1)}, u32[]{:S(2)}, u32[]{:S(2)}) collective-permute-start(f32[256,128]{1,0:T(8,128)S(1)} %get-tuple-element.68), channel_id=1, source_target_pairs={{0,3},{1,2},{2,1},{3,0},{4,7},{5,6},{6,5},{7,4},{8,11},{9,10},{10,... | collective-permute-start | bytes 393224 | tf_op jit(solution)/shard_map/ppermute | solution.py:376
  49.5 7.0 %collective-permute-start.18 = (f32[256,128]{1,0:T(8,128)S(1)}, f32[256,128]{1,0:T(8,128)S(1)}, u32[]{:S(2)}, u32[]{:S(2)}) collective-permute-start(f32[256,128]{1,0:T(8,128)S(1)} %get-tuple-element.69), channel_id=1, source_target_pairs={{0,6},{1,7},{2,4},{3,5},{4,2},{5,3},{6,0},{7,1},{8,14},{9,15},{10,... | collective-permute-start | bytes 393224 | tf_op jit(solution)/shard_map/ppermute | solution.py:376
  52.1 6.9 %collective-permute-start.19 = (f32[256,128]{1,0:T(8,128)S(1)}, f32[256,128]{1,0:T(8,128)S(1)}, u32[]{:S(2)}, u32[]{:S(2)}) collective-permute-start(f32[256,128]{1,0:T(8,128)S(1)} %get-tuple-element.70), channel_id=1, source_target_pairs={{0,7},{1,6},{2,5},{3,4},{4,3},{5,2},{6,1},{7,0},{8,15},{9,14},{10,... | collective-permute-start | bytes 393224 | tf_op jit(solution)/shard_map/ppermute | solution.py:376
  52.1 8.5 %collective-permute-start.20 = (f32[128,128]{1,0:T(8,128)S(1)}, f32[128,128]{1,0:T(8,128)S(1)}, u32[]{:S(2)}, u32[]{:S(2)}) collective-permute-start(f32[128,128]{1,0:T(8,128)S(1)} %get-tuple-element.73), channel_id=1, source_target_pairs={{0,4},{2,6},{4,0},{6,2},{1,5},{3,7},{5,1},{7,3},{8,12},{10,14},{12... | collective-permute-start | bytes 196616 | tf_op jit(solution)/shard_map/ppermute | solution.py:376
  52.7 7.9 %collective-permute-start.21 = (f32[128,128]{1,0:T(8,128)S(1)}, f32[128,128]{1,0:T(8,128)S(1)}, u32[]{:S(2)}, u32[]{:S(2)}) collective-permute-start(f32[128,128]{1,0:T(8,128)S(1)} %get-tuple-element.74), channel_id=1, source_target_pairs={{0,2},{2,0},{4,6},{6,4},{1,3},{3,1},{5,7},{7,5},{8,10},{10,8},{12,... | collective-permute-start | bytes 196616 | tf_op jit(solution)/shard_map/ppermute | solution.py:376
  53.4 8.5 %collective-permute-start.22 = (f32[128,128]{1,0:T(8,128)S(1)}, f32[128,128]{1,0:T(8,128)S(1)}, u32[]{:S(2)}, u32[]{:S(2)}) collective-permute-start(f32[128,128]{1,0:T(8,128)S(1)} %get-tuple-element.75), channel_id=1, source_target_pairs={{0,6},{2,4},{4,2},{6,0},{1,7},{3,5},{5,3},{7,1},{8,14},{10,12},{12... | collective-permute-start | bytes 196616 | tf_op jit(solution)/shard_map/ppermute | solution.py:376
  62.9 9.8 %collective-permute-start.23 = (f32[2,256,128]{2,1,0:T(8,128)S(1)}, f32[2,256,128]{2,1,0:T(8,128)S(1)}, u32[]{:S(2)}, u32[]{:S(2)}) collective-permute-start(f32[2,256,128]{2,1,0:T(8,128)S(1)} %get-tuple-element.77), channel_id=1, source_target_pairs={{0,8},{8,16},{16,24},{1,9},{9,17},{17,25},{2,10},{10,18},{18,26},{... | collective-permute-start | bytes 786440 | tf_op jit(solution)/shard_map/ppermute | solution.py:454
  66.4 7.0 %collective-permute-start.24 = (f32[64,256]{1,0:T(8,128)S(1)}, f32[64,256]{1,0:T(8,128)S(1)}, u32[]{:S(2)}, u32[]{:S(2)}) collective-permute-start(f32[64,256]{1,0:T(8,128)S(1)} %get-tuple-element.82), channel_id=1, source_target_pairs={{0,8},{8,0},{16,24},{24,16},{1,9},{9,1},{17,25},{25,17},{2,10},{10... | collective-permute-start | bytes 196616 | tf_op jit(solution)/shard_map/ppermute | solution.py:457
  73.5 5.9 %collective-permute-start.28 = (f32[64,256]{1,0:T(8,128)S(1)}, f32[64,256]{1,0:T(8,128)S(1)}, u32[]{:S(2)}, u32[]{:S(2)}) collective-permute-start(f32[64,256]{1,0:T(8,128)S(1)} %add.8), channel_id=1, source_target_pairs={{0,16},{8,24},{16,0},{24,8},{1,17},{9,25},{17,1},{25,9},{2,18},{10... | collective-permute-start | bytes 196616 | tf_op jit(solution)/shard_map/ppermute | solution.py:384
  75.7 12.5 %collective-permute-start.25 = (f32[256,128]{1,0:T(8,128)S(1)}, f32[256,128]{1,0:T(8,128)S(1)}, u32[]{:S(2)}, u32[]{:S(2)}) collective-permute-start(f32[256,128]{1,0:T(8,128)S(1)} %get-tuple-element.83), channel_id=1, source_target_pairs={{0,4},{2,6},{4,0},{6,2},{1,5},{3,7},{5,1},{7,3},{8,12},{10,14},{12... | collective-permute-start | bytes 393224 | tf_op jit(solution)/shard_map/ppermute | solution.py:376
  76.1 12.1 %collective-permute-start.26 = (f32[256,128]{1,0:T(8,128)S(1)}, f32[256,128]{1,0:T(8,128)S(1)}, u32[]{:S(2)}, u32[]{:S(2)}) collective-permute-start(f32[256,128]{1,0:T(8,128)S(1)} %get-tuple-element.84), channel_id=1, source_target_pairs={{0,2},{2,0},{4,6},{6,4},{1,3},{3,1},{5,7},{7,5},{8,10},{10,8},{12,... | collective-permute-start | bytes 393224 | tf_op jit(solution)/shard_map/ppermute | solution.py:376
  77.4 10.8 %collective-permute-start.27 = (f32[256,128]{1,0:T(8,128)S(1)}, f32[256,128]{1,0:T(8,128)S(1)}, u32[]{:S(2)}, u32[]{:S(2)}) collective-permute-start(f32[256,128]{1,0:T(8,128)S(1)} %get-tuple-element.85), channel_id=1, source_target_pairs={{0,6},{2,4},{4,2},{6,0},{1,7},{3,5},{5,3},{7,1},{8,14},{10,12},{12... | collective-permute-start | bytes 393224 | tf_op jit(solution)/shard_map/ppermute | solution.py:376

commit v20 on v19

--- a/solution.py
+++ b/solution.py
@@ -12,7 +12,7 @@
 
 GRAD_WEIGHT = 0.0625
 PLANE = ("half", "col", "core")
-EIGHT, BACK, FOUR = (2, 4, 3, 5, 6, 7, 1, 0), (1, 4, 2, 5, 3, 6, 7, 0), (2, 1, 3, 0)
+EIGHT, BACK, FOUR = (1, 2, 4, 3, 5, 6, 7, 0), (1, 4, 2, 5, 3, 6, 7, 0), (2, 1, 3, 0)
 VMEM_LIMIT = 24 * 1024 * 1024
 
 
@@ -372,8 +372,9 @@
 
 
 def deal(values, axes, order):
+    count = math.prod(lax.axis_size(axis) for axis in axes)
     return [
-        lax.ppermute(value, axes, [(k, k ^ turn) for k in range(len(order))]) if turn else value
+        lax.ppermute(value, axes, [(k, k ^ turn) for k in range(count)]) if turn else value
         for turn, value in zip(order, values)
     ]
 
@@ -442,8 +443,11 @@
         8 * 12 * width**3,
         [(8, rows, cols)] * 2 + [(8, 2 * band, cols)],
     )
-    got = deal(grad, PLANE, BACK)
-    quarters = call(pair_kernel, [shape(2 * band, cols)] * 4, (), (keep, got[0]), 4 * band * width)
+    first = deal(grad[:1], PLANE, BACK)
+    quarters = list(call(pair_kernel, [shape(2 * band, cols)] * 4, (), (keep, first[0]), 4 * band * width))
+    far = BACK.index(6)
+    grad[far], quarters[0] = lax.optimization_barrier((grad[far], quarters[0]))
+    got = first + deal(grad[1:], PLANE, BACK[1:])
     lower_sums, probe_band = call(
         add_below_kernel,
         [shape(2, rows, cols), shape(band, width)],

time: 89.5 us -> 89.6 us (level)
    ppermute x1, waiting for transfers between devices: 3.18 us -> 2.17 us  [local(): lax.ppermute(lower_sums, 'pair', [(k, k + 1) for k in range(pairs - 1)])]
  transfers between devices with their start and end apart: 29 -> 29, of which waited for: 13 -> 12; matrix products, arithmetic and copies ran while one was open for 2% -> 2% of each run, Pallas kernels for 6% -> 6%
where the time goes in v20:
time: 89.6 us; the launch traced here: 89.3 us
  starting transfers between devices  34.7 us (39%)
  waiting for transfers between devices  28.4 us (32%)
  Pallas kernels  13 us (15%)
  blocking collectives  9.28 us (10%)
  between operations  2.07 us (2%)
  local copies, waits for them, and re-layouts  1.79 us (2%)
    ppermute x23, starting transfers between devices, deal(): lax.ppermute(value, axes, [(k, k ^ turn) for k in range(count)])  24.3 us
    ppermute x23, waiting for transfers between devices, deal(): lax.ppermute(value, axes, [(k, k ^ turn) for k in range(count)])  18 us
    pallas_call x10, Pallas kernels, call(): pl.pallas_call(kernel, out_shape=[x for x, unused in outs], in_specs=[SME...  13 us
    all_gather x1, blocking collectives, local(): probe_grad = lax.all_gather(probe_band, PLANE, axis=0, tiled=True)  9.28 us
    ppermute x1, waiting for transfers between devices, local(): below = lax.ppermute(lowest, 'pair', [(k, k - 1) for k in range(1, pairs)])  7.61 us
    ppermute x1, starting transfers between devices, local(): lax.ppermute(lower_sums, 'pair', [(k, k + 1) for k in range(pairs - 1)])  3.5 us
    ppermute x1, starting transfers between devices, sum_over(): lax.ppermute(value, axis, [(k, k ^ step) for k in range(size)])  2.23 us
    ppermute x1, waiting for transfers between devices, local(): lax.ppermute(lower_sums, 'pair', [(k, k + 1) for k in range(pairs - 1)])  2.17 us
  transfers between devices with their start and end apart: 29, of which 12 were waited for; matrix products, arithmetic and copies ran while one was open for 2% of the time, Pallas kernels for 6%

profile of v20, /device:TPU:0, one launch (start us, length us, event | category | flops | bytes accessed | tf_op | source)
XLA Modules:
  0.0 89.3 jit_solution(12678008747263191484)
XLA Ops:
  0.6 1.3 %shard_map.95 = (f32[264,128]{1,0:T(8,128)S(1)}, f32[264,128]{1,0:T(8,128)S(1)}, f32[264,128]{1,0:T(8,128)S(1)}, f32[264,128]{1,0:T(8,128)S(1)}, f32[256,256]{1,0:T(8,128)S(1)}) custom-call(f32[4,256,128]{2,1,0:T(8,128)} %bitcast.9, f32[1,2,256,256]{3,2,1,0:T(8,128)} %measured.3, s32[1,2,2]{2,1,0:T(2,128)} %offsets_from.1), custom_call_target="tpu_custom_call" | custom-call | bytes 1851408 | tf_op jit(solution)/shard_map/pallas_call | solution.py:359
  1.9 3.0 %collective-permute-start = (f32[264,128]{1,0:T(8,128)S(1)}, f32[264,128]{1,0:T(8,128)S(1)}, u32[]{:S(2)}, u32[]{:S(2)}) collective-permute-start(f32[264,128]{1,0:T(8,128)S(1)} %get-tuple-element.49), channel_id=1, source_target_pairs={{0,2},{2,0},{4,6},{6,4},{1,3},{3,1},{5,7},{7,5},{8,10},{10,8},{12,... | collective-permute-start | bytes 405512 | tf_op jit(solution)/shard_map/ppermute | solution.py:377
  4.9 1.5 %collective-permute-start.1 = (f32[264,128]{1,0:T(8,128)S(1)}, f32[264,128]{1,0:T(8,128)S(1)}, u32[]{:S(2)}, u32[]{:S(2)}) collective-permute-start(f32[264,128]{1,0:T(8,128)S(1)} %get-tuple-element.50), channel_id=1, source_target_pairs={{0,4},{2,6},{4,0},{6,2},{1,5},{3,7},{5,1},{7,3},{8,12},{10,14},{12... | collective-permute-start | bytes 405512 | tf_op jit(solution)/shard_map/ppermute | solution.py:377
  6.6 1.3 %fusion = (s32[1,1]{1,0:T(1,128)}, s32[1,1]{1,0:T(1,128)}) fusion(s32[1,2]{1,0:T(1,128)} %param.11), kind=kLoop, calls=%fused_computation.8 | loop fusion | bytes 16 | tf_op jit(solution)/shard_map/slice | solution.py:417
  9.2 0.1 slice_reduce_fusion.2
  9.3 3.5 %collective-permute-done.1.refs_0_ = f32[264,128]{1,0:T(8,128)S(1)} collective-permute-done((f32[264,128]{1,0:T(8,128)S(1)}, f32[264,128]{1,0:T(8,128)S(1)}, u32[]{:S(2)}, u32[]{:S(2)}) %collective-permute-start.1) | collective-permute-done | bytes 135200 | tf_op jit(solution)/shard_map/ppermute | solution.py:377
  13.0 0.1 slice_reduce_fusion
  13.2 1.3 %collective-permute-start.4 = (f32[2,256,128]{2,1,0:T(8,128)S(1)}, f32[2,256,128]{2,1,0:T(8,128)S(1)}, u32[]{:S(2)}, u32[]{:S(2)}) collective-permute-start(f32[2,256,128]{2,1,0:T(8,128)S(1)} %shard_map.96), channel_id=1, source_target_pairs={{8,0},{16,8},{24,16},{9,1},{17,9},{25,17},{10,2},{18,10},{26,18},{... | collective-permute-start | bytes 786440 | tf_op jit(solution)/shard_map/ppermute | solution.py:410
  14.5 1.6 %collective-permute-start.12 = (f32[256,256]{1,0:T(8,128)S(1)}, f32[256,256]{1,0:T(8,128)S(1)}, u32[]{:S(2)}, u32[]{:S(2)}) collective-permute-start(f32[256,256]{1,0:T(8,128)S(1)} %get-tuple-element.62), channel_id=1, source_target_pairs={{0,4},{4,0},{1,5},{5,1},{2,6},{6,2},{3,7},{7,3},{8,12},{12,8},{9,1... | collective-permute-start | bytes 786440 | tf_op jit(solution)/shard_map/ppermute | solution.py:411
  16.2 7.6 %collective-permute-done.4.refs_4_ = f32[2,256,128]{2,1,0:T(8,128)S(1)} collective-permute-done((f32[2,256,128]{2,1,0:T(8,128)S(1)}, f32[2,256,128]{2,1,0:T(8,128)S(1)}, u32[]{:S(2)}, u32[]{:S(2)}) %collective-permute-start.4) | collective-permute-done | bytes 262176 | tf_op jit(solution)/shard_map/ppermute | solution.py:410
  23.8 1.3 %shard_map.97 = (f32[256,128]{1,0:T(8,128)S(1)}, f32[256,128]{1,0:T(8,128)S(1)}, f32[256,128]{1,0:T(8,128)S(1)}, f32[256,128]{1,0:T(8,128)S(1)}, f32[256,128]{1,...) custom-call(s32[5,8]{1,0:T(8,128)S(1)} %concatenate.7.offs, ...), custom_call_target="tpu_custom_call" | custom-call | flops 2097152 | bytes 1851392 | tf_op jit(solution)/shard_map/pallas_call | solution.py:359
  25.3 1.2 %collective-permute-start.6 = (f32[256,128]{1,0:T(8,128)S(1)}, f32[256,128]{1,0:T(8,128)S(1)}, u32[]{:S(2)}, u32[]{:S(2)}) collective-permute-start(f32[256,128]{1,0:T(8,128)S(1)} %get-tuple-element.55), channel_id=1, source_target_pairs={{0,2},{1,3},{2,0},{3,1},{4,6},{5,7},{6,4},{7,5},{8,10},{9,11},{10,... | collective-permute-start | bytes 393224 | tf_op jit(solution)/shard_map/ppermute | solution.py:377
  26.4 0.9 %collective-permute-start.7 = (f32[256,128]{1,0:T(8,128)S(1)}, f32[256,128]{1,0:T(8,128)S(1)}, u32[]{:S(2)}, u32[]{:S(2)}) collective-permute-start(f32[256,128]{1,0:T(8,128)S(1)} %get-tuple-element.56), channel_id=1, source_target_pairs={{0,4},{1,5},{2,6},{3,7},{4,0},{5,1},{6,2},{7,3},{8,12},{9,13},{10,... | collective-permute-start | bytes 393224 | tf_op jit(solution)/shard_map/ppermute | solution.py:377
  27.4 1.0 %collective-permute-start.8 = (f32[256,128]{1,0:T(8,128)S(1)}, f32[256,128]{1,0:T(8,128)S(1)}, u32[]{:S(2)}, u32[]{:S(2)}) collective-permute-start(f32[256,128]{1,0:T(8,128)S(1)} %get-tuple-element.57), channel_id=1, source_target_pairs={{0,3},{1,2},{2,1},{3,0},{4,7},{5,6},{6,5},{7,4},{8,11},{9,10},{10,... | collective-permute-start | bytes 393224 | tf_op jit(solution)/shard_map/ppermute | solution.py:377
  28.4 0.7 collective-permute-start.9
  29.1 1.5 %collective-permute-start.10 = (f32[256,128]{1,0:T(8,128)S(1)}, f32[256,128]{1,0:T(8,128)S(1)}, u32[]{:S(2)}, u32[]{:S(2)}) collective-permute-start(f32[256,128]{1,0:T(8,128)S(1)} %get-tuple-element.59), channel_id=1, source_target_pairs={{0,6},{1,7},{2,4},{3,5},{4,2},{5,3},{6,0},{7,1},{8,14},{9,15},{10,... | collective-permute-start | bytes 393224 | tf_op jit(solution)/shard_map/ppermute | solution.py:377
  30.6 1.0 %collective-permute-done.6.refs_1_ = f32[256,128]{1,0:T(8,128)S(1)} collective-permute-done((f32[256,128]{1,0:T(8,128)S(1)}, f32[256,128]{1,0:T(8,128)S(1)}, u32[]{:S(2)}, u32[]{:S(2)}) %collective-permute-start.6) | collective-permute-done | bytes 131104 | tf_op jit(solution)/shard_map/ppermute | solution.py:377
  31.6 0.3 collective-permute-start.11
  31.9 2.5 %shard_map.98 = (f32[2,256,256]{2,1,0:T(8,128)S(1)}, f32[256,256]{1,0:T(8,128)S(1)}, bf16[6,512,256]{2,1,0:T(8,128)(2,1)S(1)}) custom-call(s32[5,8]{1,0:T(8,128)S(1)} %concatenate.7.offs, f32[256,256]{1,0:T(8,128)S(1)} %collective-permute-done.12.taken, f32[2,256,256]{2,1,0:T(8,128)} %probe_from.1, f32[1,2,256,256]{3,2,1,0:T(8,128)} %measured.3, ...), custom_call_target="tpu_custom_call" | custom-call | flops 201326592 | bytes 5505024 | tf_op jit(solution)/shard_map/pallas_call | solution.py:359
  34.5 4.5 %collective-permute-done.9.refs_4_ = f32[256,128]{1,0:T(8,128)S(1)} collective-permute-done((f32[256,128]{1,0:T(8,128)S(1)}, f32[256,128]{1,0:T(8,128)S(1)}, u32[]{:S(2)}, u32[]{:S(2)}) %collective-permute-start.9) | collective-permute-done | bytes 131104 | tf_op jit(solution)/shard_map/ppermute | solution.py:377
  38.9 1.2 %collective-permute-done.11.refs_6_ = f32[256,128]{1,0:T(8,128)S(1)} collective-permute-done((f32[256,128]{1,0:T(8,128)S(1)}, f32[256,128]{1,0:T(8,128)S(1)}, u32[]{:S(2)}, u32[]{:S(2)}) %collective-permute-start.11) | collective-permute-done | bytes 131104 | tf_op jit(solution)/shard_map/ppermute | solution.py:377
  40.1 4.2 %shard_map.99 = (f32[768,128]{1,0:T(8,128)S(1)}, f32[256,128]{1,0:T(8,128)S(1)}, f32[256,128]{1,0:T(8,128)S(1)}, f32[256,128]{1,0:T(8,128)S(1)}, f32[256,128]{1,...) custom-call(s32[5,8]{1,0:T(8,128)S(1)} %concatenate.7.offs, ...), custom_call_target="tpu_custom_call" | custom-call | flops 1610612736 | bytes 5120000 | tf_op jit(solution)/shard_map/pallas_call | solution.py:359
  44.3 0.3 collective-permute-start.13
  44.6 0.8 collective-permute-start.14
  45.5 1.5 %collective-permute-start.15 = (f32[256,128]{1,0:T(8,128)S(1)}, f32[256,128]{1,0:T(8,128)S(1)}, u32[]{:S(2)}, u32[]{:S(2)}) collective-permute-start(f32[256,128]{1,0:T(8,128)S(1)} %get-tuple-element.68), channel_id=1, source_target_pairs={{0,2},{1,3},{2,0},{3,1},{4,6},{5,7},{6,4},{7,5},{8,10},{9,11},{10,... | collective-permute-start | bytes 393224 | tf_op jit(solution)/shard_map/ppermute | solution.py:377
  47.0 1.4 %collective-permute-start.17 = (f32[256,128]{1,0:T(8,128)S(1)}, f32[256,128]{1,0:T(8,128)S(1)}, u32[]{:S(2)}, u32[]{:S(2)}) collective-permute-start(f32[256,128]{1,0:T(8,128)S(1)} %get-tuple-element.70), channel_id=1, source_target_pairs={{0,3},{1,2},{2,1},{3,0},{4,7},{5,6},{6,5},{7,4},{8,11},{9,10},{10,... | collective-permute-start | bytes 393224 | tf_op jit(solution)/shard_map/ppermute | solution.py:377
  48.4 0.9 collective-permute-start.19
  49.3 1.2 %collective-permute-done.14.refs_1_ = f32[256,128]{1,0:T(8,128)S(1)} collective-permute-done((f32[256,128]{1,0:T(8,128)S(1)}, f32[256,128]{1,0:T(8,128)S(1)}, u32[]{:S(2)}, u32[]{:S(2)}) %collective-permute-start.14) | collective-permute-done | bytes 131104 | tf_op jit(solution)/shard_map/ppermute | solution.py:377
  50.5 2.1 %collective-permute-start.18 = (f32[256,128]{1,0:T(8,128)S(1)}, f32[256,128]{1,0:T(8,128)S(1)}, u32[]{:S(2)}, u32[]{:S(2)}) collective-permute-start(f32[256,128]{1,0:T(8,128)S(1)} %get-tuple-element.74), channel_id=1, source_target_pairs={{0,6},{1,7},{2,4},{3,5},{4,2},{5,3},{6,0},{7,1},{8,14},{9,15},{10,... | collective-permute-start | bytes 393224 | tf_op jit(solution)/shard_map/ppermute | solution.py:377
  52.6 0.3 collective-permute-start.20
  53.0 1.1 %collective-permute-start.21 = (f32[128,128]{1,0:T(8,128)S(1)}, f32[128,128]{1,0:T(8,128)S(1)}, u32[]{:S(2)}, u32[]{:S(2)}) collective-permute-start(f32[128,128]{1,0:T(8,128)S(1)} %get-tuple-element.78), channel_id=1, source_target_pairs={{0,2},{2,0},{4,6},{6,4},{1,3},{3,1},{5,7},{7,5},{8,10},{10,8},{12,... | collective-permute-start | bytes 196616 | tf_op jit(solution)/shard_map/ppermute | solution.py:377
  54.0 2.1 %collective-permute-start.22 = (f32[128,128]{1,0:T(8,128)S(1)}, f32[128,128]{1,0:T(8,128)S(1)}, u32[]{:S(2)}, u32[]{:S(2)}) collective-permute-start(f32[128,128]{1,0:T(8,128)S(1)} %get-tuple-element.79), channel_id=1, source_target_pairs={{0,6},{2,4},{4,2},{6,0},{1,7},{3,5},{5,3},{7,1},{8,14},{10,12},{12... | collective-permute-start | bytes 196616 | tf_op jit(solution)/shard_map/ppermute | solution.py:377
  56.1 0.4 collective-permute-done.19.refs_6_
  56.6 3.9 %collective-permute-done.20.refs_8_ = f32[128,128]{1,0:T(8,128)S(1)} collective-permute-done((f32[128,128]{1,0:T(8,128)S(1)}, f32[128,128]{1,0:T(8,128)S(1)}, u32[]{:S(2)}, u32[]{:S(2)}) %collective-permute-start.20) | collective-permute-done | bytes 65568 | tf_op jit(solution)/shard_map/ppermute | solution.py:377
  60.4 0.9 collective-permute-done.21.refs_9_
  61.3 1.5 %collective-permute-done.22.refs_10_ = f32[128,128]{1,0:T(8,128)S(1)} collective-permute-done((f32[128,128]{1,0:T(8,128)S(1)}, f32[128,128]{1,0:T(8,128)S(1)}, u32[]{:S(2)}, u32[]{:S(2)}) %collective-permute-start.22) | collective-permute-done | bytes 65568 | tf_op jit(solution)/shard_map/ppermute | solution.py:377
  62.7 1.0 %shard_map.102 = (f32[2,256,128]{2,1,0:T(8,128)S(1)}, f32[64,256]{1,0:T(8,128)S(1)}) custom-call(s32[5,8]{1,0:T(8,128)S(1)} %concatenate.7.offs, f32[768,128]{1,0:T(8,128)S(1)} %collective-permute-done.13.got.refs_0_, f32[256,128]{1,0:T(8,128)S(1)} %collective-permute-done.14.refs_1_, f32[256,128]{1,0:T(8,128)S(1)} %collective-permute-done.15.refs_2_, ...), custom_call_target="tpu_custom_call" | custom-call | flops 2097152 | bytes 1900544 | tf_op jit(solution)/shard_map/pallas_call | solution.py:359
  63.8 3.5 %collective-permute-start.23 = (f32[2,256,128]{2,1,0:T(8,128)S(1)}, f32[2,256,128]{2,1,0:T(8,128)S(1)}, u32[]{:S(2)}, u32[]{:S(2)}) collective-permute-start(f32[2,256,128]{2,1,0:T(8,128)S(1)} %get-tuple-element.81), channel_id=1, source_target_pairs={{0,8},{8,16},{16,24},{1,9},{9,17},{17,25},{2,10},{10,18},{18,26},{... | collective-permute-start | bytes 786440 | tf_op jit(solution)/shard_map/ppermute | solution.py:458
  67.3 1.6 %collective-permute-start.24 = (f32[64,256]{1,0:T(8,128)S(1)}, f32[64,256]{1,0:T(8,128)S(1)}, u32[]{:S(2)}, u32[]{:S(2)}) collective-permute-start(f32[64,256]{1,0:T(8,128)S(1)} %get-tuple-element.86), channel_id=1, source_target_pairs={{0,8},{8,0},{16,24},{24,16},{1,9},{9,1},{17,25},{25,17},{2,10},{10... | collective-permute-start | bytes 196616 | tf_op jit(solution)/shard_map/ppermute | solution.py:461
  68.9 1.5 %shard_map.101.own = f32[4,256,128]{2,1,0:T(8,128)S(1)} custom-call(s32[5,8]{1,0:T(8,128)S(1)} %concatenate.7.offs, f32[768,128]{1,0:T(8,128)S(1)} %collective-permute-done.13.got.refs_0_, f32[256,128]{1,0:T(8,128)S(1)} %collective-permute-done.14.refs_1_, f32[256,128]{1,0:T(8,128)S(1)} %collective-permute-done.15.refs_2_, ...), custom_call_target="tpu_custom_call" | custom-call | flops 4194304 | bytes 1835008 | tf_op jit(solution)/shard_map/pallas_call | solution.py:359
  70.4 2.2 %collective-permute-done.23.above = f32[2,256,128]{2,1,0:T(8,128)S(1)} collective-permute-done((f32[2,256,128]{2,1,0:T(8,128)S(1)}, f32[2,256,128]{2,1,0:T(8,128)S(1)}, u32[]{:S(2)}, u32[]{:S(2)}) %collective-permute-start.23) | collective-permute-done | bytes 262176 | tf_op jit(solution)/shard_map/ppermute | solution.py:458
  72.6 0.6 collective-permute-done.24
  73.3 2.2 %collective-permute-start.28 = (f32[64,256]{1,0:T(8,128)S(1)}, f32[64,256]{1,0:T(8,128)S(1)}, u32[]{:S(2)}, u32[]{:S(2)}) collective-permute-start(f32[64,256]{1,0:T(8,128)S(1)} %add.8), channel_id=1, source_target_pairs={{0,16},{8,24},{16,0},{24,8},{1,17},{9,25},{17,1},{25,9},{2,18},{10... | collective-permute-start | bytes 196616 | tf_op jit(solution)/shard_map/ppermute | solution.py:385
  75.5 0.9 collective-permute-start.25
  76.4 1.0 %collective-permute-start.26 = (f32[256,128]{1,0:T(8,128)S(1)}, f32[256,128]{1,0:T(8,128)S(1)}, u32[]{:S(2)}, u32[]{:S(2)}) collective-permute-start(f32[256,128]{1,0:T(8,128)S(1)} %get-tuple-element.88), channel_id=1, source_target_pairs={{0,2},{2,0},{4,6},{6,4},{1,3},{3,1},{5,7},{7,5},{8,10},{10,8},{12,... | collective-permute-start | bytes 393224 | tf_op jit(solution)/shard_map/ppermute | solution.py:377
  77.4 1.6 %collective-permute-start.27 = (f32[256,128]{1,0:T(8,128)S(1)}, f32[256,128]{1,0:T(8,128)S(1)}, u32[]{:S(2)}, u32[]{:S(2)}) collective-permute-start(f32[256,128]{1,0:T(8,128)S(1)} %get-tuple-element.89), channel_id=1, source_target_pairs={{0,6},{2,4},{4,2},{6,0},{1,7},{3,5},{5,3},{7,1},{8,14},{10,12},{12... | collective-permute-start | bytes 393224 | tf_op jit(solution)/shard_map/ppermute | solution.py:377
  79.0 9.3 %all_gather.3.refs_4_ = f32[512,256]{1,0:T(8,128)S(1)} all-gather(f32[64,256]{1,0:T(8,128)S(1)} %add.9), channel_id=1, replica_groups=mesh['pair'=4,'half'=2,'col'=2,'core'=2] {'half','col','core'}, dimensions={0}, use_global_device_ids=true | all-gather | bytes 589824 | tf_op jit(solution)/shard_map/all_gather | solution.py:470
  88.3 1.0 %shard_map.104 = (f32[4,256,128]{2,1,0:T(8,128)}, f32[512,256]{1,0:T(8,128)}) custom-call(f32[256,128]{1,0:T(8,128)S(1)} %collective-permute-done.25.refs_0_, f32[256,128]{1,0:T(8,128)S(1)} %collective-permute-done.26.refs_1_, f32[256,128]{1,0:T(8,128)S(1)} %collective-permute-done.27.refs_2_, f32[256,128]{1,0:T(8,128)S(1)} %get-tuple-element.90.refs_3_, ...), custom_call_target="tpu_custom_call" | custom-call | bytes 2097152 | tf_op jit(solution)/shard_map/pallas_call | solution.py:359
  (34 shorter events, 0.7 us)
Async XLA Ops:
  1.9 7.3 %collective-permute-start = (f32[264,128]{1,0:T(8,128)S(1)}, f32[264,128]{1,0:T(8,128)S(1)}, u32[]{:S(2)}, u32[]{:S(2)}) collective-permute-start(f32[264,128]{1,0:T(8,128)S(1)} %get-tuple-element.49), channel_id=1, source_target_pairs={{0,2},{2,0},{4,6},{6,4},{1,3},{3,1},{5,7},{7,5},{8,10},{10,8},{12,... | collective-permute-start | bytes 405512 | tf_op jit(solution)/shard_map/ppermute | solution.py:377
  4.9 7.9 %collective-permute-start.1 = (f32[264,128]{1,0:T(8,128)S(1)}, f32[264,128]{1,0:T(8,128)S(1)}, u32[]{:S(2)}, u32[]{:S(2)}) collective-permute-start(f32[264,128]{1,0:T(8,128)S(1)} %get-tuple-element.50), channel_id=1, source_target_pairs={{0,4},{2,6},{4,0},{6,2},{1,5},{3,7},{5,1},{7,3},{8,12},{10,14},{12... | collective-permute-start | bytes 405512 | tf_op jit(solution)/shard_map/ppermute | solution.py:377
  6.4 6.5 %collective-permute-start.2 = (f32[264,128]{1,0:T(8,128)S(1)}, f32[264,128]{1,0:T(8,128)S(1)}, u32[]{:S(2)}, u32[]{:S(2)}) collective-permute-start(f32[264,128]{1,0:T(8,128)S(1)} %get-tuple-element.51), channel_id=1, source_target_pairs={{0,6},{2,4},{4,2},{6,0},{1,7},{3,5},{5,3},{7,1},{8,14},{10,12},{12... | collective-permute-start | bytes 405512 | tf_op jit(solution)/shard_map/ppermute | solution.py:377
  13.1 3.0 %collective-permute-start.3 = (s32[4,4]{1,0:T(4,128)S(1)}, s32[4,4]{1,0:T(4,128)S(1)}, u32[]{:S(2)}, u32[]{:S(2)}) collective-permute-start(s32[4,4]{1,0:T(4,128)S(1)} %maximum_convert_fusion), channel_id=1, source_target_pairs={{0,1},{1,0},{2,3},{3,2},{4,5},{5,4},{6,7},{7,6},{8,9},{9,8},{10,11... | collective-permute-start | bytes 200 | tf_op jit(solution)/shard_map/ppermute | solution.py:415
  13.2 10.6 %collective-permute-start.4 = (f32[2,256,128]{2,1,0:T(8,128)S(1)}, f32[2,256,128]{2,1,0:T(8,128)S(1)}, u32[]{:S(2)}, u32[]{:S(2)}) collective-permute-start(f32[2,256,128]{2,1,0:T(8,128)S(1)} %shard_map.96), channel_id=1, source_target_pairs={{8,0},{16,8},{24,16},{9,1},{17,9},{25,17},{10,2},{18,10},{26,18},{... | collective-permute-start | bytes 786440 | tf_op jit(solution)/shard_map/ppermute | solution.py:410
  14.5 13.8 %collective-permute-start.12 = (f32[256,256]{1,0:T(8,128)S(1)}, f32[256,256]{1,0:T(8,128)S(1)}, u32[]{:S(2)}, u32[]{:S(2)}) collective-permute-start(f32[256,256]{1,0:T(8,128)S(1)} %get-tuple-element.62), channel_id=1, source_target_pairs={{0,4},{4,0},{1,5},{5,1},{2,6},{6,2},{3,7},{7,3},{8,12},{12,8},{9,1... | collective-permute-start | bytes 786440 | tf_op jit(solution)/shard_map/ppermute | solution.py:411
  25.2 3.9 %collective-permute-start.5 = (f32[256,128]{1,0:T(8,128)S(1)}, f32[256,128]{1,0:T(8,128)S(1)}, u32[]{:S(2)}, u32[]{:S(2)}) collective-permute-start(f32[256,128]{1,0:T(8,128)S(1)} %get-tuple-element.54), channel_id=1, source_target_pairs={{0,1},{1,0},{2,3},{3,2},{4,5},{5,4},{6,7},{7,6},{8,9},{9,8},{10,11... | collective-permute-start | bytes 393224 | tf_op jit(solution)/shard_map/ppermute | solution.py:377
  25.3 6.4 %collective-permute-start.6 = (f32[256,128]{1,0:T(8,128)S(1)}, f32[256,128]{1,0:T(8,128)S(1)}, u32[]{:S(2)}, u32[]{:S(2)}) collective-permute-start(f32[256,128]{1,0:T(8,128)S(1)} %get-tuple-element.55), channel_id=1, source_target_pairs={{0,2},{1,3},{2,0},{3,1},{4,6},{5,7},{6,4},{7,5},{8,10},{9,11},{10,... | collective-permute-start | bytes 393224 | tf_op jit(solution)/shard_map/ppermute | solution.py:377
  26.4 8.0 %collective-permute-start.7 = (f32[256,128]{1,0:T(8,128)S(1)}, f32[256,128]{1,0:T(8,128)S(1)}, u32[]{:S(2)}, u32[]{:S(2)}) collective-permute-start(f32[256,128]{1,0:T(8,128)S(1)} %get-tuple-element.56), channel_id=1, source_target_pairs={{0,4},{1,5},{2,6},{3,7},{4,0},{5,1},{6,2},{7,3},{8,12},{9,13},{10,... | collective-permute-start | bytes 393224 | tf_op jit(solution)/shard_map/ppermute | solution.py:377
  27.4 7.1 %collective-permute-start.8 = (f32[256,128]{1,0:T(8,128)S(1)}, f32[256,128]{1,0:T(8,128)S(1)}, u32[]{:S(2)}, u32[]{:S(2)}) collective-permute-start(f32[256,128]{1,0:T(8,128)S(1)} %get-tuple-element.57), channel_id=1, source_target_pairs={{0,3},{1,2},{2,1},{3,0},{4,7},{5,6},{6,5},{7,4},{8,11},{9,10},{10,... | collective-permute-start | bytes 393224 | tf_op jit(solution)/shard_map/ppermute | solution.py:377
  28.4 10.6 %collective-permute-start.9 = (f32[256,128]{1,0:T(8,128)S(1)}, f32[256,128]{1,0:T(8,128)S(1)}, u32[]{:S(2)}, u32[]{:S(2)}) collective-permute-start(f32[256,128]{1,0:T(8,128)S(1)} %get-tuple-element.58), channel_id=1, source_target_pairs={{0,5},{1,4},{2,7},{3,6},{4,1},{5,0},{6,3},{7,2},{8,13},{9,12},{10,... | collective-permute-start | bytes 393224 | tf_op jit(solution)/shard_map/ppermute | solution.py:377
  29.1 9.8 %collective-permute-start.10 = (f32[256,128]{1,0:T(8,128)S(1)}, f32[256,128]{1,0:T(8,128)S(1)}, u32[]{:S(2)}, u32[]{:S(2)}) collective-permute-start(f32[256,128]{1,0:T(8,128)S(1)} %get-tuple-element.59), channel_id=1, source_target_pairs={{0,6},{1,7},{2,4},{3,5},{4,2},{5,3},{6,0},{7,1},{8,14},{9,15},{10,... | collective-permute-start | bytes 393224 | tf_op jit(solution)/shard_map/ppermute | solution.py:377
  31.6 8.5 %copy-start = (f32[2,136,128]{2,1,0:T(8,128)S(1)}, f32[2,136,128]{2,1,0:T(8,128)}, u32[]{:S(2)}) copy-start(f32[2,136,128]{2,1,0:T(8,128)} %constant.17.clone.refs_11_) | copy-start | bytes 417796
  31.6 8.5 %collective-permute-start.11 = (f32[256,128]{1,0:T(8,128)S(1)}, f32[256,128]{1,0:T(8,128)S(1)}, u32[]{:S(2)}, u32[]{:S(2)}) collective-permute-start(f32[256,128]{1,0:T(8,128)S(1)} %get-tuple-element.60), channel_id=1, source_target_pairs={{0,7},{1,6},{2,5},{3,4},{4,3},{5,2},{6,1},{7,0},{8,15},{9,14},{10,... | collective-permute-start | bytes 393224 | tf_op jit(solution)/shard_map/ppermute | solution.py:377
  44.3 4.1 %collective-permute-start.13 = (f32[768,128]{1,0:T(8,128)S(1)}, f32[768,128]{1,0:T(8,128)S(1)}, u32[]{:S(2)}, u32[]{:S(2)}) collective-permute-start(f32[768,128]{1,0:T(8,128)S(1)} %get-tuple-element.66), channel_id=1, source_target_pairs={{0,1},{1,0},{2,3},{3,2},{4,5},{5,4},{6,7},{7,6},{8,9},{9,8},{10,11... | collective-permute-start | bytes 1179656 | tf_op jit(solution)/shard_map/ppermute | solution.py:377
  44.6 5.9 %collective-permute-start.14 = (f32[256,128]{1,0:T(8,128)S(1)}, f32[256,128]{1,0:T(8,128)S(1)}, u32[]{:S(2)}, u32[]{:S(2)}) collective-permute-start(f32[256,128]{1,0:T(8,128)S(1)} %get-tuple-element.67), channel_id=1, source_target_pairs={{0,4},{1,5},{2,6},{3,7},{4,0},{5,1},{6,2},{7,3},{8,12},{9,13},{10,... | collective-permute-start | bytes 393224 | tf_op jit(solution)/shard_map/ppermute | solution.py:377
  45.5 7.2 %collective-permute-start.15 = (f32[256,128]{1,0:T(8,128)S(1)}, f32[256,128]{1,0:T(8,128)S(1)}, u32[]{:S(2)}, u32[]{:S(2)}) collective-permute-start(f32[256,128]{1,0:T(8,128)S(1)} %get-tuple-element.68), channel_id=1, source_target_pairs={{0,2},{1,3},{2,0},{3,1},{4,6},{5,7},{6,4},{7,5},{8,10},{9,11},{10,... | collective-permute-start | bytes 393224 | tf_op jit(solution)/shard_map/ppermute | solution.py:377
  47.0 6.0 %collective-permute-start.16 = (f32[256,128]{1,0:T(8,128)S(1)}, f32[256,128]{1,0:T(8,128)S(1)}, u32[]{:S(2)}, u32[]{:S(2)}) collective-permute-start(f32[256,128]{1,0:T(8,128)S(1)} %get-tuple-element.69), channel_id=1, source_target_pairs={{0,5},{1,4},{2,7},{3,6},{4,1},{5,0},{6,3},{7,2},{8,13},{9,12},{10,... | collective-permute-start | bytes 393224 | tf_op jit(solution)/shard_map/ppermute | solution.py:377
  47.0 7.0 %collective-permute-start.17 = (f32[256,128]{1,0:T(8,128)S(1)}, f32[256,128]{1,0:T(8,128)S(1)}, u32[]{:S(2)}, u32[]{:S(2)}) collective-permute-start(f32[256,128]{1,0:T(8,128)S(1)} %get-tuple-element.70), channel_id=1, source_target_pairs={{0,3},{1,2},{2,1},{3,0},{4,7},{5,6},{6,5},{7,4},{8,11},{9,10},{10,... | collective-permute-start | bytes 393224 | tf_op jit(solution)/shard_map/ppermute | solution.py:377
  48.4 8.1 %collective-permute-start.19 = (f32[256,128]{1,0:T(8,128)S(1)}, f32[256,128]{1,0:T(8,128)S(1)}, u32[]{:S(2)}, u32[]{:S(2)}) collective-permute-start(f32[256,128]{1,0:T(8,128)S(1)} %get-tuple-element.75), channel_id=1, source_target_pairs={{0,7},{1,6},{2,5},{3,4},{4,3},{5,2},{6,1},{7,0},{8,15},{9,14},{10,... | collective-permute-start | bytes 393224 | tf_op jit(solution)/shard_map/ppermute | solution.py:377
  50.5 12.2 %collective-permute-start.18 = (f32[256,128]{1,0:T(8,128)S(1)}, f32[256,128]{1,0:T(8,128)S(1)}, u32[]{:S(2)}, u32[]{:S(2)}) collective-permute-start(f32[256,128]{1,0:T(8,128)S(1)} %get-tuple-element.74), channel_id=1, source_target_pairs={{0,6},{1,7},{2,4},{3,5},{4,2},{5,3},{6,0},{7,1},{8,14},{9,15},{10,... | collective-permute-start | bytes 393224 | tf_op jit(solution)/shard_map/ppermute | solution.py:377
  52.6 7.8 %collective-permute-start.20 = (f32[128,128]{1,0:T(8,128)S(1)}, f32[128,128]{1,0:T(8,128)S(1)}, u32[]{:S(2)}, u32[]{:S(2)}) collective-permute-start(f32[128,128]{1,0:T(8,128)S(1)} %get-tuple-element.77), channel_id=1, source_target_pairs={{0,4},{2,6},{4,0},{6,2},{1,5},{3,7},{5,1},{7,3},{8,12},{10,14},{12... | collective-permute-start | bytes 196616 | tf_op jit(solution)/shard_map/ppermute | solution.py:377
  53.0 8.3 %collective-permute-start.21 = (f32[128,128]{1,0:T(8,128)S(1)}, f32[128,128]{1,0:T(8,128)S(1)}, u32[]{:S(2)}, u32[]{:S(2)}) collective-permute-start(f32[128,128]{1,0:T(8,128)S(1)} %get-tuple-element.78), channel_id=1, source_target_pairs={{0,2},{2,0},{4,6},{6,4},{1,3},{3,1},{5,7},{7,5},{8,10},{10,8},{12,... | collective-permute-start | bytes 196616 | tf_op jit(solution)/shard_map/ppermute | solution.py:377
  54.0 8.7 %collective-permute-start.22 = (f32[128,128]{1,0:T(8,128)S(1)}, f32[128,128]{1,0:T(8,128)S(1)}, u32[]{:S(2)}, u32[]{:S(2)}) collective-permute-start(f32[128,128]{1,0:T(8,128)S(1)} %get-tuple-element.79), channel_id=1, source_target_pairs={{0,6},{2,4},{4,2},{6,0},{1,7},{3,5},{5,3},{7,1},{8,14},{10,12},{12... | collective-permute-start | bytes 196616 | tf_op jit(solution)/shard_map/ppermute | solution.py:377
  63.8 8.8 %collective-permute-start.23 = (f32[2,256,128]{2,1,0:T(8,128)S(1)}, f32[2,256,128]{2,1,0:T(8,128)S(1)}, u32[]{:S(2)}, u32[]{:S(2)}) collective-permute-start(f32[2,256,128]{2,1,0:T(8,128)S(1)} %get-tuple-element.81), channel_id=1, source_target_pairs={{0,8},{8,16},{16,24},{1,9},{9,17},{17,25},{2,10},{10,18},{18,26},{... | collective-permute-start | bytes 786440 | tf_op jit(solution)/shard_map/ppermute | solution.py:458
  67.3 6.0 %collective-permute-start.24 = (f32[64,256]{1,0:T(8,128)S(1)}, f32[64,256]{1,0:T(8,128)S(1)}, u32[]{:S(2)}, u32[]{:S(2)}) collective-permute-start(f32[64,256]{1,0:T(8,128)S(1)} %get-tuple-element.86), channel_id=1, source_target_pairs={{0,8},{8,0},{16,24},{24,16},{1,9},{9,1},{17,25},{25,17},{2,10},{10... | collective-permute-start | bytes 196616 | tf_op jit(solution)/shard_map/ppermute | solution.py:461
  73.3 5.7 %collective-permute-start.28 = (f32[64,256]{1,0:T(8,128)S(1)}, f32[64,256]{1,0:T(8,128)S(1)}, u32[]{:S(2)}, u32[]{:S(2)}) collective-permute-start(f32[64,256]{1,0:T(8,128)S(1)} %add.8), channel_id=1, source_target_pairs={{0,16},{8,24},{16,0},{24,8},{1,17},{9,25},{17,1},{25,9},{2,18},{10... | collective-permute-start | bytes 196616 | tf_op jit(solution)/shard_map/ppermute | solution.py:385
  75.5 12.8 %collective-permute-start.25 = (f32[256,128]{1,0:T(8,128)S(1)}, f32[256,128]{1,0:T(8,128)S(1)}, u32[]{:S(2)}, u32[]{:S(2)}) collective-permute-start(f32[256,128]{1,0:T(8,128)S(1)} %get-tuple-element.87), channel_id=1, source_target_pairs={{0,4},{2,6},{4,0},{6,2},{1,5},{3,7},{5,1},{7,3},{8,12},{10,14},{12... | collective-permute-start | bytes 393224 | tf_op jit(solution)/shard_map/ppermute | solution.py:377
  76.4 11.9 %collective-permute-start.26 = (f32[256,128]{1,0:T(8,128)S(1)}, f32[256,128]{1,0:T(8,128)S(1)}, u32[]{:S(2)}, u32[]{:S(2)}) collective-permute-start(f32[256,128]{1,0:T(8,128)S(1)} %get-tuple-element.88), channel_id=1, source_target_pairs={{0,2},{2,0},{4,6},{6,4},{1,3},{3,1},{5,7},{7,5},{8,10},{10,8},{12,... | collective-permute-start | bytes 393224 | tf_op jit(solution)/shard_map/ppermute | solution.py:377
  77.4 10.9 %collective-permute-start.27 = (f32[256,128]{1,0:T(8,128)S(1)}, f32[256,128]{1,0:T(8,128)S(1)}, u32[]{:S(2)}, u32[]{:S(2)}) collective-permute-start(f32[256,128]{1,0:T(8,128)S(1)} %get-tuple-element.89), channel_id=1, source_target_pairs={{0,6},{2,4},{4,2},{6,0},{1,7},{3,5},{5,3},{7,1},{8,14},{10,12},{12... | collective-permute-start | bytes 393224 | tf_op jit(solution)/shard_map/ppermute | solution.py:377

commit v21 on v19

--- a/solution.py
+++ b/solution.py
@@ -338,11 +338,16 @@
 
 
 def join_kernel(*refs):
-    probe, out, probe_out, sems = refs[4:]
-    half, col, unused = here()
+    halves, (out, probe_out, sems) = refs[4:6], refs[6:]
+    half, col, core = here()
     mine = 2 * half + col
     pairs = [(ref, out.at[jnp.bitwise_xor(mine, turn)]) for turn, ref in zip(FOUR, refs)]
-    for copy in fetch([(probe, probe_out), *pairs], sems):
+    band = halves[0].shape[1]
+    for side, bands in zip((core, 1 - core), halves):
+        for part in range(4):
+            start = pl.multiple_of(band * (2 * part + side), band)
+            pairs.append((bands.at[part], probe_out.at[pl.ds(start, band)]))
+    for copy in fetch(pairs, sems):
         copy.wait()
 
 
@@ -463,14 +468,15 @@
     else:
         probe_band = lax.psum(probe_band, "pair")
     sums = deal(sums, PLANE[:2], FOUR)
-    probe_grad = lax.all_gather(probe_band, PLANE, axis=0, tiled=True)
+    bands = lax.all_gather(probe_band, PLANE[:2], axis=0)
+    others = lax.ppermute(bands, "core", [(0, 1), (1, 0)])
     object_grad, probe_grad = call(
         join_kernel,
-        [(shape(planes, rows, cols), HBM), (shape(*probe_grad.shape), HBM)],
+        [(shape(planes, rows, cols), HBM), (shape(8 * band, width), HBM)],
         (),
-        [(x, ANY) for x in (*sums, probe_grad)],
+        [(x, ANY) for x in (*sums, bands, others)],
         0,
-        copies=5,
+        copies=12,
     )
     return (object_grad.reshape(object_field.shape), probe_grad.reshape(probe.shape))
 

time: 89.5 us -> 98.4 us (1.099)
  waiting for transfers between devices: 28.9 us -> 38.9 us
  blocking collectives: 8.82 us -> 7.5 us
    ppermute x23, waiting for transfers between devices: 17.2 us -> 23.8 us  [deal(): lax.ppermute(value, axes, [(k, k ^ turn) for k in range(len(order))])]
    ppermute x1, waiting for transfers between devices: 0.22 us -> 3.71 us  [sum_over(): lax.ppermute(value, axis, [(k, k ^ step) for k in range(size)])]
    all_gather x1, blocking collectives: 8.82 us -> 7.5 us  [local(): bands = lax.all_gather(probe_band, PLANE[:2], axis=0)]
  transfers between devices with their start and end apart: 29 -> 30, of which waited for: 13 -> 16; matrix products, arithmetic and copies ran while one was open for 2% -> 2% of each run, Pallas kernels for 6% -> 6%
where the time goes in v21:
time: 98.4 us; the launch traced here: 98.1 us
  waiting for transfers between devices  38.9 us (40%)
  starting transfers between devices  34.7 us (35%)
  Pallas kernels  13 us (13%)
  blocking collectives  7.5 us (8%)
  between operations  2.06 us (2%)
  local copies, waits for them, and re-layouts  1.79 us (2%)
    ppermute x23, starting transfers between devices, deal(): lax.ppermute(value, axes, [(k, k ^ turn) for k in range(len(order))])  24.4 us
    ppermute x23, waiting for transfers between devices, deal(): lax.ppermute(value, axes, [(k, k ^ turn) for k in range(len(order))])  23.8 us
    pallas_call x10, Pallas kernels, call(): pl.pallas_call(kernel, out_shape=[x for x, unused in outs], in_specs=[SME...  13 us
    ppermute x1, waiting for transfers between devices, local(): below = lax.ppermute(lowest, 'pair', [(k, k - 1) for k in range(1, pairs)])  7.61 us
    all_gather x1, blocking collectives, local(): bands = lax.all_gather(probe_band, PLANE[:2], axis=0)  7.5 us
    ppermute x1, waiting for transfers between devices, sum_over(): lax.ppermute(value, axis, [(k, k ^ step) for k in range(size)])  3.71 us
    ppermute x1, starting transfers between devices, local(): lax.ppermute(lower_sums, 'pair', [(k, k + 1) for k in range(pairs - 1)])  3.49 us
    ppermute x1, waiting for transfers between devices, local(): lax.ppermute(lower_sums, 'pair', [(k, k + 1) for k in range(pairs - 1)])  3.18 us
  transfers between devices with their start and end apart: 30, of which 16 were waited for; matrix products, arithmetic and copies ran while one was open for 2% of the time, Pallas kernels for 6%

profile of v21, /device:TPU:0, one launch (start us, length us, event | category | flops | bytes accessed | tf_op | source)
XLA Modules:
  0.0 98.1 jit_solution(14556126806902133916)
XLA Ops:
  0.6 1.3 %shard_map.95 = (f32[264,128]{1,0:T(8,128)S(1)}, f32[264,128]{1,0:T(8,128)S(1)}, f32[264,128]{1,0:T(8,128)S(1)}, f32[264,128]{1,0:T(8,128)S(1)}, f32[256,256]{1,0:T(8,128)S(1)}) custom-call(f32[4,256,128]{2,1,0:T(8,128)} %bitcast.12, f32[1,2,256,256]{3,2,1,0:T(8,128)} %measured.3, s32[1,2,2]{2,1,0:T(2,128)} %offsets_from.1), custom_call_target="tpu_custom_call" | custom-call | bytes 1851408 | tf_op jit(solution)/shard_map/pallas_call | solution.py:364
  1.9 3.0 %collective-permute-start = (f32[264,128]{1,0:T(8,128)S(1)}, f32[264,128]{1,0:T(8,128)S(1)}, u32[]{:S(2)}, u32[]{:S(2)}) collective-permute-start(f32[264,128]{1,0:T(8,128)S(1)} %get-tuple-element.47), channel_id=1, source_target_pairs={{0,2},{2,0},{4,6},{6,4},{1,3},{3,1},{5,7},{7,5},{8,10},{10,8},{12,... | collective-permute-start | bytes 405512 | tf_op jit(solution)/shard_map/ppermute | solution.py:381
  4.9 1.5 %collective-permute-start.1 = (f32[264,128]{1,0:T(8,128)S(1)}, f32[264,128]{1,0:T(8,128)S(1)}, u32[]{:S(2)}, u32[]{:S(2)}) collective-permute-start(f32[264,128]{1,0:T(8,128)S(1)} %get-tuple-element.48), channel_id=1, source_target_pairs={{0,4},{2,6},{4,0},{6,2},{1,5},{3,7},{5,1},{7,3},{8,12},{10,14},{12... | collective-permute-start | bytes 405512 | tf_op jit(solution)/shard_map/ppermute | solution.py:381
  6.6 1.3 %fusion = (s32[1,1]{1,0:T(1,128)}, s32[1,1]{1,0:T(1,128)}) fusion(s32[1,2]{1,0:T(1,128)} %param.11), kind=kLoop, calls=%fused_computation.8 | loop fusion | bytes 16 | tf_op jit(solution)/shard_map/slice | solution.py:421
  9.3 3.5 %collective-permute-done.1.refs_0_ = f32[264,128]{1,0:T(8,128)S(1)} collective-permute-done((f32[264,128]{1,0:T(8,128)S(1)}, f32[264,128]{1,0:T(8,128)S(1)}, u32[]{:S(2)}, u32[]{:S(2)}) %collective-permute-start.1) | collective-permute-done | bytes 135200 | tf_op jit(solution)/shard_map/ppermute | solution.py:381
  13.2 1.3 %collective-permute-start.4 = (f32[2,256,128]{2,1,0:T(8,128)S(1)}, f32[2,256,128]{2,1,0:T(8,128)S(1)}, u32[]{:S(2)}, u32[]{:S(2)}) collective-permute-start(f32[2,256,128]{2,1,0:T(8,128)S(1)} %shard_map.96), channel_id=1, source_target_pairs={{8,0},{16,8},{24,16},{9,1},{17,9},{25,17},{10,2},{18,10},{26,18},{... | collective-permute-start | bytes 786440 | tf_op jit(solution)/shard_map/ppermute | solution.py:414
  14.5 1.6 %collective-permute-start.12 = (f32[256,256]{1,0:T(8,128)S(1)}, f32[256,256]{1,0:T(8,128)S(1)}, u32[]{:S(2)}, u32[]{:S(2)}) collective-permute-start(f32[256,256]{1,0:T(8,128)S(1)} %get-tuple-element.60), channel_id=1, source_target_pairs={{0,4},{4,0},{1,5},{5,1},{2,6},{6,2},{3,7},{7,3},{8,12},{12,8},{9,1... | collective-permute-start | bytes 786440 | tf_op jit(solution)/shard_map/ppermute | solution.py:415
  16.2 7.6 %collective-permute-done.4.refs_4_ = f32[2,256,128]{2,1,0:T(8,128)S(1)} collective-permute-done((f32[2,256,128]{2,1,0:T(8,128)S(1)}, f32[2,256,128]{2,1,0:T(8,128)S(1)}, u32[]{:S(2)}, u32[]{:S(2)}) %collective-permute-start.4) | collective-permute-done | bytes 262176 | tf_op jit(solution)/shard_map/ppermute | solution.py:414
  23.8 1.3 %shard_map.97 = (f32[256,128]{1,0:T(8,128)S(1)}, f32[256,128]{1,0:T(8,128)S(1)}, f32[256,128]{1,0:T(8,128)S(1)}, f32[256,128]{1,0:T(8,128)S(1)}, f32[256,128]{1,...) custom-call(s32[5,8]{1,0:T(8,128)S(1)} %concatenate.7.offs, ...), custom_call_target="tpu_custom_call" | custom-call | flops 2097152 | bytes 1851392 | tf_op jit(solution)/shard_map/pallas_call | solution.py:364
  25.2 1.2 %collective-permute-start.5 = (f32[256,128]{1,0:T(8,128)S(1)}, f32[256,128]{1,0:T(8,128)S(1)}, u32[]{:S(2)}, u32[]{:S(2)}) collective-permute-start(f32[256,128]{1,0:T(8,128)S(1)} %get-tuple-element.52), channel_id=1, source_target_pairs={{0,2},{1,3},{2,0},{3,1},{4,6},{5,7},{6,4},{7,5},{8,10},{9,11},{10,... | collective-permute-start | bytes 393224 | tf_op jit(solution)/shard_map/ppermute | solution.py:381
  26.4 0.9 collective-permute-start.6
  27.3 0.2 collective-permute-start.7
  27.5 1.5 %collective-permute-start.8 = (f32[256,128]{1,0:T(8,128)S(1)}, f32[256,128]{1,0:T(8,128)S(1)}, u32[]{:S(2)}, u32[]{:S(2)}) collective-permute-start(f32[256,128]{1,0:T(8,128)S(1)} %get-tuple-element.55), channel_id=1, source_target_pairs={{0,5},{1,4},{2,7},{3,6},{4,1},{5,0},{6,3},{7,2},{8,13},{9,12},{10,... | collective-permute-start | bytes 393224 | tf_op jit(solution)/shard_map/ppermute | solution.py:381
  29.0 1.5 %collective-permute-start.9 = (f32[256,128]{1,0:T(8,128)S(1)}, f32[256,128]{1,0:T(8,128)S(1)}, u32[]{:S(2)}, u32[]{:S(2)}) collective-permute-start(f32[256,128]{1,0:T(8,128)S(1)} %get-tuple-element.56), channel_id=1, source_target_pairs={{0,6},{1,7},{2,4},{3,5},{4,2},{5,3},{6,0},{7,1},{8,14},{9,15},{10,... | collective-permute-start | bytes 393224 | tf_op jit(solution)/shard_map/ppermute | solution.py:381
  30.5 0.7 collective-permute-start.10
  31.2 1.0 %collective-permute-done.6.refs_1_ = f32[256,128]{1,0:T(8,128)S(1)} collective-permute-done((f32[256,128]{1,0:T(8,128)S(1)}, f32[256,128]{1,0:T(8,128)S(1)}, u32[]{:S(2)}, u32[]{:S(2)}) %collective-permute-start.6) | collective-permute-done | bytes 131104 | tf_op jit(solution)/shard_map/ppermute | solution.py:381
  32.2 2.5 %shard_map.98 = (f32[2,256,256]{2,1,0:T(8,128)S(1)}, f32[256,256]{1,0:T(8,128)S(1)}, bf16[6,512,256]{2,1,0:T(8,128)(2,1)S(1)}) custom-call(s32[5,8]{1,0:T(8,128)S(1)} %concatenate.7.offs, f32[256,256]{1,0:T(8,128)S(1)} %collective-permute-done.12.taken, f32[2,256,256]{2,1,0:T(8,128)} %probe_from.1, f32[1,2,256,256]{3,2,1,0:T(8,128)} %measured.3, ...), custom_call_target="tpu_custom_call" | custom-call | flops 201326592 | bytes 5505024 | tf_op jit(solution)/shard_map/pallas_call | solution.py:364
  34.7 3.5 %collective-permute-done.8.refs_3_ = f32[256,128]{1,0:T(8,128)S(1)} collective-permute-done((f32[256,128]{1,0:T(8,128)S(1)}, f32[256,128]{1,0:T(8,128)S(1)}, u32[]{:S(2)}, u32[]{:S(2)}) %collective-permute-start.8) | collective-permute-done | bytes 131104 | tf_op jit(solution)/shard_map/ppermute | solution.py:381
  38.3 1.0 %collective-permute-done.10.refs_5_ = f32[256,128]{1,0:T(8,128)S(1)} collective-permute-done((f32[256,128]{1,0:T(8,128)S(1)}, f32[256,128]{1,0:T(8,128)S(1)}, u32[]{:S(2)}, u32[]{:S(2)}) %collective-permute-start.10) | collective-permute-done | bytes 131104 | tf_op jit(solution)/shard_map/ppermute | solution.py:381
  39.3 4.2 %shard_map.99 = (f32[768,128]{1,0:T(8,128)S(1)}, f32[256,128]{1,0:T(8,128)S(1)}, f32[256,128]{1,0:T(8,128)S(1)}, f32[256,128]{1,0:T(8,128)S(1)}, f32[256,128]{1,...) custom-call(s32[5,8]{1,0:T(8,128)S(1)} %concatenate.7.offs, ...), custom_call_target="tpu_custom_call" | custom-call | flops 1610612736 | bytes 5120000 | tf_op jit(solution)/shard_map/pallas_call | solution.py:364
  43.5 0.4 collective-permute-start.13
  43.9 1.0 collective-permute-start.14
  44.8 1.5 %collective-permute-start.15 = (f32[256,128]{1,0:T(8,128)S(1)}, f32[256,128]{1,0:T(8,128)S(1)}, u32[]{:S(2)}, u32[]{:S(2)}) collective-permute-start(f32[256,128]{1,0:T(8,128)S(1)} %get-tuple-element.66), channel_id=1, source_target_pairs={{0,2},{1,3},{2,0},{3,1},{4,6},{5,7},{6,4},{7,5},{8,10},{9,11},{10,... | collective-permute-start | bytes 393224 | tf_op jit(solution)/shard_map/ppermute | solution.py:381
  46.3 1.3 %collective-permute-start.17 = (f32[256,128]{1,0:T(8,128)S(1)}, f32[256,128]{1,0:T(8,128)S(1)}, u32[]{:S(2)}, u32[]{:S(2)}) collective-permute-start(f32[256,128]{1,0:T(8,128)S(1)} %get-tuple-element.68), channel_id=1, source_target_pairs={{0,3},{1,2},{2,1},{3,0},{4,7},{5,6},{6,5},{7,4},{8,11},{9,10},{10,... | collective-permute-start | bytes 393224 | tf_op jit(solution)/shard_map/ppermute | solution.py:381
  47.6 1.9 %collective-permute-done.14.refs_1_ = f32[256,128]{1,0:T(8,128)S(1)} collective-permute-done((f32[256,128]{1,0:T(8,128)S(1)}, f32[256,128]{1,0:T(8,128)S(1)}, u32[]{:S(2)}, u32[]{:S(2)}) %collective-permute-start.14) | collective-permute-done | bytes 131104 | tf_op jit(solution)/shard_map/ppermute | solution.py:381
  49.5 2.5 %collective-permute-start.18 = (f32[256,128]{1,0:T(8,128)S(1)}, f32[256,128]{1,0:T(8,128)S(1)}, u32[]{:S(2)}, u32[]{:S(2)}) collective-permute-start(f32[256,128]{1,0:T(8,128)S(1)} %get-tuple-element.69), channel_id=1, source_target_pairs={{0,6},{1,7},{2,4},{3,5},{4,2},{5,3},{6,0},{7,1},{8,14},{9,15},{10,... | collective-permute-start | bytes 393224 | tf_op jit(solution)/shard_map/ppermute | solution.py:381
  52.1 0.6 collective-permute-start.20
  52.7 0.7 collective-permute-start.21
  53.4 2.3 %collective-permute-start.22 = (f32[128,128]{1,0:T(8,128)S(1)}, f32[128,128]{1,0:T(8,128)S(1)}, u32[]{:S(2)}, u32[]{:S(2)}) collective-permute-start(f32[128,128]{1,0:T(8,128)S(1)} %get-tuple-element.75), channel_id=1, source_target_pairs={{0,6},{2,4},{4,2},{6,0},{1,7},{3,5},{5,3},{7,1},{8,14},{10,12},{12... | collective-permute-start | bytes 196616 | tf_op jit(solution)/shard_map/ppermute | solution.py:381
  55.7 0.9 collective-permute-done.18.refs_5_
  56.6 2.4 %collective-permute-done.19.refs_6_ = f32[256,128]{1,0:T(8,128)S(1)} collective-permute-done((f32[256,128]{1,0:T(8,128)S(1)}, f32[256,128]{1,0:T(8,128)S(1)}, u32[]{:S(2)}, u32[]{:S(2)}) %collective-permute-start.19) | collective-permute-done | bytes 131104 | tf_op jit(solution)/shard_map/ppermute | solution.py:381
  58.9 1.7 %collective-permute-done.20.refs_8_ = f32[128,128]{1,0:T(8,128)S(1)} collective-permute-done((f32[128,128]{1,0:T(8,128)S(1)}, f32[128,128]{1,0:T(8,128)S(1)}, u32[]{:S(2)}, u32[]{:S(2)}) %collective-permute-start.20) | collective-permute-done | bytes 65568 | tf_op jit(solution)/shard_map/ppermute | solution.py:381
  60.6 1.3 %collective-permute-done.22.refs_10_ = f32[128,128]{1,0:T(8,128)S(1)} collective-permute-done((f32[128,128]{1,0:T(8,128)S(1)}, f32[128,128]{1,0:T(8,128)S(1)}, u32[]{:S(2)}, u32[]{:S(2)}) %collective-permute-start.22) | collective-permute-done | bytes 65568 | tf_op jit(solution)/shard_map/ppermute | solution.py:381
  61.9 1.0 %shard_map.102 = (f32[2,256,128]{2,1,0:T(8,128)S(1)}, f32[64,256]{1,0:T(8,128)S(1)}) custom-call(s32[5,8]{1,0:T(8,128)S(1)} %concatenate.7.offs, f32[768,128]{1,0:T(8,128)S(1)} %collective-permute-done.13.refs_0_.got, f32[256,128]{1,0:T(8,128)S(1)} %collective-permute-done.14.refs_1_, f32[256,128]{1,0:T(8,128)S(1)} %collective-permute-done.15.refs_2_, ...), custom_call_target="tpu_custom_call" | custom-call | flops 2097152 | bytes 1900544 | tf_op jit(solution)/shard_map/pallas_call | solution.py:364
  62.9 3.5 %collective-permute-start.23 = (f32[2,256,128]{2,1,0:T(8,128)S(1)}, f32[2,256,128]{2,1,0:T(8,128)S(1)}, u32[]{:S(2)}, u32[]{:S(2)}) collective-permute-start(f32[2,256,128]{2,1,0:T(8,128)S(1)} %get-tuple-element.77), channel_id=1, source_target_pairs={{0,8},{8,16},{16,24},{1,9},{9,17},{17,25},{2,10},{10,18},{18,26},{... | collective-permute-start | bytes 786440 | tf_op jit(solution)/shard_map/ppermute | solution.py:459
  66.4 1.6 %collective-permute-start.24 = (f32[64,256]{1,0:T(8,128)S(1)}, f32[64,256]{1,0:T(8,128)S(1)}, u32[]{:S(2)}, u32[]{:S(2)}) collective-permute-start(f32[64,256]{1,0:T(8,128)S(1)} %get-tuple-element.82), channel_id=1, source_target_pairs={{0,8},{8,0},{16,24},{24,16},{1,9},{9,1},{17,25},{25,17},{2,10},{10... | collective-permute-start | bytes 196616 | tf_op jit(solution)/shard_map/ppermute | solution.py:462
  68.1 1.5 %shard_map.100.own = f32[4,256,128]{2,1,0:T(8,128)S(1)} custom-call(s32[5,8]{1,0:T(8,128)S(1)} %concatenate.7.offs, f32[768,128]{1,0:T(8,128)S(1)} %collective-permute-done.13.refs_0_.got, f32[256,128]{1,0:T(8,128)S(1)} %collective-permute-done.14.refs_1_, f32[256,128]{1,0:T(8,128)S(1)} %collective-permute-done.15.refs_2_, ...), custom_call_target="tpu_custom_call" | custom-call | flops 4194304 | bytes 1835008 | tf_op jit(solution)/shard_map/pallas_call | solution.py:364
  69.6 3.2 %collective-permute-done.23.above = f32[2,256,128]{2,1,0:T(8,128)S(1)} collective-permute-done((f32[2,256,128]{2,1,0:T(8,128)S(1)}, f32[2,256,128]{2,1,0:T(8,128)S(1)}, u32[]{:S(2)}, u32[]{:S(2)}) %collective-permute-start.23) | collective-permute-done | bytes 262176 | tf_op jit(solution)/shard_map/ppermute | solution.py:459
  72.8 0.6 collective-permute-done.24
  73.5 2.2 %collective-permute-start.28 = (f32[64,256]{1,0:T(8,128)S(1)}, f32[64,256]{1,0:T(8,128)S(1)}, u32[]{:S(2)}, u32[]{:S(2)}) collective-permute-start(f32[64,256]{1,0:T(8,128)S(1)} %add.8), channel_id=1, source_target_pairs={{0,16},{8,24},{16,0},{24,8},{1,17},{9,25},{17,1},{25,9},{2,18},{10... | collective-permute-start | bytes 196616 | tf_op jit(solution)/shard_map/ppermute | solution.py:389
  75.7 3.7 %collective-permute-done.28 = f32[64,256]{1,0:T(8,128)S(1)} collective-permute-done((f32[64,256]{1,0:T(8,128)S(1)}, f32[64,256]{1,0:T(8,128)S(1)}, u32[]{:S(2)}, u32[]{:S(2)}) %collective-permute-start.28) | collective-permute-done | bytes 65568 | tf_op jit(solution)/shard_map/ppermute | solution.py:389
  79.4 7.5 %all-gather = f32[256,256]{1,0:T(8,128)S(1)} all-gather(f32[64,256]{1,0:T(8,128)S(1)} %add.9), channel_id=2, replica_groups=mesh['pair'=4,'half'=2,'col'=2,'core'=2] {'half','col'}, dimensions={0}, use_global_device_ids=true | all-gather | bytes 327680 | tf_op jit(solution)/shard_map/all_gather | solution.py:471
  86.9 2.1 %collective-permute-start.25 = (f32[256,128]{1,0:T(8,128)S(1)}, f32[256,128]{1,0:T(8,128)S(1)}, u32[]{:S(2)}, u32[]{:S(2)}) collective-permute-start(f32[256,128]{1,0:T(8,128)S(1)} %get-tuple-element.83), channel_id=1, source_target_pairs={{0,4},{2,6},{4,0},{6,2},{1,5},{3,7},{5,1},{7,3},{8,12},{10,14},{12... | collective-permute-start | bytes 393224 | tf_op jit(solution)/shard_map/ppermute | solution.py:381
  89.1 1.5 %collective-permute-start.27 = (f32[256,128]{1,0:T(8,128)S(1)}, f32[256,128]{1,0:T(8,128)S(1)}, u32[]{:S(2)}, u32[]{:S(2)}) collective-permute-start(f32[256,128]{1,0:T(8,128)S(1)} %get-tuple-element.85), channel_id=1, source_target_pairs={{0,6},{2,4},{4,2},{6,0},{1,7},{3,5},{5,3},{7,1},{8,14},{10,12},{12... | collective-permute-start | bytes 393224 | tf_op jit(solution)/shard_map/ppermute | solution.py:381
  90.5 2.5 %collective-permute-done.25.refs_0_ = f32[256,128]{1,0:T(8,128)S(1)} collective-permute-done((f32[256,128]{1,0:T(8,128)S(1)}, f32[256,128]{1,0:T(8,128)S(1)}, u32[]{:S(2)}, u32[]{:S(2)}) %collective-permute-start.25) | collective-permute-done | bytes 131104 | tf_op jit(solution)/shard_map/ppermute | solution.py:381
  93.1 2.2 %collective-permute-done.26.refs_1_ = f32[256,128]{1,0:T(8,128)S(1)} collective-permute-done((f32[256,128]{1,0:T(8,128)S(1)}, f32[256,128]{1,0:T(8,128)S(1)}, u32[]{:S(2)}, u32[]{:S(2)}) %collective-permute-start.26) | collective-permute-done | bytes 131104 | tf_op jit(solution)/shard_map/ppermute | solution.py:381
  95.3 1.8 %collective-permute-done.27.refs_2_ = f32[256,128]{1,0:T(8,128)S(1)} collective-permute-done((f32[256,128]{1,0:T(8,128)S(1)}, f32[256,128]{1,0:T(8,128)S(1)}, u32[]{:S(2)}, u32[]{:S(2)}) %collective-permute-start.27) | collective-permute-done | bytes 131104 | tf_op jit(solution)/shard_map/ppermute | solution.py:381
  97.1 1.1 %shard_map.104 = (f32[4,256,128]{2,1,0:T(8,128)}, f32[512,256]{1,0:T(8,128)}) custom-call(f32[256,128]{1,0:T(8,128)S(1)} %collective-permute-done.25.refs_0_, f32[256,128]{1,0:T(8,128)S(1)} %collective-permute-done.26.refs_1_, f32[256,128]{1,0:T(8,128)S(1)} %collective-permute-done.27.refs_2_, f32[256,128]{1,0:T(8,128)S(1)} %get-tuple-element.86.refs_3_, ...), custom_call_target="tpu_custom_call" | custom-call | bytes 2097152 | tf_op jit(solution)/shard_map/pallas_call | solution.py:364
  (36 shorter events, 1.0 us)
Async XLA Ops:
  1.9 7.3 %collective-permute-start = (f32[264,128]{1,0:T(8,128)S(1)}, f32[264,128]{1,0:T(8,128)S(1)}, u32[]{:S(2)}, u32[]{:S(2)}) collective-permute-start(f32[264,128]{1,0:T(8,128)S(1)} %get-tuple-element.47), channel_id=1, source_target_pairs={{0,2},{2,0},{4,6},{6,4},{1,3},{3,1},{5,7},{7,5},{8,10},{10,8},{12,... | collective-permute-start | bytes 405512 | tf_op jit(solution)/shard_map/ppermute | solution.py:381
  4.9 7.9 %collective-permute-start.1 = (f32[264,128]{1,0:T(8,128)S(1)}, f32[264,128]{1,0:T(8,128)S(1)}, u32[]{:S(2)}, u32[]{:S(2)}) collective-permute-start(f32[264,128]{1,0:T(8,128)S(1)} %get-tuple-element.48), channel_id=1, source_target_pairs={{0,4},{2,6},{4,0},{6,2},{1,5},{3,7},{5,1},{7,3},{8,12},{10,14},{12... | collective-permute-start | bytes 405512 | tf_op jit(solution)/shard_map/ppermute | solution.py:381
  6.4 6.5 %collective-permute-start.2 = (f32[264,128]{1,0:T(8,128)S(1)}, f32[264,128]{1,0:T(8,128)S(1)}, u32[]{:S(2)}, u32[]{:S(2)}) collective-permute-start(f32[264,128]{1,0:T(8,128)S(1)} %get-tuple-element.49), channel_id=1, source_target_pairs={{0,6},{2,4},{4,2},{6,0},{1,7},{3,5},{5,3},{7,1},{8,14},{10,12},{12... | collective-permute-start | bytes 405512 | tf_op jit(solution)/shard_map/ppermute | solution.py:381
  13.1 3.0 %collective-permute-start.3 = (s32[4,4]{1,0:T(4,128)S(1)}, s32[4,4]{1,0:T(4,128)S(1)}, u32[]{:S(2)}, u32[]{:S(2)}) collective-permute-start(s32[4,4]{1,0:T(4,128)S(1)} %maximum_convert_fusion), channel_id=1, source_target_pairs={{0,1},{1,0},{2,3},{3,2},{4,5},{5,4},{6,7},{7,6},{8,9},{9,8},{10,11... | collective-permute-start | bytes 200 | tf_op jit(solution)/shard_map/ppermute | solution.py:419
  13.2 10.6 %collective-permute-start.4 = (f32[2,256,128]{2,1,0:T(8,128)S(1)}, f32[2,256,128]{2,1,0:T(8,128)S(1)}, u32[]{:S(2)}, u32[]{:S(2)}) collective-permute-start(f32[2,256,128]{2,1,0:T(8,128)S(1)} %shard_map.96), channel_id=1, source_target_pairs={{8,0},{16,8},{24,16},{9,1},{17,9},{25,17},{10,2},{18,10},{26,18},{... | collective-permute-start | bytes 786440 | tf_op jit(solution)/shard_map/ppermute | solution.py:414
  14.5 14.5 %collective-permute-start.12 = (f32[256,256]{1,0:T(8,128)S(1)}, f32[256,256]{1,0:T(8,128)S(1)}, u32[]{:S(2)}, u32[]{:S(2)}) collective-permute-start(f32[256,256]{1,0:T(8,128)S(1)} %get-tuple-element.60), channel_id=1, source_target_pairs={{0,4},{4,0},{1,5},{5,1},{2,6},{6,2},{3,7},{7,3},{8,12},{12,8},{9,1... | collective-permute-start | bytes 786440 | tf_op jit(solution)/shard_map/ppermute | solution.py:415
  25.2 5.3 %collective-permute-start.5 = (f32[256,128]{1,0:T(8,128)S(1)}, f32[256,128]{1,0:T(8,128)S(1)}, u32[]{:S(2)}, u32[]{:S(2)}) collective-permute-start(f32[256,128]{1,0:T(8,128)S(1)} %get-tuple-element.52), channel_id=1, source_target_pairs={{0,2},{1,3},{2,0},{3,1},{4,6},{5,7},{6,4},{7,5},{8,10},{9,11},{10,... | collective-permute-start | bytes 393224 | tf_op jit(solution)/shard_map/ppermute | solution.py:381
  26.4 5.8 %collective-permute-start.6 = (f32[256,128]{1,0:T(8,128)S(1)}, f32[256,128]{1,0:T(8,128)S(1)}, u32[]{:S(2)}, u32[]{:S(2)}) collective-permute-start(f32[256,128]{1,0:T(8,128)S(1)} %get-tuple-element.53), channel_id=1, source_target_pairs={{0,4},{1,5},{2,6},{3,7},{4,0},{5,1},{6,2},{7,3},{8,12},{9,13},{10,... | collective-permute-start | bytes 393224 | tf_op jit(solution)/shard_map/ppermute | solution.py:381
  27.3 7.4 %collective-permute-start.7 = (f32[256,128]{1,0:T(8,128)S(1)}, f32[256,128]{1,0:T(8,128)S(1)}, u32[]{:S(2)}, u32[]{:S(2)}) collective-permute-start(f32[256,128]{1,0:T(8,128)S(1)} %get-tuple-element.54), channel_id=1, source_target_pairs={{0,3},{1,2},{2,1},{3,0},{4,7},{5,6},{6,5},{7,4},{8,11},{9,10},{10,... | collective-permute-start | bytes 393224 | tf_op jit(solution)/shard_map/ppermute | solution.py:381
  27.5 10.7 %collective-permute-start.8 = (f32[256,128]{1,0:T(8,128)S(1)}, f32[256,128]{1,0:T(8,128)S(1)}, u32[]{:S(2)}, u32[]{:S(2)}) collective-permute-start(f32[256,128]{1,0:T(8,128)S(1)} %get-tuple-element.55), channel_id=1, source_target_pairs={{0,5},{1,4},{2,7},{3,6},{4,1},{5,0},{6,3},{7,2},{8,13},{9,12},{10,... | collective-permute-start | bytes 393224 | tf_op jit(solution)/shard_map/ppermute | solution.py:381
  29.0 9.2 %collective-permute-start.9 = (f32[256,128]{1,0:T(8,128)S(1)}, f32[256,128]{1,0:T(8,128)S(1)}, u32[]{:S(2)}, u32[]{:S(2)}) collective-permute-start(f32[256,128]{1,0:T(8,128)S(1)} %get-tuple-element.56), channel_id=1, source_target_pairs={{0,6},{1,7},{2,4},{3,5},{4,2},{5,3},{6,0},{7,1},{8,14},{9,15},{10,... | collective-permute-start | bytes 393224 | tf_op jit(solution)/shard_map/ppermute | solution.py:381
  30.5 8.7 %collective-permute-start.10 = (f32[256,128]{1,0:T(8,128)S(1)}, f32[256,128]{1,0:T(8,128)S(1)}, u32[]{:S(2)}, u32[]{:S(2)}) collective-permute-start(f32[256,128]{1,0:T(8,128)S(1)} %get-tuple-element.57), channel_id=1, source_target_pairs={{0,7},{1,6},{2,5},{3,4},{4,3},{5,2},{6,1},{7,0},{8,15},{9,14},{10,... | collective-permute-start | bytes 393224 | tf_op jit(solution)/shard_map/ppermute | solution.py:381
  32.2 7.1 %copy-start = (f32[2,136,128]{2,1,0:T(8,128)S(1)}, f32[2,136,128]{2,1,0:T(8,128)}, u32[]{:S(2)}) copy-start(f32[2,136,128]{2,1,0:T(8,128)} %constant.17.clone.refs_11_) | copy-start | bytes 417796
  32.2 7.1 %collective-permute-start.11 = (f32[256,128]{1,0:T(8,128)S(1)}, f32[256,128]{1,0:T(8,128)S(1)}, u32[]{:S(2)}, u32[]{:S(2)}) collective-permute-start(f32[256,128]{1,0:T(8,128)S(1)} %get-tuple-element.58), channel_id=1, source_target_pairs={{0,1},{1,0},{2,3},{3,2},{4,5},{5,4},{6,7},{7,6},{8,9},{9,8},{10,11... | collective-permute-start | bytes 393224 | tf_op jit(solution)/shard_map/ppermute | solution.py:381
  43.5 8.6 %collective-permute-start.13 = (f32[768,128]{1,0:T(8,128)S(1)}, f32[768,128]{1,0:T(8,128)S(1)}, u32[]{:S(2)}, u32[]{:S(2)}) collective-permute-start(f32[768,128]{1,0:T(8,128)S(1)} %get-tuple-element.64), channel_id=1, source_target_pairs={{0,1},{1,0},{2,3},{3,2},{4,5},{5,4},{6,7},{7,6},{8,9},{9,8},{10,11... | collective-permute-start | bytes 1179656 | tf_op jit(solution)/shard_map/ppermute | solution.py:381
  43.9 5.7 %collective-permute-start.14 = (f32[256,128]{1,0:T(8,128)S(1)}, f32[256,128]{1,0:T(8,128)S(1)}, u32[]{:S(2)}, u32[]{:S(2)}) collective-permute-start(f32[256,128]{1,0:T(8,128)S(1)} %get-tuple-element.65), channel_id=1, source_target_pairs={{0,4},{1,5},{2,6},{3,7},{4,0},{5,1},{6,2},{7,3},{8,12},{9,13},{10,... | collective-permute-start | bytes 393224 | tf_op jit(solution)/shard_map/ppermute | solution.py:381
  44.8 7.3 %collective-permute-start.15 = (f32[256,128]{1,0:T(8,128)S(1)}, f32[256,128]{1,0:T(8,128)S(1)}, u32[]{:S(2)}, u32[]{:S(2)}) collective-permute-start(f32[256,128]{1,0:T(8,128)S(1)} %get-tuple-element.66), channel_id=1, source_target_pairs={{0,2},{1,3},{2,0},{3,1},{4,6},{5,7},{6,4},{7,5},{8,10},{9,11},{10,... | collective-permute-start | bytes 393224 | tf_op jit(solution)/shard_map/ppermute | solution.py:381
  46.3 6.4 %collective-permute-start.16 = (f32[256,128]{1,0:T(8,128)S(1)}, f32[256,128]{1,0:T(8,128)S(1)}, u32[]{:S(2)}, u32[]{:S(2)}) collective-permute-start(f32[256,128]{1,0:T(8,128)S(1)} %get-tuple-element.67), channel_id=1, source_target_pairs={{0,5},{1,4},{2,7},{3,6},{4,1},{5,0},{6,3},{7,2},{8,13},{9,12},{10,... | collective-permute-start | bytes 393224 | tf_op jit(solution)/shard_map/ppermute | solution.py:381
  46.3 7.1 %collective-permute-start.17 = (f32[256,128]{1,0:T(8,128)S(1)}, f32[256,128]{1,0:T(8,128)S(1)}, u32[]{:S(2)}, u32[]{:S(2)}) collective-permute-start(f32[256,128]{1,0:T(8,128)S(1)} %get-tuple-element.68), channel_id=1, source_target_pairs={{0,3},{1,2},{2,1},{3,0},{4,7},{5,6},{6,5},{7,4},{8,11},{9,10},{10,... | collective-permute-start | bytes 393224 | tf_op jit(solution)/shard_map/ppermute | solution.py:381
  49.5 7.0 %collective-permute-start.18 = (f32[256,128]{1,0:T(8,128)S(1)}, f32[256,128]{1,0:T(8,128)S(1)}, u32[]{:S(2)}, u32[]{:S(2)}) collective-permute-start(f32[256,128]{1,0:T(8,128)S(1)} %get-tuple-element.69), channel_id=1, source_target_pairs={{0,6},{1,7},{2,4},{3,5},{4,2},{5,3},{6,0},{7,1},{8,14},{9,15},{10,... | collective-permute-start | bytes 393224 | tf_op jit(solution)/shard_map/ppermute | solution.py:381
  52.1 6.9 %collective-permute-start.19 = (f32[256,128]{1,0:T(8,128)S(1)}, f32[256,128]{1,0:T(8,128)S(1)}, u32[]{:S(2)}, u32[]{:S(2)}) collective-permute-start(f32[256,128]{1,0:T(8,128)S(1)} %get-tuple-element.70), channel_id=1, source_target_pairs={{0,7},{1,6},{2,5},{3,4},{4,3},{5,2},{6,1},{7,0},{8,15},{9,14},{10,... | collective-permute-start | bytes 393224 | tf_op jit(solution)/shard_map/ppermute | solution.py:381
  52.1 8.5 %collective-permute-start.20 = (f32[128,128]{1,0:T(8,128)S(1)}, f32[128,128]{1,0:T(8,128)S(1)}, u32[]{:S(2)}, u32[]{:S(2)}) collective-permute-start(f32[128,128]{1,0:T(8,128)S(1)} %get-tuple-element.73), channel_id=1, source_target_pairs={{0,4},{2,6},{4,0},{6,2},{1,5},{3,7},{5,1},{7,3},{8,12},{10,14},{12... | collective-permute-start | bytes 196616 | tf_op jit(solution)/shard_map/ppermute | solution.py:381
  52.7 7.9 %collective-permute-start.21 = (f32[128,128]{1,0:T(8,128)S(1)}, f32[128,128]{1,0:T(8,128)S(1)}, u32[]{:S(2)}, u32[]{:S(2)}) collective-permute-start(f32[128,128]{1,0:T(8,128)S(1)} %get-tuple-element.74), channel_id=1, source_target_pairs={{0,2},{2,0},{4,6},{6,4},{1,3},{3,1},{5,7},{7,5},{8,10},{10,8},{12,... | collective-permute-start | bytes 196616 | tf_op jit(solution)/shard_map/ppermute | solution.py:381
  53.4 8.5 %collective-permute-start.22 = (f32[128,128]{1,0:T(8,128)S(1)}, f32[128,128]{1,0:T(8,128)S(1)}, u32[]{:S(2)}, u32[]{:S(2)}) collective-permute-start(f32[128,128]{1,0:T(8,128)S(1)} %get-tuple-element.75), channel_id=1, source_target_pairs={{0,6},{2,4},{4,2},{6,0},{1,7},{3,5},{5,3},{7,1},{8,14},{10,12},{12... | collective-permute-start | bytes 196616 | tf_op jit(solution)/shard_map/ppermute | solution.py:381
  62.9 9.8 %collective-permute-start.23 = (f32[2,256,128]{2,1,0:T(8,128)S(1)}, f32[2,256,128]{2,1,0:T(8,128)S(1)}, u32[]{:S(2)}, u32[]{:S(2)}) collective-permute-start(f32[2,256,128]{2,1,0:T(8,128)S(1)} %get-tuple-element.77), channel_id=1, source_target_pairs={{0,8},{8,16},{16,24},{1,9},{9,17},{17,25},{2,10},{10,18},{18,26},{... | collective-permute-start | bytes 786440 | tf_op jit(solution)/shard_map/ppermute | solution.py:459
  66.4 7.0 %collective-permute-start.24 = (f32[64,256]{1,0:T(8,128)S(1)}, f32[64,256]{1,0:T(8,128)S(1)}, u32[]{:S(2)}, u32[]{:S(2)}) collective-permute-start(f32[64,256]{1,0:T(8,128)S(1)} %get-tuple-element.82), channel_id=1, source_target_pairs={{0,8},{8,0},{16,24},{24,16},{1,9},{9,1},{17,25},{25,17},{2,10},{10... | collective-permute-start | bytes 196616 | tf_op jit(solution)/shard_map/ppermute | solution.py:462
  73.5 5.9 %collective-permute-start.28 = (f32[64,256]{1,0:T(8,128)S(1)}, f32[64,256]{1,0:T(8,128)S(1)}, u32[]{:S(2)}, u32[]{:S(2)}) collective-permute-start(f32[64,256]{1,0:T(8,128)S(1)} %add.8), channel_id=1, source_target_pairs={{0,16},{8,24},{16,0},{24,8},{1,17},{9,25},{17,1},{25,9},{2,18},{10... | collective-permute-start | bytes 196616 | tf_op jit(solution)/shard_map/ppermute | solution.py:389
  86.9 10.2 %collective-permute-start.29 = (f32[4,64,256]{2,1,0:T(8,128)S(1)}, f32[4,64,256]{2,1,0:T(8,128)S(1)}, u32[]{:S(2)}, u32[]{:S(2)}) collective-permute-start(f32[4,64,256]{2,1,0:T(8,128)S(1)} %bitcast.10), channel_id=1, source_target_pairs={{0,1},{1,0},{2,3},{3,2},{4,5},{5,4},{6,7},{7,6},{8,9},{9,8},{10,11... | collective-permute-start | bytes 786440 | tf_op jit(solution)/shard_map/ppermute | solution.py:472
  86.9 6.2 %collective-permute-start.25 = (f32[256,128]{1,0:T(8,128)S(1)}, f32[256,128]{1,0:T(8,128)S(1)}, u32[]{:S(2)}, u32[]{:S(2)}) collective-permute-start(f32[256,128]{1,0:T(8,128)S(1)} %get-tuple-element.83), channel_id=1, source_target_pairs={{0,4},{2,6},{4,0},{6,2},{1,5},{3,7},{5,1},{7,3},{8,12},{10,14},{12... | collective-permute-start | bytes 393224 | tf_op jit(solution)/shard_map/ppermute | solution.py:381
  89.0 6.3 %collective-permute-start.26 = (f32[256,128]{1,0:T(8,128)S(1)}, f32[256,128]{1,0:T(8,128)S(1)}, u32[]{:S(2)}, u32[]{:S(2)}) collective-permute-start(f32[256,128]{1,0:T(8,128)S(1)} %get-tuple-element.84), channel_id=1, source_target_pairs={{0,2},{2,0},{4,6},{6,4},{1,3},{3,1},{5,7},{7,5},{8,10},{10,8},{12,... | collective-permute-start | bytes 393224 | tf_op jit(solution)/shard_map/ppermute | solution.py:381
  89.1 8.0 %collective-permute-start.27 = (f32[256,128]{1,0:T(8,128)S(1)}, f32[256,128]{1,0:T(8,128)S(1)}, u32[]{:S(2)}, u32[]{:S(2)}) collective-permute-start(f32[256,128]{1,0:T(8,128)S(1)} %get-tuple-element.85), channel_id=1, source_target_pairs={{0,6},{2,4},{4,2},{6,0},{1,7},{3,5},{5,3},{7,1},{8,14},{10,12},{12... | collective-permute-start | bytes 393224 | tf_op jit(solution)/shard_map/ppermute | solution.py:381

commit v22 on v19

--- a/solution.py
+++ b/solution.py
@@ -310,16 +310,20 @@
 
 
 def add_below_kernel(offs, *refs):
-    parts, quarters, (below, probe_band) = refs[:8], refs[8:12], refs[12:]
+    parts, below = refs[:8], refs[8]
     rows, cols = below.shape[1:]
     sums = add_parts(offs, parts, 2, rows, cols)
     col = here()[1]
     for side in range(2):
         below[jnp.bitwise_xor(col, side)] = sums[side]
+
+
+def band_kernel(*refs):
+    quarters, out = refs[:4], refs[4]
     total = (quarters[0][...] + quarters[1][...]) + (quarters[2][...] + quarters[3][...])
-    band = probe_band.shape[0]
-    probe_band[:, :cols] = total[:band]
-    probe_band[:, cols:] = total[band:]
+    band, cols = out.shape[0], total.shape[1]
+    out[:, :cols] = total[:band]
+    out[:, cols:] = total[band:]
 
 
 def add_own_kernel(offs, *refs):
@@ -444,13 +448,11 @@
     )
     got = deal(grad, PLANE, BACK)
     quarters = call(pair_kernel, [shape(2 * band, cols)] * 4, (), (keep, got[0]), 4 * band * width)
-    lower_sums, probe_band = call(
-        add_below_kernel,
-        [shape(2, rows, cols), shape(band, width)],
-        scalars,
-        (*got, *deal(quarters, PLANE[:2], FOUR)),
-        32 * rows * width,
-    )
+    quarters = deal(quarters, PLANE[:2], FOUR)
+    *got, first, second = lax.optimization_barrier((*got, *quarters[:2]))
+    (lower_sums,) = call(add_below_kernel, [shape(2, rows, cols)], scalars, got, 32 * rows * width)
+    quarters = [first, second, *quarters[2:]]
+    (probe_band,) = call(band_kernel, [shape(band, width)], (), quarters, 4 * band * width)
     above = lax.ppermute(lower_sums, "pair", [(k, k + 1) for k in range(pairs - 1)])
     doubling = pairs > 1 and pairs & (pairs - 1) == 0
     if doubling:

time: 89.5 us -> 90.4 us (1.010)
  waiting for transfers between devices: 28.9 us -> 31 us
  starting transfers between devices: 34.5 us -> 32.8 us
    ppermute x23, waiting for transfers between devices: 17.2 us -> 21.6 us  [deal(): lax.ppermute(value, axes, [(k, k ^ turn) for k in range(len(order))])]
    ppermute x1, waiting for transfers between devices: 3.18 us -> 0.01 us  [local(): lax.ppermute(lower_sums, 'pair', [(k, k + 1) for k in range(pairs - 1)])]
    ppermute x1, starting transfers between devices: 2.21 us -> 1.08 us  [sum_over(): lax.ppermute(value, axis, [(k, k ^ step) for k in range(size)])]
    pallas_call x10 -> x11, Pallas kernels: 13 us -> 13 us  [call(): pl.pallas_call(kernel, out_shape=[x for x, unused in outs], in_specs=[SME...]
  transfers between devices with their start and end apart: 29 -> 29, of which waited for: 13 -> 12; matrix products, arithmetic and copies ran while one was open for 2% -> 2% of each run, Pallas kernels for 6% -> 6%
where the time goes in v22:
time: 90.4 us; the launch traced here: 90.2 us
  starting transfers between devices  32.8 us (36%)
  waiting for transfers between devices  31 us (34%)
  Pallas kernels  13 us (14%)
  blocking collectives  9.35 us (10%)
  between operations  2.08 us (2%)
  local copies, waits for them, and re-layouts  1.79 us (2%)
    ppermute x23, starting transfers between devices, deal(): lax.ppermute(value, axes, [(k, k ^ turn) for k in range(len(order))])  23.7 us
    ppermute x23, waiting for transfers between devices, deal(): lax.ppermute(value, axes, [(k, k ^ turn) for k in range(len(order))])  21.6 us
    pallas_call x11, Pallas kernels, call(): pl.pallas_call(kernel, out_shape=[x for x, unused in outs], in_specs=[SME...  13 us
    all_gather x1, blocking collectives, local(): probe_grad = lax.all_gather(probe_band, PLANE, axis=0, tiled=True)  9.35 us
    ppermute x1, waiting for transfers between devices, local(): below = lax.ppermute(lowest, 'pair', [(k, k - 1) for k in range(1, pairs)])  7.61 us
    ppermute x1, starting transfers between devices, local(): lax.ppermute(lower_sums, 'pair', [(k, k + 1) for k in range(pairs - 1)])  3.49 us
  transfers between devices with their start and end apart: 29, of which 12 were waited for; matrix products, arithmetic and copies ran while one was open for 2% of the time, Pallas kernels for 6%

profile of v22, /device:TPU:0, one launch (start us, length us, event | category | flops | bytes accessed | tf_op | source)
XLA Modules:
  0.0 90.2 jit_solution(15991323740220403615)
XLA Ops:
  0.6 1.3 %shard_map.95 = (f32[264,128]{1,0:T(8,128)S(1)}, f32[264,128]{1,0:T(8,128)S(1)}, f32[264,128]{1,0:T(8,128)S(1)}, f32[264,128]{1,0:T(8,128)S(1)}, f32[256,256]{1,0:T(8,128)S(1)}) custom-call(f32[4,256,128]{2,1,0:T(8,128)} %bitcast.9, f32[1,2,256,256]{3,2,1,0:T(8,128)} %measured.3, s32[1,2,2]{2,1,0:T(2,128)} %offsets_from.1), custom_call_target="tpu_custom_call" | custom-call | bytes 1851408 | tf_op jit(solution)/shard_map/pallas_call | solution.py:363
  1.9 3.0 %collective-permute-start = (f32[264,128]{1,0:T(8,128)S(1)}, f32[264,128]{1,0:T(8,128)S(1)}, u32[]{:S(2)}, u32[]{:S(2)}) collective-permute-start(f32[264,128]{1,0:T(8,128)S(1)} %get-tuple-element.55), channel_id=1, source_target_pairs={{0,2},{2,0},{4,6},{6,4},{1,3},{3,1},{5,7},{7,5},{8,10},{10,8},{12,... | collective-permute-start | bytes 405512 | tf_op jit(solution)/shard_map/ppermute | solution.py:380
  4.9 1.5 %collective-permute-start.1 = (f32[264,128]{1,0:T(8,128)S(1)}, f32[264,128]{1,0:T(8,128)S(1)}, u32[]{:S(2)}, u32[]{:S(2)}) collective-permute-start(f32[264,128]{1,0:T(8,128)S(1)} %get-tuple-element.56), channel_id=1, source_target_pairs={{0,4},{2,6},{4,0},{6,2},{1,5},{3,7},{5,1},{7,3},{8,12},{10,14},{12... | collective-permute-start | bytes 405512 | tf_op jit(solution)/shard_map/ppermute | solution.py:380
  6.6 1.3 %fusion = (s32[1,1]{1,0:T(1,128)}, s32[1,1]{1,0:T(1,128)}) fusion(s32[1,2]{1,0:T(1,128)} %param.11), kind=kLoop, calls=%fused_computation.8 | loop fusion | bytes 16 | tf_op jit(solution)/shard_map/slice | solution.py:420
  9.2 0.1 slice_reduce_fusion.2
  9.3 3.5 %collective-permute-done.1.refs_0_ = f32[264,128]{1,0:T(8,128)S(1)} collective-permute-done((f32[264,128]{1,0:T(8,128)S(1)}, f32[264,128]{1,0:T(8,128)S(1)}, u32[]{:S(2)}, u32[]{:S(2)}) %collective-permute-start.1) | collective-permute-done | bytes 135200 | tf_op jit(solution)/shard_map/ppermute | solution.py:380
  12.9 0.1 slice_reduce_fusion.1
  13.0 0.1 slice_reduce_fusion
  13.2 1.3 %collective-permute-start.4 = (f32[2,256,128]{2,1,0:T(8,128)S(1)}, f32[2,256,128]{2,1,0:T(8,128)S(1)}, u32[]{:S(2)}, u32[]{:S(2)}) collective-permute-start(f32[2,256,128]{2,1,0:T(8,128)S(1)} %shard_map.96), channel_id=1, source_target_pairs={{8,0},{16,8},{24,16},{9,1},{17,9},{25,17},{10,2},{18,10},{26,18},{... | collective-permute-start | bytes 786440 | tf_op jit(solution)/shard_map/ppermute | solution.py:413
  14.5 1.6 %collective-permute-start.12 = (f32[256,256]{1,0:T(8,128)S(1)}, f32[256,256]{1,0:T(8,128)S(1)}, u32[]{:S(2)}, u32[]{:S(2)}) collective-permute-start(f32[256,256]{1,0:T(8,128)S(1)} %get-tuple-element.68), channel_id=1, source_target_pairs={{0,4},{4,0},{1,5},{5,1},{2,6},{6,2},{3,7},{7,3},{8,12},{12,8},{9,1... | collective-permute-start | bytes 786440 | tf_op jit(solution)/shard_map/ppermute | solution.py:414
  16.2 7.6 %collective-permute-done.4.refs_4_ = f32[2,256,128]{2,1,0:T(8,128)S(1)} collective-permute-done((f32[2,256,128]{2,1,0:T(8,128)S(1)}, f32[2,256,128]{2,1,0:T(8,128)S(1)}, u32[]{:S(2)}, u32[]{:S(2)}) %collective-permute-start.4) | collective-permute-done | bytes 262176 | tf_op jit(solution)/shard_map/ppermute | solution.py:413
  23.8 1.3 %shard_map.97 = (f32[256,128]{1,0:T(8,128)S(1)}, f32[256,128]{1,0:T(8,128)S(1)}, f32[256,128]{1,0:T(8,128)S(1)}, f32[256,128]{1,0:T(8,128)S(1)}, f32[256,128]{1,...) custom-call(s32[5,8]{1,0:T(8,128)S(1)} %concatenate.7.offs, ...), custom_call_target="tpu_custom_call" | custom-call | flops 2097152 | bytes 1851392 | tf_op jit(solution)/shard_map/pallas_call | solution.py:363
  25.2 1.2 %collective-permute-start.5 = (f32[256,128]{1,0:T(8,128)S(1)}, f32[256,128]{1,0:T(8,128)S(1)}, u32[]{:S(2)}, u32[]{:S(2)}) collective-permute-start(f32[256,128]{1,0:T(8,128)S(1)} %get-tuple-element.60), channel_id=1, source_target_pairs={{0,2},{1,3},{2,0},{3,1},{4,6},{5,7},{6,4},{7,5},{8,10},{9,11},{10,... | collective-permute-start | bytes 393224 | tf_op jit(solution)/shard_map/ppermute | solution.py:380
  26.4 0.9 %collective-permute-start.6 = (f32[256,128]{1,0:T(8,128)S(1)}, f32[256,128]{1,0:T(8,128)S(1)}, u32[]{:S(2)}, u32[]{:S(2)}) collective-permute-start(f32[256,128]{1,0:T(8,128)S(1)} %get-tuple-element.61), channel_id=1, source_target_pairs={{0,4},{1,5},{2,6},{3,7},{4,0},{5,1},{6,2},{7,3},{8,12},{9,13},{10,... | collective-permute-start | bytes 393224 | tf_op jit(solution)/shard_map/ppermute | solution.py:380
  27.3 0.2 collective-permute-start.7
  27.5 1.5 %collective-permute-start.8 = (f32[256,128]{1,0:T(8,128)S(1)}, f32[256,128]{1,0:T(8,128)S(1)}, u32[]{:S(2)}, u32[]{:S(2)}) collective-permute-start(f32[256,128]{1,0:T(8,128)S(1)} %get-tuple-element.63), channel_id=1, source_target_pairs={{0,5},{1,4},{2,7},{3,6},{4,1},{5,0},{6,3},{7,2},{8,13},{9,12},{10,... | collective-permute-start | bytes 393224 | tf_op jit(solution)/shard_map/ppermute | solution.py:380
  29.0 1.5 %collective-permute-start.9 = (f32[256,128]{1,0:T(8,128)S(1)}, f32[256,128]{1,0:T(8,128)S(1)}, u32[]{:S(2)}, u32[]{:S(2)}) collective-permute-start(f32[256,128]{1,0:T(8,128)S(1)} %get-tuple-element.64), channel_id=1, source_target_pairs={{0,6},{1,7},{2,4},{3,5},{4,2},{5,3},{6,0},{7,1},{8,14},{9,15},{10,... | collective-permute-start | bytes 393224 | tf_op jit(solution)/shard_map/ppermute | solution.py:380
  30.5 0.7 collective-permute-start.10
  31.2 1.0 %collective-permute-done.6.refs_1_ = f32[256,128]{1,0:T(8,128)S(1)} collective-permute-done((f32[256,128]{1,0:T(8,128)S(1)}, f32[256,128]{1,0:T(8,128)S(1)}, u32[]{:S(2)}, u32[]{:S(2)}) %collective-permute-start.6) | collective-permute-done | bytes 131104 | tf_op jit(solution)/shard_map/ppermute | solution.py:380
  32.2 2.5 %shard_map.98 = (f32[2,256,256]{2,1,0:T(8,128)S(1)}, f32[256,256]{1,0:T(8,128)S(1)}, bf16[6,512,256]{2,1,0:T(8,128)(2,1)S(1)}) custom-call(s32[5,8]{1,0:T(8,128)S(1)} %concatenate.7.offs, f32[256,256]{1,0:T(8,128)S(1)} %collective-permute-done.12.taken, f32[2,256,256]{2,1,0:T(8,128)} %probe_from.1, f32[1,2,256,256]{3,2,1,0:T(8,128)} %measured.3, ...), custom_call_target="tpu_custom_call" | custom-call | flops 201326592 | bytes 5505024 | tf_op jit(solution)/shard_map/pallas_call | solution.py:363
  34.7 3.5 %collective-permute-done.8.refs_3_ = f32[256,128]{1,0:T(8,128)S(1)} collective-permute-done((f32[256,128]{1,0:T(8,128)S(1)}, f32[256,128]{1,0:T(8,128)S(1)}, u32[]{:S(2)}, u32[]{:S(2)}) %collective-permute-start.8) | collective-permute-done | bytes 131104 | tf_op jit(solution)/shard_map/ppermute | solution.py:380
  38.3 1.0 %collective-permute-done.10.refs_5_ = f32[256,128]{1,0:T(8,128)S(1)} collective-permute-done((f32[256,128]{1,0:T(8,128)S(1)}, f32[256,128]{1,0:T(8,128)S(1)}, u32[]{:S(2)}, u32[]{:S(2)}) %collective-permute-start.10) | collective-permute-done | bytes 131104 | tf_op jit(solution)/shard_map/ppermute | solution.py:380
  39.3 4.2 %shard_map.99 = (f32[768,128]{1,0:T(8,128)S(1)}, f32[256,128]{1,0:T(8,128)S(1)}, f32[256,128]{1,0:T(8,128)S(1)}, f32[256,128]{1,0:T(8,128)S(1)}, f32[256,128]{1,...) custom-call(s32[5,8]{1,0:T(8,128)S(1)} %concatenate.7.offs, ...), custom_call_target="tpu_custom_call" | custom-call | flops 1610612736 | bytes 5120000 | tf_op jit(solution)/shard_map/pallas_call | solution.py:363
  43.5 0.4 collective-permute-start.13
  43.9 1.0 %collective-permute-start.14 = (f32[256,128]{1,0:T(8,128)S(1)}, f32[256,128]{1,0:T(8,128)S(1)}, u32[]{:S(2)}, u32[]{:S(2)}) collective-permute-start(f32[256,128]{1,0:T(8,128)S(1)} %get-tuple-element.73), channel_id=1, source_target_pairs={{0,4},{1,5},{2,6},{3,7},{4,0},{5,1},{6,2},{7,3},{8,12},{9,13},{10,... | collective-permute-start | bytes 393224 | tf_op jit(solution)/shard_map/ppermute | solution.py:380
  44.8 1.5 %collective-permute-start.15 = (f32[256,128]{1,0:T(8,128)S(1)}, f32[256,128]{1,0:T(8,128)S(1)}, u32[]{:S(2)}, u32[]{:S(2)}) collective-permute-start(f32[256,128]{1,0:T(8,128)S(1)} %get-tuple-element.74), channel_id=1, source_target_pairs={{0,2},{1,3},{2,0},{3,1},{4,6},{5,7},{6,4},{7,5},{8,10},{9,11},{10,... | collective-permute-start | bytes 393224 | tf_op jit(solution)/shard_map/ppermute | solution.py:380
  46.3 1.3 %collective-permute-start.17 = (f32[256,128]{1,0:T(8,128)S(1)}, f32[256,128]{1,0:T(8,128)S(1)}, u32[]{:S(2)}, u32[]{:S(2)}) collective-permute-start(f32[256,128]{1,0:T(8,128)S(1)} %get-tuple-element.76), channel_id=1, source_target_pairs={{0,3},{1,2},{2,1},{3,0},{4,7},{5,6},{6,5},{7,4},{8,11},{9,10},{10,... | collective-permute-start | bytes 393224 | tf_op jit(solution)/shard_map/ppermute | solution.py:380
  47.6 1.9 %collective-permute-done.14.refs_1_ = f32[256,128]{1,0:T(8,128)S(1)} collective-permute-done((f32[256,128]{1,0:T(8,128)S(1)}, f32[256,128]{1,0:T(8,128)S(1)}, u32[]{:S(2)}, u32[]{:S(2)}) %collective-permute-start.14) | collective-permute-done | bytes 131104 | tf_op jit(solution)/shard_map/ppermute | solution.py:380
  49.5 2.5 %collective-permute-start.18 = (f32[256,128]{1,0:T(8,128)S(1)}, f32[256,128]{1,0:T(8,128)S(1)}, u32[]{:S(2)}, u32[]{:S(2)}) collective-permute-start(f32[256,128]{1,0:T(8,128)S(1)} %get-tuple-element.77), channel_id=1, source_target_pairs={{0,6},{1,7},{2,4},{3,5},{4,2},{5,3},{6,0},{7,1},{8,14},{9,15},{10,... | collective-permute-start | bytes 393224 | tf_op jit(solution)/shard_map/ppermute | solution.py:380
  52.1 0.6 collective-permute-start.20
  52.7 0.7 collective-permute-start.21
  53.4 3.2 %collective-permute-done.18.refs_5_ = f32[256,128]{1,0:T(8,128)S(1)} collective-permute-done((f32[256,128]{1,0:T(8,128)S(1)}, f32[256,128]{1,0:T(8,128)S(1)}, u32[]{:S(2)}, u32[]{:S(2)}) %collective-permute-start.18) | collective-permute-done | bytes 131104 | tf_op jit(solution)/shard_map/ppermute | solution.py:380
  56.6 2.4 %collective-permute-done.19.refs_6_ = f32[256,128]{1,0:T(8,128)S(1)} collective-permute-done((f32[256,128]{1,0:T(8,128)S(1)}, f32[256,128]{1,0:T(8,128)S(1)}, u32[]{:S(2)}, u32[]{:S(2)}) %collective-permute-start.19) | collective-permute-done | bytes 131104 | tf_op jit(solution)/shard_map/ppermute | solution.py:380
  58.9 1.5 %collective-permute-done.20.refs_0_ = f32[128,128]{1,0:T(8,128)S(1)} collective-permute-done((f32[128,128]{1,0:T(8,128)S(1)}, f32[128,128]{1,0:T(8,128)S(1)}, u32[]{:S(2)}, u32[]{:S(2)}) %collective-permute-start.20) | collective-permute-done | bytes 65568 | tf_op jit(solution)/shard_map/ppermute | solution.py:380
  60.5 1.0 %shard_map.102 = f32[2,256,128]{2,1,0:T(8,128)S(1)} custom-call(s32[5,8]{1,0:T(8,128)S(1)} %concatenate.7.offs, f32[768,128]{1,0:T(8,128)S(1)} %collective-permute-done.13.got.refs_0_, f32[256,128]{1,0:T(8,128)S(1)} %collective-permute-done.14.refs_1_, f32[256,128]{1,0:T(8,128)S(1)} %collective-permute-done.15.refs_2_, ...), custom_call_target="tpu_custom_call" | custom-call | flops 2097152 | bytes 1572864 | tf_op jit(solution)/shard_map/pallas_call | solution.py:363
  61.5 3.5 %collective-permute-start.22 = (f32[2,256,128]{2,1,0:T(8,128)S(1)}, f32[2,256,128]{2,1,0:T(8,128)S(1)}, u32[]{:S(2)}, u32[]{:S(2)}) collective-permute-start(f32[2,256,128]{2,1,0:T(8,128)S(1)} %shard_map.102), channel_id=1, source_target_pairs={{0,8},{8,16},{16,24},{1,9},{9,17},{17,25},{2,10},{10,18},{18,26},{... | collective-permute-start | bytes 786440 | tf_op jit(solution)/shard_map/ppermute | solution.py:456
  65.0 1.7 %collective-permute-start.23 = (f32[128,128]{1,0:T(8,128)S(1)}, f32[128,128]{1,0:T(8,128)S(1)}, u32[]{:S(2)}, u32[]{:S(2)}) collective-permute-start(f32[128,128]{1,0:T(8,128)S(1)} %get-tuple-element.97), channel_id=1, source_target_pairs={{0,6},{2,4},{4,2},{6,0},{1,7},{3,5},{5,3},{7,1},{8,14},{10,12},{12... | collective-permute-start | bytes 196616 | tf_op jit(solution)/shard_map/ppermute | solution.py:380
  66.7 3.5 %collective-permute-done.23.refs_2_ = f32[128,128]{1,0:T(8,128)S(1)} collective-permute-done((f32[128,128]{1,0:T(8,128)S(1)}, f32[128,128]{1,0:T(8,128)S(1)}, u32[]{:S(2)}, u32[]{:S(2)}) %collective-permute-start.23) | collective-permute-done | bytes 65568 | tf_op jit(solution)/shard_map/ppermute | solution.py:380
  70.2 1.6 %collective-permute-start.24 = (f32[64,256]{1,0:T(8,128)S(1)}, f32[64,256]{1,0:T(8,128)S(1)}, u32[]{:S(2)}, u32[]{:S(2)}) collective-permute-start(f32[64,256]{1,0:T(8,128)S(1)} %shard_map.104), channel_id=1, source_target_pairs={{0,8},{8,0},{16,24},{24,16},{1,9},{9,1},{17,25},{25,17},{2,10},{10... | collective-permute-start | bytes 196616 | tf_op jit(solution)/shard_map/ppermute | solution.py:459
  71.9 1.5 %shard_map.101.own = f32[4,256,128]{2,1,0:T(8,128)S(1)} custom-call(s32[5,8]{1,0:T(8,128)S(1)} %concatenate.7.offs, f32[768,128]{1,0:T(8,128)S(1)} %collective-permute-done.13.got.refs_0_, f32[256,128]{1,0:T(8,128)S(1)} %collective-permute-done.14.refs_1_, f32[256,128]{1,0:T(8,128)S(1)} %collective-permute-done.15.refs_2_, ...), custom_call_target="tpu_custom_call" | custom-call | flops 4194304 | bytes 1835008 | tf_op jit(solution)/shard_map/pallas_call | solution.py:363
  73.4 1.1 %collective-permute-done.24 = f32[64,256]{1,0:T(8,128)S(1)} collective-permute-done((f32[64,256]{1,0:T(8,128)S(1)}, f32[64,256]{1,0:T(8,128)S(1)}, u32[]{:S(2)}, u32[]{:S(2)}) %collective-permute-start.24) | collective-permute-done | bytes 65568 | tf_op jit(solution)/shard_map/ppermute | solution.py:459
  74.6 1.1 %collective-permute-start.28 = (f32[64,256]{1,0:T(8,128)S(1)}, f32[64,256]{1,0:T(8,128)S(1)}, u32[]{:S(2)}, u32[]{:S(2)}) collective-permute-start(f32[64,256]{1,0:T(8,128)S(1)} %add.8), channel_id=1, source_target_pairs={{0,16},{8,24},{16,0},{24,8},{1,17},{9,25},{17,1},{25,9},{2,18},{10... | collective-permute-start | bytes 196616 | tf_op jit(solution)/shard_map/ppermute | solution.py:388
  75.7 0.9 collective-permute-start.25
  76.5 1.3 %collective-permute-start.26 = (f32[256,128]{1,0:T(8,128)S(1)}, f32[256,128]{1,0:T(8,128)S(1)}, u32[]{:S(2)}, u32[]{:S(2)}) collective-permute-start(f32[256,128]{1,0:T(8,128)S(1)} %get-tuple-element.100), channel_id=1, source_target_pairs={{0,2},{2,0},{4,6},{6,4},{1,3},{3,1},{5,7},{7,5},{8,10},{10,8},{12,... | collective-permute-start | bytes 393224 | tf_op jit(solution)/shard_map/ppermute | solution.py:380
  77.9 1.3 %collective-permute-start.27 = (f32[256,128]{1,0:T(8,128)S(1)}, f32[256,128]{1,0:T(8,128)S(1)}, u32[]{:S(2)}, u32[]{:S(2)}) collective-permute-start(f32[256,128]{1,0:T(8,128)S(1)} %get-tuple-element.101), channel_id=1, source_target_pairs={{0,6},{2,4},{4,2},{6,0},{1,7},{3,5},{5,3},{7,1},{8,14},{10,12},{12... | collective-permute-start | bytes 393224 | tf_op jit(solution)/shard_map/ppermute | solution.py:380
  79.2 0.7 collective-permute-done.28
  79.8 9.3 %all_gather.3.refs_4_ = f32[512,256]{1,0:T(8,128)S(1)} all-gather(f32[64,256]{1,0:T(8,128)S(1)} %add.9), channel_id=1, replica_groups=mesh['pair'=4,'half'=2,'col'=2,'core'=2] {'half','col','core'}, dimensions={0}, use_global_device_ids=true | all-gather | bytes 589824 | tf_op jit(solution)/shard_map/all_gather | solution.py:468
  89.2 1.0 %shard_map.105 = (f32[4,256,128]{2,1,0:T(8,128)}, f32[512,256]{1,0:T(8,128)}) custom-call(f32[256,128]{1,0:T(8,128)S(1)} %collective-permute-done.25.refs_0_, f32[256,128]{1,0:T(8,128)S(1)} %collective-permute-done.26.refs_1_, f32[256,128]{1,0:T(8,128)S(1)} %collective-permute-done.27.refs_2_, f32[256,128]{1,0:T(8,128)S(1)} %get-tuple-element.102.refs_3_, ...), custom_call_target="tpu_custom_call" | custom-call | bytes 2097152 | tf_op jit(solution)/shard_map/pallas_call | solution.py:363
  (35 shorter events, 0.5 us)
Async XLA Ops:
  1.9 7.3 %collective-permute-start = (f32[264,128]{1,0:T(8,128)S(1)}, f32[264,128]{1,0:T(8,128)S(1)}, u32[]{:S(2)}, u32[]{:S(2)}) collective-permute-start(f32[264,128]{1,0:T(8,128)S(1)} %get-tuple-element.55), channel_id=1, source_target_pairs={{0,2},{2,0},{4,6},{6,4},{1,3},{3,1},{5,7},{7,5},{8,10},{10,8},{12,... | collective-permute-start | bytes 405512 | tf_op jit(solution)/shard_map/ppermute | solution.py:380
  4.9 7.9 %collective-permute-start.1 = (f32[264,128]{1,0:T(8,128)S(1)}, f32[264,128]{1,0:T(8,128)S(1)}, u32[]{:S(2)}, u32[]{:S(2)}) collective-permute-start(f32[264,128]{1,0:T(8,128)S(1)} %get-tuple-element.56), channel_id=1, source_target_pairs={{0,4},{2,6},{4,0},{6,2},{1,5},{3,7},{5,1},{7,3},{8,12},{10,14},{12... | collective-permute-start | bytes 405512 | tf_op jit(solution)/shard_map/ppermute | solution.py:380
  6.4 6.5 %collective-permute-start.2 = (f32[264,128]{1,0:T(8,128)S(1)}, f32[264,128]{1,0:T(8,128)S(1)}, u32[]{:S(2)}, u32[]{:S(2)}) collective-permute-start(f32[264,128]{1,0:T(8,128)S(1)} %get-tuple-element.57), channel_id=1, source_target_pairs={{0,6},{2,4},{4,2},{6,0},{1,7},{3,5},{5,3},{7,1},{8,14},{10,12},{12... | collective-permute-start | bytes 405512 | tf_op jit(solution)/shard_map/ppermute | solution.py:380
  13.1 3.0 %collective-permute-start.3 = (s32[4,4]{1,0:T(4,128)S(1)}, s32[4,4]{1,0:T(4,128)S(1)}, u32[]{:S(2)}, u32[]{:S(2)}) collective-permute-start(s32[4,4]{1,0:T(4,128)S(1)} %maximum_convert_fusion), channel_id=1, source_target_pairs={{0,1},{1,0},{2,3},{3,2},{4,5},{5,4},{6,7},{7,6},{8,9},{9,8},{10,11... | collective-permute-start | bytes 200 | tf_op jit(solution)/shard_map/ppermute | solution.py:418
  13.2 10.6 %collective-permute-start.4 = (f32[2,256,128]{2,1,0:T(8,128)S(1)}, f32[2,256,128]{2,1,0:T(8,128)S(1)}, u32[]{:S(2)}, u32[]{:S(2)}) collective-permute-start(f32[2,256,128]{2,1,0:T(8,128)S(1)} %shard_map.96), channel_id=1, source_target_pairs={{8,0},{16,8},{24,16},{9,1},{17,9},{25,17},{10,2},{18,10},{26,18},{... | collective-permute-start | bytes 786440 | tf_op jit(solution)/shard_map/ppermute | solution.py:413
  14.5 14.5 %collective-permute-start.12 = (f32[256,256]{1,0:T(8,128)S(1)}, f32[256,256]{1,0:T(8,128)S(1)}, u32[]{:S(2)}, u32[]{:S(2)}) collective-permute-start(f32[256,256]{1,0:T(8,128)S(1)} %get-tuple-element.68), channel_id=1, source_target_pairs={{0,4},{4,0},{1,5},{5,1},{2,6},{6,2},{3,7},{7,3},{8,12},{12,8},{9,1... | collective-permute-start | bytes 786440 | tf_op jit(solution)/shard_map/ppermute | solution.py:414
  25.2 5.3 %collective-permute-start.5 = (f32[256,128]{1,0:T(8,128)S(1)}, f32[256,128]{1,0:T(8,128)S(1)}, u32[]{:S(2)}, u32[]{:S(2)}) collective-permute-start(f32[256,128]{1,0:T(8,128)S(1)} %get-tuple-element.60), channel_id=1, source_target_pairs={{0,2},{1,3},{2,0},{3,1},{4,6},{5,7},{6,4},{7,5},{8,10},{9,11},{10,... | collective-permute-start | bytes 393224 | tf_op jit(solution)/shard_map/ppermute | solution.py:380
  26.4 5.8 %collective-permute-start.6 = (f32[256,128]{1,0:T(8,128)S(1)}, f32[256,128]{1,0:T(8,128)S(1)}, u32[]{:S(2)}, u32[]{:S(2)}) collective-permute-start(f32[256,128]{1,0:T(8,128)S(1)} %get-tuple-element.61), channel_id=1, source_target_pairs={{0,4},{1,5},{2,6},{3,7},{4,0},{5,1},{6,2},{7,3},{8,12},{9,13},{10,... | collective-permute-start | bytes 393224 | tf_op jit(solution)/shard_map/ppermute | solution.py:380
  27.3 7.4 %collective-permute-start.7 = (f32[256,128]{1,0:T(8,128)S(1)}, f32[256,128]{1,0:T(8,128)S(1)}, u32[]{:S(2)}, u32[]{:S(2)}) collective-permute-start(f32[256,128]{1,0:T(8,128)S(1)} %get-tuple-element.62), channel_id=1, source_target_pairs={{0,3},{1,2},{2,1},{3,0},{4,7},{5,6},{6,5},{7,4},{8,11},{9,10},{10,... | collective-permute-start | bytes 393224 | tf_op jit(solution)/shard_map/ppermute | solution.py:380
  27.5 10.7 %collective-permute-start.8 = (f32[256,128]{1,0:T(8,128)S(1)}, f32[256,128]{1,0:T(8,128)S(1)}, u32[]{:S(2)}, u32[]{:S(2)}) collective-permute-start(f32[256,128]{1,0:T(8,128)S(1)} %get-tuple-element.63), channel_id=1, source_target_pairs={{0,5},{1,4},{2,7},{3,6},{4,1},{5,0},{6,3},{7,2},{8,13},{9,12},{10,... | collective-permute-start | bytes 393224 | tf_op jit(solution)/shard_map/ppermute | solution.py:380
  29.0 9.2 %collective-permute-start.9 = (f32[256,128]{1,0:T(8,128)S(1)}, f32[256,128]{1,0:T(8,128)S(1)}, u32[]{:S(2)}, u32[]{:S(2)}) collective-permute-start(f32[256,128]{1,0:T(8,128)S(1)} %get-tuple-element.64), channel_id=1, source_target_pairs={{0,6},{1,7},{2,4},{3,5},{4,2},{5,3},{6,0},{7,1},{8,14},{9,15},{10,... | collective-permute-start | bytes 393224 | tf_op jit(solution)/shard_map/ppermute | solution.py:380
  30.5 8.7 %collective-permute-start.10 = (f32[256,128]{1,0:T(8,128)S(1)}, f32[256,128]{1,0:T(8,128)S(1)}, u32[]{:S(2)}, u32[]{:S(2)}) collective-permute-start(f32[256,128]{1,0:T(8,128)S(1)} %get-tuple-element.65), channel_id=1, source_target_pairs={{0,7},{1,6},{2,5},{3,4},{4,3},{5,2},{6,1},{7,0},{8,15},{9,14},{10,... | collective-permute-start | bytes 393224 | tf_op jit(solution)/shard_map/ppermute | solution.py:380
  32.2 7.1 %copy-start = (f32[2,136,128]{2,1,0:T(8,128)S(1)}, f32[2,136,128]{2,1,0:T(8,128)}, u32[]{:S(2)}) copy-start(f32[2,136,128]{2,1,0:T(8,128)} %constant.17.clone.refs_11_) | copy-start | bytes 417796
  32.2 7.1 %collective-permute-start.11 = (f32[256,128]{1,0:T(8,128)S(1)}, f32[256,128]{1,0:T(8,128)S(1)}, u32[]{:S(2)}, u32[]{:S(2)}) collective-permute-start(f32[256,128]{1,0:T(8,128)S(1)} %get-tuple-element.66), channel_id=1, source_target_pairs={{0,1},{1,0},{2,3},{3,2},{4,5},{5,4},{6,7},{7,6},{8,9},{9,8},{10,11... | collective-permute-start | bytes 393224 | tf_op jit(solution)/shard_map/ppermute | solution.py:380
  43.5 8.6 %collective-permute-start.13 = (f32[768,128]{1,0:T(8,128)S(1)}, f32[768,128]{1,0:T(8,128)S(1)}, u32[]{:S(2)}, u32[]{:S(2)}) collective-permute-start(f32[768,128]{1,0:T(8,128)S(1)} %get-tuple-element.72), channel_id=1, source_target_pairs={{0,1},{1,0},{2,3},{3,2},{4,5},{5,4},{6,7},{7,6},{8,9},{9,8},{10,11... | collective-permute-start | bytes 1179656 | tf_op jit(solution)/shard_map/ppermute | solution.py:380
  43.9 5.7 %collective-permute-start.14 = (f32[256,128]{1,0:T(8,128)S(1)}, f32[256,128]{1,0:T(8,128)S(1)}, u32[]{:S(2)}, u32[]{:S(2)}) collective-permute-start(f32[256,128]{1,0:T(8,128)S(1)} %get-tuple-element.73), channel_id=1, source_target_pairs={{0,4},{1,5},{2,6},{3,7},{4,0},{5,1},{6,2},{7,3},{8,12},{9,13},{10,... | collective-permute-start | bytes 393224 | tf_op jit(solution)/shard_map/ppermute | solution.py:380
  44.8 7.3 %collective-permute-start.15 = (f32[256,128]{1,0:T(8,128)S(1)}, f32[256,128]{1,0:T(8,128)S(1)}, u32[]{:S(2)}, u32[]{:S(2)}) collective-permute-start(f32[256,128]{1,0:T(8,128)S(1)} %get-tuple-element.74), channel_id=1, source_target_pairs={{0,2},{1,3},{2,0},{3,1},{4,6},{5,7},{6,4},{7,5},{8,10},{9,11},{10,... | collective-permute-start | bytes 393224 | tf_op jit(solution)/shard_map/ppermute | solution.py:380
  46.3 6.4 %collective-permute-start.16 = (f32[256,128]{1,0:T(8,128)S(1)}, f32[256,128]{1,0:T(8,128)S(1)}, u32[]{:S(2)}, u32[]{:S(2)}) collective-permute-start(f32[256,128]{1,0:T(8,128)S(1)} %get-tuple-element.75), channel_id=1, source_target_pairs={{0,5},{1,4},{2,7},{3,6},{4,1},{5,0},{6,3},{7,2},{8,13},{9,12},{10,... | collective-permute-start | bytes 393224 | tf_op jit(solution)/shard_map/ppermute | solution.py:380
  46.3 7.1 %collective-permute-start.17 = (f32[256,128]{1,0:T(8,128)S(1)}, f32[256,128]{1,0:T(8,128)S(1)}, u32[]{:S(2)}, u32[]{:S(2)}) collective-permute-start(f32[256,128]{1,0:T(8,128)S(1)} %get-tuple-element.76), channel_id=1, source_target_pairs={{0,3},{1,2},{2,1},{3,0},{4,7},{5,6},{6,5},{7,4},{8,11},{9,10},{10,... | collective-permute-start | bytes 393224 | tf_op jit(solution)/shard_map/ppermute | solution.py:380
  49.5 7.0 %collective-permute-start.18 = (f32[256,128]{1,0:T(8,128)S(1)}, f32[256,128]{1,0:T(8,128)S(1)}, u32[]{:S(2)}, u32[]{:S(2)}) collective-permute-start(f32[256,128]{1,0:T(8,128)S(1)} %get-tuple-element.77), channel_id=1, source_target_pairs={{0,6},{1,7},{2,4},{3,5},{4,2},{5,3},{6,0},{7,1},{8,14},{9,15},{10,... | collective-permute-start | bytes 393224 | tf_op jit(solution)/shard_map/ppermute | solution.py:380
  52.1 6.9 %collective-permute-start.19 = (f32[256,128]{1,0:T(8,128)S(1)}, f32[256,128]{1,0:T(8,128)S(1)}, u32[]{:S(2)}, u32[]{:S(2)}) collective-permute-start(f32[256,128]{1,0:T(8,128)S(1)} %get-tuple-element.78), channel_id=1, source_target_pairs={{0,7},{1,6},{2,5},{3,4},{4,3},{5,2},{6,1},{7,0},{8,15},{9,14},{10,... | collective-permute-start | bytes 393224 | tf_op jit(solution)/shard_map/ppermute | solution.py:380
  52.1 8.3 %collective-permute-start.20 = (f32[128,128]{1,0:T(8,128)S(1)}, f32[128,128]{1,0:T(8,128)S(1)}, u32[]{:S(2)}, u32[]{:S(2)}) collective-permute-start(f32[128,128]{1,0:T(8,128)S(1)} %get-tuple-element.81), channel_id=1, source_target_pairs={{0,4},{2,6},{4,0},{6,2},{1,5},{3,7},{5,1},{7,3},{8,12},{10,14},{12... | collective-permute-start | bytes 196616 | tf_op jit(solution)/shard_map/ppermute | solution.py:380
  52.7 7.8 %collective-permute-start.21 = (f32[128,128]{1,0:T(8,128)S(1)}, f32[128,128]{1,0:T(8,128)S(1)}, u32[]{:S(2)}, u32[]{:S(2)}) collective-permute-start(f32[128,128]{1,0:T(8,128)S(1)} %get-tuple-element.82), channel_id=1, source_target_pairs={{0,2},{2,0},{4,6},{6,4},{1,3},{3,1},{5,7},{7,5},{8,10},{10,8},{12,... | collective-permute-start | bytes 196616 | tf_op jit(solution)/shard_map/ppermute | solution.py:380
  61.5 11.9 %collective-permute-start.22 = (f32[2,256,128]{2,1,0:T(8,128)S(1)}, f32[2,256,128]{2,1,0:T(8,128)S(1)}, u32[]{:S(2)}, u32[]{:S(2)}) collective-permute-start(f32[2,256,128]{2,1,0:T(8,128)S(1)} %shard_map.102), channel_id=1, source_target_pairs={{0,8},{8,16},{16,24},{1,9},{9,17},{17,25},{2,10},{10,18},{18,26},{... | collective-permute-start | bytes 786440 | tf_op jit(solution)/shard_map/ppermute | solution.py:456
  65.0 5.2 %collective-permute-start.23 = (f32[128,128]{1,0:T(8,128)S(1)}, f32[128,128]{1,0:T(8,128)S(1)}, u32[]{:S(2)}, u32[]{:S(2)}) collective-permute-start(f32[128,128]{1,0:T(8,128)S(1)} %get-tuple-element.97), channel_id=1, source_target_pairs={{0,6},{2,4},{4,2},{6,0},{1,7},{3,5},{5,3},{7,1},{8,14},{10,12},{12... | collective-permute-start | bytes 196616 | tf_op jit(solution)/shard_map/ppermute | solution.py:380
  70.2 4.3 %collective-permute-start.24 = (f32[64,256]{1,0:T(8,128)S(1)}, f32[64,256]{1,0:T(8,128)S(1)}, u32[]{:S(2)}, u32[]{:S(2)}) collective-permute-start(f32[64,256]{1,0:T(8,128)S(1)} %shard_map.104), channel_id=1, source_target_pairs={{0,8},{8,0},{16,24},{24,16},{1,9},{9,1},{17,25},{25,17},{2,10},{10... | collective-permute-start | bytes 196616 | tf_op jit(solution)/shard_map/ppermute | solution.py:459
  74.6 5.2 %collective-permute-start.28 = (f32[64,256]{1,0:T(8,128)S(1)}, f32[64,256]{1,0:T(8,128)S(1)}, u32[]{:S(2)}, u32[]{:S(2)}) collective-permute-start(f32[64,256]{1,0:T(8,128)S(1)} %add.8), channel_id=1, source_target_pairs={{0,16},{8,24},{16,0},{24,8},{1,17},{9,25},{17,1},{25,9},{2,18},{10... | collective-permute-start | bytes 196616 | tf_op jit(solution)/shard_map/ppermute | solution.py:388
  75.7 13.5 %collective-permute-start.25 = (f32[256,128]{1,0:T(8,128)S(1)}, f32[256,128]{1,0:T(8,128)S(1)}, u32[]{:S(2)}, u32[]{:S(2)}) collective-permute-start(f32[256,128]{1,0:T(8,128)S(1)} %get-tuple-element.99), channel_id=1, source_target_pairs={{0,4},{2,6},{4,0},{6,2},{1,5},{3,7},{5,1},{7,3},{8,12},{10,14},{12... | collective-permute-start | bytes 393224 | tf_op jit(solution)/shard_map/ppermute | solution.py:380
  76.5 12.7 %collective-permute-start.26 = (f32[256,128]{1,0:T(8,128)S(1)}, f32[256,128]{1,0:T(8,128)S(1)}, u32[]{:S(2)}, u32[]{:S(2)}) collective-permute-start(f32[256,128]{1,0:T(8,128)S(1)} %get-tuple-element.100), channel_id=1, source_target_pairs={{0,2},{2,0},{4,6},{6,4},{1,3},{3,1},{5,7},{7,5},{8,10},{10,8},{12,... | collective-permute-start | bytes 393224 | tf_op jit(solution)/shard_map/ppermute | solution.py:380
  77.9 11.3 %collective-permute-start.27 = (f32[256,128]{1,0:T(8,128)S(1)}, f32[256,128]{1,0:T(8,128)S(1)}, u32[]{:S(2)}, u32[]{:S(2)}) collective-permute-start(f32[256,128]{1,0:T(8,128)S(1)} %get-tuple-element.101), channel_id=1, source_target_pairs={{0,6},{2,4},{4,2},{6,0},{1,7},{3,5},{5,3},{7,1},{8,14},{10,12},{12... | collective-permute-start | bytes 393224 | tf_op jit(solution)/shard_map/ppermute | solution.py:380

commit v23 on v19

--- a/solution.py
+++ b/solution.py
@@ -214,7 +214,7 @@
     lower, row_at, col_at = slot_place(offs, 2 * half + col, slot)
     probe_copy.wait()
     for part in range(2):
-        probe[part] = roll(probe[part], row_at, col_at)
+        probe[part] = roll(probe[part], row_at, lax.rem(col_at, target.shape[1]))
     kept_copy.wait()
     order_copy.wait()
     rest = jnp.where(lower == half, kept[...], taken[...])

time: 89.5 us -> 89.5 us (level)
  no operation moved by 1% of the time
where the time goes in v23:
time: 89.5 us; the launch traced here: 89.2 us
  starting transfers between devices  34.5 us (39%)
  waiting for transfers between devices  28.9 us (32%)
  Pallas kernels  13 us (15%)
  blocking collectives  8.82 us (10%)
  between operations  2.06 us (2%)
  local copies, waits for them, and re-layouts  1.79 us (2%)
    ppermute x23, starting transfers between devices, deal(): lax.ppermute(value, axes, [(k, k ^ turn) for k in range(len(order))])  24.3 us
    ppermute x23, waiting for transfers between devices, deal(): lax.ppermute(value, axes, [(k, k ^ turn) for k in range(len(order))])  17.2 us
    pallas_call x10, Pallas kernels, call(): pl.pallas_call(kernel, out_shape=[x for x, unused in outs], in_specs=[SME...  13 us
    all_gather x1, blocking collectives, local(): probe_grad = lax.all_gather(probe_band, PLANE, axis=0, tiled=True)  8.82 us
    ppermute x1, waiting for transfers between devices, local(): below = lax.ppermute(lowest, 'pair', [(k, k - 1) for k in range(1, pairs)])  7.61 us
    ppermute x1, starting transfers between devices, local(): lax.ppermute(lower_sums, 'pair', [(k, k + 1) for k in range(pairs - 1)])  3.49 us
    ppermute x1, waiting for transfers between devices, local(): lax.ppermute(lower_sums, 'pair', [(k, k + 1) for k in range(pairs - 1)])  3.18 us
    ppermute x1, starting transfers between devices, sum_over(): lax.ppermute(value, axis, [(k, k ^ step) for k in range(size)])  2.21 us
  transfers between devices with their start and end apart: 29, of which 13 were waited for; matrix products, arithmetic and copies ran while one was open for 2% of the time, Pallas kernels for 6%

profile of v23, /device:TPU:0, one launch (start us, length us, event | category | flops | bytes accessed | tf_op | source)
XLA Modules:
  0.0 89.2 jit_solution(10963762263549180364)
XLA Ops:
  0.6 1.3 %shard_map.95 = (f32[264,128]{1,0:T(8,128)S(1)}, f32[264,128]{1,0:T(8,128)S(1)}, f32[264,128]{1,0:T(8,128)S(1)}, f32[264,128]{1,0:T(8,128)S(1)}, f32[256,256]{1,0:T(8,128)S(1)}) custom-call(f32[4,256,128]{2,1,0:T(8,128)} %bitcast.9, f32[1,2,256,256]{3,2,1,0:T(8,128)} %measured.3, s32[1,2,2]{2,1,0:T(2,128)} %offsets_from.1), custom_call_target="tpu_custom_call" | custom-call | bytes 1851408 | tf_op jit(solution)/shard_map/pallas_call | solution.py:359
  1.9 3.0 %collective-permute-start = (f32[264,128]{1,0:T(8,128)S(1)}, f32[264,128]{1,0:T(8,128)S(1)}, u32[]{:S(2)}, u32[]{:S(2)}) collective-permute-start(f32[264,128]{1,0:T(8,128)S(1)} %get-tuple-element.47), channel_id=1, source_target_pairs={{0,2},{2,0},{4,6},{6,4},{1,3},{3,1},{5,7},{7,5},{8,10},{10,8},{12,... | collective-permute-start | bytes 405512 | tf_op jit(solution)/shard_map/ppermute | solution.py:376
  4.9 1.5 %collective-permute-start.1 = (f32[264,128]{1,0:T(8,128)S(1)}, f32[264,128]{1,0:T(8,128)S(1)}, u32[]{:S(2)}, u32[]{:S(2)}) collective-permute-start(f32[264,128]{1,0:T(8,128)S(1)} %get-tuple-element.48), channel_id=1, source_target_pairs={{0,4},{2,6},{4,0},{6,2},{1,5},{3,7},{5,1},{7,3},{8,12},{10,14},{12... | collective-permute-start | bytes 405512 | tf_op jit(solution)/shard_map/ppermute | solution.py:376
  6.6 1.3 %fusion = (s32[1,1]{1,0:T(1,128)}, s32[1,1]{1,0:T(1,128)}) fusion(s32[1,2]{1,0:T(1,128)} %param.11), kind=kLoop, calls=%fused_computation.8 | loop fusion | bytes 16 | tf_op jit(solution)/shard_map/slice | solution.py:416
  9.2 0.1 slice_reduce_fusion.2
  9.3 3.5 %collective-permute-done.1.refs_0_ = f32[264,128]{1,0:T(8,128)S(1)} collective-permute-done((f32[264,128]{1,0:T(8,128)S(1)}, f32[264,128]{1,0:T(8,128)S(1)}, u32[]{:S(2)}, u32[]{:S(2)}) %collective-permute-start.1) | collective-permute-done | bytes 135200 | tf_op jit(solution)/shard_map/ppermute | solution.py:376
  13.0 0.1 slice_reduce_fusion
  13.2 1.3 %collective-permute-start.4 = (f32[2,256,128]{2,1,0:T(8,128)S(1)}, f32[2,256,128]{2,1,0:T(8,128)S(1)}, u32[]{:S(2)}, u32[]{:S(2)}) collective-permute-start(f32[2,256,128]{2,1,0:T(8,128)S(1)} %shard_map.96), channel_id=1, source_target_pairs={{8,0},{16,8},{24,16},{9,1},{17,9},{25,17},{10,2},{18,10},{26,18},{... | collective-permute-start | bytes 786440 | tf_op jit(solution)/shard_map/ppermute | solution.py:409
  14.5 1.6 %collective-permute-start.12 = (f32[256,256]{1,0:T(8,128)S(1)}, f32[256,256]{1,0:T(8,128)S(1)}, u32[]{:S(2)}, u32[]{:S(2)}) collective-permute-start(f32[256,256]{1,0:T(8,128)S(1)} %get-tuple-element.60), channel_id=1, source_target_pairs={{0,4},{4,0},{1,5},{5,1},{2,6},{6,2},{3,7},{7,3},{8,12},{12,8},{9,1... | collective-permute-start | bytes 786440 | tf_op jit(solution)/shard_map/ppermute | solution.py:410
  16.2 7.6 %collective-permute-done.4.refs_4_ = f32[2,256,128]{2,1,0:T(8,128)S(1)} collective-permute-done((f32[2,256,128]{2,1,0:T(8,128)S(1)}, f32[2,256,128]{2,1,0:T(8,128)S(1)}, u32[]{:S(2)}, u32[]{:S(2)}) %collective-permute-start.4) | collective-permute-done | bytes 262176 | tf_op jit(solution)/shard_map/ppermute | solution.py:409
  23.8 1.3 %shard_map.97 = (f32[256,128]{1,0:T(8,128)S(1)}, f32[256,128]{1,0:T(8,128)S(1)}, f32[256,128]{1,0:T(8,128)S(1)}, f32[256,128]{1,0:T(8,128)S(1)}, f32[256,128]{1,...) custom-call(s32[5,8]{1,0:T(8,128)S(1)} %concatenate.7.offs, ...), custom_call_target="tpu_custom_call" | custom-call | flops 2097152 | bytes 1851392 | tf_op jit(solution)/shard_map/pallas_call | solution.py:359
  25.2 1.2 %collective-permute-start.5 = (f32[256,128]{1,0:T(8,128)S(1)}, f32[256,128]{1,0:T(8,128)S(1)}, u32[]{:S(2)}, u32[]{:S(2)}) collective-permute-start(f32[256,128]{1,0:T(8,128)S(1)} %get-tuple-element.52), channel_id=1, source_target_pairs={{0,2},{1,3},{2,0},{3,1},{4,6},{5,7},{6,4},{7,5},{8,10},{9,11},{10,... | collective-permute-start | bytes 393224 | tf_op jit(solution)/shard_map/ppermute | solution.py:376
  26.4 0.9 %collective-permute-start.6 = (f32[256,128]{1,0:T(8,128)S(1)}, f32[256,128]{1,0:T(8,128)S(1)}, u32[]{:S(2)}, u32[]{:S(2)}) collective-permute-start(f32[256,128]{1,0:T(8,128)S(1)} %get-tuple-element.53), channel_id=1, source_target_pairs={{0,4},{1,5},{2,6},{3,7},{4,0},{5,1},{6,2},{7,3},{8,12},{9,13},{10,... | collective-permute-start | bytes 393224 | tf_op jit(solution)/shard_map/ppermute | solution.py:376
  27.3 0.2 collective-permute-start.7
  27.5 1.5 %collective-permute-start.8 = (f32[256,128]{1,0:T(8,128)S(1)}, f32[256,128]{1,0:T(8,128)S(1)}, u32[]{:S(2)}, u32[]{:S(2)}) collective-permute-start(f32[256,128]{1,0:T(8,128)S(1)} %get-tuple-element.55), channel_id=1, source_target_pairs={{0,5},{1,4},{2,7},{3,6},{4,1},{5,0},{6,3},{7,2},{8,13},{9,12},{10,... | collective-permute-start | bytes 393224 | tf_op jit(solution)/shard_map/ppermute | solution.py:376
  29.0 1.5 %collective-permute-start.9 = (f32[256,128]{1,0:T(8,128)S(1)}, f32[256,128]{1,0:T(8,128)S(1)}, u32[]{:S(2)}, u32[]{:S(2)}) collective-permute-start(f32[256,128]{1,0:T(8,128)S(1)} %get-tuple-element.56), channel_id=1, source_target_pairs={{0,6},{1,7},{2,4},{3,5},{4,2},{5,3},{6,0},{7,1},{8,14},{9,15},{10,... | collective-permute-start | bytes 393224 | tf_op jit(solution)/shard_map/ppermute | solution.py:376
  30.5 0.7 collective-permute-start.10
  31.2 1.0 %collective-permute-done.6.refs_1_ = f32[256,128]{1,0:T(8,128)S(1)} collective-permute-done((f32[256,128]{1,0:T(8,128)S(1)}, f32[256,128]{1,0:T(8,128)S(1)}, u32[]{:S(2)}, u32[]{:S(2)}) %collective-permute-start.6) | collective-permute-done | bytes 131104 | tf_op jit(solution)/shard_map/ppermute | solution.py:376
  32.2 2.5 %shard_map.98 = (f32[2,256,256]{2,1,0:T(8,128)S(1)}, f32[256,256]{1,0:T(8,128)S(1)}, bf16[6,512,256]{2,1,0:T(8,128)(2,1)S(1)}) custom-call(s32[5,8]{1,0:T(8,128)S(1)} %concatenate.7.offs, f32[256,256]{1,0:T(8,128)S(1)} %collective-permute-done.12.taken, f32[2,256,256]{2,1,0:T(8,128)} %probe_from.1, f32[1,2,256,256]{3,2,1,0:T(8,128)} %measured.3, ...), custom_call_target="tpu_custom_call" | custom-call | flops 201326592 | bytes 5505024 | tf_op jit(solution)/shard_map/pallas_call | solution.py:359
  34.7 3.5 %collective-permute-done.8.refs_3_ = f32[256,128]{1,0:T(8,128)S(1)} collective-permute-done((f32[256,128]{1,0:T(8,128)S(1)}, f32[256,128]{1,0:T(8,128)S(1)}, u32[]{:S(2)}, u32[]{:S(2)}) %collective-permute-start.8) | collective-permute-done | bytes 131104 | tf_op jit(solution)/shard_map/ppermute | solution.py:376
  38.3 1.0 %collective-permute-done.10.refs_5_ = f32[256,128]{1,0:T(8,128)S(1)} collective-permute-done((f32[256,128]{1,0:T(8,128)S(1)}, f32[256,128]{1,0:T(8,128)S(1)}, u32[]{:S(2)}, u32[]{:S(2)}) %collective-permute-start.10) | collective-permute-done | bytes 131104 | tf_op jit(solution)/shard_map/ppermute | solution.py:376
  39.3 4.2 %shard_map.99 = (f32[768,128]{1,0:T(8,128)S(1)}, f32[256,128]{1,0:T(8,128)S(1)}, f32[256,128]{1,0:T(8,128)S(1)}, f32[256,128]{1,0:T(8,128)S(1)}, f32[256,128]{1,...) custom-call(s32[5,8]{1,0:T(8,128)S(1)} %concatenate.7.offs, ...), custom_call_target="tpu_custom_call" | custom-call | flops 1610612736 | bytes 5120000 | tf_op jit(solution)/shard_map/pallas_call | solution.py:359
  43.5 0.4 collective-permute-start.13
  43.9 1.0 %collective-permute-start.14 = (f32[256,128]{1,0:T(8,128)S(1)}, f32[256,128]{1,0:T(8,128)S(1)}, u32[]{:S(2)}, u32[]{:S(2)}) collective-permute-start(f32[256,128]{1,0:T(8,128)S(1)} %get-tuple-element.65), channel_id=1, source_target_pairs={{0,4},{1,5},{2,6},{3,7},{4,0},{5,1},{6,2},{7,3},{8,12},{9,13},{10,... | collective-permute-start | bytes 393224 | tf_op jit(solution)/shard_map/ppermute | solution.py:376
  44.8 1.5 %collective-permute-start.15 = (f32[256,128]{1,0:T(8,128)S(1)}, f32[256,128]{1,0:T(8,128)S(1)}, u32[]{:S(2)}, u32[]{:S(2)}) collective-permute-start(f32[256,128]{1,0:T(8,128)S(1)} %get-tuple-element.66), channel_id=1, source_target_pairs={{0,2},{1,3},{2,0},{3,1},{4,6},{5,7},{6,4},{7,5},{8,10},{9,11},{10,... | collective-permute-start | bytes 393224 | tf_op jit(solution)/shard_map/ppermute | solution.py:376
  46.3 1.3 %collective-permute-start.17 = (f32[256,128]{1,0:T(8,128)S(1)}, f32[256,128]{1,0:T(8,128)S(1)}, u32[]{:S(2)}, u32[]{:S(2)}) collective-permute-start(f32[256,128]{1,0:T(8,128)S(1)} %get-tuple-element.68), channel_id=1, source_target_pairs={{0,3},{1,2},{2,1},{3,0},{4,7},{5,6},{6,5},{7,4},{8,11},{9,10},{10,... | collective-permute-start | bytes 393224 | tf_op jit(solution)/shard_map/ppermute | solution.py:376
  47.6 1.9 %collective-permute-done.14.refs_1_ = f32[256,128]{1,0:T(8,128)S(1)} collective-permute-done((f32[256,128]{1,0:T(8,128)S(1)}, f32[256,128]{1,0:T(8,128)S(1)}, u32[]{:S(2)}, u32[]{:S(2)}) %collective-permute-start.14) | collective-permute-done | bytes 131104 | tf_op jit(solution)/shard_map/ppermute | solution.py:376
  49.5 2.5 %collective-permute-start.18 = (f32[256,128]{1,0:T(8,128)S(1)}, f32[256,128]{1,0:T(8,128)S(1)}, u32[]{:S(2)}, u32[]{:S(2)}) collective-permute-start(f32[256,128]{1,0:T(8,128)S(1)} %get-tuple-element.69), channel_id=1, source_target_pairs={{0,6},{1,7},{2,4},{3,5},{4,2},{5,3},{6,0},{7,1},{8,14},{9,15},{10,... | collective-permute-start | bytes 393224 | tf_op jit(solution)/shard_map/ppermute | solution.py:376
  52.1 0.6 collective-permute-start.20
  52.7 0.7 collective-permute-start.21
  53.4 2.3 %collective-permute-start.22 = (f32[128,128]{1,0:T(8,128)S(1)}, f32[128,128]{1,0:T(8,128)S(1)}, u32[]{:S(2)}, u32[]{:S(2)}) collective-permute-start(f32[128,128]{1,0:T(8,128)S(1)} %get-tuple-element.75), channel_id=1, source_target_pairs={{0,6},{2,4},{4,2},{6,0},{1,7},{3,5},{5,3},{7,1},{8,14},{10,12},{12... | collective-permute-start | bytes 196616 | tf_op jit(solution)/shard_map/ppermute | solution.py:376
  55.7 0.9 collective-permute-done.18.refs_5_
  56.6 2.4 %collective-permute-done.19.refs_6_ = f32[256,128]{1,0:T(8,128)S(1)} collective-permute-done((f32[256,128]{1,0:T(8,128)S(1)}, f32[256,128]{1,0:T(8,128)S(1)}, u32[]{:S(2)}, u32[]{:S(2)}) %collective-permute-start.19) | collective-permute-done | bytes 131104 | tf_op jit(solution)/shard_map/ppermute | solution.py:376
  58.9 1.7 %collective-permute-done.20.refs_8_ = f32[128,128]{1,0:T(8,128)S(1)} collective-permute-done((f32[128,128]{1,0:T(8,128)S(1)}, f32[128,128]{1,0:T(8,128)S(1)}, u32[]{:S(2)}, u32[]{:S(2)}) %collective-permute-start.20) | collective-permute-done | bytes 65568 | tf_op jit(solution)/shard_map/ppermute | solution.py:376
  60.6 1.3 %collective-permute-done.22.refs_10_ = f32[128,128]{1,0:T(8,128)S(1)} collective-permute-done((f32[128,128]{1,0:T(8,128)S(1)}, f32[128,128]{1,0:T(8,128)S(1)}, u32[]{:S(2)}, u32[]{:S(2)}) %collective-permute-start.22) | collective-permute-done | bytes 65568 | tf_op jit(solution)/shard_map/ppermute | solution.py:376
  61.9 1.0 %shard_map.102 = (f32[2,256,128]{2,1,0:T(8,128)S(1)}, f32[64,256]{1,0:T(8,128)S(1)}) custom-call(s32[5,8]{1,0:T(8,128)S(1)} %concatenate.7.offs, f32[768,128]{1,0:T(8,128)S(1)} %collective-permute-done.13.refs_0_.got, f32[256,128]{1,0:T(8,128)S(1)} %collective-permute-done.14.refs_1_, f32[256,128]{1,0:T(8,128)S(1)} %collective-permute-done.15.refs_2_, ...), custom_call_target="tpu_custom_call" | custom-call | flops 2097152 | bytes 1900544 | tf_op jit(solution)/shard_map/pallas_call | solution.py:359
  62.9 3.5 %collective-permute-start.23 = (f32[2,256,128]{2,1,0:T(8,128)S(1)}, f32[2,256,128]{2,1,0:T(8,128)S(1)}, u32[]{:S(2)}, u32[]{:S(2)}) collective-permute-start(f32[2,256,128]{2,1,0:T(8,128)S(1)} %get-tuple-element.77), channel_id=1, source_target_pairs={{0,8},{8,16},{16,24},{1,9},{9,17},{17,25},{2,10},{10,18},{18,26},{... | collective-permute-start | bytes 786440 | tf_op jit(solution)/shard_map/ppermute | solution.py:454
  66.4 1.6 %collective-permute-start.24 = (f32[64,256]{1,0:T(8,128)S(1)}, f32[64,256]{1,0:T(8,128)S(1)}, u32[]{:S(2)}, u32[]{:S(2)}) collective-permute-start(f32[64,256]{1,0:T(8,128)S(1)} %get-tuple-element.82), channel_id=1, source_target_pairs={{0,8},{8,0},{16,24},{24,16},{1,9},{9,1},{17,25},{25,17},{2,10},{10... | collective-permute-start | bytes 196616 | tf_op jit(solution)/shard_map/ppermute | solution.py:457
  68.1 1.5 %shard_map.100.own = f32[4,256,128]{2,1,0:T(8,128)S(1)} custom-call(s32[5,8]{1,0:T(8,128)S(1)} %concatenate.7.offs, f32[768,128]{1,0:T(8,128)S(1)} %collective-permute-done.13.refs_0_.got, f32[256,128]{1,0:T(8,128)S(1)} %collective-permute-done.14.refs_1_, f32[256,128]{1,0:T(8,128)S(1)} %collective-permute-done.15.refs_2_, ...), custom_call_target="tpu_custom_call" | custom-call | flops 4194304 | bytes 1835008 | tf_op jit(solution)/shard_map/pallas_call | solution.py:359
  69.6 3.2 %collective-permute-done.23.above = f32[2,256,128]{2,1,0:T(8,128)S(1)} collective-permute-done((f32[2,256,128]{2,1,0:T(8,128)S(1)}, f32[2,256,128]{2,1,0:T(8,128)S(1)}, u32[]{:S(2)}, u32[]{:S(2)}) %collective-permute-start.23) | collective-permute-done | bytes 262176 | tf_op jit(solution)/shard_map/ppermute | solution.py:454
  72.8 0.6 collective-permute-done.24
  73.5 2.2 %collective-permute-start.28 = (f32[64,256]{1,0:T(8,128)S(1)}, f32[64,256]{1,0:T(8,128)S(1)}, u32[]{:S(2)}, u32[]{:S(2)}) collective-permute-start(f32[64,256]{1,0:T(8,128)S(1)} %add.8), channel_id=1, source_target_pairs={{0,16},{8,24},{16,0},{24,8},{1,17},{9,25},{17,1},{25,9},{2,18},{10... | collective-permute-start | bytes 196616 | tf_op jit(solution)/shard_map/ppermute | solution.py:384
  75.7 0.4 collective-permute-start.25
  76.1 1.3 %collective-permute-start.26 = (f32[256,128]{1,0:T(8,128)S(1)}, f32[256,128]{1,0:T(8,128)S(1)}, u32[]{:S(2)}, u32[]{:S(2)}) collective-permute-start(f32[256,128]{1,0:T(8,128)S(1)} %get-tuple-element.84), channel_id=1, source_target_pairs={{0,2},{2,0},{4,6},{6,4},{1,3},{3,1},{5,7},{7,5},{8,10},{10,8},{12,... | collective-permute-start | bytes 393224 | tf_op jit(solution)/shard_map/ppermute | solution.py:376
  77.4 1.8 %collective-permute-start.27 = (f32[256,128]{1,0:T(8,128)S(1)}, f32[256,128]{1,0:T(8,128)S(1)}, u32[]{:S(2)}, u32[]{:S(2)}) collective-permute-start(f32[256,128]{1,0:T(8,128)S(1)} %get-tuple-element.85), channel_id=1, source_target_pairs={{0,6},{2,4},{4,2},{6,0},{1,7},{3,5},{5,3},{7,1},{8,14},{10,12},{12... | collective-permute-start | bytes 393224 | tf_op jit(solution)/shard_map/ppermute | solution.py:376
  79.1 0.2 collective-permute-done.28
  79.4 8.8 %all_gather.3.refs_4_ = f32[512,256]{1,0:T(8,128)S(1)} all-gather(f32[64,256]{1,0:T(8,128)S(1)} %add.9), channel_id=1, replica_groups=mesh['pair'=4,'half'=2,'col'=2,'core'=2] {'half','col','core'}, dimensions={0}, use_global_device_ids=true | all-gather | bytes 589824 | tf_op jit(solution)/shard_map/all_gather | solution.py:466
  88.2 1.0 %shard_map.104 = (f32[4,256,128]{2,1,0:T(8,128)}, f32[512,256]{1,0:T(8,128)}) custom-call(f32[256,128]{1,0:T(8,128)S(1)} %collective-permute-done.25.refs_0_, f32[256,128]{1,0:T(8,128)S(1)} %collective-permute-done.26.refs_1_, f32[256,128]{1,0:T(8,128)S(1)} %collective-permute-done.27.refs_2_, f32[256,128]{1,0:T(8,128)S(1)} %get-tuple-element.86.refs_3_, ...), custom_call_target="tpu_custom_call" | custom-call | bytes 2097152 | tf_op jit(solution)/shard_map/pallas_call | solution.py:359
  (34 shorter events, 0.6 us)
Async XLA Ops:
  1.9 7.3 %collective-permute-start = (f32[264,128]{1,0:T(8,128)S(1)}, f32[264,128]{1,0:T(8,128)S(1)}, u32[]{:S(2)}, u32[]{:S(2)}) collective-permute-start(f32[264,128]{1,0:T(8,128)S(1)} %get-tuple-element.47), channel_id=1, source_target_pairs={{0,2},{2,0},{4,6},{6,4},{1,3},{3,1},{5,7},{7,5},{8,10},{10,8},{12,... | collective-permute-start | bytes 405512 | tf_op jit(solution)/shard_map/ppermute | solution.py:376
  4.9 7.9 %collective-permute-start.1 = (f32[264,128]{1,0:T(8,128)S(1)}, f32[264,128]{1,0:T(8,128)S(1)}, u32[]{:S(2)}, u32[]{:S(2)}) collective-permute-start(f32[264,128]{1,0:T(8,128)S(1)} %get-tuple-element.48), channel_id=1, source_target_pairs={{0,4},{2,6},{4,0},{6,2},{1,5},{3,7},{5,1},{7,3},{8,12},{10,14},{12... | collective-permute-start | bytes 405512 | tf_op jit(solution)/shard_map/ppermute | solution.py:376
  6.4 6.5 %collective-permute-start.2 = (f32[264,128]{1,0:T(8,128)S(1)}, f32[264,128]{1,0:T(8,128)S(1)}, u32[]{:S(2)}, u32[]{:S(2)}) collective-permute-start(f32[264,128]{1,0:T(8,128)S(1)} %get-tuple-element.49), channel_id=1, source_target_pairs={{0,6},{2,4},{4,2},{6,0},{1,7},{3,5},{5,3},{7,1},{8,14},{10,12},{12... | collective-permute-start | bytes 405512 | tf_op jit(solution)/shard_map/ppermute | solution.py:376
  13.1 3.0 %collective-permute-start.3 = (s32[4,4]{1,0:T(4,128)S(1)}, s32[4,4]{1,0:T(4,128)S(1)}, u32[]{:S(2)}, u32[]{:S(2)}) collective-permute-start(s32[4,4]{1,0:T(4,128)S(1)} %maximum_convert_fusion), channel_id=1, source_target_pairs={{0,1},{1,0},{2,3},{3,2},{4,5},{5,4},{6,7},{7,6},{8,9},{9,8},{10,11... | collective-permute-start | bytes 200 | tf_op jit(solution)/shard_map/ppermute | solution.py:414
  13.2 10.6 %collective-permute-start.4 = (f32[2,256,128]{2,1,0:T(8,128)S(1)}, f32[2,256,128]{2,1,0:T(8,128)S(1)}, u32[]{:S(2)}, u32[]{:S(2)}) collective-permute-start(f32[2,256,128]{2,1,0:T(8,128)S(1)} %shard_map.96), channel_id=1, source_target_pairs={{8,0},{16,8},{24,16},{9,1},{17,9},{25,17},{10,2},{18,10},{26,18},{... | collective-permute-start | bytes 786440 | tf_op jit(solution)/shard_map/ppermute | solution.py:409
  14.5 14.5 %collective-permute-start.12 = (f32[256,256]{1,0:T(8,128)S(1)}, f32[256,256]{1,0:T(8,128)S(1)}, u32[]{:S(2)}, u32[]{:S(2)}) collective-permute-start(f32[256,256]{1,0:T(8,128)S(1)} %get-tuple-element.60), channel_id=1, source_target_pairs={{0,4},{4,0},{1,5},{5,1},{2,6},{6,2},{3,7},{7,3},{8,12},{12,8},{9,1... | collective-permute-start | bytes 786440 | tf_op jit(solution)/shard_map/ppermute | solution.py:410
  25.2 5.3 %collective-permute-start.5 = (f32[256,128]{1,0:T(8,128)S(1)}, f32[256,128]{1,0:T(8,128)S(1)}, u32[]{:S(2)}, u32[]{:S(2)}) collective-permute-start(f32[256,128]{1,0:T(8,128)S(1)} %get-tuple-element.52), channel_id=1, source_target_pairs={{0,2},{1,3},{2,0},{3,1},{4,6},{5,7},{6,4},{7,5},{8,10},{9,11},{10,... | collective-permute-start | bytes 393224 | tf_op jit(solution)/shard_map/ppermute | solution.py:376
  26.4 5.8 %collective-permute-start.6 = (f32[256,128]{1,0:T(8,128)S(1)}, f32[256,128]{1,0:T(8,128)S(1)}, u32[]{:S(2)}, u32[]{:S(2)}) collective-permute-start(f32[256,128]{1,0:T(8,128)S(1)} %get-tuple-element.53), channel_id=1, source_target_pairs={{0,4},{1,5},{2,6},{3,7},{4,0},{5,1},{6,2},{7,3},{8,12},{9,13},{10,... | collective-permute-start | bytes 393224 | tf_op jit(solution)/shard_map/ppermute | solution.py:376
  27.3 7.4 %collective-permute-start.7 = (f32[256,128]{1,0:T(8,128)S(1)}, f32[256,128]{1,0:T(8,128)S(1)}, u32[]{:S(2)}, u32[]{:S(2)}) collective-permute-start(f32[256,128]{1,0:T(8,128)S(1)} %get-tuple-element.54), channel_id=1, source_target_pairs={{0,3},{1,2},{2,1},{3,0},{4,7},{5,6},{6,5},{7,4},{8,11},{9,10},{10,... | collective-permute-start | bytes 393224 | tf_op jit(solution)/shard_map/ppermute | solution.py:376
  27.5 10.7 %collective-permute-start.8 = (f32[256,128]{1,0:T(8,128)S(1)}, f32[256,128]{1,0:T(8,128)S(1)}, u32[]{:S(2)}, u32[]{:S(2)}) collective-permute-start(f32[256,128]{1,0:T(8,128)S(1)} %get-tuple-element.55), channel_id=1, source_target_pairs={{0,5},{1,4},{2,7},{3,6},{4,1},{5,0},{6,3},{7,2},{8,13},{9,12},{10,... | collective-permute-start | bytes 393224 | tf_op jit(solution)/shard_map/ppermute | solution.py:376
  29.0 9.2 %collective-permute-start.9 = (f32[256,128]{1,0:T(8,128)S(1)}, f32[256,128]{1,0:T(8,128)S(1)}, u32[]{:S(2)}, u32[]{:S(2)}) collective-permute-start(f32[256,128]{1,0:T(8,128)S(1)} %get-tuple-element.56), channel_id=1, source_target_pairs={{0,6},{1,7},{2,4},{3,5},{4,2},{5,3},{6,0},{7,1},{8,14},{9,15},{10,... | collective-permute-start | bytes 393224 | tf_op jit(solution)/shard_map/ppermute | solution.py:376
  30.5 8.7 %collective-permute-start.10 = (f32[256,128]{1,0:T(8,128)S(1)}, f32[256,128]{1,0:T(8,128)S(1)}, u32[]{:S(2)}, u32[]{:S(2)}) collective-permute-start(f32[256,128]{1,0:T(8,128)S(1)} %get-tuple-element.57), channel_id=1, source_target_pairs={{0,7},{1,6},{2,5},{3,4},{4,3},{5,2},{6,1},{7,0},{8,15},{9,14},{10,... | collective-permute-start | bytes 393224 | tf_op jit(solution)/shard_map/ppermute | solution.py:376
  32.2 7.1 %copy-start = (f32[2,136,128]{2,1,0:T(8,128)S(1)}, f32[2,136,128]{2,1,0:T(8,128)}, u32[]{:S(2)}) copy-start(f32[2,136,128]{2,1,0:T(8,128)} %constant.17.clone.refs_11_) | copy-start | bytes 417796
  32.2 7.1 %collective-permute-start.11 = (f32[256,128]{1,0:T(8,128)S(1)}, f32[256,128]{1,0:T(8,128)S(1)}, u32[]{:S(2)}, u32[]{:S(2)}) collective-permute-start(f32[256,128]{1,0:T(8,128)S(1)} %get-tuple-element.58), channel_id=1, source_target_pairs={{0,1},{1,0},{2,3},{3,2},{4,5},{5,4},{6,7},{7,6},{8,9},{9,8},{10,11... | collective-permute-start | bytes 393224 | tf_op jit(solution)/shard_map/ppermute | solution.py:376
  43.5 8.6 %collective-permute-start.13 = (f32[768,128]{1,0:T(8,128)S(1)}, f32[768,128]{1,0:T(8,128)S(1)}, u32[]{:S(2)}, u32[]{:S(2)}) collective-permute-start(f32[768,128]{1,0:T(8,128)S(1)} %get-tuple-element.64), channel_id=1, source_target_pairs={{0,1},{1,0},{2,3},{3,2},{4,5},{5,4},{6,7},{7,6},{8,9},{9,8},{10,11... | collective-permute-start | bytes 1179656 | tf_op jit(solution)/shard_map/ppermute | solution.py:376
  43.9 5.7 %collective-permute-start.14 = (f32[256,128]{1,0:T(8,128)S(1)}, f32[256,128]{1,0:T(8,128)S(1)}, u32[]{:S(2)}, u32[]{:S(2)}) collective-permute-start(f32[256,128]{1,0:T(8,128)S(1)} %get-tuple-element.65), channel_id=1, source_target_pairs={{0,4},{1,5},{2,6},{3,7},{4,0},{5,1},{6,2},{7,3},{8,12},{9,13},{10,... | collective-permute-start | bytes 393224 | tf_op jit(solution)/shard_map/ppermute | solution.py:376
  44.8 7.3 %collective-permute-start.15 = (f32[256,128]{1,0:T(8,128)S(1)}, f32[256,128]{1,0:T(8,128)S(1)}, u32[]{:S(2)}, u32[]{:S(2)}) collective-permute-start(f32[256,128]{1,0:T(8,128)S(1)} %get-tuple-element.66), channel_id=1, source_target_pairs={{0,2},{1,3},{2,0},{3,1},{4,6},{5,7},{6,4},{7,5},{8,10},{9,11},{10,... | collective-permute-start | bytes 393224 | tf_op jit(solution)/shard_map/ppermute | solution.py:376
  46.3 6.4 %collective-permute-start.16 = (f32[256,128]{1,0:T(8,128)S(1)}, f32[256,128]{1,0:T(8,128)S(1)}, u32[]{:S(2)}, u32[]{:S(2)}) collective-permute-start(f32[256,128]{1,0:T(8,128)S(1)} %get-tuple-element.67), channel_id=1, source_target_pairs={{0,5},{1,4},{2,7},{3,6},{4,1},{5,0},{6,3},{7,2},{8,13},{9,12},{10,... | collective-permute-start | bytes 393224 | tf_op jit(solution)/shard_map/ppermute | solution.py:376
  46.3 7.1 %collective-permute-start.17 = (f32[256,128]{1,0:T(8,128)S(1)}, f32[256,128]{1,0:T(8,128)S(1)}, u32[]{:S(2)}, u32[]{:S(2)}) collective-permute-start(f32[256,128]{1,0:T(8,128)S(1)} %get-tuple-element.68), channel_id=1, source_target_pairs={{0,3},{1,2},{2,1},{3,0},{4,7},{5,6},{6,5},{7,4},{8,11},{9,10},{10,... | collective-permute-start | bytes 393224 | tf_op jit(solution)/shard_map/ppermute | solution.py:376
  49.5 7.0 %collective-permute-start.18 = (f32[256,128]{1,0:T(8,128)S(1)}, f32[256,128]{1,0:T(8,128)S(1)}, u32[]{:S(2)}, u32[]{:S(2)}) collective-permute-start(f32[256,128]{1,0:T(8,128)S(1)} %get-tuple-element.69), channel_id=1, source_target_pairs={{0,6},{1,7},{2,4},{3,5},{4,2},{5,3},{6,0},{7,1},{8,14},{9,15},{10,... | collective-permute-start | bytes 393224 | tf_op jit(solution)/shard_map/ppermute | solution.py:376
  52.1 6.9 %collective-permute-start.19 = (f32[256,128]{1,0:T(8,128)S(1)}, f32[256,128]{1,0:T(8,128)S(1)}, u32[]{:S(2)}, u32[]{:S(2)}) collective-permute-start(f32[256,128]{1,0:T(8,128)S(1)} %get-tuple-element.70), channel_id=1, source_target_pairs={{0,7},{1,6},{2,5},{3,4},{4,3},{5,2},{6,1},{7,0},{8,15},{9,14},{10,... | collective-permute-start | bytes 393224 | tf_op jit(solution)/shard_map/ppermute | solution.py:376
  52.1 8.5 %collective-permute-start.20 = (f32[128,128]{1,0:T(8,128)S(1)}, f32[128,128]{1,0:T(8,128)S(1)}, u32[]{:S(2)}, u32[]{:S(2)}) collective-permute-start(f32[128,128]{1,0:T(8,128)S(1)} %get-tuple-element.73), channel_id=1, source_target_pairs={{0,4},{2,6},{4,0},{6,2},{1,5},{3,7},{5,1},{7,3},{8,12},{10,14},{12... | collective-permute-start | bytes 196616 | tf_op jit(solution)/shard_map/ppermute | solution.py:376
  52.7 7.9 %collective-permute-start.21 = (f32[128,128]{1,0:T(8,128)S(1)}, f32[128,128]{1,0:T(8,128)S(1)}, u32[]{:S(2)}, u32[]{:S(2)}) collective-permute-start(f32[128,128]{1,0:T(8,128)S(1)} %get-tuple-element.74), channel_id=1, source_target_pairs={{0,2},{2,0},{4,6},{6,4},{1,3},{3,1},{5,7},{7,5},{8,10},{10,8},{12,... | collective-permute-start | bytes 196616 | tf_op jit(solution)/shard_map/ppermute | solution.py:376
  53.4 8.5 %collective-permute-start.22 = (f32[128,128]{1,0:T(8,128)S(1)}, f32[128,128]{1,0:T(8,128)S(1)}, u32[]{:S(2)}, u32[]{:S(2)}) collective-permute-start(f32[128,128]{1,0:T(8,128)S(1)} %get-tuple-element.75), channel_id=1, source_target_pairs={{0,6},{2,4},{4,2},{6,0},{1,7},{3,5},{5,3},{7,1},{8,14},{10,12},{12... | collective-permute-start | bytes 196616 | tf_op jit(solution)/shard_map/ppermute | solution.py:376
  62.9 9.8 %collective-permute-start.23 = (f32[2,256,128]{2,1,0:T(8,128)S(1)}, f32[2,256,128]{2,1,0:T(8,128)S(1)}, u32[]{:S(2)}, u32[]{:S(2)}) collective-permute-start(f32[2,256,128]{2,1,0:T(8,128)S(1)} %get-tuple-element.77), channel_id=1, source_target_pairs={{0,8},{8,16},{16,24},{1,9},{9,17},{17,25},{2,10},{10,18},{18,26},{... | collective-permute-start | bytes 786440 | tf_op jit(solution)/shard_map/ppermute | solution.py:454
  66.4 7.0 %collective-permute-start.24 = (f32[64,256]{1,0:T(8,128)S(1)}, f32[64,256]{1,0:T(8,128)S(1)}, u32[]{:S(2)}, u32[]{:S(2)}) collective-permute-start(f32[64,256]{1,0:T(8,128)S(1)} %get-tuple-element.82), channel_id=1, source_target_pairs={{0,8},{8,0},{16,24},{24,16},{1,9},{9,1},{17,25},{25,17},{2,10},{10... | collective-permute-start | bytes 196616 | tf_op jit(solution)/shard_map/ppermute | solution.py:457
  73.5 5.9 %collective-permute-start.28 = (f32[64,256]{1,0:T(8,128)S(1)}, f32[64,256]{1,0:T(8,128)S(1)}, u32[]{:S(2)}, u32[]{:S(2)}) collective-permute-start(f32[64,256]{1,0:T(8,128)S(1)} %add.8), channel_id=1, source_target_pairs={{0,16},{8,24},{16,0},{24,8},{1,17},{9,25},{17,1},{25,9},{2,18},{10... | collective-permute-start | bytes 196616 | tf_op jit(solution)/shard_map/ppermute | solution.py:384
  75.7 12.5 %collective-permute-start.25 = (f32[256,128]{1,0:T(8,128)S(1)}, f32[256,128]{1,0:T(8,128)S(1)}, u32[]{:S(2)}, u32[]{:S(2)}) collective-permute-start(f32[256,128]{1,0:T(8,128)S(1)} %get-tuple-element.83), channel_id=1, source_target_pairs={{0,4},{2,6},{4,0},{6,2},{1,5},{3,7},{5,1},{7,3},{8,12},{10,14},{12... | collective-permute-start | bytes 393224 | tf_op jit(solution)/shard_map/ppermute | solution.py:376
  76.1 12.1 %collective-permute-start.26 = (f32[256,128]{1,0:T(8,128)S(1)}, f32[256,128]{1,0:T(8,128)S(1)}, u32[]{:S(2)}, u32[]{:S(2)}) collective-permute-start(f32[256,128]{1,0:T(8,128)S(1)} %get-tuple-element.84), channel_id=1, source_target_pairs={{0,2},{2,0},{4,6},{6,4},{1,3},{3,1},{5,7},{7,5},{8,10},{10,8},{12,... | collective-permute-start | bytes 393224 | tf_op jit(solution)/shard_map/ppermute | solution.py:376
  77.4 10.8 %collective-permute-start.27 = (f32[256,128]{1,0:T(8,128)S(1)}, f32[256,128]{1,0:T(8,128)S(1)}, u32[]{:S(2)}, u32[]{:S(2)}) collective-permute-start(f32[256,128]{1,0:T(8,128)S(1)} %get-tuple-element.85), channel_id=1, source_target_pairs={{0,6},{2,4},{4,2},{6,0},{1,7},{3,5},{5,3},{7,1},{8,14},{10,12},{12... | collective-permute-start | bytes 393224 | tf_op jit(solution)/shard_map/ppermute | solution.py:376

commit v24 on v23

--- a/solution.py
+++ b/solution.py
@@ -12,7 +12,7 @@
 
 GRAD_WEIGHT = 0.0625
 PLANE = ("half", "col", "core")
-EIGHT, BACK, FOUR = (2, 4, 3, 5, 6, 7, 1, 0), (1, 4, 2, 5, 3, 6, 7, 0), (2, 1, 3, 0)
+EIGHT, BACK, FOUR = (2, 4, 3, 5, 6, 7, 1, 0), (1, 2, 4, 3, 5, 6, 7, 0), (2, 1, 3, 0)
 VMEM_LIMIT = 24 * 1024 * 1024
 
 
@@ -131,10 +131,6 @@
     return 2 * (2 * col + core) + half
 
 
-def receivers():
-    return [slot_of(half, col, core) for half in range(2) for col in range(2) for core in range(2)]
-
-
 def slot_place(offs, mine, slot):
     lower = jnp.where(slot >= offs[4, 0], 1, 0)
     holder, at = jnp.bitwise_xor(2 * lower + slot // 4, mine), 2 * (slot % 4)
@@ -177,7 +173,7 @@
 
 
 def pick_kernel(offs, *refs):
-    gotten, below, outs, (own, parts) = dict(zip(FOUR, refs)), refs[4], refs[5:13], refs[13:]
+    gotten, below, outs, own = dict(zip(FOUR, refs)), refs[4], refs[5:13], refs[13]
     rows, cols = outs[0].shape
     half, col, core = here()
     mine = 2 * half + col
@@ -185,7 +181,9 @@
         own[jnp.bitwise_xor(mine, turn)] = gotten[turn][:rows]
     row_ids = lax.broadcasted_iota(jnp.int32, (rows, cols), 0)
     col_ids = lax.broadcasted_iota(jnp.int32, (rows, cols), 1) + core * cols
-    for place, slot in enumerate(receivers()):
+    for turn, out in zip(EIGHT, outs):
+        flat = jnp.bitwise_xor(2 * mine + core, turn)
+        slot = slot_of(flat // 4, (flat // 2) % 2, flat % 2)
         lower, row_at, col_at = slot_place(offs, mine, slot)
         upper_rows = row_ids >= row_at
         left_cols = col_ids >= col_at
@@ -196,9 +194,7 @@
             bottom = jnp.where(lower == 1, below[jnp.bitwise_xor(col, side)], second)
             return jnp.where(upper_rows, top, bottom)
 
-        parts[place] = jnp.where(left_cols, merged(0), merged(1))
-    for turn, out in zip(EIGHT, outs):
-        out[...] = parts[jnp.bitwise_xor(2 * mine + core, turn)]
+        out[...] = jnp.where(left_cols, merged(0), merged(1))
 
 
 def roll(value, rows, cols):
@@ -422,7 +418,7 @@
         scalars,
         (*own, below),
         32 * rows * width,
-        [(planes, rows, cols), (8, rows, cols)],
+        [(planes, rows, cols)],
     )
     tabs, factors, order = (jnp.asarray(table) for table in tables(width))
     probe, target, tabs = call(

time: 89.5 us -> 92.2 us (1.030)
  waiting for transfers between devices: 28.9 us -> 32.9 us
  starting transfers between devices: 34.5 us -> 32.1 us
  blocking collectives: 8.82 us -> 10 us
    ppermute x23, waiting for transfers between devices: 17.2 us -> 20.9 us  [deal(): lax.ppermute(value, axes, [(k, k ^ turn) for k in range(len(order))])]
    ppermute x23, starting transfers between devices: 24.3 us -> 21.9 us  [deal(): lax.ppermute(value, axes, [(k, k ^ turn) for k in range(len(order))])]
    all_gather x1, blocking collectives: 8.82 us -> 10 us  [local(): probe_grad = lax.all_gather(probe_band, PLANE, axis=0, tiled=True)]
where the time goes in v24:
time: 92.2 us; the launch traced here: 91.9 us
  waiting for transfers between devices  32.9 us (36%)
  starting transfers between devices  32.1 us (35%)
  Pallas kernels  12.9 us (14%)
  blocking collectives  10 us (11%)
  between operations  2.06 us (2%)
  local copies, waits for them, and re-layouts  1.79 us (2%)
    ppermute x23, starting transfers between devices, deal(): lax.ppermute(value, axes, [(k, k ^ turn) for k in range(len(order))])  21.9 us
    ppermute x23, waiting for transfers between devices, deal(): lax.ppermute(value, axes, [(k, k ^ turn) for k in range(len(order))])  20.9 us
    pallas_call x10, Pallas kernels, call(): pl.pallas_call(kernel, out_shape=[x for x, unused in outs], in_specs=[SME...  12.9 us
    all_gather x1, blocking collectives, local(): probe_grad = lax.all_gather(probe_band, PLANE, axis=0, tiled=True)  10 us
    ppermute x1, waiting for transfers between devices, local(): below = lax.ppermute(lowest, 'pair', [(k, k - 1) for k in range(1, pairs)])  7.61 us
    ppermute x1, starting transfers between devices, local(): lax.ppermute(lower_sums, 'pair', [(k, k + 1) for k in range(pairs - 1)])  3.52 us
    ppermute x1, waiting for transfers between devices, local(): lax.ppermute(lower_sums, 'pair', [(k, k + 1) for k in range(pairs - 1)])  3.48 us
    ppermute x1, starting transfers between devices, sum_over(): lax.ppermute(value, axis, [(k, k ^ step) for k in range(size)])  2.21 us
  transfers between devices with their start and end apart: 29, of which 13 were waited for; matrix products, arithmetic and copies ran while one was open for 2% of the time, Pallas kernels for 6%

profile of v24, /device:TPU:0, one launch (start us, length us, event | category | flops | bytes accessed | tf_op | source)
XLA Modules:
  0.0 91.9 jit_solution(18085373233376397244)
XLA Ops:
  0.6 1.3 %shard_map.95 = (f32[264,128]{1,0:T(8,128)S(1)}, f32[264,128]{1,0:T(8,128)S(1)}, f32[264,128]{1,0:T(8,128)S(1)}, f32[264,128]{1,0:T(8,128)S(1)}, f32[256,256]{1,0:T(8,128)S(1)}) custom-call(f32[4,256,128]{2,1,0:T(8,128)} %bitcast.9, f32[1,2,256,256]{3,2,1,0:T(8,128)} %measured.3, s32[1,2,2]{2,1,0:T(2,128)} %offsets_from.1), custom_call_target="tpu_custom_call" | custom-call | bytes 1851408 | tf_op jit(solution)/shard_map/pallas_call | solution.py:355
  1.9 3.0 %collective-permute-start = (f32[264,128]{1,0:T(8,128)S(1)}, f32[264,128]{1,0:T(8,128)S(1)}, u32[]{:S(2)}, u32[]{:S(2)}) collective-permute-start(f32[264,128]{1,0:T(8,128)S(1)} %get-tuple-element.47), channel_id=1, source_target_pairs={{0,2},{2,0},{4,6},{6,4},{1,3},{3,1},{5,7},{7,5},{8,10},{10,8},{12,... | collective-permute-start | bytes 405512 | tf_op jit(solution)/shard_map/ppermute | solution.py:372
  4.9 1.5 %collective-permute-start.1 = (f32[264,128]{1,0:T(8,128)S(1)}, f32[264,128]{1,0:T(8,128)S(1)}, u32[]{:S(2)}, u32[]{:S(2)}) collective-permute-start(f32[264,128]{1,0:T(8,128)S(1)} %get-tuple-element.48), channel_id=1, source_target_pairs={{0,4},{2,6},{4,0},{6,2},{1,5},{3,7},{5,1},{7,3},{8,12},{10,14},{12... | collective-permute-start | bytes 405512 | tf_op jit(solution)/shard_map/ppermute | solution.py:372
  6.5 0.1 slice_reduce_fusion.3
  6.6 1.3 %fusion = (s32[1,1]{1,0:T(1,128)}, s32[1,1]{1,0:T(1,128)}) fusion(s32[1,2]{1,0:T(1,128)} %param.11), kind=kLoop, calls=%fused_computation.8 | loop fusion | bytes 16 | tf_op jit(solution)/shard_map/slice | solution.py:412
  9.2 0.1 slice_reduce_fusion.2
  9.3 3.5 %collective-permute-done.1.refs_0_ = f32[264,128]{1,0:T(8,128)S(1)} collective-permute-done((f32[264,128]{1,0:T(8,128)S(1)}, f32[264,128]{1,0:T(8,128)S(1)}, u32[]{:S(2)}, u32[]{:S(2)}) %collective-permute-start.1) | collective-permute-done | bytes 135200 | tf_op jit(solution)/shard_map/ppermute | solution.py:372
  12.9 0.1 slice_reduce_fusion.1
  13.0 0.1 slice_reduce_fusion
  13.2 1.3 %collective-permute-start.4 = (f32[2,256,128]{2,1,0:T(8,128)S(1)}, f32[2,256,128]{2,1,0:T(8,128)S(1)}, u32[]{:S(2)}, u32[]{:S(2)}) collective-permute-start(f32[2,256,128]{2,1,0:T(8,128)S(1)} %shard_map.96), channel_id=1, source_target_pairs={{8,0},{16,8},{24,16},{9,1},{17,9},{25,17},{10,2},{18,10},{26,18},{... | collective-permute-start | bytes 786440 | tf_op jit(solution)/shard_map/ppermute | solution.py:405
  14.5 1.6 %collective-permute-start.12 = (f32[256,256]{1,0:T(8,128)S(1)}, f32[256,256]{1,0:T(8,128)S(1)}, u32[]{:S(2)}, u32[]{:S(2)}) collective-permute-start(f32[256,256]{1,0:T(8,128)S(1)} %get-tuple-element.60), channel_id=1, source_target_pairs={{0,4},{4,0},{1,5},{5,1},{2,6},{6,2},{3,7},{7,3},{8,12},{12,8},{9,1... | collective-permute-start | bytes 786440 | tf_op jit(solution)/shard_map/ppermute | solution.py:406
  16.2 7.6 %collective-permute-done.4.refs_4_ = f32[2,256,128]{2,1,0:T(8,128)S(1)} collective-permute-done((f32[2,256,128]{2,1,0:T(8,128)S(1)}, f32[2,256,128]{2,1,0:T(8,128)S(1)}, u32[]{:S(2)}, u32[]{:S(2)}) %collective-permute-start.4) | collective-permute-done | bytes 262176 | tf_op jit(solution)/shard_map/ppermute | solution.py:405
  23.8 1.3 %shard_map.97 = (f32[256,128]{1,0:T(8,128)S(1)}, f32[256,128]{1,0:T(8,128)S(1)}, f32[256,128]{1,0:T(8,128)S(1)}, f32[256,128]{1,0:T(8,128)S(1)}, f32[256,128]{1,...) custom-call(s32[5,8]{1,0:T(8,128)S(1)} %concatenate.7.offs, ...), custom_call_target="tpu_custom_call" | custom-call | flops 2097152 | bytes 1851392 | tf_op jit(solution)/shard_map/pallas_call | solution.py:355
  25.1 1.2 %collective-permute-start.5 = (f32[256,128]{1,0:T(8,128)S(1)}, f32[256,128]{1,0:T(8,128)S(1)}, u32[]{:S(2)}, u32[]{:S(2)}) collective-permute-start(f32[256,128]{1,0:T(8,128)S(1)} %get-tuple-element.52), channel_id=1, source_target_pairs={{0,2},{1,3},{2,0},{3,1},{4,6},{5,7},{6,4},{7,5},{8,10},{9,11},{10,... | collective-permute-start | bytes 393224 | tf_op jit(solution)/shard_map/ppermute | solution.py:372
  26.3 0.9 %collective-permute-start.6 = (f32[256,128]{1,0:T(8,128)S(1)}, f32[256,128]{1,0:T(8,128)S(1)}, u32[]{:S(2)}, u32[]{:S(2)}) collective-permute-start(f32[256,128]{1,0:T(8,128)S(1)} %get-tuple-element.53), channel_id=1, source_target_pairs={{0,4},{1,5},{2,6},{3,7},{4,0},{5,1},{6,2},{7,3},{8,12},{9,13},{10,... | collective-permute-start | bytes 393224 | tf_op jit(solution)/shard_map/ppermute | solution.py:372
  27.2 0.2 collective-permute-start.7
  27.5 1.5 %collective-permute-start.8 = (f32[256,128]{1,0:T(8,128)S(1)}, f32[256,128]{1,0:T(8,128)S(1)}, u32[]{:S(2)}, u32[]{:S(2)}) collective-permute-start(f32[256,128]{1,0:T(8,128)S(1)} %get-tuple-element.55), channel_id=1, source_target_pairs={{0,5},{1,4},{2,7},{3,6},{4,1},{5,0},{6,3},{7,2},{8,13},{9,12},{10,... | collective-permute-start | bytes 393224 | tf_op jit(solution)/shard_map/ppermute | solution.py:372
  29.0 1.5 %collective-permute-start.9 = (f32[256,128]{1,0:T(8,128)S(1)}, f32[256,128]{1,0:T(8,128)S(1)}, u32[]{:S(2)}, u32[]{:S(2)}) collective-permute-start(f32[256,128]{1,0:T(8,128)S(1)} %get-tuple-element.56), channel_id=1, source_target_pairs={{0,6},{1,7},{2,4},{3,5},{4,2},{5,3},{6,0},{7,1},{8,14},{9,15},{10,... | collective-permute-start | bytes 393224 | tf_op jit(solution)/shard_map/ppermute | solution.py:372
  30.5 0.7 collective-permute-start.10
  31.1 1.0 %collective-permute-done.6.refs_1_ = f32[256,128]{1,0:T(8,128)S(1)} collective-permute-done((f32[256,128]{1,0:T(8,128)S(1)}, f32[256,128]{1,0:T(8,128)S(1)}, u32[]{:S(2)}, u32[]{:S(2)}) %collective-permute-start.6) | collective-permute-done | bytes 131104 | tf_op jit(solution)/shard_map/ppermute | solution.py:372
  32.1 2.5 %shard_map.98 = (f32[2,256,256]{2,1,0:T(8,128)S(1)}, f32[256,256]{1,0:T(8,128)S(1)}, bf16[6,512,256]{2,1,0:T(8,128)(2,1)S(1)}) custom-call(s32[5,8]{1,0:T(8,128)S(1)} %concatenate.7.offs, f32[256,256]{1,0:T(8,128)S(1)} %collective-permute-done.12.taken, f32[2,256,256]{2,1,0:T(8,128)} %probe_from.1, f32[1,2,256,256]{3,2,1,0:T(8,128)} %measured.3, ...), custom_call_target="tpu_custom_call" | custom-call | flops 201326592 | bytes 5505024 | tf_op jit(solution)/shard_map/pallas_call | solution.py:355
  34.6 3.5 %collective-permute-done.8.refs_3_ = f32[256,128]{1,0:T(8,128)S(1)} collective-permute-done((f32[256,128]{1,0:T(8,128)S(1)}, f32[256,128]{1,0:T(8,128)S(1)}, u32[]{:S(2)}, u32[]{:S(2)}) %collective-permute-start.8) | collective-permute-done | bytes 131104 | tf_op jit(solution)/shard_map/ppermute | solution.py:372
  38.2 1.0 %collective-permute-done.10.refs_5_ = f32[256,128]{1,0:T(8,128)S(1)} collective-permute-done((f32[256,128]{1,0:T(8,128)S(1)}, f32[256,128]{1,0:T(8,128)S(1)}, u32[]{:S(2)}, u32[]{:S(2)}) %collective-permute-start.10) | collective-permute-done | bytes 131104 | tf_op jit(solution)/shard_map/ppermute | solution.py:372
  39.2 4.2 %shard_map.99 = (f32[768,128]{1,0:T(8,128)S(1)}, f32[256,128]{1,0:T(8,128)S(1)}, f32[256,128]{1,0:T(8,128)S(1)}, f32[256,128]{1,0:T(8,128)S(1)}, f32[256,128]{1,...) custom-call(s32[5,8]{1,0:T(8,128)S(1)} %concatenate.7.offs, ...), custom_call_target="tpu_custom_call" | custom-call | flops 1610612736 | bytes 5120000 | tf_op jit(solution)/shard_map/pallas_call | solution.py:355
  43.4 0.4 collective-permute-start.13
  43.8 0.9 %collective-permute-start.14 = (f32[256,128]{1,0:T(8,128)S(1)}, f32[256,128]{1,0:T(8,128)S(1)}, u32[]{:S(2)}, u32[]{:S(2)}) collective-permute-start(f32[256,128]{1,0:T(8,128)S(1)} %get-tuple-element.65), channel_id=1, source_target_pairs={{0,2},{1,3},{2,0},{3,1},{4,6},{5,7},{6,4},{7,5},{8,10},{9,11},{10,... | collective-permute-start | bytes 393224 | tf_op jit(solution)/shard_map/ppermute | solution.py:372
  44.7 1.5 %collective-permute-start.15 = (f32[256,128]{1,0:T(8,128)S(1)}, f32[256,128]{1,0:T(8,128)S(1)}, u32[]{:S(2)}, u32[]{:S(2)}) collective-permute-start(f32[256,128]{1,0:T(8,128)S(1)} %get-tuple-element.66), channel_id=1, source_target_pairs={{0,4},{1,5},{2,6},{3,7},{4,0},{5,1},{6,2},{7,3},{8,12},{9,13},{10,... | collective-permute-start | bytes 393224 | tf_op jit(solution)/shard_map/ppermute | solution.py:372
  46.2 1.3 %collective-permute-start.17 = (f32[256,128]{1,0:T(8,128)S(1)}, f32[256,128]{1,0:T(8,128)S(1)}, u32[]{:S(2)}, u32[]{:S(2)}) collective-permute-start(f32[256,128]{1,0:T(8,128)S(1)} %get-tuple-element.68), channel_id=1, source_target_pairs={{0,5},{1,4},{2,7},{3,6},{4,1},{5,0},{6,3},{7,2},{8,13},{9,12},{10,... | collective-permute-start | bytes 393224 | tf_op jit(solution)/shard_map/ppermute | solution.py:372
  47.6 2.0 %collective-permute-done.14.refs_1_ = f32[256,128]{1,0:T(8,128)S(1)} collective-permute-done((f32[256,128]{1,0:T(8,128)S(1)}, f32[256,128]{1,0:T(8,128)S(1)}, u32[]{:S(2)}, u32[]{:S(2)}) %collective-permute-start.14) | collective-permute-done | bytes 131104 | tf_op jit(solution)/shard_map/ppermute | solution.py:372
  49.5 2.5 %collective-permute-start.18 = (f32[256,128]{1,0:T(8,128)S(1)}, f32[256,128]{1,0:T(8,128)S(1)}, u32[]{:S(2)}, u32[]{:S(2)}) collective-permute-start(f32[256,128]{1,0:T(8,128)S(1)} %get-tuple-element.69), channel_id=1, source_target_pairs={{0,6},{1,7},{2,4},{3,5},{4,2},{5,3},{6,0},{7,1},{8,14},{9,15},{10,... | collective-permute-start | bytes 393224 | tf_op jit(solution)/shard_map/ppermute | solution.py:372
  52.0 0.6 collective-permute-start.20
  52.6 0.7 collective-permute-start.21
  53.3 4.3 %collective-permute-done.17.refs_4_ = f32[256,128]{1,0:T(8,128)S(1)} collective-permute-done((f32[256,128]{1,0:T(8,128)S(1)}, f32[256,128]{1,0:T(8,128)S(1)}, u32[]{:S(2)}, u32[]{:S(2)}) %collective-permute-start.17) | collective-permute-done | bytes 131104 | tf_op jit(solution)/shard_map/ppermute | solution.py:372
  57.6 1.2 %collective-permute-done.19.refs_6_ = f32[256,128]{1,0:T(8,128)S(1)} collective-permute-done((f32[256,128]{1,0:T(8,128)S(1)}, f32[256,128]{1,0:T(8,128)S(1)}, u32[]{:S(2)}, u32[]{:S(2)}) %collective-permute-start.19) | collective-permute-done | bytes 131104 | tf_op jit(solution)/shard_map/ppermute | solution.py:372
  58.7 1.2 %collective-permute-done.20.refs_8_ = f32[128,128]{1,0:T(8,128)S(1)} collective-permute-done((f32[128,128]{1,0:T(8,128)S(1)}, f32[128,128]{1,0:T(8,128)S(1)}, u32[]{:S(2)}, u32[]{:S(2)}) %collective-permute-start.20) | collective-permute-done | bytes 65568 | tf_op jit(solution)/shard_map/ppermute | solution.py:372
  60.0 3.1 %collective-permute-done.22.refs_10_ = f32[128,128]{1,0:T(8,128)S(1)} collective-permute-done((f32[128,128]{1,0:T(8,128)S(1)}, f32[128,128]{1,0:T(8,128)S(1)}, u32[]{:S(2)}, u32[]{:S(2)}) %collective-permute-start.22) | collective-permute-done | bytes 65568 | tf_op jit(solution)/shard_map/ppermute | solution.py:372
  63.1 1.0 %shard_map.102 = (f32[2,256,128]{2,1,0:T(8,128)S(1)}, f32[64,256]{1,0:T(8,128)S(1)}) custom-call(s32[5,8]{1,0:T(8,128)S(1)} %concatenate.7.offs, f32[768,128]{1,0:T(8,128)S(1)} %collective-permute-done.13.refs_0_.got, f32[256,128]{1,0:T(8,128)S(1)} %collective-permute-done.14.refs_1_, f32[256,128]{1,0:T(8,128)S(1)} %collective-permute-done.15.refs_2_, ...), custom_call_target="tpu_custom_call" | custom-call | flops 2097152 | bytes 1900544 | tf_op jit(solution)/shard_map/pallas_call | solution.py:355
  64.2 3.5 %collective-permute-start.23 = (f32[2,256,128]{2,1,0:T(8,128)S(1)}, f32[2,256,128]{2,1,0:T(8,128)S(1)}, u32[]{:S(2)}, u32[]{:S(2)}) collective-permute-start(f32[2,256,128]{2,1,0:T(8,128)S(1)} %get-tuple-element.77), channel_id=1, source_target_pairs={{0,8},{8,16},{16,24},{1,9},{9,17},{17,25},{2,10},{10,18},{18,26},{... | collective-permute-start | bytes 786440 | tf_op jit(solution)/shard_map/ppermute | solution.py:450
  67.7 1.6 %collective-permute-start.24 = (f32[64,256]{1,0:T(8,128)S(1)}, f32[64,256]{1,0:T(8,128)S(1)}, u32[]{:S(2)}, u32[]{:S(2)}) collective-permute-start(f32[64,256]{1,0:T(8,128)S(1)} %get-tuple-element.82), channel_id=1, source_target_pairs={{0,8},{8,0},{16,24},{24,16},{1,9},{9,1},{17,25},{25,17},{2,10},{10... | collective-permute-start | bytes 196616 | tf_op jit(solution)/shard_map/ppermute | solution.py:453
  69.3 1.5 %shard_map.100.own = f32[4,256,128]{2,1,0:T(8,128)S(1)} custom-call(s32[5,8]{1,0:T(8,128)S(1)} %concatenate.7.offs, f32[768,128]{1,0:T(8,128)S(1)} %collective-permute-done.13.refs_0_.got, f32[256,128]{1,0:T(8,128)S(1)} %collective-permute-done.14.refs_1_, f32[256,128]{1,0:T(8,128)S(1)} %collective-permute-done.15.refs_2_, ...), custom_call_target="tpu_custom_call" | custom-call | flops 4194304 | bytes 1835008 | tf_op jit(solution)/shard_map/pallas_call | solution.py:355
  70.7 3.5 %collective-permute-done.23.above = f32[2,256,128]{2,1,0:T(8,128)S(1)} collective-permute-done((f32[2,256,128]{2,1,0:T(8,128)S(1)}, f32[2,256,128]{2,1,0:T(8,128)S(1)}, u32[]{:S(2)}, u32[]{:S(2)}) %collective-permute-start.23) | collective-permute-done | bytes 262176 | tf_op jit(solution)/shard_map/ppermute | solution.py:450
  74.3 0.6 collective-permute-done.24
  74.9 2.2 %collective-permute-start.28 = (f32[64,256]{1,0:T(8,128)S(1)}, f32[64,256]{1,0:T(8,128)S(1)}, u32[]{:S(2)}, u32[]{:S(2)}) collective-permute-start(f32[64,256]{1,0:T(8,128)S(1)} %add.8), channel_id=1, source_target_pairs={{0,16},{8,24},{16,0},{24,8},{1,17},{9,25},{17,1},{25,9},{2,18},{10... | collective-permute-start | bytes 196616 | tf_op jit(solution)/shard_map/ppermute | solution.py:380
  77.1 0.8 collective-permute-start.25
  77.9 2.7 %collective-permute-start.27 = (f32[256,128]{1,0:T(8,128)S(1)}, f32[256,128]{1,0:T(8,128)S(1)}, u32[]{:S(2)}, u32[]{:S(2)}) collective-permute-start(f32[256,128]{1,0:T(8,128)S(1)} %get-tuple-element.85), channel_id=1, source_target_pairs={{0,6},{2,4},{4,2},{6,0},{1,7},{3,5},{5,3},{7,1},{8,14},{10,12},{12... | collective-permute-start | bytes 393224 | tf_op jit(solution)/shard_map/ppermute | solution.py:372
  80.6 0.2 collective-permute-done.28
  80.9 10.0 %all_gather.3.refs_4_ = f32[512,256]{1,0:T(8,128)S(1)} all-gather(f32[64,256]{1,0:T(8,128)S(1)} %add.9), channel_id=1, replica_groups=mesh['pair'=4,'half'=2,'col'=2,'core'=2] {'half','col','core'}, dimensions={0}, use_global_device_ids=true | all-gather | bytes 589824 | tf_op jit(solution)/shard_map/all_gather | solution.py:462
  90.9 1.0 %shard_map.104 = (f32[4,256,128]{2,1,0:T(8,128)}, f32[512,256]{1,0:T(8,128)}) custom-call(f32[256,128]{1,0:T(8,128)S(1)} %collective-permute-done.25.refs_0_, f32[256,128]{1,0:T(8,128)S(1)} %collective-permute-done.26.refs_1_, f32[256,128]{1,0:T(8,128)S(1)} %collective-permute-done.27.refs_2_, f32[256,128]{1,0:T(8,128)S(1)} %get-tuple-element.86.refs_3_, ...), custom_call_target="tpu_custom_call" | custom-call | bytes 2097152 | tf_op jit(solution)/shard_map/pallas_call | solution.py:355
  (34 shorter events, 0.4 us)
Async XLA Ops:
  1.9 7.3 %collective-permute-start = (f32[264,128]{1,0:T(8,128)S(1)}, f32[264,128]{1,0:T(8,128)S(1)}, u32[]{:S(2)}, u32[]{:S(2)}) collective-permute-start(f32[264,128]{1,0:T(8,128)S(1)} %get-tuple-element.47), channel_id=1, source_target_pairs={{0,2},{2,0},{4,6},{6,4},{1,3},{3,1},{5,7},{7,5},{8,10},{10,8},{12,... | collective-permute-start | bytes 405512 | tf_op jit(solution)/shard_map/ppermute | solution.py:372
  4.9 7.9 %collective-permute-start.1 = (f32[264,128]{1,0:T(8,128)S(1)}, f32[264,128]{1,0:T(8,128)S(1)}, u32[]{:S(2)}, u32[]{:S(2)}) collective-permute-start(f32[264,128]{1,0:T(8,128)S(1)} %get-tuple-element.48), channel_id=1, source_target_pairs={{0,4},{2,6},{4,0},{6,2},{1,5},{3,7},{5,1},{7,3},{8,12},{10,14},{12... | collective-permute-start | bytes 405512 | tf_op jit(solution)/shard_map/ppermute | solution.py:372
  6.4 6.5 %collective-permute-start.2 = (f32[264,128]{1,0:T(8,128)S(1)}, f32[264,128]{1,0:T(8,128)S(1)}, u32[]{:S(2)}, u32[]{:S(2)}) collective-permute-start(f32[264,128]{1,0:T(8,128)S(1)} %get-tuple-element.49), channel_id=1, source_target_pairs={{0,6},{2,4},{4,2},{6,0},{1,7},{3,5},{5,3},{7,1},{8,14},{10,12},{12... | collective-permute-start | bytes 405512 | tf_op jit(solution)/shard_map/ppermute | solution.py:372
  13.1 3.0 %collective-permute-start.3 = (s32[4,4]{1,0:T(4,128)S(1)}, s32[4,4]{1,0:T(4,128)S(1)}, u32[]{:S(2)}, u32[]{:S(2)}) collective-permute-start(s32[4,4]{1,0:T(4,128)S(1)} %maximum_convert_fusion), channel_id=1, source_target_pairs={{0,1},{1,0},{2,3},{3,2},{4,5},{5,4},{6,7},{7,6},{8,9},{9,8},{10,11... | collective-permute-start | bytes 200 | tf_op jit(solution)/shard_map/ppermute | solution.py:410
  13.2 10.6 %collective-permute-start.4 = (f32[2,256,128]{2,1,0:T(8,128)S(1)}, f32[2,256,128]{2,1,0:T(8,128)S(1)}, u32[]{:S(2)}, u32[]{:S(2)}) collective-permute-start(f32[2,256,128]{2,1,0:T(8,128)S(1)} %shard_map.96), channel_id=1, source_target_pairs={{8,0},{16,8},{24,16},{9,1},{17,9},{25,17},{10,2},{18,10},{26,18},{... | collective-permute-start | bytes 786440 | tf_op jit(solution)/shard_map/ppermute | solution.py:405
  14.5 14.4 %collective-permute-start.12 = (f32[256,256]{1,0:T(8,128)S(1)}, f32[256,256]{1,0:T(8,128)S(1)}, u32[]{:S(2)}, u32[]{:S(2)}) collective-permute-start(f32[256,256]{1,0:T(8,128)S(1)} %get-tuple-element.60), channel_id=1, source_target_pairs={{0,4},{4,0},{1,5},{5,1},{2,6},{6,2},{3,7},{7,3},{8,12},{12,8},{9,1... | collective-permute-start | bytes 786440 | tf_op jit(solution)/shard_map/ppermute | solution.py:406
  25.1 5.3 %collective-permute-start.5 = (f32[256,128]{1,0:T(8,128)S(1)}, f32[256,128]{1,0:T(8,128)S(1)}, u32[]{:S(2)}, u32[]{:S(2)}) collective-permute-start(f32[256,128]{1,0:T(8,128)S(1)} %get-tuple-element.52), channel_id=1, source_target_pairs={{0,2},{1,3},{2,0},{3,1},{4,6},{5,7},{6,4},{7,5},{8,10},{9,11},{10,... | collective-permute-start | bytes 393224 | tf_op jit(solution)/shard_map/ppermute | solution.py:372
  26.3 5.8 %collective-permute-start.6 = (f32[256,128]{1,0:T(8,128)S(1)}, f32[256,128]{1,0:T(8,128)S(1)}, u32[]{:S(2)}, u32[]{:S(2)}) collective-permute-start(f32[256,128]{1,0:T(8,128)S(1)} %get-tuple-element.53), channel_id=1, source_target_pairs={{0,4},{1,5},{2,6},{3,7},{4,0},{5,1},{6,2},{7,3},{8,12},{9,13},{10,... | collective-permute-start | bytes 393224 | tf_op jit(solution)/shard_map/ppermute | solution.py:372
  27.2 7.4 %collective-permute-start.7 = (f32[256,128]{1,0:T(8,128)S(1)}, f32[256,128]{1,0:T(8,128)S(1)}, u32[]{:S(2)}, u32[]{:S(2)}) collective-permute-start(f32[256,128]{1,0:T(8,128)S(1)} %get-tuple-element.54), channel_id=1, source_target_pairs={{0,3},{1,2},{2,1},{3,0},{4,7},{5,6},{6,5},{7,4},{8,11},{9,10},{10,... | collective-permute-start | bytes 393224 | tf_op jit(solution)/shard_map/ppermute | solution.py:372
  27.5 10.7 %collective-permute-start.8 = (f32[256,128]{1,0:T(8,128)S(1)}, f32[256,128]{1,0:T(8,128)S(1)}, u32[]{:S(2)}, u32[]{:S(2)}) collective-permute-start(f32[256,128]{1,0:T(8,128)S(1)} %get-tuple-element.55), channel_id=1, source_target_pairs={{0,5},{1,4},{2,7},{3,6},{4,1},{5,0},{6,3},{7,2},{8,13},{9,12},{10,... | collective-permute-start | bytes 393224 | tf_op jit(solution)/shard_map/ppermute | solution.py:372
  29.0 9.2 %collective-permute-start.9 = (f32[256,128]{1,0:T(8,128)S(1)}, f32[256,128]{1,0:T(8,128)S(1)}, u32[]{:S(2)}, u32[]{:S(2)}) collective-permute-start(f32[256,128]{1,0:T(8,128)S(1)} %get-tuple-element.56), channel_id=1, source_target_pairs={{0,6},{1,7},{2,4},{3,5},{4,2},{5,3},{6,0},{7,1},{8,14},{9,15},{10,... | collective-permute-start | bytes 393224 | tf_op jit(solution)/shard_map/ppermute | solution.py:372
  30.5 8.7 %collective-permute-start.10 = (f32[256,128]{1,0:T(8,128)S(1)}, f32[256,128]{1,0:T(8,128)S(1)}, u32[]{:S(2)}, u32[]{:S(2)}) collective-permute-start(f32[256,128]{1,0:T(8,128)S(1)} %get-tuple-element.57), channel_id=1, source_target_pairs={{0,7},{1,6},{2,5},{3,4},{4,3},{5,2},{6,1},{7,0},{8,15},{9,14},{10,... | collective-permute-start | bytes 393224 | tf_op jit(solution)/shard_map/ppermute | solution.py:372
  32.1 7.1 %copy-start = (f32[2,136,128]{2,1,0:T(8,128)S(1)}, f32[2,136,128]{2,1,0:T(8,128)}, u32[]{:S(2)}) copy-start(f32[2,136,128]{2,1,0:T(8,128)} %constant.17.clone.refs_11_) | copy-start | bytes 417796
  32.1 7.1 %collective-permute-start.11 = (f32[256,128]{1,0:T(8,128)S(1)}, f32[256,128]{1,0:T(8,128)S(1)}, u32[]{:S(2)}, u32[]{:S(2)}) collective-permute-start(f32[256,128]{1,0:T(8,128)S(1)} %get-tuple-element.58), channel_id=1, source_target_pairs={{0,1},{1,0},{2,3},{3,2},{4,5},{5,4},{6,7},{7,6},{8,9},{9,8},{10,11... | collective-permute-start | bytes 393224 | tf_op jit(solution)/shard_map/ppermute | solution.py:372
  43.4 8.6 %collective-permute-start.13 = (f32[768,128]{1,0:T(8,128)S(1)}, f32[768,128]{1,0:T(8,128)S(1)}, u32[]{:S(2)}, u32[]{:S(2)}) collective-permute-start(f32[768,128]{1,0:T(8,128)S(1)} %get-tuple-element.64), channel_id=1, source_target_pairs={{0,1},{1,0},{2,3},{3,2},{4,5},{5,4},{6,7},{7,6},{8,9},{9,8},{10,11... | collective-permute-start | bytes 1179656 | tf_op jit(solution)/shard_map/ppermute | solution.py:372
  43.8 5.7 %collective-permute-start.14 = (f32[256,128]{1,0:T(8,128)S(1)}, f32[256,128]{1,0:T(8,128)S(1)}, u32[]{:S(2)}, u32[]{:S(2)}) collective-permute-start(f32[256,128]{1,0:T(8,128)S(1)} %get-tuple-element.65), channel_id=1, source_target_pairs={{0,2},{1,3},{2,0},{3,1},{4,6},{5,7},{6,4},{7,5},{8,10},{9,11},{10,... | collective-permute-start | bytes 393224 | tf_op jit(solution)/shard_map/ppermute | solution.py:372
  44.7 7.3 %collective-permute-start.15 = (f32[256,128]{1,0:T(8,128)S(1)}, f32[256,128]{1,0:T(8,128)S(1)}, u32[]{:S(2)}, u32[]{:S(2)}) collective-permute-start(f32[256,128]{1,0:T(8,128)S(1)} %get-tuple-element.66), channel_id=1, source_target_pairs={{0,4},{1,5},{2,6},{3,7},{4,0},{5,1},{6,2},{7,3},{8,12},{9,13},{10,... | collective-permute-start | bytes 393224 | tf_op jit(solution)/shard_map/ppermute | solution.py:372
  46.2 6.4 %collective-permute-start.16 = (f32[256,128]{1,0:T(8,128)S(1)}, f32[256,128]{1,0:T(8,128)S(1)}, u32[]{:S(2)}, u32[]{:S(2)}) collective-permute-start(f32[256,128]{1,0:T(8,128)S(1)} %get-tuple-element.67), channel_id=1, source_target_pairs={{0,3},{1,2},{2,1},{3,0},{4,7},{5,6},{6,5},{7,4},{8,11},{9,10},{10,... | collective-permute-start | bytes 393224 | tf_op jit(solution)/shard_map/ppermute | solution.py:372
  46.2 11.4 %collective-permute-start.17 = (f32[256,128]{1,0:T(8,128)S(1)}, f32[256,128]{1,0:T(8,128)S(1)}, u32[]{:S(2)}, u32[]{:S(2)}) collective-permute-start(f32[256,128]{1,0:T(8,128)S(1)} %get-tuple-element.68), channel_id=1, source_target_pairs={{0,5},{1,4},{2,7},{3,6},{4,1},{5,0},{6,3},{7,2},{8,13},{9,12},{10,... | collective-permute-start | bytes 393224 | tf_op jit(solution)/shard_map/ppermute | solution.py:372
  49.5 8.1 %collective-permute-start.18 = (f32[256,128]{1,0:T(8,128)S(1)}, f32[256,128]{1,0:T(8,128)S(1)}, u32[]{:S(2)}, u32[]{:S(2)}) collective-permute-start(f32[256,128]{1,0:T(8,128)S(1)} %get-tuple-element.69), channel_id=1, source_target_pairs={{0,6},{1,7},{2,4},{3,5},{4,2},{5,3},{6,0},{7,1},{8,14},{9,15},{10,... | collective-permute-start | bytes 393224 | tf_op jit(solution)/shard_map/ppermute | solution.py:372
  52.0 6.8 %collective-permute-start.19 = (f32[256,128]{1,0:T(8,128)S(1)}, f32[256,128]{1,0:T(8,128)S(1)}, u32[]{:S(2)}, u32[]{:S(2)}) collective-permute-start(f32[256,128]{1,0:T(8,128)S(1)} %get-tuple-element.70), channel_id=1, source_target_pairs={{0,7},{1,6},{2,5},{3,4},{4,3},{5,2},{6,1},{7,0},{8,15},{9,14},{10,... | collective-permute-start | bytes 393224 | tf_op jit(solution)/shard_map/ppermute | solution.py:372
  52.0 7.9 %collective-permute-start.20 = (f32[128,128]{1,0:T(8,128)S(1)}, f32[128,128]{1,0:T(8,128)S(1)}, u32[]{:S(2)}, u32[]{:S(2)}) collective-permute-start(f32[128,128]{1,0:T(8,128)S(1)} %get-tuple-element.73), channel_id=1, source_target_pairs={{0,4},{2,6},{4,0},{6,2},{1,5},{3,7},{5,1},{7,3},{8,12},{10,14},{12... | collective-permute-start | bytes 196616 | tf_op jit(solution)/shard_map/ppermute | solution.py:372
  52.6 7.3 %collective-permute-start.21 = (f32[128,128]{1,0:T(8,128)S(1)}, f32[128,128]{1,0:T(8,128)S(1)}, u32[]{:S(2)}, u32[]{:S(2)}) collective-permute-start(f32[128,128]{1,0:T(8,128)S(1)} %get-tuple-element.74), channel_id=1, source_target_pairs={{0,2},{2,0},{4,6},{6,4},{1,3},{3,1},{5,7},{7,5},{8,10},{10,8},{12,... | collective-permute-start | bytes 196616 | tf_op jit(solution)/shard_map/ppermute | solution.py:372
  57.6 5.6 %collective-permute-start.22 = (f32[128,128]{1,0:T(8,128)S(1)}, f32[128,128]{1,0:T(8,128)S(1)}, u32[]{:S(2)}, u32[]{:S(2)}) collective-permute-start(f32[128,128]{1,0:T(8,128)S(1)} %get-tuple-element.75), channel_id=1, source_target_pairs={{0,6},{2,4},{4,2},{6,0},{1,7},{3,5},{5,3},{7,1},{8,14},{10,12},{12... | collective-permute-start | bytes 196616 | tf_op jit(solution)/shard_map/ppermute | solution.py:372
  64.2 10.0 %collective-permute-start.23 = (f32[2,256,128]{2,1,0:T(8,128)S(1)}, f32[2,256,128]{2,1,0:T(8,128)S(1)}, u32[]{:S(2)}, u32[]{:S(2)}) collective-permute-start(f32[2,256,128]{2,1,0:T(8,128)S(1)} %get-tuple-element.77), channel_id=1, source_target_pairs={{0,8},{8,16},{16,24},{1,9},{9,17},{17,25},{2,10},{10,18},{18,26},{... | collective-permute-start | bytes 786440 | tf_op jit(solution)/shard_map/ppermute | solution.py:450
  67.7 7.2 %collective-permute-start.24 = (f32[64,256]{1,0:T(8,128)S(1)}, f32[64,256]{1,0:T(8,128)S(1)}, u32[]{:S(2)}, u32[]{:S(2)}) collective-permute-start(f32[64,256]{1,0:T(8,128)S(1)} %get-tuple-element.82), channel_id=1, source_target_pairs={{0,8},{8,0},{16,24},{24,16},{1,9},{9,1},{17,25},{25,17},{2,10},{10... | collective-permute-start | bytes 196616 | tf_op jit(solution)/shard_map/ppermute | solution.py:453
  74.9 5.9 %collective-permute-start.28 = (f32[64,256]{1,0:T(8,128)S(1)}, f32[64,256]{1,0:T(8,128)S(1)}, u32[]{:S(2)}, u32[]{:S(2)}) collective-permute-start(f32[64,256]{1,0:T(8,128)S(1)} %add.8), channel_id=1, source_target_pairs={{0,16},{8,24},{16,0},{24,8},{1,17},{9,25},{17,1},{25,9},{2,18},{10... | collective-permute-start | bytes 196616 | tf_op jit(solution)/shard_map/ppermute | solution.py:380
  77.1 13.8 %collective-permute-start.25 = (f32[256,128]{1,0:T(8,128)S(1)}, f32[256,128]{1,0:T(8,128)S(1)}, u32[]{:S(2)}, u32[]{:S(2)}) collective-permute-start(f32[256,128]{1,0:T(8,128)S(1)} %get-tuple-element.83), channel_id=1, source_target_pairs={{0,4},{2,6},{4,0},{6,2},{1,5},{3,7},{5,1},{7,3},{8,12},{10,14},{12... | collective-permute-start | bytes 393224 | tf_op jit(solution)/shard_map/ppermute | solution.py:372
  77.9 13.0 %collective-permute-start.26 = (f32[256,128]{1,0:T(8,128)S(1)}, f32[256,128]{1,0:T(8,128)S(1)}, u32[]{:S(2)}, u32[]{:S(2)}) collective-permute-start(f32[256,128]{1,0:T(8,128)S(1)} %get-tuple-element.84), channel_id=1, source_target_pairs={{0,2},{2,0},{4,6},{6,4},{1,3},{3,1},{5,7},{7,5},{8,10},{10,8},{12,... | collective-permute-start | bytes 393224 | tf_op jit(solution)/shard_map/ppermute | solution.py:372
  77.9 13.0 %collective-permute-start.27 = (f32[256,128]{1,0:T(8,128)S(1)}, f32[256,128]{1,0:T(8,128)S(1)}, u32[]{:S(2)}, u32[]{:S(2)}) collective-permute-start(f32[256,128]{1,0:T(8,128)S(1)} %get-tuple-element.85), channel_id=1, source_target_pairs={{0,6},{2,4},{4,2},{6,0},{1,7},{3,5},{5,3},{7,1},{8,14},{10,12},{12... | collective-permute-start | bytes 393224 | tf_op jit(solution)/shard_map/ppermute | solution.py:372

commit v25 on v24

--- a/solution.py
+++ b/solution.py
@@ -12,7 +12,7 @@
 
 GRAD_WEIGHT = 0.0625
 PLANE = ("half", "col", "core")
-EIGHT, BACK, FOUR = (2, 4, 3, 5, 6, 7, 1, 0), (1, 2, 4, 3, 5, 6, 7, 0), (2, 1, 3, 0)
+EIGHT, BACK, FOUR = (2, 4, 3, 5, 6, 7, 1, 0), (1, 4, 2, 5, 3, 6, 7, 0), (2, 1, 3, 0)
 VMEM_LIMIT = 24 * 1024 * 1024
 
 

time: 92.2 us -> 89.5 us (0.971)
  waiting for transfers between devices: 32.9 us -> 28.9 us
  starting transfers between devices: 32.1 us -> 34.5 us
  blocking collectives: 10 us -> 8.97 us
    ppermute x23, waiting for transfers between devices: 20.9 us -> 17.3 us  [deal(): lax.ppermute(value, axes, [(k, k ^ turn) for k in range(len(order))])]
    ppermute x23, starting transfers between devices: 21.9 us -> 24.2 us  [deal(): lax.ppermute(value, axes, [(k, k ^ turn) for k in range(len(order))])]
    all_gather x1, blocking collectives: 10 us -> 8.97 us  [local(): probe_grad = lax.all_gather(probe_band, PLANE, axis=0, tiled=True)]
where the time goes in v25:
time: 89.5 us; the launch traced here: 89.2 us
  starting transfers between devices  34.5 us (39%)
  waiting for transfers between devices  28.9 us (32%)
  Pallas kernels  12.9 us (14%)
  blocking collectives  8.97 us (10%)
  between operations  2.06 us (2%)
  local copies, waits for them, and re-layouts  1.79 us (2%)
    ppermute x23, starting transfers between devices, deal(): lax.ppermute(value, axes, [(k, k ^ turn) for k in range(len(order))])  24.2 us
    ppermute x23, waiting for transfers between devices, deal(): lax.ppermute(value, axes, [(k, k ^ turn) for k in range(len(order))])  17.3 us
    pallas_call x10, Pallas kernels, call(): pl.pallas_call(kernel, out_shape=[x for x, unused in outs], in_specs=[SME...  12.9 us
    all_gather x1, blocking collectives, local(): probe_grad = lax.all_gather(probe_band, PLANE, axis=0, tiled=True)  8.97 us
    ppermute x1, waiting for transfers between devices, local(): below = lax.ppermute(lowest, 'pair', [(k, k - 1) for k in range(1, pairs)])  7.61 us
    ppermute x1, starting transfers between devices, local(): lax.ppermute(lower_sums, 'pair', [(k, k + 1) for k in range(pairs - 1)])  3.5 us
    ppermute x1, waiting for transfers between devices, local(): lax.ppermute(lower_sums, 'pair', [(k, k + 1) for k in range(pairs - 1)])  3.17 us
    ppermute x1, starting transfers between devices, sum_over(): lax.ppermute(value, axis, [(k, k ^ step) for k in range(size)])  2.26 us
  transfers between devices with their start and end apart: 29, of which 13 were waited for; matrix products, arithmetic and copies ran while one was open for 2% of the time, Pallas kernels for 6%

profile of v25, /device:TPU:0, one launch (start us, length us, event | category | flops | bytes accessed | tf_op | source)
XLA Modules:
  0.0 89.2 jit_solution(12873939538528354438)
XLA Ops:
  0.6 1.3 %shard_map.95 = (f32[264,128]{1,0:T(8,128)S(1)}, f32[264,128]{1,0:T(8,128)S(1)}, f32[264,128]{1,0:T(8,128)S(1)}, f32[264,128]{1,0:T(8,128)S(1)}, f32[256,256]{1,0:T(8,128)S(1)}) custom-call(f32[4,256,128]{2,1,0:T(8,128)} %bitcast.9, f32[1,2,256,256]{3,2,1,0:T(8,128)} %measured.3, s32[1,2,2]{2,1,0:T(2,128)} %offsets_from.1), custom_call_target="tpu_custom_call" | custom-call | bytes 1851408 | tf_op jit(solution)/shard_map/pallas_call | solution.py:355
  1.9 3.0 %collective-permute-start = (f32[264,128]{1,0:T(8,128)S(1)}, f32[264,128]{1,0:T(8,128)S(1)}, u32[]{:S(2)}, u32[]{:S(2)}) collective-permute-start(f32[264,128]{1,0:T(8,128)S(1)} %get-tuple-element.47), channel_id=1, source_target_pairs={{0,2},{2,0},{4,6},{6,4},{1,3},{3,1},{5,7},{7,5},{8,10},{10,8},{12,... | collective-permute-start | bytes 405512 | tf_op jit(solution)/shard_map/ppermute | solution.py:372
  4.9 1.5 %collective-permute-start.1 = (f32[264,128]{1,0:T(8,128)S(1)}, f32[264,128]{1,0:T(8,128)S(1)}, u32[]{:S(2)}, u32[]{:S(2)}) collective-permute-start(f32[264,128]{1,0:T(8,128)S(1)} %get-tuple-element.48), channel_id=1, source_target_pairs={{0,4},{2,6},{4,0},{6,2},{1,5},{3,7},{5,1},{7,3},{8,12},{10,14},{12... | collective-permute-start | bytes 405512 | tf_op jit(solution)/shard_map/ppermute | solution.py:372
  6.6 1.3 %fusion = (s32[1,1]{1,0:T(1,128)}, s32[1,1]{1,0:T(1,128)}) fusion(s32[1,2]{1,0:T(1,128)} %param.11), kind=kLoop, calls=%fused_computation.8 | loop fusion | bytes 16 | tf_op jit(solution)/shard_map/slice | solution.py:412
  9.2 0.1 slice_reduce_fusion.2
  9.3 3.5 %collective-permute-done.1.refs_0_ = f32[264,128]{1,0:T(8,128)S(1)} collective-permute-done((f32[264,128]{1,0:T(8,128)S(1)}, f32[264,128]{1,0:T(8,128)S(1)}, u32[]{:S(2)}, u32[]{:S(2)}) %collective-permute-start.1) | collective-permute-done | bytes 135200 | tf_op jit(solution)/shard_map/ppermute | solution.py:372
  13.0 0.1 slice_reduce_fusion
  13.2 1.3 %collective-permute-start.4 = (f32[2,256,128]{2,1,0:T(8,128)S(1)}, f32[2,256,128]{2,1,0:T(8,128)S(1)}, u32[]{:S(2)}, u32[]{:S(2)}) collective-permute-start(f32[2,256,128]{2,1,0:T(8,128)S(1)} %shard_map.96), channel_id=1, source_target_pairs={{8,0},{16,8},{24,16},{9,1},{17,9},{25,17},{10,2},{18,10},{26,18},{... | collective-permute-start | bytes 786440 | tf_op jit(solution)/shard_map/ppermute | solution.py:405
  14.5 1.6 %collective-permute-start.12 = (f32[256,256]{1,0:T(8,128)S(1)}, f32[256,256]{1,0:T(8,128)S(1)}, u32[]{:S(2)}, u32[]{:S(2)}) collective-permute-start(f32[256,256]{1,0:T(8,128)S(1)} %get-tuple-element.60), channel_id=1, source_target_pairs={{0,4},{4,0},{1,5},{5,1},{2,6},{6,2},{3,7},{7,3},{8,12},{12,8},{9,1... | collective-permute-start | bytes 786440 | tf_op jit(solution)/shard_map/ppermute | solution.py:406
  16.2 7.6 %collective-permute-done.4.refs_4_ = f32[2,256,128]{2,1,0:T(8,128)S(1)} collective-permute-done((f32[2,256,128]{2,1,0:T(8,128)S(1)}, f32[2,256,128]{2,1,0:T(8,128)S(1)}, u32[]{:S(2)}, u32[]{:S(2)}) %collective-permute-start.4) | collective-permute-done | bytes 262176 | tf_op jit(solution)/shard_map/ppermute | solution.py:405
  23.8 1.3 %shard_map.97 = (f32[256,128]{1,0:T(8,128)S(1)}, f32[256,128]{1,0:T(8,128)S(1)}, f32[256,128]{1,0:T(8,128)S(1)}, f32[256,128]{1,0:T(8,128)S(1)}, f32[256,128]{1,...) custom-call(s32[5,8]{1,0:T(8,128)S(1)} %concatenate.7.offs, ...), custom_call_target="tpu_custom_call" | custom-call | flops 2097152 | bytes 1851392 | tf_op jit(solution)/shard_map/pallas_call | solution.py:355
  25.1 1.2 %collective-permute-start.5 = (f32[256,128]{1,0:T(8,128)S(1)}, f32[256,128]{1,0:T(8,128)S(1)}, u32[]{:S(2)}, u32[]{:S(2)}) collective-permute-start(f32[256,128]{1,0:T(8,128)S(1)} %get-tuple-element.52), channel_id=1, source_target_pairs={{0,2},{1,3},{2,0},{3,1},{4,6},{5,7},{6,4},{7,5},{8,10},{9,11},{10,... | collective-permute-start | bytes 393224 | tf_op jit(solution)/shard_map/ppermute | solution.py:372
  26.3 0.9 %collective-permute-start.6 = (f32[256,128]{1,0:T(8,128)S(1)}, f32[256,128]{1,0:T(8,128)S(1)}, u32[]{:S(2)}, u32[]{:S(2)}) collective-permute-start(f32[256,128]{1,0:T(8,128)S(1)} %get-tuple-element.53), channel_id=1, source_target_pairs={{0,4},{1,5},{2,6},{3,7},{4,0},{5,1},{6,2},{7,3},{8,12},{9,13},{10,... | collective-permute-start | bytes 393224 | tf_op jit(solution)/shard_map/ppermute | solution.py:372
  27.2 0.2 collective-permute-start.7
  27.5 1.5 %collective-permute-start.8 = (f32[256,128]{1,0:T(8,128)S(1)}, f32[256,128]{1,0:T(8,128)S(1)}, u32[]{:S(2)}, u32[]{:S(2)}) collective-permute-start(f32[256,128]{1,0:T(8,128)S(1)} %get-tuple-element.55), channel_id=1, source_target_pairs={{0,5},{1,4},{2,7},{3,6},{4,1},{5,0},{6,3},{7,2},{8,13},{9,12},{10,... | collective-permute-start | bytes 393224 | tf_op jit(solution)/shard_map/ppermute | solution.py:372
  29.0 1.5 %collective-permute-start.9 = (f32[256,128]{1,0:T(8,128)S(1)}, f32[256,128]{1,0:T(8,128)S(1)}, u32[]{:S(2)}, u32[]{:S(2)}) collective-permute-start(f32[256,128]{1,0:T(8,128)S(1)} %get-tuple-element.56), channel_id=1, source_target_pairs={{0,6},{1,7},{2,4},{3,5},{4,2},{5,3},{6,0},{7,1},{8,14},{9,15},{10,... | collective-permute-start | bytes 393224 | tf_op jit(solution)/shard_map/ppermute | solution.py:372
  30.5 0.7 collective-permute-start.10
  31.1 1.0 %collective-permute-done.6.refs_1_ = f32[256,128]{1,0:T(8,128)S(1)} collective-permute-done((f32[256,128]{1,0:T(8,128)S(1)}, f32[256,128]{1,0:T(8,128)S(1)}, u32[]{:S(2)}, u32[]{:S(2)}) %collective-permute-start.6) | collective-permute-done | bytes 131104 | tf_op jit(solution)/shard_map/ppermute | solution.py:372
  32.1 2.5 %shard_map.98 = (f32[2,256,256]{2,1,0:T(8,128)S(1)}, f32[256,256]{1,0:T(8,128)S(1)}, bf16[6,512,256]{2,1,0:T(8,128)(2,1)S(1)}) custom-call(s32[5,8]{1,0:T(8,128)S(1)} %concatenate.7.offs, f32[256,256]{1,0:T(8,128)S(1)} %collective-permute-done.12.taken, f32[2,256,256]{2,1,0:T(8,128)} %probe_from.1, f32[1,2,256,256]{3,2,1,0:T(8,128)} %measured.3, ...), custom_call_target="tpu_custom_call" | custom-call | flops 201326592 | bytes 5505024 | tf_op jit(solution)/shard_map/pallas_call | solution.py:355
  34.6 3.5 %collective-permute-done.8.refs_3_ = f32[256,128]{1,0:T(8,128)S(1)} collective-permute-done((f32[256,128]{1,0:T(8,128)S(1)}, f32[256,128]{1,0:T(8,128)S(1)}, u32[]{:S(2)}, u32[]{:S(2)}) %collective-permute-start.8) | collective-permute-done | bytes 131104 | tf_op jit(solution)/shard_map/ppermute | solution.py:372
  38.2 1.0 %collective-permute-done.10.refs_5_ = f32[256,128]{1,0:T(8,128)S(1)} collective-permute-done((f32[256,128]{1,0:T(8,128)S(1)}, f32[256,128]{1,0:T(8,128)S(1)}, u32[]{:S(2)}, u32[]{:S(2)}) %collective-permute-start.10) | collective-permute-done | bytes 131104 | tf_op jit(solution)/shard_map/ppermute | solution.py:372
  39.2 4.2 %shard_map.99 = (f32[768,128]{1,0:T(8,128)S(1)}, f32[256,128]{1,0:T(8,128)S(1)}, f32[256,128]{1,0:T(8,128)S(1)}, f32[256,128]{1,0:T(8,128)S(1)}, f32[256,128]{1,...) custom-call(s32[5,8]{1,0:T(8,128)S(1)} %concatenate.7.offs, ...), custom_call_target="tpu_custom_call" | custom-call | flops 1610612736 | bytes 5120000 | tf_op jit(solution)/shard_map/pallas_call | solution.py:355
  43.4 0.4 collective-permute-start.13
  43.8 1.0 %collective-permute-start.14 = (f32[256,128]{1,0:T(8,128)S(1)}, f32[256,128]{1,0:T(8,128)S(1)}, u32[]{:S(2)}, u32[]{:S(2)}) collective-permute-start(f32[256,128]{1,0:T(8,128)S(1)} %get-tuple-element.65), channel_id=1, source_target_pairs={{0,4},{1,5},{2,6},{3,7},{4,0},{5,1},{6,2},{7,3},{8,12},{9,13},{10,... | collective-permute-start | bytes 393224 | tf_op jit(solution)/shard_map/ppermute | solution.py:372
  44.8 1.4 %collective-permute-start.15 = (f32[256,128]{1,0:T(8,128)S(1)}, f32[256,128]{1,0:T(8,128)S(1)}, u32[]{:S(2)}, u32[]{:S(2)}) collective-permute-start(f32[256,128]{1,0:T(8,128)S(1)} %get-tuple-element.66), channel_id=1, source_target_pairs={{0,2},{1,3},{2,0},{3,1},{4,6},{5,7},{6,4},{7,5},{8,10},{9,11},{10,... | collective-permute-start | bytes 393224 | tf_op jit(solution)/shard_map/ppermute | solution.py:372
  46.2 1.3 %collective-permute-start.17 = (f32[256,128]{1,0:T(8,128)S(1)}, f32[256,128]{1,0:T(8,128)S(1)}, u32[]{:S(2)}, u32[]{:S(2)}) collective-permute-start(f32[256,128]{1,0:T(8,128)S(1)} %get-tuple-element.68), channel_id=1, source_target_pairs={{0,3},{1,2},{2,1},{3,0},{4,7},{5,6},{6,5},{7,4},{8,11},{9,10},{10,... | collective-permute-start | bytes 393224 | tf_op jit(solution)/shard_map/ppermute | solution.py:372
  47.6 2.0 %collective-permute-done.14.refs_1_ = f32[256,128]{1,0:T(8,128)S(1)} collective-permute-done((f32[256,128]{1,0:T(8,128)S(1)}, f32[256,128]{1,0:T(8,128)S(1)}, u32[]{:S(2)}, u32[]{:S(2)}) %collective-permute-start.14) | collective-permute-done | bytes 131104 | tf_op jit(solution)/shard_map/ppermute | solution.py:372
  49.5 2.5 %collective-permute-start.18 = (f32[256,128]{1,0:T(8,128)S(1)}, f32[256,128]{1,0:T(8,128)S(1)}, u32[]{:S(2)}, u32[]{:S(2)}) collective-permute-start(f32[256,128]{1,0:T(8,128)S(1)} %get-tuple-element.69), channel_id=1, source_target_pairs={{0,6},{1,7},{2,4},{3,5},{4,2},{5,3},{6,0},{7,1},{8,14},{9,15},{10,... | collective-permute-start | bytes 393224 | tf_op jit(solution)/shard_map/ppermute | solution.py:372
  52.0 0.6 collective-permute-start.20
  52.6 0.7 collective-permute-start.21
  53.3 2.3 %collective-permute-start.22 = (f32[128,128]{1,0:T(8,128)S(1)}, f32[128,128]{1,0:T(8,128)S(1)}, u32[]{:S(2)}, u32[]{:S(2)}) collective-permute-start(f32[128,128]{1,0:T(8,128)S(1)} %get-tuple-element.75), channel_id=1, source_target_pairs={{0,6},{2,4},{4,2},{6,0},{1,7},{3,5},{5,3},{7,1},{8,14},{10,12},{12... | collective-permute-start | bytes 196616 | tf_op jit(solution)/shard_map/ppermute | solution.py:372
  55.6 1.0 %collective-permute-done.18.refs_5_ = f32[256,128]{1,0:T(8,128)S(1)} collective-permute-done((f32[256,128]{1,0:T(8,128)S(1)}, f32[256,128]{1,0:T(8,128)S(1)}, u32[]{:S(2)}, u32[]{:S(2)}) %collective-permute-start.18) | collective-permute-done | bytes 131104 | tf_op jit(solution)/shard_map/ppermute | solution.py:372
  56.6 2.3 %collective-permute-done.19.refs_6_ = f32[256,128]{1,0:T(8,128)S(1)} collective-permute-done((f32[256,128]{1,0:T(8,128)S(1)}, f32[256,128]{1,0:T(8,128)S(1)}, u32[]{:S(2)}, u32[]{:S(2)}) %collective-permute-start.19) | collective-permute-done | bytes 131104 | tf_op jit(solution)/shard_map/ppermute | solution.py:372
  58.8 1.8 %collective-permute-done.20.refs_8_ = f32[128,128]{1,0:T(8,128)S(1)} collective-permute-done((f32[128,128]{1,0:T(8,128)S(1)}, f32[128,128]{1,0:T(8,128)S(1)}, u32[]{:S(2)}, u32[]{:S(2)}) %collective-permute-start.20) | collective-permute-done | bytes 65568 | tf_op jit(solution)/shard_map/ppermute | solution.py:372
  60.6 1.2 %collective-permute-done.22.refs_10_ = f32[128,128]{1,0:T(8,128)S(1)} collective-permute-done((f32[128,128]{1,0:T(8,128)S(1)}, f32[128,128]{1,0:T(8,128)S(1)}, u32[]{:S(2)}, u32[]{:S(2)}) %collective-permute-start.22) | collective-permute-done | bytes 65568 | tf_op jit(solution)/shard_map/ppermute | solution.py:372
  61.9 1.0 %shard_map.102 = (f32[2,256,128]{2,1,0:T(8,128)S(1)}, f32[64,256]{1,0:T(8,128)S(1)}) custom-call(s32[5,8]{1,0:T(8,128)S(1)} %concatenate.7.offs, f32[768,128]{1,0:T(8,128)S(1)} %collective-permute-done.13.refs_0_.got, f32[256,128]{1,0:T(8,128)S(1)} %collective-permute-done.14.refs_1_, f32[256,128]{1,0:T(8,128)S(1)} %collective-permute-done.15.refs_2_, ...), custom_call_target="tpu_custom_call" | custom-call | flops 2097152 | bytes 1900544 | tf_op jit(solution)/shard_map/pallas_call | solution.py:355
  62.9 3.5 %collective-permute-start.23 = (f32[2,256,128]{2,1,0:T(8,128)S(1)}, f32[2,256,128]{2,1,0:T(8,128)S(1)}, u32[]{:S(2)}, u32[]{:S(2)}) collective-permute-start(f32[2,256,128]{2,1,0:T(8,128)S(1)} %get-tuple-element.77), channel_id=1, source_target_pairs={{0,8},{8,16},{16,24},{1,9},{9,17},{17,25},{2,10},{10,18},{18,26},{... | collective-permute-start | bytes 786440 | tf_op jit(solution)/shard_map/ppermute | solution.py:450
  66.4 1.6 %collective-permute-start.24 = (f32[64,256]{1,0:T(8,128)S(1)}, f32[64,256]{1,0:T(8,128)S(1)}, u32[]{:S(2)}, u32[]{:S(2)}) collective-permute-start(f32[64,256]{1,0:T(8,128)S(1)} %get-tuple-element.82), channel_id=1, source_target_pairs={{0,8},{8,0},{16,24},{24,16},{1,9},{9,1},{17,25},{25,17},{2,10},{10... | collective-permute-start | bytes 196616 | tf_op jit(solution)/shard_map/ppermute | solution.py:453
  68.0 1.5 %shard_map.100.own = f32[4,256,128]{2,1,0:T(8,128)S(1)} custom-call(s32[5,8]{1,0:T(8,128)S(1)} %concatenate.7.offs, f32[768,128]{1,0:T(8,128)S(1)} %collective-permute-done.13.refs_0_.got, f32[256,128]{1,0:T(8,128)S(1)} %collective-permute-done.14.refs_1_, f32[256,128]{1,0:T(8,128)S(1)} %collective-permute-done.15.refs_2_, ...), custom_call_target="tpu_custom_call" | custom-call | flops 4194304 | bytes 1835008 | tf_op jit(solution)/shard_map/pallas_call | solution.py:355
  69.5 3.2 %collective-permute-done.23.above = f32[2,256,128]{2,1,0:T(8,128)S(1)} collective-permute-done((f32[2,256,128]{2,1,0:T(8,128)S(1)}, f32[2,256,128]{2,1,0:T(8,128)S(1)}, u32[]{:S(2)}, u32[]{:S(2)}) %collective-permute-start.23) | collective-permute-done | bytes 262176 | tf_op jit(solution)/shard_map/ppermute | solution.py:450
  72.7 0.6 collective-permute-done.24
  73.4 2.3 %collective-permute-start.28 = (f32[64,256]{1,0:T(8,128)S(1)}, f32[64,256]{1,0:T(8,128)S(1)}, u32[]{:S(2)}, u32[]{:S(2)}) collective-permute-start(f32[64,256]{1,0:T(8,128)S(1)} %add.8), channel_id=1, source_target_pairs={{0,16},{8,24},{16,0},{24,8},{1,17},{9,25},{17,1},{25,9},{2,18},{10... | collective-permute-start | bytes 196616 | tf_op jit(solution)/shard_map/ppermute | solution.py:380
  75.6 0.4 collective-permute-start.25
  76.0 1.3 %collective-permute-start.26 = (f32[256,128]{1,0:T(8,128)S(1)}, f32[256,128]{1,0:T(8,128)S(1)}, u32[]{:S(2)}, u32[]{:S(2)}) collective-permute-start(f32[256,128]{1,0:T(8,128)S(1)} %get-tuple-element.84), channel_id=1, source_target_pairs={{0,2},{2,0},{4,6},{6,4},{1,3},{3,1},{5,7},{7,5},{8,10},{10,8},{12,... | collective-permute-start | bytes 393224 | tf_op jit(solution)/shard_map/ppermute | solution.py:372
  77.3 1.8 %collective-permute-start.27 = (f32[256,128]{1,0:T(8,128)S(1)}, f32[256,128]{1,0:T(8,128)S(1)}, u32[]{:S(2)}, u32[]{:S(2)}) collective-permute-start(f32[256,128]{1,0:T(8,128)S(1)} %get-tuple-element.85), channel_id=1, source_target_pairs={{0,6},{2,4},{4,2},{6,0},{1,7},{3,5},{5,3},{7,1},{8,14},{10,12},{12... | collective-permute-start | bytes 393224 | tf_op jit(solution)/shard_map/ppermute | solution.py:372
  79.1 0.1 collective-permute-done.28
  79.3 9.0 %all_gather.3.refs_4_ = f32[512,256]{1,0:T(8,128)S(1)} all-gather(f32[64,256]{1,0:T(8,128)S(1)} %add.9), channel_id=1, replica_groups=mesh['pair'=4,'half'=2,'col'=2,'core'=2] {'half','col','core'}, dimensions={0}, use_global_device_ids=true | all-gather | bytes 589824 | tf_op jit(solution)/shard_map/all_gather | solution.py:462
  88.2 1.0 %shard_map.104 = (f32[4,256,128]{2,1,0:T(8,128)}, f32[512,256]{1,0:T(8,128)}) custom-call(f32[256,128]{1,0:T(8,128)S(1)} %collective-permute-done.25.refs_0_, f32[256,128]{1,0:T(8,128)S(1)} %collective-permute-done.26.refs_1_, f32[256,128]{1,0:T(8,128)S(1)} %collective-permute-done.27.refs_2_, f32[256,128]{1,0:T(8,128)S(1)} %get-tuple-element.86.refs_3_, ...), custom_call_target="tpu_custom_call" | custom-call | bytes 2097152 | tf_op jit(solution)/shard_map/pallas_call | solution.py:355
  (34 shorter events, 0.6 us)
Async XLA Ops:
  1.9 7.3 %collective-permute-start = (f32[264,128]{1,0:T(8,128)S(1)}, f32[264,128]{1,0:T(8,128)S(1)}, u32[]{:S(2)}, u32[]{:S(2)}) collective-permute-start(f32[264,128]{1,0:T(8,128)S(1)} %get-tuple-element.47), channel_id=1, source_target_pairs={{0,2},{2,0},{4,6},{6,4},{1,3},{3,1},{5,7},{7,5},{8,10},{10,8},{12,... | collective-permute-start | bytes 405512 | tf_op jit(solution)/shard_map/ppermute | solution.py:372
  4.9 7.9 %collective-permute-start.1 = (f32[264,128]{1,0:T(8,128)S(1)}, f32[264,128]{1,0:T(8,128)S(1)}, u32[]{:S(2)}, u32[]{:S(2)}) collective-permute-start(f32[264,128]{1,0:T(8,128)S(1)} %get-tuple-element.48), channel_id=1, source_target_pairs={{0,4},{2,6},{4,0},{6,2},{1,5},{3,7},{5,1},{7,3},{8,12},{10,14},{12... | collective-permute-start | bytes 405512 | tf_op jit(solution)/shard_map/ppermute | solution.py:372
  6.4 6.5 %collective-permute-start.2 = (f32[264,128]{1,0:T(8,128)S(1)}, f32[264,128]{1,0:T(8,128)S(1)}, u32[]{:S(2)}, u32[]{:S(2)}) collective-permute-start(f32[264,128]{1,0:T(8,128)S(1)} %get-tuple-element.49), channel_id=1, source_target_pairs={{0,6},{2,4},{4,2},{6,0},{1,7},{3,5},{5,3},{7,1},{8,14},{10,12},{12... | collective-permute-start | bytes 405512 | tf_op jit(solution)/shard_map/ppermute | solution.py:372
  13.1 3.0 %collective-permute-start.3 = (s32[4,4]{1,0:T(4,128)S(1)}, s32[4,4]{1,0:T(4,128)S(1)}, u32[]{:S(2)}, u32[]{:S(2)}) collective-permute-start(s32[4,4]{1,0:T(4,128)S(1)} %maximum_convert_fusion), channel_id=1, source_target_pairs={{0,1},{1,0},{2,3},{3,2},{4,5},{5,4},{6,7},{7,6},{8,9},{9,8},{10,11... | collective-permute-start | bytes 200 | tf_op jit(solution)/shard_map/ppermute | solution.py:410
  13.2 10.6 %collective-permute-start.4 = (f32[2,256,128]{2,1,0:T(8,128)S(1)}, f32[2,256,128]{2,1,0:T(8,128)S(1)}, u32[]{:S(2)}, u32[]{:S(2)}) collective-permute-start(f32[2,256,128]{2,1,0:T(8,128)S(1)} %shard_map.96), channel_id=1, source_target_pairs={{8,0},{16,8},{24,16},{9,1},{17,9},{25,17},{10,2},{18,10},{26,18},{... | collective-permute-start | bytes 786440 | tf_op jit(solution)/shard_map/ppermute | solution.py:405
  14.5 14.4 %collective-permute-start.12 = (f32[256,256]{1,0:T(8,128)S(1)}, f32[256,256]{1,0:T(8,128)S(1)}, u32[]{:S(2)}, u32[]{:S(2)}) collective-permute-start(f32[256,256]{1,0:T(8,128)S(1)} %get-tuple-element.60), channel_id=1, source_target_pairs={{0,4},{4,0},{1,5},{5,1},{2,6},{6,2},{3,7},{7,3},{8,12},{12,8},{9,1... | collective-permute-start | bytes 786440 | tf_op jit(solution)/shard_map/ppermute | solution.py:406
  25.1 5.3 %collective-permute-start.5 = (f32[256,128]{1,0:T(8,128)S(1)}, f32[256,128]{1,0:T(8,128)S(1)}, u32[]{:S(2)}, u32[]{:S(2)}) collective-permute-start(f32[256,128]{1,0:T(8,128)S(1)} %get-tuple-element.52), channel_id=1, source_target_pairs={{0,2},{1,3},{2,0},{3,1},{4,6},{5,7},{6,4},{7,5},{8,10},{9,11},{10,... | collective-permute-start | bytes 393224 | tf_op jit(solution)/shard_map/ppermute | solution.py:372
  26.3 5.8 %collective-permute-start.6 = (f32[256,128]{1,0:T(8,128)S(1)}, f32[256,128]{1,0:T(8,128)S(1)}, u32[]{:S(2)}, u32[]{:S(2)}) collective-permute-start(f32[256,128]{1,0:T(8,128)S(1)} %get-tuple-element.53), channel_id=1, source_target_pairs={{0,4},{1,5},{2,6},{3,7},{4,0},{5,1},{6,2},{7,3},{8,12},{9,13},{10,... | collective-permute-start | bytes 393224 | tf_op jit(solution)/shard_map/ppermute | solution.py:372
  27.2 7.4 %collective-permute-start.7 = (f32[256,128]{1,0:T(8,128)S(1)}, f32[256,128]{1,0:T(8,128)S(1)}, u32[]{:S(2)}, u32[]{:S(2)}) collective-permute-start(f32[256,128]{1,0:T(8,128)S(1)} %get-tuple-element.54), channel_id=1, source_target_pairs={{0,3},{1,2},{2,1},{3,0},{4,7},{5,6},{6,5},{7,4},{8,11},{9,10},{10,... | collective-permute-start | bytes 393224 | tf_op jit(solution)/shard_map/ppermute | solution.py:372
  27.5 10.7 %collective-permute-start.8 = (f32[256,128]{1,0:T(8,128)S(1)}, f32[256,128]{1,0:T(8,128)S(1)}, u32[]{:S(2)}, u32[]{:S(2)}) collective-permute-start(f32[256,128]{1,0:T(8,128)S(1)} %get-tuple-element.55), channel_id=1, source_target_pairs={{0,5},{1,4},{2,7},{3,6},{4,1},{5,0},{6,3},{7,2},{8,13},{9,12},{10,... | collective-permute-start | bytes 393224 | tf_op jit(solution)/shard_map/ppermute | solution.py:372
  29.0 9.2 %collective-permute-start.9 = (f32[256,128]{1,0:T(8,128)S(1)}, f32[256,128]{1,0:T(8,128)S(1)}, u32[]{:S(2)}, u32[]{:S(2)}) collective-permute-start(f32[256,128]{1,0:T(8,128)S(1)} %get-tuple-element.56), channel_id=1, source_target_pairs={{0,6},{1,7},{2,4},{3,5},{4,2},{5,3},{6,0},{7,1},{8,14},{9,15},{10,... | collective-permute-start | bytes 393224 | tf_op jit(solution)/shard_map/ppermute | solution.py:372
  30.5 8.7 %collective-permute-start.10 = (f32[256,128]{1,0:T(8,128)S(1)}, f32[256,128]{1,0:T(8,128)S(1)}, u32[]{:S(2)}, u32[]{:S(2)}) collective-permute-start(f32[256,128]{1,0:T(8,128)S(1)} %get-tuple-element.57), channel_id=1, source_target_pairs={{0,7},{1,6},{2,5},{3,4},{4,3},{5,2},{6,1},{7,0},{8,15},{9,14},{10,... | collective-permute-start | bytes 393224 | tf_op jit(solution)/shard_map/ppermute | solution.py:372
  32.1 7.1 %copy-start = (f32[2,136,128]{2,1,0:T(8,128)S(1)}, f32[2,136,128]{2,1,0:T(8,128)}, u32[]{:S(2)}) copy-start(f32[2,136,128]{2,1,0:T(8,128)} %constant.17.clone.refs_11_) | copy-start | bytes 417796
  32.1 7.1 %collective-permute-start.11 = (f32[256,128]{1,0:T(8,128)S(1)}, f32[256,128]{1,0:T(8,128)S(1)}, u32[]{:S(2)}, u32[]{:S(2)}) collective-permute-start(f32[256,128]{1,0:T(8,128)S(1)} %get-tuple-element.58), channel_id=1, source_target_pairs={{0,1},{1,0},{2,3},{3,2},{4,5},{5,4},{6,7},{7,6},{8,9},{9,8},{10,11... | collective-permute-start | bytes 393224 | tf_op jit(solution)/shard_map/ppermute | solution.py:372
  43.4 8.6 %collective-permute-start.13 = (f32[768,128]{1,0:T(8,128)S(1)}, f32[768,128]{1,0:T(8,128)S(1)}, u32[]{:S(2)}, u32[]{:S(2)}) collective-permute-start(f32[768,128]{1,0:T(8,128)S(1)} %get-tuple-element.64), channel_id=1, source_target_pairs={{0,1},{1,0},{2,3},{3,2},{4,5},{5,4},{6,7},{7,6},{8,9},{9,8},{10,11... | collective-permute-start | bytes 1179656 | tf_op jit(solution)/shard_map/ppermute | solution.py:372
  43.8 5.7 %collective-permute-start.14 = (f32[256,128]{1,0:T(8,128)S(1)}, f32[256,128]{1,0:T(8,128)S(1)}, u32[]{:S(2)}, u32[]{:S(2)}) collective-permute-start(f32[256,128]{1,0:T(8,128)S(1)} %get-tuple-element.65), channel_id=1, source_target_pairs={{0,4},{1,5},{2,6},{3,7},{4,0},{5,1},{6,2},{7,3},{8,12},{9,13},{10,... | collective-permute-start | bytes 393224 | tf_op jit(solution)/shard_map/ppermute | solution.py:372
  44.8 7.3 %collective-permute-start.15 = (f32[256,128]{1,0:T(8,128)S(1)}, f32[256,128]{1,0:T(8,128)S(1)}, u32[]{:S(2)}, u32[]{:S(2)}) collective-permute-start(f32[256,128]{1,0:T(8,128)S(1)} %get-tuple-element.66), channel_id=1, source_target_pairs={{0,2},{1,3},{2,0},{3,1},{4,6},{5,7},{6,4},{7,5},{8,10},{9,11},{10,... | collective-permute-start | bytes 393224 | tf_op jit(solution)/shard_map/ppermute | solution.py:372
  46.2 6.4 %collective-permute-start.16 = (f32[256,128]{1,0:T(8,128)S(1)}, f32[256,128]{1,0:T(8,128)S(1)}, u32[]{:S(2)}, u32[]{:S(2)}) collective-permute-start(f32[256,128]{1,0:T(8,128)S(1)} %get-tuple-element.67), channel_id=1, source_target_pairs={{0,5},{1,4},{2,7},{3,6},{4,1},{5,0},{6,3},{7,2},{8,13},{9,12},{10,... | collective-permute-start | bytes 393224 | tf_op jit(solution)/shard_map/ppermute | solution.py:372
  46.2 7.1 %collective-permute-start.17 = (f32[256,128]{1,0:T(8,128)S(1)}, f32[256,128]{1,0:T(8,128)S(1)}, u32[]{:S(2)}, u32[]{:S(2)}) collective-permute-start(f32[256,128]{1,0:T(8,128)S(1)} %get-tuple-element.68), channel_id=1, source_target_pairs={{0,3},{1,2},{2,1},{3,0},{4,7},{5,6},{6,5},{7,4},{8,11},{9,10},{10,... | collective-permute-start | bytes 393224 | tf_op jit(solution)/shard_map/ppermute | solution.py:372
  49.5 7.0 %collective-permute-start.18 = (f32[256,128]{1,0:T(8,128)S(1)}, f32[256,128]{1,0:T(8,128)S(1)}, u32[]{:S(2)}, u32[]{:S(2)}) collective-permute-start(f32[256,128]{1,0:T(8,128)S(1)} %get-tuple-element.69), channel_id=1, source_target_pairs={{0,6},{1,7},{2,4},{3,5},{4,2},{5,3},{6,0},{7,1},{8,14},{9,15},{10,... | collective-permute-start | bytes 393224 | tf_op jit(solution)/shard_map/ppermute | solution.py:372
  52.0 6.9 %collective-permute-start.19 = (f32[256,128]{1,0:T(8,128)S(1)}, f32[256,128]{1,0:T(8,128)S(1)}, u32[]{:S(2)}, u32[]{:S(2)}) collective-permute-start(f32[256,128]{1,0:T(8,128)S(1)} %get-tuple-element.70), channel_id=1, source_target_pairs={{0,7},{1,6},{2,5},{3,4},{4,3},{5,2},{6,1},{7,0},{8,15},{9,14},{10,... | collective-permute-start | bytes 393224 | tf_op jit(solution)/shard_map/ppermute | solution.py:372
  52.0 8.6 %collective-permute-start.20 = (f32[128,128]{1,0:T(8,128)S(1)}, f32[128,128]{1,0:T(8,128)S(1)}, u32[]{:S(2)}, u32[]{:S(2)}) collective-permute-start(f32[128,128]{1,0:T(8,128)S(1)} %get-tuple-element.73), channel_id=1, source_target_pairs={{0,4},{2,6},{4,0},{6,2},{1,5},{3,7},{5,1},{7,3},{8,12},{10,14},{12... | collective-permute-start | bytes 196616 | tf_op jit(solution)/shard_map/ppermute | solution.py:372
  52.6 8.0 %collective-permute-start.21 = (f32[128,128]{1,0:T(8,128)S(1)}, f32[128,128]{1,0:T(8,128)S(1)}, u32[]{:S(2)}, u32[]{:S(2)}) collective-permute-start(f32[128,128]{1,0:T(8,128)S(1)} %get-tuple-element.74), channel_id=1, source_target_pairs={{0,2},{2,0},{4,6},{6,4},{1,3},{3,1},{5,7},{7,5},{8,10},{10,8},{12,... | collective-permute-start | bytes 196616 | tf_op jit(solution)/shard_map/ppermute | solution.py:372
  53.3 8.6 %collective-permute-start.22 = (f32[128,128]{1,0:T(8,128)S(1)}, f32[128,128]{1,0:T(8,128)S(1)}, u32[]{:S(2)}, u32[]{:S(2)}) collective-permute-start(f32[128,128]{1,0:T(8,128)S(1)} %get-tuple-element.75), channel_id=1, source_target_pairs={{0,6},{2,4},{4,2},{6,0},{1,7},{3,5},{5,3},{7,1},{8,14},{10,12},{12... | collective-permute-start | bytes 196616 | tf_op jit(solution)/shard_map/ppermute | solution.py:372
  62.9 9.8 %collective-permute-start.23 = (f32[2,256,128]{2,1,0:T(8,128)S(1)}, f32[2,256,128]{2,1,0:T(8,128)S(1)}, u32[]{:S(2)}, u32[]{:S(2)}) collective-permute-start(f32[2,256,128]{2,1,0:T(8,128)S(1)} %get-tuple-element.77), channel_id=1, source_target_pairs={{0,8},{8,16},{16,24},{1,9},{9,17},{17,25},{2,10},{10,18},{18,26},{... | collective-permute-start | bytes 786440 | tf_op jit(solution)/shard_map/ppermute | solution.py:450
  66.4 7.0 %collective-permute-start.24 = (f32[64,256]{1,0:T(8,128)S(1)}, f32[64,256]{1,0:T(8,128)S(1)}, u32[]{:S(2)}, u32[]{:S(2)}) collective-permute-start(f32[64,256]{1,0:T(8,128)S(1)} %get-tuple-element.82), channel_id=1, source_target_pairs={{0,8},{8,0},{16,24},{24,16},{1,9},{9,1},{17,25},{25,17},{2,10},{10... | collective-permute-start | bytes 196616 | tf_op jit(solution)/shard_map/ppermute | solution.py:453
  73.4 5.9 %collective-permute-start.28 = (f32[64,256]{1,0:T(8,128)S(1)}, f32[64,256]{1,0:T(8,128)S(1)}, u32[]{:S(2)}, u32[]{:S(2)}) collective-permute-start(f32[64,256]{1,0:T(8,128)S(1)} %add.8), channel_id=1, source_target_pairs={{0,16},{8,24},{16,0},{24,8},{1,17},{9,25},{17,1},{25,9},{2,18},{10... | collective-permute-start | bytes 196616 | tf_op jit(solution)/shard_map/ppermute | solution.py:380
  75.6 12.6 %collective-permute-start.25 = (f32[256,128]{1,0:T(8,128)S(1)}, f32[256,128]{1,0:T(8,128)S(1)}, u32[]{:S(2)}, u32[]{:S(2)}) collective-permute-start(f32[256,128]{1,0:T(8,128)S(1)} %get-tuple-element.83), channel_id=1, source_target_pairs={{0,4},{2,6},{4,0},{6,2},{1,5},{3,7},{5,1},{7,3},{8,12},{10,14},{12... | collective-permute-start | bytes 393224 | tf_op jit(solution)/shard_map/ppermute | solution.py:372
  76.0 12.2 %collective-permute-start.26 = (f32[256,128]{1,0:T(8,128)S(1)}, f32[256,128]{1,0:T(8,128)S(1)}, u32[]{:S(2)}, u32[]{:S(2)}) collective-permute-start(f32[256,128]{1,0:T(8,128)S(1)} %get-tuple-element.84), channel_id=1, source_target_pairs={{0,2},{2,0},{4,6},{6,4},{1,3},{3,1},{5,7},{7,5},{8,10},{10,8},{12,... | collective-permute-start | bytes 393224 | tf_op jit(solution)/shard_map/ppermute | solution.py:372
  77.3 10.9 %collective-permute-start.27 = (f32[256,128]{1,0:T(8,128)S(1)}, f32[256,128]{1,0:T(8,128)S(1)}, u32[]{:S(2)}, u32[]{:S(2)}) collective-permute-start(f32[256,128]{1,0:T(8,128)S(1)} %get-tuple-element.85), channel_id=1, source_target_pairs={{0,6},{2,4},{4,2},{6,0},{1,7},{3,5},{5,3},{7,1},{8,14},{10,12},{12... | collective-permute-start | bytes 393224 | tf_op jit(solution)/shard_map/ppermute | solution.py:372

commit v26 on v25

--- a/solution.py
+++ b/solution.py
@@ -12,7 +12,7 @@
 
 GRAD_WEIGHT = 0.0625
 PLANE = ("half", "col", "core")
-EIGHT, BACK, FOUR = (2, 4, 3, 5, 6, 7, 1, 0), (1, 4, 2, 5, 3, 6, 7, 0), (2, 1, 3, 0)
+EIGHT, BACK, FOUR = (4, 2, 5, 3, 6, 7, 1, 0), (1, 4, 2, 5, 3, 6, 7, 0), (2, 1, 3, 0)
 VMEM_LIMIT = 24 * 1024 * 1024
 
 

time: 89.5 us -> 90.3 us (level)
  blocking collectives: 8.97 us -> 10.1 us
  starting transfers between devices: 34.5 us -> 33.5 us
    ppermute x23, waiting for transfers between devices: 17.3 us -> 18.7 us  [deal(): lax.ppermute(value, axes, [(k, k ^ turn) for k in range(len(order))])]
    all_gather x1, blocking collectives: 8.97 us -> 10.1 us  [local(): probe_grad = lax.all_gather(probe_band, PLANE, axis=0, tiled=True)]
    ppermute x23, starting transfers between devices: 24.2 us -> 23.2 us  [deal(): lax.ppermute(value, axes, [(k, k ^ turn) for k in range(len(order))])]
where the time goes in v26:
time: 90.3 us; the launch traced here: 90.1 us
  starting transfers between devices  33.5 us (37%)
  waiting for transfers between devices  29.6 us (33%)
  Pallas kernels  12.9 us (14%)
  blocking collectives  10.1 us (11%)
  between operations  2.06 us (2%)
  local copies, waits for them, and re-layouts  1.79 us (2%)
    ppermute x23, starting transfers between devices, deal(): lax.ppermute(value, axes, [(k, k ^ turn) for k in range(len(order))])  23.2 us
    ppermute x23, waiting for transfers between devices, deal(): lax.ppermute(value, axes, [(k, k ^ turn) for k in range(len(order))])  18.7 us
    pallas_call x10, Pallas kernels, call(): pl.pallas_call(kernel, out_shape=[x for x, unused in outs], in_specs=[SME...  12.9 us
    all_gather x1, blocking collectives, local(): probe_grad = lax.all_gather(probe_band, PLANE, axis=0, tiled=True)  10.1 us
    ppermute x1, waiting for transfers between devices, local(): below = lax.ppermute(lowest, 'pair', [(k, k - 1) for k in range(1, pairs)])  7.61 us
    ppermute x1, starting transfers between devices, local(): lax.ppermute(lower_sums, 'pair', [(k, k + 1) for k in range(pairs - 1)])  3.5 us
    ppermute x1, waiting for transfers between devices, local(): lax.ppermute(lower_sums, 'pair', [(k, k + 1) for k in range(pairs - 1)])  2.62 us
    ppermute x1, starting transfers between devices, sum_over(): lax.ppermute(value, axis, [(k, k ^ step) for k in range(size)])  2.23 us
  transfers between devices with their start and end apart: 29, of which 13 were waited for; matrix products, arithmetic and copies ran while one was open for 2% of the time, Pallas kernels for 6%

profile of v26, /device:TPU:0, one launch (start us, length us, event | category | flops | bytes accessed | tf_op | source)
XLA Modules:
  0.0 90.1 jit_solution(4959696146793083801)
XLA Ops:
  0.6 1.3 %shard_map.95 = (f32[264,128]{1,0:T(8,128)S(1)}, f32[264,128]{1,0:T(8,128)S(1)}, f32[264,128]{1,0:T(8,128)S(1)}, f32[264,128]{1,0:T(8,128)S(1)}, f32[256,256]{1,0:T(8,128)S(1)}) custom-call(f32[4,256,128]{2,1,0:T(8,128)} %bitcast.9, f32[1,2,256,256]{3,2,1,0:T(8,128)} %measured.3, s32[1,2,2]{2,1,0:T(2,128)} %offsets_from.1), custom_call_target="tpu_custom_call" | custom-call | bytes 1851408 | tf_op jit(solution)/shard_map/pallas_call | solution.py:355
  1.9 3.0 %collective-permute-start = (f32[264,128]{1,0:T(8,128)S(1)}, f32[264,128]{1,0:T(8,128)S(1)}, u32[]{:S(2)}, u32[]{:S(2)}) collective-permute-start(f32[264,128]{1,0:T(8,128)S(1)} %get-tuple-element.47), channel_id=1, source_target_pairs={{0,2},{2,0},{4,6},{6,4},{1,3},{3,1},{5,7},{7,5},{8,10},{10,8},{12,... | collective-permute-start | bytes 405512 | tf_op jit(solution)/shard_map/ppermute | solution.py:372
  4.9 1.5 %collective-permute-start.1 = (f32[264,128]{1,0:T(8,128)S(1)}, f32[264,128]{1,0:T(8,128)S(1)}, u32[]{:S(2)}, u32[]{:S(2)}) collective-permute-start(f32[264,128]{1,0:T(8,128)S(1)} %get-tuple-element.48), channel_id=1, source_target_pairs={{0,4},{2,6},{4,0},{6,2},{1,5},{3,7},{5,1},{7,3},{8,12},{10,14},{12... | collective-permute-start | bytes 405512 | tf_op jit(solution)/shard_map/ppermute | solution.py:372
  6.6 1.3 %fusion = (s32[1,1]{1,0:T(1,128)}, s32[1,1]{1,0:T(1,128)}) fusion(s32[1,2]{1,0:T(1,128)} %param.11), kind=kLoop, calls=%fused_computation.8 | loop fusion | bytes 16 | tf_op jit(solution)/shard_map/slice | solution.py:412
  9.2 0.1 slice_reduce_fusion.2
  9.3 3.5 %collective-permute-done.1.refs_0_ = f32[264,128]{1,0:T(8,128)S(1)} collective-permute-done((f32[264,128]{1,0:T(8,128)S(1)}, f32[264,128]{1,0:T(8,128)S(1)}, u32[]{:S(2)}, u32[]{:S(2)}) %collective-permute-start.1) | collective-permute-done | bytes 135200 | tf_op jit(solution)/shard_map/ppermute | solution.py:372
  13.0 0.1 slice_reduce_fusion
  13.2 1.3 %collective-permute-start.4 = (f32[2,256,128]{2,1,0:T(8,128)S(1)}, f32[2,256,128]{2,1,0:T(8,128)S(1)}, u32[]{:S(2)}, u32[]{:S(2)}) collective-permute-start(f32[2,256,128]{2,1,0:T(8,128)S(1)} %shard_map.96), channel_id=1, source_target_pairs={{8,0},{16,8},{24,16},{9,1},{17,9},{25,17},{10,2},{18,10},{26,18},{... | collective-permute-start | bytes 786440 | tf_op jit(solution)/shard_map/ppermute | solution.py:405
  14.5 1.6 %collective-permute-start.12 = (f32[256,256]{1,0:T(8,128)S(1)}, f32[256,256]{1,0:T(8,128)S(1)}, u32[]{:S(2)}, u32[]{:S(2)}) collective-permute-start(f32[256,256]{1,0:T(8,128)S(1)} %get-tuple-element.60), channel_id=1, source_target_pairs={{0,4},{4,0},{1,5},{5,1},{2,6},{6,2},{3,7},{7,3},{8,12},{12,8},{9,1... | collective-permute-start | bytes 786440 | tf_op jit(solution)/shard_map/ppermute | solution.py:406
  16.2 7.6 %collective-permute-done.4.refs_4_ = f32[2,256,128]{2,1,0:T(8,128)S(1)} collective-permute-done((f32[2,256,128]{2,1,0:T(8,128)S(1)}, f32[2,256,128]{2,1,0:T(8,128)S(1)}, u32[]{:S(2)}, u32[]{:S(2)}) %collective-permute-start.4) | collective-permute-done | bytes 262176 | tf_op jit(solution)/shard_map/ppermute | solution.py:405
  23.8 1.3 %shard_map.97 = (f32[256,128]{1,0:T(8,128)S(1)}, f32[256,128]{1,0:T(8,128)S(1)}, f32[256,128]{1,0:T(8,128)S(1)}, f32[256,128]{1,0:T(8,128)S(1)}, f32[256,128]{1,...) custom-call(s32[5,8]{1,0:T(8,128)S(1)} %concatenate.7.offs, ...), custom_call_target="tpu_custom_call" | custom-call | flops 2097152 | bytes 1851392 | tf_op jit(solution)/shard_map/pallas_call | solution.py:355
  25.1 1.6 %collective-permute-start.5 = (f32[256,128]{1,0:T(8,128)S(1)}, f32[256,128]{1,0:T(8,128)S(1)}, u32[]{:S(2)}, u32[]{:S(2)}) collective-permute-start(f32[256,128]{1,0:T(8,128)S(1)} %get-tuple-element.52), channel_id=1, source_target_pairs={{0,4},{1,5},{2,6},{3,7},{4,0},{5,1},{6,2},{7,3},{8,12},{9,13},{10,... | collective-permute-start | bytes 393224 | tf_op jit(solution)/shard_map/ppermute | solution.py:372
  26.7 0.5 collective-permute-start.6
  27.2 1.7 %collective-permute-start.8 = (f32[256,128]{1,0:T(8,128)S(1)}, f32[256,128]{1,0:T(8,128)S(1)}, u32[]{:S(2)}, u32[]{:S(2)}) collective-permute-start(f32[256,128]{1,0:T(8,128)S(1)} %get-tuple-element.55), channel_id=1, source_target_pairs={{0,3},{1,2},{2,1},{3,0},{4,7},{5,6},{6,5},{7,4},{8,11},{9,10},{10,... | collective-permute-start | bytes 393224 | tf_op jit(solution)/shard_map/ppermute | solution.py:372
  29.0 1.5 %collective-permute-start.9 = (f32[256,128]{1,0:T(8,128)S(1)}, f32[256,128]{1,0:T(8,128)S(1)}, u32[]{:S(2)}, u32[]{:S(2)}) collective-permute-start(f32[256,128]{1,0:T(8,128)S(1)} %get-tuple-element.56), channel_id=1, source_target_pairs={{0,6},{1,7},{2,4},{3,5},{4,2},{5,3},{6,0},{7,1},{8,14},{9,15},{10,... | collective-permute-start | bytes 393224 | tf_op jit(solution)/shard_map/ppermute | solution.py:372
  30.5 0.7 collective-permute-start.10
  31.1 2.0 %collective-permute-done.6.refs_1_ = f32[256,128]{1,0:T(8,128)S(1)} collective-permute-done((f32[256,128]{1,0:T(8,128)S(1)}, f32[256,128]{1,0:T(8,128)S(1)}, u32[]{:S(2)}, u32[]{:S(2)}) %collective-permute-start.6) | collective-permute-done | bytes 131104 | tf_op jit(solution)/shard_map/ppermute | solution.py:372
  33.1 2.5 %shard_map.98 = (f32[2,256,256]{2,1,0:T(8,128)S(1)}, f32[256,256]{1,0:T(8,128)S(1)}, bf16[6,512,256]{2,1,0:T(8,128)(2,1)S(1)}) custom-call(s32[5,8]{1,0:T(8,128)S(1)} %concatenate.7.offs, f32[256,256]{1,0:T(8,128)S(1)} %collective-permute-done.12.taken, f32[2,256,256]{2,1,0:T(8,128)} %probe_from.1, f32[1,2,256,256]{3,2,1,0:T(8,128)} %measured.3, ...), custom_call_target="tpu_custom_call" | custom-call | flops 201326592 | bytes 5505024 | tf_op jit(solution)/shard_map/pallas_call | solution.py:355
  35.6 2.1 %collective-permute-done.9.refs_4_ = f32[256,128]{1,0:T(8,128)S(1)} collective-permute-done((f32[256,128]{1,0:T(8,128)S(1)}, f32[256,128]{1,0:T(8,128)S(1)}, u32[]{:S(2)}, u32[]{:S(2)}) %collective-permute-start.9) | collective-permute-done | bytes 131104 | tf_op jit(solution)/shard_map/ppermute | solution.py:372
  37.7 1.9 %collective-permute-done.10.refs_5_ = f32[256,128]{1,0:T(8,128)S(1)} collective-permute-done((f32[256,128]{1,0:T(8,128)S(1)}, f32[256,128]{1,0:T(8,128)S(1)}, u32[]{:S(2)}, u32[]{:S(2)}) %collective-permute-start.10) | collective-permute-done | bytes 131104 | tf_op jit(solution)/shard_map/ppermute | solution.py:372
  39.6 4.2 %shard_map.99 = (f32[768,128]{1,0:T(8,128)S(1)}, f32[256,128]{1,0:T(8,128)S(1)}, f32[256,128]{1,0:T(8,128)S(1)}, f32[256,128]{1,0:T(8,128)S(1)}, f32[256,128]{1,...) custom-call(s32[5,8]{1,0:T(8,128)S(1)} %concatenate.7.offs, ...), custom_call_target="tpu_custom_call" | custom-call | flops 1610612736 | bytes 5120000 | tf_op jit(solution)/shard_map/pallas_call | solution.py:355
  43.8 0.4 collective-permute-start.13
  44.1 1.5 %collective-permute-start.14 = (f32[256,128]{1,0:T(8,128)S(1)}, f32[256,128]{1,0:T(8,128)S(1)}, u32[]{:S(2)}, u32[]{:S(2)}) collective-permute-start(f32[256,128]{1,0:T(8,128)S(1)} %get-tuple-element.65), channel_id=1, source_target_pairs={{0,4},{1,5},{2,6},{3,7},{4,0},{5,1},{6,2},{7,3},{8,12},{9,13},{10,... | collective-permute-start | bytes 393224 | tf_op jit(solution)/shard_map/ppermute | solution.py:372
  45.6 0.6 collective-permute-start.15
  46.2 0.2 collective-permute-start.16
  46.4 1.5 %collective-permute-start.17 = (f32[256,128]{1,0:T(8,128)S(1)}, f32[256,128]{1,0:T(8,128)S(1)}, u32[]{:S(2)}, u32[]{:S(2)}) collective-permute-start(f32[256,128]{1,0:T(8,128)S(1)} %get-tuple-element.68), channel_id=1, source_target_pairs={{0,3},{1,2},{2,1},{3,0},{4,7},{5,6},{6,5},{7,4},{8,11},{9,10},{10,... | collective-permute-start | bytes 393224 | tf_op jit(solution)/shard_map/ppermute | solution.py:372
  47.9 2.4 %collective-permute-done.14.refs_1_ = f32[256,128]{1,0:T(8,128)S(1)} collective-permute-done((f32[256,128]{1,0:T(8,128)S(1)}, f32[256,128]{1,0:T(8,128)S(1)}, u32[]{:S(2)}, u32[]{:S(2)}) %collective-permute-start.14) | collective-permute-done | bytes 131104 | tf_op jit(solution)/shard_map/ppermute | solution.py:372
  50.3 1.5 %collective-permute-start.18 = (f32[256,128]{1,0:T(8,128)S(1)}, f32[256,128]{1,0:T(8,128)S(1)}, u32[]{:S(2)}, u32[]{:S(2)}) collective-permute-start(f32[256,128]{1,0:T(8,128)S(1)} %get-tuple-element.69), channel_id=1, source_target_pairs={{0,6},{1,7},{2,4},{3,5},{4,2},{5,3},{6,0},{7,1},{8,14},{9,15},{10,... | collective-permute-start | bytes 393224 | tf_op jit(solution)/shard_map/ppermute | solution.py:372
  51.8 0.2 collective-permute-done.15.refs_2_
  52.0 0.7 collective-permute-start.20
  52.7 1.2 %collective-permute-start.21 = (f32[128,128]{1,0:T(8,128)S(1)}, f32[128,128]{1,0:T(8,128)S(1)}, u32[]{:S(2)}, u32[]{:S(2)}) collective-permute-start(f32[128,128]{1,0:T(8,128)S(1)} %get-tuple-element.74), channel_id=1, source_target_pairs={{0,2},{2,0},{4,6},{6,4},{1,3},{3,1},{5,7},{7,5},{8,10},{10,8},{12,... | collective-permute-start | bytes 196616 | tf_op jit(solution)/shard_map/ppermute | solution.py:372
  53.9 1.6 %collective-permute-start.22 = (f32[128,128]{1,0:T(8,128)S(1)}, f32[128,128]{1,0:T(8,128)S(1)}, u32[]{:S(2)}, u32[]{:S(2)}) collective-permute-start(f32[128,128]{1,0:T(8,128)S(1)} %get-tuple-element.75), channel_id=1, source_target_pairs={{0,6},{2,4},{4,2},{6,0},{1,7},{3,5},{5,3},{7,1},{8,14},{10,12},{12... | collective-permute-start | bytes 196616 | tf_op jit(solution)/shard_map/ppermute | solution.py:372
  55.5 2.0 %collective-permute-done.18.refs_5_ = f32[256,128]{1,0:T(8,128)S(1)} collective-permute-done((f32[256,128]{1,0:T(8,128)S(1)}, f32[256,128]{1,0:T(8,128)S(1)}, u32[]{:S(2)}, u32[]{:S(2)}) %collective-permute-start.18) | collective-permute-done | bytes 131104 | tf_op jit(solution)/shard_map/ppermute | solution.py:372
  57.5 1.0 %collective-permute-done.19.refs_6_ = f32[256,128]{1,0:T(8,128)S(1)} collective-permute-done((f32[256,128]{1,0:T(8,128)S(1)}, f32[256,128]{1,0:T(8,128)S(1)}, u32[]{:S(2)}, u32[]{:S(2)}) %collective-permute-start.19) | collective-permute-done | bytes 131104 | tf_op jit(solution)/shard_map/ppermute | solution.py:372
  58.6 2.9 %collective-permute-done.20.refs_8_ = f32[128,128]{1,0:T(8,128)S(1)} collective-permute-done((f32[128,128]{1,0:T(8,128)S(1)}, f32[128,128]{1,0:T(8,128)S(1)}, u32[]{:S(2)}, u32[]{:S(2)}) %collective-permute-start.20) | collective-permute-done | bytes 65568 | tf_op jit(solution)/shard_map/ppermute | solution.py:372
  61.4 0.8 collective-permute-done.22.refs_10_
  62.2 1.0 %shard_map.102 = (f32[2,256,128]{2,1,0:T(8,128)S(1)}, f32[64,256]{1,0:T(8,128)S(1)}) custom-call(s32[5,8]{1,0:T(8,128)S(1)} %concatenate.7.offs, f32[768,128]{1,0:T(8,128)S(1)} %collective-permute-done.13.refs_0_.got, f32[256,128]{1,0:T(8,128)S(1)} %collective-permute-done.14.refs_1_, f32[256,128]{1,0:T(8,128)S(1)} %collective-permute-done.15.refs_2_, ...), custom_call_target="tpu_custom_call" | custom-call | flops 2097152 | bytes 1900544 | tf_op jit(solution)/shard_map/pallas_call | solution.py:355
  63.3 3.5 %collective-permute-start.23 = (f32[2,256,128]{2,1,0:T(8,128)S(1)}, f32[2,256,128]{2,1,0:T(8,128)S(1)}, u32[]{:S(2)}, u32[]{:S(2)}) collective-permute-start(f32[2,256,128]{2,1,0:T(8,128)S(1)} %get-tuple-element.77), channel_id=1, source_target_pairs={{0,8},{8,16},{16,24},{1,9},{9,17},{17,25},{2,10},{10,18},{18,26},{... | collective-permute-start | bytes 786440 | tf_op jit(solution)/shard_map/ppermute | solution.py:450
  66.8 1.6 %collective-permute-start.24 = (f32[64,256]{1,0:T(8,128)S(1)}, f32[64,256]{1,0:T(8,128)S(1)}, u32[]{:S(2)}, u32[]{:S(2)}) collective-permute-start(f32[64,256]{1,0:T(8,128)S(1)} %get-tuple-element.82), channel_id=1, source_target_pairs={{0,8},{8,0},{16,24},{24,16},{1,9},{9,1},{17,25},{25,17},{2,10},{10... | collective-permute-start | bytes 196616 | tf_op jit(solution)/shard_map/ppermute | solution.py:453
  68.4 1.5 %shard_map.100.own = f32[4,256,128]{2,1,0:T(8,128)S(1)} custom-call(s32[5,8]{1,0:T(8,128)S(1)} %concatenate.7.offs, f32[768,128]{1,0:T(8,128)S(1)} %collective-permute-done.13.refs_0_.got, f32[256,128]{1,0:T(8,128)S(1)} %collective-permute-done.14.refs_1_, f32[256,128]{1,0:T(8,128)S(1)} %collective-permute-done.15.refs_2_, ...), custom_call_target="tpu_custom_call" | custom-call | flops 4194304 | bytes 1835008 | tf_op jit(solution)/shard_map/pallas_call | solution.py:355
  69.9 2.6 %collective-permute-done.23.above = f32[2,256,128]{2,1,0:T(8,128)S(1)} collective-permute-done((f32[2,256,128]{2,1,0:T(8,128)S(1)}, f32[2,256,128]{2,1,0:T(8,128)S(1)}, u32[]{:S(2)}, u32[]{:S(2)}) %collective-permute-start.23) | collective-permute-done | bytes 262176 | tf_op jit(solution)/shard_map/ppermute | solution.py:450
  72.6 0.6 collective-permute-done.24
  73.2 2.2 %collective-permute-start.28 = (f32[64,256]{1,0:T(8,128)S(1)}, f32[64,256]{1,0:T(8,128)S(1)}, u32[]{:S(2)}, u32[]{:S(2)}) collective-permute-start(f32[64,256]{1,0:T(8,128)S(1)} %add.8), channel_id=1, source_target_pairs={{0,16},{8,24},{16,0},{24,8},{1,17},{9,25},{17,1},{25,9},{2,18},{10... | collective-permute-start | bytes 196616 | tf_op jit(solution)/shard_map/ppermute | solution.py:380
  75.4 1.3 %collective-permute-start.25 = (f32[256,128]{1,0:T(8,128)S(1)}, f32[256,128]{1,0:T(8,128)S(1)}, u32[]{:S(2)}, u32[]{:S(2)}) collective-permute-start(f32[256,128]{1,0:T(8,128)S(1)} %get-tuple-element.83), channel_id=1, source_target_pairs={{0,4},{2,6},{4,0},{6,2},{1,5},{3,7},{5,1},{7,3},{8,12},{10,14},{12... | collective-permute-start | bytes 393224 | tf_op jit(solution)/shard_map/ppermute | solution.py:372
  76.7 0.8 collective-permute-start.26
  77.5 1.5 %collective-permute-start.27 = (f32[256,128]{1,0:T(8,128)S(1)}, f32[256,128]{1,0:T(8,128)S(1)}, u32[]{:S(2)}, u32[]{:S(2)}) collective-permute-start(f32[256,128]{1,0:T(8,128)S(1)} %get-tuple-element.85), channel_id=1, source_target_pairs={{0,6},{2,4},{4,2},{6,0},{1,7},{3,5},{5,3},{7,1},{8,14},{10,12},{12... | collective-permute-start | bytes 393224 | tf_op jit(solution)/shard_map/ppermute | solution.py:372
  78.9 10.1 %all_gather.3.refs_4_ = f32[512,256]{1,0:T(8,128)S(1)} all-gather(f32[64,256]{1,0:T(8,128)S(1)} %add.9), channel_id=1, replica_groups=mesh['pair'=4,'half'=2,'col'=2,'core'=2] {'half','col','core'}, dimensions={0}, use_global_device_ids=true | all-gather | bytes 589824 | tf_op jit(solution)/shard_map/all_gather | solution.py:462
  89.1 1.0 %shard_map.104 = (f32[4,256,128]{2,1,0:T(8,128)}, f32[512,256]{1,0:T(8,128)}) custom-call(f32[256,128]{1,0:T(8,128)S(1)} %collective-permute-done.25.refs_0_, f32[256,128]{1,0:T(8,128)S(1)} %collective-permute-done.26.refs_1_, f32[256,128]{1,0:T(8,128)S(1)} %collective-permute-done.27.refs_2_, f32[256,128]{1,0:T(8,128)S(1)} %get-tuple-element.86.refs_3_, ...), custom_call_target="tpu_custom_call" | custom-call | bytes 2097152 | tf_op jit(solution)/shard_map/pallas_call | solution.py:355
  (34 shorter events, 0.6 us)
Async XLA Ops:
  1.9 7.3 %collective-permute-start = (f32[264,128]{1,0:T(8,128)S(1)}, f32[264,128]{1,0:T(8,128)S(1)}, u32[]{:S(2)}, u32[]{:S(2)}) collective-permute-start(f32[264,128]{1,0:T(8,128)S(1)} %get-tuple-element.47), channel_id=1, source_target_pairs={{0,2},{2,0},{4,6},{6,4},{1,3},{3,1},{5,7},{7,5},{8,10},{10,8},{12,... | collective-permute-start | bytes 405512 | tf_op jit(solution)/shard_map/ppermute | solution.py:372
  4.9 7.9 %collective-permute-start.1 = (f32[264,128]{1,0:T(8,128)S(1)}, f32[264,128]{1,0:T(8,128)S(1)}, u32[]{:S(2)}, u32[]{:S(2)}) collective-permute-start(f32[264,128]{1,0:T(8,128)S(1)} %get-tuple-element.48), channel_id=1, source_target_pairs={{0,4},{2,6},{4,0},{6,2},{1,5},{3,7},{5,1},{7,3},{8,12},{10,14},{12... | collective-permute-start | bytes 405512 | tf_op jit(solution)/shard_map/ppermute | solution.py:372
  6.4 6.5 %collective-permute-start.2 = (f32[264,128]{1,0:T(8,128)S(1)}, f32[264,128]{1,0:T(8,128)S(1)}, u32[]{:S(2)}, u32[]{:S(2)}) collective-permute-start(f32[264,128]{1,0:T(8,128)S(1)} %get-tuple-element.49), channel_id=1, source_target_pairs={{0,6},{2,4},{4,2},{6,0},{1,7},{3,5},{5,3},{7,1},{8,14},{10,12},{12... | collective-permute-start | bytes 405512 | tf_op jit(solution)/shard_map/ppermute | solution.py:372
  13.1 3.0 %collective-permute-start.3 = (s32[4,4]{1,0:T(4,128)S(1)}, s32[4,4]{1,0:T(4,128)S(1)}, u32[]{:S(2)}, u32[]{:S(2)}) collective-permute-start(s32[4,4]{1,0:T(4,128)S(1)} %maximum_convert_fusion), channel_id=1, source_target_pairs={{0,1},{1,0},{2,3},{3,2},{4,5},{5,4},{6,7},{7,6},{8,9},{9,8},{10,11... | collective-permute-start | bytes 200 | tf_op jit(solution)/shard_map/ppermute | solution.py:410
  13.2 10.6 %collective-permute-start.4 = (f32[2,256,128]{2,1,0:T(8,128)S(1)}, f32[2,256,128]{2,1,0:T(8,128)S(1)}, u32[]{:S(2)}, u32[]{:S(2)}) collective-permute-start(f32[2,256,128]{2,1,0:T(8,128)S(1)} %shard_map.96), channel_id=1, source_target_pairs={{8,0},{16,8},{24,16},{9,1},{17,9},{25,17},{10,2},{18,10},{26,18},{... | collective-permute-start | bytes 786440 | tf_op jit(solution)/shard_map/ppermute | solution.py:405
  14.5 14.4 %collective-permute-start.12 = (f32[256,256]{1,0:T(8,128)S(1)}, f32[256,256]{1,0:T(8,128)S(1)}, u32[]{:S(2)}, u32[]{:S(2)}) collective-permute-start(f32[256,256]{1,0:T(8,128)S(1)} %get-tuple-element.60), channel_id=1, source_target_pairs={{0,4},{4,0},{1,5},{5,1},{2,6},{6,2},{3,7},{7,3},{8,12},{12,8},{9,1... | collective-permute-start | bytes 786440 | tf_op jit(solution)/shard_map/ppermute | solution.py:406
  25.1 5.3 %collective-permute-start.5 = (f32[256,128]{1,0:T(8,128)S(1)}, f32[256,128]{1,0:T(8,128)S(1)}, u32[]{:S(2)}, u32[]{:S(2)}) collective-permute-start(f32[256,128]{1,0:T(8,128)S(1)} %get-tuple-element.52), channel_id=1, source_target_pairs={{0,4},{1,5},{2,6},{3,7},{4,0},{5,1},{6,2},{7,3},{8,12},{9,13},{10,... | collective-permute-start | bytes 393224 | tf_op jit(solution)/shard_map/ppermute | solution.py:372
  26.7 6.4 %collective-permute-start.6 = (f32[256,128]{1,0:T(8,128)S(1)}, f32[256,128]{1,0:T(8,128)S(1)}, u32[]{:S(2)}, u32[]{:S(2)}) collective-permute-start(f32[256,128]{1,0:T(8,128)S(1)} %get-tuple-element.53), channel_id=1, source_target_pairs={{0,2},{1,3},{2,0},{3,1},{4,6},{5,7},{6,4},{7,5},{8,10},{9,11},{10,... | collective-permute-start | bytes 393224 | tf_op jit(solution)/shard_map/ppermute | solution.py:372
  27.2 8.4 %collective-permute-start.7 = (f32[256,128]{1,0:T(8,128)S(1)}, f32[256,128]{1,0:T(8,128)S(1)}, u32[]{:S(2)}, u32[]{:S(2)}) collective-permute-start(f32[256,128]{1,0:T(8,128)S(1)} %get-tuple-element.54), channel_id=1, source_target_pairs={{0,5},{1,4},{2,7},{3,6},{4,1},{5,0},{6,3},{7,2},{8,13},{9,12},{10,... | collective-permute-start | bytes 393224 | tf_op jit(solution)/shard_map/ppermute | solution.py:372
  27.2 8.4 %collective-permute-start.8 = (f32[256,128]{1,0:T(8,128)S(1)}, f32[256,128]{1,0:T(8,128)S(1)}, u32[]{:S(2)}, u32[]{:S(2)}) collective-permute-start(f32[256,128]{1,0:T(8,128)S(1)} %get-tuple-element.55), channel_id=1, source_target_pairs={{0,3},{1,2},{2,1},{3,0},{4,7},{5,6},{6,5},{7,4},{8,11},{9,10},{10,... | collective-permute-start | bytes 393224 | tf_op jit(solution)/shard_map/ppermute | solution.py:372
  29.0 8.7 %collective-permute-start.9 = (f32[256,128]{1,0:T(8,128)S(1)}, f32[256,128]{1,0:T(8,128)S(1)}, u32[]{:S(2)}, u32[]{:S(2)}) collective-permute-start(f32[256,128]{1,0:T(8,128)S(1)} %get-tuple-element.56), channel_id=1, source_target_pairs={{0,6},{1,7},{2,4},{3,5},{4,2},{5,3},{6,0},{7,1},{8,14},{9,15},{10,... | collective-permute-start | bytes 393224 | tf_op jit(solution)/shard_map/ppermute | solution.py:372
  30.5 9.1 %collective-permute-start.10 = (f32[256,128]{1,0:T(8,128)S(1)}, f32[256,128]{1,0:T(8,128)S(1)}, u32[]{:S(2)}, u32[]{:S(2)}) collective-permute-start(f32[256,128]{1,0:T(8,128)S(1)} %get-tuple-element.57), channel_id=1, source_target_pairs={{0,7},{1,6},{2,5},{3,4},{4,3},{5,2},{6,1},{7,0},{8,15},{9,14},{10,... | collective-permute-start | bytes 393224 | tf_op jit(solution)/shard_map/ppermute | solution.py:372
  33.1 6.5 %copy-start = (f32[2,136,128]{2,1,0:T(8,128)S(1)}, f32[2,136,128]{2,1,0:T(8,128)}, u32[]{:S(2)}) copy-start(f32[2,136,128]{2,1,0:T(8,128)} %constant.17.clone.refs_11_) | copy-start | bytes 417796
  33.1 6.5 %collective-permute-start.11 = (f32[256,128]{1,0:T(8,128)S(1)}, f32[256,128]{1,0:T(8,128)S(1)}, u32[]{:S(2)}, u32[]{:S(2)}) collective-permute-start(f32[256,128]{1,0:T(8,128)S(1)} %get-tuple-element.58), channel_id=1, source_target_pairs={{0,1},{1,0},{2,3},{3,2},{4,5},{5,4},{6,7},{7,6},{8,9},{9,8},{10,11... | collective-permute-start | bytes 393224 | tf_op jit(solution)/shard_map/ppermute | solution.py:372
  43.8 8.0 %collective-permute-start.13 = (f32[768,128]{1,0:T(8,128)S(1)}, f32[768,128]{1,0:T(8,128)S(1)}, u32[]{:S(2)}, u32[]{:S(2)}) collective-permute-start(f32[768,128]{1,0:T(8,128)S(1)} %get-tuple-element.64), channel_id=1, source_target_pairs={{0,1},{1,0},{2,3},{3,2},{4,5},{5,4},{6,7},{7,6},{8,9},{9,8},{10,11... | collective-permute-start | bytes 1179656 | tf_op jit(solution)/shard_map/ppermute | solution.py:372
  44.1 6.1 %collective-permute-start.14 = (f32[256,128]{1,0:T(8,128)S(1)}, f32[256,128]{1,0:T(8,128)S(1)}, u32[]{:S(2)}, u32[]{:S(2)}) collective-permute-start(f32[256,128]{1,0:T(8,128)S(1)} %get-tuple-element.65), channel_id=1, source_target_pairs={{0,4},{1,5},{2,6},{3,7},{4,0},{5,1},{6,2},{7,3},{8,12},{9,13},{10,... | collective-permute-start | bytes 393224 | tf_op jit(solution)/shard_map/ppermute | solution.py:372
  45.6 6.4 %collective-permute-start.15 = (f32[256,128]{1,0:T(8,128)S(1)}, f32[256,128]{1,0:T(8,128)S(1)}, u32[]{:S(2)}, u32[]{:S(2)}) collective-permute-start(f32[256,128]{1,0:T(8,128)S(1)} %get-tuple-element.66), channel_id=1, source_target_pairs={{0,2},{1,3},{2,0},{3,1},{4,6},{5,7},{6,4},{7,5},{8,10},{9,11},{10,... | collective-permute-start | bytes 393224 | tf_op jit(solution)/shard_map/ppermute | solution.py:372
  46.2 6.5 %collective-permute-start.16 = (f32[256,128]{1,0:T(8,128)S(1)}, f32[256,128]{1,0:T(8,128)S(1)}, u32[]{:S(2)}, u32[]{:S(2)}) collective-permute-start(f32[256,128]{1,0:T(8,128)S(1)} %get-tuple-element.67), channel_id=1, source_target_pairs={{0,5},{1,4},{2,7},{3,6},{4,1},{5,0},{6,3},{7,2},{8,13},{9,12},{10,... | collective-permute-start | bytes 393224 | tf_op jit(solution)/shard_map/ppermute | solution.py:372
  46.4 7.5 %collective-permute-start.17 = (f32[256,128]{1,0:T(8,128)S(1)}, f32[256,128]{1,0:T(8,128)S(1)}, u32[]{:S(2)}, u32[]{:S(2)}) collective-permute-start(f32[256,128]{1,0:T(8,128)S(1)} %get-tuple-element.68), channel_id=1, source_target_pairs={{0,3},{1,2},{2,1},{3,0},{4,7},{5,6},{6,5},{7,4},{8,11},{9,10},{10,... | collective-permute-start | bytes 393224 | tf_op jit(solution)/shard_map/ppermute | solution.py:372
  50.3 7.3 %collective-permute-start.18 = (f32[256,128]{1,0:T(8,128)S(1)}, f32[256,128]{1,0:T(8,128)S(1)}, u32[]{:S(2)}, u32[]{:S(2)}) collective-permute-start(f32[256,128]{1,0:T(8,128)S(1)} %get-tuple-element.69), channel_id=1, source_target_pairs={{0,6},{1,7},{2,4},{3,5},{4,2},{5,3},{6,0},{7,1},{8,14},{9,15},{10,... | collective-permute-start | bytes 393224 | tf_op jit(solution)/shard_map/ppermute | solution.py:372
  51.8 6.8 %collective-permute-start.19 = (f32[256,128]{1,0:T(8,128)S(1)}, f32[256,128]{1,0:T(8,128)S(1)}, u32[]{:S(2)}, u32[]{:S(2)}) collective-permute-start(f32[256,128]{1,0:T(8,128)S(1)} %get-tuple-element.70), channel_id=1, source_target_pairs={{0,7},{1,6},{2,5},{3,4},{4,3},{5,2},{6,1},{7,0},{8,15},{9,14},{10,... | collective-permute-start | bytes 393224 | tf_op jit(solution)/shard_map/ppermute | solution.py:372
  52.0 9.4 %collective-permute-start.20 = (f32[128,128]{1,0:T(8,128)S(1)}, f32[128,128]{1,0:T(8,128)S(1)}, u32[]{:S(2)}, u32[]{:S(2)}) collective-permute-start(f32[128,128]{1,0:T(8,128)S(1)} %get-tuple-element.73), channel_id=1, source_target_pairs={{0,4},{2,6},{4,0},{6,2},{1,5},{3,7},{5,1},{7,3},{8,12},{10,14},{12... | collective-permute-start | bytes 196616 | tf_op jit(solution)/shard_map/ppermute | solution.py:372
  52.7 8.7 %collective-permute-start.21 = (f32[128,128]{1,0:T(8,128)S(1)}, f32[128,128]{1,0:T(8,128)S(1)}, u32[]{:S(2)}, u32[]{:S(2)}) collective-permute-start(f32[128,128]{1,0:T(8,128)S(1)} %get-tuple-element.74), channel_id=1, source_target_pairs={{0,2},{2,0},{4,6},{6,4},{1,3},{3,1},{5,7},{7,5},{8,10},{10,8},{12,... | collective-permute-start | bytes 196616 | tf_op jit(solution)/shard_map/ppermute | solution.py:372
  53.9 8.3 %collective-permute-start.22 = (f32[128,128]{1,0:T(8,128)S(1)}, f32[128,128]{1,0:T(8,128)S(1)}, u32[]{:S(2)}, u32[]{:S(2)}) collective-permute-start(f32[128,128]{1,0:T(8,128)S(1)} %get-tuple-element.75), channel_id=1, source_target_pairs={{0,6},{2,4},{4,2},{6,0},{1,7},{3,5},{5,3},{7,1},{8,14},{10,12},{12... | collective-permute-start | bytes 196616 | tf_op jit(solution)/shard_map/ppermute | solution.py:372
  63.3 9.2 %collective-permute-start.23 = (f32[2,256,128]{2,1,0:T(8,128)S(1)}, f32[2,256,128]{2,1,0:T(8,128)S(1)}, u32[]{:S(2)}, u32[]{:S(2)}) collective-permute-start(f32[2,256,128]{2,1,0:T(8,128)S(1)} %get-tuple-element.77), channel_id=1, source_target_pairs={{0,8},{8,16},{16,24},{1,9},{9,17},{17,25},{2,10},{10,18},{18,26},{... | collective-permute-start | bytes 786440 | tf_op jit(solution)/shard_map/ppermute | solution.py:450
  66.8 6.4 %collective-permute-start.24 = (f32[64,256]{1,0:T(8,128)S(1)}, f32[64,256]{1,0:T(8,128)S(1)}, u32[]{:S(2)}, u32[]{:S(2)}) collective-permute-start(f32[64,256]{1,0:T(8,128)S(1)} %get-tuple-element.82), channel_id=1, source_target_pairs={{0,8},{8,0},{16,24},{24,16},{1,9},{9,1},{17,25},{25,17},{2,10},{10... | collective-permute-start | bytes 196616 | tf_op jit(solution)/shard_map/ppermute | solution.py:453
  73.2 5.7 %collective-permute-start.28 = (f32[64,256]{1,0:T(8,128)S(1)}, f32[64,256]{1,0:T(8,128)S(1)}, u32[]{:S(2)}, u32[]{:S(2)}) collective-permute-start(f32[64,256]{1,0:T(8,128)S(1)} %add.8), channel_id=1, source_target_pairs={{0,16},{8,24},{16,0},{24,8},{1,17},{9,25},{17,1},{25,9},{2,18},{10... | collective-permute-start | bytes 196616 | tf_op jit(solution)/shard_map/ppermute | solution.py:380
  75.4 13.6 %collective-permute-start.25 = (f32[256,128]{1,0:T(8,128)S(1)}, f32[256,128]{1,0:T(8,128)S(1)}, u32[]{:S(2)}, u32[]{:S(2)}) collective-permute-start(f32[256,128]{1,0:T(8,128)S(1)} %get-tuple-element.83), channel_id=1, source_target_pairs={{0,4},{2,6},{4,0},{6,2},{1,5},{3,7},{5,1},{7,3},{8,12},{10,14},{12... | collective-permute-start | bytes 393224 | tf_op jit(solution)/shard_map/ppermute | solution.py:372
  76.7 12.4 %collective-permute-start.26 = (f32[256,128]{1,0:T(8,128)S(1)}, f32[256,128]{1,0:T(8,128)S(1)}, u32[]{:S(2)}, u32[]{:S(2)}) collective-permute-start(f32[256,128]{1,0:T(8,128)S(1)} %get-tuple-element.84), channel_id=1, source_target_pairs={{0,2},{2,0},{4,6},{6,4},{1,3},{3,1},{5,7},{7,5},{8,10},{10,8},{12,... | collective-permute-start | bytes 393224 | tf_op jit(solution)/shard_map/ppermute | solution.py:372
  77.5 11.6 %collective-permute-start.27 = (f32[256,128]{1,0:T(8,128)S(1)}, f32[256,128]{1,0:T(8,128)S(1)}, u32[]{:S(2)}, u32[]{:S(2)}) collective-permute-start(f32[256,128]{1,0:T(8,128)S(1)} %get-tuple-element.85), channel_id=1, source_target_pairs={{0,6},{2,4},{4,2},{6,0},{1,7},{3,5},{5,3},{7,1},{8,14},{10,12},{12... | collective-permute-start | bytes 393224 | tf_op jit(solution)/shard_map/ppermute | solution.py:372
